TPU v7x, 32 devices: a whole 2x2x4 slice. The times are simulated.
32 devices in a mesh: case: 2 (over y), px: 4 (over z), py: 4 (over x, core).
Axes of the slice: x: 2, y: 2, z: 4, core: 2. Of those that a mesh axis runs over, the one named last changes fastest.
Arguments:
- prior_basis: float32 [256, 8, 16, 128], P('case', 'px', 'py'), parts along dimension 0, may hold values from -6 to 6
- previous: float32 [64, 8, 16, 128], P('case', 'px', 'py'), parts along dimension 0, may hold values from -6 to 6
- neighbours: int32 [5, 8, 16], P(None, 'px', 'py'), may hold values from 0 to 8
- tile_kinds: int32 [5, 8, 16], P(None, 'px', 'py'), may hold values from 0 to 7
- stiff_tiles: float32 [8, 128, 128], replicated, may hold values from -0.3 to 0.3
- mass_tiles: float32 [8, 128, 128], replicated, may hold values from -0.18 to 0.18
Outputs:
- new_block: float32 [64, 8, 16, 128], P('case', 'px', 'py'), parts along dimension 0
- coupling: float32 [256, 32], P('case'), parts along dimension 0
- r_factor: float32 [64, 32], P('case'), parts along dimension 0
- reduced: float32 [4, 160, 32], P('case'), parts along dimension 0
There are 2 independent parts, one for each index of `case`. A program takes and returns all parts, laid end to end along the dimension named above; an argument that names none is the same for every part. Nothing has to cross between parts.
Inputs may be any that keep to these rules, and one draw needn't show every extreme that they name: `neighbours`: entry v couples a tile to the tile offset by (v // 3 - 1, v % 3 - 1) along the two tile indices.
All inputs are finite; a program needn't handle non-finite values.
Results may differ from a plain program's by a relative error of at most 0.0003.
Values sent between devices are 32-bit elements; how exact they have to be, the bound alone decides.
No kernel may reach another device: no remote copies, remote signals or barrier semaphores. Data moves between devices by JAX's collectives and lax.ppermute only.
A program may use at most 64 MiB of HBM per device.

v0:
```python
import jax
import jax.numpy as jnp
from jax import lax
from jax.sharding import PartitionSpec as P

NNZ = 5


def extended(block, sides, width):
    for axis, dim in sides:
        count = lax.axis_size(axis)
        forward = [(i, i + 1) for i in range(count - 1)]
        backward = [(target, source) for source, target in forward]
        low = lax.ppermute(
            lax.slice_in_dim(block, block.shape[dim] - width, None, axis=dim), axis, forward
        )
        high = lax.ppermute(lax.slice_in_dim(block, 0, width, axis=dim), axis, backward)
        block = jnp.concatenate([low, block, high], axis=dim)
    return block


def apply_pattern(padded, center, neighbours, tile_kinds, tile_table, diagonal):
    count_x, count_y = (center.shape[1], center.shape[2])
    result_sum = diagonal * center
    for entry_index in range(NNZ):
        chosen = jnp.zeros_like(center)
        for neighbour in range(9):
            shifted = padded[
                :,
                neighbour // 3 : neighbour // 3 + count_x,
                neighbour % 3 : neighbour % 3 + count_y,
                :,
            ]
            chosen = chosen + jnp.where(
                (neighbours[entry_index] == neighbour)[None, :, :, None],
                shifted,
                jnp.zeros_like(shifted),
            )
        tile_blocks = tile_table[tile_kinds[entry_index]]
        result_sum = result_sum + jnp.einsum(
            "bxyc,xycd->bxyd", chosen, tile_blocks, precision=lax.Precision.HIGHEST
        )
    return result_sum


def pair_products(left, right):
    return jnp.einsum("nxyt,bxyt->nb", left, right, precision=lax.Precision.HIGHEST)


def solve_lower(lower_factor, matrix):
    return jax.scipy.linalg.solve_triangular(lower_factor, matrix, lower=True)


def shards(prior_basis, previous, neighbours, tile_kinds, stiff_tiles, mass_tiles):
    block_size = previous.shape[0]
    prior_count = prior_basis.shape[0]
    total_rows = (
        prior_basis.shape[1]
        * prior_basis.shape[2]
        * prior_basis.shape[3]
        * lax.axis_size("px")
        * lax.axis_size("py")
    )
    inverse_rows = 1.0 / total_rows
    current = prior_basis[prior_count - block_size :]
    padded_current, padded_previous = (
        extended(current, (("px", 1), ("py", 2)), 1),
        extended(previous, (("px", 1), ("py", 2)), 1),
    )
    residual = apply_pattern(
        padded_current, current, neighbours, tile_kinds, stiff_tiles, 4.0
    ) + apply_pattern(padded_previous, previous, neighbours, tile_kinds, mass_tiles, 1.0)
    coupling = lax.psum(pair_products(prior_basis, residual), ("px", "py")) * inverse_rows
    weighted = residual - jnp.einsum(
        "nb,nxyt->bxyt", coupling, prior_basis, precision=lax.Precision.HIGHEST
    )
    gram = lax.psum(pair_products(weighted, weighted), ("px", "py")) * inverse_rows
    lower_factor = jnp.linalg.cholesky(gram)
    new_block = solve_lower(lower_factor, weighted.reshape(block_size, -1)).reshape(weighted.shape)
    padded_new = extended(new_block, (("px", 1), ("py", 2)), 1)
    stiff_new = apply_pattern(padded_new, new_block, neighbours, tile_kinds, stiff_tiles, 4.0)
    mass_new = apply_pattern(padded_new, new_block, neighbours, tile_kinds, mass_tiles, 1.0)
    prior_stiff, block_stiff, prior_mass, block_mass = lax.psum(
        (
            pair_products(prior_basis, stiff_new),
            pair_products(new_block, stiff_new),
            pair_products(prior_basis, mass_new),
            pair_products(new_block, mass_new),
        ),
        ("px", "py"),
    )
    reduced = (
        jnp.stack(
            [
                jnp.concatenate([prior_stiff, block_stiff], axis=0),
                jnp.concatenate([prior_mass, block_mass], axis=0),
            ]
        )
        * inverse_rows
    )
    return (new_block, coupling, lower_factor.T, reduced)


def solution(mesh):
    placed = (
        P("case", "px", "py", None),
        P("case", "px", "py", None),
        P(None, "px", "py"),
        P(None, "px", "py"),
        P(),
        P(),
    )
    return jax.shard_map(
        shards,
        mesh=mesh,
        in_specs=placed,
        out_specs=(
            P("case", "px", "py", None),
            P("case", None),
            P("case", None),
            P("case", None, None),
        ),
        check_vma=False,
    )
```

profile of v0, /device:TPU:0, one launch (start us, length us, event | category | flops | bytes accessed | tf_op | source)
XLA Modules:
  0.0 271.9 jit_solution(9100911778998125324)
XLA Ops:
  0.6 0.9 fusion.345
  2.2 1.3 collective-permute-start.1
  4.2 6.2 %collective-permute-start = (f32[32,1,4,128]{3,0,2,1:T(8,128)}, f32[32,1,4,128]{3,0,2,1:T(8,128)}, u32[]{:S(2)}, u32[]{:S(2)}) collective-permute-start(f32[32,1,4,128]{3,0,2,1:T(8,128)} %copy.87), channel_id=1, source_target_pairs={{0,4},{4,8},{8,12},{1,5},{5,9},{9,13},{2,6},{6,10},{10,14},{3,7},{... | collective-permute-start | bytes 196616 | tf_op jit(solution)/shard_map/ppermute | solution.py:14
  10.4 0.7 fusion.348
  11.0 3.3 %collective-permute-start.4 = (f32[32,1,4,128]{3,0,2,1:T(8,128)}, f32[32,1,4,128]{3,0,2,1:T(8,128)S(1)}, u32[]{:S(2)}, u32[]{:S(2)}) collective-permute-start(f32[32,1,4,128]{3,0,2,1:T(8,128)} %get-tuple-element.90), channel_id=1, source_target_pairs={{0,4},{4,8},{8,12},{1,5},{5,9},{9,13},{2,6},{6,10},{10,14},{3,7},{... | collective-permute-start | bytes 196616 | tf_op jit(solution)/shard_map/ppermute | solution.py:14
  14.3 1.3 collective-permute-start.5
  15.7 0.7 copy-done.18
  16.9 1.4 gather_fusion
  18.2 1.4 gather_fusion.1
  20.2 1.4 gather_fusion.6
  21.7 1.4 gather_fusion.2
  23.8 1.4 gather_fusion.3
  25.9 1.4 gather_fusion.4
  28.2 0.7 copy-done.19
  28.8 2.3 compare_reduce_fusion.7
  31.5 0.8 pad_maximum_fusion.15
  32.3 1.4 collective-permute-start.2
  33.7 1.3 collective-permute-start.3
  35.1 4.8 %collective-permute-start.6 = (f32[32,4,1,128]{3,0,2,1:T(8,128)S(1)}, f32[32,4,1,128]{3,0,2,1:T(8,128)S(1)}, u32[]{:S(2)}, u32[]{:S(2)}) collective-permute-start(f32[32,4,1,128]{3,0,2,1:T(8,128)S(1)} %get-tuple-element.81), channel_id=1, source_target_pairs={{0,1},{1,2},{2,3},{4,5},{5,6},{6,7},{8,9},{9,10},{10,11},{12,13},{... | collective-permute-start | bytes 196616 | tf_op jit(solution)/shard_map/ppermute | solution.py:14
  39.9 1.3 collective-permute-start.7
  41.2 1.0 maximum_maximum_fusion
  42.2 2.0 collective-permute-done.7
  44.4 1.5 fusion.20
  46.0 0.7 fusion.15
  47.0 1.6 fusion.19
  48.7 1.4 fusion.14
  50.1 1.5 fusion.18
  51.7 0.7 fusion.13
  52.8 1.5 fusion.17
  54.4 0.7 fusion.12
  55.4 1.5 fusion.16
  57.1 0.7 fusion.11
  58.8 61.9 %psum.42 = f32[128,32]{0,1:T(8,128)S(1)} all-reduce(f32[128,32]{0,1:T(8,128)S(1)} %convolution_bitcast_fusion.25), channel_id=1, replica_groups=mesh['case'=2,'px'=4,'py'=4] {'px','py'}, use_global_device_ids=true, to_apply=%region_0.1 | all-reduce | flops 4096 | bytes 32768 | tf_op jit(solution)/shard_map/psum | solution.py:73
  120.6 1.3 convolution_subtract_fusion
  122.5 57.8 %psum.43 = f32[32,32]{0,1:T(8,128)S(1)} all-reduce(f32[32,32]{0,1:T(8,128)S(1)} %convolution_bitcast_fusion.24), channel_id=1, replica_groups=mesh['case'=2,'px'=4,'py'=4] {'px','py'}, use_global_device_ids=true, to_apply=%region_1.2 | all-reduce | flops 1024 | bytes 8192 | tf_op jit(solution)/shard_map/psum | solution.py:77
  180.4 2.9 %cholesky.16 = f32[32,32]{1,0:T(8,128)S(1)} custom-call(f32[32,32]{1,0:T(8,128)S(1)} %fusion.329), custom_call_target="Cholesky" | custom-call | tf_op jit(solution)/shard_map/jit(cholesky)/cholesky | solution.py:78
  184.0 0.7 fusion.330
  184.6 2.4 custom-call.7
  187.4 1.3 collective-permute-start.9
  188.7 4.5 %collective-permute-start.8 = (f32[32,1,4,128]{3,0,2,1:T(8,128)S(1)}, f32[32,1,4,128]{3,0,2,1:T(8,128)S(1)}, u32[]{:S(2)}, u32[]{:S(2)}) collective-permute-start(f32[32,1,4,128]{3,0,2,1:T(8,128)S(1)} %get-tuple-element.87), channel_id=1, source_target_pairs={{0,4},{4,8},{8,12},{1,5},{5,9},{9,13},{2,6},{6,10},{10,14},{3,7},{... | collective-permute-start | bytes 196616 | tf_op jit(solution)/shard_map/ppermute | solution.py:14
  193.6 1.6 collective-permute-done.8
  195.2 0.6 pad_maximum_fusion.12
  195.8 1.3 collective-permute-start.10
  197.1 1.3 collective-permute-start.11
  198.4 0.7 copy.60
  199.2 0.7 copy.61
  202.1 0.9 select_add_fusion.3
  213.1 58.1 %all-reduce = (f32[32,32]{0,1:T(8,128)S(1)}, f32[128,32]{0,1:T(8,128)S(1)}, f32[32,32]{0,1:T(8,128)S(1)}, f32[128,32]{0,1:T(8,128)S(1)}) all-reduce(f32[32,32]{0,1:T(8,128)S(1)} %convolution_bitcast_fusion.20, f32[128,32]{0,1:T(8,128)S(1)} %convolution_bitcast_fusion.21, ...), channel_id=1, replica_groups=mesh['case'=2,'px'=4,'py'=4] {'px','py'}, use_global_device_ids=true, to_apply=%region_7.8 | all-reduce | flops 10240 | bytes 81920 | tf_op jit(solution)/shard_map/psum | solution.py:83
  (270 shorter events, 21.6 us)
Async XLA Ops:
  0.6 16.2 %copy-start = (f32[8,128,128]{2,1,0:T(8,128)S(1)}, f32[8,128,128]{2,1,0:T(8,128)}, u32[]{:S(2)}) copy-start(f32[8,128,128]{2,1,0:T(8,128)} %param.10) | copy-start | bytes 1572868
  2.2 29.2 %collective-permute-start.1 = (f32[32,1,4,128]{3,0,2,1:T(8,128)}, f32[32,1,4,128]{3,0,2,1:T(8,128)}, u32[]{:S(2)}, u32[]{:S(2)}) collective-permute-start(f32[32,1,4,128]{3,0,2,1:T(8,128)} %copy.86), channel_id=1, source_target_pairs={{4,0},{8,4},{12,8},{5,1},{9,5},{13,9},{6,2},{10,6},{14,10},{7,3},{... | collective-permute-start | bytes 196616 | tf_op jit(solution)/shard_map/ppermute | solution.py:17
  4.2 27.3 %collective-permute-start = (f32[32,1,4,128]{3,0,2,1:T(8,128)}, f32[32,1,4,128]{3,0,2,1:T(8,128)}, u32[]{:S(2)}, u32[]{:S(2)}) collective-permute-start(f32[32,1,4,128]{3,0,2,1:T(8,128)} %copy.87), channel_id=1, source_target_pairs={{0,4},{4,8},{8,12},{1,5},{5,9},{9,13},{2,6},{6,10},{10,14},{3,7},{... | collective-permute-start | bytes 196616 | tf_op jit(solution)/shard_map/ppermute | solution.py:14
  11.0 24.0 %collective-permute-start.4 = (f32[32,1,4,128]{3,0,2,1:T(8,128)}, f32[32,1,4,128]{3,0,2,1:T(8,128)S(1)}, u32[]{:S(2)}, u32[]{:S(2)}) collective-permute-start(f32[32,1,4,128]{3,0,2,1:T(8,128)} %get-tuple-element.90), channel_id=1, source_target_pairs={{0,4},{4,8},{8,12},{1,5},{5,9},{9,13},{2,6},{6,10},{10,14},{3,7},{... | collective-permute-start | bytes 196616 | tf_op jit(solution)/shard_map/ppermute | solution.py:14
  14.3 20.7 %collective-permute-start.5 = (f32[32,1,4,128]{3,0,2,1:T(8,128)}, f32[32,1,4,128]{3,0,2,1:T(8,128)S(1)}, u32[]{:S(2)}, u32[]{:S(2)}) collective-permute-start(f32[32,1,4,128]{3,0,2,1:T(8,128)} %get-tuple-element.89), channel_id=1, source_target_pairs={{4,0},{8,4},{12,8},{5,1},{9,5},{13,9},{6,2},{10,6},{14,10},{7,3},{... | collective-permute-start | bytes 196616 | tf_op jit(solution)/shard_map/ppermute | solution.py:17
  31.1 14.8 %copy-start.29 = (pred[2,4]{1,0:T(4,128)(4,1)}, pred[2,4]{1,0:T(4,128)(4,1)S(1)}, u32[]{:S(2)}) copy-start(pred[2,4]{1,0:T(4,128)(4,1)S(1)} %get-tuple-element.107) | copy-start | bytes 28
  31.1 14.8 %copy-start.31 = (pred[2,4]{1,0:T(4,128)(4,1)}, pred[2,4]{1,0:T(4,128)(4,1)S(1)}, u32[]{:S(2)}) copy-start(pred[2,4]{1,0:T(4,128)(4,1)S(1)} %get-tuple-element.108) | copy-start | bytes 28
  31.1 14.8 %copy-start.33 = (pred[2,4]{1,0:T(4,128)(4,1)}, pred[2,4]{1,0:T(4,128)(4,1)S(1)}, u32[]{:S(2)}) copy-start(pred[2,4]{1,0:T(4,128)(4,1)S(1)} %get-tuple-element.109) | copy-start | bytes 28
  31.1 14.8 %copy-start.35 = (pred[2,4]{1,0:T(4,128)(4,1)}, pred[2,4]{1,0:T(4,128)(4,1)S(1)}, u32[]{:S(2)}) copy-start(pred[2,4]{1,0:T(4,128)(4,1)S(1)} %get-tuple-element.110) | copy-start | bytes 28
  31.1 14.8 %copy-start.37 = (pred[2,4]{1,0:T(4,128)(4,1)}, pred[2,4]{1,0:T(4,128)(4,1)S(1)}, u32[]{:S(2)}) copy-start(pred[2,4]{1,0:T(4,128)(4,1)S(1)} %get-tuple-element.113) | copy-start | bytes 28
  31.1 17.5 %copy-start.93 = (pred[2,4]{1,0:T(4,128)(4,1)}, pred[2,4]{1,0:T(4,128)(4,1)S(1)}, u32[]{:S(2)}) copy-start(pred[2,4]{1,0:T(4,128)(4,1)S(1)} %get-tuple-element.95) | copy-start | bytes 28
  31.2 17.5 %copy-start.95 = (pred[2,4]{1,0:T(4,128)(4,1)}, pred[2,4]{1,0:T(4,128)(4,1)S(1)}, u32[]{:S(2)}) copy-start(pred[2,4]{1,0:T(4,128)(4,1)S(1)} %get-tuple-element.96) | copy-start | bytes 28
  31.2 17.5 %copy-start.97 = (pred[2,4]{1,0:T(4,128)(4,1)}, pred[2,4]{1,0:T(4,128)(4,1)S(1)}, u32[]{:S(2)}) copy-start(pred[2,4]{1,0:T(4,128)(4,1)S(1)} %get-tuple-element.97) | copy-start | bytes 28
  31.2 20.5 %copy-start.75 = (pred[2,4]{1,0:T(4,128)(4,1)}, pred[2,4]{1,0:T(4,128)(4,1)S(1)}, u32[]{:S(2)}) copy-start(pred[2,4]{1,0:T(4,128)(4,1)S(1)} %get-tuple-element.32) | copy-start | bytes 28
  31.2 20.5 %copy-start.77 = (pred[2,4]{1,0:T(4,128)(4,1)}, pred[2,4]{1,0:T(4,128)(4,1)S(1)}, u32[]{:S(2)}) copy-start(pred[2,4]{1,0:T(4,128)(4,1)S(1)} %get-tuple-element.33) | copy-start | bytes 28
  31.2 20.5 %copy-start.79 = (pred[2,4]{1,0:T(4,128)(4,1)}, pred[2,4]{1,0:T(4,128)(4,1)S(1)}, u32[]{:S(2)}) copy-start(pred[2,4]{1,0:T(4,128)(4,1)S(1)} %get-tuple-element.34) | copy-start | bytes 28
  31.2 20.5 %copy-start.81 = (pred[2,4]{1,0:T(4,128)(4,1)}, pred[2,4]{1,0:T(4,128)(4,1)S(1)}, u32[]{:S(2)}) copy-start(pred[2,4]{1,0:T(4,128)(4,1)S(1)} %get-tuple-element.35) | copy-start | bytes 28
  31.2 20.5 %copy-start.83 = (pred[2,4]{1,0:T(4,128)(4,1)}, pred[2,4]{1,0:T(4,128)(4,1)S(1)}, u32[]{:S(2)}) copy-start(pred[2,4]{1,0:T(4,128)(4,1)S(1)} %get-tuple-element.36) | copy-start | bytes 28
  31.2 20.5 %copy-start.85 = (pred[2,4]{1,0:T(4,128)(4,1)}, pred[2,4]{1,0:T(4,128)(4,1)S(1)}, u32[]{:S(2)}) copy-start(pred[2,4]{1,0:T(4,128)(4,1)S(1)} %get-tuple-element.37) | copy-start | bytes 28
  31.2 20.5 %copy-start.87 = (pred[2,4]{1,0:T(4,128)(4,1)}, pred[2,4]{1,0:T(4,128)(4,1)S(1)}, u32[]{:S(2)}) copy-start(pred[2,4]{1,0:T(4,128)(4,1)S(1)} %get-tuple-element.93) | copy-start | bytes 28
  31.2 20.5 %copy-start.89 = (pred[2,4]{1,0:T(4,128)(4,1)}, pred[2,4]{1,0:T(4,128)(4,1)S(1)}, u32[]{:S(2)}) copy-start(pred[2,4]{1,0:T(4,128)(4,1)S(1)} %get-tuple-element.94) | copy-start | bytes 28
  31.3 20.5 %copy-start.91 = (pred[2,4]{1,0:T(4,128)(4,1)}, pred[2,4]{1,0:T(4,128)(4,1)S(1)}, u32[]{:S(2)}) copy-start(pred[2,4]{1,0:T(4,128)(4,1)S(1)} %get-tuple-element.115) | copy-start | bytes 28
  31.3 23.0 %copy-start.57 = (pred[2,4]{1,0:T(4,128)(4,1)}, pred[2,4]{1,0:T(4,128)(4,1)S(1)}, u32[]{:S(2)}) copy-start(pred[2,4]{1,0:T(4,128)(4,1)S(1)} %get-tuple-element.38) | copy-start | bytes 28
  31.3 23.0 %copy-start.59 = (pred[2,4]{1,0:T(4,128)(4,1)}, pred[2,4]{1,0:T(4,128)(4,1)S(1)}, u32[]{:S(2)}) copy-start(pred[2,4]{1,0:T(4,128)(4,1)S(1)} %get-tuple-element.39) | copy-start | bytes 28
  31.3 23.0 %copy-start.61 = (pred[2,4]{1,0:T(4,128)(4,1)}, pred[2,4]{1,0:T(4,128)(4,1)S(1)}, u32[]{:S(2)}) copy-start(pred[2,4]{1,0:T(4,128)(4,1)S(1)} %get-tuple-element.40) | copy-start | bytes 28
  31.3 23.0 %copy-start.63 = (pred[2,4]{1,0:T(4,128)(4,1)}, pred[2,4]{1,0:T(4,128)(4,1)S(1)}, u32[]{:S(2)}) copy-start(pred[2,4]{1,0:T(4,128)(4,1)S(1)} %get-tuple-element.41) | copy-start | bytes 28
  31.3 23.0 %copy-start.65 = (pred[2,4]{1,0:T(4,128)(4,1)}, pred[2,4]{1,0:T(4,128)(4,1)S(1)}, u32[]{:S(2)}) copy-start(pred[2,4]{1,0:T(4,128)(4,1)S(1)} %get-tuple-element.42) | copy-start | bytes 28
  31.3 23.0 %copy-start.67 = (pred[2,4]{1,0:T(4,128)(4,1)}, pred[2,4]{1,0:T(4,128)(4,1)S(1)}, u32[]{:S(2)}) copy-start(pred[2,4]{1,0:T(4,128)(4,1)S(1)} %get-tuple-element.43) | copy-start | bytes 28
  31.3 23.0 %copy-start.69 = (pred[2,4]{1,0:T(4,128)(4,1)}, pred[2,4]{1,0:T(4,128)(4,1)S(1)}, u32[]{:S(2)}) copy-start(pred[2,4]{1,0:T(4,128)(4,1)S(1)} %get-tuple-element.44) | copy-start | bytes 28
  31.3 23.0 %copy-start.71 = (pred[2,4]{1,0:T(4,128)(4,1)}, pred[2,4]{1,0:T(4,128)(4,1)S(1)}, u32[]{:S(2)}) copy-start(pred[2,4]{1,0:T(4,128)(4,1)S(1)} %get-tuple-element.45) | copy-start | bytes 28
  31.3 23.0 %copy-start.73 = (pred[2,4]{1,0:T(4,128)(4,1)}, pred[2,4]{1,0:T(4,128)(4,1)S(1)}, u32[]{:S(2)}) copy-start(pred[2,4]{1,0:T(4,128)(4,1)S(1)} %get-tuple-element.112) | copy-start | bytes 28
  31.4 25.6 %copy-start.39 = (pred[2,4]{1,0:T(4,128)(4,1)}, pred[2,4]{1,0:T(4,128)(4,1)S(1)}, u32[]{:S(2)}) copy-start(pred[2,4]{1,0:T(4,128)(4,1)S(1)} %get-tuple-element.31) | copy-start | bytes 28
  31.4 25.6 %copy-start.41 = (pred[2,4]{1,0:T(4,128)(4,1)}, pred[2,4]{1,0:T(4,128)(4,1)S(1)}, u32[]{:S(2)}) copy-start(pred[2,4]{1,0:T(4,128)(4,1)S(1)} %get-tuple-element.46) | copy-start | bytes 28
  31.4 25.6 %copy-start.43 = (pred[2,4]{1,0:T(4,128)(4,1)}, pred[2,4]{1,0:T(4,128)(4,1)S(1)}, u32[]{:S(2)}) copy-start(pred[2,4]{1,0:T(4,128)(4,1)S(1)} %get-tuple-element.47) | copy-start | bytes 28
  31.4 25.6 %copy-start.45 = (pred[2,4]{1,0:T(4,128)(4,1)}, pred[2,4]{1,0:T(4,128)(4,1)S(1)}, u32[]{:S(2)}) copy-start(pred[2,4]{1,0:T(4,128)(4,1)S(1)} %get-tuple-element.48) | copy-start | bytes 28
  31.4 25.6 %copy-start.47 = (pred[2,4]{1,0:T(4,128)(4,1)}, pred[2,4]{1,0:T(4,128)(4,1)S(1)}, u32[]{:S(2)}) copy-start(pred[2,4]{1,0:T(4,128)(4,1)S(1)} %get-tuple-element.49) | copy-start | bytes 28
  31.4 25.6 %copy-start.49 = (pred[2,4]{1,0:T(4,128)(4,1)}, pred[2,4]{1,0:T(4,128)(4,1)S(1)}, u32[]{:S(2)}) copy-start(pred[2,4]{1,0:T(4,128)(4,1)S(1)} %get-tuple-element.111) | copy-start | bytes 28
  31.4 25.6 %copy-start.51 = (pred[2,4]{1,0:T(4,128)(4,1)}, pred[2,4]{1,0:T(4,128)(4,1)S(1)}, u32[]{:S(2)}) copy-start(pred[2,4]{1,0:T(4,128)(4,1)S(1)} %get-tuple-element.116) | copy-start | bytes 28
  31.4 25.6 %copy-start.53 = (pred[2,4]{1,0:T(4,128)(4,1)}, pred[2,4]{1,0:T(4,128)(4,1)S(1)}, u32[]{:S(2)}) copy-start(pred[2,4]{1,0:T(4,128)(4,1)S(1)} %get-tuple-element.117) | copy-start | bytes 28
  31.4 25.6 %copy-start.55 = (pred[2,4]{1,0:T(4,128)(4,1)}, pred[2,4]{1,0:T(4,128)(4,1)S(1)}, u32[]{:S(2)}) copy-start(pred[2,4]{1,0:T(4,128)(4,1)S(1)} %get-tuple-element.118) | copy-start | bytes 28
  32.3 8.9 %collective-permute-start.2 = (f32[32,4,1,128]{3,0,2,1:T(8,128)S(1)}, f32[32,4,1,128]{3,0,2,1:T(8,128)S(1)}, u32[]{:S(2)}, u32[]{:S(2)}) collective-permute-start(f32[32,4,1,128]{3,0,2,1:T(8,128)S(1)} %get-tuple-element.85), channel_id=1, source_target_pairs={{0,1},{1,2},{2,3},{4,5},{5,6},{6,7},{8,9},{9,10},{10,11},{12,13},{... | collective-permute-start | bytes 196616 | tf_op jit(solution)/shard_map/ppermute | solution.py:14
  33.7 7.5 %collective-permute-start.3 = (f32[32,4,1,128]{3,0,2,1:T(8,128)S(1)}, f32[32,4,1,128]{3,0,2,1:T(8,128)S(1)}, u32[]{:S(2)}, u32[]{:S(2)}) collective-permute-start(f32[32,4,1,128]{3,0,2,1:T(8,128)S(1)} %get-tuple-element.86), channel_id=1, source_target_pairs={{1,0},{2,1},{3,2},{5,4},{6,5},{7,6},{9,8},{10,9},{11,10},{13,12},{... | collective-permute-start | bytes 196616 | tf_op jit(solution)/shard_map/ppermute | solution.py:17
  35.1 7.1 %collective-permute-start.6 = (f32[32,4,1,128]{3,0,2,1:T(8,128)S(1)}, f32[32,4,1,128]{3,0,2,1:T(8,128)S(1)}, u32[]{:S(2)}, u32[]{:S(2)}) collective-permute-start(f32[32,4,1,128]{3,0,2,1:T(8,128)S(1)} %get-tuple-element.81), channel_id=1, source_target_pairs={{0,1},{1,2},{2,3},{4,5},{5,6},{6,7},{8,9},{9,10},{10,11},{12,13},{... | collective-permute-start | bytes 196616 | tf_op jit(solution)/shard_map/ppermute | solution.py:14
  39.9 4.4 %collective-permute-start.7 = (f32[32,4,1,128]{3,0,2,1:T(8,128)S(1)}, f32[32,4,1,128]{3,0,2,1:T(8,128)S(1)}, u32[]{:S(2)}, u32[]{:S(2)}) collective-permute-start(f32[32,4,1,128]{3,0,2,1:T(8,128)S(1)} %get-tuple-element.82), channel_id=1, source_target_pairs={{1,0},{2,1},{3,2},{5,4},{6,5},{7,6},{9,8},{10,9},{11,10},{13,12},{... | collective-permute-start | bytes 196616 | tf_op jit(solution)/shard_map/ppermute | solution.py:17
  187.4 6.2 %collective-permute-start.9 = (f32[32,1,4,128]{3,0,2,1:T(8,128)S(1)}, f32[32,1,4,128]{3,0,2,1:T(8,128)S(1)}, u32[]{:S(2)}, u32[]{:S(2)}) collective-permute-start(f32[32,1,4,128]{3,0,2,1:T(8,128)S(1)} %get-tuple-element.88), channel_id=1, source_target_pairs={{4,0},{8,4},{12,8},{5,1},{9,5},{13,9},{6,2},{10,6},{14,10},{7,3},{... | collective-permute-start | bytes 196616 | tf_op jit(solution)/shard_map/ppermute | solution.py:17
  188.7 6.4 %collective-permute-start.8 = (f32[32,1,4,128]{3,0,2,1:T(8,128)S(1)}, f32[32,1,4,128]{3,0,2,1:T(8,128)S(1)}, u32[]{:S(2)}, u32[]{:S(2)}) collective-permute-start(f32[32,1,4,128]{3,0,2,1:T(8,128)S(1)} %get-tuple-element.87), channel_id=1, source_target_pairs={{0,4},{4,8},{8,12},{1,5},{5,9},{9,13},{2,6},{6,10},{10,14},{3,7},{... | collective-permute-start | bytes 196616 | tf_op jit(solution)/shard_map/ppermute | solution.py:14
  195.8 4.0 %collective-permute-start.10 = (f32[32,4,1,128]{3,0,2,1:T(8,128)}, f32[32,4,1,128]{3,0,2,1:T(8,128)S(1)}, u32[]{:S(2)}, u32[]{:S(2)}) collective-permute-start(f32[32,4,1,128]{3,0,2,1:T(8,128)} %get-tuple-element.76), channel_id=1, source_target_pairs={{0,1},{1,2},{2,3},{4,5},{5,6},{6,7},{8,9},{9,10},{10,11},{12,13},{... | collective-permute-start | bytes 196616 | tf_op jit(solution)/shard_map/ppermute | solution.py:14
  197.1 3.4 %collective-permute-start.11 = (f32[32,4,1,128]{3,0,2,1:T(8,128)}, f32[32,4,1,128]{3,0,2,1:T(8,128)S(1)}, u32[]{:S(2)}, u32[]{:S(2)}) collective-permute-start(f32[32,4,1,128]{3,0,2,1:T(8,128)} %get-tuple-element.77), channel_id=1, source_target_pairs={{1,0},{2,1},{3,2},{5,4},{6,5},{7,6},{9,8},{10,9},{11,10},{13,12},{... | collective-permute-start | bytes 196616 | tf_op jit(solution)/shard_map/ppermute | solution.py:17
  (64 other events, 117.8 us)
where the time goes:
time: 273 us; the launch traced here: 272 us
  blocking collectives  178 us (65%)
  starting transfers between devices  29.2 us (11%)
  local copies, waits for them, and re-layouts  22.7 us (8%)
  matrix products  21.5 us (8%)
  other arithmetic  13.8 us (5%)
  waiting for transfers between devices  4.58 us (2%)
    psum x1, blocking collectives, shards(): lax.psum(pair_products(prior_basis, residual), ('px', 'py')) * inverse_rows  61.9 us
    psum x1, blocking collectives, shards(): lax.psum((pair_products(prior_basis, stiff_new), pair_products(new_block,...  58.1 us
    psum x1, blocking collectives, shards(): lax.psum(pair_products(weighted, weighted), ('px', 'py')) * inverse_rows  57.8 us
    ppermute x6, starting transfers between devices, extended(): lax.ppermute(lax.slice_in_dim(block, block.shape[dim] - width, None, axis...  21.5 us
    dot_general x20, matrix products, apply_pattern(): jnp.einsum('bxyc,xycd->bxyd', chosen, tile_blocks, precision=lax.Precisio...  17.2 us
    gather x10, local copies, waits for them, and re-layouts, apply_pattern(): tile_blocks = tile_table[tile_kinds[entry_index]]  10.6 us
    unnamed x206, local copies, waits for them, and re-layouts  9.09 us
    ppermute x6, starting transfers between devices, extended(): lax.ppermute(lax.slice_in_dim(block, 0, width, axis=dim), axis, backward)  7.74 us
  transfers between devices with their start and end apart: 12, of which 4 were waited for; matrix products, arithmetic and copies ran while one was open for 7% of the time, Pallas kernels for 0%

commit v1 on v0

v1 whole, which is shorter than its diff:
```python
import jax
import jax.numpy as jnp
from jax import lax
from jax.sharding import PartitionSpec as P

NNZ = 5
HIGHEST = lax.Precision.HIGHEST


def extended(block, sides, width):
    for axis, dim in sides:
        count = lax.axis_size(axis)
        forward = [(i, i + 1) for i in range(count - 1)]
        backward = [(target, source) for source, target in forward]
        low = lax.ppermute(
            lax.slice_in_dim(block, block.shape[dim] - width, None, axis=dim), axis, forward
        )
        high = lax.ppermute(lax.slice_in_dim(block, 0, width, axis=dim), axis, backward)
        block = jnp.concatenate([low, block, high], axis=dim)
    return block


def chosen_tiles(padded, center, neighbours, entry_index):
    count_x, count_y = (center.shape[1], center.shape[2])
    chosen = jnp.zeros_like(center)
    for neighbour in range(9):
        shifted = padded[
            :,
            neighbour // 3 : neighbour // 3 + count_x,
            neighbour % 3 : neighbour % 3 + count_y,
            :,
        ]
        chosen = chosen + jnp.where(
            (neighbours[entry_index] == neighbour)[None, :, :, None],
            shifted,
            jnp.zeros_like(shifted),
        )
    return chosen


def tile_products(chosen, tile_blocks):
    return jnp.einsum("bxyc,xycd->bxyd", chosen, tile_blocks, precision=HIGHEST)


def pair_products(left, right):
    return jnp.einsum("nxyt,bxyt->nb", left, right, precision=HIGHEST)


def butterfly_sum(value):
    for axis in ("py", "px"):
        count = lax.axis_size(axis)
        step = 1
        while step < count:
            swap = [(i, i ^ step) for i in range(count)]
            value = value + lax.ppermute(value, axis, swap)
            step *= 2
    return value


def exchange_sum(value):
    axes = ("px", "py")
    count = lax.axis_size(axes)
    copies = jnp.broadcast_to(value[None], (count,) + value.shape)
    return jnp.sum(lax.all_to_all(copies, axes, 0, 0), axis=0)


def shards(prior_basis, previous, neighbours, tile_kinds, stiff_tiles, mass_tiles):
    block = previous.shape[0]
    prior = prior_basis.shape[0]
    total_rows = (
        prior_basis.shape[1]
        * prior_basis.shape[2]
        * prior_basis.shape[3]
        * lax.axis_size("px")
        * lax.axis_size("py")
    )
    inverse_rows = 1.0 / total_rows
    both = jnp.concatenate([prior_basis[prior - block :], previous], axis=0)
    padded = extended(both, (("px", 1), ("py", 2)), 1)
    residual = 4.0 * both[:block] + both[block:]
    stiff_blocks = [stiff_tiles[tile_kinds[k]] for k in range(NNZ)]
    mass_blocks = [mass_tiles[tile_kinds[k]] for k in range(NNZ)]
    for k in range(NNZ):
        chosen = chosen_tiles(padded, both, neighbours, k)
        residual = residual + tile_products(chosen[:block], stiff_blocks[k])
        residual = residual + tile_products(chosen[block:], mass_blocks[k])
    coupling = exchange_sum(pair_products(prior_basis, residual)) * inverse_rows
    weighted = residual - jnp.einsum("nb,nxyt->bxyt", coupling, prior_basis, precision=HIGHEST)
    padded = extended(weighted, (("px", 1), ("py", 2)), 1)
    stiff_weighted = 4.0 * weighted
    mass_weighted = weighted
    for k in range(NNZ):
        chosen = chosen_tiles(padded, weighted, neighbours, k)
        stiff_weighted = stiff_weighted + tile_products(chosen, stiff_blocks[k])
        mass_weighted = mass_weighted + tile_products(chosen, mass_blocks[k])
    left = jnp.concatenate([prior_basis, weighted], axis=0)
    right = jnp.concatenate([stiff_weighted, mass_weighted, weighted], axis=0)
    sums = butterfly_sum(pair_products(left, right)) * inverse_rows
    gram = sums[prior:, 2 * block :]
    lower = jnp.linalg.cholesky(gram)
    inverse = jax.scipy.linalg.solve_triangular(
        lower, jnp.eye(block, dtype=jnp.float32), lower=True
    )
    new_block = jnp.einsum("ab,bxyt->axyt", inverse, weighted, precision=HIGHEST)
    rows = jnp.concatenate(
        [sums[:prior], jnp.dot(inverse, sums[prior:], precision=HIGHEST)], axis=0
    )
    rows = rows[:, : 2 * block].reshape(-1, 2, block)
    reduced = jnp.einsum("nmb,ab->mna", rows, inverse, precision=HIGHEST)
    return (new_block, coupling, lower.T, reduced)


def solution(mesh):
    placed = (
        P("case", "px", "py", None),
        P("case", "px", "py", None),
        P(None, "px", "py"),
        P(None, "px", "py"),
        P(),
        P(),
    )
    return jax.shard_map(
        shards,
        mesh=mesh,
        in_specs=placed,
        out_specs=(
            P("case", "px", "py", None),
            P("case", None),
            P("case", None),
            P("case", None, None),
        ),
        check_vma=False,
    )
```

time: 273 us -> 123 us (0.45)
  blocking collectives: 178 us -> 17.7 us
  waiting for transfers between devices: 4.58 us -> 27.2 us
  starting transfers between devices: 29.2 us -> 20.1 us
  matrix products: 21.5 us -> 15.3 us
  local copies, waits for them, and re-layouts: 22.7 us -> 25.7 us
    psum x3 -> x0, blocking collectives: 178 us -> none  [the longest x1 61.9 us: shards(): lax.psum(pair_products(prior_basis, residual), ('px', 'py')) * inverse_rows]
    all_to_all x0 -> x1, blocking collectives: none -> 17.7 us  [exchange_sum(): return jnp.sum(lax.all_to_all(copies, axes, 0, 0), axis=0)]
    ppermute x0 -> x4, waiting for transfers between devices: none -> 14.8 us  [butterfly_sum(): value = value + lax.ppermute(value, axis, swap)]
    ppermute x6 -> x4, starting transfers between devices: 21.5 us -> 9.7 us  [extended(): lax.ppermute(lax.slice_in_dim(block, block.shape[dim] - width, None, axis...]
    ppermute x6 -> x4, waiting for transfers between devices: 2.98 us -> 10.9 us  [extended(): lax.ppermute(lax.slice_in_dim(block, 0, width, axis=dim), axis, backward)]
    dot_general x27 -> x26, matrix products: 21.2 us -> 15.1 us  [the longest x20 12 us: tile_products(): return jnp.einsum('bxyc,xycd->bxyd', chosen, tile_blocks, precision=HIGHEST)]
    ppermute x0 -> x4, starting transfers between devices: none -> 5.1 us  [butterfly_sum(): value = value + lax.ppermute(value, axis, swap)]
    unnamed x206 -> x208, local copies, waits for them, and re-layouts: 9.09 us -> 12.8 us
  transfers between devices with their start and end apart: 12 -> 12, of which waited for: 4 -> 9; matrix products, arithmetic and copies ran while one was open for 7% -> 12% of each run, Pallas kernels for 0% -> 0%
where the time goes in v1:
time: 123 us; the launch traced here: 122 us
  waiting for transfers between devices  27.2 us (22%)
  local copies, waits for them, and re-layouts  25.7 us (21%)
  starting transfers between devices  20.1 us (16%)
  blocking collectives  17.7 us (14%)
  matrix products  15.3 us (12%)
  other arithmetic  13.4 us (11%)
  between operations  2.13 us (2%)
    all_to_all x1, blocking collectives, exchange_sum(): return jnp.sum(lax.all_to_all(copies, axes, 0, 0), axis=0)  17.7 us
    ppermute x4, waiting for transfers between devices, butterfly_sum(): value = value + lax.ppermute(value, axis, swap)  14.8 us
    unnamed x208, local copies, waits for them, and re-layouts  12.8 us
    dot_general x20, matrix products, tile_products(): return jnp.einsum('bxyc,xycd->bxyd', chosen, tile_blocks, precision=HIGHEST)  12 us
    ppermute x4, waiting for transfers between devices, extended(): lax.ppermute(lax.slice_in_dim(block, 0, width, axis=dim), axis, backward)  10.9 us
    ppermute x4, starting transfers between devices, extended(): lax.ppermute(lax.slice_in_dim(block, block.shape[dim] - width, None, axis...  9.7 us
    gather x5, local copies, waits for them, and re-layouts, shards(): stiff_blocks = [stiff_tiles[tile_kinds[k]] for k in range(NNZ)]  6.11 us
    ppermute x4, starting transfers between devices, extended(): lax.ppermute(lax.slice_in_dim(block, 0, width, axis=dim), axis, backward)  5.35 us
  transfers between devices with their start and end apart: 12, of which 9 were waited for; matrix products, arithmetic and copies ran while one was open for 12% of the time, Pallas kernels for 0%

profile of v1, /device:TPU:0, one launch (start us, length us, event | category | flops | bytes accessed | tf_op | source)
XLA Modules:
  0.0 121.6 jit_solution(3890718311840461735)
XLA Ops:
  0.6 1.2 copy.41
  1.9 1.0 copy-done.20
  3.0 4.9 %collective-permute-start = (f32[64,1,4,128]{3,0,2,1:T(8,128)S(1)}, f32[64,1,4,128]{3,0,2,1:T(8,128)S(1)}, u32[]{:S(2)}, u32[]{:S(2)}) collective-permute-start(f32[64,1,4,128]{3,0,2,1:T(8,128)S(1)} %get-tuple-element.74), channel_id=1, source_target_pairs={{0,4},{4,8},{8,12},{1,5},{5,9},{9,13},{2,6},{6,10},{10,14},{3,7},{... | collective-permute-start | bytes 393224 | tf_op jit(solution)/shard_map/ppermute | solution.py:15
  7.9 1.3 %collective-permute-start.1 = (f32[64,1,4,128]{3,0,2,1:T(8,128)S(1)}, f32[64,1,4,128]{3,0,2,1:T(8,128)S(1)}, u32[]{:S(2)}, u32[]{:S(2)}) collective-permute-start(f32[64,1,4,128]{3,0,2,1:T(8,128)S(1)} %get-tuple-element.75), channel_id=1, source_target_pairs={{4,0},{8,4},{12,8},{5,1},{9,5},{13,9},{6,2},{10,6},{14,10},{7,3},{... | collective-permute-start | bytes 393224 | tf_op jit(solution)/shard_map/ppermute | solution.py:18
  10.0 0.6 collective-permute-done
  10.7 4.1 %collective-permute-done.1 = f32[64,1,4,128]{3,0,2,1:T(8,128)S(1)} collective-permute-done((f32[64,1,4,128]{3,0,2,1:T(8,128)S(1)}, f32[64,1,4,128]{3,0,2,1:T(8,128)S(1)}, u32[]{:S(2)}, u32[]{:S(2)}) %collective-permute-start.1) | collective-permute-done | bytes 131104 | tf_op jit(solution)/shard_map/ppermute | solution.py:18
  14.8 0.7 pad_maximum_fusion.12
  15.5 1.3 %collective-permute-start.2 = (f32[64,4,1,128]{3,0,2,1:T(8,128)}, f32[64,4,1,128]{3,0,2,1:T(8,128)S(1)}, u32[]{:S(2)}, u32[]{:S(2)}) collective-permute-start(f32[64,4,1,128]{3,0,2,1:T(8,128)} %get-tuple-element.68), channel_id=1, source_target_pairs={{0,1},{1,2},{2,3},{4,5},{5,6},{6,7},{8,9},{9,10},{10,11},{12,13},{... | collective-permute-start | bytes 393224 | tf_op jit(solution)/shard_map/ppermute | solution.py:15
  16.8 1.3 %collective-permute-start.3 = (f32[64,4,1,128]{3,0,2,1:T(8,128)}, f32[64,4,1,128]{3,0,2,1:T(8,128)S(1)}, u32[]{:S(2)}, u32[]{:S(2)}) collective-permute-start(f32[64,4,1,128]{3,0,2,1:T(8,128)} %get-tuple-element.69), channel_id=1, source_target_pairs={{1,0},{2,1},{3,2},{5,4},{6,5},{7,6},{9,8},{10,9},{11,10},{13,12},{... | collective-permute-start | bytes 393224 | tf_op jit(solution)/shard_map/ppermute | solution.py:18
  18.1 1.4 %gather_fusion = f32[8,128,128]{2,1,0:T(8,128)} fusion(f32[8,128,128]{2,1,0:T(8,128)S(1)} %copy-done, s32[1024]{0:T(1024)S(1)} %pad_clamp_fusion.4), kind=kCustom, calls=%fused_computation | custom fusion | bytes 1048608 | tf_op jit(solution)/shard_map/gather | solution.py:81
  19.5 1.4 %gather_fusion.1 = f32[8,128,128]{2,1,0:T(8,128)} fusion(f32[8,128,128]{2,1,0:T(8,128)S(1)} %copy-done.1, s32[1024]{0:T(1024)S(1)} %pad_clamp_fusion.4), kind=kCustom, calls=%fused_computation.1 | custom fusion | bytes 1048608 | tf_op jit(solution)/shard_map/gather | solution.py:82
  20.9 1.4 %gather_fusion.2 = f32[8,128,128]{2,1,0:T(8,128)} fusion(f32[8,128,128]{2,1,0:T(8,128)S(1)} %copy-done, s32[1024]{0:T(1024)S(1)} %pad_clamp_fusion.3), kind=kCustom, calls=%fused_computation.2 | custom fusion | bytes 1048608 | tf_op jit(solution)/shard_map/gather | solution.py:81
  22.3 1.4 %gather_fusion.3 = f32[8,128,128]{2,1,0:T(8,128)} fusion(f32[8,128,128]{2,1,0:T(8,128)S(1)} %copy-done.1, s32[1024]{0:T(1024)S(1)} %pad_clamp_fusion.3), kind=kCustom, calls=%fused_computation.3 | custom fusion | bytes 1048608 | tf_op jit(solution)/shard_map/gather | solution.py:82
  23.7 1.4 %gather_fusion.4 = f32[8,128,128]{2,1,0:T(8,128)} fusion(f32[8,128,128]{2,1,0:T(8,128)S(1)} %copy-done, s32[1024]{0:T(1024)S(1)} %pad_clamp_fusion.2), kind=kCustom, calls=%fused_computation.4 | custom fusion | bytes 1048608 | tf_op jit(solution)/shard_map/gather | solution.py:81
  25.1 1.4 %gather_fusion.5 = f32[8,128,128]{2,1,0:T(8,128)} fusion(f32[8,128,128]{2,1,0:T(8,128)S(1)} %copy-done.1, s32[1024]{0:T(1024)S(1)} %pad_clamp_fusion.2), kind=kCustom, calls=%fused_computation.5 | custom fusion | bytes 1048608 | tf_op jit(solution)/shard_map/gather | solution.py:82
  26.4 1.4 %gather_fusion.6 = f32[8,128,128]{2,1,0:T(8,128)} fusion(f32[8,128,128]{2,1,0:T(8,128)S(1)} %copy-done, s32[1024]{0:T(1024)S(1)} %pad_clamp_fusion.1), kind=kCustom, calls=%fused_computation.6 | custom fusion | bytes 1048608 | tf_op jit(solution)/shard_map/gather | solution.py:81
  29.7 2.1 %compare_reduce_fusion.7 = (pred[2,4]{1,0:T(4,128)(4,1)S(1)}, pred[2,4]{1,0:T(4,128)(4,1)S(1)}, pred[2,4]{1,0:T(4,128)(4,1)S(1)}, pred[2,4]{1,0:T(4,128)(4,1)S(1...) fusion(s32[5,2,4]{0,2,1:T(4,128)S(1)} %copy-done.22), kind=kLoop, calls=%fused_computation.142 | loop fusion | flops 360 | bytes 520 | tf_op jit(solution)/shard_map/eq | solution.py:34
  32.5 1.0 select_add_fusion.4
  33.5 1.5 %fusion.19 = f32[32,2,4,128]{3,0,2,1:T(8,128)S(1)} fusion(f32[2,4,128,128]{3,2,1,0:T(8,128)S(1)} %bitcast.199, f32[64,2,4,128]{3,0,2,1:T(8,128)S(1)} %select_add_fusion.4, f32[128,2,4,128]{3,0,2,1:T(8,128)} %copy-done.17, f32[32,2,4,128]{3,2,1,0:T(4,128)S(1)} %copy-done.20), kind=kOutput, calls=%fused_computation.50 | convolution fusion | flops 50429952 | bytes 1048576 | tf_op jit(solution)/shard_map/bxyc,xycd->bxyd/dot_general | solution.py:42
  36.0 0.8 copy-done.10
  38.3 0.8 copy-done.6
  40.5 0.8 copy-done.2
  45.0 17.7 %all_to_all.5 = f32[16,128,32]{1,2,0:T(8,128)S(1)} all-to-all(f32[16,128,32]{1,2,0:T(8,128)S(1)} %broadcast_in_dim.609), channel_id=1, replica_groups=mesh['case'=2,'px'=4,'py'=4] {'px','py'}, dimensions={0} | all-to-all | bytes 524288 | tf_op jit(solution)/shard_map/all_to_all | solution.py:64
  63.4 1.9 %collective-permute-start.4 = (f32[32,1,4,128]{3,0,2,1:T(8,128)S(1)}, f32[32,1,4,128]{3,0,2,1:T(8,128)S(1)}, u32[]{:S(2)}, u32[]{:S(2)}) collective-permute-start(f32[32,1,4,128]{3,0,2,1:T(8,128)S(1)} %get-tuple-element.76), channel_id=1, source_target_pairs={{0,4},{4,8},{8,12},{1,5},{5,9},{9,13},{2,6},{6,10},{10,14},{3,7},{... | collective-permute-start | bytes 196616 | tf_op jit(solution)/shard_map/ppermute | solution.py:15
  65.3 1.3 %collective-permute-start.5 = (f32[32,1,4,128]{3,0,2,1:T(8,128)S(1)}, f32[32,1,4,128]{3,0,2,1:T(8,128)S(1)}, u32[]{:S(2)}, u32[]{:S(2)}) collective-permute-start(f32[32,1,4,128]{3,0,2,1:T(8,128)S(1)} %get-tuple-element.77), channel_id=1, source_target_pairs={{4,0},{8,4},{12,8},{5,1},{9,5},{13,9},{6,2},{10,6},{14,10},{7,3},{... | collective-permute-start | bytes 196616 | tf_op jit(solution)/shard_map/ppermute | solution.py:18
  66.6 0.9 collective-permute-done.4
  67.5 4.1 %collective-permute-done.5 = f32[32,1,4,128]{3,0,2,1:T(8,128)S(1)} collective-permute-done((f32[32,1,4,128]{3,0,2,1:T(8,128)S(1)}, f32[32,1,4,128]{3,0,2,1:T(8,128)S(1)}, u32[]{:S(2)}, u32[]{:S(2)}) %collective-permute-start.5) | collective-permute-done | bytes 65568 | tf_op jit(solution)/shard_map/ppermute | solution.py:18
  71.6 1.5 %collective-permute-start.6 = (f32[32,4,1,128]{3,0,2,1:T(8,128)S(1)}, f32[32,4,1,128]{3,0,2,1:T(8,128)S(1)}, u32[]{:S(2)}, u32[]{:S(2)}) collective-permute-start(f32[32,4,1,128]{3,0,2,1:T(8,128)S(1)} %get-tuple-element.72), channel_id=1, source_target_pairs={{0,1},{1,2},{2,3},{4,5},{5,6},{6,7},{8,9},{9,10},{10,11},{12,13},{... | collective-permute-start | bytes 196616 | tf_op jit(solution)/shard_map/ppermute | solution.py:15
  73.2 1.5 %collective-permute-start.7 = (f32[32,4,1,128]{3,0,2,1:T(8,128)S(1)}, f32[32,4,1,128]{3,0,2,1:T(8,128)S(1)}, u32[]{:S(2)}, u32[]{:S(2)}) collective-permute-start(f32[32,4,1,128]{3,0,2,1:T(8,128)S(1)} %get-tuple-element.73), channel_id=1, source_target_pairs={{1,0},{2,1},{3,2},{5,4},{6,5},{7,6},{9,8},{10,9},{11,10},{13,12},{... | collective-permute-start | bytes 196616 | tf_op jit(solution)/shard_map/ppermute | solution.py:18
  74.7 2.6 %collective-permute-done.7 = f32[32,4,1,128]{3,0,2,1:T(8,128)S(1)} collective-permute-done((f32[32,4,1,128]{3,0,2,1:T(8,128)S(1)}, f32[32,4,1,128]{3,0,2,1:T(8,128)S(1)}, u32[]{:S(2)}, u32[]{:S(2)}) %collective-permute-start.7) | collective-permute-done | bytes 65568 | tf_op jit(solution)/shard_map/ppermute | solution.py:18
  78.1 0.9 select_add_fusion.9
  81.1 0.9 copy-done.11
  83.9 0.9 copy-done.7
  86.7 0.9 copy-done.3
  90.6 0.8 convolution_bitcast_fusion.20
  91.4 3.0 %collective-permute-start.8 = (f32[160,96]{0,1:T(8,128)S(1)}, f32[160,96]{0,1:T(8,128)S(1)}, u32[]{:S(2)}, u32[]{:S(2)}) collective-permute-start(f32[160,96]{0,1:T(8,128)S(1)} %convolution_bitcast_fusion.20), channel_id=1, source_target_pairs={{0,1},{1,0},{2,3},{3,2},{4,5},{5,4},{6,7},{7,6},{8,9},{9,8},{10,11... | collective-permute-start | bytes 184328 | tf_op jit(solution)/shard_map/ppermute | solution.py:55
  94.4 0.9 collective-permute-done.8
  95.6 4.9 %collective-permute-done.9 = f32[160,96]{0,1:T(8,128)S(1)} collective-permute-done((f32[160,96]{0,1:T(8,128)S(1)}, f32[160,96]{0,1:T(8,128)S(1)}, u32[]{:S(2)}, u32[]{:S(2)}) %collective-permute-start.9) | collective-permute-done | bytes 61472 | tf_op jit(solution)/shard_map/ppermute | solution.py:55
  100.6 4.5 %collective-permute-done.10 = f32[160,96]{0,1:T(8,128)S(1)} collective-permute-done((f32[160,96]{0,1:T(8,128)S(1)}, f32[160,96]{0,1:T(8,128)S(1)}, u32[]{:S(2)}, u32[]{:S(2)}) %collective-permute-start.10) | collective-permute-done | bytes 61472 | tf_op jit(solution)/shard_map/ppermute | solution.py:55
  105.2 1.6 %collective-permute-start.11 = (f32[160,96]{0,1:T(8,128)S(1)}, f32[160,96]{0,1:T(8,128)S(1)}, u32[]{:S(2)}, u32[]{:S(2)}) collective-permute-start(f32[160,96]{0,1:T(8,128)S(1)} %add.490), channel_id=1, source_target_pairs={{0,8},{4,12},{8,0},{12,4},{1,9},{5,13},{9,1},{13,5},{2,10},{6,14},... | collective-permute-start | bytes 184328 | tf_op jit(solution)/shard_map/ppermute | solution.py:55
  106.8 4.6 %collective-permute-done.11 = f32[160,96]{0,1:T(8,128)S(1)} collective-permute-done((f32[160,96]{0,1:T(8,128)S(1)}, f32[160,96]{0,1:T(8,128)S(1)}, u32[]{:S(2)}, u32[]{:S(2)}) %collective-permute-start.11) | collective-permute-done | bytes 61472 | tf_op jit(solution)/shard_map/ppermute | solution.py:55
  111.5 2.9 %cholesky.17 = f32[32,32]{1,0:T(8,128)S(1)} custom-call(f32[32,32]{1,0:T(8,128)S(1)} %fusion.48), custom_call_target="Cholesky" | custom-call | tf_op jit(solution)/shard_map/jit(cholesky)/cholesky | solution.py:100
  114.4 0.6 compare_reduce_fusion.45
  115.1 0.7 fusion.49
  115.7 2.4 %custom-call.7 = f32[1,32,32]{1,2,0:T(8,128)S(1)} custom-call(f32[1,32,32]{2,1,0:T(8,128)S(1)} %get-tuple-element.79), custom_call_target="InvertDiagBlocksLowerTriangular" | custom-call | tf_op jit(solution)/shard_map/jit(_solve_triangular)/triangular_solve | solution.py:101
  119.4 0.8 convolution_bitcast_fusion.21
  120.2 0.7 copy.46
  121.0 0.7 copy.47
  (272 shorter events, 22.1 us)
Async XLA Ops:
  0.6 17.5 %copy-start = (f32[8,128,128]{2,1,0:T(8,128)S(1)}, f32[8,128,128]{2,1,0:T(8,128)}, u32[]{:S(2)}) copy-start(f32[8,128,128]{2,1,0:T(8,128)} %param.10) | copy-start | bytes 1572868
  2.9 6.3 %copy-start.21 = (s32[5,2,4]{0,2,1:T(4,128)S(1)}, s32[5,2,4]{0,2,1:T(4,128)}, u32[]{:S(2)}) copy-start(s32[5,2,4]{0,2,1:T(4,128)} %param.9) | copy-start | bytes 484
  3.0 7.7 %collective-permute-start = (f32[64,1,4,128]{3,0,2,1:T(8,128)S(1)}, f32[64,1,4,128]{3,0,2,1:T(8,128)S(1)}, u32[]{:S(2)}, u32[]{:S(2)}) collective-permute-start(f32[64,1,4,128]{3,0,2,1:T(8,128)S(1)} %get-tuple-element.74), channel_id=1, source_target_pairs={{0,4},{4,8},{8,12},{1,5},{5,9},{9,13},{2,6},{6,10},{10,14},{3,7},{... | collective-permute-start | bytes 393224 | tf_op jit(solution)/shard_map/ppermute | solution.py:15
  7.9 6.9 %collective-permute-start.1 = (f32[64,1,4,128]{3,0,2,1:T(8,128)S(1)}, f32[64,1,4,128]{3,0,2,1:T(8,128)S(1)}, u32[]{:S(2)}, u32[]{:S(2)}) collective-permute-start(f32[64,1,4,128]{3,0,2,1:T(8,128)S(1)} %get-tuple-element.75), channel_id=1, source_target_pairs={{4,0},{8,4},{12,8},{5,1},{9,5},{13,9},{6,2},{10,6},{14,10},{7,3},{... | collective-permute-start | bytes 393224 | tf_op jit(solution)/shard_map/ppermute | solution.py:18
  15.5 16.7 %collective-permute-start.2 = (f32[64,4,1,128]{3,0,2,1:T(8,128)}, f32[64,4,1,128]{3,0,2,1:T(8,128)S(1)}, u32[]{:S(2)}, u32[]{:S(2)}) collective-permute-start(f32[64,4,1,128]{3,0,2,1:T(8,128)} %get-tuple-element.68), channel_id=1, source_target_pairs={{0,1},{1,2},{2,3},{4,5},{5,6},{6,7},{8,9},{9,10},{10,11},{12,13},{... | collective-permute-start | bytes 393224 | tf_op jit(solution)/shard_map/ppermute | solution.py:15
  16.8 15.4 %collective-permute-start.3 = (f32[64,4,1,128]{3,0,2,1:T(8,128)}, f32[64,4,1,128]{3,0,2,1:T(8,128)S(1)}, u32[]{:S(2)}, u32[]{:S(2)}) collective-permute-start(f32[64,4,1,128]{3,0,2,1:T(8,128)} %get-tuple-element.69), channel_id=1, source_target_pairs={{1,0},{2,1},{3,2},{5,4},{6,5},{7,6},{9,8},{10,9},{11,10},{13,12},{... | collective-permute-start | bytes 393224 | tf_op jit(solution)/shard_map/ppermute | solution.py:18
  31.9 3.8 %copy-start.72 = (pred[2,4]{1,0:T(4,128)(4,1)}, pred[2,4]{1,0:T(4,128)(4,1)S(1)}, u32[]{:S(2)}) copy-start(pred[2,4]{1,0:T(4,128)(4,1)S(1)} %get-tuple-element.82) | copy-start | bytes 28
  31.9 3.8 %copy-start.74 = (pred[2,4]{1,0:T(4,128)(4,1)}, pred[2,4]{1,0:T(4,128)(4,1)S(1)}, u32[]{:S(2)}) copy-start(pred[2,4]{1,0:T(4,128)(4,1)S(1)} %get-tuple-element.83) | copy-start | bytes 28
  31.9 3.8 %copy-start.76 = (pred[2,4]{1,0:T(4,128)(4,1)}, pred[2,4]{1,0:T(4,128)(4,1)S(1)}, u32[]{:S(2)}) copy-start(pred[2,4]{1,0:T(4,128)(4,1)S(1)} %get-tuple-element.84) | copy-start | bytes 28
  31.9 3.8 %copy-start.78 = (pred[2,4]{1,0:T(4,128)(4,1)}, pred[2,4]{1,0:T(4,128)(4,1)S(1)}, u32[]{:S(2)}) copy-start(pred[2,4]{1,0:T(4,128)(4,1)S(1)} %get-tuple-element.85) | copy-start | bytes 28
  31.9 3.8 %copy-start.80 = (pred[2,4]{1,0:T(4,128)(4,1)}, pred[2,4]{1,0:T(4,128)(4,1)S(1)}, u32[]{:S(2)}) copy-start(pred[2,4]{1,0:T(4,128)(4,1)S(1)} %get-tuple-element.86) | copy-start | bytes 28
  31.9 3.8 %copy-start.82 = (pred[2,4]{1,0:T(4,128)(4,1)}, pred[2,4]{1,0:T(4,128)(4,1)S(1)}, u32[]{:S(2)}) copy-start(pred[2,4]{1,0:T(4,128)(4,1)S(1)} %get-tuple-element.87) | copy-start | bytes 28
  31.9 3.8 %copy-start.84 = (pred[2,4]{1,0:T(4,128)(4,1)}, pred[2,4]{1,0:T(4,128)(4,1)S(1)}, u32[]{:S(2)}) copy-start(pred[2,4]{1,0:T(4,128)(4,1)S(1)} %get-tuple-element.88) | copy-start | bytes 28
  31.9 3.8 %copy-start.86 = (pred[2,4]{1,0:T(4,128)(4,1)}, pred[2,4]{1,0:T(4,128)(4,1)S(1)}, u32[]{:S(2)}) copy-start(pred[2,4]{1,0:T(4,128)(4,1)S(1)} %get-tuple-element.89) | copy-start | bytes 28
  32.0 3.8 %copy-start.88 = (pred[2,4]{1,0:T(4,128)(4,1)}, pred[2,4]{1,0:T(4,128)(4,1)S(1)}, u32[]{:S(2)}) copy-start(pred[2,4]{1,0:T(4,128)(4,1)S(1)} %get-tuple-element.101) | copy-start | bytes 28
  32.0 5.9 %copy-start.54 = (pred[2,4]{1,0:T(4,128)(4,1)}, pred[2,4]{1,0:T(4,128)(4,1)S(1)}, u32[]{:S(2)}) copy-start(pred[2,4]{1,0:T(4,128)(4,1)S(1)} %get-tuple-element.36) | copy-start | bytes 28
  32.0 5.9 %copy-start.56 = (pred[2,4]{1,0:T(4,128)(4,1)}, pred[2,4]{1,0:T(4,128)(4,1)S(1)}, u32[]{:S(2)}) copy-start(pred[2,4]{1,0:T(4,128)(4,1)S(1)} %get-tuple-element.37) | copy-start | bytes 28
  32.0 5.9 %copy-start.58 = (pred[2,4]{1,0:T(4,128)(4,1)}, pred[2,4]{1,0:T(4,128)(4,1)S(1)}, u32[]{:S(2)}) copy-start(pred[2,4]{1,0:T(4,128)(4,1)S(1)} %get-tuple-element.38) | copy-start | bytes 28
  32.0 5.9 %copy-start.60 = (pred[2,4]{1,0:T(4,128)(4,1)}, pred[2,4]{1,0:T(4,128)(4,1)S(1)}, u32[]{:S(2)}) copy-start(pred[2,4]{1,0:T(4,128)(4,1)S(1)} %get-tuple-element.39) | copy-start | bytes 28
  32.0 5.9 %copy-start.62 = (pred[2,4]{1,0:T(4,128)(4,1)}, pred[2,4]{1,0:T(4,128)(4,1)S(1)}, u32[]{:S(2)}) copy-start(pred[2,4]{1,0:T(4,128)(4,1)S(1)} %get-tuple-element.40) | copy-start | bytes 28
  32.0 5.9 %copy-start.64 = (pred[2,4]{1,0:T(4,128)(4,1)}, pred[2,4]{1,0:T(4,128)(4,1)S(1)}, u32[]{:S(2)}) copy-start(pred[2,4]{1,0:T(4,128)(4,1)S(1)} %get-tuple-element.41) | copy-start | bytes 28
  32.0 5.9 %copy-start.66 = (pred[2,4]{1,0:T(4,128)(4,1)}, pred[2,4]{1,0:T(4,128)(4,1)S(1)}, u32[]{:S(2)}) copy-start(pred[2,4]{1,0:T(4,128)(4,1)S(1)} %get-tuple-element.80) | copy-start | bytes 28
  32.0 5.9 %copy-start.68 = (pred[2,4]{1,0:T(4,128)(4,1)}, pred[2,4]{1,0:T(4,128)(4,1)S(1)}, u32[]{:S(2)}) copy-start(pred[2,4]{1,0:T(4,128)(4,1)S(1)} %get-tuple-element.81) | copy-start | bytes 28
  32.0 5.9 %copy-start.70 = (pred[2,4]{1,0:T(4,128)(4,1)}, pred[2,4]{1,0:T(4,128)(4,1)S(1)}, u32[]{:S(2)}) copy-start(pred[2,4]{1,0:T(4,128)(4,1)S(1)} %get-tuple-element.102) | copy-start | bytes 28
  32.1 8.1 %copy-start.36 = (pred[2,4]{1,0:T(4,128)(4,1)}, pred[2,4]{1,0:T(4,128)(4,1)S(1)}, u32[]{:S(2)}) copy-start(pred[2,4]{1,0:T(4,128)(4,1)S(1)} %get-tuple-element.42) | copy-start | bytes 28
  32.1 8.1 %copy-start.38 = (pred[2,4]{1,0:T(4,128)(4,1)}, pred[2,4]{1,0:T(4,128)(4,1)S(1)}, u32[]{:S(2)}) copy-start(pred[2,4]{1,0:T(4,128)(4,1)S(1)} %get-tuple-element.43) | copy-start | bytes 28
  32.1 8.1 %copy-start.40 = (pred[2,4]{1,0:T(4,128)(4,1)}, pred[2,4]{1,0:T(4,128)(4,1)S(1)}, u32[]{:S(2)}) copy-start(pred[2,4]{1,0:T(4,128)(4,1)S(1)} %get-tuple-element.44) | copy-start | bytes 28
  32.1 8.1 %copy-start.42 = (pred[2,4]{1,0:T(4,128)(4,1)}, pred[2,4]{1,0:T(4,128)(4,1)S(1)}, u32[]{:S(2)}) copy-start(pred[2,4]{1,0:T(4,128)(4,1)S(1)} %get-tuple-element.45) | copy-start | bytes 28
  32.1 8.1 %copy-start.44 = (pred[2,4]{1,0:T(4,128)(4,1)}, pred[2,4]{1,0:T(4,128)(4,1)S(1)}, u32[]{:S(2)}) copy-start(pred[2,4]{1,0:T(4,128)(4,1)S(1)} %get-tuple-element.46) | copy-start | bytes 28
  32.1 8.1 %copy-start.46 = (pred[2,4]{1,0:T(4,128)(4,1)}, pred[2,4]{1,0:T(4,128)(4,1)S(1)}, u32[]{:S(2)}) copy-start(pred[2,4]{1,0:T(4,128)(4,1)S(1)} %get-tuple-element.47) | copy-start | bytes 28
  32.1 8.1 %copy-start.48 = (pred[2,4]{1,0:T(4,128)(4,1)}, pred[2,4]{1,0:T(4,128)(4,1)S(1)}, u32[]{:S(2)}) copy-start(pred[2,4]{1,0:T(4,128)(4,1)S(1)} %get-tuple-element.48) | copy-start | bytes 28
  32.1 8.1 %copy-start.50 = (pred[2,4]{1,0:T(4,128)(4,1)}, pred[2,4]{1,0:T(4,128)(4,1)S(1)}, u32[]{:S(2)}) copy-start(pred[2,4]{1,0:T(4,128)(4,1)S(1)} %get-tuple-element.49) | copy-start | bytes 28
  32.1 8.1 %copy-start.52 = (pred[2,4]{1,0:T(4,128)(4,1)}, pred[2,4]{1,0:T(4,128)(4,1)S(1)}, u32[]{:S(2)}) copy-start(pred[2,4]{1,0:T(4,128)(4,1)S(1)} %get-tuple-element.99) | copy-start | bytes 28
  32.1 10.3 %copy-start.24 = (pred[2,4]{1,0:T(4,128)(4,1)}, pred[2,4]{1,0:T(4,128)(4,1)S(1)}, u32[]{:S(2)}) copy-start(pred[2,4]{1,0:T(4,128)(4,1)S(1)} %get-tuple-element.52) | copy-start | bytes 28
  32.2 10.3 %copy-start.26 = (pred[2,4]{1,0:T(4,128)(4,1)}, pred[2,4]{1,0:T(4,128)(4,1)S(1)}, u32[]{:S(2)}) copy-start(pred[2,4]{1,0:T(4,128)(4,1)S(1)} %get-tuple-element.53) | copy-start | bytes 28
  32.2 10.3 %copy-start.28 = (pred[2,4]{1,0:T(4,128)(4,1)}, pred[2,4]{1,0:T(4,128)(4,1)S(1)}, u32[]{:S(2)}) copy-start(pred[2,4]{1,0:T(4,128)(4,1)S(1)} %get-tuple-element.98) | copy-start | bytes 28
  32.2 10.3 %copy-start.30 = (pred[2,4]{1,0:T(4,128)(4,1)}, pred[2,4]{1,0:T(4,128)(4,1)S(1)}, u32[]{:S(2)}) copy-start(pred[2,4]{1,0:T(4,128)(4,1)S(1)} %get-tuple-element.103) | copy-start | bytes 28
  32.2 10.3 %copy-start.32 = (pred[2,4]{1,0:T(4,128)(4,1)}, pred[2,4]{1,0:T(4,128)(4,1)S(1)}, u32[]{:S(2)}) copy-start(pred[2,4]{1,0:T(4,128)(4,1)S(1)} %get-tuple-element.104) | copy-start | bytes 28
  32.2 10.3 %copy-start.34 = (pred[2,4]{1,0:T(4,128)(4,1)}, pred[2,4]{1,0:T(4,128)(4,1)S(1)}, u32[]{:S(2)}) copy-start(pred[2,4]{1,0:T(4,128)(4,1)S(1)} %get-tuple-element.105) | copy-start | bytes 28
  63.4 4.1 %collective-permute-start.4 = (f32[32,1,4,128]{3,0,2,1:T(8,128)S(1)}, f32[32,1,4,128]{3,0,2,1:T(8,128)S(1)}, u32[]{:S(2)}, u32[]{:S(2)}) collective-permute-start(f32[32,1,4,128]{3,0,2,1:T(8,128)S(1)} %get-tuple-element.76), channel_id=1, source_target_pairs={{0,4},{4,8},{8,12},{1,5},{5,9},{9,13},{2,6},{6,10},{10,14},{3,7},{... | collective-permute-start | bytes 196616 | tf_op jit(solution)/shard_map/ppermute | solution.py:15
  65.3 6.3 %collective-permute-start.5 = (f32[32,1,4,128]{3,0,2,1:T(8,128)S(1)}, f32[32,1,4,128]{3,0,2,1:T(8,128)S(1)}, u32[]{:S(2)}, u32[]{:S(2)}) collective-permute-start(f32[32,1,4,128]{3,0,2,1:T(8,128)S(1)} %get-tuple-element.77), channel_id=1, source_target_pairs={{4,0},{8,4},{12,8},{5,1},{9,5},{13,9},{6,2},{10,6},{14,10},{7,3},{... | collective-permute-start | bytes 196616 | tf_op jit(solution)/shard_map/ppermute | solution.py:18
  71.6 3.0 %collective-permute-start.6 = (f32[32,4,1,128]{3,0,2,1:T(8,128)S(1)}, f32[32,4,1,128]{3,0,2,1:T(8,128)S(1)}, u32[]{:S(2)}, u32[]{:S(2)}) collective-permute-start(f32[32,4,1,128]{3,0,2,1:T(8,128)S(1)} %get-tuple-element.72), channel_id=1, source_target_pairs={{0,1},{1,2},{2,3},{4,5},{5,6},{6,7},{8,9},{9,10},{10,11},{12,13},{... | collective-permute-start | bytes 196616 | tf_op jit(solution)/shard_map/ppermute | solution.py:15
  73.2 4.1 %collective-permute-start.7 = (f32[32,4,1,128]{3,0,2,1:T(8,128)S(1)}, f32[32,4,1,128]{3,0,2,1:T(8,128)S(1)}, u32[]{:S(2)}, u32[]{:S(2)}) collective-permute-start(f32[32,4,1,128]{3,0,2,1:T(8,128)S(1)} %get-tuple-element.73), channel_id=1, source_target_pairs={{1,0},{2,1},{3,2},{5,4},{6,5},{7,6},{9,8},{10,9},{11,10},{13,12},{... | collective-permute-start | bytes 196616 | tf_op jit(solution)/shard_map/ppermute | solution.py:18
  91.4 3.9 %collective-permute-start.8 = (f32[160,96]{0,1:T(8,128)S(1)}, f32[160,96]{0,1:T(8,128)S(1)}, u32[]{:S(2)}, u32[]{:S(2)}) collective-permute-start(f32[160,96]{0,1:T(8,128)S(1)} %convolution_bitcast_fusion.20), channel_id=1, source_target_pairs={{0,1},{1,0},{2,3},{3,2},{4,5},{5,4},{6,7},{7,6},{8,9},{9,8},{10,11... | collective-permute-start | bytes 184328 | tf_op jit(solution)/shard_map/ppermute | solution.py:55
  95.3 5.1 %collective-permute-start.9 = (f32[160,96]{0,1:T(8,128)S(1)}, f32[160,96]{0,1:T(8,128)S(1)}, u32[]{:S(2)}, u32[]{:S(2)}) collective-permute-start(f32[160,96]{0,1:T(8,128)S(1)} %add.488), channel_id=1, source_target_pairs={{0,2},{1,3},{2,0},{3,1},{4,6},{5,7},{6,4},{7,5},{8,10},{9,11},{10,... | collective-permute-start | bytes 184328 | tf_op jit(solution)/shard_map/ppermute | solution.py:55
  100.5 4.7 %collective-permute-start.10 = (f32[160,96]{0,1:T(8,128)S(1)}, f32[160,96]{0,1:T(8,128)S(1)}, u32[]{:S(2)}, u32[]{:S(2)}) collective-permute-start(f32[160,96]{0,1:T(8,128)S(1)} %add.489), channel_id=1, source_target_pairs={{0,4},{4,0},{8,12},{12,8},{1,5},{5,1},{9,13},{13,9},{2,6},{6,2},{1... | collective-permute-start | bytes 184328 | tf_op jit(solution)/shard_map/ppermute | solution.py:55
  105.2 6.2 %collective-permute-start.11 = (f32[160,96]{0,1:T(8,128)S(1)}, f32[160,96]{0,1:T(8,128)S(1)}, u32[]{:S(2)}, u32[]{:S(2)}) collective-permute-start(f32[160,96]{0,1:T(8,128)S(1)} %add.490), channel_id=1, source_target_pairs={{0,8},{4,12},{8,0},{12,4},{1,9},{5,13},{9,1},{13,5},{2,10},{6,14},... | collective-permute-start | bytes 184328 | tf_op jit(solution)/shard_map/ppermute | solution.py:55
  111.4 7.0 %copy-start.19 = (f32[160,96]{0,1:T(8,128)}, f32[160,96]{0,1:T(8,128)S(1)}, u32[]{:S(2)}) copy-start(f32[160,96]{0,1:T(8,128)S(1)} %add_multiply_fusion) | copy-start | bytes 184324
  (67 other events, 53.0 us)

commit v2 on v0

v2 whole, which is shorter than its diff:
```python
import functools

import jax
import jax.numpy as jnp
from jax import lax
from jax.experimental import pallas as pl
from jax.experimental.pallas import tpu as pltpu
from jax.sharding import PartitionSpec as P

F32 = jnp.float32
BF16 = jnp.bfloat16
VMEM = pl.BlockSpec(memory_space=pltpu.VMEM)
SMEM = pl.BlockSpec(memory_space=pltpu.SMEM)
PARAMS = pltpu.CompilerParams(vmem_limit_bytes=24 * 1024 * 1024)


def split(value):
    high = value.astype(BF16)
    return high, (value - high.astype(F32)).astype(BF16)


def mul(left, right):
    return jnp.dot(left, right, preferred_element_type=F32)


def mul_t(left, right):
    return lax.dot_general(left, right, (((1,), (1,)), ((), ())), preferred_element_type=F32)


def mul3(left, right):
    left_high, left_low = split(left)
    right_high, right_low = split(right)
    return mul(left_high, right_high) + (mul(left_high, right_low) + mul(left_low, right_high))


def mul3_t(left, right):
    left_high, left_low = split(left)
    right_high, right_low = split(right)
    return mul_t(left_high, right_high) + (
        mul_t(left_high, right_low) + mul_t(left_low, right_high)
    )


def tables_kernel(stiff_ref, mass_ref, high_ref, low_ref):
    side = stiff_ref.shape[1]
    for kind in range(stiff_ref.shape[0]):
        for place, ref in enumerate((stiff_ref, mass_ref)):
            high, low = split(ref[kind])
            high_ref[kind, place * side : (place + 1) * side, :] = high
            low_ref[kind, place * side : (place + 1) * side, :] = low


def pack_kernel(count_x, count_y, basis_ref, previous_ref, low_ref, high_ref):
    tiles = count_x * count_y
    block = previous_ref.shape[0] // tiles
    first = basis_ref.shape[0] - block * tiles
    for row, ref in ((0, low_ref), (count_x - 1, high_ref)):
        for j in range(count_y):
            tile = row * count_y + j
            ref[j, :block, :] = basis_ref[pl.ds(first + tile, block, stride=tiles), :]
            ref[j, block:, :] = previous_ref[pl.ds(tile, block, stride=tiles), :]


def fill_extended(ext_ref, store, rows, sides):
    width = len(rows) and rows[0].shape[0]
    for i, row in enumerate(rows):
        for j in range(width):
            store(ext_ref, i * (width + 2) + j + 1, row[j])
    for i in range(len(rows)):
        store(ext_ref, i * (width + 2), sides[0][i])
        store(ext_ref, i * (width + 2) + width + 1, sides[1][i])


def source_of(neighbours_ref, k, tile, count_y):
    neighbour = neighbours_ref[k, tile]
    down = neighbour // 3
    return (tile // count_y + down) * (count_y + 2) + tile % count_y + neighbour - 3 * down


def residual_kernel(
    neighbours_ref,
    kinds_ref,
    low_ref,
    high_ref,
    from_low_ref,
    from_high_ref,
    side_low_ref,
    side_high_ref,
    basis_ref,
    table_high_ref,
    table_low_ref,
    residual_low_ref,
    residual_high_ref,
    partial_ref,
    ext_ref,
):
    count_y = low_ref.shape[0]
    block = low_ref.shape[1] // 2
    tiles = 2 * count_y
    prior = basis_ref.shape[0] // tiles

    def store(ext, place, value):
        for part in range(2):
            high, low = split(value[part * block : (part + 1) * block])
            ext[place, :block, part * 128 : (part + 1) * 128] = high
            ext[place, block:, part * 128 : (part + 1) * 128] = low

    fill_extended(
        ext_ref,
        store,
        (from_low_ref, low_ref, high_ref, from_high_ref),
        (side_low_ref, side_high_ref),
    )
    partial = jnp.zeros((block, prior), F32)
    for tile in range(tiles):
        own = (low_ref, high_ref)[tile // count_y][tile % count_y]
        total = 4.0 * own[:block] + own[block:]
        for k in range(neighbours_ref.shape[0]):
            source = source_of(neighbours_ref, k, tile, count_y)
            kind = kinds_ref[k, tile]
            chosen = ext_ref[source]
            both = mul(chosen, table_high_ref[kind])
            total = total + (
                both[:block] + (both[block:] + mul(chosen[:block], table_low_ref[kind]))
            )
        (residual_low_ref, residual_high_ref)[tile // count_y][tile % count_y] = total
        partial = partial + mul3_t(total, basis_ref[pl.ds(tile, prior, stride=tiles), :])
    partial_ref[...] = partial


def weighted_kernel(
    inverse_rows,
    partial_ref,
    other_ref,
    residual_low_ref,
    residual_high_ref,
    basis_ref,
    weighted_low_ref,
    weighted_high_ref,
    coupling_ref,
):
    count_y = residual_low_ref.shape[0]
    tiles = 2 * count_y
    prior = basis_ref.shape[0] // tiles
    coupling = (partial_ref[...] + other_ref[...]) * inverse_rows
    for tile in range(tiles):
        place = (tile // count_y, tile % count_y)
        moved = mul3(coupling, basis_ref[pl.ds(tile, prior, stride=tiles), :])
        (weighted_low_ref, weighted_high_ref)[place[0]][place[1]] = (
            (residual_low_ref, residual_high_ref)[place[0]][place[1]] - moved
        )
    coupling_ref[...] = coupling.T


def operators_kernel(
    neighbours_ref,
    kinds_ref,
    low_ref,
    high_ref,
    from_low_ref,
    from_high_ref,
    side_low_ref,
    side_high_ref,
    basis_ref,
    table_high_ref,
    table_low_ref,
    sums_ref,
    ext_ref,
):
    count_y, block, side = low_ref.shape
    tiles = 2 * count_y
    prior = basis_ref.shape[0] // tiles

    def store(ext, place, value):
        high, low = split(value)
        ext[place, :block, :] = high
        ext[place, block:, :] = low

    fill_extended(
        ext_ref,
        store,
        (from_low_ref, low_ref, high_ref, from_high_ref),
        (side_low_ref, side_high_ref),
    )
    with_basis = jnp.zeros((2 * block, prior), F32)
    with_own = jnp.zeros((block, 4 * block), F32)
    for tile in range(tiles):
        own = (low_ref, high_ref)[tile // count_y][tile % count_y]
        totals = [4.0 * own, own]
        for k in range(neighbours_ref.shape[0]):
            source = source_of(neighbours_ref, k, tile, count_y)
            kind = kinds_ref[k, tile]
            chosen = ext_ref[source]
            for part in range(2):
                span = slice(part * side, (part + 1) * side)
                both = mul(chosen, table_high_ref[kind, span, :])
                totals[part] = totals[part] + (
                    both[:block] + (both[block:] + mul(chosen[:block], table_low_ref[kind, span, :]))
                )
        applied = jnp.concatenate(totals, axis=0)
        with_basis = with_basis + mul3_t(applied, basis_ref[pl.ds(tile, prior, stride=tiles), :])
        right = jnp.concatenate([applied, own, jnp.zeros_like(own)], axis=0)
        with_own = with_own + mul3_t(own, right)
    sums_ref[: 2 * block, :] = with_basis
    sums_ref[2 * block :, :] = with_own


def factor_kernel(
    inverse_rows,
    sums_ref,
    weighted_low_ref,
    weighted_high_ref,
    new_ref,
    factor_ref,
    reduced_ref,
):
    count_y, block, _ = weighted_low_ref.shape
    prior = sums_ref.shape[1]
    tiles = 2 * count_y
    with_own = sums_ref[2 * block :, :] * inverse_rows
    gram = with_own[:, 2 * block : 3 * block]
    row_ids = lax.broadcasted_iota(jnp.int32, (block, block), 0)
    column_ids = lax.broadcasted_iota(jnp.int32, (block, block), 1)
    unit = jnp.where(row_ids == column_ids, 1.0, 0.0).astype(F32)
    work = jnp.concatenate([gram, unit], axis=1)
    rows = lax.broadcasted_iota(jnp.int32, (block, 1), 0)
    scale = jnp.zeros((block, 1), F32)
    for j in range(block):
        row = work[j : j + 1, :]
        pivot = row[:, j : j + 1]
        ratio = work[:, j : j + 1] / pivot
        scale = jnp.where(rows == j, lax.rsqrt(pivot), scale)
        work = work - jnp.where(rows > j, ratio, 0.0) * row
    work = work * scale
    factor_ref[...] = jnp.where(column_ids >= row_ids, work[:, :block], 0.0)
    inverse = work[:, block:]
    for tile in range(tiles):
        own = (weighted_low_ref, weighted_high_ref)[tile // count_y][tile % count_y]
        new_ref[pl.ds(tile, block, stride=tiles), :] = mul3(inverse, own)
    for part in range(2):
        span = slice(part * block, (part + 1) * block)
        from_basis = mul3(inverse, sums_ref[span, :] * inverse_rows)
        reduced_ref[part, :prior, :] = from_basis.T
        reduced_ref[part, prior:, :] = mul3_t(mul3(inverse, with_own[:, span]), inverse)


def swap(value, axis, step):
    count = lax.axis_size(axis)
    return lax.ppermute(value, axis, [(i, i ^ step) for i in range(count)])


def butterfly_steps():
    steps = []
    for axis in ("py", "px"):
        step = 1
        while step < lax.axis_size(axis):
            steps.append((axis, step))
            step *= 2
    return steps


def halved_sum(value):
    half = value.shape[0] // 2
    upper = lax.axis_index("py") % 2 == 1
    first, second = value[:half], value[half:]
    kept = jnp.where(upper, second, first)
    kept = kept + swap(jnp.where(upper, first, second), "py", 1)
    for axis, step in butterfly_steps()[1:]:
        kept = kept + swap(kept, axis, step)
    other = swap(kept, "py", 1)
    return jnp.concatenate(
        [jnp.where(upper, other, kept), jnp.where(upper, kept, other)], axis=0
    )


def line(value, axis, forward):
    count = lax.axis_size(axis)
    pairs = [(i, i + 1) for i in range(count - 1)]
    if not forward:
        pairs = [(target, source) for source, target in pairs]
    return lax.ppermute(value, axis, pairs)


def halo(low, high):
    from_low = line(high, "px", True)
    from_high = line(low, "px", False)
    rows = (from_low, low, high, from_high)
    side_low = line(jnp.concatenate([row[-1:] for row in rows], axis=0), "py", True)
    side_high = line(jnp.concatenate([row[:1] for row in rows], axis=0), "py", False)
    return from_low, from_high, side_low, side_high


def shape(*dims, dtype=F32):
    return jax.ShapeDtypeStruct(dims, dtype)


def shards(prior_basis, previous, neighbours, tile_kinds, stiff_tiles, mass_tiles):
    block = previous.shape[0]
    prior, count_x, count_y, side = prior_basis.shape
    tiles = count_x * count_y
    inverse_rows = 1.0 / (tiles * side * lax.axis_size("px") * lax.axis_size("py"))
    basis = prior_basis.reshape(-1, side)
    neighbours = neighbours.reshape(-1, tiles)
    tile_kinds = tile_kinds.reshape(-1, tiles)
    places = 4 * (count_y + 2)

    def call(kernel, inputs, outputs, scratch=(), smem=0):
        return pl.pallas_call(
            kernel,
            out_shape=outputs,
            in_specs=[SMEM] * smem + [VMEM] * (len(inputs) - smem),
            out_specs=[VMEM] * len(outputs),
            scratch_shapes=scratch,
            compiler_params=PARAMS,
        )(*inputs)

    low, high = call(
        functools.partial(pack_kernel, count_x, count_y),
        (basis, previous.reshape(-1, side)),
        [shape(count_y, 2 * block, side)] * 2,
    )
    table_high, table_low = call(
        tables_kernel,
        (stiff_tiles, mass_tiles),
        [shape(stiff_tiles.shape[0], 2 * side, side, dtype=BF16)] * 2,
    )
    residual_low, residual_high, partial = call(
        residual_kernel,
        (neighbours, tile_kinds, low, high, *halo(low, high), basis, table_high, table_low),
        [shape(count_y, block, side)] * 2 + [shape(block, prior)],
        [pltpu.VMEM((places, 2 * block, 2 * side), BF16)],
        smem=2,
    )
    steps = butterfly_steps()
    for axis, step in steps[:-1]:
        partial = partial + swap(partial, axis, step)
    weighted_low, weighted_high, coupling = call(
        functools.partial(weighted_kernel, inverse_rows),
        (partial, swap(partial, *steps[-1]), residual_low, residual_high, basis),
        [shape(count_y, block, side)] * 2 + [shape(prior, block)],
    )
    (sums,) = call(
        operators_kernel,
        (
            neighbours,
            tile_kinds,
            weighted_low,
            weighted_high,
            *halo(weighted_low, weighted_high),
            basis,
            table_high,
            table_low,
        ),
        [shape(3 * block, prior)],
        [pltpu.VMEM((places, 2 * block, side), BF16)],
        smem=2,
    )
    new_block, factor, reduced = call(
        functools.partial(factor_kernel, inverse_rows),
        (halved_sum(sums), weighted_low, weighted_high),
        [
            shape(block * tiles, side),
            shape(block, block),
            shape(2, prior + block, block),
        ],
    )
    return (new_block.reshape(previous.shape), coupling, factor, reduced)


def solution(mesh):
    placed = (
        P("case", "px", "py", None),
        P("case", "px", "py", None),
        P(None, "px", "py"),
        P(None, "px", "py"),
        P(),
        P(),
    )
    return jax.shard_map(
        shards,
        mesh=mesh,
        in_specs=placed,
        out_specs=(
            P("case", "px", "py", None),
            P("case", None),
            P("case", None),
            P("case", None, None),
        ),
        check_vma=False,
    )
```

time: 273 us -> 79.8 us (0.29)
  blocking collectives: 178 us -> 0 us
  matrix products: 21.5 us -> 0 us
  local copies, waits for them, and re-layouts: 22.7 us -> 4.84 us
  waiting for transfers between devices: 4.58 us -> 22.1 us
  other arithmetic: 13.8 us -> 0.76 us
  Pallas kernels: 0 us -> 11.6 us
  starting transfers between devices: 29.2 us -> 39.2 us
    psum x3 -> x0, blocking collectives: 178 us -> none  [the longest x1 61.9 us: shards(): lax.psum(pair_products(prior_basis, residual), ('px', 'py')) * inverse_rows]
    dot_general x27 -> x0, matrix products: 21.2 us -> none  [the longest x20 17.2 us: apply_pattern(): jnp.einsum('bxyc,xycd->bxyd', chosen, tile_blocks, precision=lax.Precisio...]
    ppermute x12 -> x17, waiting for transfers between devices: 4.58 us -> 22.1 us  [the longest x9 13.5 us: swap(): return lax.ppermute(value, axis, [(i, i ^ step) for i in range(count)])]
    pallas_call x0 -> x6, Pallas kernels: none -> 11.6 us  [call(): pl.pallas_call(kernel, out_shape=outputs, in_specs=[SMEM] * smem + [VMEM]...]
    gather x10 -> x0, local copies, waits for them, and re-layouts: 10.6 us -> none  [apply_pattern(): tile_blocks = tile_table[tile_kinds[entry_index]]]
    ppermute x12 -> x17, starting transfers between devices: 29.2 us -> 39.2 us  [the longest x8 20.8 us: line(): return lax.ppermute(value, axis, pairs)]
    another operation x6 -> x0, other arithmetic: 6.04 us -> none  [the longest x3 3.59 us: shards(): lower_factor = jnp.linalg.cholesky(gram)]
    unnamed x206 -> x16, local copies, waits for them, and re-layouts: 9.09 us -> 4.64 us
  transfers between devices with their start and end apart: 12 -> 17, of which waited for: 4 -> 14; matrix products, arithmetic and copies ran while one was open for 7% -> 2% of each run, Pallas kernels for 0% -> 0%
where the time goes in v2:
time: 79.8 us; the launch traced here: 79.4 us
  starting transfers between devices  39.2 us (49%)
  waiting for transfers between devices  22.1 us (28%)
  Pallas kernels  11.6 us (15%)
  local copies, waits for them, and re-layouts  4.84 us (6%)
  between operations  0.87 us (1%)
    ppermute x8, starting transfers between devices, line(): return lax.ppermute(value, axis, pairs)  20.8 us
    ppermute x9, starting transfers between devices, swap(): return lax.ppermute(value, axis, [(i, i ^ step) for i in range(count)])  18.4 us
    ppermute x9, waiting for transfers between devices, swap(): return lax.ppermute(value, axis, [(i, i ^ step) for i in range(count)])  13.5 us
    pallas_call x6, Pallas kernels, call(): pl.pallas_call(kernel, out_shape=outputs, in_specs=[SMEM] * smem + [VMEM]...  11.6 us
    ppermute x8, waiting for transfers between devices, line(): return lax.ppermute(value, axis, pairs)  8.53 us
    unnamed x16, local copies, waits for them, and re-layouts  4.64 us
  transfers between devices with their start and end apart: 17, of which 14 were waited for; matrix products, arithmetic and copies ran while one was open for 2% of the time, Pallas kernels for 0%

profile of v2, /device:TPU:0, one launch (start us, length us, event | category | flops | bytes accessed | tf_op | source)
XLA Modules:
  0.0 79.4 jit_solution(9934140351365485596)
XLA Ops:
  0.6 1.0 %copy-done = f32[128,2,4,128]{3,2,1,0:T(4,128)S(1)} copy-done((f32[128,2,4,128]{3,2,1,0:T(4,128)S(1)}, f32[128,2,4,128]{3,2,1,0:T(4,128)}, u32[]{:S(2)}) %copy-start) | copy-done | bytes 524312
  1.7 0.9 %copy-done.4 = f32[32,2,4,128]{3,2,1,0:T(4,128)S(1)} copy-done((f32[32,2,4,128]{3,2,1,0:T(4,128)S(1)}, f32[32,2,4,128]{3,2,1,0:T(4,128)}, u32[]{:S(2)}) %copy-start.4) | copy-done | bytes 131096
  2.6 4.9 %collective-permute-start = (f32[4,64,128]{2,1,0:T(8,128)S(1)}, f32[4,64,128]{2,1,0:T(8,128)S(1)}, u32[]{:S(2)}, u32[]{:S(2)}) collective-permute-start(f32[4,64,128]{2,1,0:T(8,128)S(1)} %get-tuple-element.18.high_ref), channel_id=1, source_target_pairs={{0,4},{4,8},{8,12},{1,5},{5,9},{9,13},{2,6},{6,10},{10,14},{3,7},{... | collective-permute-start | bytes 393224 | tf_op jit(solution)/shard_map/ppermute | solution.py:281
  7.6 0.0 copy-start.2
  7.6 0.0 copy-start.3
  7.6 1.4 %collective-permute-start.1 = (f32[4,64,128]{2,1,0:T(8,128)S(1)}, f32[4,64,128]{2,1,0:T(8,128)S(1)}, u32[]{:S(2)}, u32[]{:S(2)}) collective-permute-start(f32[4,64,128]{2,1,0:T(8,128)S(1)} %get-tuple-element.17.low_ref), channel_id=1, source_target_pairs={{4,0},{8,4},{12,8},{5,1},{9,5},{13,9},{6,2},{10,6},{14,10},{7,3},{... | collective-permute-start | bytes 393224 | tf_op jit(solution)/shard_map/ppermute | solution.py:281
  9.0 1.3 %collective-permute-done.from_low_ref = f32[4,64,128]{2,1,0:T(8,128)S(1)} collective-permute-done((f32[4,64,128]{2,1,0:T(8,128)S(1)}, f32[4,64,128]{2,1,0:T(8,128)S(1)}, u32[]{:S(2)}, u32[]{:S(2)}) %collective-permute-start) | collective-permute-done | bytes 131104 | tf_op jit(solution)/shard_map/ppermute | solution.py:281
  10.3 4.3 %collective-permute-done.1.from_high_ref = f32[4,64,128]{2,1,0:T(8,128)S(1)} collective-permute-done((f32[4,64,128]{2,1,0:T(8,128)S(1)}, f32[4,64,128]{2,1,0:T(8,128)S(1)}, u32[]{:S(2)}, u32[]{:S(2)}) %collective-permute-start.1) | collective-permute-done | bytes 131104 | tf_op jit(solution)/shard_map/ppermute | solution.py:281
  14.6 1.3 %collective-permute-start.3 = (f32[4,64,128]{2,1,0:T(8,128)S(1)}, f32[4,64,128]{2,1,0:T(8,128)S(1)}, u32[]{:S(2)}, u32[]{:S(2)}) collective-permute-start(f32[4,64,128]{2,1,0:T(8,128)S(1)} %pad_maximum_fusion.1), channel_id=1, source_target_pairs={{1,0},{2,1},{3,2},{5,4},{6,5},{7,6},{9,8},{10,9},{11,10},{13,12},{... | collective-permute-start | bytes 393224 | tf_op jit(solution)/shard_map/ppermute | solution.py:281
  15.9 0.0 copy-start.5
  15.9 0.7 pad_maximum_fusion
  16.6 3.0 %collective-permute-start.2 = (f32[4,64,128]{2,1,0:T(8,128)}, f32[4,64,128]{2,1,0:T(8,128)S(1)}, u32[]{:S(2)}, u32[]{:S(2)}) collective-permute-start(f32[4,64,128]{2,1,0:T(8,128)} %pad_maximum_fusion), channel_id=1, source_target_pairs={{0,1},{1,2},{2,3},{4,5},{5,6},{6,7},{8,9},{9,10},{10,11},{12,13},{... | collective-permute-start | bytes 393224 | tf_op jit(solution)/shard_map/ppermute | solution.py:281
  19.6 0.0 copy-start.6
  19.6 0.1 copy.12.neighbours_ref
  19.7 0.6 copy-done.6
  20.3 0.1 copy.13.kinds_ref
  20.4 0.1 shard_map.94
  20.5 0.3 collective-permute-done.2.side_low_ref
  20.8 0.7 copy-done.1
  21.5 2.9 %shard_map.95 = (f32[4,32,128]{2,1,0:T(8,128)S(1)}, f32[4,32,128]{2,1,0:T(8,128)S(1)}, f32[32,128]{1,0:T(8,128)S(1)}) custom-call(s32[5,8]{1,0:T(8,128)S(1)} %copy.12.neighbours_ref, s32[5,8]{1,0:T(8,128)S(1)} %copy.13.kinds_ref, f32[4,64,128]{2,1,0:T(8,128)S(1)} %get-tuple-element.17.low_ref, f32[4,64,128]{2,1,0:T(8,128)S(1)} %get-tuple-element.18.high_ref, ...), custom_call_target="tpu_custom_call" | custom-call | tf_op jit(solution)/shard_map/pallas_call | solution.py:308
  24.4 1.6 %collective-permute-start.4 = (f32[32,128]{1,0:T(8,128)S(1)}, f32[32,128]{1,0:T(8,128)S(1)}, u32[]{:S(2)}, u32[]{:S(2)}) collective-permute-start(f32[32,128]{1,0:T(8,128)S(1)} %get-tuple-element.21), channel_id=1, source_target_pairs={{0,1},{1,0},{2,3},{3,2},{4,5},{5,4},{6,7},{7,6},{8,9},{9,8},{10,11... | collective-permute-start | bytes 49160 | tf_op jit(solution)/shard_map/ppermute | solution.py:249
  25.9 0.8 %collective-permute-done.4 = f32[32,128]{1,0:T(8,128)S(1)} collective-permute-done((f32[32,128]{1,0:T(8,128)S(1)}, f32[32,128]{1,0:T(8,128)S(1)}, u32[]{:S(2)}, u32[]{:S(2)}) %collective-permute-start.4) | collective-permute-done | bytes 16416 | tf_op jit(solution)/shard_map/ppermute | solution.py:249
  26.8 2.6 %collective-permute-start.5 = (f32[32,128]{1,0:T(8,128)S(1)}, f32[32,128]{1,0:T(8,128)S(1)}, u32[]{:S(2)}, u32[]{:S(2)}) collective-permute-start(f32[32,128]{1,0:T(8,128)S(1)} %add.26), channel_id=1, source_target_pairs={{0,2},{1,3},{2,0},{3,1},{4,6},{5,7},{6,4},{7,5},{8,10},{9,11},{10,... | collective-permute-start | bytes 49160 | tf_op jit(solution)/shard_map/ppermute | solution.py:249
  29.3 1.7 %collective-permute-done.5 = f32[32,128]{1,0:T(8,128)S(1)} collective-permute-done((f32[32,128]{1,0:T(8,128)S(1)}, f32[32,128]{1,0:T(8,128)S(1)}, u32[]{:S(2)}, u32[]{:S(2)}) %collective-permute-start.5) | collective-permute-done | bytes 16416 | tf_op jit(solution)/shard_map/ppermute | solution.py:249
  31.0 1.6 %collective-permute-start.6 = (f32[32,128]{1,0:T(8,128)S(1)}, f32[32,128]{1,0:T(8,128)S(1)}, u32[]{:S(2)}, u32[]{:S(2)}) collective-permute-start(f32[32,128]{1,0:T(8,128)S(1)} %add.27), channel_id=1, source_target_pairs={{0,4},{4,0},{8,12},{12,8},{1,5},{5,1},{9,13},{13,9},{2,6},{6,2},{1... | collective-permute-start | bytes 49160 | tf_op jit(solution)/shard_map/ppermute | solution.py:249
  32.6 2.2 %collective-permute-done.6 = f32[32,128]{1,0:T(8,128)S(1)} collective-permute-done((f32[32,128]{1,0:T(8,128)S(1)}, f32[32,128]{1,0:T(8,128)S(1)}, u32[]{:S(2)}, u32[]{:S(2)}) %collective-permute-start.6) | collective-permute-done | bytes 16416 | tf_op jit(solution)/shard_map/ppermute | solution.py:249
  34.8 2.6 %collective-permute-start.7 = (f32[32,128]{1,0:T(8,128)S(1)}, f32[32,128]{1,0:T(8,128)S(1)}, u32[]{:S(2)}, u32[]{:S(2)}) collective-permute-start(f32[32,128]{1,0:T(8,128)S(1)} %add.28.partial_ref), channel_id=1, source_target_pairs={{0,8},{4,12},{8,0},{12,4},{1,9},{5,13},{9,1},{13,5},{2,10},{6,14},... | collective-permute-start | bytes 49160 | tf_op jit(solution)/shard_map/ppermute | solution.py:249
  37.4 2.1 %collective-permute-done.7.other_ref = f32[32,128]{1,0:T(8,128)S(1)} collective-permute-done((f32[32,128]{1,0:T(8,128)S(1)}, f32[32,128]{1,0:T(8,128)S(1)}, u32[]{:S(2)}, u32[]{:S(2)}) %collective-permute-start.7) | collective-permute-done | bytes 16416 | tf_op jit(solution)/shard_map/ppermute | solution.py:249
  39.4 0.3 shard_map.96
  39.8 1.3 %collective-permute-start.9 = (f32[4,32,128]{2,1,0:T(8,128)S(1)}, f32[4,32,128]{2,1,0:T(8,128)S(1)}, u32[]{:S(2)}, u32[]{:S(2)}) collective-permute-start(f32[4,32,128]{2,1,0:T(8,128)S(1)} %get-tuple-element.24.low_ref.weighted_low_ref), channel_id=1, source_target_pairs={{4,0},{8,4},{12,8},{5,1},{9,5},{13,9},{6,2},{10,6},{14,10},{7,3},{... | collective-permute-start | bytes 196616 | tf_op jit(solution)/shard_map/ppermute | solution.py:281
  41.1 4.5 %collective-permute-start.8 = (f32[4,32,128]{2,1,0:T(8,128)S(1)}, f32[4,32,128]{2,1,0:T(8,128)S(1)}, u32[]{:S(2)}, u32[]{:S(2)}) collective-permute-start(f32[4,32,128]{2,1,0:T(8,128)S(1)} %get-tuple-element.25.high_ref.weighted_high_ref), channel_id=1, source_target_pairs={{0,4},{4,8},{8,12},{1,5},{5,9},{9,13},{2,6},{6,10},{10,14},{3,7},{... | collective-permute-start | bytes 196616 | tf_op jit(solution)/shard_map/ppermute | solution.py:281
  45.6 1.9 %collective-permute-done.8.from_low_ref = f32[4,32,128]{2,1,0:T(8,128)S(1)} collective-permute-done((f32[4,32,128]{2,1,0:T(8,128)S(1)}, f32[4,32,128]{2,1,0:T(8,128)S(1)}, u32[]{:S(2)}, u32[]{:S(2)}) %collective-permute-start.8) | collective-permute-done | bytes 65568 | tf_op jit(solution)/shard_map/ppermute | solution.py:281
  47.5 1.3 %collective-permute-start.11 = (f32[4,32,128]{2,1,0:T(8,128)S(1)}, f32[4,32,128]{2,1,0:T(8,128)S(1)}, u32[]{:S(2)}, u32[]{:S(2)}) collective-permute-start(f32[4,32,128]{2,1,0:T(8,128)S(1)} %pad_maximum_fusion.3), channel_id=1, source_target_pairs={{1,0},{2,1},{3,2},{5,4},{6,5},{7,6},{9,8},{10,9},{11,10},{13,12},{... | collective-permute-start | bytes 196616 | tf_op jit(solution)/shard_map/ppermute | solution.py:281
  48.9 3.0 %collective-permute-start.10 = (f32[4,32,128]{2,1,0:T(8,128)S(1)}, f32[4,32,128]{2,1,0:T(8,128)S(1)}, u32[]{:S(2)}, u32[]{:S(2)}) collective-permute-start(f32[4,32,128]{2,1,0:T(8,128)S(1)} %pad_maximum_fusion.2), channel_id=1, source_target_pairs={{0,1},{1,2},{2,3},{4,5},{5,6},{6,7},{8,9},{9,10},{10,11},{12,13},{... | collective-permute-start | bytes 196616 | tf_op jit(solution)/shard_map/ppermute | solution.py:281
  51.9 0.9 %collective-permute-done.10.side_low_ref = f32[4,32,128]{2,1,0:T(8,128)S(1)} collective-permute-done((f32[4,32,128]{2,1,0:T(8,128)S(1)}, f32[4,32,128]{2,1,0:T(8,128)S(1)}, u32[]{:S(2)}, u32[]{:S(2)}) %collective-permute-start.10) | collective-permute-done | bytes 65568 | tf_op jit(solution)/shard_map/ppermute | solution.py:281
  52.8 4.5 %shard_map.97 = f32[96,128]{1,0:T(8,128)S(1)} custom-call(s32[5,8]{1,0:T(8,128)S(1)} %copy.12.neighbours_ref, s32[5,8]{1,0:T(8,128)S(1)} %copy.13.kinds_ref, f32[4,32,128]{2,1,0:T(8,128)S(1)} %get-tuple-element.24.low_ref.weighted_low_ref, f32[4,32,128]{2,1,0:T(8,128)S(1)} %get-tuple-element.25.high_ref.weighted_high_ref, ...), custom_call_target="tpu_custom_call" | custom-call | tf_op jit(solution)/shard_map/pallas_call | solution.py:308
  57.3 2.1 %collective-permute-start.12 = (f32[48,128]{1,0:T(8,128)S(1)}, f32[48,128]{1,0:T(8,128)S(1)}, u32[]{:S(2)}, u32[]{:S(2)}) collective-permute-start(f32[48,128]{1,0:T(8,128)S(1)} %slice_select_fusion), channel_id=1, source_target_pairs={{0,1},{1,0},{2,3},{3,2},{4,5},{5,4},{6,7},{7,6},{8,9},{9,8},{10,11... | collective-permute-start | bytes 73736 | tf_op jit(solution)/shard_map/ppermute | solution.py:249
  59.4 0.8 %collective-permute-done.12 = f32[48,128]{1,0:T(8,128)S(1)} collective-permute-done((f32[48,128]{1,0:T(8,128)S(1)}, f32[48,128]{1,0:T(8,128)S(1)}, u32[]{:S(2)}, u32[]{:S(2)}) %collective-permute-start.12) | collective-permute-done | bytes 24608 | tf_op jit(solution)/shard_map/ppermute | solution.py:249
  60.3 2.6 %collective-permute-start.13 = (f32[48,128]{1,0:T(8,128)S(1)}, f32[48,128]{1,0:T(8,128)S(1)}, u32[]{:S(2)}, u32[]{:S(2)}) collective-permute-start(f32[48,128]{1,0:T(8,128)S(1)} %select_add_fusion), channel_id=1, source_target_pairs={{0,2},{1,3},{2,0},{3,1},{4,6},{5,7},{6,4},{7,5},{8,10},{9,11},{10,... | collective-permute-start | bytes 73736 | tf_op jit(solution)/shard_map/ppermute | solution.py:249
  62.9 1.8 %collective-permute-done.13 = f32[48,128]{1,0:T(8,128)S(1)} collective-permute-done((f32[48,128]{1,0:T(8,128)S(1)}, f32[48,128]{1,0:T(8,128)S(1)}, u32[]{:S(2)}, u32[]{:S(2)}) %collective-permute-start.13) | collective-permute-done | bytes 24608 | tf_op jit(solution)/shard_map/ppermute | solution.py:249
  64.7 2.4 %collective-permute-start.14 = (f32[48,128]{1,0:T(8,128)S(1)}, f32[48,128]{1,0:T(8,128)S(1)}, u32[]{:S(2)}, u32[]{:S(2)}) collective-permute-start(f32[48,128]{1,0:T(8,128)S(1)} %add.30), channel_id=1, source_target_pairs={{0,4},{4,0},{8,12},{12,8},{1,5},{5,1},{9,13},{13,9},{2,6},{6,2},{1... | collective-permute-start | bytes 73736 | tf_op jit(solution)/shard_map/ppermute | solution.py:249
  67.1 1.8 %collective-permute-done.14 = f32[48,128]{1,0:T(8,128)S(1)} collective-permute-done((f32[48,128]{1,0:T(8,128)S(1)}, f32[48,128]{1,0:T(8,128)S(1)}, u32[]{:S(2)}, u32[]{:S(2)}) %collective-permute-start.14) | collective-permute-done | bytes 24608 | tf_op jit(solution)/shard_map/ppermute | solution.py:249
  68.9 3.0 %collective-permute-start.15 = (f32[48,128]{1,0:T(8,128)S(1)}, f32[48,128]{1,0:T(8,128)S(1)}, u32[]{:S(2)}, u32[]{:S(2)}) collective-permute-start(f32[48,128]{1,0:T(8,128)S(1)} %add.31), channel_id=1, source_target_pairs={{0,8},{4,12},{8,0},{12,4},{1,9},{5,13},{9,1},{13,5},{2,10},{6,14},... | collective-permute-start | bytes 73736 | tf_op jit(solution)/shard_map/ppermute | solution.py:249
  71.9 1.8 %collective-permute-done.15 = f32[48,128]{1,0:T(8,128)S(1)} collective-permute-done((f32[48,128]{1,0:T(8,128)S(1)}, f32[48,128]{1,0:T(8,128)S(1)}, u32[]{:S(2)}, u32[]{:S(2)}) %collective-permute-start.15) | collective-permute-done | bytes 24608 | tf_op jit(solution)/shard_map/ppermute | solution.py:249
  73.7 0.7 copy.14
  74.4 0.5 collective-permute-done.16
  74.9 3.8 %shard_map.98 = (f32[256,128]{1,0:T(8,128)}, f32[32,32]{1,0:T(8,128)}, f32[2,160,32]{2,1,0:T(8,128)S(1)}) custom-call(f32[96,128]{1,0:T(8,128)S(1)} %pad_maximum_fusion.4.sums_ref, f32[4,32,128]{2,1,0:T(8,128)S(1)} %get-tuple-element.24.low_ref.weighted_low_ref, f32[4,32,128]{2,1,0:T(8,128)S(1)} %get-tuple-element.25.high_ref.weighted_high_ref), custom_call_target="tpu_custom_call" | custom-call | tf_op jit(solution)/shard_map/pallas_call | solution.py:308
  78.7 0.7 copy.15
  (31 shorter events, 0.2 us)
Async XLA Ops:
  0.6 1.0 %copy-start = (f32[128,2,4,128]{3,2,1,0:T(4,128)S(1)}, f32[128,2,4,128]{3,2,1,0:T(4,128)}, u32[]{:S(2)}) copy-start(f32[128,2,4,128]{3,2,1,0:T(4,128)} %param.6) | copy-start | bytes 1572868
  1.7 0.9 %copy-start.4 = (f32[32,2,4,128]{3,2,1,0:T(4,128)S(1)}, f32[32,2,4,128]{3,2,1,0:T(4,128)}, u32[]{:S(2)}) copy-start(f32[32,2,4,128]{3,2,1,0:T(4,128)} %param.7) | copy-start | bytes 393220
  2.6 7.7 %collective-permute-start = (f32[4,64,128]{2,1,0:T(8,128)S(1)}, f32[4,64,128]{2,1,0:T(8,128)S(1)}, u32[]{:S(2)}, u32[]{:S(2)}) collective-permute-start(f32[4,64,128]{2,1,0:T(8,128)S(1)} %get-tuple-element.18.high_ref), channel_id=1, source_target_pairs={{0,4},{4,8},{8,12},{1,5},{5,9},{9,13},{2,6},{6,10},{10,14},{3,7},{... | collective-permute-start | bytes 393224 | tf_op jit(solution)/shard_map/ppermute | solution.py:281
  7.6 12.8 %copy-start.2 = (f32[8,128,128]{2,1,0:T(8,128)S(1)}, f32[8,128,128]{2,1,0:T(8,128)}, u32[]{:S(2)}) copy-start(f32[8,128,128]{2,1,0:T(8,128)} %stiff_ref.1) | copy-start | bytes 1572868
  7.6 12.8 %copy-start.3 = (f32[8,128,128]{2,1,0:T(8,128)S(1)}, f32[8,128,128]{2,1,0:T(8,128)}, u32[]{:S(2)}) copy-start(f32[8,128,128]{2,1,0:T(8,128)} %mass_ref.1) | copy-start | bytes 1572868
  7.6 7.0 %collective-permute-start.1 = (f32[4,64,128]{2,1,0:T(8,128)S(1)}, f32[4,64,128]{2,1,0:T(8,128)S(1)}, u32[]{:S(2)}, u32[]{:S(2)}) collective-permute-start(f32[4,64,128]{2,1,0:T(8,128)S(1)} %get-tuple-element.17.low_ref), channel_id=1, source_target_pairs={{4,0},{8,4},{12,8},{5,1},{9,5},{13,9},{6,2},{10,6},{14,10},{7,3},{... | collective-permute-start | bytes 393224 | tf_op jit(solution)/shard_map/ppermute | solution.py:281
  14.6 5.9 %collective-permute-start.3 = (f32[4,64,128]{2,1,0:T(8,128)S(1)}, f32[4,64,128]{2,1,0:T(8,128)S(1)}, u32[]{:S(2)}, u32[]{:S(2)}) collective-permute-start(f32[4,64,128]{2,1,0:T(8,128)S(1)} %pad_maximum_fusion.1), channel_id=1, source_target_pairs={{1,0},{2,1},{3,2},{5,4},{6,5},{7,6},{9,8},{10,9},{11,10},{13,12},{... | collective-permute-start | bytes 393224 | tf_op jit(solution)/shard_map/ppermute | solution.py:281
  15.9 3.7 %copy-start.5 = (s32[5,2,4]{0,2,1:T(4,128)S(1)}, s32[5,2,4]{0,2,1:T(4,128)}, u32[]{:S(2)}) copy-start(s32[5,2,4]{0,2,1:T(4,128)} %param.8) | copy-start | bytes 484
  16.6 4.2 %collective-permute-start.2 = (f32[4,64,128]{2,1,0:T(8,128)}, f32[4,64,128]{2,1,0:T(8,128)S(1)}, u32[]{:S(2)}, u32[]{:S(2)}) collective-permute-start(f32[4,64,128]{2,1,0:T(8,128)} %pad_maximum_fusion), channel_id=1, source_target_pairs={{0,1},{1,2},{2,3},{4,5},{5,6},{6,7},{8,9},{9,10},{10,11},{12,13},{... | collective-permute-start | bytes 393224 | tf_op jit(solution)/shard_map/ppermute | solution.py:281
  19.6 0.7 copy-start.6
  20.4 1.0 %copy-start.1 = (f32[128,2,4,128]{3,2,1,0:T(4,128)S(1)}, f32[128,2,4,128]{3,2,1,0:T(4,128)}, u32[]{:S(2)}) copy-start(f32[128,2,4,128]{3,2,1,0:T(4,128)} %param.6) | copy-start | bytes 1572868
  24.4 2.4 %collective-permute-start.4 = (f32[32,128]{1,0:T(8,128)S(1)}, f32[32,128]{1,0:T(8,128)S(1)}, u32[]{:S(2)}, u32[]{:S(2)}) collective-permute-start(f32[32,128]{1,0:T(8,128)S(1)} %get-tuple-element.21), channel_id=1, source_target_pairs={{0,1},{1,0},{2,3},{3,2},{4,5},{5,4},{6,7},{7,6},{8,9},{9,8},{10,11... | collective-permute-start | bytes 49160 | tf_op jit(solution)/shard_map/ppermute | solution.py:249
  26.8 4.3 %collective-permute-start.5 = (f32[32,128]{1,0:T(8,128)S(1)}, f32[32,128]{1,0:T(8,128)S(1)}, u32[]{:S(2)}, u32[]{:S(2)}) collective-permute-start(f32[32,128]{1,0:T(8,128)S(1)} %add.26), channel_id=1, source_target_pairs={{0,2},{1,3},{2,0},{3,1},{4,6},{5,7},{6,4},{7,5},{8,10},{9,11},{10,... | collective-permute-start | bytes 49160 | tf_op jit(solution)/shard_map/ppermute | solution.py:249
  31.0 3.7 %collective-permute-start.6 = (f32[32,128]{1,0:T(8,128)S(1)}, f32[32,128]{1,0:T(8,128)S(1)}, u32[]{:S(2)}, u32[]{:S(2)}) collective-permute-start(f32[32,128]{1,0:T(8,128)S(1)} %add.27), channel_id=1, source_target_pairs={{0,4},{4,0},{8,12},{12,8},{1,5},{5,1},{9,13},{13,9},{2,6},{6,2},{1... | collective-permute-start | bytes 49160 | tf_op jit(solution)/shard_map/ppermute | solution.py:249
  34.8 4.6 %collective-permute-start.7 = (f32[32,128]{1,0:T(8,128)S(1)}, f32[32,128]{1,0:T(8,128)S(1)}, u32[]{:S(2)}, u32[]{:S(2)}) collective-permute-start(f32[32,128]{1,0:T(8,128)S(1)} %add.28.partial_ref), channel_id=1, source_target_pairs={{0,8},{4,12},{8,0},{12,4},{1,9},{5,13},{9,1},{13,5},{2,10},{6,14},... | collective-permute-start | bytes 49160 | tf_op jit(solution)/shard_map/ppermute | solution.py:249
  39.8 7.8 %collective-permute-start.9 = (f32[4,32,128]{2,1,0:T(8,128)S(1)}, f32[4,32,128]{2,1,0:T(8,128)S(1)}, u32[]{:S(2)}, u32[]{:S(2)}) collective-permute-start(f32[4,32,128]{2,1,0:T(8,128)S(1)} %get-tuple-element.24.low_ref.weighted_low_ref), channel_id=1, source_target_pairs={{4,0},{8,4},{12,8},{5,1},{9,5},{13,9},{6,2},{10,6},{14,10},{7,3},{... | collective-permute-start | bytes 196616 | tf_op jit(solution)/shard_map/ppermute | solution.py:281
  41.1 6.4 %collective-permute-start.8 = (f32[4,32,128]{2,1,0:T(8,128)S(1)}, f32[4,32,128]{2,1,0:T(8,128)S(1)}, u32[]{:S(2)}, u32[]{:S(2)}) collective-permute-start(f32[4,32,128]{2,1,0:T(8,128)S(1)} %get-tuple-element.25.high_ref.weighted_high_ref), channel_id=1, source_target_pairs={{0,4},{4,8},{8,12},{1,5},{5,9},{9,13},{2,6},{6,10},{10,14},{3,7},{... | collective-permute-start | bytes 196616 | tf_op jit(solution)/shard_map/ppermute | solution.py:281
  47.5 4.4 %collective-permute-start.11 = (f32[4,32,128]{2,1,0:T(8,128)S(1)}, f32[4,32,128]{2,1,0:T(8,128)S(1)}, u32[]{:S(2)}, u32[]{:S(2)}) collective-permute-start(f32[4,32,128]{2,1,0:T(8,128)S(1)} %pad_maximum_fusion.3), channel_id=1, source_target_pairs={{1,0},{2,1},{3,2},{5,4},{6,5},{7,6},{9,8},{10,9},{11,10},{13,12},{... | collective-permute-start | bytes 196616 | tf_op jit(solution)/shard_map/ppermute | solution.py:281
  48.9 3.9 %collective-permute-start.10 = (f32[4,32,128]{2,1,0:T(8,128)S(1)}, f32[4,32,128]{2,1,0:T(8,128)S(1)}, u32[]{:S(2)}, u32[]{:S(2)}) collective-permute-start(f32[4,32,128]{2,1,0:T(8,128)S(1)} %pad_maximum_fusion.2), channel_id=1, source_target_pairs={{0,1},{1,2},{2,3},{4,5},{5,6},{6,7},{8,9},{9,10},{10,11},{12,13},{... | collective-permute-start | bytes 196616 | tf_op jit(solution)/shard_map/ppermute | solution.py:281
  57.3 3.0 %collective-permute-start.12 = (f32[48,128]{1,0:T(8,128)S(1)}, f32[48,128]{1,0:T(8,128)S(1)}, u32[]{:S(2)}, u32[]{:S(2)}) collective-permute-start(f32[48,128]{1,0:T(8,128)S(1)} %slice_select_fusion), channel_id=1, source_target_pairs={{0,1},{1,0},{2,3},{3,2},{4,5},{5,4},{6,7},{7,6},{8,9},{9,8},{10,11... | collective-permute-start | bytes 73736 | tf_op jit(solution)/shard_map/ppermute | solution.py:249
  60.3 4.4 %collective-permute-start.13 = (f32[48,128]{1,0:T(8,128)S(1)}, f32[48,128]{1,0:T(8,128)S(1)}, u32[]{:S(2)}, u32[]{:S(2)}) collective-permute-start(f32[48,128]{1,0:T(8,128)S(1)} %select_add_fusion), channel_id=1, source_target_pairs={{0,2},{1,3},{2,0},{3,1},{4,6},{5,7},{6,4},{7,5},{8,10},{9,11},{10,... | collective-permute-start | bytes 73736 | tf_op jit(solution)/shard_map/ppermute | solution.py:249
  64.7 4.2 %collective-permute-start.14 = (f32[48,128]{1,0:T(8,128)S(1)}, f32[48,128]{1,0:T(8,128)S(1)}, u32[]{:S(2)}, u32[]{:S(2)}) collective-permute-start(f32[48,128]{1,0:T(8,128)S(1)} %add.30), channel_id=1, source_target_pairs={{0,4},{4,0},{8,12},{12,8},{1,5},{5,1},{9,13},{13,9},{2,6},{6,2},{1... | collective-permute-start | bytes 73736 | tf_op jit(solution)/shard_map/ppermute | solution.py:249
  68.9 4.8 %collective-permute-start.15 = (f32[48,128]{1,0:T(8,128)S(1)}, f32[48,128]{1,0:T(8,128)S(1)}, u32[]{:S(2)}, u32[]{:S(2)}) collective-permute-start(f32[48,128]{1,0:T(8,128)S(1)} %add.31), channel_id=1, source_target_pairs={{0,8},{4,12},{8,0},{12,4},{1,9},{5,13},{9,1},{13,5},{2,10},{6,14},... | collective-permute-start | bytes 73736 | tf_op jit(solution)/shard_map/ppermute | solution.py:249
  73.7 1.2 %collective-permute-start.16 = (f32[48,128]{1,0:T(8,128)S(1)}, f32[48,128]{1,0:T(8,128)S(1)}, u32[]{:S(2)}, u32[]{:S(2)}) collective-permute-start(f32[48,128]{1,0:T(8,128)S(1)} %add.32), channel_id=1, source_target_pairs={{0,1},{1,0},{2,3},{3,2},{4,5},{5,4},{6,7},{7,6},{8,9},{9,8},{10,11... | collective-permute-start | bytes 73736 | tf_op jit(solution)/shard_map/ppermute | solution.py:249

commit v3 on v2

--- a/solution.py
+++ b/solution.py
@@ -131,7 +131,6 @@
 def weighted_kernel(
     inverse_rows,
     partial_ref,
-    other_ref,
     residual_low_ref,
     residual_high_ref,
     basis_ref,
@@ -142,14 +141,14 @@
     count_y = residual_low_ref.shape[0]
     tiles = 2 * count_y
     prior = basis_ref.shape[0] // tiles
-    coupling = (partial_ref[...] + other_ref[...]) * inverse_rows
+    coupling = partial_ref[...] * inverse_rows
     for tile in range(tiles):
         place = (tile // count_y, tile % count_y)
         moved = mul3(coupling, basis_ref[pl.ds(tile, prior, stride=tiles), :])
         (weighted_low_ref, weighted_high_ref)[place[0]][place[1]] = (
             (residual_low_ref, residual_high_ref)[place[0]][place[1]] - moved
         )
-    coupling_ref[...] = coupling.T
+    coupling_ref[...] = coupling
 
 
 def operators_kernel(
@@ -239,38 +238,19 @@
         new_ref[pl.ds(tile, block, stride=tiles), :] = mul3(inverse, own)
     for part in range(2):
         span = slice(part * block, (part + 1) * block)
-        from_basis = mul3(inverse, sums_ref[span, :] * inverse_rows)
-        reduced_ref[part, :prior, :] = from_basis.T
-        reduced_ref[part, prior:, :] = mul3_t(mul3(inverse, with_own[:, span]), inverse)
-
-
-def swap(value, axis, step):
-    count = lax.axis_size(axis)
-    return lax.ppermute(value, axis, [(i, i ^ step) for i in range(count)])
-
-
-def butterfly_steps():
-    steps = []
-    for axis in ("py", "px"):
-        step = 1
-        while step < lax.axis_size(axis):
-            steps.append((axis, step))
-            step *= 2
-    return steps
-
-
-def halved_sum(value):
-    half = value.shape[0] // 2
-    upper = lax.axis_index("py") % 2 == 1
-    first, second = value[:half], value[half:]
-    kept = jnp.where(upper, second, first)
-    kept = kept + swap(jnp.where(upper, first, second), "py", 1)
-    for axis, step in butterfly_steps()[1:]:
-        kept = kept + swap(kept, axis, step)
-    other = swap(kept, "py", 1)
-    return jnp.concatenate(
-        [jnp.where(upper, other, kept), jnp.where(upper, kept, other)], axis=0
-    )
+        reduced_ref[part, :, :prior] = mul3(inverse, sums_ref[span, :] * inverse_rows)
+        reduced_ref[part, :, prior:] = mul3_t(mul3_t(inverse, with_own[:, span]), inverse)
+
+
+def total_over_mesh(value):
+    axes = ("px", "py")
+    count = lax.axis_size(axes)
+    chunk = value.size // count
+    width = 128 if chunk % 128 == 0 else chunk
+    parts = lax.all_to_all(value.reshape(count, chunk // width, width), axes, 0, 0)
+    own = jnp.sum(parts, axis=0)
+    parts = lax.all_to_all(jnp.broadcast_to(own[None], parts.shape), axes, 0, 0)
+    return parts.reshape(value.shape)
 
 
 def line(value, axis, forward):
@@ -331,13 +311,10 @@
         [pltpu.VMEM((places, 2 * block, 2 * side), BF16)],
         smem=2,
     )
-    steps = butterfly_steps()
-    for axis, step in steps[:-1]:
-        partial = partial + swap(partial, axis, step)
     weighted_low, weighted_high, coupling = call(
         functools.partial(weighted_kernel, inverse_rows),
-        (partial, swap(partial, *steps[-1]), residual_low, residual_high, basis),
-        [shape(count_y, block, side)] * 2 + [shape(prior, block)],
+        (total_over_mesh(partial), residual_low, residual_high, basis),
+        [shape(count_y, block, side)] * 2 + [shape(block, prior)],
     )
     (sums,) = call(
         operators_kernel,
@@ -357,14 +334,19 @@
     )
     new_block, factor, reduced = call(
         functools.partial(factor_kernel, inverse_rows),
-        (halved_sum(sums), weighted_low, weighted_high),
+        (total_over_mesh(sums), weighted_low, weighted_high),
         [
             shape(block * tiles, side),
             shape(block, block),
-            shape(2, prior + block, block),
+            shape(2, block, prior + block),
         ],
     )
-    return (new_block.reshape(previous.shape), coupling, factor, reduced)
+    return (
+        new_block.reshape(previous.shape),
+        coupling.T,
+        factor,
+        reduced.swapaxes(1, 2),
+    )
 
 
 def solution(mesh):

time: 79.8 us -> 92.3 us (1.16)
  blocking collectives: 0 us -> 46.9 us
  starting transfers between devices: 39.2 us -> 18 us
  waiting for transfers between devices: 22.1 us -> 10.3 us
  local copies, waits for them, and re-layouts: 4.84 us -> 2.81 us
    all_to_all x0 -> x4, blocking collectives: none -> 46.9 us  [the longest x2 28.3 us: total_over_mesh(): lax.all_to_all(value.reshape(count, chunk // width, width), axes, 0, 0)]
    ppermute x9 -> x0, starting transfers between devices: 18.4 us -> none  [swap(): return lax.ppermute(value, axis, [(i, i ^ step) for i in range(count)])]
    ppermute x9 -> x0, waiting for transfers between devices: 13.5 us -> none  [swap(): return lax.ppermute(value, axis, [(i, i ^ step) for i in range(count)])]
    ppermute x8, starting transfers between devices: 20.8 us -> 18 us  [line(): return lax.ppermute(value, axis, pairs)]
    unnamed x16 -> x14, local copies, waits for them, and re-layouts: 4.64 us -> 2.56 us
    ppermute x8, waiting for transfers between devices: 8.53 us -> 10.3 us  [line(): return lax.ppermute(value, axis, pairs)]
  transfers between devices with their start and end apart: 17 -> 8, of which waited for: 14 -> 6; matrix products, arithmetic and copies ran while one was open for 2% -> 1% of each run, Pallas kernels for 0% -> 0%
where the time goes in v3:
time: 92.3 us; the launch traced here: 91.7 us
  blocking collectives  46.9 us (51%)
  starting transfers between devices  18 us (20%)
  Pallas kernels  12.2 us (13%)
  waiting for transfers between devices  10.3 us (11%)
  local copies, waits for them, and re-layouts  2.81 us (3%)
    all_to_all x2, blocking collectives, total_over_mesh(): lax.all_to_all(value.reshape(count, chunk // width, width), axes, 0, 0)  28.3 us
    all_to_all x2, blocking collectives, total_over_mesh(): parts = lax.all_to_all(jnp.broadcast_to(own[None], parts.shape), axes, 0, 0)  18.5 us
    ppermute x8, starting transfers between devices, line(): return lax.ppermute(value, axis, pairs)  18 us
    pallas_call x6, Pallas kernels, call(): pl.pallas_call(kernel, out_shape=outputs, in_specs=[SMEM] * smem + [VMEM]...  12.2 us
    ppermute x8, waiting for transfers between devices, line(): return lax.ppermute(value, axis, pairs)  10.3 us
    unnamed x14, local copies, waits for them, and re-layouts  2.56 us
  transfers between devices with their start and end apart: 8, of which 6 were waited for; matrix products, arithmetic and copies ran while one was open for 1% of the time, Pallas kernels for 0%

profile of v3, /device:TPU:0, one launch (start us, length us, event | category | flops | bytes accessed | tf_op | source)
XLA Modules:
  0.0 91.7 jit_solution(17754550698456335873)
XLA Ops:
  0.6 0.0 copy-start
  0.6 1.0 %copy-done = f32[128,2,4,128]{3,2,1,0:T(4,128)S(1)} copy-done((f32[128,2,4,128]{3,2,1,0:T(4,128)S(1)}, f32[128,2,4,128]{3,2,1,0:T(4,128)}, u32[]{:S(2)}) %copy-start) | copy-done | bytes 524312
  1.7 0.0 copy-start.4
  1.7 0.9 copy-done.4
  2.6 1.3 %collective-permute-start.1 = (f32[4,64,128]{2,1,0:T(8,128)S(1)}, f32[4,64,128]{2,1,0:T(8,128)S(1)}, u32[]{:S(2)}, u32[]{:S(2)}) collective-permute-start(f32[4,64,128]{2,1,0:T(8,128)S(1)} %get-tuple-element.17.low_ref), channel_id=1, source_target_pairs={{4,0},{8,4},{12,8},{5,1},{9,5},{13,9},{6,2},{10,6},{14,10},{7,3},{... | collective-permute-start | bytes 393224 | tf_op jit(solution)/shard_map/ppermute | solution.py:261
  3.9 0.0 copy-start.2
  3.9 0.0 copy-start.3
  4.0 5.7 %collective-permute-start = (f32[4,64,128]{2,1,0:T(8,128)S(1)}, f32[4,64,128]{2,1,0:T(8,128)S(1)}, u32[]{:S(2)}, u32[]{:S(2)}) collective-permute-start(f32[4,64,128]{2,1,0:T(8,128)S(1)} %get-tuple-element.18.high_ref), channel_id=1, source_target_pairs={{0,4},{4,8},{8,12},{1,5},{5,9},{9,13},{2,6},{6,10},{10,14},{3,7},{... | collective-permute-start | bytes 393224 | tf_op jit(solution)/shard_map/ppermute | solution.py:261
  9.7 1.4 %collective-permute-done.1.from_high_ref = f32[4,64,128]{2,1,0:T(8,128)S(1)} collective-permute-done((f32[4,64,128]{2,1,0:T(8,128)S(1)}, f32[4,64,128]{2,1,0:T(8,128)S(1)}, u32[]{:S(2)}, u32[]{:S(2)}) %collective-permute-start.1) | collective-permute-done | bytes 131104 | tf_op jit(solution)/shard_map/ppermute | solution.py:261
  11.1 1.3 %collective-permute-done.from_low_ref = f32[4,64,128]{2,1,0:T(8,128)S(1)} collective-permute-done((f32[4,64,128]{2,1,0:T(8,128)S(1)}, f32[4,64,128]{2,1,0:T(8,128)S(1)}, u32[]{:S(2)}, u32[]{:S(2)}) %collective-permute-start) | collective-permute-done | bytes 131104 | tf_op jit(solution)/shard_map/ppermute | solution.py:261
  12.4 1.3 %collective-permute-start.2 = (f32[4,64,128]{2,1,0:T(8,128)S(1)}, f32[4,64,128]{2,1,0:T(8,128)S(1)}, u32[]{:S(2)}, u32[]{:S(2)}) collective-permute-start(f32[4,64,128]{2,1,0:T(8,128)S(1)} %pad_maximum_fusion), channel_id=1, source_target_pairs={{0,1},{1,2},{2,3},{4,5},{5,6},{6,7},{8,9},{9,10},{10,11},{12,13},{... | collective-permute-start | bytes 393224 | tf_op jit(solution)/shard_map/ppermute | solution.py:261
  13.7 0.0 copy-start.5
  13.7 0.7 pad_maximum_fusion.1
  14.4 1.3 %collective-permute-start.3 = (f32[4,64,128]{2,1,0:T(8,128)}, f32[4,64,128]{2,1,0:T(8,128)S(1)}, u32[]{:S(2)}, u32[]{:S(2)}) collective-permute-start(f32[4,64,128]{2,1,0:T(8,128)} %pad_maximum_fusion.1), channel_id=1, source_target_pairs={{1,0},{2,1},{3,2},{5,4},{6,5},{7,6},{9,8},{10,9},{11,10},{13,12},{... | collective-permute-start | bytes 393224 | tf_op jit(solution)/shard_map/ppermute | solution.py:261
  15.7 0.0 copy-done.5
  15.7 0.0 copy-start.6
  15.7 0.1 copy.16.neighbours_ref
  15.8 0.6 copy-done.6
  16.4 0.1 copy.17.kinds_ref
  16.5 0.0 copy-done.2
  16.5 0.0 copy-done.3
  16.5 0.0 copy-start.1
  16.5 0.1 shard_map.94
  16.6 0.0 collective-permute-done.2.side_low_ref
  16.6 3.2 %collective-permute-done.3.side_high_ref = f32[4,64,128]{2,1,0:T(8,128)S(1)} collective-permute-done((f32[4,64,128]{2,1,0:T(8,128)}, f32[4,64,128]{2,1,0:T(8,128)S(1)}, u32[]{:S(2)}, u32[]{:S(2)}) %collective-permute-start.3) | collective-permute-done | bytes 131104 | tf_op jit(solution)/shard_map/ppermute | solution.py:261
  19.8 0.0 copy-done.1
  19.8 2.9 %shard_map.95 = (f32[4,32,128]{2,1,0:T(8,128)S(1)}, f32[4,32,128]{2,1,0:T(8,128)S(1)}, f32[32,128]{1,0:T(8,128)S(1)}) custom-call(s32[5,8]{1,0:T(8,128)S(1)} %copy.16.neighbours_ref, s32[5,8]{1,0:T(8,128)S(1)} %copy.17.kinds_ref, f32[4,64,128]{2,1,0:T(8,128)S(1)} %get-tuple-element.17.low_ref, f32[4,64,128]{2,1,0:T(8,128)S(1)} %get-tuple-element.18.high_ref, ...), custom_call_target="tpu_custom_call" | custom-call | tf_op jit(solution)/shard_map/pallas_call | solution.py:288
  22.7 15.3 %all_to_all.20 = f32[16,2,128]{2,1,0:T(2,128)S(1)} all-to-all(f32[16,2,128]{2,1,0:T(2,128)S(1)} %bitcast.15), channel_id=1, replica_groups=mesh['case'=2,'px'=4,'py'=4] {'px','py'}, dimensions={0} | all-to-all | bytes 32768 | tf_op jit(solution)/shard_map/all_to_all | solution.py:250
  38.0 9.1 %all_to_all.21 = f32[16,2,128]{2,1,0:T(2,128)S(1)} all-to-all(f32[16,2,128]{2,1,0:T(2,128)S(1)} %broadcast_in_dim.4), channel_id=1, replica_groups=mesh['case'=2,'px'=4,'py'=4] {'px','py'}, dimensions={0} | all-to-all | bytes 32768 | tf_op jit(solution)/shard_map/all_to_all | solution.py:252
  47.1 0.6 shard_map.96
  47.7 1.3 %collective-permute-start.5 = (f32[4,32,128]{2,1,0:T(8,128)S(1)}, f32[4,32,128]{2,1,0:T(8,128)S(1)}, u32[]{:S(2)}, u32[]{:S(2)}) collective-permute-start(f32[4,32,128]{2,1,0:T(8,128)S(1)} %get-tuple-element.24.low_ref.weighted_low_ref), channel_id=1, source_target_pairs={{4,0},{8,4},{12,8},{5,1},{9,5},{13,9},{6,2},{10,6},{14,10},{7,3},{... | collective-permute-start | bytes 196616 | tf_op jit(solution)/shard_map/ppermute | solution.py:261
  49.0 4.5 %collective-permute-start.4 = (f32[4,32,128]{2,1,0:T(8,128)S(1)}, f32[4,32,128]{2,1,0:T(8,128)S(1)}, u32[]{:S(2)}, u32[]{:S(2)}) collective-permute-start(f32[4,32,128]{2,1,0:T(8,128)S(1)} %get-tuple-element.25.high_ref.weighted_high_ref), channel_id=1, source_target_pairs={{0,4},{4,8},{8,12},{1,5},{5,9},{9,13},{2,6},{6,10},{10,14},{3,7},{... | collective-permute-start | bytes 196616 | tf_op jit(solution)/shard_map/ppermute | solution.py:261
  53.6 0.3 collective-permute-done.5.from_high_ref
  53.9 1.6 %collective-permute-done.4.from_low_ref = f32[4,32,128]{2,1,0:T(8,128)S(1)} collective-permute-done((f32[4,32,128]{2,1,0:T(8,128)S(1)}, f32[4,32,128]{2,1,0:T(8,128)S(1)}, u32[]{:S(2)}, u32[]{:S(2)}) %collective-permute-start.4) | collective-permute-done | bytes 65568 | tf_op jit(solution)/shard_map/ppermute | solution.py:261
  55.5 1.3 %collective-permute-start.6 = (f32[4,32,128]{2,1,0:T(8,128)S(1)}, f32[4,32,128]{2,1,0:T(8,128)S(1)}, u32[]{:S(2)}, u32[]{:S(2)}) collective-permute-start(f32[4,32,128]{2,1,0:T(8,128)S(1)} %pad_maximum_fusion.2), channel_id=1, source_target_pairs={{0,1},{1,2},{2,3},{4,5},{5,6},{6,7},{8,9},{9,10},{10,11},{12,13},{... | collective-permute-start | bytes 196616 | tf_op jit(solution)/shard_map/ppermute | solution.py:261
  56.8 1.3 %collective-permute-start.7 = (f32[4,32,128]{2,1,0:T(8,128)S(1)}, f32[4,32,128]{2,1,0:T(8,128)S(1)}, u32[]{:S(2)}, u32[]{:S(2)}) collective-permute-start(f32[4,32,128]{2,1,0:T(8,128)S(1)} %pad_maximum_fusion.3), channel_id=1, source_target_pairs={{1,0},{2,1},{3,2},{5,4},{6,5},{7,6},{9,8},{10,9},{11,10},{13,12},{... | collective-permute-start | bytes 196616 | tf_op jit(solution)/shard_map/ppermute | solution.py:261
  58.1 0.0 collective-permute-done.6.side_low_ref
  58.1 2.5 %collective-permute-done.7.side_high_ref = f32[4,32,128]{2,1,0:T(8,128)S(1)} collective-permute-done((f32[4,32,128]{2,1,0:T(8,128)S(1)}, f32[4,32,128]{2,1,0:T(8,128)S(1)}, u32[]{:S(2)}, u32[]{:S(2)}) %collective-permute-start.7) | collective-permute-done | bytes 65568 | tf_op jit(solution)/shard_map/ppermute | solution.py:261
  60.6 4.5 %shard_map.97 = f32[96,128]{1,0:T(8,128)S(1)} custom-call(s32[5,8]{1,0:T(8,128)S(1)} %copy.16.neighbours_ref, s32[5,8]{1,0:T(8,128)S(1)} %copy.17.kinds_ref, f32[4,32,128]{2,1,0:T(8,128)S(1)} %get-tuple-element.24.low_ref.weighted_low_ref, f32[4,32,128]{2,1,0:T(8,128)S(1)} %get-tuple-element.25.high_ref.weighted_high_ref, ...), custom_call_target="tpu_custom_call" | custom-call | tf_op jit(solution)/shard_map/pallas_call | solution.py:288
  65.1 13.0 %all_to_all.22 = f32[16,6,128]{2,1,0:T(8,128)S(1)} all-to-all(f32[16,6,128]{2,1,0:T(8,128)S(1)} %reshape.43), channel_id=1, replica_groups=mesh['case'=2,'px'=4,'py'=4] {'px','py'}, dimensions={0} | all-to-all | bytes 98304 | tf_op jit(solution)/shard_map/all_to_all | solution.py:250
  78.2 9.5 %all_to_all.23 = f32[16,6,128]{2,1,0:T(8,128)S(1)} all-to-all(f32[16,6,128]{2,1,0:T(8,128)S(1)} %broadcast_in_dim.5), channel_id=1, replica_groups=mesh['case'=2,'px'=4,'py'=4] {'px','py'}, dimensions={0} | all-to-all | bytes 98304 | tf_op jit(solution)/shard_map/all_to_all | solution.py:252
  87.7 4.1 %shard_map.98 = (f32[256,128]{1,0:T(8,128)}, f32[32,32]{1,0:T(8,128)}, f32[2,32,160]{2,1,0:T(8,128)}) custom-call(f32[96,128]{1,0:T(8,128)S(1)} %reshape.44.sums_ref, f32[4,32,128]{2,1,0:T(8,128)S(1)} %get-tuple-element.24.low_ref.weighted_low_ref, f32[4,32,128]{2,1,0:T(8,128)S(1)} %get-tuple-element.25.high_ref.weighted_high_ref), custom_call_target="tpu_custom_call" | custom-call | tf_op jit(solution)/shard_map/pallas_call | solution.py:288
  (17 shorter events, 0.2 us)
Async XLA Ops:
  0.6 1.0 %copy-start = (f32[128,2,4,128]{3,2,1,0:T(4,128)S(1)}, f32[128,2,4,128]{3,2,1,0:T(4,128)}, u32[]{:S(2)}) copy-start(f32[128,2,4,128]{3,2,1,0:T(4,128)} %param.6) | copy-start | bytes 1572868
  1.7 0.9 copy-start.4
  2.6 8.4 %collective-permute-start.1 = (f32[4,64,128]{2,1,0:T(8,128)S(1)}, f32[4,64,128]{2,1,0:T(8,128)S(1)}, u32[]{:S(2)}, u32[]{:S(2)}) collective-permute-start(f32[4,64,128]{2,1,0:T(8,128)S(1)} %get-tuple-element.17.low_ref), channel_id=1, source_target_pairs={{4,0},{8,4},{12,8},{5,1},{9,5},{13,9},{6,2},{10,6},{14,10},{7,3},{... | collective-permute-start | bytes 393224 | tf_op jit(solution)/shard_map/ppermute | solution.py:261
  3.9 12.5 %copy-start.2 = (f32[8,128,128]{2,1,0:T(8,128)S(1)}, f32[8,128,128]{2,1,0:T(8,128)}, u32[]{:S(2)}) copy-start(f32[8,128,128]{2,1,0:T(8,128)} %stiff_ref.1) | copy-start | bytes 1572868
  3.9 12.5 %copy-start.3 = (f32[8,128,128]{2,1,0:T(8,128)S(1)}, f32[8,128,128]{2,1,0:T(8,128)}, u32[]{:S(2)}) copy-start(f32[8,128,128]{2,1,0:T(8,128)} %mass_ref.1) | copy-start | bytes 1572868
  4.0 8.4 %collective-permute-start = (f32[4,64,128]{2,1,0:T(8,128)S(1)}, f32[4,64,128]{2,1,0:T(8,128)S(1)}, u32[]{:S(2)}, u32[]{:S(2)}) collective-permute-start(f32[4,64,128]{2,1,0:T(8,128)S(1)} %get-tuple-element.18.high_ref), channel_id=1, source_target_pairs={{0,4},{4,8},{8,12},{1,5},{5,9},{9,13},{2,6},{6,10},{10,14},{3,7},{... | collective-permute-start | bytes 393224 | tf_op jit(solution)/shard_map/ppermute | solution.py:261
  12.4 4.2 %collective-permute-start.2 = (f32[4,64,128]{2,1,0:T(8,128)S(1)}, f32[4,64,128]{2,1,0:T(8,128)S(1)}, u32[]{:S(2)}, u32[]{:S(2)}) collective-permute-start(f32[4,64,128]{2,1,0:T(8,128)S(1)} %pad_maximum_fusion), channel_id=1, source_target_pairs={{0,1},{1,2},{2,3},{4,5},{5,6},{6,7},{8,9},{9,10},{10,11},{12,13},{... | collective-permute-start | bytes 393224 | tf_op jit(solution)/shard_map/ppermute | solution.py:261
  13.7 2.0 %copy-start.5 = (s32[5,2,4]{0,2,1:T(4,128)S(1)}, s32[5,2,4]{0,2,1:T(4,128)}, u32[]{:S(2)}) copy-start(s32[5,2,4]{0,2,1:T(4,128)} %param.8) | copy-start | bytes 484
  14.4 5.4 %collective-permute-start.3 = (f32[4,64,128]{2,1,0:T(8,128)}, f32[4,64,128]{2,1,0:T(8,128)S(1)}, u32[]{:S(2)}, u32[]{:S(2)}) collective-permute-start(f32[4,64,128]{2,1,0:T(8,128)} %pad_maximum_fusion.1), channel_id=1, source_target_pairs={{1,0},{2,1},{3,2},{5,4},{6,5},{7,6},{9,8},{10,9},{11,10},{13,12},{... | collective-permute-start | bytes 393224 | tf_op jit(solution)/shard_map/ppermute | solution.py:261
  15.7 0.7 copy-start.6
  16.5 3.3 %copy-start.1 = (f32[128,2,4,128]{3,2,1,0:T(4,128)S(1)}, f32[128,2,4,128]{3,2,1,0:T(4,128)}, u32[]{:S(2)}) copy-start(f32[128,2,4,128]{3,2,1,0:T(4,128)} %param.6) | copy-start | bytes 1572868
  47.7 6.1 %collective-permute-start.5 = (f32[4,32,128]{2,1,0:T(8,128)S(1)}, f32[4,32,128]{2,1,0:T(8,128)S(1)}, u32[]{:S(2)}, u32[]{:S(2)}) collective-permute-start(f32[4,32,128]{2,1,0:T(8,128)S(1)} %get-tuple-element.24.low_ref.weighted_low_ref), channel_id=1, source_target_pairs={{4,0},{8,4},{12,8},{5,1},{9,5},{13,9},{6,2},{10,6},{14,10},{7,3},{... | collective-permute-start | bytes 196616 | tf_op jit(solution)/shard_map/ppermute | solution.py:261
  49.0 6.4 %collective-permute-start.4 = (f32[4,32,128]{2,1,0:T(8,128)S(1)}, f32[4,32,128]{2,1,0:T(8,128)S(1)}, u32[]{:S(2)}, u32[]{:S(2)}) collective-permute-start(f32[4,32,128]{2,1,0:T(8,128)S(1)} %get-tuple-element.25.high_ref.weighted_high_ref), channel_id=1, source_target_pairs={{0,4},{4,8},{8,12},{1,5},{5,9},{9,13},{2,6},{6,10},{10,14},{3,7},{... | collective-permute-start | bytes 196616 | tf_op jit(solution)/shard_map/ppermute | solution.py:261
  55.5 2.6 %collective-permute-start.6 = (f32[4,32,128]{2,1,0:T(8,128)S(1)}, f32[4,32,128]{2,1,0:T(8,128)S(1)}, u32[]{:S(2)}, u32[]{:S(2)}) collective-permute-start(f32[4,32,128]{2,1,0:T(8,128)S(1)} %pad_maximum_fusion.2), channel_id=1, source_target_pairs={{0,1},{1,2},{2,3},{4,5},{5,6},{6,7},{8,9},{9,10},{10,11},{12,13},{... | collective-permute-start | bytes 196616 | tf_op jit(solution)/shard_map/ppermute | solution.py:261
  56.8 3.8 %collective-permute-start.7 = (f32[4,32,128]{2,1,0:T(8,128)S(1)}, f32[4,32,128]{2,1,0:T(8,128)S(1)}, u32[]{:S(2)}, u32[]{:S(2)}) collective-permute-start(f32[4,32,128]{2,1,0:T(8,128)S(1)} %pad_maximum_fusion.3), channel_id=1, source_target_pairs={{1,0},{2,1},{3,2},{5,4},{6,5},{7,6},{9,8},{10,9},{11,10},{13,12},{... | collective-permute-start | bytes 196616 | tf_op jit(solution)/shard_map/ppermute | solution.py:261

commit v4 on v3

--- a/solution.py
+++ b/solution.py
@@ -41,24 +41,30 @@
     )
 
 
-def tables_kernel(stiff_ref, mass_ref, high_ref, low_ref):
+def tables_kernel(stiff_ref, mass_ref, deep_high_ref, deep_low_ref, wide_high_ref, wide_low_ref):
     side = stiff_ref.shape[1]
     for kind in range(stiff_ref.shape[0]):
         for place, ref in enumerate((stiff_ref, mass_ref)):
             high, low = split(ref[kind])
-            high_ref[kind, place * side : (place + 1) * side, :] = high
-            low_ref[kind, place * side : (place + 1) * side, :] = low
-
-
-def pack_kernel(count_x, count_y, basis_ref, previous_ref, low_ref, high_ref):
+            span = slice(place * side, (place + 1) * side)
+            deep_high_ref[kind, span, :] = high
+            deep_low_ref[kind, span, :] = low
+            wide_high_ref[kind, :, span] = high
+            wide_low_ref[kind, :, span] = low
+
+
+def pack_kernel(
+    count_x, count_y, basis_ref, previous_ref, low_ref, high_ref, low_rest_ref, high_rest_ref
+):
     tiles = count_x * count_y
     block = previous_ref.shape[0] // tiles
-    first = basis_ref.shape[0] - block * tiles
-    for row, ref in ((0, low_ref), (count_x - 1, high_ref)):
+    rest = low_rest_ref.shape[1]
+    for row, ref, rest_ref in ((0, low_ref, low_rest_ref), (count_x - 1, high_ref, high_rest_ref)):
         for j in range(count_y):
             tile = row * count_y + j
-            ref[j, :block, :] = basis_ref[pl.ds(first + tile, block, stride=tiles), :]
+            ref[j, :block, :] = basis_ref[pl.ds(rest * tiles + tile, block, stride=tiles), :]
             ref[j, block:, :] = previous_ref[pl.ds(tile, block, stride=tiles), :]
+            rest_ref[j] = basis_ref[pl.ds(tile, rest, stride=tiles), :]
 
 
 def fill_extended(ext_ref, store, rows, sides):
@@ -89,8 +95,8 @@
     basis_ref,
     table_high_ref,
     table_low_ref,
-    residual_low_ref,
-    residual_high_ref,
+    message_low_ref,
+    message_high_ref,
     partial_ref,
     ext_ref,
 ):
@@ -123,80 +129,110 @@
             total = total + (
                 both[:block] + (both[block:] + mul(chosen[:block], table_low_ref[kind]))
             )
-        (residual_low_ref, residual_high_ref)[tile // count_y][tile % count_y] = total
+        (message_low_ref, message_high_ref)[tile // count_y][tile % count_y] = total
         partial = partial + mul3_t(total, basis_ref[pl.ds(tile, prior, stride=tiles), :])
     partial_ref[...] = partial
-
-
-def weighted_kernel(
+    message_low_ref[count_y] = partial
+    message_high_ref[count_y] = partial
+
+
+def sides_kernel(
+    ends_ref, low_ref, high_ref, from_low_ref, from_high_ref, partial_ref, side_low_ref, side_high_ref
+):
+    last = low_ref.shape[0] - 2
+    keep_low = ends_ref[0].astype(F32)
+    keep_high = ends_ref[1].astype(F32)
+    for ref, j in ((side_low_ref, 0), (side_high_ref, last)):
+        ref[0] = from_low_ref[j] * keep_low
+        ref[1] = low_ref[j]
+        ref[2] = high_ref[j]
+        ref[3] = from_high_ref[j] * keep_high
+        ref[4] = partial_ref[...]
+
+
+def operators_kernel(
     inverse_rows,
-    partial_ref,
-    residual_low_ref,
-    residual_high_ref,
-    basis_ref,
-    weighted_low_ref,
-    weighted_high_ref,
-    coupling_ref,
-):
-    count_y = residual_low_ref.shape[0]
-    tiles = 2 * count_y
-    prior = basis_ref.shape[0] // tiles
-    coupling = partial_ref[...] * inverse_rows
-    for tile in range(tiles):
-        place = (tile // count_y, tile % count_y)
-        moved = mul3(coupling, basis_ref[pl.ds(tile, prior, stride=tiles), :])
-        (weighted_low_ref, weighted_high_ref)[place[0]][place[1]] = (
-            (residual_low_ref, residual_high_ref)[place[0]][place[1]] - moved
-        )
-    coupling_ref[...] = coupling
-
-
-def operators_kernel(
+    ends_ref,
     neighbours_ref,
     kinds_ref,
+    partial_ref,
     low_ref,
     high_ref,
     from_low_ref,
     from_high_ref,
     side_low_ref,
     side_high_ref,
+    block_from_low_ref,
+    block_from_high_ref,
+    block_side_low_ref,
+    block_side_high_ref,
+    rest_from_low_ref,
+    rest_from_high_ref,
+    rest_side_low_ref,
+    rest_side_high_ref,
     basis_ref,
     table_high_ref,
     table_low_ref,
+    weighted_low_ref,
+    weighted_high_ref,
+    coupling_ref,
     sums_ref,
     ext_ref,
 ):
-    count_y, block, side = low_ref.shape
+    count_y, block, side = weighted_low_ref.shape
     tiles = 2 * count_y
     prior = basis_ref.shape[0] // tiles
-
-    def store(ext, place, value):
+    wide = count_y + 2
+    coupling = partial_ref[...] * inverse_rows
+    coupling_ref[...] = coupling
+    coupling_high, coupling_low = split(coupling)
+
+    def moved(basis_tile):
+        high, low = split(basis_tile)
+        return mul(coupling_high, high) + (mul(coupling_high, low) + mul(coupling_low, high))
+
+    def store(place, value):
         high, low = split(value)
-        ext[place, :block, :] = high
-        ext[place, block:, :] = low
-
-    fill_extended(
-        ext_ref,
-        store,
-        (from_low_ref, low_ref, high_ref, from_high_ref),
-        (side_low_ref, side_high_ref),
-    )
+        ext_ref[place, :block, :] = high
+        ext_ref[place, block:, :] = low
+
+    for tile in range(tiles):
+        i, j = tile // count_y, tile % count_y
+        value = (low_ref, high_ref)[i][j] - moved(basis_ref[pl.ds(tile, prior, stride=tiles), :])
+        (weighted_low_ref, weighted_high_ref)[i][j] = value
+        store((i + 1) * wide + j + 1, value)
+    outside = [
+        (j + 1, from_low_ref, block_from_low_ref, rest_from_low_ref, j, 0)
+        for j in range(count_y)
+    ]
+    outside += [
+        (3 * wide + j + 1, from_high_ref, block_from_high_ref, rest_from_high_ref, j, 1)
+        for j in range(count_y)
+    ]
+    outside += [
+        (i * wide, side_low_ref, block_side_low_ref, rest_side_low_ref, i, 2) for i in range(4)
+    ]
+    outside += [
+        (i * wide + wide - 1, side_high_ref, block_side_high_ref, rest_side_high_ref, i, 3)
+        for i in range(4)
+    ]
+    for place, ref, block_ref, rest_ref, at, end in outside:
+        basis_tile = jnp.concatenate([rest_ref[at], block_ref[at, :block]], axis=0)
+        store(place, ref[at] * ends_ref[end].astype(F32) - moved(basis_tile))
     with_basis = jnp.zeros((2 * block, prior), F32)
     with_own = jnp.zeros((block, 4 * block), F32)
     for tile in range(tiles):
-        own = (low_ref, high_ref)[tile // count_y][tile % count_y]
-        totals = [4.0 * own, own]
+        own = (weighted_low_ref, weighted_high_ref)[tile // count_y][tile % count_y]
+        totals = jnp.concatenate([4.0 * own, own], axis=1)
         for k in range(neighbours_ref.shape[0]):
             source = source_of(neighbours_ref, k, tile, count_y)
             kind = kinds_ref[k, tile]
             chosen = ext_ref[source]
-            for part in range(2):
-                span = slice(part * side, (part + 1) * side)
-                both = mul(chosen, table_high_ref[kind, span, :])
-                totals[part] = totals[part] + (
-                    both[:block] + (both[block:] + mul(chosen[:block], table_low_ref[kind, span, :]))
-                )
-        applied = jnp.concatenate(totals, axis=0)
+            both = mul(chosen, table_high_ref[kind])
+            totals = totals + (
+                both[:block] + (both[block:] + mul(chosen[:block], table_low_ref[kind]))
+            )
+        applied = jnp.concatenate([totals[:, :side], totals[:, side:]], axis=0)
         with_basis = with_basis + mul3_t(applied, basis_ref[pl.ds(tile, prior, stride=tiles), :])
         right = jnp.concatenate([applied, own, jnp.zeros_like(own)], axis=0)
         with_own = with_own + mul3_t(own, right)
@@ -223,14 +259,20 @@
     unit = jnp.where(row_ids == column_ids, 1.0, 0.0).astype(F32)
     work = jnp.concatenate([gram, unit], axis=1)
     rows = lax.broadcasted_iota(jnp.int32, (block, 1), 0)
-    scale = jnp.zeros((block, 1), F32)
-    for j in range(block):
-        row = work[j : j + 1, :]
-        pivot = row[:, j : j + 1]
-        ratio = work[:, j : j + 1] / pivot
-        scale = jnp.where(rows == j, lax.rsqrt(pivot), scale)
-        work = work - jnp.where(rows > j, ratio, 0.0) * row
-    work = work * scale
+    for j in range(0, block, 2):
+        first, second = work[j : j + 1, :], work[j + 1 : j + 2, :]
+        inverse_first = 1.0 / first[:, j : j + 1]
+        across = first[:, j + 1 : j + 2]
+        ratio = second[:, j : j + 1] * inverse_first
+        second = second - ratio * first
+        inverse_second = 1.0 / second[:, j + 1 : j + 2]
+        first_ratio = work[:, j : j + 1] * inverse_first
+        second_ratio = (work[:, j + 1 : j + 2] - first_ratio * across) * inverse_second
+        work = work - (
+            jnp.where(rows > j, first_ratio, 0.0) * first
+            + jnp.where(rows > j + 1, second_ratio, 0.0) * second
+        )
+    work = work * lax.rsqrt(jnp.sum(work[:, :block] * unit, axis=1, keepdims=True))
     factor_ref[...] = jnp.where(column_ids >= row_ids, work[:, :block], 0.0)
     inverse = work[:, block:]
     for tile in range(tiles):
@@ -242,15 +284,47 @@
         reduced_ref[part, :, prior:] = mul3_t(mul3_t(inverse, with_own[:, span]), inverse)
 
 
-def total_over_mesh(value):
-    axes = ("px", "py")
-    count = lax.axis_size(axes)
-    chunk = value.size // count
-    width = 128 if chunk % 128 == 0 else chunk
-    parts = lax.all_to_all(value.reshape(count, chunk // width, width), axes, 0, 0)
-    own = jnp.sum(parts, axis=0)
-    parts = lax.all_to_all(jnp.broadcast_to(own[None], parts.shape), axes, 0, 0)
-    return parts.reshape(value.shape)
+def swap(value, axis, step):
+    count = lax.axis_size(axis)
+    return lax.ppermute(value, axis, [(i, i ^ step) for i in range(count)])
+
+
+def shift(value, axis, step):
+    count = lax.axis_size(axis)
+    return lax.ppermute(value, axis, [(i, (i + step) % count) for i in range(count)])
+
+
+def total_along(value, axis, first=1):
+    if lax.axis_size(axis) == 4 and first == 1:
+        opposite = shift(value, axis, 2)
+        return (value + opposite) + (shift(value, axis, 1) + shift(value, axis, -1))
+    step = first
+    while step < lax.axis_size(axis):
+        value = value + swap(value, axis, step)
+        step *= 2
+    return value
+
+
+def halved_total(value):
+    half = value.shape[0] // 2
+    upper = lax.axis_index("py") % 2 == 1
+    first, second = value[:half], value[half:]
+    kept = jnp.where(upper, second, first)
+    kept = kept + swap(jnp.where(upper, first, second), "py", 1)
+    kept = total_along(kept, "py", 2)
+    kept = total_along(kept, "px")
+    other = swap(kept, "py", 1)
+    return jnp.concatenate(
+        [jnp.where(upper, other, kept), jnp.where(upper, kept, other)], axis=0
+    )
+
+
+def halo_and_total(low, high, partial, axis):
+    if lax.axis_size(axis) == 4:
+        from_low, from_high = shift(high, axis, 1), shift(low, axis, -1)
+        opposite = shift(partial, axis, 2)
+        return from_low, from_high, (partial + opposite) + (from_low[-1] + from_high[-1])
+    return line(high, axis, True), line(low, axis, False), total_along(partial, axis)
 
 
 def line(value, axis, forward):
@@ -261,13 +335,16 @@
     return lax.ppermute(value, axis, pairs)
 
 
-def halo(low, high):
-    from_low = line(high, "px", True)
-    from_high = line(low, "px", False)
+def sides(low, high, from_low, from_high):
     rows = (from_low, low, high, from_high)
-    side_low = line(jnp.concatenate([row[-1:] for row in rows], axis=0), "py", True)
-    side_high = line(jnp.concatenate([row[:1] for row in rows], axis=0), "py", False)
-    return from_low, from_high, side_low, side_high
+    return (
+        jnp.concatenate([row[:1] for row in rows], axis=0),
+        jnp.concatenate([row[-1:] for row in rows], axis=0),
+    )
+
+
+def halo(low, high, axis):
+    return line(high, axis, True), line(low, axis, False)
 
 
 def shape(*dims, dtype=F32):
@@ -294,47 +371,83 @@
             compiler_params=PARAMS,
         )(*inputs)
 
-    low, high = call(
+    low, high, low_rest, high_rest = call(
         functools.partial(pack_kernel, count_x, count_y),
         (basis, previous.reshape(-1, side)),
-        [shape(count_y, 2 * block, side)] * 2,
-    )
-    table_high, table_low = call(
+        [shape(count_y, 2 * block, side)] * 2 + [shape(count_y, prior - block, side)] * 2,
+    )
+    kinds = stiff_tiles.shape[0]
+    deep_high, deep_low, wide_high, wide_low = call(
         tables_kernel,
         (stiff_tiles, mass_tiles),
-        [shape(stiff_tiles.shape[0], 2 * side, side, dtype=BF16)] * 2,
-    )
-    residual_low, residual_high, partial = call(
+        [shape(kinds, 2 * side, side, dtype=BF16)] * 2
+        + [shape(kinds, side, 2 * side, dtype=BF16)] * 2,
+    )
+    ends = []
+    for axis in ("px", "py"):
+        ends += [lax.axis_index(axis) > 0, lax.axis_index(axis) < lax.axis_size(axis) - 1]
+    ends = jnp.stack(ends).astype(jnp.int32)
+
+    block_rows = halo(low, high, "px")
+    side_low, side_high = sides(low, high, *block_rows)
+    block_sides = halo(side_low, side_high, "py")
+    low_rest, high_rest, _ = lax.optimization_barrier((low_rest, high_rest, side_low))
+    rest_rows = halo(low_rest, high_rest, "px")
+    rest_sides = halo(*sides(low_rest, high_rest, *rest_rows), "py")
+
+    message_low, message_high, partial = call(
         residual_kernel,
-        (neighbours, tile_kinds, low, high, *halo(low, high), basis, table_high, table_low),
-        [shape(count_y, block, side)] * 2 + [shape(block, prior)],
-        [pltpu.VMEM((places, 2 * block, 2 * side), BF16)],
-        smem=2,
-    )
-    weighted_low, weighted_high, coupling = call(
-        functools.partial(weighted_kernel, inverse_rows),
-        (total_over_mesh(partial), residual_low, residual_high, basis),
-        [shape(count_y, block, side)] * 2 + [shape(block, prior)],
-    )
-    (sums,) = call(
-        operators_kernel,
         (
             neighbours,
             tile_kinds,
-            weighted_low,
-            weighted_high,
-            *halo(weighted_low, weighted_high),
+            low,
+            high,
+            *block_rows,
+            *block_sides,
             basis,
-            table_high,
-            table_low,
+            deep_high,
+            deep_low,
         ),
-        [shape(3 * block, prior)],
+        [shape(count_y + 1, block, side)] * 2 + [shape(block, prior)],
+        [pltpu.VMEM((places, 2 * block, 2 * side), BF16)],
+        smem=2,
+    )
+    from_low, from_high, partial = halo_and_total(message_low, message_high, partial, "px")
+    side_low, side_high = call(
+        sides_kernel,
+        (ends, message_low, message_high, from_low, from_high, partial),
+        [shape(5, block, side)] * 2,
+        smem=1,
+    )
+    from_side_low, from_side_high, partial = halo_and_total(side_low, side_high, partial, "py")
+    weighted_low, weighted_high, coupling, sums = call(
+        functools.partial(operators_kernel, inverse_rows),
+        (
+            ends,
+            neighbours,
+            tile_kinds,
+            partial,
+            message_low,
+            message_high,
+            from_low,
+            from_high,
+            from_side_low,
+            from_side_high,
+            *block_rows,
+            *block_sides,
+            *rest_rows,
+            *rest_sides,
+            basis,
+            wide_high,
+            wide_low,
+        ),
+        [shape(count_y, block, side)] * 2 + [shape(block, prior), shape(3 * block, prior)],
         [pltpu.VMEM((places, 2 * block, side), BF16)],
-        smem=2,
+        smem=3,
     )
     new_block, factor, reduced = call(
         functools.partial(factor_kernel, inverse_rows),
-        (total_over_mesh(sums), weighted_low, weighted_high),
+        (halved_total(sums), weighted_low, weighted_high),
         [
             shape(block * tiles, side),
             shape(block, block),

time: 92.3 us -> 71.1 us (0.77)
  blocking collectives: 46.9 us -> 0 us
  starting transfers between devices: 18 us -> 34.9 us
  waiting for transfers between devices: 10.3 us -> 17.9 us
  local copies, waits for them, and re-layouts: 2.81 us -> 4.49 us
    all_to_all x4 -> x0, blocking collectives: 46.9 us -> none  [the longest x2 28.3 us: total_over_mesh(): lax.all_to_all(value.reshape(count, chunk // width, width), axes, 0, 0)]
    ppermute x0 -> x12, starting transfers between devices: none -> 16.1 us  [the longest x9 12.4 us: shift(): lax.ppermute(value, axis, [(i, (i + step) % count) for i in range(count)])]
    ppermute x0 -> x12, waiting for transfers between devices: none -> 15.2 us  [the longest x9 9.38 us: shift(): lax.ppermute(value, axis, [(i, (i + step) % count) for i in range(count)])]
    ppermute x8, waiting for transfers between devices: 10.3 us -> 2.75 us  [line(): return lax.ppermute(value, axis, pairs)]
    unnamed x14, local copies, waits for them, and re-layouts: 2.56 us -> 4.27 us
  transfers between devices with their start and end apart: 8 -> 20, of which waited for: 6 -> 9; matrix products, arithmetic and copies ran while one was open for 1% -> 0% of each run, Pallas kernels for 0% -> 5%
where the time goes in v4:
time: 71.1 us; the launch traced here: 70.6 us
  starting transfers between devices  34.9 us (49%)
  waiting for transfers between devices  17.9 us (25%)
  Pallas kernels  12.2 us (17%)
  local copies, waits for them, and re-layouts  4.49 us (6%)
  between operations  0.92 us (1%)
    ppermute x8, starting transfers between devices, line(): return lax.ppermute(value, axis, pairs)  18.8 us
    ppermute x9, starting transfers between devices, shift(): lax.ppermute(value, axis, [(i, (i + step) % count) for i in range(count)])  12.4 us
    pallas_call x6, Pallas kernels, call(): pl.pallas_call(kernel, out_shape=outputs, in_specs=[SMEM] * smem + [VMEM]...  12.2 us
    ppermute x9, waiting for transfers between devices, shift(): lax.ppermute(value, axis, [(i, (i + step) % count) for i in range(count)])  9.38 us
    ppermute x3, waiting for transfers between devices, swap(): return lax.ppermute(value, axis, [(i, i ^ step) for i in range(count)])  5.79 us
    unnamed x14, local copies, waits for them, and re-layouts  4.27 us
    ppermute x3, starting transfers between devices, swap(): return lax.ppermute(value, axis, [(i, i ^ step) for i in range(count)])  3.67 us
    ppermute x8, waiting for transfers between devices, line(): return lax.ppermute(value, axis, pairs)  2.75 us
  transfers between devices with their start and end apart: 20, of which 9 were waited for; matrix products, arithmetic and copies ran while one was open for 0% of the time, Pallas kernels for 5%

profile of v4, /device:TPU:0, one launch (start us, length us, event | category | flops | bytes accessed | tf_op | source)
XLA Modules:
  0.0 70.6 jit_solution(12217920287072627453)
XLA Ops:
  0.6 0.0 copy-start
  0.6 1.0 %copy-done = f32[128,2,4,128]{3,2,1,0:T(4,128)S(1)} copy-done((f32[128,2,4,128]{3,2,1,0:T(4,128)S(1)}, f32[128,2,4,128]{3,2,1,0:T(4,128)}, u32[]{:S(2)}) %copy-start) | copy-done | bytes 524312
  1.7 0.9 %copy-done.4 = f32[32,2,4,128]{3,2,1,0:T(4,128)S(1)} copy-done((f32[32,2,4,128]{3,2,1,0:T(4,128)S(1)}, f32[32,2,4,128]{3,2,1,0:T(4,128)}, u32[]{:S(2)}) %copy-start.4) | copy-done | bytes 131096
  2.6 0.1 shard_map.93
  2.7 5.1 %collective-permute-start = (f32[4,64,128]{2,1,0:T(8,128)S(1)}, f32[4,64,128]{2,1,0:T(8,128)S(1)}, u32[]{:S(2)}, u32[]{:S(2)}) collective-permute-start(f32[4,64,128]{2,1,0:T(8,128)S(1)} %get-tuple-element.27.high_ref), channel_id=1, source_target_pairs={{0,4},{4,8},{8,12},{1,5},{5,9},{9,13},{2,6},{6,10},{10,14},{3,7},{... | collective-permute-start | bytes 393224 | tf_op jit(solution)/shard_map/ppermute | solution.py:335
  7.8 1.3 %collective-permute-start.1 = (f32[4,64,128]{2,1,0:T(8,128)S(1)}, f32[4,64,128]{2,1,0:T(8,128)S(1)}, u32[]{:S(2)}, u32[]{:S(2)}) collective-permute-start(f32[4,64,128]{2,1,0:T(8,128)S(1)} %get-tuple-element.26.low_ref), channel_id=1, source_target_pairs={{4,0},{8,4},{12,8},{5,1},{9,5},{13,9},{6,2},{10,6},{14,10},{7,3},{... | collective-permute-start | bytes 393224 | tf_op jit(solution)/shard_map/ppermute | solution.py:335
  9.1 0.0 copy-start.5
  9.1 0.7 copy-done.5
  9.8 0.1 copy.12.neighbours_ref
  9.9 0.6 copy-done.6
  10.5 0.1 copy.13.kinds_ref
  10.6 1.0 %copy-done.3 = f32[8,128,128]{2,1,0:T(8,128)S(1)} copy-done((f32[8,128,128]{2,1,0:T(8,128)S(1)}, f32[8,128,128]{2,1,0:T(8,128)}, u32[]{:S(2)}) %copy-start.3) | copy-done | bytes 524312
  11.6 0.2 shard_map.94
  11.8 0.1 add_convert_fusion.ends_ref
  11.9 2.7 %collective-permute-done.1.from_high_ref.block_from_high_ref = f32[4,64,128]{2,1,0:T(8,128)S(1)} collective-permute-done((f32[4,64,128]{2,1,0:T(8,128)S(1)}, f32[4,64,128]{2,1,0:T(8,128)S(1)}, u32[]{:S(2)}, u32[]{:S(2)}) %collective-permute-start.1) | collective-permute-done | bytes 131104 | tf_op jit(solution)/shard_map/ppermute | solution.py:335
  14.7 0.0 collective-permute-done.from_low_ref.block_from_low_ref
  14.7 1.4 %collective-permute-start.3 = (f32[4,64,128]{2,1,0:T(8,128)S(1)}, f32[4,64,128]{2,1,0:T(8,128)S(1)}, u32[]{:S(2)}, u32[]{:S(2)}) collective-permute-start(f32[4,64,128]{2,1,0:T(8,128)S(1)} %pad_maximum_fusion.3), channel_id=1, source_target_pairs={{1,0},{2,1},{3,2},{5,4},{6,5},{7,6},{9,8},{10,9},{11,10},{13,12},{... | collective-permute-start | bytes 393224 | tf_op jit(solution)/shard_map/ppermute | solution.py:335
  16.1 3.5 %collective-permute-start.10 = (f32[4,96,128]{2,1,0:T(8,128)S(1)}, f32[4,96,128]{2,1,0:T(8,128)S(1)}, u32[]{:S(2)}, u32[]{:S(2)}) collective-permute-start(f32[4,96,128]{2,1,0:T(8,128)S(1)} %get-tuple-element.37), channel_id=1, source_target_pairs={{0,4},{4,8},{8,12},{1,5},{5,9},{9,13},{2,6},{6,10},{10,14},{3,7},{... | collective-permute-start | bytes 589832 | tf_op jit(solution)/shard_map/ppermute | solution.py:335
  19.7 2.8 %collective-permute-start.2 = (f32[4,64,128]{2,1,0:T(8,128)S(1)}, f32[4,64,128]{2,1,0:T(8,128)S(1)}, u32[]{:S(2)}, u32[]{:S(2)}) collective-permute-start(f32[4,64,128]{2,1,0:T(8,128)S(1)} %pad_maximum_fusion.2), channel_id=1, source_target_pairs={{0,1},{1,2},{2,3},{4,5},{5,6},{6,7},{8,9},{9,10},{10,11},{12,13},{... | collective-permute-start | bytes 393224 | tf_op jit(solution)/shard_map/ppermute | solution.py:335
  22.4 1.3 %collective-permute-start.11 = (f32[4,96,128]{2,1,0:T(8,128)S(1)}, f32[4,96,128]{2,1,0:T(8,128)S(1)}, u32[]{:S(2)}, u32[]{:S(2)}) collective-permute-start(f32[4,96,128]{2,1,0:T(8,128)S(1)} %get-tuple-element.38), channel_id=1, source_target_pairs={{4,0},{8,4},{12,8},{5,1},{9,5},{13,9},{6,2},{10,6},{14,10},{7,3},{... | collective-permute-start | bytes 589832 | tf_op jit(solution)/shard_map/ppermute | solution.py:335
  23.8 0.0 collective-permute-done.3.side_high_ref.block_side_high_ref
  23.8 2.9 %shard_map.95 = (f32[5,32,128]{2,1,0:T(8,128)S(1)}, f32[5,32,128]{2,1,0:T(8,128)S(1)}, f32[32,128]{1,0:T(8,128)S(1)}) custom-call(s32[5,8]{1,0:T(8,128)S(1)} %copy.12.neighbours_ref, s32[5,8]{1,0:T(8,128)S(1)} %copy.13.kinds_ref, f32[4,64,128]{2,1,0:T(8,128)S(1)} %get-tuple-element.26.low_ref, f32[4,64,128]{2,1,0:T(8,128)S(1)} %get-tuple-element.27.high_ref, ...), custom_call_target="tpu_custom_call" | custom-call | tf_op jit(solution)/shard_map/pallas_call | solution.py:365
  26.7 2.7 %collective-permute-start.5 = (f32[5,32,128]{2,1,0:T(8,128)S(1)}, f32[5,32,128]{2,1,0:T(8,128)S(1)}, u32[]{:S(2)}, u32[]{:S(2)}) collective-permute-start(f32[5,32,128]{2,1,0:T(8,128)S(1)} %get-tuple-element.31.high_ref), channel_id=1, source_target_pairs={{0,4},{4,8},{8,12},{12,0},{1,5},{5,9},{9,13},{13,1},{2,6},{6,10},{... | collective-permute-start | bytes 245768 | tf_op jit(solution)/shard_map/ppermute | solution.py:294
  29.4 1.2 %collective-permute-start.6 = (f32[5,32,128]{2,1,0:T(8,128)S(1)}, f32[5,32,128]{2,1,0:T(8,128)S(1)}, u32[]{:S(2)}, u32[]{:S(2)}) collective-permute-start(f32[5,32,128]{2,1,0:T(8,128)S(1)} %get-tuple-element.32.low_ref), channel_id=1, source_target_pairs={{0,12},{4,0},{8,4},{12,8},{1,13},{5,1},{9,5},{13,9},{2,14},{6,2},{... | collective-permute-start | bytes 245768 | tf_op jit(solution)/shard_map/ppermute | solution.py:294
  30.5 1.9 %collective-permute-start.4 = (f32[32,128]{1,0:T(8,128)S(1)}, f32[32,128]{1,0:T(8,128)S(1)}, u32[]{:S(2)}, u32[]{:S(2)}) collective-permute-start(f32[32,128]{1,0:T(8,128)S(1)} %get-tuple-element.30), channel_id=1, source_target_pairs={{0,8},{4,12},{8,0},{12,4},{1,9},{5,13},{9,1},{13,5},{2,10},{6,14},... | collective-permute-start | bytes 49160 | tf_op jit(solution)/shard_map/ppermute | solution.py:294
  32.4 0.0 collective-permute-done.10.rest_from_low_ref
  32.5 2.2 %collective-permute-start.12 = (f32[4,96,128]{2,1,0:T(8,128)S(1)}, f32[4,96,128]{2,1,0:T(8,128)S(1)}, u32[]{:S(2)}, u32[]{:S(2)}) collective-permute-start(f32[4,96,128]{2,1,0:T(8,128)S(1)} %pad_maximum_fusion), channel_id=1, source_target_pairs={{0,1},{1,2},{2,3},{4,5},{5,6},{6,7},{8,9},{9,10},{10,11},{12,13},{... | collective-permute-start | bytes 589832 | tf_op jit(solution)/shard_map/ppermute | solution.py:335
  34.6 2.6 %collective-permute-done.4 = f32[32,128]{1,0:T(8,128)S(1)} collective-permute-done((f32[32,128]{1,0:T(8,128)S(1)}, f32[32,128]{1,0:T(8,128)S(1)}, u32[]{:S(2)}, u32[]{:S(2)}) %collective-permute-start.4) | collective-permute-done | bytes 16416 | tf_op jit(solution)/shard_map/ppermute | solution.py:294
  37.2 0.0 collective-permute-done.5.from_low_ref
  37.2 0.0 collective-permute-done.6.from_high_ref
  37.2 2.3 %collective-permute-start.7 = (f32[32,128]{1,0:T(8,128)S(1)}, f32[32,128]{1,0:T(8,128)S(1)}, u32[]{:S(2)}, u32[]{:S(2)}) collective-permute-start(f32[32,128]{1,0:T(8,128)S(1)} %fusion.3.partial_ref), channel_id=1, source_target_pairs={{0,2},{1,3},{2,0},{3,1},{4,6},{5,7},{6,4},{7,5},{8,10},{9,11},{10,... | collective-permute-start | bytes 49160 | tf_op jit(solution)/shard_map/ppermute | solution.py:294
  39.6 0.6 shard_map.96
  40.1 0.1 collective-permute-start.9
  40.2 0.5 collective-permute-start.8
  40.7 1.3 %collective-permute-start.13 = (f32[4,96,128]{2,1,0:T(8,128)S(1)}, f32[4,96,128]{2,1,0:T(8,128)S(1)}, u32[]{:S(2)}, u32[]{:S(2)}) collective-permute-start(f32[4,96,128]{2,1,0:T(8,128)S(1)} %pad_maximum_fusion.1), channel_id=1, source_target_pairs={{1,0},{2,1},{3,2},{5,4},{6,5},{7,6},{9,8},{10,9},{11,10},{13,12},{... | collective-permute-start | bytes 589832 | tf_op jit(solution)/shard_map/ppermute | solution.py:335
  42.0 0.8 %collective-permute-done.9.side_high_ref = f32[5,32,128]{2,1,0:T(8,128)S(1)} collective-permute-done((f32[5,32,128]{2,1,0:T(8,128)S(1)}, f32[5,32,128]{2,1,0:T(8,128)S(1)}, u32[]{:S(2)}, u32[]{:S(2)}) %collective-permute-start.9) | collective-permute-done | bytes 81952 | tf_op jit(solution)/shard_map/ppermute | solution.py:294
  42.8 1.3 %collective-permute-done.8.side_low_ref = f32[5,32,128]{2,1,0:T(8,128)S(1)} collective-permute-done((f32[5,32,128]{2,1,0:T(8,128)S(1)}, f32[5,32,128]{2,1,0:T(8,128)S(1)}, u32[]{:S(2)}, u32[]{:S(2)}) %collective-permute-start.8) | collective-permute-done | bytes 81952 | tf_op jit(solution)/shard_map/ppermute | solution.py:294
  44.1 3.8 %shard_map.97 = (f32[4,32,128]{2,1,0:T(8,128)S(1)}, f32[4,32,128]{2,1,0:T(8,128)S(1)}, f32[32,128]{1,0:T(8,128)}, f32[96,128]{1,0:T(8,128)S(1)}) custom-call(s32[4]{0:T(128)S(1)} %add_convert_fusion.ends_ref, s32[5,8]{1,0:T(8,128)S(1)} %copy.12.neighbours_ref, s32[5,8]{1,0:T(8,128)S(1)} %copy.13.kinds_ref, f32[32,128]{1,0:T(8,128)S(1)} %fusion.1.partial_ref, ...), custom_call_target="tpu_custom_call" | custom-call | tf_op jit(solution)/shard_map/pallas_call | solution.py:365
  47.9 3.5 %collective-permute-start.14 = (f32[48,128]{1,0:T(8,128)S(1)}, f32[48,128]{1,0:T(8,128)S(1)}, u32[]{:S(2)}, u32[]{:S(2)}) collective-permute-start(f32[48,128]{1,0:T(8,128)S(1)} %slice_select_fusion), channel_id=1, source_target_pairs={{0,1},{1,0},{2,3},{3,2},{4,5},{5,4},{6,7},{7,6},{8,9},{9,8},{10,11... | collective-permute-start | bytes 73736 | tf_op jit(solution)/shard_map/ppermute | solution.py:289
  51.5 0.8 %collective-permute-done.14 = f32[48,128]{1,0:T(8,128)S(1)} collective-permute-done((f32[48,128]{1,0:T(8,128)S(1)}, f32[48,128]{1,0:T(8,128)S(1)}, u32[]{:S(2)}, u32[]{:S(2)}) %collective-permute-start.14) | collective-permute-done | bytes 24608 | tf_op jit(solution)/shard_map/ppermute | solution.py:289
  52.3 0.1 collective-permute-start.15
  52.4 3.8 %collective-permute-done.15 = f32[48,128]{1,0:T(8,128)S(1)} collective-permute-done((f32[48,128]{1,0:T(8,128)S(1)}, f32[48,128]{1,0:T(8,128)S(1)}, u32[]{:S(2)}, u32[]{:S(2)}) %collective-permute-start.15) | collective-permute-done | bytes 24608 | tf_op jit(solution)/shard_map/ppermute | solution.py:289
  56.2 3.8 %collective-permute-start.18 = (f32[48,128]{1,0:T(8,128)S(1)}, f32[48,128]{1,0:T(8,128)S(1)}, u32[]{:S(2)}, u32[]{:S(2)}) collective-permute-start(f32[48,128]{1,0:T(8,128)S(1)} %add.53), channel_id=1, source_target_pairs={{0,12},{4,0},{8,4},{12,8},{1,13},{5,1},{9,5},{13,9},{2,14},{6,2},{... | collective-permute-start | bytes 73736 | tf_op jit(solution)/shard_map/ppermute | solution.py:294
  60.0 1.9 %collective-permute-done.17 = f32[48,128]{1,0:T(8,128)S(1)} collective-permute-done((f32[48,128]{1,0:T(8,128)S(1)}, f32[48,128]{1,0:T(8,128)S(1)}, u32[]{:S(2)}, u32[]{:S(2)}) %collective-permute-start.17) | collective-permute-done | bytes 24608 | tf_op jit(solution)/shard_map/ppermute | solution.py:294
  61.9 2.8 %collective-permute-done.16 = f32[48,128]{1,0:T(8,128)S(1)} collective-permute-done((f32[48,128]{1,0:T(8,128)S(1)}, f32[48,128]{1,0:T(8,128)S(1)}, u32[]{:S(2)}, u32[]{:S(2)}) %collective-permute-start.16) | collective-permute-done | bytes 24608 | tf_op jit(solution)/shard_map/ppermute | solution.py:294
  64.7 0.1 collective-permute-start.19
  64.8 1.2 %collective-permute-done.19 = f32[48,128]{1,0:T(8,128)S(1)} collective-permute-done((f32[48,128]{1,0:T(8,128)S(1)}, f32[48,128]{1,0:T(8,128)S(1)}, u32[]{:S(2)}, u32[]{:S(2)}) %collective-permute-start.19) | collective-permute-done | bytes 24608 | tf_op jit(solution)/shard_map/ppermute | solution.py:289
  66.0 4.6 %shard_map.98 = (f32[256,128]{1,0:T(8,128)}, f32[32,32]{1,0:T(8,128)}, f32[2,32,160]{2,1,0:T(8,128)}) custom-call(f32[96,128]{1,0:T(8,128)S(1)} %pad_maximum_fusion.4.sums_ref, f32[4,32,128]{2,1,0:T(8,128)S(1)} %get-tuple-element.42.weighted_low_ref, f32[4,32,128]{2,1,0:T(8,128)S(1)} %get-tuple-element.43.weighted_high_ref), custom_call_target="tpu_custom_call" | custom-call | tf_op jit(solution)/shard_map/pallas_call | solution.py:365
  (34 shorter events, 0.2 us)
Async XLA Ops:
  0.6 1.0 %copy-start = (f32[128,2,4,128]{3,2,1,0:T(4,128)S(1)}, f32[128,2,4,128]{3,2,1,0:T(4,128)}, u32[]{:S(2)}) copy-start(f32[128,2,4,128]{3,2,1,0:T(4,128)} %param.6) | copy-start | bytes 1572868
  1.7 0.9 %copy-start.4 = (f32[32,2,4,128]{3,2,1,0:T(4,128)S(1)}, f32[32,2,4,128]{3,2,1,0:T(4,128)}, u32[]{:S(2)}) copy-start(f32[32,2,4,128]{3,2,1,0:T(4,128)} %param.7) | copy-start | bytes 393220
  2.6 8.0 %copy-start.2 = (f32[8,128,128]{2,1,0:T(8,128)S(1)}, f32[8,128,128]{2,1,0:T(8,128)}, u32[]{:S(2)}) copy-start(f32[8,128,128]{2,1,0:T(8,128)} %stiff_ref.1) | copy-start | bytes 1572868
  2.7 11.9 %collective-permute-start = (f32[4,64,128]{2,1,0:T(8,128)S(1)}, f32[4,64,128]{2,1,0:T(8,128)S(1)}, u32[]{:S(2)}, u32[]{:S(2)}) collective-permute-start(f32[4,64,128]{2,1,0:T(8,128)S(1)} %get-tuple-element.27.high_ref), channel_id=1, source_target_pairs={{0,4},{4,8},{8,12},{1,5},{5,9},{9,13},{2,6},{6,10},{10,14},{3,7},{... | collective-permute-start | bytes 393224 | tf_op jit(solution)/shard_map/ppermute | solution.py:335
  7.8 6.9 %collective-permute-start.1 = (f32[4,64,128]{2,1,0:T(8,128)S(1)}, f32[4,64,128]{2,1,0:T(8,128)S(1)}, u32[]{:S(2)}, u32[]{:S(2)}) collective-permute-start(f32[4,64,128]{2,1,0:T(8,128)S(1)} %get-tuple-element.26.low_ref), channel_id=1, source_target_pairs={{4,0},{8,4},{12,8},{5,1},{9,5},{13,9},{6,2},{10,6},{14,10},{7,3},{... | collective-permute-start | bytes 393224 | tf_op jit(solution)/shard_map/ppermute | solution.py:335
  9.1 0.7 copy-start.5
  9.8 0.7 copy-start.6
  10.6 1.0 %copy-start.3 = (f32[8,128,128]{2,1,0:T(8,128)S(1)}, f32[8,128,128]{2,1,0:T(8,128)}, u32[]{:S(2)}) copy-start(f32[8,128,128]{2,1,0:T(8,128)} %mass_ref.1) | copy-start | bytes 1572868
  14.6 9.1 %copy-start.1 = (f32[128,2,4,128]{3,2,1,0:T(4,128)S(1)}, f32[128,2,4,128]{3,2,1,0:T(4,128)}, u32[]{:S(2)}) copy-start(f32[128,2,4,128]{3,2,1,0:T(4,128)} %param.6) | copy-start | bytes 1572868
  14.7 9.1 %collective-permute-start.3 = (f32[4,64,128]{2,1,0:T(8,128)S(1)}, f32[4,64,128]{2,1,0:T(8,128)S(1)}, u32[]{:S(2)}, u32[]{:S(2)}) collective-permute-start(f32[4,64,128]{2,1,0:T(8,128)S(1)} %pad_maximum_fusion.3), channel_id=1, source_target_pairs={{1,0},{2,1},{3,2},{5,4},{6,5},{7,6},{9,8},{10,9},{11,10},{13,12},{... | collective-permute-start | bytes 393224 | tf_op jit(solution)/shard_map/ppermute | solution.py:335
  16.1 16.3 %collective-permute-start.10 = (f32[4,96,128]{2,1,0:T(8,128)S(1)}, f32[4,96,128]{2,1,0:T(8,128)S(1)}, u32[]{:S(2)}, u32[]{:S(2)}) collective-permute-start(f32[4,96,128]{2,1,0:T(8,128)S(1)} %get-tuple-element.37), channel_id=1, source_target_pairs={{0,4},{4,8},{8,12},{1,5},{5,9},{9,13},{2,6},{6,10},{10,14},{3,7},{... | collective-permute-start | bytes 589832 | tf_op jit(solution)/shard_map/ppermute | solution.py:335
  19.7 4.1 %collective-permute-start.2 = (f32[4,64,128]{2,1,0:T(8,128)S(1)}, f32[4,64,128]{2,1,0:T(8,128)S(1)}, u32[]{:S(2)}, u32[]{:S(2)}) collective-permute-start(f32[4,64,128]{2,1,0:T(8,128)S(1)} %pad_maximum_fusion.2), channel_id=1, source_target_pairs={{0,1},{1,2},{2,3},{4,5},{5,6},{6,7},{8,9},{9,10},{10,11},{12,13},{... | collective-permute-start | bytes 393224 | tf_op jit(solution)/shard_map/ppermute | solution.py:335
  22.4 10.0 %collective-permute-start.11 = (f32[4,96,128]{2,1,0:T(8,128)S(1)}, f32[4,96,128]{2,1,0:T(8,128)S(1)}, u32[]{:S(2)}, u32[]{:S(2)}) collective-permute-start(f32[4,96,128]{2,1,0:T(8,128)S(1)} %get-tuple-element.38), channel_id=1, source_target_pairs={{4,0},{8,4},{12,8},{5,1},{9,5},{13,9},{6,2},{10,6},{14,10},{7,3},{... | collective-permute-start | bytes 589832 | tf_op jit(solution)/shard_map/ppermute | solution.py:335
  26.7 10.5 %collective-permute-start.5 = (f32[5,32,128]{2,1,0:T(8,128)S(1)}, f32[5,32,128]{2,1,0:T(8,128)S(1)}, u32[]{:S(2)}, u32[]{:S(2)}) collective-permute-start(f32[5,32,128]{2,1,0:T(8,128)S(1)} %get-tuple-element.31.high_ref), channel_id=1, source_target_pairs={{0,4},{4,8},{8,12},{12,0},{1,5},{5,9},{9,13},{13,1},{2,6},{6,10},{... | collective-permute-start | bytes 245768 | tf_op jit(solution)/shard_map/ppermute | solution.py:294
  29.4 7.8 %collective-permute-start.6 = (f32[5,32,128]{2,1,0:T(8,128)S(1)}, f32[5,32,128]{2,1,0:T(8,128)S(1)}, u32[]{:S(2)}, u32[]{:S(2)}) collective-permute-start(f32[5,32,128]{2,1,0:T(8,128)S(1)} %get-tuple-element.32.low_ref), channel_id=1, source_target_pairs={{0,12},{4,0},{8,4},{12,8},{1,13},{5,1},{9,5},{13,9},{2,14},{6,2},{... | collective-permute-start | bytes 245768 | tf_op jit(solution)/shard_map/ppermute | solution.py:294
  30.5 6.7 %collective-permute-start.4 = (f32[32,128]{1,0:T(8,128)S(1)}, f32[32,128]{1,0:T(8,128)S(1)}, u32[]{:S(2)}, u32[]{:S(2)}) collective-permute-start(f32[32,128]{1,0:T(8,128)S(1)} %get-tuple-element.30), channel_id=1, source_target_pairs={{0,8},{4,12},{8,0},{12,4},{1,9},{5,13},{9,1},{13,5},{2,10},{6,14},... | collective-permute-start | bytes 49160 | tf_op jit(solution)/shard_map/ppermute | solution.py:294
  32.5 11.6 %collective-permute-start.12 = (f32[4,96,128]{2,1,0:T(8,128)S(1)}, f32[4,96,128]{2,1,0:T(8,128)S(1)}, u32[]{:S(2)}, u32[]{:S(2)}) collective-permute-start(f32[4,96,128]{2,1,0:T(8,128)S(1)} %pad_maximum_fusion), channel_id=1, source_target_pairs={{0,1},{1,2},{2,3},{4,5},{5,6},{6,7},{8,9},{9,10},{10,11},{12,13},{... | collective-permute-start | bytes 589832 | tf_op jit(solution)/shard_map/ppermute | solution.py:335
  37.2 4.8 %collective-permute-start.7 = (f32[32,128]{1,0:T(8,128)S(1)}, f32[32,128]{1,0:T(8,128)S(1)}, u32[]{:S(2)}, u32[]{:S(2)}) collective-permute-start(f32[32,128]{1,0:T(8,128)S(1)} %fusion.3.partial_ref), channel_id=1, source_target_pairs={{0,2},{1,3},{2,0},{3,1},{4,6},{5,7},{6,4},{7,5},{8,10},{9,11},{10,... | collective-permute-start | bytes 49160 | tf_op jit(solution)/shard_map/ppermute | solution.py:294
  40.1 2.7 %collective-permute-start.9 = (f32[5,32,128]{2,1,0:T(8,128)S(1)}, f32[5,32,128]{2,1,0:T(8,128)S(1)}, u32[]{:S(2)}, u32[]{:S(2)}) collective-permute-start(f32[5,32,128]{2,1,0:T(8,128)S(1)} %get-tuple-element.34), channel_id=1, source_target_pairs={{0,3},{1,0},{2,1},{3,2},{4,7},{5,4},{6,5},{7,6},{8,11},{9,8},{10,9... | collective-permute-start | bytes 245768 | tf_op jit(solution)/shard_map/ppermute | solution.py:294
  40.2 3.9 %collective-permute-start.8 = (f32[5,32,128]{2,1,0:T(8,128)S(1)}, f32[5,32,128]{2,1,0:T(8,128)S(1)}, u32[]{:S(2)}, u32[]{:S(2)}) collective-permute-start(f32[5,32,128]{2,1,0:T(8,128)S(1)} %get-tuple-element.33), channel_id=1, source_target_pairs={{0,1},{1,2},{2,3},{3,0},{4,5},{5,6},{6,7},{7,4},{8,9},{9,10},{10,1... | collective-permute-start | bytes 245768 | tf_op jit(solution)/shard_map/ppermute | solution.py:294
  40.7 3.4 %collective-permute-start.13 = (f32[4,96,128]{2,1,0:T(8,128)S(1)}, f32[4,96,128]{2,1,0:T(8,128)S(1)}, u32[]{:S(2)}, u32[]{:S(2)}) collective-permute-start(f32[4,96,128]{2,1,0:T(8,128)S(1)} %pad_maximum_fusion.1), channel_id=1, source_target_pairs={{1,0},{2,1},{3,2},{5,4},{6,5},{7,6},{9,8},{10,9},{11,10},{13,12},{... | collective-permute-start | bytes 589832 | tf_op jit(solution)/shard_map/ppermute | solution.py:335
  47.9 4.4 %collective-permute-start.14 = (f32[48,128]{1,0:T(8,128)S(1)}, f32[48,128]{1,0:T(8,128)S(1)}, u32[]{:S(2)}, u32[]{:S(2)}) collective-permute-start(f32[48,128]{1,0:T(8,128)S(1)} %slice_select_fusion), channel_id=1, source_target_pairs={{0,1},{1,0},{2,3},{3,2},{4,5},{5,4},{6,7},{7,6},{8,9},{9,8},{10,11... | collective-permute-start | bytes 73736 | tf_op jit(solution)/shard_map/ppermute | solution.py:289
  52.3 3.8 %collective-permute-start.15 = (f32[48,128]{1,0:T(8,128)S(1)}, f32[48,128]{1,0:T(8,128)S(1)}, u32[]{:S(2)}, u32[]{:S(2)}) collective-permute-start(f32[48,128]{1,0:T(8,128)S(1)} %select_add_fusion), channel_id=1, source_target_pairs={{0,2},{1,3},{2,0},{3,1},{4,6},{5,7},{6,4},{7,5},{8,10},{9,11},{10,... | collective-permute-start | bytes 73736 | tf_op jit(solution)/shard_map/ppermute | solution.py:289
  56.2 5.7 %collective-permute-start.17 = (f32[48,128]{1,0:T(8,128)S(1)}, f32[48,128]{1,0:T(8,128)S(1)}, u32[]{:S(2)}, u32[]{:S(2)}) collective-permute-start(f32[48,128]{1,0:T(8,128)S(1)} %add.53), channel_id=1, source_target_pairs={{0,4},{4,8},{8,12},{12,0},{1,5},{5,9},{9,13},{13,1},{2,6},{6,10},{... | collective-permute-start | bytes 73736 | tf_op jit(solution)/shard_map/ppermute | solution.py:294
  56.2 5.7 %collective-permute-start.18 = (f32[48,128]{1,0:T(8,128)S(1)}, f32[48,128]{1,0:T(8,128)S(1)}, u32[]{:S(2)}, u32[]{:S(2)}) collective-permute-start(f32[48,128]{1,0:T(8,128)S(1)} %add.53), channel_id=1, source_target_pairs={{0,12},{4,0},{8,4},{12,8},{1,13},{5,1},{9,5},{13,9},{2,14},{6,2},{... | collective-permute-start | bytes 73736 | tf_op jit(solution)/shard_map/ppermute | solution.py:294
  60.0 4.7 %collective-permute-start.16 = (f32[48,128]{1,0:T(8,128)S(1)}, f32[48,128]{1,0:T(8,128)S(1)}, u32[]{:S(2)}, u32[]{:S(2)}) collective-permute-start(f32[48,128]{1,0:T(8,128)S(1)} %add.53), channel_id=1, source_target_pairs={{0,8},{4,12},{8,0},{12,4},{1,9},{5,13},{9,1},{13,5},{2,10},{6,14},... | collective-permute-start | bytes 73736 | tf_op jit(solution)/shard_map/ppermute | solution.py:294
  64.7 1.3 %collective-permute-start.19 = (f32[48,128]{1,0:T(8,128)S(1)}, f32[48,128]{1,0:T(8,128)S(1)}, u32[]{:S(2)}, u32[]{:S(2)}) collective-permute-start(f32[48,128]{1,0:T(8,128)S(1)} %add_add_fusion), channel_id=1, source_target_pairs={{0,1},{1,0},{2,3},{3,2},{4,5},{5,4},{6,7},{7,6},{8,9},{9,8},{10,11... | collective-permute-start | bytes 73736 | tf_op jit(solution)/shard_map/ppermute | solution.py:289

commit v5 on v4

v5 whole, which is shorter than its diff:
```python
import functools

import jax
import jax.numpy as jnp
from jax import lax
from jax.experimental import pallas as pl
from jax.experimental.pallas import tpu as pltpu
from jax.sharding import PartitionSpec as P

F32 = jnp.float32
BF16 = jnp.bfloat16
VMEM = pl.BlockSpec(memory_space=pltpu.VMEM)
SMEM = pl.BlockSpec(memory_space=pltpu.SMEM)
PARAMS = pltpu.CompilerParams(vmem_limit_bytes=24 * 1024 * 1024)


def split(value):
    high = value.astype(BF16)
    return high, (value - high.astype(F32)).astype(BF16)


def mul(left, right):
    return jnp.dot(left, right, preferred_element_type=F32)


def mul_t(left, right):
    return lax.dot_general(left, right, (((1,), (1,)), ((), ())), preferred_element_type=F32)


def mul3(left, right):
    left_high, left_low = split(left)
    right_high, right_low = split(right)
    return mul(left_high, right_high) + (mul(left_high, right_low) + mul(left_low, right_high))


def mul3_t(left, right):
    left_high, left_low = split(left)
    right_high, right_low = split(right)
    return mul_t(left_high, right_high) + (
        mul_t(left_high, right_low) + mul_t(left_low, right_high)
    )


def tables_kernel(stiff_ref, mass_ref, deep_high_ref, deep_low_ref, wide_high_ref, wide_low_ref):
    side = stiff_ref.shape[1]
    for kind in range(stiff_ref.shape[0]):
        for place, ref in enumerate((stiff_ref, mass_ref)):
            high, low = split(ref[kind])
            span = slice(place * side, (place + 1) * side)
            deep_high_ref[kind, span, :] = high
            deep_low_ref[kind, span, :] = low
            wide_high_ref[kind, :, span] = high
            wide_low_ref[kind, :, span] = low


def pack_kernel(count_x, count_y, basis_ref, previous_ref, low_ref, high_ref):
    tiles = count_x * count_y
    prior, block = basis_ref.shape[0] // tiles, previous_ref.shape[0] // tiles
    for column, ref in ((0, low_ref), (count_y - 1, high_ref)):
        for i in range(count_x):
            tile = i * count_y + column
            ref[i, :prior, :] = basis_ref[pl.ds(tile, prior, stride=tiles), :]
            ref[i, prior:, :] = previous_ref[pl.ds(tile, block, stride=tiles), :]


def rows_kernel(
    basis_ref,
    previous_ref,
    side_low_ref,
    side_high_ref,
    low_ref,
    high_ref,
    low_rest_ref,
    high_rest_ref,
):
    wide, rest, _ = low_rest_ref.shape
    block = low_ref.shape[1] // 2
    tiles = 2 * (wide - 2)
    for i, ref, rest_ref in ((0, low_ref, low_rest_ref), (1, high_ref, high_rest_ref)):
        for j, side_ref in ((0, side_low_ref), (wide - 1, side_high_ref)):
            rest_ref[j] = side_ref[i, :rest, :]
            ref[j] = side_ref[i, rest:, :]
        for j in range(wide - 2):
            tile = i * (wide - 2) + j
            rest_ref[j + 1] = basis_ref[pl.ds(tile, rest, stride=tiles), :]
            ref[j + 1, :block, :] = basis_ref[pl.ds(rest * tiles + tile, block, stride=tiles), :]
            ref[j + 1, block:, :] = previous_ref[pl.ds(tile, block, stride=tiles), :]


def source_of(neighbours_ref, k, tile, count_y):
    neighbour = neighbours_ref[k, tile]
    down = neighbour // 3
    return (tile // count_y + down) * (count_y + 2) + tile % count_y + neighbour - 3 * down


def residual_kernel(
    neighbours_ref,
    kinds_ref,
    from_low_ref,
    low_ref,
    high_ref,
    from_high_ref,
    low_rest_ref,
    high_rest_ref,
    table_high_ref,
    table_low_ref,
    residual_low_ref,
    residual_high_ref,
    message_low_ref,
    message_high_ref,
    partial_ref,
    ext_ref,
):
    wide = low_ref.shape[0]
    count_y = wide - 2
    block = low_ref.shape[1] // 2
    side = low_ref.shape[2]
    prior = low_rest_ref.shape[1] + block
    for i, ref in enumerate((from_low_ref, low_ref, high_ref, from_high_ref)):
        for j in range(wide):
            for part in range(2):
                high, low = split(ref[j, part * block : (part + 1) * block, :])
                ext_ref[i * wide + j, :block, part * side : (part + 1) * side] = high
                ext_ref[i * wide + j, block:, part * side : (part + 1) * side] = low
    partial = jnp.zeros((block, prior), F32)
    for tile in range(2 * count_y):
        i, j = tile // count_y, tile % count_y
        own = (low_ref, high_ref)[i][j + 1]
        total = 4.0 * own[:block] + own[block:]
        for k in range(neighbours_ref.shape[0]):
            source = source_of(neighbours_ref, k, tile, count_y)
            kind = kinds_ref[k, tile]
            chosen = ext_ref[source]
            both = mul(chosen, table_high_ref[kind])
            total = total + (
                both[:block] + (both[block:] + mul(chosen[:block], table_low_ref[kind]))
            )
        (residual_low_ref, residual_high_ref)[i][j] = total
        if j == 0:
            message_low_ref[i] = total
        if j == count_y - 1:
            message_high_ref[i] = total
        basis_tile = jnp.concatenate(
            [(low_rest_ref, high_rest_ref)[i][j + 1], own[:block]], axis=0
        )
        partial = partial + mul3_t(total, basis_tile)
    partial_ref[...] = partial
    message_low_ref[2] = partial
    message_high_ref[2] = partial


def residual_rows_kernel(
    low_ref, high_ref, side_low_ref, side_high_ref, partial_ref, row_low_ref, row_high_ref
):
    count_y = low_ref.shape[0]
    for i, ref, row_ref in ((0, low_ref, row_low_ref), (1, high_ref, row_high_ref)):
        row_ref[0] = side_low_ref[i]
        row_ref[1 : count_y + 1] = ref[...]
        row_ref[count_y + 1] = side_high_ref[i]
        row_ref[count_y + 2] = partial_ref[...]


def operators_kernel(
    inverse_rows,
    ends_ref,
    neighbours_ref,
    kinds_ref,
    partial_ref,
    *refs,
):
    row_refs, block_refs, rest_refs = refs[:4], refs[4:8], refs[8:12]
    table_high_ref, table_low_ref = refs[12:14]
    weighted_low_ref, weighted_high_ref, coupling_ref, sums_ref, ext_ref = refs[14:]
    count_y, block, side = weighted_low_ref.shape
    wide = count_y + 2
    prior = rest_refs[0].shape[1] + block
    coupling = partial_ref[...] * inverse_rows
    coupling_ref[...] = coupling
    coupling_high, coupling_low = split(coupling)

    def basis_tile(i, j):
        return jnp.concatenate([rest_refs[i][j], block_refs[i][j, :block, :]], axis=0)

    for i in range(4):
        for j in range(wide):
            high, low = split(basis_tile(i, j))
            moved = mul(coupling_high, high) + (
                mul(coupling_high, low) + mul(coupling_low, high)
            )
            value = row_refs[i][j]
            if j == 0:
                value = value * ends_ref[0].astype(F32)
            if j == wide - 1:
                value = value * ends_ref[1].astype(F32)
            value = value - moved
            if 0 < i < 3 and 0 < j < wide - 1:
                (weighted_low_ref, weighted_high_ref)[i - 1][j - 1] = value
            high, low = split(value)
            ext_ref[i * wide + j, :block, :] = high
            ext_ref[i * wide + j, block:, :] = low
    with_basis = jnp.zeros((2 * block, prior), F32)
    with_own = jnp.zeros((block, 4 * block), F32)
    for tile in range(2 * count_y):
        i, j = tile // count_y, tile % count_y
        own = (weighted_low_ref, weighted_high_ref)[i][j]
        totals = jnp.concatenate([4.0 * own, own], axis=1)
        for k in range(neighbours_ref.shape[0]):
            source = source_of(neighbours_ref, k, tile, count_y)
            kind = kinds_ref[k, tile]
            chosen = ext_ref[source]
            both = mul(chosen, table_high_ref[kind])
            totals = totals + (
                both[:block] + (both[block:] + mul(chosen[:block], table_low_ref[kind]))
            )
        applied = jnp.concatenate([totals[:, :side], totals[:, side:]], axis=0)
        with_basis = with_basis + mul3_t(applied, basis_tile(i + 1, j + 1))
        right = jnp.concatenate([applied, own, jnp.zeros_like(own)], axis=0)
        with_own = with_own + mul3_t(own, right)
    sums_ref[: 2 * block, :] = with_basis
    sums_ref[2 * block :, :] = with_own


def factor_kernel(
    inverse_rows,
    sums_ref,
    weighted_low_ref,
    weighted_high_ref,
    new_ref,
    factor_ref,
    reduced_ref,
):
    count_y, block, _ = weighted_low_ref.shape
    prior = sums_ref.shape[1]
    tiles = 2 * count_y
    with_own = sums_ref[2 * block :, :] * inverse_rows
    gram = with_own[:, 2 * block : 3 * block]
    row_ids = lax.broadcasted_iota(jnp.int32, (block, block), 0)
    column_ids = lax.broadcasted_iota(jnp.int32, (block, block), 1)
    unit = jnp.where(row_ids == column_ids, 1.0, 0.0).astype(F32)
    work = jnp.concatenate([gram, unit], axis=1)
    rows = lax.broadcasted_iota(jnp.int32, work.shape, 0)
    group = 4
    for j in range(0, block, group):
        columns = [
            jnp.broadcast_to(work[:, j + a : j + a + 1], work.shape) for a in range(group)
        ]
        pivots = [work[j + a : j + a + 1, :] for a in range(group)]
        for a in range(group):
            at = j + a
            ratio = columns[a] * (1.0 / columns[a][at : at + 1, :])
            for b in range(a + 1, group):
                columns[b] = columns[b] - ratio * columns[b][at : at + 1, :]
                pivots[b] = pivots[b] - ratio[j + b : j + b + 1, :] * pivots[a]
            work = work - jnp.where(rows > at, ratio, 0.0) * pivots[a]
    work = work * lax.rsqrt(jnp.sum(work[:, :block] * unit, axis=1, keepdims=True))
    factor_ref[...] = jnp.where(column_ids >= row_ids, work[:, :block], 0.0)
    inverse = work[:, block:]
    for tile in range(tiles):
        own = (weighted_low_ref, weighted_high_ref)[tile // count_y][tile % count_y]
        new_ref[pl.ds(tile, block, stride=tiles), :] = mul3(inverse, own)
    for part in range(2):
        span = slice(part * block, (part + 1) * block)
        reduced_ref[part, :, :prior] = mul3(inverse, sums_ref[span, :] * inverse_rows)
        reduced_ref[part, :, prior:] = mul3_t(mul3_t(inverse, with_own[:, span]), inverse)


def permute(value, axis, target):
    count = lax.axis_size(axis)
    pairs = [(i, target(i)) for i in range(count)]
    return lax.ppermute(value, axis, [pair for pair in pairs if 0 <= pair[1] < count])


def swap(value, axis, step):
    return permute(value, axis, lambda i: i ^ step)


def shift(value, axis, step):
    count = lax.axis_size(axis)
    return permute(value, axis, lambda i: (i + step) % count)


def line(value, axis, step):
    return permute(value, axis, lambda i: i + step)


def total_along(value, axis, first=1):
    if lax.axis_size(axis) == 4 and first == 1:
        opposite = shift(value, axis, 2)
        return (value + opposite) + (shift(value, axis, 1) + shift(value, axis, -1))
    step = first
    while step < lax.axis_size(axis):
        value = value + swap(value, axis, step)
        step *= 2
    return value


def halved_total(value):
    half = value.shape[0] // 2
    upper = lax.axis_index("py") % 2 == 1
    first, second = value[:half], value[half:]
    kept = jnp.where(upper, second, first)
    kept = kept + swap(jnp.where(upper, first, second), "py", 1)
    kept = total_along(kept, "py", 2)
    kept = total_along(kept, "px")
    other = swap(kept, "py", 1)
    return jnp.concatenate(
        [jnp.where(upper, other, kept), jnp.where(upper, kept, other)], axis=0
    )


def ring_with_total(low, high, partial, axis):
    if lax.axis_size(axis) == 4:
        from_low, from_high = shift(high, axis, 1), shift(low, axis, -1)
        opposite = shift(partial, axis, 2)
        return from_low, from_high, (partial + opposite) + (from_low[-1] + from_high[-1])
    return line(high, axis, 1), line(low, axis, -1), total_along(partial, axis)


def line_with_total(low, high, partial, axis):
    from_low, from_high = line(high, axis, 1), line(low, axis, -1)
    if lax.axis_size(axis) == 4:
        opposite = swap(partial, axis, 2)
        far = permute(partial, axis, lambda i: {0: 3, 3: 0}.get(i, -1))
        near = from_low[-1] + from_high[-1]
        return from_low, from_high, (partial + opposite) + (near + far)
    return from_low, from_high, total_along(partial, axis)


def shape(*dims, dtype=F32):
    return jax.ShapeDtypeStruct(dims, dtype)


def shards(prior_basis, previous, neighbours, tile_kinds, stiff_tiles, mass_tiles):
    block = previous.shape[0]
    prior, count_x, count_y, side = prior_basis.shape
    tiles = count_x * count_y
    wide = count_y + 2
    rest = prior - block
    kinds = stiff_tiles.shape[0]
    inverse_rows = 1.0 / (tiles * side * lax.axis_size("px") * lax.axis_size("py"))
    basis = prior_basis.reshape(-1, side)
    previous_rows = previous.reshape(-1, side)
    neighbours = neighbours.reshape(-1, tiles)
    tile_kinds = tile_kinds.reshape(-1, tiles)
    position = lax.axis_index("py")
    ends = jnp.stack([position > 0, position < lax.axis_size("py") - 1]).astype(jnp.int32)

    def call(kernel, inputs, outputs, scratch=(), smem=0):
        return pl.pallas_call(
            kernel,
            out_shape=outputs,
            in_specs=[SMEM] * smem + [VMEM] * (len(inputs) - smem),
            out_specs=[VMEM] * len(outputs),
            scratch_shapes=scratch,
            compiler_params=PARAMS,
        )(*inputs)

    side_low, side_high = call(
        functools.partial(pack_kernel, count_x, count_y),
        (basis, previous_rows),
        [shape(count_x, prior + block, side)] * 2,
    )
    deep_high, deep_low, wide_high, wide_low = call(
        tables_kernel,
        (stiff_tiles, mass_tiles),
        [shape(kinds, 2 * side, side, dtype=BF16)] * 2
        + [shape(kinds, side, 2 * side, dtype=BF16)] * 2,
    )
    from_side_low, from_side_high = line(side_high, "py", 1), line(side_low, "py", -1)
    low, high, low_rest, high_rest = call(
        rows_kernel,
        (basis, previous_rows, from_side_low, from_side_high),
        [shape(wide, 2 * block, side)] * 2 + [shape(wide, rest, side)] * 2,
    )
    block_rows = (line(high, "px", 1), low, high, line(low, "px", -1))
    rest_rows = (line(high_rest, "px", 1), low_rest, high_rest, line(low_rest, "px", -1))
    residual_low, residual_high, message_low, message_high, partial = call(
        residual_kernel,
        (neighbours, tile_kinds, *block_rows, low_rest, high_rest, deep_high, deep_low),
        [shape(count_y, block, side)] * 2 + [shape(3, block, side)] * 2 + [shape(block, prior)],
        [pltpu.VMEM((4 * wide, 2 * block, 2 * side), BF16)],
        smem=2,
    )
    from_side_low, from_side_high, partial = ring_with_total(
        message_low, message_high, partial, "py"
    )
    from_side_low, *rest_rows = lax.optimization_barrier((from_side_low, *rest_rows))
    row_low, row_high = call(
        residual_rows_kernel,
        (residual_low, residual_high, from_side_low, from_side_high, partial),
        [shape(wide + 1, block, side)] * 2,
    )
    from_low, from_high, partial = line_with_total(row_low, row_high, partial, "px")
    weighted_low, weighted_high, coupling, sums = call(
        functools.partial(operators_kernel, inverse_rows),
        (
            ends,
            neighbours,
            tile_kinds,
            partial,
            *(from_low, row_low, row_high, from_high),
            *block_rows,
            *rest_rows,
            wide_high,
            wide_low,
        ),
        [shape(count_y, block, side)] * 2 + [shape(block, prior), shape(3 * block, prior)],
        [pltpu.VMEM((4 * wide, 2 * block, side), BF16)],
        smem=3,
    )
    new_block, factor, reduced = call(
        functools.partial(factor_kernel, inverse_rows),
        (halved_total(sums), weighted_low, weighted_high),
        [
            shape(block * tiles, side),
            shape(block, block),
            shape(2, block, prior + block),
        ],
    )
    return (
        new_block.reshape(previous.shape),
        coupling.T,
        factor,
        reduced.swapaxes(1, 2),
    )


def solution(mesh):
    placed = (
        P("case", "px", "py", None),
        P("case", "px", "py", None),
        P(None, "px", "py"),
        P(None, "px", "py"),
        P(),
        P(),
    )
    return jax.shard_map(
        shards,
        mesh=mesh,
        in_specs=placed,
        out_specs=(
            P("case", "px", "py", None),
            P("case", None),
            P("case", None),
            P("case", None, None),
        ),
        check_vma=False,
    )
```

time: 71.1 us -> 70 us (0.985)
  starting transfers between devices: 34.9 us -> 38.5 us
  Pallas kernels: 12.2 us -> 10 us
  local copies, waits for them, and re-layouts: 4.49 us -> 2.72 us
    ppermute x20 -> x19, starting transfers between devices: 34.9 us -> 38.5 us  [permute(): lax.ppermute(value, axis, [pair for pair in pairs if 0 <= pair[1] < count])]
    pallas_call x6 -> x7, Pallas kernels: 12.2 us -> 10 us  [call(): pl.pallas_call(kernel, out_shape=outputs, in_specs=[SMEM] * smem + [VMEM]...]
    unnamed x14 -> x12, local copies, waits for them, and re-layouts: 4.27 us -> 2.55 us
    ppermute x20 -> x19, waiting for transfers between devices: 17.9 us -> 17.4 us  [permute(): lax.ppermute(value, axis, [pair for pair in pairs if 0 <= pair[1] < count])]
  transfers between devices with their start and end apart: 20 -> 19, of which waited for: 9 -> 9; matrix products, arithmetic and copies ran while one was open for 0% -> 0% of each run, Pallas kernels for 5% -> 4%
where the time goes in v5:
time: 70 us; the launch traced here: 69.6 us
  starting transfers between devices  38.5 us (55%)
  waiting for transfers between devices  17.4 us (25%)
  Pallas kernels  10 us (14%)
  local copies, waits for them, and re-layouts  2.72 us (4%)
  between operations  0.85 us (1%)
    ppermute x19, starting transfers between devices, permute(): lax.ppermute(value, axis, [pair for pair in pairs if 0 <= pair[1] < count])  38.5 us
    ppermute x19, waiting for transfers between devices, permute(): lax.ppermute(value, axis, [pair for pair in pairs if 0 <= pair[1] < count])  17.4 us
    pallas_call x7, Pallas kernels, call(): pl.pallas_call(kernel, out_shape=outputs, in_specs=[SMEM] * smem + [VMEM]...  10 us
    unnamed x12, local copies, waits for them, and re-layouts  2.55 us
  transfers between devices with their start and end apart: 19, of which 9 were waited for; matrix products, arithmetic and copies ran while one was open for 0% of the time, Pallas kernels for 4%

profile of v5, /device:TPU:0, one launch (start us, length us, event | category | flops | bytes accessed | tf_op | source)
XLA Modules:
  0.0 69.6 jit_solution(11351145244617219035)
XLA Ops:
  0.6 1.0 %copy-done = f32[128,2,4,128]{3,2,1,0:T(4,128)S(1)} copy-done((f32[128,2,4,128]{3,2,1,0:T(4,128)S(1)}, f32[128,2,4,128]{3,2,1,0:T(4,128)}, u32[]{:S(2)}) %copy-start) | copy-done | bytes 524312
  1.7 0.9 %copy-done.1 = f32[32,2,4,128]{3,2,1,0:T(4,128)S(1)} copy-done((f32[32,2,4,128]{3,2,1,0:T(4,128)S(1)}, f32[32,2,4,128]{3,2,1,0:T(4,128)}, u32[]{:S(2)}) %copy-start.1) | copy-done | bytes 131096
  2.6 0.1 shard_map.93
  2.6 0.0 copy-start.2
  2.7 2.5 %collective-permute-start = (f32[2,160,128]{2,1,0:T(8,128)S(1)}, f32[2,160,128]{2,1,0:T(8,128)S(1)}, u32[]{:S(2)}, u32[]{:S(2)}) collective-permute-start(f32[2,160,128]{2,1,0:T(8,128)S(1)} %get-tuple-element.33), channel_id=1, source_target_pairs={{0,1},{1,2},{2,3},{4,5},{5,6},{6,7},{8,9},{9,10},{10,11},{12,13},{... | collective-permute-start | bytes 491528 | tf_op jit(solution)/shard_map/ppermute | solution.py:270
  5.2 1.3 %collective-permute-start.1 = (f32[2,160,128]{2,1,0:T(8,128)S(1)}, f32[2,160,128]{2,1,0:T(8,128)S(1)}, u32[]{:S(2)}, u32[]{:S(2)}) collective-permute-start(f32[2,160,128]{2,1,0:T(8,128)S(1)} %get-tuple-element.34), channel_id=1, source_target_pairs={{1,0},{2,1},{3,2},{5,4},{6,5},{7,6},{9,8},{10,9},{11,10},{13,12},{... | collective-permute-start | bytes 491528 | tf_op jit(solution)/shard_map/ppermute | solution.py:270
  6.5 0.0 collective-permute-done.side_low_ref
  6.5 4.1 %collective-permute-done.1.side_high_ref = f32[2,160,128]{2,1,0:T(8,128)S(1)} collective-permute-done((f32[2,160,128]{2,1,0:T(8,128)S(1)}, f32[2,160,128]{2,1,0:T(8,128)S(1)}, u32[]{:S(2)}, u32[]{:S(2)}) %collective-permute-start.1) | collective-permute-done | bytes 163872 | tf_op jit(solution)/shard_map/ppermute | solution.py:270
  10.6 0.1 shard_map.94
  10.7 0.0 copy-start.4
  10.7 3.5 %collective-permute-start.2 = (f32[6,64,128]{2,1,0:T(8,128)S(1)}, f32[6,64,128]{2,1,0:T(8,128)S(1)}, u32[]{:S(2)}, u32[]{:S(2)}) collective-permute-start(f32[6,64,128]{2,1,0:T(8,128)S(1)} %get-tuple-element.35.high_ref.refs_6_), channel_id=1, source_target_pairs={{0,4},{4,8},{8,12},{1,5},{5,9},{9,13},{2,6},{6,10},{10,14},{3,7},{... | collective-permute-start | bytes 589832 | tf_op jit(solution)/shard_map/ppermute | solution.py:270
  14.2 1.3 %collective-permute-start.3 = (f32[6,64,128]{2,1,0:T(8,128)S(1)}, f32[6,64,128]{2,1,0:T(8,128)S(1)}, u32[]{:S(2)}, u32[]{:S(2)}) collective-permute-start(f32[6,64,128]{2,1,0:T(8,128)S(1)} %get-tuple-element.36.low_ref.refs_5_), channel_id=1, source_target_pairs={{4,0},{8,4},{12,8},{5,1},{9,5},{13,9},{6,2},{10,6},{14,10},{7,3},{... | collective-permute-start | bytes 589832 | tf_op jit(solution)/shard_map/ppermute | solution.py:270
  15.5 5.3 %collective-permute-start.8 = (f32[6,96,128]{2,1,0:T(8,128)S(1)}, f32[6,96,128]{2,1,0:T(8,128)}, u32[]{:S(2)}, u32[]{:S(2)}) collective-permute-start(f32[6,96,128]{2,1,0:T(8,128)S(1)} %get-tuple-element.51.high_rest_ref.refs_10_), channel_id=1, source_target_pairs={{0,4},{4,8},{8,12},{1,5},{5,9},{9,13},{2,6},{6,10},{10,14},{3,7},{... | collective-permute-start | bytes 884744 | tf_op jit(solution)/shard_map/ppermute | solution.py:270
  20.8 1.3 %collective-permute-start.9 = (f32[6,96,128]{2,1,0:T(8,128)S(1)}, f32[6,96,128]{2,1,0:T(8,128)}, u32[]{:S(2)}, u32[]{:S(2)}) collective-permute-start(f32[6,96,128]{2,1,0:T(8,128)S(1)} %get-tuple-element.50.low_rest_ref.refs_9_), channel_id=1, source_target_pairs={{4,0},{8,4},{12,8},{5,1},{9,5},{13,9},{6,2},{10,6},{14,10},{7,3},{... | collective-permute-start | bytes 884744 | tf_op jit(solution)/shard_map/ppermute | solution.py:270
  22.1 0.0 copy-start.5
  22.1 0.1 copy.12.neighbours_ref
  22.2 0.6 copy-done.5
  22.8 0.1 copy.13.kinds_ref
  22.8 0.2 shard_map.95
  23.1 0.0 collective-permute-done.2.from_low_ref.refs_4_
  23.1 0.0 collective-permute-done.3.from_high_ref.refs_7_
  23.1 2.9 %shard_map.96 = (f32[4,32,128]{2,1,0:T(8,128)S(1)}, f32[4,32,128]{2,1,0:T(8,128)S(1)}, f32[3,32,128]{2,1,0:T(8,128)S(1)}, f32[3,32,128]{2,1,0:T(8,128)S(1)}, f32[32,128]{1,0:T(8,128)S(1)}) custom-call(s32[5,8]{1,0:T(8,128)S(1)} %copy.12.neighbours_ref, s32[5,8]{1,0:T(8,128)S(1)} %copy.13.kinds_ref, ...), custom_call_target="tpu_custom_call" | custom-call | tf_op jit(solution)/shard_map/pallas_call | solution.py:349
  26.0 3.0 %collective-permute-start.5 = (f32[3,32,128]{2,1,0:T(8,128)S(1)}, f32[3,32,128]{2,1,0:T(8,128)S(1)}, u32[]{:S(2)}, u32[]{:S(2)}) collective-permute-start(f32[3,32,128]{2,1,0:T(8,128)S(1)} %get-tuple-element.42), channel_id=1, source_target_pairs={{0,1},{1,2},{2,3},{3,0},{4,5},{5,6},{6,7},{7,4},{8,9},{9,10},{10,1... | collective-permute-start | bytes 147464 | tf_op jit(solution)/shard_map/ppermute | solution.py:270
  29.0 2.3 %collective-permute-start.4 = (f32[32,128]{1,0:T(8,128)S(1)}, f32[32,128]{1,0:T(8,128)S(1)}, u32[]{:S(2)}, u32[]{:S(2)}) collective-permute-start(f32[32,128]{1,0:T(8,128)S(1)} %get-tuple-element.41), channel_id=1, source_target_pairs={{0,2},{1,3},{2,0},{3,1},{4,6},{5,7},{6,4},{7,5},{8,10},{9,11},{10,... | collective-permute-start | bytes 49160 | tf_op jit(solution)/shard_map/ppermute | solution.py:270
  31.3 2.2 %collective-permute-done.4 = f32[32,128]{1,0:T(8,128)S(1)} collective-permute-done((f32[32,128]{1,0:T(8,128)S(1)}, f32[32,128]{1,0:T(8,128)S(1)}, u32[]{:S(2)}, u32[]{:S(2)}) %collective-permute-start.4) | collective-permute-done | bytes 16416 | tf_op jit(solution)/shard_map/ppermute | solution.py:270
  33.6 0.0 collective-permute-done.5.side_low_ref
  33.6 0.0 collective-permute-done.6.side_high_ref
  33.6 0.0 collective-permute-done.8.refs_8_
  33.6 0.0 collective-permute-done.9.refs_11_
  33.6 4.6 %collective-permute-start.10 = (f32[7,32,128]{2,1,0:T(8,128)S(1)}, f32[7,32,128]{2,1,0:T(8,128)S(1)}, u32[]{:S(2)}, u32[]{:S(2)}) collective-permute-start(f32[7,32,128]{2,1,0:T(8,128)S(1)} %get-tuple-element.47.refs_2_), channel_id=1, source_target_pairs={{0,4},{4,8},{8,12},{1,5},{5,9},{9,13},{2,6},{6,10},{10,14},{3,7},{... | collective-permute-start | bytes 344072 | tf_op jit(solution)/shard_map/ppermute | solution.py:270
  38.2 1.3 %collective-permute-start.11 = (f32[7,32,128]{2,1,0:T(8,128)S(1)}, f32[7,32,128]{2,1,0:T(8,128)S(1)}, u32[]{:S(2)}, u32[]{:S(2)}) collective-permute-start(f32[7,32,128]{2,1,0:T(8,128)S(1)} %get-tuple-element.48.refs_1_), channel_id=1, source_target_pairs={{4,0},{8,4},{12,8},{5,1},{9,5},{13,9},{6,2},{10,6},{14,10},{7,3},{... | collective-permute-start | bytes 344072 | tf_op jit(solution)/shard_map/ppermute | solution.py:270
  39.5 6.6 %collective-permute-start.12 = (f32[32,128]{1,0:T(8,128)S(1)}, f32[32,128]{1,0:T(8,128)S(1)}, u32[]{:S(2)}, u32[]{:S(2)}) collective-permute-start(f32[32,128]{1,0:T(8,128)S(1)} %fusion.4.partial_ref), channel_id=1, source_target_pairs={{0,12},{12,0},{1,13},{13,1},{2,14},{14,2},{3,15},{15,3},{16,28},{2... | collective-permute-start | bytes 49160 | tf_op jit(solution)/shard_map/ppermute | solution.py:270
  46.1 0.1 collective-permute-start.7
  46.2 0.1 add_convert_fusion.ends_ref
  46.3 1.5 %collective-permute-done.12 = f32[32,128]{1,0:T(8,128)S(1)} collective-permute-done((f32[32,128]{1,0:T(8,128)S(1)}, f32[32,128]{1,0:T(8,128)S(1)}, u32[]{:S(2)}, u32[]{:S(2)}) %collective-permute-start.12) | collective-permute-done | bytes 16416 | tf_op jit(solution)/shard_map/ppermute | solution.py:270
  47.8 3.0 %collective-permute-done.7 = f32[32,128]{1,0:T(8,128)S(1)} collective-permute-done((f32[32,128]{1,0:T(8,128)S(1)}, f32[32,128]{1,0:T(8,128)S(1)}, u32[]{:S(2)}, u32[]{:S(2)}) %collective-permute-start.7) | collective-permute-done | bytes 16416 | tf_op jit(solution)/shard_map/ppermute | solution.py:270
  50.8 4.1 %shard_map.98 = (f32[4,32,128]{2,1,0:T(8,128)S(1)}, f32[4,32,128]{2,1,0:T(8,128)S(1)}, f32[32,128]{1,0:T(8,128)}, f32[96,128]{1,0:T(8,128)S(1)}) custom-call(s32[2]{0:T(128)S(1)} %add_convert_fusion.ends_ref, s32[5,8]{1,0:T(8,128)S(1)} %copy.12.neighbours_ref, s32[5,8]{1,0:T(8,128)S(1)} %copy.13.kinds_ref, f32[32,128]{1,0:T(8,128)S(1)} %fusion.2.partial_ref, ...), custom_call_target="tpu_custom_call" | custom-call | tf_op jit(solution)/shard_map/pallas_call | solution.py:349
  54.9 1.2 %collective-permute-done.13 = f32[48,128]{1,0:T(8,128)S(1)} collective-permute-done((f32[48,128]{1,0:T(8,128)S(1)}, f32[48,128]{1,0:T(8,128)S(1)}, u32[]{:S(2)}, u32[]{:S(2)}) %collective-permute-start.13) | collective-permute-done | bytes 24608 | tf_op jit(solution)/shard_map/ppermute | solution.py:270
  56.1 1.5 %collective-permute-start.14 = (f32[48,128]{1,0:T(8,128)S(1)}, f32[48,128]{1,0:T(8,128)S(1)}, u32[]{:S(2)}, u32[]{:S(2)}) collective-permute-start(f32[48,128]{1,0:T(8,128)S(1)} %select_add_fusion), channel_id=1, source_target_pairs={{0,2},{1,3},{2,0},{3,1},{4,6},{5,7},{6,4},{7,5},{8,10},{9,11},{10,... | collective-permute-start | bytes 73736 | tf_op jit(solution)/shard_map/ppermute | solution.py:270
  57.6 2.3 %collective-permute-done.14 = f32[48,128]{1,0:T(8,128)S(1)} collective-permute-done((f32[48,128]{1,0:T(8,128)S(1)}, f32[48,128]{1,0:T(8,128)S(1)}, u32[]{:S(2)}, u32[]{:S(2)}) %collective-permute-start.14) | collective-permute-done | bytes 24608 | tf_op jit(solution)/shard_map/ppermute | solution.py:270
  60.0 0.1 collective-permute-start.15
  60.1 1.3 %collective-permute-start.16 = (f32[48,128]{1,0:T(8,128)S(1)}, f32[48,128]{1,0:T(8,128)S(1)}, u32[]{:S(2)}, u32[]{:S(2)}) collective-permute-start(f32[48,128]{1,0:T(8,128)S(1)} %add.57), channel_id=1, source_target_pairs={{0,4},{4,8},{8,12},{12,0},{1,5},{5,9},{9,13},{13,1},{2,6},{6,10},{... | collective-permute-start | bytes 73736 | tf_op jit(solution)/shard_map/ppermute | solution.py:270
  61.4 2.5 %collective-permute-start.17 = (f32[48,128]{1,0:T(8,128)S(1)}, f32[48,128]{1,0:T(8,128)S(1)}, u32[]{:S(2)}, u32[]{:S(2)}) collective-permute-start(f32[48,128]{1,0:T(8,128)S(1)} %add.57), channel_id=1, source_target_pairs={{0,12},{4,0},{8,4},{12,8},{1,13},{5,1},{9,5},{13,9},{2,14},{6,2},{... | collective-permute-start | bytes 73736 | tf_op jit(solution)/shard_map/ppermute | solution.py:270
  63.9 0.8 %collective-permute-done.15 = f32[48,128]{1,0:T(8,128)S(1)} collective-permute-done((f32[48,128]{1,0:T(8,128)S(1)}, f32[48,128]{1,0:T(8,128)S(1)}, u32[]{:S(2)}, u32[]{:S(2)}) %collective-permute-start.15) | collective-permute-done | bytes 24608 | tf_op jit(solution)/shard_map/ppermute | solution.py:270
  64.7 1.0 %collective-permute-done.16 = f32[48,128]{1,0:T(8,128)S(1)} collective-permute-done((f32[48,128]{1,0:T(8,128)S(1)}, f32[48,128]{1,0:T(8,128)S(1)}, u32[]{:S(2)}, u32[]{:S(2)}) %collective-permute-start.16) | collective-permute-done | bytes 24608 | tf_op jit(solution)/shard_map/ppermute | solution.py:270
  65.7 0.1 collective-permute-start.18
  65.8 1.2 %collective-permute-done.18 = f32[48,128]{1,0:T(8,128)S(1)} collective-permute-done((f32[48,128]{1,0:T(8,128)S(1)}, f32[48,128]{1,0:T(8,128)S(1)}, u32[]{:S(2)}, u32[]{:S(2)}) %collective-permute-start.18) | collective-permute-done | bytes 24608 | tf_op jit(solution)/shard_map/ppermute | solution.py:270
  67.0 2.6 %shard_map.99 = (f32[256,128]{1,0:T(8,128)}, f32[32,32]{1,0:T(8,128)}, f32[2,32,160]{2,1,0:T(8,128)}) custom-call(f32[96,128]{1,0:T(8,128)S(1)} %pad_maximum_fusion.sums_ref, f32[4,32,128]{2,1,0:T(8,128)S(1)} %get-tuple-element.56.weighted_low_ref, f32[4,32,128]{2,1,0:T(8,128)S(1)} %get-tuple-element.57.weighted_high_ref), custom_call_target="tpu_custom_call" | custom-call | tf_op jit(solution)/shard_map/pallas_call | solution.py:349
  (20 shorter events, 0.1 us)
Async XLA Ops:
  0.6 1.0 %copy-start = (f32[128,2,4,128]{3,2,1,0:T(4,128)S(1)}, f32[128,2,4,128]{3,2,1,0:T(4,128)}, u32[]{:S(2)}) copy-start(f32[128,2,4,128]{3,2,1,0:T(4,128)} %param.6) | copy-start | bytes 1572868
  1.7 0.9 %copy-start.1 = (f32[32,2,4,128]{3,2,1,0:T(4,128)S(1)}, f32[32,2,4,128]{3,2,1,0:T(4,128)}, u32[]{:S(2)}) copy-start(f32[32,2,4,128]{3,2,1,0:T(4,128)} %param.7) | copy-start | bytes 393220
  2.6 20.3 %copy-start.3 = (f32[8,128,128]{2,1,0:T(8,128)S(1)}, f32[8,128,128]{2,1,0:T(8,128)}, u32[]{:S(2)}) copy-start(f32[8,128,128]{2,1,0:T(8,128)} %mass_ref.1) | copy-start | bytes 1572868
  2.6 20.2 %copy-start.2 = (f32[8,128,128]{2,1,0:T(8,128)S(1)}, f32[8,128,128]{2,1,0:T(8,128)}, u32[]{:S(2)}) copy-start(f32[8,128,128]{2,1,0:T(8,128)} %stiff_ref.1) | copy-start | bytes 1572868
  2.7 3.8 %collective-permute-start = (f32[2,160,128]{2,1,0:T(8,128)S(1)}, f32[2,160,128]{2,1,0:T(8,128)S(1)}, u32[]{:S(2)}, u32[]{:S(2)}) collective-permute-start(f32[2,160,128]{2,1,0:T(8,128)S(1)} %get-tuple-element.33), channel_id=1, source_target_pairs={{0,1},{1,2},{2,3},{4,5},{5,6},{6,7},{8,9},{9,10},{10,11},{12,13},{... | collective-permute-start | bytes 491528 | tf_op jit(solution)/shard_map/ppermute | solution.py:270
  5.2 5.4 %collective-permute-start.1 = (f32[2,160,128]{2,1,0:T(8,128)S(1)}, f32[2,160,128]{2,1,0:T(8,128)S(1)}, u32[]{:S(2)}, u32[]{:S(2)}) collective-permute-start(f32[2,160,128]{2,1,0:T(8,128)S(1)} %get-tuple-element.34), channel_id=1, source_target_pairs={{1,0},{2,1},{3,2},{5,4},{6,5},{7,6},{9,8},{10,9},{11,10},{13,12},{... | collective-permute-start | bytes 491528 | tf_op jit(solution)/shard_map/ppermute | solution.py:270
  10.7 11.4 %copy-start.4 = (s32[5,2,4]{0,2,1:T(4,128)S(1)}, s32[5,2,4]{0,2,1:T(4,128)}, u32[]{:S(2)}) copy-start(s32[5,2,4]{0,2,1:T(4,128)} %param.8) | copy-start | bytes 484
  10.7 12.4 %collective-permute-start.2 = (f32[6,64,128]{2,1,0:T(8,128)S(1)}, f32[6,64,128]{2,1,0:T(8,128)S(1)}, u32[]{:S(2)}, u32[]{:S(2)}) collective-permute-start(f32[6,64,128]{2,1,0:T(8,128)S(1)} %get-tuple-element.35.high_ref.refs_6_), channel_id=1, source_target_pairs={{0,4},{4,8},{8,12},{1,5},{5,9},{9,13},{2,6},{6,10},{10,14},{3,7},{... | collective-permute-start | bytes 589832 | tf_op jit(solution)/shard_map/ppermute | solution.py:270
  14.2 8.9 %collective-permute-start.3 = (f32[6,64,128]{2,1,0:T(8,128)S(1)}, f32[6,64,128]{2,1,0:T(8,128)S(1)}, u32[]{:S(2)}, u32[]{:S(2)}) collective-permute-start(f32[6,64,128]{2,1,0:T(8,128)S(1)} %get-tuple-element.36.low_ref.refs_5_), channel_id=1, source_target_pairs={{4,0},{8,4},{12,8},{5,1},{9,5},{13,9},{6,2},{10,6},{14,10},{7,3},{... | collective-permute-start | bytes 589832 | tf_op jit(solution)/shard_map/ppermute | solution.py:270
  15.5 18.1 %collective-permute-start.8 = (f32[6,96,128]{2,1,0:T(8,128)S(1)}, f32[6,96,128]{2,1,0:T(8,128)}, u32[]{:S(2)}, u32[]{:S(2)}) collective-permute-start(f32[6,96,128]{2,1,0:T(8,128)S(1)} %get-tuple-element.51.high_rest_ref.refs_10_), channel_id=1, source_target_pairs={{0,4},{4,8},{8,12},{1,5},{5,9},{9,13},{2,6},{6,10},{10,14},{3,7},{... | collective-permute-start | bytes 884744 | tf_op jit(solution)/shard_map/ppermute | solution.py:270
  20.8 12.8 %collective-permute-start.9 = (f32[6,96,128]{2,1,0:T(8,128)S(1)}, f32[6,96,128]{2,1,0:T(8,128)}, u32[]{:S(2)}, u32[]{:S(2)}) collective-permute-start(f32[6,96,128]{2,1,0:T(8,128)S(1)} %get-tuple-element.50.low_rest_ref.refs_9_), channel_id=1, source_target_pairs={{4,0},{8,4},{12,8},{5,1},{9,5},{13,9},{6,2},{10,6},{14,10},{7,3},{... | collective-permute-start | bytes 884744 | tf_op jit(solution)/shard_map/ppermute | solution.py:270
  22.1 0.7 copy-start.5
  26.0 7.6 %collective-permute-start.5 = (f32[3,32,128]{2,1,0:T(8,128)S(1)}, f32[3,32,128]{2,1,0:T(8,128)S(1)}, u32[]{:S(2)}, u32[]{:S(2)}) collective-permute-start(f32[3,32,128]{2,1,0:T(8,128)S(1)} %get-tuple-element.42), channel_id=1, source_target_pairs={{0,1},{1,2},{2,3},{3,0},{4,5},{5,6},{6,7},{7,4},{8,9},{9,10},{10,1... | collective-permute-start | bytes 147464 | tf_op jit(solution)/shard_map/ppermute | solution.py:270
  29.0 4.6 %collective-permute-start.6 = (f32[3,32,128]{2,1,0:T(8,128)S(1)}, f32[3,32,128]{2,1,0:T(8,128)S(1)}, u32[]{:S(2)}, u32[]{:S(2)}) collective-permute-start(f32[3,32,128]{2,1,0:T(8,128)S(1)} %get-tuple-element.43), channel_id=1, source_target_pairs={{0,3},{1,0},{2,1},{3,2},{4,7},{5,4},{6,5},{7,6},{8,11},{9,8},{10,9... | collective-permute-start | bytes 147464 | tf_op jit(solution)/shard_map/ppermute | solution.py:270
  29.0 4.5 %collective-permute-start.4 = (f32[32,128]{1,0:T(8,128)S(1)}, f32[32,128]{1,0:T(8,128)S(1)}, u32[]{:S(2)}, u32[]{:S(2)}) collective-permute-start(f32[32,128]{1,0:T(8,128)S(1)} %get-tuple-element.41), channel_id=1, source_target_pairs={{0,2},{1,3},{2,0},{3,1},{4,6},{5,7},{6,4},{7,5},{8,10},{9,11},{10,... | collective-permute-start | bytes 49160 | tf_op jit(solution)/shard_map/ppermute | solution.py:270
  33.6 17.2 %collective-permute-start.10 = (f32[7,32,128]{2,1,0:T(8,128)S(1)}, f32[7,32,128]{2,1,0:T(8,128)S(1)}, u32[]{:S(2)}, u32[]{:S(2)}) collective-permute-start(f32[7,32,128]{2,1,0:T(8,128)S(1)} %get-tuple-element.47.refs_2_), channel_id=1, source_target_pairs={{0,4},{4,8},{8,12},{1,5},{5,9},{9,13},{2,6},{6,10},{10,14},{3,7},{... | collective-permute-start | bytes 344072 | tf_op jit(solution)/shard_map/ppermute | solution.py:270
  38.2 12.6 %collective-permute-start.11 = (f32[7,32,128]{2,1,0:T(8,128)S(1)}, f32[7,32,128]{2,1,0:T(8,128)S(1)}, u32[]{:S(2)}, u32[]{:S(2)}) collective-permute-start(f32[7,32,128]{2,1,0:T(8,128)S(1)} %get-tuple-element.48.refs_1_), channel_id=1, source_target_pairs={{4,0},{8,4},{12,8},{5,1},{9,5},{13,9},{6,2},{10,6},{14,10},{7,3},{... | collective-permute-start | bytes 344072 | tf_op jit(solution)/shard_map/ppermute | solution.py:270
  39.5 8.3 %collective-permute-start.12 = (f32[32,128]{1,0:T(8,128)S(1)}, f32[32,128]{1,0:T(8,128)S(1)}, u32[]{:S(2)}, u32[]{:S(2)}) collective-permute-start(f32[32,128]{1,0:T(8,128)S(1)} %fusion.4.partial_ref), channel_id=1, source_target_pairs={{0,12},{12,0},{1,13},{13,1},{2,14},{14,2},{3,15},{15,3},{16,28},{2... | collective-permute-start | bytes 49160 | tf_op jit(solution)/shard_map/ppermute | solution.py:270
  46.1 4.7 %collective-permute-start.7 = (f32[32,128]{1,0:T(8,128)S(1)}, f32[32,128]{1,0:T(8,128)S(1)}, u32[]{:S(2)}, u32[]{:S(2)}) collective-permute-start(f32[32,128]{1,0:T(8,128)S(1)} %fusion.4.partial_ref), channel_id=1, source_target_pairs={{0,8},{4,12},{8,0},{12,4},{1,9},{5,13},{9,1},{13,5},{2,10},{6,14},... | collective-permute-start | bytes 49160 | tf_op jit(solution)/shard_map/ppermute | solution.py:270
  54.9 1.2 %collective-permute-start.13 = (f32[48,128]{1,0:T(8,128)S(1)}, f32[48,128]{1,0:T(8,128)S(1)}, u32[]{:S(2)}, u32[]{:S(2)}) collective-permute-start(f32[48,128]{1,0:T(8,128)S(1)} %slice_select_fusion), channel_id=1, source_target_pairs={{0,1},{1,0},{2,3},{3,2},{4,5},{5,4},{6,7},{7,6},{8,9},{9,8},{10,11... | collective-permute-start | bytes 73736 | tf_op jit(solution)/shard_map/ppermute | solution.py:270
  56.1 3.8 %collective-permute-start.14 = (f32[48,128]{1,0:T(8,128)S(1)}, f32[48,128]{1,0:T(8,128)S(1)}, u32[]{:S(2)}, u32[]{:S(2)}) collective-permute-start(f32[48,128]{1,0:T(8,128)S(1)} %select_add_fusion), channel_id=1, source_target_pairs={{0,2},{1,3},{2,0},{3,1},{4,6},{5,7},{6,4},{7,5},{8,10},{9,11},{10,... | collective-permute-start | bytes 73736 | tf_op jit(solution)/shard_map/ppermute | solution.py:270
  60.0 4.7 %collective-permute-start.15 = (f32[48,128]{1,0:T(8,128)S(1)}, f32[48,128]{1,0:T(8,128)S(1)}, u32[]{:S(2)}, u32[]{:S(2)}) collective-permute-start(f32[48,128]{1,0:T(8,128)S(1)} %add.57), channel_id=1, source_target_pairs={{0,8},{4,12},{8,0},{12,4},{1,9},{5,13},{9,1},{13,5},{2,10},{6,14},... | collective-permute-start | bytes 73736 | tf_op jit(solution)/shard_map/ppermute | solution.py:270
  60.1 5.6 %collective-permute-start.16 = (f32[48,128]{1,0:T(8,128)S(1)}, f32[48,128]{1,0:T(8,128)S(1)}, u32[]{:S(2)}, u32[]{:S(2)}) collective-permute-start(f32[48,128]{1,0:T(8,128)S(1)} %add.57), channel_id=1, source_target_pairs={{0,4},{4,8},{8,12},{12,0},{1,5},{5,9},{9,13},{13,1},{2,6},{6,10},{... | collective-permute-start | bytes 73736 | tf_op jit(solution)/shard_map/ppermute | solution.py:270
  61.4 4.3 %collective-permute-start.17 = (f32[48,128]{1,0:T(8,128)S(1)}, f32[48,128]{1,0:T(8,128)S(1)}, u32[]{:S(2)}, u32[]{:S(2)}) collective-permute-start(f32[48,128]{1,0:T(8,128)S(1)} %add.57), channel_id=1, source_target_pairs={{0,12},{4,0},{8,4},{12,8},{1,13},{5,1},{9,5},{13,9},{2,14},{6,2},{... | collective-permute-start | bytes 73736 | tf_op jit(solution)/shard_map/ppermute | solution.py:270
  65.7 1.3 %collective-permute-start.18 = (f32[48,128]{1,0:T(8,128)S(1)}, f32[48,128]{1,0:T(8,128)S(1)}, u32[]{:S(2)}, u32[]{:S(2)}) collective-permute-start(f32[48,128]{1,0:T(8,128)S(1)} %add_add_fusion), channel_id=1, source_target_pairs={{0,1},{1,0},{2,3},{3,2},{4,5},{5,4},{6,7},{7,6},{8,9},{9,8},{10,11... | collective-permute-start | bytes 73736 | tf_op jit(solution)/shard_map/ppermute | solution.py:270

commit v6 on v5

v6 whole, which is shorter than its diff:
```python
import functools

import jax
import jax.numpy as jnp
from jax import lax
from jax.experimental import pallas as pl
from jax.experimental.pallas import tpu as pltpu
from jax.sharding import PartitionSpec as P

F32 = jnp.float32
BF16 = jnp.bfloat16
VMEM = pl.BlockSpec(memory_space=pltpu.VMEM)
SMEM = pl.BlockSpec(memory_space=pltpu.SMEM)
PARAMS = pltpu.CompilerParams(vmem_limit_bytes=24 * 1024 * 1024)


def split(value):
    high = value.astype(BF16)
    return high, (value - high.astype(F32)).astype(BF16)


def mul(left, right):
    return jnp.dot(left, right, preferred_element_type=F32)


def mul_t(left, right):
    return lax.dot_general(left, right, (((1,), (1,)), ((), ())), preferred_element_type=F32)


def mul3(left, right):
    left_high, left_low = split(left)
    right_high, right_low = split(right)
    return mul(left_high, right_high) + (mul(left_high, right_low) + mul(left_low, right_high))


def mul3_t(left, right):
    left_high, left_low = split(left)
    right_high, right_low = split(right)
    return mul_t(left_high, right_high) + (
        mul_t(left_high, right_low) + mul_t(left_low, right_high)
    )


def tables_kernel(stiff_ref, mass_ref, deep_high_ref, deep_low_ref, wide_high_ref, wide_low_ref):
    side = stiff_ref.shape[1]
    for kind in range(stiff_ref.shape[0]):
        for place, ref in enumerate((stiff_ref, mass_ref)):
            high, low = split(ref[kind])
            span = slice(place * side, (place + 1) * side)
            deep_high_ref[kind, span, :] = high
            deep_low_ref[kind, span, :] = low
            wide_high_ref[kind, :, span] = high
            wide_low_ref[kind, :, span] = low


def pick(flag, first, second):
    flag = flag > 0.0
    return jnp.where(flag, first, second), jnp.where(flag, second, first)


def flag_at(flags_ref, place):
    return flags_ref[place : place + 1, :]


def pack_kernel(flags_ref, basis_ref, previous_ref, side_a_ref, side_b_ref, row_a_ref, row_b_ref):
    count_x, sides, side = side_a_ref.shape
    count_y, both, _ = row_a_ref.shape
    tiles = count_x * count_y
    block = both // 2
    rest = sides - both

    def tile_of(i, j):
        tile = i * count_y + j
        return (
            basis_ref[pl.ds(tile, rest, stride=tiles), :],
            basis_ref[pl.ds(rest * tiles + tile, block, stride=tiles), :],
            previous_ref[pl.ds(tile, block, stride=tiles), :],
        )

    spans = (slice(0, rest), slice(rest, rest + block), slice(rest + block, sides))
    for i in range(count_x):
        for span, low, high in zip(spans, tile_of(i, 0), tile_of(i, count_y - 1)):
            side_a_ref[i, span, :], side_b_ref[i, span, :] = pick(
                flag_at(flags_ref, 0), low, high
            )
    for j in range(count_y):
        for part in range(2):
            span = slice(part * block, (part + 1) * block)
            row_a_ref[j, span, :], row_b_ref[j, span, :] = pick(
                flag_at(flags_ref, 1), tile_of(0, j)[part + 1], tile_of(1, j)[part + 1]
            )


def corners_kernel(
    flags_ref,
    basis_ref,
    side_a_ref,
    side_b_ref,
    corner_a_ref,
    corner_b_ref,
    rest_a_ref,
    rest_b_ref,
):
    wide, rest, _ = rest_a_ref.shape
    tiles = 2 * (wide - 2)
    odd_y, odd_x = flag_at(flags_ref, 0), flag_at(flags_ref, 1)
    ends = [pick(odd_y, side_a_ref[i], side_b_ref[i]) for i in range(2)]
    for place, j in ((0, 0), (1, wide - 1)):
        corner_a_ref[place], corner_b_ref[place] = pick(
            odd_x, ends[0][place][rest:], ends[1][place][rest:]
        )
        rest_a_ref[j], rest_b_ref[j] = pick(
            odd_x, ends[0][place][:rest], ends[1][place][:rest]
        )
    for j in range(wide - 2):
        rest_a_ref[j + 1], rest_b_ref[j + 1] = pick(
            odd_x,
            basis_ref[pl.ds(j, rest, stride=tiles), :],
            basis_ref[pl.ds(wide - 2 + j, rest, stride=tiles), :],
        )


def source_of(neighbours_ref, k, tile, count_y):
    neighbour = neighbours_ref[k, tile]
    down = neighbour // 3
    return (tile // count_y + down) * (count_y + 2) + tile % count_y + neighbour - 3 * down


def residual_kernel(
    neighbours_ref,
    kinds_ref,
    flags_ref,
    row_a_ref,
    row_b_ref,
    from_row_a_ref,
    from_row_b_ref,
    from_side_a_ref,
    from_side_b_ref,
    from_corner_a_ref,
    from_corner_b_ref,
    rest_a_ref,
    rest_b_ref,
    table_high_ref,
    table_low_ref,
    residual_low_ref,
    residual_high_ref,
    message_a_ref,
    message_b_ref,
    partial_ref,
    current_ref,
    ext_ref,
):
    count_y, both, side = row_a_ref.shape
    wide = count_y + 2
    block = both // 2
    rest = rest_a_ref.shape[1]
    odd_y, odd_x, in_low_y, in_high_y, in_low_x, in_high_x = (
        flag_at(flags_ref, place) for place in range(6)
    )

    def store(i, j, value):
        current_ref[i * wide + j] = value[:block]
        for part in range(2):
            high, low = split(value[part * block : (part + 1) * block])
            ext_ref[i * wide + j, :block, part * side : (part + 1) * side] = high
            ext_ref[i * wide + j, block:, part * side : (part + 1) * side] = low

    own = {}
    for j in range(count_y):
        own[0, j], own[1, j] = pick(odd_x, row_a_ref[j], row_b_ref[j])
        store(1, j + 1, own[0, j])
        store(2, j + 1, own[1, j])
        low, high = pick(odd_x, from_row_a_ref[j], from_row_b_ref[j])
        store(0, j + 1, low * in_low_x)
        store(3, j + 1, high * in_high_x)
    for i in range(2):
        low, high = pick(odd_y, from_side_a_ref[i, rest:, :], from_side_b_ref[i, rest:, :])
        store(i + 1, 0, low * in_low_y)
        store(i + 1, wide - 1, high * in_high_y)
    for place, j, inside in ((0, 0, in_low_y), (1, wide - 1, in_high_y)):
        low, high = pick(odd_x, from_corner_a_ref[place], from_corner_b_ref[place])
        store(0, j, low * (in_low_x * inside))
        store(3, j, high * (in_high_x * inside))
    partial = jnp.zeros((block, rest + block), F32)
    ends = {}
    for tile in range(2 * count_y):
        i, j = tile // count_y, tile % count_y
        total = 4.0 * own[i, j][:block] + own[i, j][block:]
        for k in range(neighbours_ref.shape[0]):
            source = source_of(neighbours_ref, k, tile, count_y)
            kind = kinds_ref[k, tile]
            chosen = ext_ref[source]
            pair = mul(chosen, table_high_ref[kind])
            total = total + (
                pair[:block] + (pair[block:] + mul(chosen[:block], table_low_ref[kind]))
            )
        (residual_low_ref, residual_high_ref)[i][j] = total
        ends[i, j] = total
        rest_tile = pick(odd_x, rest_a_ref[j + 1], rest_b_ref[j + 1])[i]
        basis_tile = jnp.concatenate([rest_tile, own[i, j][:block]], axis=0)
        partial = partial + mul3_t(total, basis_tile)
    for i in range(2):
        message_a_ref[i], message_b_ref[i] = pick(odd_y, ends[i, 0], ends[i, count_y - 1])
    message_a_ref[2] = partial
    partial_ref[...] = partial


def residual_rows_kernel(
    flags_ref, low_ref, high_ref, side_a_ref, side_b_ref, partial_ref, row_a_ref, row_b_ref
):
    count_y = low_ref.shape[0]
    odd_y, odd_x = flag_at(flags_ref, 0), flag_at(flags_ref, 1)
    sides = [pick(odd_y, side_a_ref[i], side_b_ref[i]) for i in range(2)]
    for place, j in ((0, 0), (1, count_y + 1)):
        row_a_ref[j], row_b_ref[j] = pick(odd_x, sides[0][place], sides[1][place])
    for j in range(count_y):
        row_a_ref[j + 1], row_b_ref[j + 1] = pick(odd_x, low_ref[j], high_ref[j])
    row_a_ref[count_y + 2] = partial_ref[...]


def operators_kernel(
    inverse_rows,
    neighbours_ref,
    kinds_ref,
    flags_ref,
    partial_ref,
    row_a_ref,
    row_b_ref,
    from_row_a_ref,
    from_row_b_ref,
    rest_a_ref,
    rest_b_ref,
    from_rest_a_ref,
    from_rest_b_ref,
    current_ref,
    table_high_ref,
    table_low_ref,
    weighted_low_ref,
    weighted_high_ref,
    coupling_ref,
    sums_ref,
    ext_ref,
    basis_ref,
):
    count_y, block, side = weighted_low_ref.shape
    wide, rest, _ = rest_a_ref.shape
    prior = rest + block
    odd_y, odd_x, in_low_y, in_high_y, in_low_x, in_high_x = (
        flag_at(flags_ref, place) for place in range(6)
    )
    coupling = partial_ref[...] * inverse_rows
    coupling_ref[...] = coupling
    coupling_high, coupling_low = split(coupling)

    for j in range(wide):
        rows = list(pick(odd_x, from_row_a_ref[j], from_row_b_ref[j]))
        rows[1:1] = pick(odd_x, row_a_ref[j], row_b_ref[j])
        rests = list(pick(odd_x, from_rest_a_ref[j], from_rest_b_ref[j]))
        rests[1:1] = pick(odd_x, rest_a_ref[j], rest_b_ref[j])
        for i in range(4):
            tile = jnp.concatenate([rests[i], current_ref[i * wide + j]], axis=0)
            high, low = split(tile)
            value = rows[i] - (
                mul(coupling_high, high) + (mul(coupling_high, low) + mul(coupling_low, high))
            )
            if i == 0:
                value = value * in_low_x
            if i == 3:
                value = value * in_high_x
            if j == 0:
                value = value * in_low_y
            if j == wide - 1:
                value = value * in_high_y
            if 0 < i < 3 and 0 < j < wide - 1:
                (weighted_low_ref, weighted_high_ref)[i - 1][j - 1] = value
                place = (i - 1) * count_y + j - 1
                basis_ref[place, :prior, :] = high
                basis_ref[place, prior:, :] = low
            high, low = split(value)
            ext_ref[i * wide + j, :block, :] = high
            ext_ref[i * wide + j, block:, :] = low
    with_basis = jnp.zeros((2 * block, prior), F32)
    with_own = jnp.zeros((block, 4 * block), F32)
    for tile in range(2 * count_y):
        i, j = tile // count_y, tile % count_y
        own = (weighted_low_ref, weighted_high_ref)[i][j]
        totals = jnp.concatenate([4.0 * own, own], axis=1)
        for k in range(neighbours_ref.shape[0]):
            source = source_of(neighbours_ref, k, tile, count_y)
            kind = kinds_ref[k, tile]
            chosen = ext_ref[source]
            pair = mul(chosen, table_high_ref[kind])
            totals = totals + (
                pair[:block] + (pair[block:] + mul(chosen[:block], table_low_ref[kind]))
            )
        applied = jnp.concatenate([totals[:, :side], totals[:, side:]], axis=0)
        high, low = split(applied)
        basis_high, basis_low = basis_ref[tile, :prior, :], basis_ref[tile, prior:, :]
        with_basis = with_basis + (
            mul_t(high, basis_high) + (mul_t(high, basis_low) + mul_t(low, basis_high))
        )
        right = jnp.concatenate([applied, own, jnp.zeros_like(own)], axis=0)
        with_own = with_own + mul3_t(own, right)
    sums_ref[: 2 * block, :] = with_basis
    sums_ref[2 * block :, :] = with_own


def factor_kernel(
    inverse_rows,
    sums_ref,
    weighted_low_ref,
    weighted_high_ref,
    new_ref,
    factor_ref,
    reduced_ref,
):
    count_y, block, _ = weighted_low_ref.shape
    prior = sums_ref.shape[1]
    tiles = 2 * count_y
    with_own = sums_ref[2 * block :, :] * inverse_rows
    gram = with_own[:, 2 * block : 3 * block]
    row_ids = lax.broadcasted_iota(jnp.int32, (block, block), 0)
    column_ids = lax.broadcasted_iota(jnp.int32, (block, block), 1)
    unit = jnp.where(row_ids == column_ids, 1.0, 0.0).astype(F32)
    work = jnp.concatenate([gram, unit], axis=1)
    rows = lax.broadcasted_iota(jnp.int32, work.shape, 0)
    group = 4
    for j in range(0, block, group):
        columns = [
            jnp.broadcast_to(work[:, j + a : j + a + 1], work.shape) for a in range(group)
        ]
        pivots = [work[j + a : j + a + 1, :] for a in range(group)]
        for a in range(group):
            at = j + a
            ratio = columns[a] * (1.0 / columns[a][at : at + 1, :])
            for b in range(a + 1, group):
                columns[b] = columns[b] - ratio * columns[b][at : at + 1, :]
                pivots[b] = pivots[b] - ratio[j + b : j + b + 1, :] * pivots[a]
            work = work - jnp.where(rows > at, ratio, 0.0) * pivots[a]
    work = work * lax.rsqrt(jnp.sum(work[:, :block] * unit, axis=1, keepdims=True))
    factor_ref[...] = jnp.where(column_ids >= row_ids, work[:, :block], 0.0)
    inverse = work[:, block:]
    for tile in range(tiles):
        own = (weighted_low_ref, weighted_high_ref)[tile // count_y][tile % count_y]
        new_ref[pl.ds(tile, block, stride=tiles), :] = mul3(inverse, own)
    for part in range(2):
        span = slice(part * block, (part + 1) * block)
        reduced_ref[part, :, :prior] = mul3(inverse, sums_ref[span, :] * inverse_rows)
        reduced_ref[part, :, prior:] = mul3_t(mul3_t(inverse, with_own[:, span]), inverse)


def swap(value, axis, step):
    return lax.ppermute(value, axis, [(i, i ^ step) for i in range(lax.axis_size(axis))])


def other_swap(value, axis):
    count = lax.axis_size(axis)
    pairs = [(i, ((i + 1) ^ 1) - 1) for i in range(count)]
    return lax.ppermute(value, axis, [(i, j if 0 <= j < count else i) for i, j in pairs])


def exchange(message_a, message_b, axis):
    return swap(message_a, axis, 1), other_swap(message_b, axis)


def total_along(value, axis, first=1, near=None):
    if lax.axis_size(axis) == 4 and first == 1:
        near = swap(value, axis, 1) if near is None else near
        return (value + swap(value, axis, 2)) + (near + swap(value, axis, 3))
    step = first
    while step < lax.axis_size(axis):
        value = value + swap(value, axis, step)
        step *= 2
    return value


def halved_total(value):
    half = value.shape[0] // 2
    upper = lax.axis_index("py") % 2 == 1
    first, second = value[:half], value[half:]
    kept = jnp.where(upper, second, first)
    kept = kept + swap(jnp.where(upper, first, second), "py", 1)
    kept = total_along(kept, "py", 2)
    kept = total_along(kept, "px")
    other = swap(kept, "py", 1)
    return jnp.concatenate(
        [jnp.where(upper, other, kept), jnp.where(upper, kept, other)], axis=0
    )


def shape(*dims, dtype=F32):
    return jax.ShapeDtypeStruct(dims, dtype)


def shards(prior_basis, previous, neighbours, tile_kinds, stiff_tiles, mass_tiles):
    block = previous.shape[0]
    prior, count_x, count_y, side = prior_basis.shape
    tiles = count_x * count_y
    wide = count_y + 2
    rest = prior - block
    kinds = stiff_tiles.shape[0]
    inverse_rows = 1.0 / (tiles * side * lax.axis_size("px") * lax.axis_size("py"))
    basis = prior_basis.reshape(-1, side)
    previous_rows = previous.reshape(-1, side)
    neighbours = neighbours.reshape(-1, tiles)
    tile_kinds = tile_kinds.reshape(-1, tiles)
    at_y, at_x = lax.axis_index("py"), lax.axis_index("px")
    flags = [at_y % 2 == 1, at_x % 2 == 1]
    flags += [at_y > 0, at_y < lax.axis_size("py") - 1]
    flags += [at_x > 0, at_x < lax.axis_size("px") - 1]
    flags = jnp.stack(flags + flags[:2]).astype(F32)
    flags = jnp.broadcast_to(flags[:, None], (8, side))

    def call(kernel, inputs, outputs, scratch=(), smem=0):
        return pl.pallas_call(
            kernel,
            out_shape=outputs,
            in_specs=[SMEM] * smem + [VMEM] * (len(inputs) - smem),
            out_specs=[VMEM] * len(outputs),
            scratch_shapes=scratch,
            compiler_params=PARAMS,
        )(*inputs)

    side_a, side_b, row_a, row_b = call(
        pack_kernel,
        (flags, basis, previous_rows),
        [shape(count_x, prior + block, side)] * 2 + [shape(count_y, 2 * block, side)] * 2,
    )
    tables = call(
        tables_kernel,
        (stiff_tiles, mass_tiles),
        [shape(kinds, 2 * side, side, dtype=BF16)] * 2
        + [shape(kinds, side, 2 * side, dtype=BF16)] * 2,
    )
    from_side_a, from_side_b = exchange(side_a, side_b, "py")
    from_row_a, from_row_b = exchange(row_a, row_b, "px")
    from_side_a, neighbours, tile_kinds, *tables = lax.optimization_barrier(
        (from_side_a, neighbours, tile_kinds, *tables)
    )
    corner_a, corner_b, rest_a, rest_b = call(
        corners_kernel,
        (flags, basis, from_side_a, from_side_b),
        [shape(2, 2 * block, side)] * 2 + [shape(wide, rest, side)] * 2,
    )
    from_corner_a, from_corner_b = exchange(corner_a, corner_b, "px")
    from_rest_a, from_rest_b = exchange(rest_a, rest_b, "px")
    residual_low, residual_high, message_a, message_b, partial, current = call(
        residual_kernel,
        (
            neighbours,
            tile_kinds,
            flags,
            row_a,
            row_b,
            from_row_a,
            from_row_b,
            from_side_a,
            from_side_b,
            from_corner_a,
            from_corner_b,
            rest_a,
            rest_b,
            *tables[:2],
        ),
        [shape(count_y, block, side)] * 2
        + [shape(3, block, side), shape(2, block, side)]
        + [shape(block, prior), shape(4 * wide, block, side)],
        [pltpu.VMEM((4 * wide, 2 * block, 2 * side), BF16)],
        smem=2,
    )
    from_side_a, from_side_b = exchange(message_a, message_b, "py")
    partial = total_along(partial + from_side_a[-1], "py", 2)
    from_side_a, from_rest_a, from_rest_b = lax.optimization_barrier(
        (from_side_a, from_rest_a, from_rest_b)
    )
    row_a, row_b = call(
        residual_rows_kernel,
        (flags, residual_low, residual_high, from_side_a, from_side_b, partial),
        [shape(wide + 1, block, side), shape(wide, block, side)],
    )
    from_row_a, from_row_b = exchange(row_a, row_b, "px")
    partial = total_along(partial, "px", near=from_row_a[-1])
    weighted_low, weighted_high, coupling, sums = call(
        functools.partial(operators_kernel, inverse_rows),
        (
            neighbours,
            tile_kinds,
            flags,
            partial,
            row_a,
            row_b,
            from_row_a,
            from_row_b,
            rest_a,
            rest_b,
            from_rest_a,
            from_rest_b,
            current,
            *tables[2:],
        ),
        [shape(count_y, block, side)] * 2 + [shape(block, prior), shape(3 * block, prior)],
        [
            pltpu.VMEM((4 * wide, 2 * block, side), BF16),
            pltpu.VMEM((tiles, 2 * prior, side), BF16),
        ],
        smem=2,
    )
    new_block, factor, reduced = call(
        functools.partial(factor_kernel, inverse_rows),
        (halved_total(sums), weighted_low, weighted_high),
        [
            shape(block * tiles, side),
            shape(block, block),
            shape(2, block, prior + block),
        ],
    )
    return (
        new_block.reshape(previous.shape),
        coupling.T,
        factor,
        reduced.swapaxes(1, 2),
    )


def solution(mesh):
    placed = (
        P("case", "px", "py", None),
        P("case", "px", "py", None),
        P(None, "px", "py"),
        P(None, "px", "py"),
        P(),
        P(),
    )
    return jax.shard_map(
        shards,
        mesh=mesh,
        in_specs=placed,
        out_specs=(
            P("case", "px", "py", None),
            P("case", None),
            P("case", None),
            P("case", None, None),
        ),
        check_vma=False,
    )
```

time: 70 us -> 64.2 us (0.917)
  starting transfers between devices: 38.5 us -> 31.2 us
  waiting for transfers between devices: 17.4 us -> 15.2 us
  local copies, waits for them, and re-layouts: 2.72 us -> 4.89 us
  Pallas kernels: 10 us -> 11.5 us
    ppermute x19 -> x21, starting transfers between devices: 38.5 us -> 31.2 us  [the longest x15 23.4 us: swap(): lax.ppermute(value, axis, [(i, i ^ step) for i in range(lax.axis_size(axi...]
    ppermute x19 -> x21, waiting for transfers between devices: 17.4 us -> 15.2 us  [the longest x15 15.2 us: swap(): lax.ppermute(value, axis, [(i, i ^ step) for i in range(lax.axis_size(axi...]
    unnamed x12 -> x18, local copies, waits for them, and re-layouts: 2.55 us -> 4.55 us
    pallas_call x7, Pallas kernels: 10 us -> 11.5 us  [call(): pl.pallas_call(kernel, out_shape=outputs, in_specs=[SMEM] * smem + [VMEM]...]
  transfers between devices with their start and end apart: 19 -> 21, of which waited for: 9 -> 10; matrix products, arithmetic and copies ran while one was open for 0% -> 0% of each run, Pallas kernels for 4% -> 7%
where the time goes in v6:
time: 64.2 us; the launch traced here: 63.7 us
  starting transfers between devices  31.2 us (49%)
  waiting for transfers between devices  15.2 us (24%)
  Pallas kernels  11.5 us (18%)
  local copies, waits for them, and re-layouts  4.89 us (8%)
  between operations  0.8 us (1%)
    ppermute x15, starting transfers between devices, swap(): lax.ppermute(value, axis, [(i, i ^ step) for i in range(lax.axis_size(axi...  23.4 us
    ppermute x15, waiting for transfers between devices, swap(): lax.ppermute(value, axis, [(i, i ^ step) for i in range(lax.axis_size(axi...  15.2 us
    pallas_call x7, Pallas kernels, call(): pl.pallas_call(kernel, out_shape=outputs, in_specs=[SMEM] * smem + [VMEM]...  11.5 us
    ppermute x6, starting transfers between devices, other_swap(): lax.ppermute(value, axis, [(i, j if 0 <= j < count else i) for i, j in pa...  7.85 us
    unnamed x18, local copies, waits for them, and re-layouts  4.55 us
  transfers between devices with their start and end apart: 21, of which 10 were waited for; matrix products, arithmetic and copies ran while one was open for 0% of the time, Pallas kernels for 7%

profile of v6, /device:TPU:0, one launch (start us, length us, event | category | flops | bytes accessed | tf_op | source)
XLA Modules:
  0.0 63.7 jit_solution(11226393541142227688)
XLA Ops:
  0.7 0.1 stack.29
  0.8 0.1 broadcast_in_dim.2.flags_ref
  0.8 1.0 %copy-done = f32[128,2,4,128]{3,2,1,0:T(4,128)S(1)} copy-done((f32[128,2,4,128]{3,2,1,0:T(4,128)S(1)}, f32[128,2,4,128]{3,2,1,0:T(4,128)}, u32[]{:S(2)}) %copy-start) | copy-done | bytes 524312
  1.9 0.9 %copy-done.4 = f32[32,2,4,128]{3,2,1,0:T(4,128)S(1)} copy-done((f32[32,2,4,128]{3,2,1,0:T(4,128)S(1)}, f32[32,2,4,128]{3,2,1,0:T(4,128)}, u32[]{:S(2)}) %copy-start.4) | copy-done | bytes 131096
  2.8 0.7 %shard_map.93 = (f32[2,160,128]{2,1,0:T(8,128)S(1)}, f32[2,160,128]{2,1,0:T(8,128)S(1)}, f32[4,64,128]{2,1,0:T(8,128)S(1)}, f32[4,64,128]{2,1,0:T(8,128)}) custom-call(f32[8,128]{1,0:T(8,128)S(1)} %broadcast_in_dim.2.flags_ref, f32[1024,128]{1,0:T(8,128)S(1)} %bitcast.23, f32[256,128]{1,0:T(8,128)S(1)} %bitcast.25), custom_call_target="tpu_custom_call" | custom-call | tf_op jit(solution)/shard_map/pallas_call | solution.py:415
  3.5 0.5 collective-permute-start
  4.0 0.7 %collective-permute-start.3 = (f32[2,160,128]{2,1,0:T(8,128)S(1)}, f32[2,160,128]{2,1,0:T(8,128)S(1)}, u32[]{:S(2)}, u32[]{:S(2)}) collective-permute-start(f32[2,160,128]{2,1,0:T(8,128)S(1)} %get-tuple-element.51), channel_id=1, source_target_pairs={{0,0},{1,2},{2,1},{3,3},{4,4},{5,6},{6,5},{7,7},{8,8},{9,10},{10,9... | collective-permute-start | bytes 491528 | tf_op jit(solution)/shard_map/ppermute | solution.py:359
  4.7 2.6 %collective-permute-start.1 = (f32[4,64,128]{2,1,0:T(8,128)S(1)}, f32[4,64,128]{2,1,0:T(8,128)S(1)}, u32[]{:S(2)}, u32[]{:S(2)}) collective-permute-start(f32[4,64,128]{2,1,0:T(8,128)S(1)} %get-tuple-element.48.row_a_ref), channel_id=1, source_target_pairs={{0,4},{4,0},{8,12},{12,8},{1,5},{5,1},{9,13},{13,9},{2,6},{6,2},{1... | collective-permute-start | bytes 393224 | tf_op jit(solution)/shard_map/ppermute | solution.py:353
  7.3 2.3 %collective-permute-start.2 = (f32[4,64,128]{2,1,0:T(8,128)}, f32[4,64,128]{2,1,0:T(8,128)}, u32[]{:S(2)}, u32[]{:S(2)}) collective-permute-start(f32[4,64,128]{2,1,0:T(8,128)} %get-tuple-element.49.row_b_ref), channel_id=1, source_target_pairs={{0,0},{4,8},{8,4},{12,12},{1,1},{5,9},{9,5},{13,13},{2,2},{6,10},{... | collective-permute-start | bytes 393224 | tf_op jit(solution)/shard_map/ppermute | solution.py:359
  9.6 1.0 %copy-done.3 = f32[8,128,128]{2,1,0:T(8,128)S(1)} copy-done((f32[8,128,128]{2,1,0:T(8,128)S(1)}, f32[8,128,128]{2,1,0:T(8,128)}, u32[]{:S(2)}) %copy-start.3) | copy-done | bytes 524312
  10.6 0.2 shard_map.94
  10.8 0.0 collective-permute-done.side_a_ref.from_side_a_ref
  10.9 0.0 collective-permute-done.3.side_b_ref.from_side_b_ref
  10.9 0.7 %shard_map.95 = (f32[2,64,128]{2,1,0:T(8,128)}, f32[2,64,128]{2,1,0:T(8,128)}, f32[6,96,128]{2,1,0:T(8,128)S(1)}, f32[6,96,128]{2,1,0:T(8,128)S(1)}) custom-call(f32[8,128]{1,0:T(8,128)S(1)} %broadcast_in_dim.2.flags_ref, f32[1024,128]{1,0:T(8,128)S(1)} %bitcast.24, f32[2,160,128]{2,1,0:T(8,128)S(1)} %collective-permute-done.side_a_ref.from_side_a_ref, ...), custom_call_target="tpu_custom_call" | custom-call | tf_op jit(solution)/shard_map/pallas_call | solution.py:415
  11.6 2.9 %collective-permute-start.4 = (f32[2,64,128]{2,1,0:T(8,128)}, f32[2,64,128]{2,1,0:T(8,128)S(1)}, u32[]{:S(2)}, u32[]{:S(2)}) collective-permute-start(f32[2,64,128]{2,1,0:T(8,128)} %get-tuple-element.52), channel_id=1, source_target_pairs={{0,4},{4,0},{8,12},{12,8},{1,5},{5,1},{9,13},{13,9},{2,6},{6,2},{1... | collective-permute-start | bytes 196616 | tf_op jit(solution)/shard_map/ppermute | solution.py:353
  14.5 2.1 %collective-permute-start.5 = (f32[2,64,128]{2,1,0:T(8,128)}, f32[2,64,128]{2,1,0:T(8,128)}, u32[]{:S(2)}, u32[]{:S(2)}) collective-permute-start(f32[2,64,128]{2,1,0:T(8,128)} %get-tuple-element.53), channel_id=1, source_target_pairs={{0,0},{4,8},{8,4},{12,12},{1,1},{5,9},{9,5},{13,13},{2,2},{6,10},{... | collective-permute-start | bytes 196616 | tf_op jit(solution)/shard_map/ppermute | solution.py:359
  16.6 0.6 collective-permute-start.9
  17.2 0.0 collective-permute-done.1.from_row_a_ref
  17.2 0.6 %copy-done.5 = f32[4,64,128]{2,1,0:T(8,128)} copy-done((f32[4,64,128]{2,1,0:T(8,128)}, f32[4,64,128]{2,1,0:T(8,128)S(1)}, u32[]{:S(2)}) %copy-start.5) | copy-done | bytes 131096
  17.8 1.5 %collective-permute-start.10 = (f32[6,96,128]{2,1,0:T(8,128)S(1)}, f32[6,96,128]{2,1,0:T(8,128)}, u32[]{:S(2)}, u32[]{:S(2)}) collective-permute-start(f32[6,96,128]{2,1,0:T(8,128)S(1)} %get-tuple-element.55.rest_b_ref), channel_id=1, source_target_pairs={{0,0},{4,8},{8,4},{12,12},{1,1},{5,9},{9,5},{13,13},{2,2},{6,10},{... | collective-permute-start | bytes 884744 | tf_op jit(solution)/shard_map/ppermute | solution.py:359
  19.3 0.1 copy.12.neighbours_ref
  19.4 0.1 copy.13.kinds_ref
  19.5 0.0 collective-permute-done.2.from_row_b_ref
  19.5 0.0 collective-permute-done.4.from_corner_a_ref
  19.5 0.9 %copy-done.6 = f32[4,64,128]{2,1,0:T(8,128)S(1)} copy-done((f32[4,64,128]{2,1,0:T(8,128)S(1)}, f32[4,64,128]{2,1,0:T(8,128)}, u32[]{:S(2)}) %copy-start.6) | copy-done | bytes 131096
  20.4 3.3 %shard_map.96 = (f32[4,32,128]{2,1,0:T(8,128)S(1)}, f32[4,32,128]{2,1,0:T(8,128)S(1)}, f32[3,32,128]{2,1,0:T(8,128)S(1)}, f32[2,32,128]{2,1,0:T(8,128)S(1)}, f32...) custom-call(s32[5,8]{1,0:T(8,128)S(1)} %copy.12.neighbours_ref, s32[5,8]{1,0:T(8,128)S(1)} %copy.13.kinds_ref, ...), custom_call_target="tpu_custom_call" | custom-call | tf_op jit(solution)/shard_map/pallas_call | solution.py:415
  23.7 1.8 %collective-permute-start.6 = (f32[3,32,128]{2,1,0:T(8,128)S(1)}, f32[3,32,128]{2,1,0:T(8,128)S(1)}, u32[]{:S(2)}, u32[]{:S(2)}) collective-permute-start(f32[3,32,128]{2,1,0:T(8,128)S(1)} %get-tuple-element.59), channel_id=1, source_target_pairs={{0,1},{1,0},{2,3},{3,2},{4,5},{5,4},{6,7},{7,6},{8,9},{9,8},{10,11... | collective-permute-start | bytes 147464 | tf_op jit(solution)/shard_map/ppermute | solution.py:353
  25.5 0.7 %collective-permute-start.11 = (f32[2,32,128]{2,1,0:T(8,128)S(1)}, f32[2,32,128]{2,1,0:T(8,128)S(1)}, u32[]{:S(2)}, u32[]{:S(2)}) collective-permute-start(f32[2,32,128]{2,1,0:T(8,128)S(1)} %get-tuple-element.63), channel_id=1, source_target_pairs={{0,0},{1,2},{2,1},{3,3},{4,4},{5,6},{6,5},{7,7},{8,8},{9,10},{10,9... | collective-permute-start | bytes 98312 | tf_op jit(solution)/shard_map/ppermute | solution.py:359
  26.1 0.2 collective-permute-done.6.side_a_ref
  26.4 2.8 %collective-permute-start.7 = (f32[32,128]{1,0:T(8,128)S(1)}, f32[32,128]{1,0:T(8,128)S(1)}, u32[]{:S(2)}, u32[]{:S(2)}) collective-permute-start(f32[32,128]{1,0:T(8,128)S(1)} %fusion.2), channel_id=1, source_target_pairs={{0,2},{1,3},{2,0},{3,1},{4,6},{5,7},{6,4},{7,5},{8,10},{9,11},{10,... | collective-permute-start | bytes 49160 | tf_op jit(solution)/shard_map/ppermute | solution.py:353
  29.1 2.0 %collective-permute-done.7 = f32[32,128]{1,0:T(8,128)S(1)} collective-permute-done((f32[32,128]{1,0:T(8,128)S(1)}, f32[32,128]{1,0:T(8,128)S(1)}, u32[]{:S(2)}, u32[]{:S(2)}) %collective-permute-start.7) | collective-permute-done | bytes 16416 | tf_op jit(solution)/shard_map/ppermute | solution.py:353
  31.1 2.1 %collective-permute-start.12 = (f32[7,32,128]{2,1,0:T(8,128)S(1)}, f32[7,32,128]{2,1,0:T(8,128)S(1)}, u32[]{:S(2)}, u32[]{:S(2)}) collective-permute-start(f32[7,32,128]{2,1,0:T(8,128)S(1)} %get-tuple-element.64.row_a_ref), channel_id=1, source_target_pairs={{0,4},{4,0},{8,12},{12,8},{1,5},{5,1},{9,13},{13,9},{2,6},{6,2},{1... | collective-permute-start | bytes 344072 | tf_op jit(solution)/shard_map/ppermute | solution.py:353
  33.2 2.9 %collective-permute-start.13 = (f32[32,128]{1,0:T(8,128)S(1)}, f32[32,128]{1,0:T(8,128)S(1)}, u32[]{:S(2)}, u32[]{:S(2)}) collective-permute-start(f32[32,128]{1,0:T(8,128)S(1)} %add.41.partial_ref), channel_id=1, source_target_pairs={{0,12},{4,8},{8,4},{12,0},{1,13},{5,9},{9,5},{13,1},{2,14},{6,10},... | collective-permute-start | bytes 49160 | tf_op jit(solution)/shard_map/ppermute | solution.py:353
  36.2 0.7 %collective-permute-start.14 = (f32[6,32,128]{2,1,0:T(8,128)S(1)}, f32[6,32,128]{2,1,0:T(8,128)S(1)}, u32[]{:S(2)}, u32[]{:S(2)}) collective-permute-start(f32[6,32,128]{2,1,0:T(8,128)S(1)} %get-tuple-element.65.row_b_ref), channel_id=1, source_target_pairs={{0,0},{4,8},{8,4},{12,12},{1,1},{5,9},{9,5},{13,13},{2,2},{6,10},{... | collective-permute-start | bytes 294920 | tf_op jit(solution)/shard_map/ppermute | solution.py:359
  36.8 3.6 %collective-permute-done.13 = f32[32,128]{1,0:T(8,128)S(1)} collective-permute-done((f32[32,128]{1,0:T(8,128)S(1)}, f32[32,128]{1,0:T(8,128)S(1)}, u32[]{:S(2)}, u32[]{:S(2)}) %collective-permute-start.13) | collective-permute-done | bytes 16416 | tf_op jit(solution)/shard_map/ppermute | solution.py:353
  40.5 0.4 collective-permute-done.8
  40.8 3.9 %shard_map.98 = (f32[4,32,128]{2,1,0:T(8,128)S(1)}, f32[4,32,128]{2,1,0:T(8,128)S(1)}, f32[32,128]{1,0:T(8,128)}, f32[96,128]{1,0:T(8,128)S(1)}) custom-call(s32[5,8]{1,0:T(8,128)S(1)} %copy.12.neighbours_ref, s32[5,8]{1,0:T(8,128)S(1)} %copy.13.kinds_ref, f32[8,128]{1,0:T(8,128)S(1)} %broadcast_in_dim.2.flags_ref, f32[32,128]{1,0:T(8,128)S(1)} %fusion.1.partial_ref, ...), custom_call_target="tpu_custom_call" | custom-call | tf_op jit(solution)/shard_map/pallas_call | solution.py:415
  44.7 1.2 %collective-permute-done.15 = f32[48,128]{1,0:T(8,128)S(1)} collective-permute-done((f32[48,128]{1,0:T(8,128)S(1)}, f32[48,128]{1,0:T(8,128)S(1)}, u32[]{:S(2)}, u32[]{:S(2)}) %collective-permute-start.15) | collective-permute-done | bytes 24608 | tf_op jit(solution)/shard_map/ppermute | solution.py:353
  45.9 1.9 %collective-permute-start.16 = (f32[48,128]{1,0:T(8,128)S(1)}, f32[48,128]{1,0:T(8,128)S(1)}, u32[]{:S(2)}, u32[]{:S(2)}) collective-permute-start(f32[48,128]{1,0:T(8,128)S(1)} %select_add_fusion), channel_id=1, source_target_pairs={{0,2},{1,3},{2,0},{3,1},{4,6},{5,7},{6,4},{7,5},{8,10},{9,11},{10,... | collective-permute-start | bytes 73736 | tf_op jit(solution)/shard_map/ppermute | solution.py:353
  47.9 1.9 %collective-permute-done.16 = f32[48,128]{1,0:T(8,128)S(1)} collective-permute-done((f32[48,128]{1,0:T(8,128)S(1)}, f32[48,128]{1,0:T(8,128)S(1)}, u32[]{:S(2)}, u32[]{:S(2)}) %collective-permute-start.16) | collective-permute-done | bytes 24608 | tf_op jit(solution)/shard_map/ppermute | solution.py:353
  49.8 1.2 %collective-permute-start.19 = (f32[48,128]{1,0:T(8,128)S(1)}, f32[48,128]{1,0:T(8,128)S(1)}, u32[]{:S(2)}, u32[]{:S(2)}) collective-permute-start(f32[48,128]{1,0:T(8,128)S(1)} %add.46), channel_id=1, source_target_pairs={{0,12},{4,8},{8,4},{12,0},{1,13},{5,9},{9,5},{13,1},{2,14},{6,10},... | collective-permute-start | bytes 73736 | tf_op jit(solution)/shard_map/ppermute | solution.py:353
  51.0 4.1 %collective-permute-start.18 = (f32[48,128]{1,0:T(8,128)S(1)}, f32[48,128]{1,0:T(8,128)S(1)}, u32[]{:S(2)}, u32[]{:S(2)}) collective-permute-start(f32[48,128]{1,0:T(8,128)S(1)} %add.46), channel_id=1, source_target_pairs={{0,4},{4,0},{8,12},{12,8},{1,5},{5,1},{9,13},{13,9},{2,6},{6,2},{1... | collective-permute-start | bytes 73736 | tf_op jit(solution)/shard_map/ppermute | solution.py:353
  55.1 0.3 collective-permute-done.19
  55.4 1.5 %collective-permute-done.18 = f32[48,128]{1,0:T(8,128)S(1)} collective-permute-done((f32[48,128]{1,0:T(8,128)S(1)}, f32[48,128]{1,0:T(8,128)S(1)}, u32[]{:S(2)}, u32[]{:S(2)}) %collective-permute-start.18) | collective-permute-done | bytes 24608 | tf_op jit(solution)/shard_map/ppermute | solution.py:353
  56.9 2.9 %collective-permute-done.17 = f32[48,128]{1,0:T(8,128)S(1)} collective-permute-done((f32[48,128]{1,0:T(8,128)S(1)}, f32[48,128]{1,0:T(8,128)S(1)}, u32[]{:S(2)}, u32[]{:S(2)}) %collective-permute-start.17) | collective-permute-done | bytes 24608 | tf_op jit(solution)/shard_map/ppermute | solution.py:353
  59.8 0.1 collective-permute-start.20
  59.9 1.2 %collective-permute-done.20 = f32[48,128]{1,0:T(8,128)S(1)} collective-permute-done((f32[48,128]{1,0:T(8,128)S(1)}, f32[48,128]{1,0:T(8,128)S(1)}, u32[]{:S(2)}, u32[]{:S(2)}) %collective-permute-start.20) | collective-permute-done | bytes 24608 | tf_op jit(solution)/shard_map/ppermute | solution.py:353
  61.1 2.6 %shard_map.99 = (f32[256,128]{1,0:T(8,128)}, f32[32,32]{1,0:T(8,128)}, f32[2,32,160]{2,1,0:T(8,128)}) custom-call(f32[96,128]{1,0:T(8,128)S(1)} %pad_maximum_fusion.sums_ref, f32[4,32,128]{2,1,0:T(8,128)S(1)} %get-tuple-element.72.weighted_low_ref, f32[4,32,128]{2,1,0:T(8,128)S(1)} %get-tuple-element.73.weighted_high_ref), custom_call_target="tpu_custom_call" | custom-call | tf_op jit(solution)/shard_map/pallas_call | solution.py:415
  (33 shorter events, 0.1 us)
Async XLA Ops:
  0.8 1.0 %copy-start = (f32[128,2,4,128]{3,2,1,0:T(4,128)S(1)}, f32[128,2,4,128]{3,2,1,0:T(4,128)}, u32[]{:S(2)}) copy-start(f32[128,2,4,128]{3,2,1,0:T(4,128)} %param.6) | copy-start | bytes 1572868
  1.9 0.9 %copy-start.4 = (f32[32,2,4,128]{3,2,1,0:T(4,128)S(1)}, f32[32,2,4,128]{3,2,1,0:T(4,128)}, u32[]{:S(2)}) copy-start(f32[32,2,4,128]{3,2,1,0:T(4,128)} %param.7) | copy-start | bytes 393220
  2.8 6.8 %copy-start.2 = (f32[8,128,128]{2,1,0:T(8,128)S(1)}, f32[8,128,128]{2,1,0:T(8,128)}, u32[]{:S(2)}) copy-start(f32[8,128,128]{2,1,0:T(8,128)} %stiff_ref.1) | copy-start | bytes 1572868
  3.5 7.3 %collective-permute-start = (f32[2,160,128]{2,1,0:T(8,128)S(1)}, f32[2,160,128]{2,1,0:T(8,128)S(1)}, u32[]{:S(2)}, u32[]{:S(2)}) collective-permute-start(f32[2,160,128]{2,1,0:T(8,128)S(1)} %get-tuple-element.41), channel_id=1, source_target_pairs={{0,1},{1,0},{2,3},{3,2},{4,5},{5,4},{6,7},{7,6},{8,9},{9,8},{10,11... | collective-permute-start | bytes 491528 | tf_op jit(solution)/shard_map/ppermute | solution.py:353
  4.0 6.9 %collective-permute-start.3 = (f32[2,160,128]{2,1,0:T(8,128)S(1)}, f32[2,160,128]{2,1,0:T(8,128)S(1)}, u32[]{:S(2)}, u32[]{:S(2)}) collective-permute-start(f32[2,160,128]{2,1,0:T(8,128)S(1)} %get-tuple-element.51), channel_id=1, source_target_pairs={{0,0},{1,2},{2,1},{3,3},{4,4},{5,6},{6,5},{7,7},{8,8},{9,10},{10,9... | collective-permute-start | bytes 491528 | tf_op jit(solution)/shard_map/ppermute | solution.py:359
  4.7 12.5 %collective-permute-start.1 = (f32[4,64,128]{2,1,0:T(8,128)S(1)}, f32[4,64,128]{2,1,0:T(8,128)S(1)}, u32[]{:S(2)}, u32[]{:S(2)}) collective-permute-start(f32[4,64,128]{2,1,0:T(8,128)S(1)} %get-tuple-element.48.row_a_ref), channel_id=1, source_target_pairs={{0,4},{4,0},{8,12},{12,8},{1,5},{5,1},{9,13},{13,9},{2,6},{6,2},{1... | collective-permute-start | bytes 393224 | tf_op jit(solution)/shard_map/ppermute | solution.py:353
  7.3 3.6 %copy-start.1 = (f32[128,2,4,128]{3,2,1,0:T(4,128)S(1)}, f32[128,2,4,128]{3,2,1,0:T(4,128)}, u32[]{:S(2)}) copy-start(f32[128,2,4,128]{3,2,1,0:T(4,128)} %param.6) | copy-start | bytes 1572868
  7.3 12.2 %collective-permute-start.2 = (f32[4,64,128]{2,1,0:T(8,128)}, f32[4,64,128]{2,1,0:T(8,128)}, u32[]{:S(2)}, u32[]{:S(2)}) collective-permute-start(f32[4,64,128]{2,1,0:T(8,128)} %get-tuple-element.49.row_b_ref), channel_id=1, source_target_pairs={{0,0},{4,8},{8,4},{12,12},{1,1},{5,9},{9,5},{13,13},{2,2},{6,10},{... | collective-permute-start | bytes 393224 | tf_op jit(solution)/shard_map/ppermute | solution.py:359
  9.6 1.0 %copy-start.3 = (f32[8,128,128]{2,1,0:T(8,128)S(1)}, f32[8,128,128]{2,1,0:T(8,128)}, u32[]{:S(2)}) copy-start(f32[8,128,128]{2,1,0:T(8,128)} %mass_ref.1) | copy-start | bytes 1572868
  11.6 7.7 %copy-start.7 = (s32[5,2,4]{0,2,1:T(4,128)S(1)}, s32[5,2,4]{0,2,1:T(4,128)}, u32[]{:S(2)}) copy-start(s32[5,2,4]{0,2,1:T(4,128)} %param.8) | copy-start | bytes 484
  11.6 7.9 %collective-permute-start.4 = (f32[2,64,128]{2,1,0:T(8,128)}, f32[2,64,128]{2,1,0:T(8,128)S(1)}, u32[]{:S(2)}, u32[]{:S(2)}) collective-permute-start(f32[2,64,128]{2,1,0:T(8,128)} %get-tuple-element.52), channel_id=1, source_target_pairs={{0,4},{4,0},{8,12},{12,8},{1,5},{5,1},{9,13},{13,9},{2,6},{6,2},{1... | collective-permute-start | bytes 196616 | tf_op jit(solution)/shard_map/ppermute | solution.py:353
  14.5 5.0 %collective-permute-start.5 = (f32[2,64,128]{2,1,0:T(8,128)}, f32[2,64,128]{2,1,0:T(8,128)}, u32[]{:S(2)}, u32[]{:S(2)}) collective-permute-start(f32[2,64,128]{2,1,0:T(8,128)} %get-tuple-element.53), channel_id=1, source_target_pairs={{0,0},{4,8},{8,4},{12,12},{1,1},{5,9},{9,5},{13,13},{2,2},{6,10},{... | collective-permute-start | bytes 196616 | tf_op jit(solution)/shard_map/ppermute | solution.py:359
  16.6 14.5 %collective-permute-start.9 = (f32[6,96,128]{2,1,0:T(8,128)S(1)}, f32[6,96,128]{2,1,0:T(8,128)S(1)}, u32[]{:S(2)}, u32[]{:S(2)}) collective-permute-start(f32[6,96,128]{2,1,0:T(8,128)S(1)} %get-tuple-element.54.rest_a_ref), channel_id=1, source_target_pairs={{0,4},{4,0},{8,12},{12,8},{1,5},{5,1},{9,13},{13,9},{2,6},{6,2},{1... | collective-permute-start | bytes 884744 | tf_op jit(solution)/shard_map/ppermute | solution.py:353
  17.2 0.6 %copy-start.5 = (f32[4,64,128]{2,1,0:T(8,128)}, f32[4,64,128]{2,1,0:T(8,128)S(1)}, u32[]{:S(2)}) copy-start(f32[4,64,128]{2,1,0:T(8,128)S(1)} %collective-permute-done.1.from_row_a_ref) | copy-start | bytes 393220
  17.8 1.6 %copy-start.8 = (s32[5,2,4]{0,2,1:T(4,128)S(1)}, s32[5,2,4]{0,2,1:T(4,128)}, u32[]{:S(2)}) copy-start(s32[5,2,4]{0,2,1:T(4,128)} %param.9) | copy-start | bytes 484
  17.8 13.3 %collective-permute-start.10 = (f32[6,96,128]{2,1,0:T(8,128)S(1)}, f32[6,96,128]{2,1,0:T(8,128)}, u32[]{:S(2)}, u32[]{:S(2)}) collective-permute-start(f32[6,96,128]{2,1,0:T(8,128)S(1)} %get-tuple-element.55.rest_b_ref), channel_id=1, source_target_pairs={{0,0},{4,8},{8,4},{12,12},{1,1},{5,9},{9,5},{13,13},{2,2},{6,10},{... | collective-permute-start | bytes 884744 | tf_op jit(solution)/shard_map/ppermute | solution.py:359
  19.5 0.9 %copy-start.6 = (f32[4,64,128]{2,1,0:T(8,128)S(1)}, f32[4,64,128]{2,1,0:T(8,128)}, u32[]{:S(2)}) copy-start(f32[4,64,128]{2,1,0:T(8,128)} %copy-done.5) | copy-start | bytes 393220
  23.7 2.6 %collective-permute-start.6 = (f32[3,32,128]{2,1,0:T(8,128)S(1)}, f32[3,32,128]{2,1,0:T(8,128)S(1)}, u32[]{:S(2)}, u32[]{:S(2)}) collective-permute-start(f32[3,32,128]{2,1,0:T(8,128)S(1)} %get-tuple-element.59), channel_id=1, source_target_pairs={{0,1},{1,0},{2,3},{3,2},{4,5},{5,4},{6,7},{7,6},{8,9},{9,8},{10,11... | collective-permute-start | bytes 147464 | tf_op jit(solution)/shard_map/ppermute | solution.py:353
  25.5 5.6 %collective-permute-start.11 = (f32[2,32,128]{2,1,0:T(8,128)S(1)}, f32[2,32,128]{2,1,0:T(8,128)S(1)}, u32[]{:S(2)}, u32[]{:S(2)}) collective-permute-start(f32[2,32,128]{2,1,0:T(8,128)S(1)} %get-tuple-element.63), channel_id=1, source_target_pairs={{0,0},{1,2},{2,1},{3,3},{4,4},{5,6},{6,5},{7,7},{8,8},{9,10},{10,9... | collective-permute-start | bytes 98312 | tf_op jit(solution)/shard_map/ppermute | solution.py:359
  26.4 4.7 %collective-permute-start.7 = (f32[32,128]{1,0:T(8,128)S(1)}, f32[32,128]{1,0:T(8,128)S(1)}, u32[]{:S(2)}, u32[]{:S(2)}) collective-permute-start(f32[32,128]{1,0:T(8,128)S(1)} %fusion.2), channel_id=1, source_target_pairs={{0,2},{1,3},{2,0},{3,1},{4,6},{5,7},{6,4},{7,5},{8,10},{9,11},{10,... | collective-permute-start | bytes 49160 | tf_op jit(solution)/shard_map/ppermute | solution.py:353
  31.1 9.7 %collective-permute-start.12 = (f32[7,32,128]{2,1,0:T(8,128)S(1)}, f32[7,32,128]{2,1,0:T(8,128)S(1)}, u32[]{:S(2)}, u32[]{:S(2)}) collective-permute-start(f32[7,32,128]{2,1,0:T(8,128)S(1)} %get-tuple-element.64.row_a_ref), channel_id=1, source_target_pairs={{0,4},{4,0},{8,12},{12,8},{1,5},{5,1},{9,13},{13,9},{2,6},{6,2},{1... | collective-permute-start | bytes 344072 | tf_op jit(solution)/shard_map/ppermute | solution.py:353
  33.2 7.2 %collective-permute-start.13 = (f32[32,128]{1,0:T(8,128)S(1)}, f32[32,128]{1,0:T(8,128)S(1)}, u32[]{:S(2)}, u32[]{:S(2)}) collective-permute-start(f32[32,128]{1,0:T(8,128)S(1)} %add.41.partial_ref), channel_id=1, source_target_pairs={{0,12},{4,8},{8,4},{12,0},{1,13},{5,9},{9,5},{13,1},{2,14},{6,10},... | collective-permute-start | bytes 49160 | tf_op jit(solution)/shard_map/ppermute | solution.py:353
  36.2 4.7 %collective-permute-start.8 = (f32[32,128]{1,0:T(8,128)S(1)}, f32[32,128]{1,0:T(8,128)S(1)}, u32[]{:S(2)}, u32[]{:S(2)}) collective-permute-start(f32[32,128]{1,0:T(8,128)S(1)} %add.41.partial_ref), channel_id=1, source_target_pairs={{0,8},{4,12},{8,0},{12,4},{1,9},{5,13},{9,1},{13,5},{2,10},{6,14},... | collective-permute-start | bytes 49160 | tf_op jit(solution)/shard_map/ppermute | solution.py:353
  36.2 4.7 %collective-permute-start.14 = (f32[6,32,128]{2,1,0:T(8,128)S(1)}, f32[6,32,128]{2,1,0:T(8,128)S(1)}, u32[]{:S(2)}, u32[]{:S(2)}) collective-permute-start(f32[6,32,128]{2,1,0:T(8,128)S(1)} %get-tuple-element.65.row_b_ref), channel_id=1, source_target_pairs={{0,0},{4,8},{8,4},{12,12},{1,1},{5,9},{9,5},{13,13},{2,2},{6,10},{... | collective-permute-start | bytes 294920 | tf_op jit(solution)/shard_map/ppermute | solution.py:359
  44.7 1.2 %collective-permute-start.15 = (f32[48,128]{1,0:T(8,128)S(1)}, f32[48,128]{1,0:T(8,128)S(1)}, u32[]{:S(2)}, u32[]{:S(2)}) collective-permute-start(f32[48,128]{1,0:T(8,128)S(1)} %slice_select_fusion), channel_id=1, source_target_pairs={{0,1},{1,0},{2,3},{3,2},{4,5},{5,4},{6,7},{7,6},{8,9},{9,8},{10,11... | collective-permute-start | bytes 73736 | tf_op jit(solution)/shard_map/ppermute | solution.py:353
  45.9 3.8 %collective-permute-start.16 = (f32[48,128]{1,0:T(8,128)S(1)}, f32[48,128]{1,0:T(8,128)S(1)}, u32[]{:S(2)}, u32[]{:S(2)}) collective-permute-start(f32[48,128]{1,0:T(8,128)S(1)} %select_add_fusion), channel_id=1, source_target_pairs={{0,2},{1,3},{2,0},{3,1},{4,6},{5,7},{6,4},{7,5},{8,10},{9,11},{10,... | collective-permute-start | bytes 73736 | tf_op jit(solution)/shard_map/ppermute | solution.py:353
  49.8 5.6 %collective-permute-start.19 = (f32[48,128]{1,0:T(8,128)S(1)}, f32[48,128]{1,0:T(8,128)S(1)}, u32[]{:S(2)}, u32[]{:S(2)}) collective-permute-start(f32[48,128]{1,0:T(8,128)S(1)} %add.46), channel_id=1, source_target_pairs={{0,12},{4,8},{8,4},{12,0},{1,13},{5,9},{9,5},{13,1},{2,14},{6,10},... | collective-permute-start | bytes 73736 | tf_op jit(solution)/shard_map/ppermute | solution.py:353
  51.0 5.9 %collective-permute-start.18 = (f32[48,128]{1,0:T(8,128)S(1)}, f32[48,128]{1,0:T(8,128)S(1)}, u32[]{:S(2)}, u32[]{:S(2)}) collective-permute-start(f32[48,128]{1,0:T(8,128)S(1)} %add.46), channel_id=1, source_target_pairs={{0,4},{4,0},{8,12},{12,8},{1,5},{5,1},{9,13},{13,9},{2,6},{6,2},{1... | collective-permute-start | bytes 73736 | tf_op jit(solution)/shard_map/ppermute | solution.py:353
  55.1 4.7 %collective-permute-start.17 = (f32[48,128]{1,0:T(8,128)S(1)}, f32[48,128]{1,0:T(8,128)S(1)}, u32[]{:S(2)}, u32[]{:S(2)}) collective-permute-start(f32[48,128]{1,0:T(8,128)S(1)} %add.46), channel_id=1, source_target_pairs={{0,8},{4,12},{8,0},{12,4},{1,9},{5,13},{9,1},{13,5},{2,10},{6,14},... | collective-permute-start | bytes 73736 | tf_op jit(solution)/shard_map/ppermute | solution.py:353
  59.8 1.3 %collective-permute-start.20 = (f32[48,128]{1,0:T(8,128)S(1)}, f32[48,128]{1,0:T(8,128)S(1)}, u32[]{:S(2)}, u32[]{:S(2)}) collective-permute-start(f32[48,128]{1,0:T(8,128)S(1)} %add_add_fusion), channel_id=1, source_target_pairs={{0,1},{1,0},{2,3},{3,2},{4,5},{5,4},{6,7},{7,6},{8,9},{9,8},{10,11... | collective-permute-start | bytes 73736 | tf_op jit(solution)/shard_map/ppermute | solution.py:353

commit v7 on v6

--- a/solution.py
+++ b/solution.py
@@ -11,7 +11,7 @@
 BF16 = jnp.bfloat16
 VMEM = pl.BlockSpec(memory_space=pltpu.VMEM)
 SMEM = pl.BlockSpec(memory_space=pltpu.SMEM)
-PARAMS = pltpu.CompilerParams(vmem_limit_bytes=24 * 1024 * 1024)
+MIB = 1024 * 1024
 
 
 def split(value):
@@ -41,16 +41,13 @@
     )
 
 
-def tables_kernel(stiff_ref, mass_ref, deep_high_ref, deep_low_ref, wide_high_ref, wide_low_ref):
+def split_tables(stiff_ref, mass_ref, high_ref, low_ref, axis):
     side = stiff_ref.shape[1]
     for kind in range(stiff_ref.shape[0]):
         for place, ref in enumerate((stiff_ref, mass_ref)):
-            high, low = split(ref[kind])
-            span = slice(place * side, (place + 1) * side)
-            deep_high_ref[kind, span, :] = high
-            deep_low_ref[kind, span, :] = low
-            wide_high_ref[kind, :, span] = high
-            wide_low_ref[kind, :, span] = low
+            span = [kind, slice(None), slice(None)]
+            span[axis] = slice(place * side, (place + 1) * side)
+            high_ref[tuple(span)], low_ref[tuple(span)] = split(ref[kind])
 
 
 def pick(flag, first, second):
@@ -62,38 +59,27 @@
     return flags_ref[place : place + 1, :]
 
 
-def pack_kernel(flags_ref, basis_ref, previous_ref, side_a_ref, side_b_ref, row_a_ref, row_b_ref):
-    count_x, sides, side = side_a_ref.shape
+def pack_kernel(flags_ref, vectors_ref, side_a_ref, side_b_ref, row_a_ref, row_b_ref):
+    count_x, sides, _ = side_a_ref.shape
     count_y, both, _ = row_a_ref.shape
     tiles = count_x * count_y
-    block = both // 2
-    rest = sides - both
-
-    def tile_of(i, j):
-        tile = i * count_y + j
-        return (
-            basis_ref[pl.ds(tile, rest, stride=tiles), :],
-            basis_ref[pl.ds(rest * tiles + tile, block, stride=tiles), :],
-            previous_ref[pl.ds(tile, block, stride=tiles), :],
+    odd_y, odd_x = flag_at(flags_ref, 0), flag_at(flags_ref, 1)
+
+    def tile_of(i, j, count):
+        first = (sides - count) * tiles + i * count_y + j
+        return vectors_ref[pl.ds(first, count, stride=tiles), :]
+
+    for i in range(count_x):
+        side_a_ref[i], side_b_ref[i] = pick(
+            odd_y, tile_of(i, 0, sides), tile_of(i, count_y - 1, sides)
         )
-
-    spans = (slice(0, rest), slice(rest, rest + block), slice(rest + block, sides))
-    for i in range(count_x):
-        for span, low, high in zip(spans, tile_of(i, 0), tile_of(i, count_y - 1)):
-            side_a_ref[i, span, :], side_b_ref[i, span, :] = pick(
-                flag_at(flags_ref, 0), low, high
-            )
     for j in range(count_y):
-        for part in range(2):
-            span = slice(part * block, (part + 1) * block)
-            row_a_ref[j, span, :], row_b_ref[j, span, :] = pick(
-                flag_at(flags_ref, 1), tile_of(0, j)[part + 1], tile_of(1, j)[part + 1]
-            )
+        row_a_ref[j], row_b_ref[j] = pick(odd_x, tile_of(0, j, both), tile_of(1, j, both))
 
 
 def corners_kernel(
     flags_ref,
-    basis_ref,
+    vectors_ref,
     side_a_ref,
     side_b_ref,
     corner_a_ref,
@@ -115,20 +101,13 @@
     for j in range(wide - 2):
         rest_a_ref[j + 1], rest_b_ref[j + 1] = pick(
             odd_x,
-            basis_ref[pl.ds(j, rest, stride=tiles), :],
-            basis_ref[pl.ds(wide - 2 + j, rest, stride=tiles), :],
+            vectors_ref[pl.ds(j, rest, stride=tiles), :],
+            vectors_ref[pl.ds(wide - 2 + j, rest, stride=tiles), :],
         )
 
 
-def source_of(neighbours_ref, k, tile, count_y):
-    neighbour = neighbours_ref[k, tile]
-    down = neighbour // 3
-    return (tile // count_y + down) * (count_y + 2) + tile % count_y + neighbour - 3 * down
-
-
 def residual_kernel(
-    neighbours_ref,
-    kinds_ref,
+    codes_ref,
     flags_ref,
     row_a_ref,
     row_b_ref,
@@ -140,8 +119,8 @@
     from_corner_b_ref,
     rest_a_ref,
     rest_b_ref,
-    table_high_ref,
-    table_low_ref,
+    stiff_ref,
+    mass_ref,
     residual_low_ref,
     residual_high_ref,
     message_a_ref,
@@ -149,7 +128,10 @@
     partial_ref,
     current_ref,
     ext_ref,
+    table_high_ref,
+    table_low_ref,
 ):
+    split_tables(stiff_ref, mass_ref, table_high_ref, table_low_ref, 1)
     count_y, both, side = row_a_ref.shape
     wide = count_y + 2
     block = both // 2
@@ -186,10 +168,9 @@
     for tile in range(2 * count_y):
         i, j = tile // count_y, tile % count_y
         total = 4.0 * own[i, j][:block] + own[i, j][block:]
-        for k in range(neighbours_ref.shape[0]):
-            source = source_of(neighbours_ref, k, tile, count_y)
-            kind = kinds_ref[k, tile]
-            chosen = ext_ref[source]
+        for k in range(codes_ref.shape[1]):
+            kind = codes_ref[1, k, tile]
+            chosen = ext_ref[codes_ref[0, k, tile]]
             pair = mul(chosen, table_high_ref[kind])
             total = total + (
                 pair[:block] + (pair[block:] + mul(chosen[:block], table_low_ref[kind]))
@@ -206,7 +187,7 @@
 
 
 def residual_rows_kernel(
-    flags_ref, low_ref, high_ref, side_a_ref, side_b_ref, partial_ref, row_a_ref, row_b_ref
+    flags_ref, low_ref, high_ref, side_a_ref, side_b_ref, row_a_ref, row_b_ref
 ):
     count_y = low_ref.shape[0]
     odd_y, odd_x = flag_at(flags_ref, 0), flag_at(flags_ref, 1)
@@ -215,13 +196,11 @@
         row_a_ref[j], row_b_ref[j] = pick(odd_x, sides[0][place], sides[1][place])
     for j in range(count_y):
         row_a_ref[j + 1], row_b_ref[j + 1] = pick(odd_x, low_ref[j], high_ref[j])
-    row_a_ref[count_y + 2] = partial_ref[...]
 
 
 def operators_kernel(
     inverse_rows,
-    neighbours_ref,
-    kinds_ref,
+    codes_ref,
     flags_ref,
     partial_ref,
     row_a_ref,
@@ -233,15 +212,18 @@
     from_rest_a_ref,
     from_rest_b_ref,
     current_ref,
-    table_high_ref,
-    table_low_ref,
+    stiff_ref,
+    mass_ref,
     weighted_low_ref,
     weighted_high_ref,
     coupling_ref,
     sums_ref,
     ext_ref,
     basis_ref,
+    table_high_ref,
+    table_low_ref,
 ):
+    split_tables(stiff_ref, mass_ref, table_high_ref, table_low_ref, 2)
     count_y, block, side = weighted_low_ref.shape
     wide, rest, _ = rest_a_ref.shape
     prior = rest + block
@@ -285,10 +267,9 @@
         i, j = tile // count_y, tile % count_y
         own = (weighted_low_ref, weighted_high_ref)[i][j]
         totals = jnp.concatenate([4.0 * own, own], axis=1)
-        for k in range(neighbours_ref.shape[0]):
-            source = source_of(neighbours_ref, k, tile, count_y)
-            kind = kinds_ref[k, tile]
-            chosen = ext_ref[source]
+        for k in range(codes_ref.shape[1]):
+            kind = codes_ref[1, k, tile]
+            chosen = ext_ref[codes_ref[0, k, tile]]
             pair = mul(chosen, table_high_ref[kind])
             totals = totals + (
                 pair[:block] + (pair[block:] + mul(chosen[:block], table_low_ref[kind]))
@@ -363,10 +344,13 @@
     return swap(message_a, axis, 1), other_swap(message_b, axis)
 
 
-def total_along(value, axis, first=1, near=None):
-    if lax.axis_size(axis) == 4 and first == 1:
-        near = swap(value, axis, 1) if near is None else near
-        return (value + swap(value, axis, 2)) + (near + swap(value, axis, 3))
+def total_at_once(value, axis):
+    if lax.axis_size(axis) != 4:
+        return total_along(value, axis)
+    return (value + swap(value, axis, 2)) + (swap(value, axis, 1) + swap(value, axis, 3))
+
+
+def total_along(value, axis, first=1):
     step = first
     while step < lax.axis_size(axis):
         value = value + swap(value, axis, step)
@@ -381,7 +365,7 @@
     kept = jnp.where(upper, second, first)
     kept = kept + swap(jnp.where(upper, first, second), "py", 1)
     kept = total_along(kept, "py", 2)
-    kept = total_along(kept, "px")
+    kept = total_at_once(kept, "px")
     other = swap(kept, "py", 1)
     return jnp.concatenate(
         [jnp.where(upper, other, kept), jnp.where(upper, kept, other)], axis=0
@@ -400,10 +384,12 @@
     rest = prior - block
     kinds = stiff_tiles.shape[0]
     inverse_rows = 1.0 / (tiles * side * lax.axis_size("px") * lax.axis_size("py"))
-    basis = prior_basis.reshape(-1, side)
-    previous_rows = previous.reshape(-1, side)
-    neighbours = neighbours.reshape(-1, tiles)
-    tile_kinds = tile_kinds.reshape(-1, tiles)
+    vectors = jnp.concatenate(
+        [prior_basis.reshape(-1, side), previous.reshape(-1, side)], axis=0
+    )
+    place = jnp.arange(count_x)[:, None] * wide + jnp.arange(count_y)[None, :]
+    sources = place[None] + (neighbours // 3) * wide + neighbours % 3
+    codes = jnp.stack([sources, tile_kinds]).astype(jnp.int32).reshape(2, -1, tiles)
     at_y, at_x = lax.axis_index("py"), lax.axis_index("px")
     flags = [at_y % 2 == 1, at_x % 2 == 1]
     flags += [at_y > 0, at_y < lax.axis_size("py") - 1]
@@ -411,35 +397,28 @@
     flags = jnp.stack(flags + flags[:2]).astype(F32)
     flags = jnp.broadcast_to(flags[:, None], (8, side))
 
-    def call(kernel, inputs, outputs, scratch=(), smem=0):
+    def call(kernel, inputs, outputs, scratch=(), smem=0, limit=8):
+        specs = [SMEM] * smem + [VMEM] * (len(inputs) - smem)
         return pl.pallas_call(
             kernel,
             out_shape=outputs,
-            in_specs=[SMEM] * smem + [VMEM] * (len(inputs) - smem),
+            in_specs=specs,
             out_specs=[VMEM] * len(outputs),
             scratch_shapes=scratch,
-            compiler_params=PARAMS,
+            compiler_params=pltpu.CompilerParams(vmem_limit_bytes=limit * MIB),
         )(*inputs)
 
     side_a, side_b, row_a, row_b = call(
         pack_kernel,
-        (flags, basis, previous_rows),
+        (flags, vectors),
         [shape(count_x, prior + block, side)] * 2 + [shape(count_y, 2 * block, side)] * 2,
-    )
-    tables = call(
-        tables_kernel,
-        (stiff_tiles, mass_tiles),
-        [shape(kinds, 2 * side, side, dtype=BF16)] * 2
-        + [shape(kinds, side, 2 * side, dtype=BF16)] * 2,
     )
     from_side_a, from_side_b = exchange(side_a, side_b, "py")
     from_row_a, from_row_b = exchange(row_a, row_b, "px")
-    from_side_a, neighbours, tile_kinds, *tables = lax.optimization_barrier(
-        (from_side_a, neighbours, tile_kinds, *tables)
-    )
+    from_side_a, codes = lax.optimization_barrier((from_side_a, codes))
     corner_a, corner_b, rest_a, rest_b = call(
         corners_kernel,
-        (flags, basis, from_side_a, from_side_b),
+        (flags, vectors, from_side_a, from_side_b),
         [shape(2, 2 * block, side)] * 2 + [shape(wide, rest, side)] * 2,
     )
     from_corner_a, from_corner_b = exchange(corner_a, corner_b, "px")
@@ -447,8 +426,7 @@
     residual_low, residual_high, message_a, message_b, partial, current = call(
         residual_kernel,
         (
-            neighbours,
-            tile_kinds,
+            codes,
             flags,
             row_a,
             row_b,
@@ -460,31 +438,32 @@
             from_corner_b,
             rest_a,
             rest_b,
-            *tables[:2],
+            stiff_tiles,
+            mass_tiles,
         ),
         [shape(count_y, block, side)] * 2
         + [shape(3, block, side), shape(2, block, side)]
         + [shape(block, prior), shape(4 * wide, block, side)],
-        [pltpu.VMEM((4 * wide, 2 * block, 2 * side), BF16)],
-        smem=2,
+        [pltpu.VMEM((4 * wide, 2 * block, 2 * side), BF16)]
+        + [pltpu.VMEM((kinds, 2 * side, side), BF16)] * 2,
+        smem=1,
     )
     from_side_a, from_side_b = exchange(message_a, message_b, "py")
     partial = total_along(partial + from_side_a[-1], "py", 2)
-    from_side_a, from_rest_a, from_rest_b = lax.optimization_barrier(
-        (from_side_a, from_rest_a, from_rest_b)
+    partial, from_rest_a, from_rest_b = lax.optimization_barrier(
+        (partial, from_rest_a, from_rest_b)
     )
     row_a, row_b = call(
         residual_rows_kernel,
-        (flags, residual_low, residual_high, from_side_a, from_side_b, partial),
-        [shape(wide + 1, block, side), shape(wide, block, side)],
+        (flags, residual_low, residual_high, from_side_a, from_side_b),
+        [shape(wide, block, side)] * 2,
     )
     from_row_a, from_row_b = exchange(row_a, row_b, "px")
-    partial = total_along(partial, "px", near=from_row_a[-1])
+    partial = total_along(partial, "px")
     weighted_low, weighted_high, coupling, sums = call(
         functools.partial(operators_kernel, inverse_rows),
         (
-            neighbours,
-            tile_kinds,
+            codes,
             flags,
             partial,
             row_a,
@@ -496,14 +475,16 @@
             from_rest_a,
             from_rest_b,
             current,
-            *tables[2:],
+            stiff_tiles,
+            mass_tiles,
         ),
         [shape(count_y, block, side)] * 2 + [shape(block, prior), shape(3 * block, prior)],
         [
             pltpu.VMEM((4 * wide, 2 * block, side), BF16),
             pltpu.VMEM((tiles, 2 * prior, side), BF16),
-        ],
-        smem=2,
+        ]
+        + [pltpu.VMEM((kinds, side, 2 * side), BF16)] * 2,
+        smem=1,
     )
     new_block, factor, reduced = call(
         functools.partial(factor_kernel, inverse_rows),

time: 64.2 us -> 63.2 us (0.984)
  starting transfers between devices: 31.2 us -> 36.5 us
  local copies, waits for them, and re-layouts: 4.89 us -> 0.36 us
  Pallas kernels: 11.5 us -> 9.6 us
  other arithmetic: 0.06 us -> 1.38 us
  waiting for transfers between devices: 15.2 us -> 14.3 us
    ppermute x15, starting transfers between devices: 23.4 us -> 32.4 us  [swap(): lax.ppermute(value, axis, [(i, i ^ step) for i in range(lax.axis_size(axi...]
    unnamed x18 -> x8, local copies, waits for them, and re-layouts: 4.55 us -> 0.01 us
    ppermute x6, starting transfers between devices: 7.85 us -> 4.07 us  [other_swap(): lax.ppermute(value, axis, [(i, j if 0 <= j < count else i) for i, j in pa...]
    pallas_call x7 -> x6, Pallas kernels: 11.5 us -> 9.6 us  [call(): pl.pallas_call(kernel, out_shape=outputs, in_specs=specs, out_specs=[VMEM...]
    concatenate x0 -> x1, other arithmetic: none -> 1.16 us  [shards(): jnp.concatenate([prior_basis.reshape(-1, side), previous.reshape(-1, side...]
    ppermute x15, waiting for transfers between devices: 15.2 us -> 14.2 us  [swap(): lax.ppermute(value, axis, [(i, i ^ step) for i in range(lax.axis_size(axi...]
  transfers between devices with their start and end apart: 21 -> 21, of which waited for: 10 -> 10; matrix products, arithmetic and copies ran while one was open for 0% -> 1% of each run, Pallas kernels for 7% -> 5%
where the time goes in v7:
time: 63.2 us; the launch traced here: 62.9 us
  starting transfers between devices  36.5 us (58%)
  waiting for transfers between devices  14.3 us (23%)
  Pallas kernels  9.6 us (15%)
  other arithmetic  1.38 us (2%)
  between operations  0.85 us (1%)
    ppermute x15, starting transfers between devices, swap(): lax.ppermute(value, axis, [(i, i ^ step) for i in range(lax.axis_size(axi...  32.4 us
    ppermute x15, waiting for transfers between devices, swap(): lax.ppermute(value, axis, [(i, i ^ step) for i in range(lax.axis_size(axi...  14.2 us
    pallas_call x6, Pallas kernels, call(): pl.pallas_call(kernel, out_shape=outputs, in_specs=specs, out_specs=[VMEM...  9.6 us
    ppermute x6, starting transfers between devices, other_swap(): lax.ppermute(value, axis, [(i, j if 0 <= j < count else i) for i, j in pa...  4.07 us
  transfers between devices with their start and end apart: 21, of which 10 were waited for; matrix products, arithmetic and copies ran while one was open for 1% of the time, Pallas kernels for 5%

profile of v7, /device:TPU:0, one launch (start us, length us, event | category | flops | bytes accessed | tf_op | source)
XLA Modules:
  0.0 62.9 jit_solution(16323158899561938592)
XLA Ops:
  0.7 0.1 stack.38
  0.8 1.2 %pad_maximum_fusion.vectors_ref = f32[1280,128]{1,0:T(8,128)S(1)} fusion(f32[256,128]{1,0:T(8,128)} %bitcast.18, f32[1024,128]{1,0:T(8,128)} %bitcast.17), kind=kLoop, calls=%fused_computation | loop fusion | flops 163840 | bytes 1310720 | tf_op jit(solution)/shard_map/concatenate | solution.py:387
  1.9 0.1 broadcast_in_dim.2.flags_ref
  2.0 0.1 shard_map.93
  2.1 0.5 collective-permute-start
  2.6 0.8 %collective-permute-start.3 = (f32[2,160,128]{2,1,0:T(8,128)S(1)}, f32[2,160,128]{2,1,0:T(8,128)S(1)}, u32[]{:S(2)}, u32[]{:S(2)}) collective-permute-start(f32[2,160,128]{2,1,0:T(8,128)S(1)} %get-tuple-element.37), channel_id=1, source_target_pairs={{0,0},{1,2},{2,1},{3,3},{4,4},{5,6},{6,5},{7,7},{8,8},{9,10},{10,9... | collective-permute-start | bytes 491528 | tf_op jit(solution)/shard_map/ppermute | solution.py:340
  3.4 2.7 %collective-permute-start.1 = (f32[4,64,128]{2,1,0:T(8,128)S(1)}, f32[4,64,128]{2,1,0:T(8,128)S(1)}, u32[]{:S(2)}, u32[]{:S(2)}) collective-permute-start(f32[4,64,128]{2,1,0:T(8,128)S(1)} %get-tuple-element.34.row_a_ref), channel_id=1, source_target_pairs={{0,4},{4,0},{8,12},{12,8},{1,5},{5,1},{9,13},{13,9},{2,6},{6,2},{1... | collective-permute-start | bytes 393224 | tf_op jit(solution)/shard_map/ppermute | solution.py:334
  6.1 0.7 %collective-permute-start.2 = (f32[4,64,128]{2,1,0:T(8,128)S(1)}, f32[4,64,128]{2,1,0:T(8,128)S(1)}, u32[]{:S(2)}, u32[]{:S(2)}) collective-permute-start(f32[4,64,128]{2,1,0:T(8,128)S(1)} %get-tuple-element.35.row_b_ref), channel_id=1, source_target_pairs={{0,0},{4,8},{8,4},{12,12},{1,1},{5,9},{9,5},{13,13},{2,2},{6,10},{... | collective-permute-start | bytes 393224 | tf_op jit(solution)/shard_map/ppermute | solution.py:340
  6.8 0.1 iota_add_fusion
  6.9 0.1 fusion.1
  6.9 0.1 copy.10
  7.0 0.1 copy.11
  7.1 0.0 collective-permute-done.side_a_ref.from_side_a_ref
  7.1 0.0 collective-permute-done.3.side_b_ref.from_side_b_ref
  7.1 0.1 shard_map.94
  7.2 4.5 %collective-permute-start.4 = (f32[2,64,128]{2,1,0:T(8,128)S(1)}, f32[2,64,128]{2,1,0:T(8,128)S(1)}, u32[]{:S(2)}, u32[]{:S(2)}) collective-permute-start(f32[2,64,128]{2,1,0:T(8,128)S(1)} %get-tuple-element.38), channel_id=1, source_target_pairs={{0,4},{4,0},{8,12},{12,8},{1,5},{5,1},{9,13},{13,9},{2,6},{6,2},{1... | collective-permute-start | bytes 196616 | tf_op jit(solution)/shard_map/ppermute | solution.py:334
  11.7 0.7 %collective-permute-start.5 = (f32[2,64,128]{2,1,0:T(8,128)S(1)}, f32[2,64,128]{2,1,0:T(8,128)S(1)}, u32[]{:S(2)}, u32[]{:S(2)}) collective-permute-start(f32[2,64,128]{2,1,0:T(8,128)S(1)} %get-tuple-element.39), channel_id=1, source_target_pairs={{0,0},{4,8},{8,4},{12,12},{1,1},{5,9},{9,5},{13,13},{2,2},{6,10},{... | collective-permute-start | bytes 196616 | tf_op jit(solution)/shard_map/ppermute | solution.py:340
  12.3 1.3 %collective-permute-start.8 = (f32[6,96,128]{2,1,0:T(8,128)S(1)}, f32[6,96,128]{2,1,0:T(8,128)S(1)}, u32[]{:S(2)}, u32[]{:S(2)}) collective-permute-start(f32[6,96,128]{2,1,0:T(8,128)S(1)} %get-tuple-element.40.rest_a_ref), channel_id=1, source_target_pairs={{0,4},{4,0},{8,12},{12,8},{1,5},{5,1},{9,13},{13,9},{2,6},{6,2},{1... | collective-permute-start | bytes 884744 | tf_op jit(solution)/shard_map/ppermute | solution.py:334
  13.7 0.0 collective-permute-done.1.from_row_a_ref
  13.7 0.7 %collective-permute-start.9 = (f32[6,96,128]{2,1,0:T(8,128)S(1)}, f32[6,96,128]{2,1,0:T(8,128)S(1)}, u32[]{:S(2)}, u32[]{:S(2)}) collective-permute-start(f32[6,96,128]{2,1,0:T(8,128)S(1)} %get-tuple-element.41.rest_b_ref), channel_id=1, source_target_pairs={{0,0},{4,8},{8,4},{12,12},{1,1},{5,9},{9,5},{13,13},{2,2},{6,10},{... | collective-permute-start | bytes 884744 | tf_op jit(solution)/shard_map/ppermute | solution.py:340
  14.4 0.0 collective-permute-done.2.from_row_b_ref
  14.4 0.0 collective-permute-done.4.from_corner_a_ref
  14.4 3.1 %shard_map.95 = (f32[4,32,128]{2,1,0:T(8,128)S(1)}, f32[4,32,128]{2,1,0:T(8,128)S(1)}, f32[3,32,128]{2,1,0:T(8,128)S(1)}, f32[2,32,128]{2,1,0:T(8,128)S(1)}, f32...) custom-call(s32[2,5,8]{2,1,0:T(8,128)S(1)} %pad_add_fusion.codes_ref, f32[8,128]{1,0:T(8,128)S(1)} %broadcast_in_dim.2.flags_ref, ...), custom_call_target="tpu_custom_call" | custom-call | tf_op jit(solution)/shard_map/pallas_call | solution.py:402
  17.5 3.6 %collective-permute-start.6 = (f32[3,32,128]{2,1,0:T(8,128)S(1)}, f32[3,32,128]{2,1,0:T(8,128)S(1)}, u32[]{:S(2)}, u32[]{:S(2)}) collective-permute-start(f32[3,32,128]{2,1,0:T(8,128)S(1)} %get-tuple-element.43), channel_id=1, source_target_pairs={{0,1},{1,0},{2,3},{3,2},{4,5},{5,4},{6,7},{7,6},{8,9},{9,8},{10,11... | collective-permute-start | bytes 147464 | tf_op jit(solution)/shard_map/ppermute | solution.py:334
  21.1 0.7 %collective-permute-start.12 = (f32[2,32,128]{2,1,0:T(8,128)S(1)}, f32[2,32,128]{2,1,0:T(8,128)S(1)}, u32[]{:S(2)}, u32[]{:S(2)}) collective-permute-start(f32[2,32,128]{2,1,0:T(8,128)S(1)} %get-tuple-element.47), channel_id=1, source_target_pairs={{0,0},{1,2},{2,1},{3,3},{4,4},{5,6},{6,5},{7,7},{8,8},{9,10},{10,9... | collective-permute-start | bytes 98312 | tf_op jit(solution)/shard_map/ppermute | solution.py:340
  21.7 0.0 collective-permute-done.12.side_b_ref
  21.8 0.2 collective-permute-done.6.side_a_ref
  22.0 1.6 %collective-permute-start.13 = (f32[6,32,128]{2,1,0:T(8,128)S(1)}, f32[6,32,128]{2,1,0:T(8,128)S(1)}, u32[]{:S(2)}, u32[]{:S(2)}) collective-permute-start(f32[6,32,128]{2,1,0:T(8,128)S(1)} %get-tuple-element.48.row_a_ref), channel_id=1, source_target_pairs={{0,4},{4,0},{8,12},{12,8},{1,5},{5,1},{9,13},{13,9},{2,6},{6,2},{1... | collective-permute-start | bytes 294920 | tf_op jit(solution)/shard_map/ppermute | solution.py:334
  23.6 0.7 %collective-permute-start.14 = (f32[6,32,128]{2,1,0:T(8,128)S(1)}, f32[6,32,128]{2,1,0:T(8,128)S(1)}, u32[]{:S(2)}, u32[]{:S(2)}) collective-permute-start(f32[6,32,128]{2,1,0:T(8,128)S(1)} %get-tuple-element.49.row_b_ref), channel_id=1, source_target_pairs={{0,0},{4,8},{8,4},{12,12},{1,1},{5,9},{9,5},{13,13},{2,2},{6,10},{... | collective-permute-start | bytes 294920 | tf_op jit(solution)/shard_map/ppermute | solution.py:340
  24.3 6.8 %collective-permute-start.7 = (f32[32,128]{1,0:T(8,128)S(1)}, f32[32,128]{1,0:T(8,128)S(1)}, u32[]{:S(2)}, u32[]{:S(2)}) collective-permute-start(f32[32,128]{1,0:T(8,128)S(1)} %fusion), channel_id=1, source_target_pairs={{0,2},{1,3},{2,0},{3,1},{4,6},{5,7},{6,4},{7,5},{8,10},{9,11},{10,... | collective-permute-start | bytes 49160 | tf_op jit(solution)/shard_map/ppermute | solution.py:334
  31.0 1.7 %collective-permute-done.7 = f32[32,128]{1,0:T(8,128)S(1)} collective-permute-done((f32[32,128]{1,0:T(8,128)S(1)}, f32[32,128]{1,0:T(8,128)S(1)}, u32[]{:S(2)}, u32[]{:S(2)}) %collective-permute-start.7) | collective-permute-done | bytes 16416 | tf_op jit(solution)/shard_map/ppermute | solution.py:334
  32.8 3.1 %collective-permute-start.10 = (f32[32,128]{1,0:T(8,128)S(1)}, f32[32,128]{1,0:T(8,128)S(1)}, u32[]{:S(2)}, u32[]{:S(2)}) collective-permute-start(f32[32,128]{1,0:T(8,128)S(1)} %add.80), channel_id=1, source_target_pairs={{0,4},{4,0},{8,12},{12,8},{1,5},{5,1},{9,13},{13,9},{2,6},{6,2},{1... | collective-permute-start | bytes 49160 | tf_op jit(solution)/shard_map/ppermute | solution.py:334
  35.9 1.7 %collective-permute-done.10 = f32[32,128]{1,0:T(8,128)S(1)} collective-permute-done((f32[32,128]{1,0:T(8,128)S(1)}, f32[32,128]{1,0:T(8,128)S(1)}, u32[]{:S(2)}, u32[]{:S(2)}) %collective-permute-start.10) | collective-permute-done | bytes 16416 | tf_op jit(solution)/shard_map/ppermute | solution.py:334
  37.6 1.7 %collective-permute-start.11 = (f32[32,128]{1,0:T(8,128)S(1)}, f32[32,128]{1,0:T(8,128)S(1)}, u32[]{:S(2)}, u32[]{:S(2)}) collective-permute-start(f32[32,128]{1,0:T(8,128)S(1)} %add.81), channel_id=1, source_target_pairs={{0,8},{4,12},{8,0},{12,4},{1,9},{5,13},{9,1},{13,5},{2,10},{6,14},... | collective-permute-start | bytes 49160 | tf_op jit(solution)/shard_map/ppermute | solution.py:334
  39.3 3.0 %collective-permute-done.11 = f32[32,128]{1,0:T(8,128)S(1)} collective-permute-done((f32[32,128]{1,0:T(8,128)S(1)}, f32[32,128]{1,0:T(8,128)S(1)}, u32[]{:S(2)}, u32[]{:S(2)}) %collective-permute-start.11) | collective-permute-done | bytes 16416 | tf_op jit(solution)/shard_map/ppermute | solution.py:334
  42.3 3.7 %shard_map.97 = (f32[4,32,128]{2,1,0:T(8,128)S(1)}, f32[4,32,128]{2,1,0:T(8,128)S(1)}, f32[32,128]{1,0:T(8,128)}, f32[96,128]{1,0:T(8,128)S(1)}) custom-call(s32[2,5,8]{2,1,0:T(8,128)S(1)} %pad_add_fusion.codes_ref, f32[8,128]{1,0:T(8,128)S(1)} %broadcast_in_dim.2.flags_ref, f32[32,128]{1,0:T(8,128)S(1)} %add.82.partial_ref, ...), custom_call_target="tpu_custom_call" | custom-call | tf_op jit(solution)/shard_map/pallas_call | solution.py:402
  46.0 1.2 %collective-permute-done.15 = f32[48,128]{1,0:T(8,128)S(1)} collective-permute-done((f32[48,128]{1,0:T(8,128)S(1)}, f32[48,128]{1,0:T(8,128)S(1)}, u32[]{:S(2)}, u32[]{:S(2)}) %collective-permute-start.15) | collective-permute-done | bytes 24608 | tf_op jit(solution)/shard_map/ppermute | solution.py:334
  47.2 2.2 %collective-permute-start.16 = (f32[48,128]{1,0:T(8,128)S(1)}, f32[48,128]{1,0:T(8,128)S(1)}, u32[]{:S(2)}, u32[]{:S(2)}) collective-permute-start(f32[48,128]{1,0:T(8,128)S(1)} %select_add_fusion), channel_id=1, source_target_pairs={{0,2},{1,3},{2,0},{3,1},{4,6},{5,7},{6,4},{7,5},{8,10},{9,11},{10,... | collective-permute-start | bytes 73736 | tf_op jit(solution)/shard_map/ppermute | solution.py:334
  49.4 1.8 %collective-permute-done.16 = f32[48,128]{1,0:T(8,128)S(1)} collective-permute-done((f32[48,128]{1,0:T(8,128)S(1)}, f32[48,128]{1,0:T(8,128)S(1)}, u32[]{:S(2)}, u32[]{:S(2)}) %collective-permute-start.16) | collective-permute-done | bytes 24608 | tf_op jit(solution)/shard_map/ppermute | solution.py:334
  51.2 1.5 %collective-permute-start.17 = (f32[48,128]{1,0:T(8,128)S(1)}, f32[48,128]{1,0:T(8,128)S(1)}, u32[]{:S(2)}, u32[]{:S(2)}) collective-permute-start(f32[48,128]{1,0:T(8,128)S(1)} %add.84), channel_id=1, source_target_pairs={{0,8},{4,12},{8,0},{12,4},{1,9},{5,13},{9,1},{13,5},{2,10},{6,14},... | collective-permute-start | bytes 73736 | tf_op jit(solution)/shard_map/ppermute | solution.py:334
  52.7 0.7 %collective-permute-start.18 = (f32[48,128]{1,0:T(8,128)S(1)}, f32[48,128]{1,0:T(8,128)S(1)}, u32[]{:S(2)}, u32[]{:S(2)}) collective-permute-start(f32[48,128]{1,0:T(8,128)S(1)} %add.84), channel_id=1, source_target_pairs={{0,4},{4,0},{8,12},{12,8},{1,5},{5,1},{9,13},{13,9},{2,6},{6,2},{1... | collective-permute-start | bytes 73736 | tf_op jit(solution)/shard_map/ppermute | solution.py:334
  53.4 2.2 %collective-permute-start.19 = (f32[48,128]{1,0:T(8,128)S(1)}, f32[48,128]{1,0:T(8,128)S(1)}, u32[]{:S(2)}, u32[]{:S(2)}) collective-permute-start(f32[48,128]{1,0:T(8,128)S(1)} %add.84), channel_id=1, source_target_pairs={{0,12},{4,8},{8,4},{12,0},{1,13},{5,9},{9,5},{13,1},{2,14},{6,10},... | collective-permute-start | bytes 73736 | tf_op jit(solution)/shard_map/ppermute | solution.py:334
  55.6 0.5 collective-permute-done.17
  56.1 0.5 collective-permute-done.18
  56.5 2.5 %collective-permute-done.19 = f32[48,128]{1,0:T(8,128)S(1)} collective-permute-done((f32[48,128]{1,0:T(8,128)S(1)}, f32[48,128]{1,0:T(8,128)S(1)}, u32[]{:S(2)}, u32[]{:S(2)}) %collective-permute-start.19) | collective-permute-done | bytes 24608 | tf_op jit(solution)/shard_map/ppermute | solution.py:334
  59.1 0.1 collective-permute-start.20
  59.1 1.2 %collective-permute-done.20 = f32[48,128]{1,0:T(8,128)S(1)} collective-permute-done((f32[48,128]{1,0:T(8,128)S(1)}, f32[48,128]{1,0:T(8,128)S(1)}, u32[]{:S(2)}, u32[]{:S(2)}) %collective-permute-start.20) | collective-permute-done | bytes 24608 | tf_op jit(solution)/shard_map/ppermute | solution.py:334
  60.3 2.6 %shard_map.98 = (f32[256,128]{1,0:T(8,128)}, f32[32,32]{1,0:T(8,128)}, f32[2,32,160]{2,1,0:T(8,128)}) custom-call(f32[96,128]{1,0:T(8,128)S(1)} %pad_maximum_fusion.1.sums_ref, f32[4,32,128]{2,1,0:T(8,128)S(1)} %get-tuple-element.54.weighted_low_ref, f32[4,32,128]{2,1,0:T(8,128)S(1)} %get-tuple-element.55.weighted_high_ref), custom_call_target="tpu_custom_call" | custom-call | tf_op jit(solution)/shard_map/pallas_call | solution.py:402
  (28 shorter events, 0.1 us)
Async XLA Ops:
  2.0 4.8 %copy-start.2 = (s32[5,2,4]{0,2,1:T(4,128)S(1)}, s32[5,2,4]{0,2,1:T(4,128)}, u32[]{:S(2)}) copy-start(s32[5,2,4]{0,2,1:T(4,128)} %param.8) | copy-start | bytes 484
  2.0 5.0 %copy-start.3 = (s32[5,2,4]{0,2,1:T(4,128)S(1)}, s32[5,2,4]{0,2,1:T(4,128)}, u32[]{:S(2)}) copy-start(s32[5,2,4]{0,2,1:T(4,128)} %param.9) | copy-start | bytes 484
  2.1 5.0 %collective-permute-start = (f32[2,160,128]{2,1,0:T(8,128)S(1)}, f32[2,160,128]{2,1,0:T(8,128)S(1)}, u32[]{:S(2)}, u32[]{:S(2)}) collective-permute-start(f32[2,160,128]{2,1,0:T(8,128)S(1)} %get-tuple-element.32), channel_id=1, source_target_pairs={{0,1},{1,0},{2,3},{3,2},{4,5},{5,4},{6,7},{7,6},{8,9},{9,8},{10,11... | collective-permute-start | bytes 491528 | tf_op jit(solution)/shard_map/ppermute | solution.py:334
  2.6 11.8 %copy-start.1 = (f32[8,128,128]{2,1,0:T(8,128)S(1)}, f32[8,128,128]{2,1,0:T(8,128)}, u32[]{:S(2)}) copy-start(f32[8,128,128]{2,1,0:T(8,128)} %mass_ref.3) | copy-start | bytes 1572868
  2.6 11.8 %copy-start = (f32[8,128,128]{2,1,0:T(8,128)S(1)}, f32[8,128,128]{2,1,0:T(8,128)}, u32[]{:S(2)}) copy-start(f32[8,128,128]{2,1,0:T(8,128)} %stiff_ref.3) | copy-start | bytes 1572868
  2.6 4.5 %collective-permute-start.3 = (f32[2,160,128]{2,1,0:T(8,128)S(1)}, f32[2,160,128]{2,1,0:T(8,128)S(1)}, u32[]{:S(2)}, u32[]{:S(2)}) collective-permute-start(f32[2,160,128]{2,1,0:T(8,128)S(1)} %get-tuple-element.37), channel_id=1, source_target_pairs={{0,0},{1,2},{2,1},{3,3},{4,4},{5,6},{6,5},{7,7},{8,8},{9,10},{10,9... | collective-permute-start | bytes 491528 | tf_op jit(solution)/shard_map/ppermute | solution.py:340
  3.4 10.3 %collective-permute-start.1 = (f32[4,64,128]{2,1,0:T(8,128)S(1)}, f32[4,64,128]{2,1,0:T(8,128)S(1)}, u32[]{:S(2)}, u32[]{:S(2)}) collective-permute-start(f32[4,64,128]{2,1,0:T(8,128)S(1)} %get-tuple-element.34.row_a_ref), channel_id=1, source_target_pairs={{0,4},{4,0},{8,12},{12,8},{1,5},{5,1},{9,13},{13,9},{2,6},{6,2},{1... | collective-permute-start | bytes 393224 | tf_op jit(solution)/shard_map/ppermute | solution.py:334
  6.1 8.3 %collective-permute-start.2 = (f32[4,64,128]{2,1,0:T(8,128)S(1)}, f32[4,64,128]{2,1,0:T(8,128)S(1)}, u32[]{:S(2)}, u32[]{:S(2)}) collective-permute-start(f32[4,64,128]{2,1,0:T(8,128)S(1)} %get-tuple-element.35.row_b_ref), channel_id=1, source_target_pairs={{0,0},{4,8},{8,4},{12,12},{1,1},{5,9},{9,5},{13,13},{2,2},{6,10},{... | collective-permute-start | bytes 393224 | tf_op jit(solution)/shard_map/ppermute | solution.py:340
  7.2 7.2 %collective-permute-start.4 = (f32[2,64,128]{2,1,0:T(8,128)S(1)}, f32[2,64,128]{2,1,0:T(8,128)S(1)}, u32[]{:S(2)}, u32[]{:S(2)}) collective-permute-start(f32[2,64,128]{2,1,0:T(8,128)S(1)} %get-tuple-element.38), channel_id=1, source_target_pairs={{0,4},{4,0},{8,12},{12,8},{1,5},{5,1},{9,13},{13,9},{2,6},{6,2},{1... | collective-permute-start | bytes 196616 | tf_op jit(solution)/shard_map/ppermute | solution.py:334
  11.7 2.7 %collective-permute-start.5 = (f32[2,64,128]{2,1,0:T(8,128)S(1)}, f32[2,64,128]{2,1,0:T(8,128)S(1)}, u32[]{:S(2)}, u32[]{:S(2)}) collective-permute-start(f32[2,64,128]{2,1,0:T(8,128)S(1)} %get-tuple-element.39), channel_id=1, source_target_pairs={{0,0},{4,8},{8,4},{12,12},{1,1},{5,9},{9,5},{13,13},{2,2},{6,10},{... | collective-permute-start | bytes 196616 | tf_op jit(solution)/shard_map/ppermute | solution.py:340
  12.3 20.4 %collective-permute-start.8 = (f32[6,96,128]{2,1,0:T(8,128)S(1)}, f32[6,96,128]{2,1,0:T(8,128)S(1)}, u32[]{:S(2)}, u32[]{:S(2)}) collective-permute-start(f32[6,96,128]{2,1,0:T(8,128)S(1)} %get-tuple-element.40.rest_a_ref), channel_id=1, source_target_pairs={{0,4},{4,0},{8,12},{12,8},{1,5},{5,1},{9,13},{13,9},{2,6},{6,2},{1... | collective-permute-start | bytes 884744 | tf_op jit(solution)/shard_map/ppermute | solution.py:334
  13.7 19.1 %collective-permute-start.9 = (f32[6,96,128]{2,1,0:T(8,128)S(1)}, f32[6,96,128]{2,1,0:T(8,128)S(1)}, u32[]{:S(2)}, u32[]{:S(2)}) collective-permute-start(f32[6,96,128]{2,1,0:T(8,128)S(1)} %get-tuple-element.41.rest_b_ref), channel_id=1, source_target_pairs={{0,0},{4,8},{8,4},{12,12},{1,1},{5,9},{9,5},{13,13},{2,2},{6,10},{... | collective-permute-start | bytes 884744 | tf_op jit(solution)/shard_map/ppermute | solution.py:340
  17.5 4.4 %collective-permute-start.6 = (f32[3,32,128]{2,1,0:T(8,128)S(1)}, f32[3,32,128]{2,1,0:T(8,128)S(1)}, u32[]{:S(2)}, u32[]{:S(2)}) collective-permute-start(f32[3,32,128]{2,1,0:T(8,128)S(1)} %get-tuple-element.43), channel_id=1, source_target_pairs={{0,1},{1,0},{2,3},{3,2},{4,5},{5,4},{6,7},{7,6},{8,9},{9,8},{10,11... | collective-permute-start | bytes 147464 | tf_op jit(solution)/shard_map/ppermute | solution.py:334
  21.1 0.7 %collective-permute-start.12 = (f32[2,32,128]{2,1,0:T(8,128)S(1)}, f32[2,32,128]{2,1,0:T(8,128)S(1)}, u32[]{:S(2)}, u32[]{:S(2)}) collective-permute-start(f32[2,32,128]{2,1,0:T(8,128)S(1)} %get-tuple-element.47), channel_id=1, source_target_pairs={{0,0},{1,2},{2,1},{3,3},{4,4},{5,6},{6,5},{7,7},{8,8},{9,10},{10,9... | collective-permute-start | bytes 98312 | tf_op jit(solution)/shard_map/ppermute | solution.py:340
  22.0 20.3 %collective-permute-start.13 = (f32[6,32,128]{2,1,0:T(8,128)S(1)}, f32[6,32,128]{2,1,0:T(8,128)S(1)}, u32[]{:S(2)}, u32[]{:S(2)}) collective-permute-start(f32[6,32,128]{2,1,0:T(8,128)S(1)} %get-tuple-element.48.row_a_ref), channel_id=1, source_target_pairs={{0,4},{4,0},{8,12},{12,8},{1,5},{5,1},{9,13},{13,9},{2,6},{6,2},{1... | collective-permute-start | bytes 294920 | tf_op jit(solution)/shard_map/ppermute | solution.py:334
  23.6 18.7 %collective-permute-start.14 = (f32[6,32,128]{2,1,0:T(8,128)S(1)}, f32[6,32,128]{2,1,0:T(8,128)S(1)}, u32[]{:S(2)}, u32[]{:S(2)}) collective-permute-start(f32[6,32,128]{2,1,0:T(8,128)S(1)} %get-tuple-element.49.row_b_ref), channel_id=1, source_target_pairs={{0,0},{4,8},{8,4},{12,12},{1,1},{5,9},{9,5},{13,13},{2,2},{6,10},{... | collective-permute-start | bytes 294920 | tf_op jit(solution)/shard_map/ppermute | solution.py:340
  24.3 8.5 %collective-permute-start.7 = (f32[32,128]{1,0:T(8,128)S(1)}, f32[32,128]{1,0:T(8,128)S(1)}, u32[]{:S(2)}, u32[]{:S(2)}) collective-permute-start(f32[32,128]{1,0:T(8,128)S(1)} %fusion), channel_id=1, source_target_pairs={{0,2},{1,3},{2,0},{3,1},{4,6},{5,7},{6,4},{7,5},{8,10},{9,11},{10,... | collective-permute-start | bytes 49160 | tf_op jit(solution)/shard_map/ppermute | solution.py:334
  32.8 4.9 %collective-permute-start.10 = (f32[32,128]{1,0:T(8,128)S(1)}, f32[32,128]{1,0:T(8,128)S(1)}, u32[]{:S(2)}, u32[]{:S(2)}) collective-permute-start(f32[32,128]{1,0:T(8,128)S(1)} %add.80), channel_id=1, source_target_pairs={{0,4},{4,0},{8,12},{12,8},{1,5},{5,1},{9,13},{13,9},{2,6},{6,2},{1... | collective-permute-start | bytes 49160 | tf_op jit(solution)/shard_map/ppermute | solution.py:334
  37.6 4.6 %collective-permute-start.11 = (f32[32,128]{1,0:T(8,128)S(1)}, f32[32,128]{1,0:T(8,128)S(1)}, u32[]{:S(2)}, u32[]{:S(2)}) collective-permute-start(f32[32,128]{1,0:T(8,128)S(1)} %add.81), channel_id=1, source_target_pairs={{0,8},{4,12},{8,0},{12,4},{1,9},{5,13},{9,1},{13,5},{2,10},{6,14},... | collective-permute-start | bytes 49160 | tf_op jit(solution)/shard_map/ppermute | solution.py:334
  46.0 1.2 %collective-permute-start.15 = (f32[48,128]{1,0:T(8,128)S(1)}, f32[48,128]{1,0:T(8,128)S(1)}, u32[]{:S(2)}, u32[]{:S(2)}) collective-permute-start(f32[48,128]{1,0:T(8,128)S(1)} %slice_select_fusion), channel_id=1, source_target_pairs={{0,1},{1,0},{2,3},{3,2},{4,5},{5,4},{6,7},{7,6},{8,9},{9,8},{10,11... | collective-permute-start | bytes 73736 | tf_op jit(solution)/shard_map/ppermute | solution.py:334
  47.2 4.0 %collective-permute-start.16 = (f32[48,128]{1,0:T(8,128)S(1)}, f32[48,128]{1,0:T(8,128)S(1)}, u32[]{:S(2)}, u32[]{:S(2)}) collective-permute-start(f32[48,128]{1,0:T(8,128)S(1)} %select_add_fusion), channel_id=1, source_target_pairs={{0,2},{1,3},{2,0},{3,1},{4,6},{5,7},{6,4},{7,5},{8,10},{9,11},{10,... | collective-permute-start | bytes 73736 | tf_op jit(solution)/shard_map/ppermute | solution.py:334
  51.2 4.9 %collective-permute-start.17 = (f32[48,128]{1,0:T(8,128)S(1)}, f32[48,128]{1,0:T(8,128)S(1)}, u32[]{:S(2)}, u32[]{:S(2)}) collective-permute-start(f32[48,128]{1,0:T(8,128)S(1)} %add.84), channel_id=1, source_target_pairs={{0,8},{4,12},{8,0},{12,4},{1,9},{5,13},{9,1},{13,5},{2,10},{6,14},... | collective-permute-start | bytes 73736 | tf_op jit(solution)/shard_map/ppermute | solution.py:334
  52.7 3.8 %collective-permute-start.18 = (f32[48,128]{1,0:T(8,128)S(1)}, f32[48,128]{1,0:T(8,128)S(1)}, u32[]{:S(2)}, u32[]{:S(2)}) collective-permute-start(f32[48,128]{1,0:T(8,128)S(1)} %add.84), channel_id=1, source_target_pairs={{0,4},{4,0},{8,12},{12,8},{1,5},{5,1},{9,13},{13,9},{2,6},{6,2},{1... | collective-permute-start | bytes 73736 | tf_op jit(solution)/shard_map/ppermute | solution.py:334
  53.4 5.6 %collective-permute-start.19 = (f32[48,128]{1,0:T(8,128)S(1)}, f32[48,128]{1,0:T(8,128)S(1)}, u32[]{:S(2)}, u32[]{:S(2)}) collective-permute-start(f32[48,128]{1,0:T(8,128)S(1)} %add.84), channel_id=1, source_target_pairs={{0,12},{4,8},{8,4},{12,0},{1,13},{5,9},{9,5},{13,1},{2,14},{6,10},... | collective-permute-start | bytes 73736 | tf_op jit(solution)/shard_map/ppermute | solution.py:334
  59.1 1.3 %collective-permute-start.20 = (f32[48,128]{1,0:T(8,128)S(1)}, f32[48,128]{1,0:T(8,128)S(1)}, u32[]{:S(2)}, u32[]{:S(2)}) collective-permute-start(f32[48,128]{1,0:T(8,128)S(1)} %add_add_fusion), channel_id=1, source_target_pairs={{0,1},{1,0},{2,3},{3,2},{4,5},{5,4},{6,7},{7,6},{8,9},{9,8},{10,11... | collective-permute-start | bytes 73736 | tf_op jit(solution)/shard_map/ppermute | solution.py:334

commit v8 on v7

--- a/solution.py
+++ b/solution.py
@@ -59,51 +59,55 @@
     return flags_ref[place : place + 1, :]
 
 
-def pack_kernel(flags_ref, vectors_ref, side_a_ref, side_b_ref, row_a_ref, row_b_ref):
-    count_x, sides, _ = side_a_ref.shape
-    count_y, both, _ = row_a_ref.shape
-    tiles = count_x * count_y
-    odd_y, odd_x = flag_at(flags_ref, 0), flag_at(flags_ref, 1)
-
-    def tile_of(i, j, count):
-        first = (sides - count) * tiles + i * count_y + j
-        return vectors_ref[pl.ds(first, count, stride=tiles), :]
-
-    for i in range(count_x):
-        side_a_ref[i], side_b_ref[i] = pick(
-            odd_y, tile_of(i, 0, sides), tile_of(i, count_y - 1, sides)
-        )
-    for j in range(count_y):
-        row_a_ref[j], row_b_ref[j] = pick(odd_x, tile_of(0, j, both), tile_of(1, j, both))
-
-
-def corners_kernel(
+def pack_kernel(
     flags_ref,
     vectors_ref,
     side_a_ref,
     side_b_ref,
-    corner_a_ref,
-    corner_b_ref,
+    row_a_ref,
+    row_b_ref,
     rest_a_ref,
     rest_b_ref,
 ):
-    wide, rest, _ = rest_a_ref.shape
-    tiles = 2 * (wide - 2)
+    count_y, both, _ = row_a_ref.shape
+    rest = rest_a_ref.shape[1]
+    tiles = 2 * count_y
+    odd_y, odd_x = flag_at(flags_ref, 0), flag_at(flags_ref, 1)
+
+    def block_tile(i, j):
+        return vectors_ref[pl.ds(rest * tiles + i * count_y + j, both, stride=tiles), :]
+
+    def rest_tile(i, j):
+        return vectors_ref[pl.ds(i * count_y + j, rest, stride=tiles), :]
+
+    for i in range(2):
+        side_a_ref[i], side_b_ref[i] = pick(odd_y, block_tile(i, 0), block_tile(i, count_y - 1))
+    for j in range(count_y):
+        row_a_ref[j], row_b_ref[j] = pick(odd_x, block_tile(0, j), block_tile(1, j))
+        rest_a_ref[j], rest_b_ref[j] = pick(odd_x, rest_tile(0, j), rest_tile(1, j))
+
+
+def corners_kernel(flags_ref, side_a_ref, side_b_ref, corner_a_ref, corner_b_ref):
     odd_y, odd_x = flag_at(flags_ref, 0), flag_at(flags_ref, 1)
     ends = [pick(odd_y, side_a_ref[i], side_b_ref[i]) for i in range(2)]
-    for place, j in ((0, 0), (1, wide - 1)):
-        corner_a_ref[place], corner_b_ref[place] = pick(
-            odd_x, ends[0][place][rest:], ends[1][place][rest:]
-        )
-        rest_a_ref[j], rest_b_ref[j] = pick(
-            odd_x, ends[0][place][:rest], ends[1][place][:rest]
-        )
-    for j in range(wide - 2):
-        rest_a_ref[j + 1], rest_b_ref[j + 1] = pick(
-            odd_x,
-            vectors_ref[pl.ds(j, rest, stride=tiles), :],
-            vectors_ref[pl.ds(wide - 2 + j, rest, stride=tiles), :],
-        )
+    for place in range(2):
+        corner_a_ref[place], corner_b_ref[place] = pick(odd_x, ends[0][place], ends[1][place])
+
+
+def columns_kernel(
+    flags_ref, row_a_ref, row_b_ref, from_row_a_ref, from_row_b_ref, *refs
+):
+    odd_y, odd_x = flag_at(flags_ref, 0), flag_at(flags_ref, 1)
+    side_a_ref, side_b_ref = refs[-2:]
+    columns = []
+    for j in (0, row_b_ref.shape[0] - 1):
+        column = list(pick(odd_x, from_row_a_ref[j], from_row_b_ref[j]))
+        column[1:1] = pick(odd_x, row_a_ref[j], row_b_ref[j])
+        columns.append(column)
+    for i in range(4):
+        side_a_ref[i], side_b_ref[i] = pick(odd_y, columns[0][i], columns[1][i])
+    if len(refs) == 3:
+        side_a_ref[4] = refs[0][...]
 
 
 def residual_kernel(
@@ -121,10 +125,8 @@
     rest_b_ref,
     stiff_ref,
     mass_ref,
-    residual_low_ref,
-    residual_high_ref,
-    message_a_ref,
-    message_b_ref,
+    residual_a_ref,
+    residual_b_ref,
     partial_ref,
     current_ref,
     ext_ref,
@@ -156,7 +158,7 @@
         store(0, j + 1, low * in_low_x)
         store(3, j + 1, high * in_high_x)
     for i in range(2):
-        low, high = pick(odd_y, from_side_a_ref[i, rest:, :], from_side_b_ref[i, rest:, :])
+        low, high = pick(odd_y, from_side_a_ref[i], from_side_b_ref[i])
         store(i + 1, 0, low * in_low_y)
         store(i + 1, wide - 1, high * in_high_y)
     for place, j, inside in ((0, 0, in_low_y), (1, wide - 1, in_high_y)):
@@ -164,7 +166,7 @@
         store(0, j, low * (in_low_x * inside))
         store(3, j, high * (in_high_x * inside))
     partial = jnp.zeros((block, rest + block), F32)
-    ends = {}
+    totals = {}
     for tile in range(2 * count_y):
         i, j = tile // count_y, tile % count_y
         total = 4.0 * own[i, j][:block] + own[i, j][block:]
@@ -175,27 +177,14 @@
             total = total + (
                 pair[:block] + (pair[block:] + mul(chosen[:block], table_low_ref[kind]))
             )
-        (residual_low_ref, residual_high_ref)[i][j] = total
-        ends[i, j] = total
-        rest_tile = pick(odd_x, rest_a_ref[j + 1], rest_b_ref[j + 1])[i]
+        totals[i, j] = total
+        rest_tile = pick(odd_x, rest_a_ref[j], rest_b_ref[j])[i]
         basis_tile = jnp.concatenate([rest_tile, own[i, j][:block]], axis=0)
         partial = partial + mul3_t(total, basis_tile)
-    for i in range(2):
-        message_a_ref[i], message_b_ref[i] = pick(odd_y, ends[i, 0], ends[i, count_y - 1])
-    message_a_ref[2] = partial
+    for j in range(count_y):
+        residual_a_ref[j], residual_b_ref[j] = pick(odd_x, totals[0, j], totals[1, j])
+    residual_a_ref[count_y] = partial
     partial_ref[...] = partial
-
-
-def residual_rows_kernel(
-    flags_ref, low_ref, high_ref, side_a_ref, side_b_ref, row_a_ref, row_b_ref
-):
-    count_y = low_ref.shape[0]
-    odd_y, odd_x = flag_at(flags_ref, 0), flag_at(flags_ref, 1)
-    sides = [pick(odd_y, side_a_ref[i], side_b_ref[i]) for i in range(2)]
-    for place, j in ((0, 0), (1, count_y + 1)):
-        row_a_ref[j], row_b_ref[j] = pick(odd_x, sides[0][place], sides[1][place])
-    for j in range(count_y):
-        row_a_ref[j + 1], row_b_ref[j + 1] = pick(odd_x, low_ref[j], high_ref[j])
 
 
 def operators_kernel(
@@ -207,10 +196,14 @@
     row_b_ref,
     from_row_a_ref,
     from_row_b_ref,
+    from_side_a_ref,
+    from_side_b_ref,
     rest_a_ref,
     rest_b_ref,
     from_rest_a_ref,
     from_rest_b_ref,
+    rest_side_a_ref,
+    rest_side_b_ref,
     current_ref,
     stiff_ref,
     mass_ref,
@@ -225,7 +218,8 @@
 ):
     split_tables(stiff_ref, mass_ref, table_high_ref, table_low_ref, 2)
     count_y, block, side = weighted_low_ref.shape
-    wide, rest, _ = rest_a_ref.shape
+    wide = count_y + 2
+    rest = rest_a_ref.shape[1]
     prior = rest + block
     odd_y, odd_x, in_low_y, in_high_y, in_low_x, in_high_x = (
         flag_at(flags_ref, place) for place in range(6)
@@ -235,10 +229,15 @@
     coupling_high, coupling_low = split(coupling)
 
     for j in range(wide):
-        rows = list(pick(odd_x, from_row_a_ref[j], from_row_b_ref[j]))
-        rows[1:1] = pick(odd_x, row_a_ref[j], row_b_ref[j])
-        rests = list(pick(odd_x, from_rest_a_ref[j], from_rest_b_ref[j]))
-        rests[1:1] = pick(odd_x, rest_a_ref[j], rest_b_ref[j])
+        if 0 < j < wide - 1:
+            rows = list(pick(odd_x, from_row_a_ref[j - 1], from_row_b_ref[j - 1]))
+            rows[1:1] = pick(odd_x, row_a_ref[j - 1], row_b_ref[j - 1])
+            rests = list(pick(odd_x, from_rest_a_ref[j - 1], from_rest_b_ref[j - 1]))
+            rests[1:1] = pick(odd_x, rest_a_ref[j - 1], rest_b_ref[j - 1])
+        else:
+            high = j // (wide - 1)
+            rows = [pick(odd_y, from_side_a_ref[i], from_side_b_ref[i])[high] for i in range(4)]
+            rests = [pick(odd_y, rest_side_a_ref[i], rest_side_b_ref[i])[high] for i in range(4)]
         for i in range(4):
             tile = jnp.concatenate([rests[i], current_ref[i * wide + j]], axis=0)
             high, low = split(tile)
@@ -330,31 +329,24 @@
         reduced_ref[part, :, prior:] = mul3_t(mul3_t(inverse, with_own[:, span]), inverse)
 
 
-def swap(value, axis, step):
-    return lax.ppermute(value, axis, [(i, i ^ step) for i in range(lax.axis_size(axis))])
-
-
-def other_swap(value, axis):
+def swap(value, mask):
+    axes = ("px", "py")
+    pairs = [(i, i ^ mask) for i in range(lax.axis_size(axes))]
+    return lax.ppermute(value, axes, pairs)
+
+
+def exchange(message_a, message_b, axis):
     count = lax.axis_size(axis)
     pairs = [(i, ((i + 1) ^ 1) - 1) for i in range(count)]
-    return lax.ppermute(value, axis, [(i, j if 0 <= j < count else i) for i, j in pairs])
-
-
-def exchange(message_a, message_b, axis):
-    return swap(message_a, axis, 1), other_swap(message_b, axis)
-
-
-def total_at_once(value, axis):
-    if lax.axis_size(axis) != 4:
-        return total_along(value, axis)
-    return (value + swap(value, axis, 2)) + (swap(value, axis, 1) + swap(value, axis, 3))
-
-
-def total_along(value, axis, first=1):
-    step = first
-    while step < lax.axis_size(axis):
-        value = value + swap(value, axis, step)
-        step *= 2
+    pairs = [(i, j if 0 <= j < count else i) for i, j in pairs]
+    near = [(i, i ^ 1) for i in range(count)]
+    return lax.ppermute(message_a, axis, near), lax.ppermute(message_b, axis, pairs)
+
+
+def total_over(value, first, last):
+    while first < last:
+        value = value + swap(value, first)
+        first *= 2
     return value
 
 
@@ -363,10 +355,10 @@
     upper = lax.axis_index("py") % 2 == 1
     first, second = value[:half], value[half:]
     kept = jnp.where(upper, second, first)
-    kept = kept + swap(jnp.where(upper, first, second), "py", 1)
-    kept = total_along(kept, "py", 2)
-    kept = total_at_once(kept, "px")
-    other = swap(kept, "py", 1)
+    kept = kept + swap(jnp.where(upper, first, second), 1)
+    kept = (kept + swap(kept, 6)) + (swap(kept, 2) + swap(kept, 4))
+    kept = total_over(kept, 8, lax.axis_size(("px", "py")))
+    other = swap(kept, 1)
     return jnp.concatenate(
         [jnp.where(upper, other, kept), jnp.where(upper, kept, other)], axis=0
     )
@@ -397,7 +389,7 @@
     flags = jnp.stack(flags + flags[:2]).astype(F32)
     flags = jnp.broadcast_to(flags[:, None], (8, side))
 
-    def call(kernel, inputs, outputs, scratch=(), smem=0, limit=8):
+    def call(kernel, inputs, outputs, scratch=(), smem=0, limit=8, cost=None):
         specs = [SMEM] * smem + [VMEM] * (len(inputs) - smem)
         return pl.pallas_call(
             kernel,
@@ -406,24 +398,33 @@
             out_specs=[VMEM] * len(outputs),
             scratch_shapes=scratch,
             compiler_params=pltpu.CompilerParams(vmem_limit_bytes=limit * MIB),
+            cost_estimate=cost,
         )(*inputs)
 
-    side_a, side_b, row_a, row_b = call(
+    side_a, side_b, row_a, row_b, rest_a, rest_b = call(
         pack_kernel,
         (flags, vectors),
-        [shape(count_x, prior + block, side)] * 2 + [shape(count_y, 2 * block, side)] * 2,
+        [shape(count_x, 2 * block, side)] * 2
+        + [shape(count_y, 2 * block, side)] * 2
+        + [shape(count_y, rest, side)] * 2,
     )
     from_side_a, from_side_b = exchange(side_a, side_b, "py")
     from_row_a, from_row_b = exchange(row_a, row_b, "px")
+    from_rest_a, from_rest_b = exchange(rest_a, rest_b, "px")
     from_side_a, codes = lax.optimization_barrier((from_side_a, codes))
-    corner_a, corner_b, rest_a, rest_b = call(
+    corner_a, corner_b = call(
         corners_kernel,
-        (flags, vectors, from_side_a, from_side_b),
-        [shape(2, 2 * block, side)] * 2 + [shape(wide, rest, side)] * 2,
+        (flags, from_side_a, from_side_b),
+        [shape(2, 2 * block, side)] * 2,
     )
     from_corner_a, from_corner_b = exchange(corner_a, corner_b, "px")
-    from_rest_a, from_rest_b = exchange(rest_a, rest_b, "px")
-    residual_low, residual_high, message_a, message_b, partial, current = call(
+    rest_side_a, rest_side_b = call(
+        columns_kernel,
+        (flags, rest_a, rest_b, from_rest_a, from_rest_b),
+        [shape(4, rest, side)] * 2,
+    )
+    rest_side_a, rest_side_b = exchange(rest_side_a, rest_side_b, "py")
+    residual_a, residual_b, partial, current = call(
         residual_kernel,
         (
             codes,
@@ -441,39 +442,46 @@
             stiff_tiles,
             mass_tiles,
         ),
-        [shape(count_y, block, side)] * 2
-        + [shape(3, block, side), shape(2, block, side)]
+        [shape(count_y + 1, block, side), shape(count_y, block, side)]
         + [shape(block, prior), shape(4 * wide, block, side)],
         [pltpu.VMEM((4 * wide, 2 * block, 2 * side), BF16)]
         + [pltpu.VMEM((kinds, 2 * side, side), BF16)] * 2,
         smem=1,
-    )
-    from_side_a, from_side_b = exchange(message_a, message_b, "py")
-    partial = total_along(partial + from_side_a[-1], "py", 2)
-    partial, from_rest_a, from_rest_b = lax.optimization_barrier(
-        (partial, from_rest_a, from_rest_b)
-    )
-    row_a, row_b = call(
-        residual_rows_kernel,
-        (flags, residual_low, residual_high, from_side_a, from_side_b),
-        [shape(wide, block, side)] * 2,
-    )
-    from_row_a, from_row_b = exchange(row_a, row_b, "px")
-    partial = total_along(partial, "px")
+        cost=pl.CostEstimate(flops=10**9, bytes_accessed=0, transcendentals=0),
+    )
+    count_py = lax.axis_size("py")
+    from_row_a, from_row_b = exchange(residual_a, residual_b, "px")
+    partial = total_over(
+        partial + from_row_a[-1], 2 * count_py, count_py * lax.axis_size("px")
+    )
+    partial, rest_side_a, rest_side_b = lax.optimization_barrier(
+        (partial, rest_side_a, rest_side_b)
+    )
+    side_a, side_b = call(
+        columns_kernel,
+        (flags, residual_a, residual_b, from_row_a, from_row_b, partial),
+        [shape(5, block, side), shape(4, block, side)],
+    )
+    from_side_a, from_side_b = exchange(side_a, side_b, "py")
+    partial = total_over(partial + from_side_a[-1], 2, count_py)
     weighted_low, weighted_high, coupling, sums = call(
         functools.partial(operators_kernel, inverse_rows),
         (
             codes,
             flags,
             partial,
-            row_a,
-            row_b,
+            residual_a,
+            residual_b,
             from_row_a,
             from_row_b,
+            from_side_a,
+            from_side_b,
             rest_a,
             rest_b,
             from_rest_a,
             from_rest_b,
+            rest_side_a,
+            rest_side_b,
             current,
             stiff_tiles,
             mass_tiles,

time: 63.2 us -> 61.5 us (0.973)
  starting transfers between devices: 36.5 us -> 32.4 us
  waiting for transfers between devices: 14.3 us -> 15.9 us
    ppermute x21 -> x22, starting transfers between devices: 36.5 us -> 32.4 us  [the longest x7 15.9 us: exchange(): lax.ppermute(message_a, axis, near)]
    ppermute x21 -> x22, waiting for transfers between devices: 14.3 us -> 15.9 us  [the longest x8 15.3 us: swap(): return lax.ppermute(value, axes, pairs)]
    pallas_call x6 -> x7, Pallas kernels: 9.6 us -> 9.6 us  [call(): pl.pallas_call(kernel, out_shape=outputs, in_specs=specs, out_specs=[VMEM...]
  transfers between devices with their start and end apart: 21 -> 22, of which waited for: 10 -> 10; matrix products, arithmetic and copies ran while one was open for 1% -> 1% of each run, Pallas kernels for 5% -> 5%
where the time goes in v8:
time: 61.5 us; the launch traced here: 61.1 us
  starting transfers between devices  32.4 us (53%)
  waiting for transfers between devices  15.9 us (26%)
  Pallas kernels  9.6 us (16%)
  other arithmetic  1.43 us (2%)
  local copies, waits for them, and re-layouts  0.96 us (2%)
  between operations  0.89 us (1%)
    ppermute x7, starting transfers between devices, exchange(): lax.ppermute(message_a, axis, near)  15.9 us
    ppermute x8, waiting for transfers between devices, swap(): return lax.ppermute(value, axes, pairs)  15.3 us
    ppermute x8, starting transfers between devices, swap(): return lax.ppermute(value, axes, pairs)  11.7 us
    pallas_call x7, Pallas kernels, call(): pl.pallas_call(kernel, out_shape=outputs, in_specs=specs, out_specs=[VMEM...  9.6 us
    ppermute x7, starting transfers between devices, exchange(): lax.ppermute(message_b, axis, pairs)  4.72 us
  transfers between devices with their start and end apart: 22, of which 10 were waited for; matrix products, arithmetic and copies ran while one was open for 1% of the time, Pallas kernels for 5%

profile of v8, /device:TPU:0, one launch (start us, length us, event | category | flops | bytes accessed | tf_op | source)
XLA Modules:
  0.0 61.1 jit_solution(8924132534692452301)
XLA Ops:
  0.7 0.1 stack.38
  0.8 1.2 %pad_maximum_fusion.vectors_ref = f32[1280,128]{1,0:T(8,128)S(1)} fusion(f32[256,128]{1,0:T(8,128)} %bitcast.22, f32[1024,128]{1,0:T(8,128)} %bitcast.21), kind=kLoop, calls=%fused_computation | loop fusion | flops 163840 | bytes 1310720 | tf_op jit(solution)/shard_map/concatenate | solution.py:379
  2.0 0.0 copy-start
  2.0 0.1 broadcast_in_dim.2.flags_ref
  2.1 0.1 shard_map.93
  2.2 0.5 collective-permute-start
  2.7 0.8 %collective-permute-start.3 = (f32[2,64,128]{2,1,0:T(8,128)S(1)}, f32[2,64,128]{2,1,0:T(8,128)S(1)}, u32[]{:S(2)}, u32[]{:S(2)}) collective-permute-start(f32[2,64,128]{2,1,0:T(8,128)S(1)} %get-tuple-element.37), channel_id=1, source_target_pairs={{0,0},{1,2},{2,1},{3,3},{4,4},{5,6},{6,5},{7,7},{8,8},{9,10},{10,9... | collective-permute-start | bytes 196616 | tf_op jit(solution)/shard_map/ppermute | solution.py:343
  3.5 2.5 %collective-permute-start.1 = (f32[4,64,128]{2,1,0:T(8,128)S(1)}, f32[4,64,128]{2,1,0:T(8,128)S(1)}, u32[]{:S(2)}, u32[]{:S(2)}) collective-permute-start(f32[4,64,128]{2,1,0:T(8,128)S(1)} %get-tuple-element.34.row_a_ref), channel_id=1, source_target_pairs={{0,4},{4,0},{8,12},{12,8},{1,5},{5,1},{9,13},{13,9},{2,6},{6,2},{1... | collective-permute-start | bytes 393224 | tf_op jit(solution)/shard_map/ppermute | solution.py:343
  6.1 0.7 %collective-permute-start.2 = (f32[4,64,128]{2,1,0:T(8,128)S(1)}, f32[4,64,128]{2,1,0:T(8,128)S(1)}, u32[]{:S(2)}, u32[]{:S(2)}) collective-permute-start(f32[4,64,128]{2,1,0:T(8,128)S(1)} %get-tuple-element.35.row_b_ref), channel_id=1, source_target_pairs={{0,0},{4,8},{8,4},{12,12},{1,1},{5,9},{9,5},{13,13},{2,2},{6,10},{... | collective-permute-start | bytes 393224 | tf_op jit(solution)/shard_map/ppermute | solution.py:343
  6.7 0.1 iota_add_fusion
  6.8 0.1 fusion.2
  6.9 0.1 copy.10
  7.0 0.6 copy-done.3
  7.6 0.1 copy.11
  7.7 0.0 collective-permute-done.3.side_b_ref.from_side_b_ref
  7.7 4.5 %collective-permute-start.4 = (f32[2,64,128]{2,1,0:T(8,128)S(1)}, f32[2,64,128]{2,1,0:T(8,128)S(1)}, u32[]{:S(2)}, u32[]{:S(2)}) collective-permute-start(f32[2,64,128]{2,1,0:T(8,128)S(1)} %get-tuple-element.38), channel_id=1, source_target_pairs={{0,4},{4,0},{8,12},{12,8},{1,5},{5,1},{9,13},{13,9},{2,6},{6,2},{1... | collective-permute-start | bytes 196616 | tf_op jit(solution)/shard_map/ppermute | solution.py:343
  12.1 0.7 %collective-permute-start.5 = (f32[2,64,128]{2,1,0:T(8,128)S(1)}, f32[2,64,128]{2,1,0:T(8,128)S(1)}, u32[]{:S(2)}, u32[]{:S(2)}) collective-permute-start(f32[2,64,128]{2,1,0:T(8,128)S(1)} %get-tuple-element.39), channel_id=1, source_target_pairs={{0,0},{4,8},{8,4},{12,12},{1,1},{5,9},{9,5},{13,13},{2,2},{6,10},{... | collective-permute-start | bytes 196616 | tf_op jit(solution)/shard_map/ppermute | solution.py:343
  12.8 1.3 %collective-permute-start.8 = (f32[4,96,128]{2,1,0:T(8,128)S(1)}, f32[4,96,128]{2,1,0:T(8,128)S(1)}, u32[]{:S(2)}, u32[]{:S(2)}) collective-permute-start(f32[4,96,128]{2,1,0:T(8,128)S(1)} %get-tuple-element.40.rest_a_ref.row_a_ref), channel_id=1, source_target_pairs={{0,4},{4,0},{8,12},{12,8},{1,5},{5,1},{9,13},{13,9},{2,6},{6,2},{1... | collective-permute-start | bytes 589832 | tf_op jit(solution)/shard_map/ppermute | solution.py:343
  14.2 0.2 collective-permute-done.4.from_corner_a_ref
  14.4 0.7 %collective-permute-start.9 = (f32[4,96,128]{2,1,0:T(8,128)S(1)}, f32[4,96,128]{2,1,0:T(8,128)S(1)}, u32[]{:S(2)}, u32[]{:S(2)}) collective-permute-start(f32[4,96,128]{2,1,0:T(8,128)S(1)} %get-tuple-element.41.rest_b_ref.row_b_ref), channel_id=1, source_target_pairs={{0,0},{4,8},{8,4},{12,12},{1,1},{5,9},{9,5},{13,13},{2,2},{6,10},{... | collective-permute-start | bytes 589832 | tf_op jit(solution)/shard_map/ppermute | solution.py:343
  15.1 0.0 collective-permute-done.5.from_corner_b_ref
  15.1 0.0 collective-permute-done.2.from_row_b_ref
  15.1 3.1 %shard_map.95 = (f32[5,32,128]{2,1,0:T(8,128)S(1)}, f32[4,32,128]{2,1,0:T(8,128)S(1)}, f32[32,128]{1,0:T(8,128)S(1)}, f32[24,32,128]{2,1,0:T(8,128)S(1)}) custom-call(s32[2,5,8]{2,1,0:T(8,128)S(1)} %pad_add_fusion.codes_ref, f32[8,128]{1,0:T(8,128)S(1)} %broadcast_in_dim.2.flags_ref, f32[4,64,128]{2,1,0:T(8,128)S(1)} %get-tuple-element.34.row_a_ref, ...), custom_call_target="tpu_custom_call" | custom-call | flops 1000000000 | tf_op jit(solution)/shard_map/pallas_call | solution.py:394
  18.2 3.3 %collective-permute-start.6 = (f32[5,32,128]{2,1,0:T(8,128)S(1)}, f32[5,32,128]{2,1,0:T(8,128)S(1)}, u32[]{:S(2)}, u32[]{:S(2)}) collective-permute-start(f32[5,32,128]{2,1,0:T(8,128)S(1)} %get-tuple-element.43.row_a_ref), channel_id=1, source_target_pairs={{0,4},{4,0},{8,12},{12,8},{1,5},{5,1},{9,13},{13,9},{2,6},{6,2},{1... | collective-permute-start | bytes 245768 | tf_op jit(solution)/shard_map/ppermute | solution.py:343
  21.5 0.7 %collective-permute-start.12 = (f32[4,32,128]{2,1,0:T(8,128)S(1)}, f32[4,32,128]{2,1,0:T(8,128)S(1)}, u32[]{:S(2)}, u32[]{:S(2)}) collective-permute-start(f32[4,32,128]{2,1,0:T(8,128)S(1)} %get-tuple-element.47.row_b_ref), channel_id=1, source_target_pairs={{0,0},{4,8},{8,4},{12,12},{1,1},{5,9},{9,5},{13,13},{2,2},{6,10},{... | collective-permute-start | bytes 196616 | tf_op jit(solution)/shard_map/ppermute | solution.py:343
  22.2 0.0 collective-permute-done.8.from_row_a_ref.from_rest_a_ref
  22.2 1.3 %collective-permute-start.10 = (f32[4,96,128]{2,1,0:T(8,128)S(1)}, f32[4,96,128]{2,1,0:T(8,128)S(1)}, u32[]{:S(2)}, u32[]{:S(2)}) collective-permute-start(f32[4,96,128]{2,1,0:T(8,128)S(1)} %get-tuple-element.44), channel_id=1, source_target_pairs={{0,1},{1,0},{2,3},{3,2},{4,5},{5,4},{6,7},{7,6},{8,9},{9,8},{10,11... | collective-permute-start | bytes 589832 | tf_op jit(solution)/shard_map/ppermute | solution.py:343
  23.5 0.7 %collective-permute-start.11 = (f32[4,96,128]{2,1,0:T(8,128)S(1)}, f32[4,96,128]{2,1,0:T(8,128)S(1)}, u32[]{:S(2)}, u32[]{:S(2)}) collective-permute-start(f32[4,96,128]{2,1,0:T(8,128)S(1)} %get-tuple-element.45), channel_id=1, source_target_pairs={{0,0},{1,2},{2,1},{3,3},{4,4},{5,6},{6,5},{7,7},{8,8},{9,10},{10,9... | collective-permute-start | bytes 589832 | tf_op jit(solution)/shard_map/ppermute | solution.py:343
  24.2 3.8 %collective-permute-start.7 = (f32[32,128]{1,0:T(8,128)S(1)}, f32[32,128]{1,0:T(8,128)S(1)}, u32[]{:S(2)}, u32[]{:S(2)}) collective-permute-start(f32[32,128]{1,0:T(8,128)S(1)} %fusion.1), channel_id=1, source_target_pairs={{0,8},{1,9},{2,10},{3,11},{4,12},{5,13},{6,14},{7,15},{8,0},{9,1},... | collective-permute-start | bytes 49160 | tf_op jit(solution)/shard_map/ppermute | solution.py:335
  28.0 1.7 %collective-permute-done.7 = f32[32,128]{1,0:T(8,128)S(1)} collective-permute-done((f32[32,128]{1,0:T(8,128)S(1)}, f32[32,128]{1,0:T(8,128)S(1)}, u32[]{:S(2)}, u32[]{:S(2)}) %collective-permute-start.7) | collective-permute-done | bytes 16416 | tf_op jit(solution)/shard_map/ppermute | solution.py:335
  29.8 2.5 %collective-permute-start.13 = (f32[5,32,128]{2,1,0:T(8,128)S(1)}, f32[5,32,128]{2,1,0:T(8,128)S(1)}, u32[]{:S(2)}, u32[]{:S(2)}) collective-permute-start(f32[5,32,128]{2,1,0:T(8,128)S(1)} %get-tuple-element.48), channel_id=1, source_target_pairs={{0,1},{1,0},{2,3},{3,2},{4,5},{5,4},{6,7},{7,6},{8,9},{9,8},{10,11... | collective-permute-start | bytes 245768 | tf_op jit(solution)/shard_map/ppermute | solution.py:343
  32.3 0.7 %collective-permute-start.15 = (f32[4,32,128]{2,1,0:T(8,128)S(1)}, f32[4,32,128]{2,1,0:T(8,128)S(1)}, u32[]{:S(2)}, u32[]{:S(2)}) collective-permute-start(f32[4,32,128]{2,1,0:T(8,128)S(1)} %get-tuple-element.49), channel_id=1, source_target_pairs={{0,0},{1,2},{2,1},{3,3},{4,4},{5,6},{6,5},{7,7},{8,8},{9,10},{10,9... | collective-permute-start | bytes 196616 | tf_op jit(solution)/shard_map/ppermute | solution.py:343
  33.0 0.3 collective-permute-done.13.from_side_a_ref
  33.2 2.7 %collective-permute-start.14 = (f32[32,128]{1,0:T(8,128)S(1)}, f32[32,128]{1,0:T(8,128)S(1)}, u32[]{:S(2)}, u32[]{:S(2)}) collective-permute-start(f32[32,128]{1,0:T(8,128)S(1)} %fusion), channel_id=1, source_target_pairs={{0,2},{1,3},{2,0},{3,1},{4,6},{5,7},{6,4},{7,5},{8,10},{9,11},{10,... | collective-permute-start | bytes 49160 | tf_op jit(solution)/shard_map/ppermute | solution.py:335
  35.9 2.3 %collective-permute-done.14 = f32[32,128]{1,0:T(8,128)S(1)} collective-permute-done((f32[32,128]{1,0:T(8,128)S(1)}, f32[32,128]{1,0:T(8,128)S(1)}, u32[]{:S(2)}, u32[]{:S(2)}) %collective-permute-start.14) | collective-permute-done | bytes 16416 | tf_op jit(solution)/shard_map/ppermute | solution.py:335
  38.3 3.7 %shard_map.98 = (f32[4,32,128]{2,1,0:T(8,128)S(1)}, f32[4,32,128]{2,1,0:T(8,128)S(1)}, f32[32,128]{1,0:T(8,128)}, f32[96,128]{1,0:T(8,128)S(1)}) custom-call(s32[2,5,8]{2,1,0:T(8,128)S(1)} %pad_add_fusion.codes_ref, f32[8,128]{1,0:T(8,128)S(1)} %broadcast_in_dim.2.flags_ref, f32[32,128]{1,0:T(8,128)S(1)} %add.82.partial_ref, ...), custom_call_target="tpu_custom_call" | custom-call | tf_op jit(solution)/shard_map/pallas_call | solution.py:394
  42.0 0.1 collective-permute-start.16
  42.1 1.1 %collective-permute-done.16 = f32[48,128]{1,0:T(8,128)S(1)} collective-permute-done((f32[48,128]{1,0:T(8,128)S(1)}, f32[48,128]{1,0:T(8,128)S(1)}, u32[]{:S(2)}, u32[]{:S(2)}) %collective-permute-start.16) | collective-permute-done | bytes 24608 | tf_op jit(solution)/shard_map/ppermute | solution.py:335
  43.2 3.2 %collective-permute-start.19 = (f32[48,128]{1,0:T(8,128)S(1)}, f32[48,128]{1,0:T(8,128)S(1)}, u32[]{:S(2)}, u32[]{:S(2)}) collective-permute-start(f32[48,128]{1,0:T(8,128)S(1)} %select_add_fusion), channel_id=1, source_target_pairs={{0,4},{1,5},{2,6},{3,7},{4,0},{5,1},{6,2},{7,3},{8,12},{9,13},{10,... | collective-permute-start | bytes 73736 | tf_op jit(solution)/shard_map/ppermute | solution.py:335
  46.4 1.4 %collective-permute-start.18 = (f32[48,128]{1,0:T(8,128)S(1)}, f32[48,128]{1,0:T(8,128)S(1)}, u32[]{:S(2)}, u32[]{:S(2)}) collective-permute-start(f32[48,128]{1,0:T(8,128)S(1)} %select_add_fusion), channel_id=1, source_target_pairs={{0,2},{1,3},{2,0},{3,1},{4,6},{5,7},{6,4},{7,5},{8,10},{9,11},{10,... | collective-permute-start | bytes 73736 | tf_op jit(solution)/shard_map/ppermute | solution.py:335
  47.8 0.1 collective-permute-start.17
  47.9 0.3 collective-permute-done.19
  48.2 2.0 %collective-permute-done.18 = f32[48,128]{1,0:T(8,128)S(1)} collective-permute-done((f32[48,128]{1,0:T(8,128)S(1)}, f32[48,128]{1,0:T(8,128)S(1)}, u32[]{:S(2)}, u32[]{:S(2)}) %collective-permute-start.18) | collective-permute-done | bytes 24608 | tf_op jit(solution)/shard_map/ppermute | solution.py:335
  50.2 2.3 %collective-permute-done.17 = f32[48,128]{1,0:T(8,128)S(1)} collective-permute-done((f32[48,128]{1,0:T(8,128)S(1)}, f32[48,128]{1,0:T(8,128)S(1)}, u32[]{:S(2)}, u32[]{:S(2)}) %collective-permute-start.17) | collective-permute-done | bytes 24608 | tf_op jit(solution)/shard_map/ppermute | solution.py:335
  52.5 0.4 collective-permute-start.20
  52.9 4.4 %collective-permute-done.20 = f32[48,128]{1,0:T(8,128)S(1)} collective-permute-done((f32[48,128]{1,0:T(8,128)S(1)}, f32[48,128]{1,0:T(8,128)S(1)}, u32[]{:S(2)}, u32[]{:S(2)}) %collective-permute-start.20) | collective-permute-done | bytes 24608 | tf_op jit(solution)/shard_map/ppermute | solution.py:335
  57.3 1.2 %collective-permute-done.21 = f32[48,128]{1,0:T(8,128)S(1)} collective-permute-done((f32[48,128]{1,0:T(8,128)S(1)}, f32[48,128]{1,0:T(8,128)S(1)}, u32[]{:S(2)}, u32[]{:S(2)}) %collective-permute-start.21) | collective-permute-done | bytes 24608 | tf_op jit(solution)/shard_map/ppermute | solution.py:335
  58.5 2.6 %shard_map.99 = (f32[256,128]{1,0:T(8,128)}, f32[32,32]{1,0:T(8,128)}, f32[2,32,160]{2,1,0:T(8,128)}) custom-call(f32[96,128]{1,0:T(8,128)S(1)} %pad_maximum_fusion.1.sums_ref, f32[4,32,128]{2,1,0:T(8,128)S(1)} %get-tuple-element.54.weighted_low_ref, f32[4,32,128]{2,1,0:T(8,128)S(1)} %get-tuple-element.55.weighted_high_ref), custom_call_target="tpu_custom_call" | custom-call | tf_op jit(solution)/shard_map/pallas_call | solution.py:394
  (31 shorter events, 0.2 us)
Async XLA Ops:
  0.8 14.3 %copy-start.1 = (f32[8,128,128]{2,1,0:T(8,128)S(1)}, f32[8,128,128]{2,1,0:T(8,128)}, u32[]{:S(2)}) copy-start(f32[8,128,128]{2,1,0:T(8,128)} %mass_ref.3) | copy-start | bytes 1572868
  2.0 13.1 %copy-start = (f32[8,128,128]{2,1,0:T(8,128)S(1)}, f32[8,128,128]{2,1,0:T(8,128)}, u32[]{:S(2)}) copy-start(f32[8,128,128]{2,1,0:T(8,128)} %stiff_ref.3) | copy-start | bytes 1572868
  2.2 5.5 %collective-permute-start = (f32[2,64,128]{2,1,0:T(8,128)S(1)}, f32[2,64,128]{2,1,0:T(8,128)S(1)}, u32[]{:S(2)}, u32[]{:S(2)}) collective-permute-start(f32[2,64,128]{2,1,0:T(8,128)S(1)} %get-tuple-element.32), channel_id=1, source_target_pairs={{0,1},{1,0},{2,3},{3,2},{4,5},{5,4},{6,7},{7,6},{8,9},{9,8},{10,11... | collective-permute-start | bytes 196616 | tf_op jit(solution)/shard_map/ppermute | solution.py:343
  2.7 4.1 %copy-start.2 = (s32[5,2,4]{0,2,1:T(4,128)S(1)}, s32[5,2,4]{0,2,1:T(4,128)}, u32[]{:S(2)}) copy-start(s32[5,2,4]{0,2,1:T(4,128)} %param.8) | copy-start | bytes 484
  2.7 4.9 %collective-permute-start.3 = (f32[2,64,128]{2,1,0:T(8,128)S(1)}, f32[2,64,128]{2,1,0:T(8,128)S(1)}, u32[]{:S(2)}, u32[]{:S(2)}) collective-permute-start(f32[2,64,128]{2,1,0:T(8,128)S(1)} %get-tuple-element.37), channel_id=1, source_target_pairs={{0,0},{1,2},{2,1},{3,3},{4,4},{5,6},{6,5},{7,7},{8,8},{9,10},{10,9... | collective-permute-start | bytes 196616 | tf_op jit(solution)/shard_map/ppermute | solution.py:343
  3.5 11.6 %collective-permute-start.1 = (f32[4,64,128]{2,1,0:T(8,128)S(1)}, f32[4,64,128]{2,1,0:T(8,128)S(1)}, u32[]{:S(2)}, u32[]{:S(2)}) collective-permute-start(f32[4,64,128]{2,1,0:T(8,128)S(1)} %get-tuple-element.34.row_a_ref), channel_id=1, source_target_pairs={{0,4},{4,0},{8,12},{12,8},{1,5},{5,1},{9,13},{13,9},{2,6},{6,2},{1... | collective-permute-start | bytes 393224 | tf_op jit(solution)/shard_map/ppermute | solution.py:343
  6.1 9.0 %collective-permute-start.2 = (f32[4,64,128]{2,1,0:T(8,128)S(1)}, f32[4,64,128]{2,1,0:T(8,128)S(1)}, u32[]{:S(2)}, u32[]{:S(2)}) collective-permute-start(f32[4,64,128]{2,1,0:T(8,128)S(1)} %get-tuple-element.35.row_b_ref), channel_id=1, source_target_pairs={{0,0},{4,8},{8,4},{12,12},{1,1},{5,9},{9,5},{13,13},{2,2},{6,10},{... | collective-permute-start | bytes 393224 | tf_op jit(solution)/shard_map/ppermute | solution.py:343
  6.9 0.7 %copy-start.3 = (s32[5,2,4]{0,2,1:T(4,128)S(1)}, s32[5,2,4]{0,2,1:T(4,128)}, u32[]{:S(2)}) copy-start(s32[5,2,4]{0,2,1:T(4,128)} %param.9) | copy-start | bytes 484
  7.7 6.7 %collective-permute-start.4 = (f32[2,64,128]{2,1,0:T(8,128)S(1)}, f32[2,64,128]{2,1,0:T(8,128)S(1)}, u32[]{:S(2)}, u32[]{:S(2)}) collective-permute-start(f32[2,64,128]{2,1,0:T(8,128)S(1)} %get-tuple-element.38), channel_id=1, source_target_pairs={{0,4},{4,0},{8,12},{12,8},{1,5},{5,1},{9,13},{13,9},{2,6},{6,2},{1... | collective-permute-start | bytes 196616 | tf_op jit(solution)/shard_map/ppermute | solution.py:343
  12.1 2.9 %collective-permute-start.5 = (f32[2,64,128]{2,1,0:T(8,128)S(1)}, f32[2,64,128]{2,1,0:T(8,128)S(1)}, u32[]{:S(2)}, u32[]{:S(2)}) collective-permute-start(f32[2,64,128]{2,1,0:T(8,128)S(1)} %get-tuple-element.39), channel_id=1, source_target_pairs={{0,0},{4,8},{8,4},{12,12},{1,1},{5,9},{9,5},{13,13},{2,2},{6,10},{... | collective-permute-start | bytes 196616 | tf_op jit(solution)/shard_map/ppermute | solution.py:343
  12.8 9.4 %collective-permute-start.8 = (f32[4,96,128]{2,1,0:T(8,128)S(1)}, f32[4,96,128]{2,1,0:T(8,128)S(1)}, u32[]{:S(2)}, u32[]{:S(2)}) collective-permute-start(f32[4,96,128]{2,1,0:T(8,128)S(1)} %get-tuple-element.40.rest_a_ref.row_a_ref), channel_id=1, source_target_pairs={{0,4},{4,0},{8,12},{12,8},{1,5},{5,1},{9,13},{13,9},{2,6},{6,2},{1... | collective-permute-start | bytes 589832 | tf_op jit(solution)/shard_map/ppermute | solution.py:343
  14.4 7.8 %collective-permute-start.9 = (f32[4,96,128]{2,1,0:T(8,128)S(1)}, f32[4,96,128]{2,1,0:T(8,128)S(1)}, u32[]{:S(2)}, u32[]{:S(2)}) collective-permute-start(f32[4,96,128]{2,1,0:T(8,128)S(1)} %get-tuple-element.41.rest_b_ref.row_b_ref), channel_id=1, source_target_pairs={{0,0},{4,8},{8,4},{12,12},{1,1},{5,9},{9,5},{13,13},{2,2},{6,10},{... | collective-permute-start | bytes 589832 | tf_op jit(solution)/shard_map/ppermute | solution.py:343
  18.2 6.0 %collective-permute-start.6 = (f32[5,32,128]{2,1,0:T(8,128)S(1)}, f32[5,32,128]{2,1,0:T(8,128)S(1)}, u32[]{:S(2)}, u32[]{:S(2)}) collective-permute-start(f32[5,32,128]{2,1,0:T(8,128)S(1)} %get-tuple-element.43.row_a_ref), channel_id=1, source_target_pairs={{0,4},{4,0},{8,12},{12,8},{1,5},{5,1},{9,13},{13,9},{2,6},{6,2},{1... | collective-permute-start | bytes 245768 | tf_op jit(solution)/shard_map/ppermute | solution.py:343
  21.5 8.3 %collective-permute-start.12 = (f32[4,32,128]{2,1,0:T(8,128)S(1)}, f32[4,32,128]{2,1,0:T(8,128)S(1)}, u32[]{:S(2)}, u32[]{:S(2)}) collective-permute-start(f32[4,32,128]{2,1,0:T(8,128)S(1)} %get-tuple-element.47.row_b_ref), channel_id=1, source_target_pairs={{0,0},{4,8},{8,4},{12,12},{1,1},{5,9},{9,5},{13,13},{2,2},{6,10},{... | collective-permute-start | bytes 196616 | tf_op jit(solution)/shard_map/ppermute | solution.py:343
  22.2 7.5 %collective-permute-start.10 = (f32[4,96,128]{2,1,0:T(8,128)S(1)}, f32[4,96,128]{2,1,0:T(8,128)S(1)}, u32[]{:S(2)}, u32[]{:S(2)}) collective-permute-start(f32[4,96,128]{2,1,0:T(8,128)S(1)} %get-tuple-element.44), channel_id=1, source_target_pairs={{0,1},{1,0},{2,3},{3,2},{4,5},{5,4},{6,7},{7,6},{8,9},{9,8},{10,11... | collective-permute-start | bytes 589832 | tf_op jit(solution)/shard_map/ppermute | solution.py:343
  23.5 6.2 %collective-permute-start.11 = (f32[4,96,128]{2,1,0:T(8,128)S(1)}, f32[4,96,128]{2,1,0:T(8,128)S(1)}, u32[]{:S(2)}, u32[]{:S(2)}) collective-permute-start(f32[4,96,128]{2,1,0:T(8,128)S(1)} %get-tuple-element.45), channel_id=1, source_target_pairs={{0,0},{1,2},{2,1},{3,3},{4,4},{5,6},{6,5},{7,7},{8,8},{9,10},{10,9... | collective-permute-start | bytes 589832 | tf_op jit(solution)/shard_map/ppermute | solution.py:343
  24.2 5.5 %collective-permute-start.7 = (f32[32,128]{1,0:T(8,128)S(1)}, f32[32,128]{1,0:T(8,128)S(1)}, u32[]{:S(2)}, u32[]{:S(2)}) collective-permute-start(f32[32,128]{1,0:T(8,128)S(1)} %fusion.1), channel_id=1, source_target_pairs={{0,8},{1,9},{2,10},{3,11},{4,12},{5,13},{6,14},{7,15},{8,0},{9,1},... | collective-permute-start | bytes 49160 | tf_op jit(solution)/shard_map/ppermute | solution.py:335
  29.8 3.4 %collective-permute-start.13 = (f32[5,32,128]{2,1,0:T(8,128)S(1)}, f32[5,32,128]{2,1,0:T(8,128)S(1)}, u32[]{:S(2)}, u32[]{:S(2)}) collective-permute-start(f32[5,32,128]{2,1,0:T(8,128)S(1)} %get-tuple-element.48), channel_id=1, source_target_pairs={{0,1},{1,0},{2,3},{3,2},{4,5},{5,4},{6,7},{7,6},{8,9},{9,8},{10,11... | collective-permute-start | bytes 245768 | tf_op jit(solution)/shard_map/ppermute | solution.py:343
  32.3 6.0 %collective-permute-start.15 = (f32[4,32,128]{2,1,0:T(8,128)S(1)}, f32[4,32,128]{2,1,0:T(8,128)S(1)}, u32[]{:S(2)}, u32[]{:S(2)}) collective-permute-start(f32[4,32,128]{2,1,0:T(8,128)S(1)} %get-tuple-element.49), channel_id=1, source_target_pairs={{0,0},{1,2},{2,1},{3,3},{4,4},{5,6},{6,5},{7,7},{8,8},{9,10},{10,9... | collective-permute-start | bytes 196616 | tf_op jit(solution)/shard_map/ppermute | solution.py:343
  33.2 5.0 %collective-permute-start.14 = (f32[32,128]{1,0:T(8,128)S(1)}, f32[32,128]{1,0:T(8,128)S(1)}, u32[]{:S(2)}, u32[]{:S(2)}) collective-permute-start(f32[32,128]{1,0:T(8,128)S(1)} %fusion), channel_id=1, source_target_pairs={{0,2},{1,3},{2,0},{3,1},{4,6},{5,7},{6,4},{7,5},{8,10},{9,11},{10,... | collective-permute-start | bytes 49160 | tf_op jit(solution)/shard_map/ppermute | solution.py:335
  42.0 1.2 %collective-permute-start.16 = (f32[48,128]{1,0:T(8,128)S(1)}, f32[48,128]{1,0:T(8,128)S(1)}, u32[]{:S(2)}, u32[]{:S(2)}) collective-permute-start(f32[48,128]{1,0:T(8,128)S(1)} %slice_select_fusion), channel_id=1, source_target_pairs={{0,1},{1,0},{2,3},{3,2},{4,5},{5,4},{6,7},{7,6},{8,9},{9,8},{10,11... | collective-permute-start | bytes 73736 | tf_op jit(solution)/shard_map/ppermute | solution.py:335
  43.2 5.0 %collective-permute-start.19 = (f32[48,128]{1,0:T(8,128)S(1)}, f32[48,128]{1,0:T(8,128)S(1)}, u32[]{:S(2)}, u32[]{:S(2)}) collective-permute-start(f32[48,128]{1,0:T(8,128)S(1)} %select_add_fusion), channel_id=1, source_target_pairs={{0,4},{1,5},{2,6},{3,7},{4,0},{5,1},{6,2},{7,3},{8,12},{9,13},{10,... | collective-permute-start | bytes 73736 | tf_op jit(solution)/shard_map/ppermute | solution.py:335
  46.4 3.8 %collective-permute-start.18 = (f32[48,128]{1,0:T(8,128)S(1)}, f32[48,128]{1,0:T(8,128)S(1)}, u32[]{:S(2)}, u32[]{:S(2)}) collective-permute-start(f32[48,128]{1,0:T(8,128)S(1)} %select_add_fusion), channel_id=1, source_target_pairs={{0,2},{1,3},{2,0},{3,1},{4,6},{5,7},{6,4},{7,5},{8,10},{9,11},{10,... | collective-permute-start | bytes 73736 | tf_op jit(solution)/shard_map/ppermute | solution.py:335
  47.8 4.7 %collective-permute-start.17 = (f32[48,128]{1,0:T(8,128)S(1)}, f32[48,128]{1,0:T(8,128)S(1)}, u32[]{:S(2)}, u32[]{:S(2)}) collective-permute-start(f32[48,128]{1,0:T(8,128)S(1)} %select_add_fusion), channel_id=1, source_target_pairs={{0,6},{1,7},{2,4},{3,5},{4,2},{5,3},{6,0},{7,1},{8,14},{9,15},{10,... | collective-permute-start | bytes 73736 | tf_op jit(solution)/shard_map/ppermute | solution.py:335
  52.5 4.8 %collective-permute-start.20 = (f32[48,128]{1,0:T(8,128)S(1)}, f32[48,128]{1,0:T(8,128)S(1)}, u32[]{:S(2)}, u32[]{:S(2)}) collective-permute-start(f32[48,128]{1,0:T(8,128)S(1)} %add_add_fusion), channel_id=1, source_target_pairs={{0,8},{1,9},{2,10},{3,11},{4,12},{5,13},{6,14},{7,15},{8,0},{9,1},... | collective-permute-start | bytes 73736 | tf_op jit(solution)/shard_map/ppermute | solution.py:335
  57.3 1.2 %collective-permute-start.21 = (f32[48,128]{1,0:T(8,128)S(1)}, f32[48,128]{1,0:T(8,128)S(1)}, u32[]{:S(2)}, u32[]{:S(2)}) collective-permute-start(f32[48,128]{1,0:T(8,128)S(1)} %add.87), channel_id=1, source_target_pairs={{0,1},{1,0},{2,3},{3,2},{4,5},{5,4},{6,7},{7,6},{8,9},{9,8},{10,11... | collective-permute-start | bytes 73736 | tf_op jit(solution)/shard_map/ppermute | solution.py:335

commit v9 on v8

--- a/solution.py
+++ b/solution.py
@@ -10,7 +10,7 @@
 F32 = jnp.float32
 BF16 = jnp.bfloat16
 VMEM = pl.BlockSpec(memory_space=pltpu.VMEM)
-SMEM = pl.BlockSpec(memory_space=pltpu.SMEM)
+ANY = pl.BlockSpec(memory_space=pl.ANY)
 MIB = 1024 * 1024
 
 
@@ -59,32 +59,43 @@
     return flags_ref[place : place + 1, :]
 
 
-def pack_kernel(
-    flags_ref,
-    vectors_ref,
-    side_a_ref,
-    side_b_ref,
-    row_a_ref,
-    row_b_ref,
-    rest_a_ref,
-    rest_b_ref,
-):
+def code_copies(code_refs, local_refs, semaphores):
+    return [
+        pltpu.make_async_copy(ref, local, semaphores.at[n])
+        for n, (ref, local) in enumerate(zip(code_refs, local_refs))
+    ]
+
+
+def source_and_kind(neighbours_ref, kinds_ref, tile, k, count_y):
+    neighbour = neighbours_ref[tile, k]
+    down = (neighbour * 11) >> 5
+    first = (tile // count_y) * (count_y + 2) + tile % count_y
+    return first + neighbour + down * (count_y - 1), kinds_ref[tile, k]
+
+
+def pack_kernel(flags_ref, block_ref, side_a_ref, side_b_ref, row_a_ref, row_b_ref):
     count_y, both, _ = row_a_ref.shape
-    rest = rest_a_ref.shape[1]
     tiles = 2 * count_y
     odd_y, odd_x = flag_at(flags_ref, 0), flag_at(flags_ref, 1)
 
-    def block_tile(i, j):
-        return vectors_ref[pl.ds(rest * tiles + i * count_y + j, both, stride=tiles), :]
-
-    def rest_tile(i, j):
-        return vectors_ref[pl.ds(i * count_y + j, rest, stride=tiles), :]
+    def tile_of(i, j):
+        return block_ref[pl.ds(i * count_y + j, both, stride=tiles), :]
 
     for i in range(2):
-        side_a_ref[i], side_b_ref[i] = pick(odd_y, block_tile(i, 0), block_tile(i, count_y - 1))
+        side_a_ref[i], side_b_ref[i] = pick(odd_y, tile_of(i, 0), tile_of(i, count_y - 1))
     for j in range(count_y):
-        row_a_ref[j], row_b_ref[j] = pick(odd_x, block_tile(0, j), block_tile(1, j))
-        rest_a_ref[j], rest_b_ref[j] = pick(odd_x, rest_tile(0, j), rest_tile(1, j))
+        row_a_ref[j], row_b_ref[j] = pick(odd_x, tile_of(0, j), tile_of(1, j))
+
+
+def rest_kernel(flags_ref, basis_ref, rest_a_ref, rest_b_ref):
+    count_y, rest, _ = rest_a_ref.shape
+    odd_x = flag_at(flags_ref, 1)
+    for j in range(count_y):
+        rest_a_ref[j], rest_b_ref[j] = pick(
+            odd_x,
+            basis_ref[pl.ds(j, rest, stride=2 * count_y), :],
+            basis_ref[pl.ds(count_y + j, rest, stride=2 * count_y), :],
+        )
 
 
 def corners_kernel(flags_ref, side_a_ref, side_b_ref, corner_a_ref, corner_b_ref):
@@ -111,7 +122,8 @@
 
 
 def residual_kernel(
-    codes_ref,
+    neighbours_hbm_ref,
+    kinds_hbm_ref,
     flags_ref,
     row_a_ref,
     row_b_ref,
@@ -132,7 +144,15 @@
     ext_ref,
     table_high_ref,
     table_low_ref,
+    neighbours_ref,
+    kinds_ref,
+    semaphores,
 ):
+    copies = code_copies(
+        (neighbours_hbm_ref, kinds_hbm_ref), (neighbours_ref, kinds_ref), semaphores
+    )
+    for copy in copies:
+        copy.start()
     split_tables(stiff_ref, mass_ref, table_high_ref, table_low_ref, 1)
     count_y, both, side = row_a_ref.shape
     wide = count_y + 2
@@ -165,14 +185,16 @@
         low, high = pick(odd_x, from_corner_a_ref[place], from_corner_b_ref[place])
         store(0, j, low * (in_low_x * inside))
         store(3, j, high * (in_high_x * inside))
+    for copy in copies:
+        copy.wait()
     partial = jnp.zeros((block, rest + block), F32)
     totals = {}
     for tile in range(2 * count_y):
         i, j = tile // count_y, tile % count_y
         total = 4.0 * own[i, j][:block] + own[i, j][block:]
-        for k in range(codes_ref.shape[1]):
-            kind = codes_ref[1, k, tile]
-            chosen = ext_ref[codes_ref[0, k, tile]]
+        for k in range(neighbours_ref.shape[1]):
+            source, kind = source_and_kind(neighbours_ref, kinds_ref, tile, k, count_y)
+            chosen = ext_ref[source]
             pair = mul(chosen, table_high_ref[kind])
             total = total + (
                 pair[:block] + (pair[block:] + mul(chosen[:block], table_low_ref[kind]))
@@ -187,9 +209,37 @@
     partial_ref[...] = partial
 
 
+def prepare_kernel(
+    flags_ref,
+    rest_a_ref,
+    rest_b_ref,
+    from_rest_a_ref,
+    from_rest_b_ref,
+    current_ref,
+    stiff_ref,
+    mass_ref,
+    basis_ref,
+    table_high_ref,
+    table_low_ref,
+):
+    count_y, rest, _ = rest_a_ref.shape
+    prior = rest + current_ref.shape[1]
+    odd_x = flag_at(flags_ref, 1)
+    split_tables(stiff_ref, mass_ref, table_high_ref, table_low_ref, 2)
+    for j in range(count_y):
+        rests = list(pick(odd_x, from_rest_a_ref[j], from_rest_b_ref[j]))
+        rests[1:1] = pick(odd_x, rest_a_ref[j], rest_b_ref[j])
+        for i in range(4):
+            tile = jnp.concatenate([rests[i], current_ref[i * (count_y + 2) + j + 1]], axis=0)
+            high, low = split(tile)
+            basis_ref[i * count_y + j, :prior, :] = high
+            basis_ref[i * count_y + j, prior:, :] = low
+
+
 def operators_kernel(
     inverse_rows,
-    codes_ref,
+    neighbours_hbm_ref,
+    kinds_hbm_ref,
     flags_ref,
     partial_ref,
     row_a_ref,
@@ -198,28 +248,30 @@
     from_row_b_ref,
     from_side_a_ref,
     from_side_b_ref,
-    rest_a_ref,
-    rest_b_ref,
-    from_rest_a_ref,
-    from_rest_b_ref,
     rest_side_a_ref,
     rest_side_b_ref,
     current_ref,
-    stiff_ref,
-    mass_ref,
+    basis_ref,
+    table_high_ref,
+    table_low_ref,
     weighted_low_ref,
     weighted_high_ref,
     coupling_ref,
-    sums_ref,
+    sent_ref,
+    kept_ref,
     ext_ref,
-    basis_ref,
-    table_high_ref,
-    table_low_ref,
+    neighbours_ref,
+    kinds_ref,
+    semaphores,
 ):
-    split_tables(stiff_ref, mass_ref, table_high_ref, table_low_ref, 2)
+    copies = code_copies(
+        (neighbours_hbm_ref, kinds_hbm_ref), (neighbours_ref, kinds_ref), semaphores
+    )
+    for copy in copies:
+        copy.start()
     count_y, block, side = weighted_low_ref.shape
     wide = count_y + 2
-    rest = rest_a_ref.shape[1]
+    rest = rest_side_a_ref.shape[1]
     prior = rest + block
     odd_y, odd_x, in_low_y, in_high_y, in_low_x, in_high_x = (
         flag_at(flags_ref, place) for place in range(6)
@@ -227,20 +279,25 @@
     coupling = partial_ref[...] * inverse_rows
     coupling_ref[...] = coupling
     coupling_high, coupling_low = split(coupling)
+
+    def basis_parts(i, j):
+        if 0 < j < wide - 1:
+            place = i * count_y + j - 1
+            return basis_ref[place, :prior, :], basis_ref[place, prior:, :]
+        rest_tile = pick(odd_y, rest_side_a_ref[i], rest_side_b_ref[i])[j // (wide - 1)]
+        return split(jnp.concatenate([rest_tile, current_ref[i * wide + j]], axis=0))
 
     for j in range(wide):
         if 0 < j < wide - 1:
             rows = list(pick(odd_x, from_row_a_ref[j - 1], from_row_b_ref[j - 1]))
             rows[1:1] = pick(odd_x, row_a_ref[j - 1], row_b_ref[j - 1])
-            rests = list(pick(odd_x, from_rest_a_ref[j - 1], from_rest_b_ref[j - 1]))
-            rests[1:1] = pick(odd_x, rest_a_ref[j - 1], rest_b_ref[j - 1])
         else:
-            high = j // (wide - 1)
-            rows = [pick(odd_y, from_side_a_ref[i], from_side_b_ref[i])[high] for i in range(4)]
-            rests = [pick(odd_y, rest_side_a_ref[i], rest_side_b_ref[i])[high] for i in range(4)]
+            rows = [
+                pick(odd_y, from_side_a_ref[i], from_side_b_ref[i])[j // (wide - 1)]
+                for i in range(4)
+            ]
         for i in range(4):
-            tile = jnp.concatenate([rests[i], current_ref[i * wide + j]], axis=0)
-            high, low = split(tile)
+            high, low = basis_parts(i, j)
             value = rows[i] - (
                 mul(coupling_high, high) + (mul(coupling_high, low) + mul(coupling_low, high))
             )
@@ -254,35 +311,52 @@
                 value = value * in_high_y
             if 0 < i < 3 and 0 < j < wide - 1:
                 (weighted_low_ref, weighted_high_ref)[i - 1][j - 1] = value
-                place = (i - 1) * count_y + j - 1
-                basis_ref[place, :prior, :] = high
-                basis_ref[place, prior:, :] = low
             high, low = split(value)
             ext_ref[i * wide + j, :block, :] = high
             ext_ref[i * wide + j, block:, :] = low
+    for copy in copies:
+        copy.wait()
     with_basis = jnp.zeros((2 * block, prior), F32)
     with_own = jnp.zeros((block, 4 * block), F32)
     for tile in range(2 * count_y):
         i, j = tile // count_y, tile % count_y
         own = (weighted_low_ref, weighted_high_ref)[i][j]
         totals = jnp.concatenate([4.0 * own, own], axis=1)
-        for k in range(codes_ref.shape[1]):
-            kind = codes_ref[1, k, tile]
-            chosen = ext_ref[codes_ref[0, k, tile]]
+        for k in range(neighbours_ref.shape[1]):
+            source, kind = source_and_kind(neighbours_ref, kinds_ref, tile, k, count_y)
+            chosen = ext_ref[source]
             pair = mul(chosen, table_high_ref[kind])
             totals = totals + (
                 pair[:block] + (pair[block:] + mul(chosen[:block], table_low_ref[kind]))
             )
         applied = jnp.concatenate([totals[:, :side], totals[:, side:]], axis=0)
         high, low = split(applied)
-        basis_high, basis_low = basis_ref[tile, :prior, :], basis_ref[tile, prior:, :]
+        basis_high, basis_low = basis_parts(i + 1, j + 1)
         with_basis = with_basis + (
             mul_t(high, basis_high) + (mul_t(high, basis_low) + mul_t(low, basis_high))
         )
         right = jnp.concatenate([applied, own, jnp.zeros_like(own)], axis=0)
         with_own = with_own + mul3_t(own, right)
-    sums_ref[: 2 * block, :] = with_basis
-    sums_ref[2 * block :, :] = with_own
+    halves = [
+        jnp.concatenate(
+            [
+                with_basis[part * block : (part + 1) * block],
+                folded(with_own[:, part * block : (part + 1) * block]),
+                folded(with_own[:, 2 * block : 3 * block]),
+            ],
+            axis=0,
+        )
+        for part in range(2)
+    ]
+    sent_ref[...], kept_ref[...] = pick(odd_y, halves[0], halves[1])
+
+
+def folded(square):
+    return jnp.concatenate([square[n * 8 : (n + 1) * 8] for n in range(4)], axis=1)
+
+
+def unfolded(rows):
+    return jnp.concatenate([rows[:, n * 32 : (n + 1) * 32] for n in range(4)], axis=0)
 
 
 def factor_kernel(
@@ -292,13 +366,13 @@
     weighted_high_ref,
     new_ref,
     factor_ref,
+    inverse_ref,
     reduced_ref,
 ):
     count_y, block, _ = weighted_low_ref.shape
     prior = sums_ref.shape[1]
     tiles = 2 * count_y
-    with_own = sums_ref[2 * block :, :] * inverse_rows
-    gram = with_own[:, 2 * block : 3 * block]
+    gram = unfolded(sums_ref[block + 8 :, :]) * inverse_rows
     row_ids = lax.broadcasted_iota(jnp.int32, (block, block), 0)
     column_ids = lax.broadcasted_iota(jnp.int32, (block, block), 1)
     unit = jnp.where(row_ids == column_ids, 1.0, 0.0).astype(F32)
@@ -323,10 +397,25 @@
     for tile in range(tiles):
         own = (weighted_low_ref, weighted_high_ref)[tile // count_y][tile % count_y]
         new_ref[pl.ds(tile, block, stride=tiles), :] = mul3(inverse, own)
-    for part in range(2):
-        span = slice(part * block, (part + 1) * block)
-        reduced_ref[part, :, :prior] = mul3(inverse, sums_ref[span, :] * inverse_rows)
-        reduced_ref[part, :, prior:] = mul3_t(mul3_t(inverse, with_own[:, span]), inverse)
+    inverse_ref[...] = inverse
+    reduce_half(inverse, sums_ref, inverse_rows, reduced_ref)
+
+
+def reduce_half(inverse, sums_ref, inverse_rows, out_ref):
+    block, prior = inverse.shape[0], sums_ref.shape[1]
+    out_ref[:, :prior] = mul3(inverse, sums_ref[:block, :] * inverse_rows)
+    own = unfolded(sums_ref[block : block + 8, :]) * inverse_rows
+    out_ref[:, prior:] = mul3_t(mul3_t(inverse, own), inverse)
+
+
+def reduced_kernel(inverse_rows, flags_ref, inverse_ref, other_ref, half_ref, out_ref, work_ref):
+    reduce_half(inverse_ref[...], other_ref, inverse_rows, work_ref)
+    odd_y = flag_at(flags_ref, 0)
+    for span in (slice(0, 128), slice(128, out_ref.shape[2])):
+        flag = odd_y[:, : work_ref[:, span].shape[1]]
+        out_ref[0, :, span], out_ref[1, :, span] = pick(
+            flag, work_ref[:, span], half_ref[:, span]
+        )
 
 
 def swap(value, mask):
@@ -350,18 +439,10 @@
     return value
 
 
-def halved_total(value):
-    half = value.shape[0] // 2
-    upper = lax.axis_index("py") % 2 == 1
-    first, second = value[:half], value[half:]
-    kept = jnp.where(upper, second, first)
-    kept = kept + swap(jnp.where(upper, first, second), 1)
+def half_total(sent, kept):
+    kept = kept + swap(sent, 1)
     kept = (kept + swap(kept, 6)) + (swap(kept, 2) + swap(kept, 4))
-    kept = total_over(kept, 8, lax.axis_size(("px", "py")))
-    other = swap(kept, 1)
-    return jnp.concatenate(
-        [jnp.where(upper, other, kept), jnp.where(upper, kept, other)], axis=0
-    )
+    return total_over(kept, 8, lax.axis_size(("px", "py")))
 
 
 def shape(*dims, dtype=F32):
@@ -376,21 +457,19 @@
     rest = prior - block
     kinds = stiff_tiles.shape[0]
     inverse_rows = 1.0 / (tiles * side * lax.axis_size("px") * lax.axis_size("py"))
-    vectors = jnp.concatenate(
-        [prior_basis.reshape(-1, side), previous.reshape(-1, side)], axis=0
-    )
-    place = jnp.arange(count_x)[:, None] * wide + jnp.arange(count_y)[None, :]
-    sources = place[None] + (neighbours // 3) * wide + neighbours % 3
-    codes = jnp.stack([sources, tile_kinds]).astype(jnp.int32).reshape(2, -1, tiles)
+    basis = prior_basis.reshape(-1, side)
+    block_vectors = jnp.concatenate([basis[rest * tiles :], previous.reshape(-1, side)], axis=0)
+    codes = [array.transpose(1, 2, 0).reshape(tiles, -1) for array in (neighbours, tile_kinds)]
+    code_scratch = [pltpu.SMEM(array.shape, jnp.int32) for array in codes]
+    code_scratch += [pltpu.SemaphoreType.DMA((2,))]
     at_y, at_x = lax.axis_index("py"), lax.axis_index("px")
-    flags = [at_y % 2 == 1, at_x % 2 == 1]
-    flags += [at_y > 0, at_y < lax.axis_size("py") - 1]
-    flags += [at_x > 0, at_x < lax.axis_size("px") - 1]
-    flags = jnp.stack(flags + flags[:2]).astype(F32)
-    flags = jnp.broadcast_to(flags[:, None], (8, side))
-
-    def call(kernel, inputs, outputs, scratch=(), smem=0, limit=8, cost=None):
-        specs = [SMEM] * smem + [VMEM] * (len(inputs) - smem)
+    bits = (at_y & 1) + 2 * (at_x & 1)
+    bits += 4 * (at_y > 0) + 8 * (at_y < lax.axis_size("py") - 1)
+    bits += 16 * (at_x > 0) + 32 * (at_x < lax.axis_size("px") - 1)
+    flags = ((bits >> lax.broadcasted_iota(jnp.int32, (8, side), 0)) & 1).astype(F32)
+
+    def call(kernel, inputs, outputs, scratch=(), plain=0, limit=8, cost=None):
+        specs = [ANY] * plain + [VMEM] * (len(inputs) - plain)
         return pl.pallas_call(
             kernel,
             out_shape=outputs,
@@ -401,17 +480,16 @@
             cost_estimate=cost,
         )(*inputs)
 
-    side_a, side_b, row_a, row_b, rest_a, rest_b = call(
+    side_a, side_b, row_a, row_b = call(
         pack_kernel,
-        (flags, vectors),
-        [shape(count_x, 2 * block, side)] * 2
-        + [shape(count_y, 2 * block, side)] * 2
-        + [shape(count_y, rest, side)] * 2,
-    )
+        (flags, block_vectors),
+        [shape(count_x, 2 * block, side)] * 2 + [shape(count_y, 2 * block, side)] * 2,
+    )
+    rest_a, rest_b = call(rest_kernel, (flags, basis), [shape(count_y, rest, side)] * 2)
     from_side_a, from_side_b = exchange(side_a, side_b, "py")
     from_row_a, from_row_b = exchange(row_a, row_b, "px")
+    from_side_a, rest_a, rest_b = lax.optimization_barrier((from_side_a, rest_a, rest_b))
     from_rest_a, from_rest_b = exchange(rest_a, rest_b, "px")
-    from_side_a, codes = lax.optimization_barrier((from_side_a, codes))
     corner_a, corner_b = call(
         corners_kernel,
         (flags, from_side_a, from_side_b),
@@ -427,7 +505,7 @@
     residual_a, residual_b, partial, current = call(
         residual_kernel,
         (
-            codes,
+            *codes,
             flags,
             row_a,
             row_b,
@@ -445,8 +523,9 @@
         [shape(count_y + 1, block, side), shape(count_y, block, side)]
         + [shape(block, prior), shape(4 * wide, block, side)],
         [pltpu.VMEM((4 * wide, 2 * block, 2 * side), BF16)]
-        + [pltpu.VMEM((kinds, 2 * side, side), BF16)] * 2,
-        smem=1,
+        + [pltpu.VMEM((kinds, 2 * side, side), BF16)] * 2
+        + code_scratch,
+        plain=2,
         cost=pl.CostEstimate(flops=10**9, bytes_accessed=0, transcendentals=0),
     )
     count_py = lax.axis_size("py")
@@ -464,10 +543,17 @@
     )
     from_side_a, from_side_b = exchange(side_a, side_b, "py")
     partial = total_over(partial + from_side_a[-1], 2, count_py)
-    weighted_low, weighted_high, coupling, sums = call(
+    basis_parts, wide_high, wide_low = call(
+        prepare_kernel,
+        (flags, rest_a, rest_b, from_rest_a, from_rest_b, current, stiff_tiles, mass_tiles),
+        [shape(4 * count_y, 2 * prior, side, dtype=BF16)]
+        + [shape(kinds, side, 2 * side, dtype=BF16)] * 2,
+        cost=pl.CostEstimate(flops=10**9, bytes_accessed=0, transcendentals=0),
+    )
+    weighted_low, weighted_high, coupling, sent, kept = call(
         functools.partial(operators_kernel, inverse_rows),
         (
-            codes,
+            *codes,
             flags,
             partial,
             residual_a,
@@ -476,32 +562,37 @@
             from_row_b,
             from_side_a,
             from_side_b,
-            rest_a,
-            rest_b,
-            from_rest_a,
-            from_rest_b,
             rest_side_a,
             rest_side_b,
             current,
-            stiff_tiles,
-            mass_tiles,
+            basis_parts,
+            wide_high,
+            wide_low,
         ),
-        [shape(count_y, block, side)] * 2 + [shape(block, prior), shape(3 * block, prior)],
-        [
-            pltpu.VMEM((4 * wide, 2 * block, side), BF16),
-            pltpu.VMEM((tiles, 2 * prior, side), BF16),
-        ]
-        + [pltpu.VMEM((kinds, side, 2 * side), BF16)] * 2,
-        smem=1,
-    )
-    new_block, factor, reduced = call(
+        [shape(count_y, block, side)] * 2
+        + [shape(block, prior)]
+        + [shape(block + 16, prior)] * 2,
+        [pltpu.VMEM((4 * wide, 2 * block, side), BF16)] + code_scratch,
+        plain=2,
+    )
+    kept = half_total(sent, kept)
+    other = swap(kept[: block + 8], 1)
+    new_block, factor, inverse, half = call(
         functools.partial(factor_kernel, inverse_rows),
-        (halved_total(sums), weighted_low, weighted_high),
+        (kept, weighted_low, weighted_high),
         [
             shape(block * tiles, side),
             shape(block, block),
-            shape(2, block, prior + block),
+            shape(block, block),
+            shape(block, prior + block),
         ],
+        cost=pl.CostEstimate(flops=10**9, bytes_accessed=0, transcendentals=0),
+    )
+    (reduced,) = call(
+        functools.partial(reduced_kernel, inverse_rows),
+        (flags, inverse, other, half),
+        [shape(2, block, prior + block)],
+        [pltpu.VMEM((block, prior + block), F32)],
     )
     return (
         new_block.reshape(previous.shape),

time: 61.5 us -> 59.3 us (0.964)
  waiting for transfers between devices: 15.9 us -> 13.5 us
    ppermute x8, waiting for transfers between devices: 15.3 us -> 13 us  [swap(): return lax.ppermute(value, axes, pairs)]
    slice x0 -> x3, local copies, waits for them, and re-layouts: none -> 0.9 us  [the longest x2 0.89 us: shards(): basis[rest * tiles:]]
    pallas_call x7 -> x10, Pallas kernels: 9.6 us -> 10.1 us  [call(): pl.pallas_call(kernel, out_shape=outputs, in_specs=specs, out_specs=[VMEM...]
  transfers between devices with their start and end apart: 22 -> 22, of which waited for: 10 -> 9; matrix products, arithmetic and copies ran while one was open for 1% -> 0% of each run, Pallas kernels for 5% -> 9%
where the time goes in v9:
time: 59.3 us; the launch traced here: 59 us
  starting transfers between devices  32.4 us (55%)
  waiting for transfers between devices  13.5 us (23%)
  Pallas kernels  10.1 us (17%)
  other arithmetic  1.02 us (2%)
  local copies, waits for them, and re-layouts  0.99 us (2%)
  between operations  0.97 us (2%)
    ppermute x7, starting transfers between devices, exchange(): lax.ppermute(message_a, axis, near)  16.1 us
    ppermute x8, waiting for transfers between devices, swap(): return lax.ppermute(value, axes, pairs)  13 us
    ppermute x8, starting transfers between devices, swap(): return lax.ppermute(value, axes, pairs)  11.7 us
    pallas_call x10, Pallas kernels, call(): pl.pallas_call(kernel, out_shape=outputs, in_specs=specs, out_specs=[VMEM...  10.1 us
    ppermute x7, starting transfers between devices, exchange(): lax.ppermute(message_b, axis, pairs)  4.59 us
  transfers between devices with their start and end apart: 22, of which 9 were waited for; matrix products, arithmetic and copies ran while one was open for 0% of the time, Pallas kernels for 9%

profile of v9, /device:TPU:0, one launch (start us, length us, event | category | flops | bytes accessed | tf_op | source)
XLA Modules:
  0.0 59.0 jit_solution(6580944954877859700)
XLA Ops:
  0.7 0.0 slice-start
  0.7 0.9 %slice-done = f32[32,2,4,128]{3,2,1,0:T(4,128)S(1)} async-done(((f32[128,2,4,128]{3,2,1,0:T(4,128)}), f32[32,2,4,128]{3,2,1,0:T(4,128)S(1)}, s32[]{:S(2)}) %slice-start) | async-done | bytes 131096 | tf_op jit(solution)/shard_map/slice | solution.py:461
  1.6 1.0 %pad_maximum_fusion.block_ref = f32[512,128]{1,0:T(8,128)S(1)} fusion(f32[256,128]{1,0:T(8,128)} %bitcast.26, f32[256,128]{1,0:T(8,128)S(1)} %bitcast.21), kind=kLoop, calls=%fused_computation | loop fusion | flops 65536 | bytes 524288 | tf_op jit(solution)/shard_map/concatenate | solution.py:461
  2.6 0.0 copy-start.3
  2.6 0.1 iota.7.flags_ref
  2.6 0.1 shard_map.93
  2.7 0.5 collective-permute-start.2
  3.2 0.7 %collective-permute-start.3 = (f32[2,64,128]{2,1,0:T(8,128)S(1)}, f32[2,64,128]{2,1,0:T(8,128)S(1)}, u32[]{:S(2)}, u32[]{:S(2)}) collective-permute-start(f32[2,64,128]{2,1,0:T(8,128)S(1)} %get-tuple-element.44), channel_id=1, source_target_pairs={{0,0},{1,2},{2,1},{3,3},{4,4},{5,6},{6,5},{7,7},{8,8},{9,10},{10,9... | collective-permute-start | bytes 196616 | tf_op jit(solution)/shard_map/ppermute | solution.py:432
  3.9 2.7 %collective-permute-start = (f32[4,64,128]{2,1,0:T(8,128)S(1)}, f32[4,64,128]{2,1,0:T(8,128)S(1)}, u32[]{:S(2)}, u32[]{:S(2)}) collective-permute-start(f32[4,64,128]{2,1,0:T(8,128)S(1)} %get-tuple-element.38.row_a_ref), channel_id=1, source_target_pairs={{0,4},{4,0},{8,12},{12,8},{1,5},{5,1},{9,13},{13,9},{2,6},{6,2},{1... | collective-permute-start | bytes 393224 | tf_op jit(solution)/shard_map/ppermute | solution.py:432
  6.5 0.7 %collective-permute-start.1 = (f32[4,64,128]{2,1,0:T(8,128)S(1)}, f32[4,64,128]{2,1,0:T(8,128)S(1)}, u32[]{:S(2)}, u32[]{:S(2)}) collective-permute-start(f32[4,64,128]{2,1,0:T(8,128)S(1)} %get-tuple-element.39.row_b_ref), channel_id=1, source_target_pairs={{0,0},{4,8},{8,4},{12,12},{1,1},{5,9},{9,5},{13,13},{2,2},{6,10},{... | collective-permute-start | bytes 393224 | tf_op jit(solution)/shard_map/ppermute | solution.py:432
  7.2 0.1 shard_map.94
  7.3 0.0 collective-permute-done.3.side_b_ref.from_side_b_ref
  7.3 0.0 copy-start.2
  7.3 0.0 copy-start.1
  7.4 4.5 %collective-permute-start.4 = (f32[2,64,128]{2,1,0:T(8,128)S(1)}, f32[2,64,128]{2,1,0:T(8,128)S(1)}, u32[]{:S(2)}, u32[]{:S(2)}) collective-permute-start(f32[2,64,128]{2,1,0:T(8,128)S(1)} %get-tuple-element.45), channel_id=1, source_target_pairs={{0,4},{4,0},{8,12},{12,8},{1,5},{5,1},{9,13},{13,9},{2,6},{6,2},{1... | collective-permute-start | bytes 196616 | tf_op jit(solution)/shard_map/ppermute | solution.py:432
  11.8 0.7 %collective-permute-start.5 = (f32[2,64,128]{2,1,0:T(8,128)S(1)}, f32[2,64,128]{2,1,0:T(8,128)S(1)}, u32[]{:S(2)}, u32[]{:S(2)}) collective-permute-start(f32[2,64,128]{2,1,0:T(8,128)S(1)} %get-tuple-element.46), channel_id=1, source_target_pairs={{0,0},{4,8},{8,4},{12,12},{1,1},{5,9},{9,5},{13,13},{2,2},{6,10},{... | collective-permute-start | bytes 196616 | tf_op jit(solution)/shard_map/ppermute | solution.py:432
  12.5 1.3 %collective-permute-start.8 = (f32[4,96,128]{2,1,0:T(8,128)S(1)}, f32[4,96,128]{2,1,0:T(8,128)S(1)}, u32[]{:S(2)}, u32[]{:S(2)}) collective-permute-start(f32[4,96,128]{2,1,0:T(8,128)S(1)} %get-tuple-element.47.rest_a_ref.row_a_ref), channel_id=1, source_target_pairs={{0,4},{4,0},{8,12},{12,8},{1,5},{5,1},{9,13},{13,9},{2,6},{6,2},{1... | collective-permute-start | bytes 589832 | tf_op jit(solution)/shard_map/ppermute | solution.py:432
  13.8 0.2 collective-permute-done.4.from_corner_a_ref
  14.1 0.7 %collective-permute-start.9 = (f32[4,96,128]{2,1,0:T(8,128)S(1)}, f32[4,96,128]{2,1,0:T(8,128)S(1)}, u32[]{:S(2)}, u32[]{:S(2)}) collective-permute-start(f32[4,96,128]{2,1,0:T(8,128)S(1)} %get-tuple-element.48.rest_b_ref.row_b_ref), channel_id=1, source_target_pairs={{0,0},{4,8},{8,4},{12,12},{1,1},{5,9},{9,5},{13,13},{2,2},{6,10},{... | collective-permute-start | bytes 589832 | tf_op jit(solution)/shard_map/ppermute | solution.py:432
  14.8 0.0 collective-permute-done.1.from_row_b_ref
  14.8 2.8 %shard_map.96 = (f32[5,32,128]{2,1,0:T(8,128)S(1)}, f32[4,32,128]{2,1,0:T(8,128)S(1)}, f32[32,128]{1,0:T(8,128)S(1)}, f32[24,32,128]{2,1,0:T(8,128)S(1)}) custom-call(s32[8,5]{1,0:T(8,128)S(1)} %bitcast.22, s32[8,5]{1,0:T(8,128)S(1)} %bitcast.24, f32[8,128]{1,0:T(8,128)S(1)} %iota.7.flags_ref, f32[4,64,128]{2,1,0:T(8,128)S(1)} %get-tuple-element.38.row_a_ref, ...), custom_call_target="tpu_custom_call" | custom-call | flops 1000000000 | tf_op jit(solution)/shard_map/pallas_call | solution.py:473
  17.7 3.3 %collective-permute-start.6 = (f32[5,32,128]{2,1,0:T(8,128)S(1)}, f32[5,32,128]{2,1,0:T(8,128)S(1)}, u32[]{:S(2)}, u32[]{:S(2)}) collective-permute-start(f32[5,32,128]{2,1,0:T(8,128)S(1)} %get-tuple-element.50.row_a_ref), channel_id=1, source_target_pairs={{0,4},{4,0},{8,12},{12,8},{1,5},{5,1},{9,13},{13,9},{2,6},{6,2},{1... | collective-permute-start | bytes 245768 | tf_op jit(solution)/shard_map/ppermute | solution.py:432
  21.0 0.7 %collective-permute-start.12 = (f32[4,32,128]{2,1,0:T(8,128)S(1)}, f32[4,32,128]{2,1,0:T(8,128)S(1)}, u32[]{:S(2)}, u32[]{:S(2)}) collective-permute-start(f32[4,32,128]{2,1,0:T(8,128)S(1)} %get-tuple-element.54.row_b_ref), channel_id=1, source_target_pairs={{0,0},{4,8},{8,4},{12,12},{1,1},{5,9},{9,5},{13,13},{2,2},{6,10},{... | collective-permute-start | bytes 196616 | tf_op jit(solution)/shard_map/ppermute | solution.py:432
  21.7 0.0 collective-permute-done.8.from_row_a_ref.from_rest_a_ref
  21.7 1.3 %collective-permute-start.10 = (f32[4,96,128]{2,1,0:T(8,128)S(1)}, f32[4,96,128]{2,1,0:T(8,128)S(1)}, u32[]{:S(2)}, u32[]{:S(2)}) collective-permute-start(f32[4,96,128]{2,1,0:T(8,128)S(1)} %get-tuple-element.51), channel_id=1, source_target_pairs={{0,1},{1,0},{2,3},{3,2},{4,5},{5,4},{6,7},{7,6},{8,9},{9,8},{10,11... | collective-permute-start | bytes 589832 | tf_op jit(solution)/shard_map/ppermute | solution.py:432
  23.1 0.7 %collective-permute-start.11 = (f32[4,96,128]{2,1,0:T(8,128)S(1)}, f32[4,96,128]{2,1,0:T(8,128)S(1)}, u32[]{:S(2)}, u32[]{:S(2)}) collective-permute-start(f32[4,96,128]{2,1,0:T(8,128)S(1)} %get-tuple-element.52), channel_id=1, source_target_pairs={{0,0},{1,2},{2,1},{3,3},{4,4},{5,6},{6,5},{7,7},{8,8},{9,10},{10,9... | collective-permute-start | bytes 589832 | tf_op jit(solution)/shard_map/ppermute | solution.py:432
  23.7 3.7 %collective-permute-start.7 = (f32[32,128]{1,0:T(8,128)S(1)}, f32[32,128]{1,0:T(8,128)S(1)}, u32[]{:S(2)}, u32[]{:S(2)}) collective-permute-start(f32[32,128]{1,0:T(8,128)S(1)} %fusion.1), channel_id=1, source_target_pairs={{0,8},{1,9},{2,10},{3,11},{4,12},{5,13},{6,14},{7,15},{8,0},{9,1},... | collective-permute-start | bytes 49160 | tf_op jit(solution)/shard_map/ppermute | solution.py:424
  27.5 1.7 %collective-permute-done.7 = f32[32,128]{1,0:T(8,128)S(1)} collective-permute-done((f32[32,128]{1,0:T(8,128)S(1)}, f32[32,128]{1,0:T(8,128)S(1)}, u32[]{:S(2)}, u32[]{:S(2)}) %collective-permute-start.7) | collective-permute-done | bytes 16416 | tf_op jit(solution)/shard_map/ppermute | solution.py:424
  29.2 2.4 %collective-permute-start.13 = (f32[5,32,128]{2,1,0:T(8,128)S(1)}, f32[5,32,128]{2,1,0:T(8,128)S(1)}, u32[]{:S(2)}, u32[]{:S(2)}) collective-permute-start(f32[5,32,128]{2,1,0:T(8,128)S(1)} %get-tuple-element.55), channel_id=1, source_target_pairs={{0,1},{1,0},{2,3},{3,2},{4,5},{5,4},{6,7},{7,6},{8,9},{9,8},{10,11... | collective-permute-start | bytes 245768 | tf_op jit(solution)/shard_map/ppermute | solution.py:432
  31.7 0.7 %collective-permute-start.15 = (f32[4,32,128]{2,1,0:T(8,128)S(1)}, f32[4,32,128]{2,1,0:T(8,128)S(1)}, u32[]{:S(2)}, u32[]{:S(2)}) collective-permute-start(f32[4,32,128]{2,1,0:T(8,128)S(1)} %get-tuple-element.56), channel_id=1, source_target_pairs={{0,0},{1,2},{2,1},{3,3},{4,4},{5,6},{6,5},{7,7},{8,8},{9,10},{10,9... | collective-permute-start | bytes 196616 | tf_op jit(solution)/shard_map/ppermute | solution.py:432
  32.3 0.3 collective-permute-done.13.from_side_a_ref
  32.6 2.7 %collective-permute-start.14 = (f32[32,128]{1,0:T(8,128)S(1)}, f32[32,128]{1,0:T(8,128)S(1)}, u32[]{:S(2)}, u32[]{:S(2)}) collective-permute-start(f32[32,128]{1,0:T(8,128)S(1)} %fusion), channel_id=1, source_target_pairs={{0,2},{1,3},{2,0},{3,1},{4,6},{5,7},{6,4},{7,5},{8,10},{9,11},{10,... | collective-permute-start | bytes 49160 | tf_op jit(solution)/shard_map/ppermute | solution.py:424
  35.3 0.3 shard_map.99
  35.6 2.0 %collective-permute-done.14 = f32[32,128]{1,0:T(8,128)S(1)} collective-permute-done((f32[32,128]{1,0:T(8,128)S(1)}, f32[32,128]{1,0:T(8,128)S(1)}, u32[]{:S(2)}, u32[]{:S(2)}) %collective-permute-start.14) | collective-permute-done | bytes 16416 | tf_op jit(solution)/shard_map/ppermute | solution.py:424
  37.6 3.4 %shard_map.100 = (f32[4,32,128]{2,1,0:T(8,128)S(1)}, f32[4,32,128]{2,1,0:T(8,128)S(1)}, f32[32,128]{1,0:T(8,128)}, f32[48,128]{1,0:T(8,128)S(1)}, f32[48,128]{1,0:T(8,128)S(1)}) custom-call(s32[8,5]{1,0:T(8,128)S(1)} %bitcast.23, s32[8,5]{1,0:T(8,128)S(1)} %bitcast.25, f32[8,128]{1,0:T(8,128)S(1)} %iota.7.flags_ref, f32[32,128]{1,0:T(8,128)S(1)} %add.50.partial_ref, ...), custom_call_target="tpu_custom_call" | custom-call | tf_op jit(solution)/shard_map/pallas_call | solution.py:473
  41.0 0.2 collective-permute-start.16
  41.2 1.1 %collective-permute-done.16 = f32[48,128]{1,0:T(8,128)S(1)} collective-permute-done((f32[48,128]{1,0:T(8,128)S(1)}, f32[48,128]{1,0:T(8,128)S(1)}, u32[]{:S(2)}, u32[]{:S(2)}) %collective-permute-start.16) | collective-permute-done | bytes 24608 | tf_op jit(solution)/shard_map/ppermute | solution.py:424
  42.3 4.1 %collective-permute-start.17 = (f32[48,128]{1,0:T(8,128)S(1)}, f32[48,128]{1,0:T(8,128)S(1)}, u32[]{:S(2)}, u32[]{:S(2)}) collective-permute-start(f32[48,128]{1,0:T(8,128)S(1)} %add.51), channel_id=1, source_target_pairs={{0,6},{1,7},{2,4},{3,5},{4,2},{5,3},{6,0},{7,1},{8,14},{9,15},{10,... | collective-permute-start | bytes 73736 | tf_op jit(solution)/shard_map/ppermute | solution.py:424
  46.4 0.6 %collective-permute-start.18 = (f32[48,128]{1,0:T(8,128)S(1)}, f32[48,128]{1,0:T(8,128)S(1)}, u32[]{:S(2)}, u32[]{:S(2)}) collective-permute-start(f32[48,128]{1,0:T(8,128)S(1)} %add.51), channel_id=1, source_target_pairs={{0,2},{1,3},{2,0},{3,1},{4,6},{5,7},{6,4},{7,5},{8,10},{9,11},{10,... | collective-permute-start | bytes 73736 | tf_op jit(solution)/shard_map/ppermute | solution.py:424
  47.0 0.0 collective-permute-start.19
  47.0 1.2 %collective-permute-done.17 = f32[48,128]{1,0:T(8,128)S(1)} collective-permute-done((f32[48,128]{1,0:T(8,128)S(1)}, f32[48,128]{1,0:T(8,128)S(1)}, u32[]{:S(2)}, u32[]{:S(2)}) %collective-permute-start.17) | collective-permute-done | bytes 24608 | tf_op jit(solution)/shard_map/ppermute | solution.py:424
  48.2 2.0 %collective-permute-done.18 = f32[48,128]{1,0:T(8,128)S(1)} collective-permute-done((f32[48,128]{1,0:T(8,128)S(1)}, f32[48,128]{1,0:T(8,128)S(1)}, u32[]{:S(2)}, u32[]{:S(2)}) %collective-permute-start.18) | collective-permute-done | bytes 24608 | tf_op jit(solution)/shard_map/ppermute | solution.py:424
  50.2 0.6 %collective-permute-done.19 = f32[48,128]{1,0:T(8,128)S(1)} collective-permute-done((f32[48,128]{1,0:T(8,128)S(1)}, f32[48,128]{1,0:T(8,128)S(1)}, u32[]{:S(2)}, u32[]{:S(2)}) %collective-permute-start.19) | collective-permute-done | bytes 24608 | tf_op jit(solution)/shard_map/ppermute | solution.py:424
  50.8 0.3 collective-permute-start.20
  51.2 4.4 %collective-permute-done.20 = f32[48,128]{1,0:T(8,128)S(1)} collective-permute-done((f32[48,128]{1,0:T(8,128)S(1)}, f32[48,128]{1,0:T(8,128)S(1)}, u32[]{:S(2)}, u32[]{:S(2)}) %collective-permute-start.20) | collective-permute-done | bytes 24608 | tf_op jit(solution)/shard_map/ppermute | solution.py:424
  55.6 0.1 collective-permute-start.21
  55.7 2.3 %shard_map.101 = (f32[256,128]{1,0:T(8,128)}, f32[32,32]{1,0:T(8,128)}, f32[32,32]{1,0:T(8,128)S(1)}, f32[32,160]{1,0:T(8,128)S(1)}) custom-call(f32[48,128]{1,0:T(8,128)S(1)} %add.55.sums_ref, f32[4,32,128]{2,1,0:T(8,128)S(1)} %get-tuple-element.65.weighted_low_ref, f32[4,32,128]{2,1,0:T(8,128)S(1)} %get-tuple-element.66.weighted_high_ref), custom_call_target="tpu_custom_call" | custom-call | flops 1000000000 | tf_op jit(solution)/shard_map/pallas_call | solution.py:473
  58.0 1.0 %shard_map.102 = f32[2,32,160]{2,1,0:T(8,128)} custom-call(f32[8,128]{1,0:T(8,128)S(1)} %iota.7.flags_ref, f32[32,32]{1,0:T(8,128)S(1)} %get-tuple-element.70.inverse_ref, f32[40,128]{1,0:T(8,128)S(1)} %collective-permute-done.21.other_ref, f32[32,160]{1,0:T(8,128)S(1)} %get-tuple-element.71.half_ref), custom_call_target="tpu_custom_call" | custom-call | tf_op jit(solution)/shard_map/pallas_call | solution.py:473
  (29 shorter events, 0.2 us)
Async XLA Ops:
  0.7 0.9 %slice-start = ((f32[128,2,4,128]{3,2,1,0:T(4,128)}), f32[32,2,4,128]{3,2,1,0:T(4,128)S(1)}, s32[]{:S(2)}) async-start(f32[128,2,4,128]{3,2,1,0:T(4,128)} %param.6), calls=%async_computation | async-start | bytes 262144 | tf_op jit(solution)/shard_map/slice | solution.py:461
  0.7 6.5 %copy-start = (f32[128,2,4,128]{3,2,1,0:T(4,128)S(1)}, f32[128,2,4,128]{3,2,1,0:T(4,128)}, u32[]{:S(2)}) copy-start(f32[128,2,4,128]{3,2,1,0:T(4,128)} %param.6) | copy-start | bytes 1572868
  1.6 13.2 %copy-start.4 = (f32[8,128,128]{2,1,0:T(8,128)S(1)}, f32[8,128,128]{2,1,0:T(8,128)}, u32[]{:S(2)}) copy-start(f32[8,128,128]{2,1,0:T(8,128)} %mass_ref.3) | copy-start | bytes 1572868
  2.6 12.2 %copy-start.3 = (f32[8,128,128]{2,1,0:T(8,128)S(1)}, f32[8,128,128]{2,1,0:T(8,128)}, u32[]{:S(2)}) copy-start(f32[8,128,128]{2,1,0:T(8,128)} %stiff_ref.3) | copy-start | bytes 1572868
  2.7 4.6 %collective-permute-start.2 = (f32[2,64,128]{2,1,0:T(8,128)S(1)}, f32[2,64,128]{2,1,0:T(8,128)S(1)}, u32[]{:S(2)}, u32[]{:S(2)}) collective-permute-start(f32[2,64,128]{2,1,0:T(8,128)S(1)} %get-tuple-element.40), channel_id=1, source_target_pairs={{0,1},{1,0},{2,3},{3,2},{4,5},{5,4},{6,7},{7,6},{8,9},{9,8},{10,11... | collective-permute-start | bytes 196616 | tf_op jit(solution)/shard_map/ppermute | solution.py:432
  3.2 4.1 %collective-permute-start.3 = (f32[2,64,128]{2,1,0:T(8,128)S(1)}, f32[2,64,128]{2,1,0:T(8,128)S(1)}, u32[]{:S(2)}, u32[]{:S(2)}) collective-permute-start(f32[2,64,128]{2,1,0:T(8,128)S(1)} %get-tuple-element.44), channel_id=1, source_target_pairs={{0,0},{1,2},{2,1},{3,3},{4,4},{5,6},{6,5},{7,7},{8,8},{9,10},{10,9... | collective-permute-start | bytes 196616 | tf_op jit(solution)/shard_map/ppermute | solution.py:432
  3.9 10.9 %collective-permute-start = (f32[4,64,128]{2,1,0:T(8,128)S(1)}, f32[4,64,128]{2,1,0:T(8,128)S(1)}, u32[]{:S(2)}, u32[]{:S(2)}) collective-permute-start(f32[4,64,128]{2,1,0:T(8,128)S(1)} %get-tuple-element.38.row_a_ref), channel_id=1, source_target_pairs={{0,4},{4,0},{8,12},{12,8},{1,5},{5,1},{9,13},{13,9},{2,6},{6,2},{1... | collective-permute-start | bytes 393224 | tf_op jit(solution)/shard_map/ppermute | solution.py:432
  6.5 8.2 %collective-permute-start.1 = (f32[4,64,128]{2,1,0:T(8,128)S(1)}, f32[4,64,128]{2,1,0:T(8,128)S(1)}, u32[]{:S(2)}, u32[]{:S(2)}) collective-permute-start(f32[4,64,128]{2,1,0:T(8,128)S(1)} %get-tuple-element.39.row_b_ref), channel_id=1, source_target_pairs={{0,0},{4,8},{8,4},{12,12},{1,1},{5,9},{9,5},{13,13},{2,2},{6,10},{... | collective-permute-start | bytes 393224 | tf_op jit(solution)/shard_map/ppermute | solution.py:432
  7.3 7.5 %copy-start.2 = (s32[5,2,4]{0,2,1:T(4,128)S(1)}, s32[5,2,4]{0,2,1:T(4,128)}, u32[]{:S(2)}) copy-start(s32[5,2,4]{0,2,1:T(4,128)} %param.9) | copy-start | bytes 484
  7.3 7.4 %copy-start.1 = (s32[5,2,4]{0,2,1:T(4,128)S(1)}, s32[5,2,4]{0,2,1:T(4,128)}, u32[]{:S(2)}) copy-start(s32[5,2,4]{0,2,1:T(4,128)} %param.8) | copy-start | bytes 484
  7.4 6.7 %collective-permute-start.4 = (f32[2,64,128]{2,1,0:T(8,128)S(1)}, f32[2,64,128]{2,1,0:T(8,128)S(1)}, u32[]{:S(2)}, u32[]{:S(2)}) collective-permute-start(f32[2,64,128]{2,1,0:T(8,128)S(1)} %get-tuple-element.45), channel_id=1, source_target_pairs={{0,4},{4,0},{8,12},{12,8},{1,5},{5,1},{9,13},{13,9},{2,6},{6,2},{1... | collective-permute-start | bytes 196616 | tf_op jit(solution)/shard_map/ppermute | solution.py:432
  11.8 2.9 %collective-permute-start.5 = (f32[2,64,128]{2,1,0:T(8,128)S(1)}, f32[2,64,128]{2,1,0:T(8,128)S(1)}, u32[]{:S(2)}, u32[]{:S(2)}) collective-permute-start(f32[2,64,128]{2,1,0:T(8,128)S(1)} %get-tuple-element.46), channel_id=1, source_target_pairs={{0,0},{4,8},{8,4},{12,12},{1,1},{5,9},{9,5},{13,13},{2,2},{6,10},{... | collective-permute-start | bytes 196616 | tf_op jit(solution)/shard_map/ppermute | solution.py:432
  12.5 9.2 %collective-permute-start.8 = (f32[4,96,128]{2,1,0:T(8,128)S(1)}, f32[4,96,128]{2,1,0:T(8,128)S(1)}, u32[]{:S(2)}, u32[]{:S(2)}) collective-permute-start(f32[4,96,128]{2,1,0:T(8,128)S(1)} %get-tuple-element.47.rest_a_ref.row_a_ref), channel_id=1, source_target_pairs={{0,4},{4,0},{8,12},{12,8},{1,5},{5,1},{9,13},{13,9},{2,6},{6,2},{1... | collective-permute-start | bytes 589832 | tf_op jit(solution)/shard_map/ppermute | solution.py:432
  14.1 7.6 %collective-permute-start.9 = (f32[4,96,128]{2,1,0:T(8,128)S(1)}, f32[4,96,128]{2,1,0:T(8,128)S(1)}, u32[]{:S(2)}, u32[]{:S(2)}) collective-permute-start(f32[4,96,128]{2,1,0:T(8,128)S(1)} %get-tuple-element.48.rest_b_ref.row_b_ref), channel_id=1, source_target_pairs={{0,0},{4,8},{8,4},{12,12},{1,1},{5,9},{9,5},{13,13},{2,2},{6,10},{... | collective-permute-start | bytes 589832 | tf_op jit(solution)/shard_map/ppermute | solution.py:432
  17.7 6.1 %collective-permute-start.6 = (f32[5,32,128]{2,1,0:T(8,128)S(1)}, f32[5,32,128]{2,1,0:T(8,128)S(1)}, u32[]{:S(2)}, u32[]{:S(2)}) collective-permute-start(f32[5,32,128]{2,1,0:T(8,128)S(1)} %get-tuple-element.50.row_a_ref), channel_id=1, source_target_pairs={{0,4},{4,0},{8,12},{12,8},{1,5},{5,1},{9,13},{13,9},{2,6},{6,2},{1... | collective-permute-start | bytes 245768 | tf_op jit(solution)/shard_map/ppermute | solution.py:432
  21.0 8.2 %collective-permute-start.12 = (f32[4,32,128]{2,1,0:T(8,128)S(1)}, f32[4,32,128]{2,1,0:T(8,128)S(1)}, u32[]{:S(2)}, u32[]{:S(2)}) collective-permute-start(f32[4,32,128]{2,1,0:T(8,128)S(1)} %get-tuple-element.54.row_b_ref), channel_id=1, source_target_pairs={{0,0},{4,8},{8,4},{12,12},{1,1},{5,9},{9,5},{13,13},{2,2},{6,10},{... | collective-permute-start | bytes 196616 | tf_op jit(solution)/shard_map/ppermute | solution.py:432
  21.7 7.5 %collective-permute-start.10 = (f32[4,96,128]{2,1,0:T(8,128)S(1)}, f32[4,96,128]{2,1,0:T(8,128)S(1)}, u32[]{:S(2)}, u32[]{:S(2)}) collective-permute-start(f32[4,96,128]{2,1,0:T(8,128)S(1)} %get-tuple-element.51), channel_id=1, source_target_pairs={{0,1},{1,0},{2,3},{3,2},{4,5},{5,4},{6,7},{7,6},{8,9},{9,8},{10,11... | collective-permute-start | bytes 589832 | tf_op jit(solution)/shard_map/ppermute | solution.py:432
  23.1 6.2 %collective-permute-start.11 = (f32[4,96,128]{2,1,0:T(8,128)S(1)}, f32[4,96,128]{2,1,0:T(8,128)S(1)}, u32[]{:S(2)}, u32[]{:S(2)}) collective-permute-start(f32[4,96,128]{2,1,0:T(8,128)S(1)} %get-tuple-element.52), channel_id=1, source_target_pairs={{0,0},{1,2},{2,1},{3,3},{4,4},{5,6},{6,5},{7,7},{8,8},{9,10},{10,9... | collective-permute-start | bytes 589832 | tf_op jit(solution)/shard_map/ppermute | solution.py:432
  23.7 5.4 %collective-permute-start.7 = (f32[32,128]{1,0:T(8,128)S(1)}, f32[32,128]{1,0:T(8,128)S(1)}, u32[]{:S(2)}, u32[]{:S(2)}) collective-permute-start(f32[32,128]{1,0:T(8,128)S(1)} %fusion.1), channel_id=1, source_target_pairs={{0,8},{1,9},{2,10},{3,11},{4,12},{5,13},{6,14},{7,15},{8,0},{9,1},... | collective-permute-start | bytes 49160 | tf_op jit(solution)/shard_map/ppermute | solution.py:424
  29.2 3.4 %collective-permute-start.13 = (f32[5,32,128]{2,1,0:T(8,128)S(1)}, f32[5,32,128]{2,1,0:T(8,128)S(1)}, u32[]{:S(2)}, u32[]{:S(2)}) collective-permute-start(f32[5,32,128]{2,1,0:T(8,128)S(1)} %get-tuple-element.55), channel_id=1, source_target_pairs={{0,1},{1,0},{2,3},{3,2},{4,5},{5,4},{6,7},{7,6},{8,9},{9,8},{10,11... | collective-permute-start | bytes 245768 | tf_op jit(solution)/shard_map/ppermute | solution.py:432
  31.7 6.0 %collective-permute-start.15 = (f32[4,32,128]{2,1,0:T(8,128)S(1)}, f32[4,32,128]{2,1,0:T(8,128)S(1)}, u32[]{:S(2)}, u32[]{:S(2)}) collective-permute-start(f32[4,32,128]{2,1,0:T(8,128)S(1)} %get-tuple-element.56), channel_id=1, source_target_pairs={{0,0},{1,2},{2,1},{3,3},{4,4},{5,6},{6,5},{7,7},{8,8},{9,10},{10,9... | collective-permute-start | bytes 196616 | tf_op jit(solution)/shard_map/ppermute | solution.py:432
  32.6 5.0 %collective-permute-start.14 = (f32[32,128]{1,0:T(8,128)S(1)}, f32[32,128]{1,0:T(8,128)S(1)}, u32[]{:S(2)}, u32[]{:S(2)}) collective-permute-start(f32[32,128]{1,0:T(8,128)S(1)} %fusion), channel_id=1, source_target_pairs={{0,2},{1,3},{2,0},{3,1},{4,6},{5,7},{6,4},{7,5},{8,10},{9,11},{10,... | collective-permute-start | bytes 49160 | tf_op jit(solution)/shard_map/ppermute | solution.py:424
  41.0 1.3 %collective-permute-start.16 = (f32[48,128]{1,0:T(8,128)S(1)}, f32[48,128]{1,0:T(8,128)S(1)}, u32[]{:S(2)}, u32[]{:S(2)}) collective-permute-start(f32[48,128]{1,0:T(8,128)S(1)} %get-tuple-element.64), channel_id=1, source_target_pairs={{0,1},{1,0},{2,3},{3,2},{4,5},{5,4},{6,7},{7,6},{8,9},{9,8},{10,11... | collective-permute-start | bytes 73736 | tf_op jit(solution)/shard_map/ppermute | solution.py:424
  42.3 5.9 %collective-permute-start.17 = (f32[48,128]{1,0:T(8,128)S(1)}, f32[48,128]{1,0:T(8,128)S(1)}, u32[]{:S(2)}, u32[]{:S(2)}) collective-permute-start(f32[48,128]{1,0:T(8,128)S(1)} %add.51), channel_id=1, source_target_pairs={{0,6},{1,7},{2,4},{3,5},{4,2},{5,3},{6,0},{7,1},{8,14},{9,15},{10,... | collective-permute-start | bytes 73736 | tf_op jit(solution)/shard_map/ppermute | solution.py:424
  46.4 3.8 %collective-permute-start.18 = (f32[48,128]{1,0:T(8,128)S(1)}, f32[48,128]{1,0:T(8,128)S(1)}, u32[]{:S(2)}, u32[]{:S(2)}) collective-permute-start(f32[48,128]{1,0:T(8,128)S(1)} %add.51), channel_id=1, source_target_pairs={{0,2},{1,3},{2,0},{3,1},{4,6},{5,7},{6,4},{7,5},{8,10},{9,11},{10,... | collective-permute-start | bytes 73736 | tf_op jit(solution)/shard_map/ppermute | solution.py:424
  47.0 3.8 %collective-permute-start.19 = (f32[48,128]{1,0:T(8,128)S(1)}, f32[48,128]{1,0:T(8,128)S(1)}, u32[]{:S(2)}, u32[]{:S(2)}) collective-permute-start(f32[48,128]{1,0:T(8,128)S(1)} %add.51), channel_id=1, source_target_pairs={{0,4},{1,5},{2,6},{3,7},{4,0},{5,1},{6,2},{7,3},{8,12},{9,13},{10,... | collective-permute-start | bytes 73736 | tf_op jit(solution)/shard_map/ppermute | solution.py:424
  50.8 4.8 %collective-permute-start.20 = (f32[48,128]{1,0:T(8,128)S(1)}, f32[48,128]{1,0:T(8,128)S(1)}, u32[]{:S(2)}, u32[]{:S(2)}) collective-permute-start(f32[48,128]{1,0:T(8,128)S(1)} %add_add_fusion), channel_id=1, source_target_pairs={{0,8},{1,9},{2,10},{3,11},{4,12},{5,13},{6,14},{7,15},{8,0},{9,1},... | collective-permute-start | bytes 73736 | tf_op jit(solution)/shard_map/ppermute | solution.py:424
  55.6 2.4 %collective-permute-start.21 = (f32[40,128]{1,0:T(8,128)S(1)}, f32[40,128]{1,0:T(8,128)S(1)}, u32[]{:S(2)}, u32[]{:S(2)}) collective-permute-start(f32[40,128]{1,0:T(8,128)S(1)} %slice.22), channel_id=1, source_target_pairs={{0,1},{1,0},{2,3},{3,2},{4,5},{5,4},{6,7},{7,6},{8,9},{9,8},{10,11... | collective-permute-start | bytes 61448 | tf_op jit(solution)/shard_map/ppermute | solution.py:424

commit v10 on v9

--- a/solution.py
+++ b/solution.py
@@ -41,13 +41,36 @@
     )
 
 
-def split_tables(stiff_ref, mass_ref, high_ref, low_ref, axis):
+def split_tables(stiff_ref, mass_ref, table_ref, parts_axis):
     side = stiff_ref.shape[1]
+    spans = (slice(0, side), slice(side, 2 * side))
     for kind in range(stiff_ref.shape[0]):
-        for place, ref in enumerate((stiff_ref, mass_ref)):
-            span = [kind, slice(None), slice(None)]
-            span[axis] = slice(place * side, (place + 1) * side)
-            high_ref[tuple(span)], low_ref[tuple(span)] = split(ref[kind])
+        for matrix, ref in zip(spans, (stiff_ref, mass_ref)):
+            for part, value in zip(spans, split(ref[kind])):
+                if parts_axis == 1:
+                    table_ref[kind, matrix, part] = value
+                else:
+                    table_ref[kind, part, matrix] = value
+
+
+def stacked(value):
+    return jnp.concatenate(split(value), axis=0)
+
+
+def deep(value):
+    high, low = split(value)
+    upper = jnp.concatenate([high, high], axis=1)
+    return jnp.concatenate([upper, jnp.concatenate([low, jnp.zeros_like(low)], axis=1)], axis=0)
+
+
+def halves_sum(value):
+    half = value.shape[0] // 2
+    return value[:half] + value[half:]
+
+
+def pair_sum(left, right_high, right_low):
+    rows = left.shape[0] // 2
+    return halves_sum(mul_t(left, right_high)) + mul_t(left[:rows], right_low)
 
 
 def pick(flag, first, second):
@@ -73,13 +96,15 @@
     return first + neighbour + down * (count_y - 1), kinds_ref[tile, k]
 
 
-def pack_kernel(flags_ref, block_ref, side_a_ref, side_b_ref, row_a_ref, row_b_ref):
+def pack_kernel(flags_ref, vectors_ref, side_a_ref, side_b_ref, row_a_ref, row_b_ref):
     count_y, both, _ = row_a_ref.shape
     tiles = 2 * count_y
     odd_y, odd_x = flag_at(flags_ref, 0), flag_at(flags_ref, 1)
 
+    first = vectors_ref.shape[0] - both * tiles
+
     def tile_of(i, j):
-        return block_ref[pl.ds(i * count_y + j, both, stride=tiles), :]
+        return vectors_ref[pl.ds(first + i * count_y + j, both, stride=tiles), :]
 
     for i in range(2):
         side_a_ref[i], side_b_ref[i] = pick(odd_y, tile_of(i, 0), tile_of(i, count_y - 1))
@@ -87,14 +112,14 @@
         row_a_ref[j], row_b_ref[j] = pick(odd_x, tile_of(0, j), tile_of(1, j))
 
 
-def rest_kernel(flags_ref, basis_ref, rest_a_ref, rest_b_ref):
+def rest_kernel(flags_ref, vectors_ref, rest_a_ref, rest_b_ref):
     count_y, rest, _ = rest_a_ref.shape
     odd_x = flag_at(flags_ref, 1)
     for j in range(count_y):
         rest_a_ref[j], rest_b_ref[j] = pick(
             odd_x,
-            basis_ref[pl.ds(j, rest, stride=2 * count_y), :],
-            basis_ref[pl.ds(count_y + j, rest, stride=2 * count_y), :],
+            vectors_ref[pl.ds(j, rest, stride=2 * count_y), :],
+            vectors_ref[pl.ds(count_y + j, rest, stride=2 * count_y), :],
         )
 
 
@@ -142,8 +167,7 @@
     partial_ref,
     current_ref,
     ext_ref,
-    table_high_ref,
-    table_low_ref,
+    table_ref,
     neighbours_ref,
     kinds_ref,
     semaphores,
@@ -153,7 +177,7 @@
     )
     for copy in copies:
         copy.start()
-    split_tables(stiff_ref, mass_ref, table_high_ref, table_low_ref, 1)
+    split_tables(stiff_ref, mass_ref, table_ref, 1)
     count_y, both, side = row_a_ref.shape
     wide = count_y + 2
     block = both // 2
@@ -194,15 +218,12 @@
         total = 4.0 * own[i, j][:block] + own[i, j][block:]
         for k in range(neighbours_ref.shape[1]):
             source, kind = source_and_kind(neighbours_ref, kinds_ref, tile, k, count_y)
-            chosen = ext_ref[source]
-            pair = mul(chosen, table_high_ref[kind])
-            total = total + (
-                pair[:block] + (pair[block:] + mul(chosen[:block], table_low_ref[kind]))
-            )
+            pair = mul(ext_ref[source], table_ref[kind])
+            total = total + (pair[:block, :side] + (pair[block:, :side] + pair[:block, side:]))
         totals[i, j] = total
         rest_tile = pick(odd_x, rest_a_ref[j], rest_b_ref[j])[i]
         basis_tile = jnp.concatenate([rest_tile, own[i, j][:block]], axis=0)
-        partial = partial + mul3_t(total, basis_tile)
+        partial = partial + pair_sum(stacked(total), *split(basis_tile))
     for j in range(count_y):
         residual_a_ref[j], residual_b_ref[j] = pick(odd_x, totals[0, j], totals[1, j])
     residual_a_ref[count_y] = partial
@@ -219,21 +240,20 @@
     stiff_ref,
     mass_ref,
     basis_ref,
-    table_high_ref,
-    table_low_ref,
+    table_ref,
 ):
     count_y, rest, _ = rest_a_ref.shape
     prior = rest + current_ref.shape[1]
     odd_x = flag_at(flags_ref, 1)
-    split_tables(stiff_ref, mass_ref, table_high_ref, table_low_ref, 2)
+    split_tables(stiff_ref, mass_ref, table_ref, 0)
     for j in range(count_y):
         rests = list(pick(odd_x, from_rest_a_ref[j], from_rest_b_ref[j]))
         rests[1:1] = pick(odd_x, rest_a_ref[j], rest_b_ref[j])
         for i in range(4):
             tile = jnp.concatenate([rests[i], current_ref[i * (count_y + 2) + j + 1]], axis=0)
-            high, low = split(tile)
-            basis_ref[i * count_y + j, :prior, :] = high
-            basis_ref[i * count_y + j, prior:, :] = low
+            basis_ref[i * count_y + j, :prior, :], basis_ref[i * count_y + j, prior:, :] = split(
+                tile
+            )
 
 
 def operators_kernel(
@@ -252,8 +272,7 @@
     rest_side_b_ref,
     current_ref,
     basis_ref,
-    table_high_ref,
-    table_low_ref,
+    table_ref,
     weighted_low_ref,
     weighted_high_ref,
     coupling_ref,
@@ -278,14 +297,13 @@
     )
     coupling = partial_ref[...] * inverse_rows
     coupling_ref[...] = coupling
-    coupling_high, coupling_low = split(coupling)
+    coupling_deep = deep(coupling)
 
     def basis_parts(i, j):
         if 0 < j < wide - 1:
-            place = i * count_y + j - 1
-            return basis_ref[place, :prior, :], basis_ref[place, prior:, :]
+            return basis_ref[i * count_y + j - 1]
         rest_tile = pick(odd_y, rest_side_a_ref[i], rest_side_b_ref[i])[j // (wide - 1)]
-        return split(jnp.concatenate([rest_tile, current_ref[i * wide + j]], axis=0))
+        return stacked(jnp.concatenate([rest_tile, current_ref[i * wide + j]], axis=0))
 
     for j in range(wide):
         if 0 < j < wide - 1:
@@ -297,10 +315,7 @@
                 for i in range(4)
             ]
         for i in range(4):
-            high, low = basis_parts(i, j)
-            value = rows[i] - (
-                mul(coupling_high, high) + (mul(coupling_high, low) + mul(coupling_low, high))
-            )
+            value = rows[i] - halves_sum(mul(coupling_deep, basis_parts(i, j)))
             if i == 0:
                 value = value * in_low_x
             if i == 3:
@@ -311,9 +326,7 @@
                 value = value * in_high_y
             if 0 < i < 3 and 0 < j < wide - 1:
                 (weighted_low_ref, weighted_high_ref)[i - 1][j - 1] = value
-            high, low = split(value)
-            ext_ref[i * wide + j, :block, :] = high
-            ext_ref[i * wide + j, block:, :] = low
+            ext_ref[i * wide + j] = deep(value)
     for copy in copies:
         copy.wait()
     with_basis = jnp.zeros((2 * block, prior), F32)
@@ -324,19 +337,14 @@
         totals = jnp.concatenate([4.0 * own, own], axis=1)
         for k in range(neighbours_ref.shape[1]):
             source, kind = source_and_kind(neighbours_ref, kinds_ref, tile, k, count_y)
-            chosen = ext_ref[source]
-            pair = mul(chosen, table_high_ref[kind])
-            totals = totals + (
-                pair[:block] + (pair[block:] + mul(chosen[:block], table_low_ref[kind]))
-            )
+            totals = totals + halves_sum(mul(ext_ref[source], table_ref[kind]))
         applied = jnp.concatenate([totals[:, :side], totals[:, side:]], axis=0)
-        high, low = split(applied)
-        basis_high, basis_low = basis_parts(i + 1, j + 1)
-        with_basis = with_basis + (
-            mul_t(high, basis_high) + (mul_t(high, basis_low) + mul_t(low, basis_high))
+        basis_tile = basis_parts(i + 1, j + 1)
+        with_basis = with_basis + pair_sum(
+            stacked(applied), basis_tile[:prior], basis_tile[prior:]
         )
         right = jnp.concatenate([applied, own, jnp.zeros_like(own)], axis=0)
-        with_own = with_own + mul3_t(own, right)
+        with_own = with_own + pair_sum(stacked(own), *split(right))
     halves = [
         jnp.concatenate(
             [
@@ -364,10 +372,12 @@
     sums_ref,
     weighted_low_ref,
     weighted_high_ref,
-    new_ref,
+    new_hbm_ref,
     factor_ref,
     inverse_ref,
     reduced_ref,
+    new_ref,
+    semaphore,
 ):
     count_y, block, _ = weighted_low_ref.shape
     prior = sums_ref.shape[1]
@@ -392,13 +402,16 @@
                 pivots[b] = pivots[b] - ratio[j + b : j + b + 1, :] * pivots[a]
             work = work - jnp.where(rows > at, ratio, 0.0) * pivots[a]
     work = work * lax.rsqrt(jnp.sum(work[:, :block] * unit, axis=1, keepdims=True))
-    factor_ref[...] = jnp.where(column_ids >= row_ids, work[:, :block], 0.0)
     inverse = work[:, block:]
     for tile in range(tiles):
         own = (weighted_low_ref, weighted_high_ref)[tile // count_y][tile % count_y]
         new_ref[pl.ds(tile, block, stride=tiles), :] = mul3(inverse, own)
+    copy = pltpu.make_async_copy(new_ref, new_hbm_ref, semaphore)
+    copy.start()
+    factor_ref[...] = jnp.where(column_ids >= row_ids, work[:, :block], 0.0)
     inverse_ref[...] = inverse
     reduce_half(inverse, sums_ref, inverse_rows, reduced_ref)
+    copy.wait()
 
 
 def reduce_half(inverse, sums_ref, inverse_rows, out_ref):
@@ -458,7 +471,7 @@
     kinds = stiff_tiles.shape[0]
     inverse_rows = 1.0 / (tiles * side * lax.axis_size("px") * lax.axis_size("py"))
     basis = prior_basis.reshape(-1, side)
-    block_vectors = jnp.concatenate([basis[rest * tiles :], previous.reshape(-1, side)], axis=0)
+    vectors = jnp.concatenate([basis, previous.reshape(-1, side)], axis=0)
     codes = [array.transpose(1, 2, 0).reshape(tiles, -1) for array in (neighbours, tile_kinds)]
     code_scratch = [pltpu.SMEM(array.shape, jnp.int32) for array in codes]
     code_scratch += [pltpu.SemaphoreType.DMA((2,))]
@@ -468,13 +481,13 @@
     bits += 16 * (at_x > 0) + 32 * (at_x < lax.axis_size("px") - 1)
     flags = ((bits >> lax.broadcasted_iota(jnp.int32, (8, side), 0)) & 1).astype(F32)
 
-    def call(kernel, inputs, outputs, scratch=(), plain=0, limit=8, cost=None):
+    def call(kernel, inputs, outputs, scratch=(), plain=0, plain_out=0, limit=8, cost=None):
         specs = [ANY] * plain + [VMEM] * (len(inputs) - plain)
         return pl.pallas_call(
             kernel,
             out_shape=outputs,
             in_specs=specs,
-            out_specs=[VMEM] * len(outputs),
+            out_specs=[ANY] * plain_out + [VMEM] * (len(outputs) - plain_out),
             scratch_shapes=scratch,
             compiler_params=pltpu.CompilerParams(vmem_limit_bytes=limit * MIB),
             cost_estimate=cost,
@@ -482,10 +495,10 @@
 
     side_a, side_b, row_a, row_b = call(
         pack_kernel,
-        (flags, block_vectors),
+        (flags, vectors),
         [shape(count_x, 2 * block, side)] * 2 + [shape(count_y, 2 * block, side)] * 2,
     )
-    rest_a, rest_b = call(rest_kernel, (flags, basis), [shape(count_y, rest, side)] * 2)
+    rest_a, rest_b = call(rest_kernel, (flags, vectors), [shape(count_y, rest, side)] * 2)
     from_side_a, from_side_b = exchange(side_a, side_b, "py")
     from_row_a, from_row_b = exchange(row_a, row_b, "px")
     from_side_a, rest_a, rest_b = lax.optimization_barrier((from_side_a, rest_a, rest_b))
@@ -523,7 +536,7 @@
         [shape(count_y + 1, block, side), shape(count_y, block, side)]
         + [shape(block, prior), shape(4 * wide, block, side)],
         [pltpu.VMEM((4 * wide, 2 * block, 2 * side), BF16)]
-        + [pltpu.VMEM((kinds, 2 * side, side), BF16)] * 2
+        + [pltpu.VMEM((kinds, 2 * side, 2 * side), BF16)]
         + code_scratch,
         plain=2,
         cost=pl.CostEstimate(flops=10**9, bytes_accessed=0, transcendentals=0),
@@ -543,11 +556,11 @@
     )
     from_side_a, from_side_b = exchange(side_a, side_b, "py")
     partial = total_over(partial + from_side_a[-1], 2, count_py)
-    basis_parts, wide_high, wide_low = call(
+    basis_parts, table = call(
         prepare_kernel,
         (flags, rest_a, rest_b, from_rest_a, from_rest_b, current, stiff_tiles, mass_tiles),
         [shape(4 * count_y, 2 * prior, side, dtype=BF16)]
-        + [shape(kinds, side, 2 * side, dtype=BF16)] * 2,
+        + [shape(kinds, 2 * side, 2 * side, dtype=BF16)],
         cost=pl.CostEstimate(flops=10**9, bytes_accessed=0, transcendentals=0),
     )
     weighted_low, weighted_high, coupling, sent, kept = call(
@@ -566,13 +579,12 @@
             rest_side_b,
             current,
             basis_parts,
-            wide_high,
-            wide_low,
+            table,
         ),
         [shape(count_y, block, side)] * 2
         + [shape(block, prior)]
         + [shape(block + 16, prior)] * 2,
-        [pltpu.VMEM((4 * wide, 2 * block, side), BF16)] + code_scratch,
+        [pltpu.VMEM((4 * wide, 2 * block, 2 * side), BF16)] + code_scratch,
         plain=2,
     )
     kept = half_total(sent, kept)
@@ -586,6 +598,8 @@
             shape(block, block),
             shape(block, prior + block),
         ],
+        [pltpu.VMEM((block * tiles, side), F32), pltpu.SemaphoreType.DMA],
+        plain_out=1,
         cost=pl.CostEstimate(flops=10**9, bytes_accessed=0, transcendentals=0),
     )
     (reduced,) = call(

time: 59.3 us -> 58.5 us (0.987)
  local copies, waits for them, and re-layouts: 0.99 us -> 0.1 us
    slice x2 -> x0, local copies, waits for them, and re-layouts: 0.89 us -> none  [shards(): basis[rest * tiles:]]
  transfers between devices with their start and end apart: 22 -> 22, of which waited for: 9 -> 9; matrix products, arithmetic and copies ran while one was open for 0% -> 0% of each run, Pallas kernels for 9% -> 10%
where the time goes in v10:
time: 58.5 us; the launch traced here: 58.2 us
  starting transfers between devices  32.4 us (55%)
  waiting for transfers between devices  13.5 us (23%)
  Pallas kernels  9.95 us (17%)
  other arithmetic  1.2 us (2%)
  between operations  0.96 us (2%)
    ppermute x7, starting transfers between devices, exchange(): lax.ppermute(message_a, axis, near)  16 us
    ppermute x8, waiting for transfers between devices, swap(): return lax.ppermute(value, axes, pairs)  13 us
    ppermute x8, starting transfers between devices, swap(): return lax.ppermute(value, axes, pairs)  11.8 us
    pallas_call x10, Pallas kernels, call(): pl.pallas_call(kernel, out_shape=outputs, in_specs=specs, out_specs=[ANY]...  9.95 us
    ppermute x7, starting transfers between devices, exchange(): lax.ppermute(message_b, axis, pairs)  4.59 us
  transfers between devices with their start and end apart: 22, of which 9 were waited for; matrix products, arithmetic and copies ran while one was open for 0% of the time, Pallas kernels for 10%

profile of v10, /device:TPU:0, one launch (start us, length us, event | category | flops | bytes accessed | tf_op | source)
XLA Modules:
  0.0 58.2 jit_solution(5385548075121641186)
XLA Ops:
  0.7 1.2 %pad_maximum_fusion.vectors_ref = f32[1280,128]{1,0:T(8,128)S(1)} fusion(f32[256,128]{1,0:T(8,128)} %bitcast.24, f32[1024,128]{1,0:T(8,128)} %bitcast.23), kind=kLoop, calls=%fused_computation | loop fusion | flops 163840 | bytes 1310720 | tf_op jit(solution)/shard_map/concatenate | solution.py:474
  1.8 0.1 iota.7.flags_ref
  1.9 0.1 shard_map.93
  2.0 0.0 copy-start.2
  2.0 0.5 collective-permute-start.2
  2.5 0.7 %collective-permute-start.3 = (f32[2,64,128]{2,1,0:T(8,128)S(1)}, f32[2,64,128]{2,1,0:T(8,128)S(1)}, u32[]{:S(2)}, u32[]{:S(2)}) collective-permute-start(f32[2,64,128]{2,1,0:T(8,128)S(1)} %get-tuple-element.43), channel_id=1, source_target_pairs={{0,0},{1,2},{2,1},{3,3},{4,4},{5,6},{6,5},{7,7},{8,8},{9,10},{10,9... | collective-permute-start | bytes 196616 | tf_op jit(solution)/shard_map/ppermute | solution.py:445
  3.1 2.8 %collective-permute-start = (f32[4,64,128]{2,1,0:T(8,128)S(1)}, f32[4,64,128]{2,1,0:T(8,128)S(1)}, u32[]{:S(2)}, u32[]{:S(2)}) collective-permute-start(f32[4,64,128]{2,1,0:T(8,128)S(1)} %get-tuple-element.37.row_a_ref), channel_id=1, source_target_pairs={{0,4},{4,0},{8,12},{12,8},{1,5},{5,1},{9,13},{13,9},{2,6},{6,2},{1... | collective-permute-start | bytes 393224 | tf_op jit(solution)/shard_map/ppermute | solution.py:445
  5.9 0.7 %collective-permute-start.1 = (f32[4,64,128]{2,1,0:T(8,128)S(1)}, f32[4,64,128]{2,1,0:T(8,128)S(1)}, u32[]{:S(2)}, u32[]{:S(2)}) collective-permute-start(f32[4,64,128]{2,1,0:T(8,128)S(1)} %get-tuple-element.38.row_b_ref), channel_id=1, source_target_pairs={{0,0},{4,8},{8,4},{12,12},{1,1},{5,9},{9,5},{13,13},{2,2},{6,10},{... | collective-permute-start | bytes 393224 | tf_op jit(solution)/shard_map/ppermute | solution.py:445
  6.6 0.1 shard_map.94
  6.7 0.0 collective-permute-done.2.side_a_ref.from_side_a_ref
  6.7 0.0 collective-permute-done.3.side_b_ref.from_side_b_ref
  6.7 0.0 copy-start.1
  6.7 0.0 copy-start
  6.8 4.5 %collective-permute-start.4 = (f32[2,64,128]{2,1,0:T(8,128)S(1)}, f32[2,64,128]{2,1,0:T(8,128)S(1)}, u32[]{:S(2)}, u32[]{:S(2)}) collective-permute-start(f32[2,64,128]{2,1,0:T(8,128)S(1)} %get-tuple-element.44), channel_id=1, source_target_pairs={{0,4},{4,0},{8,12},{12,8},{1,5},{5,1},{9,13},{13,9},{2,6},{6,2},{1... | collective-permute-start | bytes 196616 | tf_op jit(solution)/shard_map/ppermute | solution.py:445
  11.2 0.7 %collective-permute-start.5 = (f32[2,64,128]{2,1,0:T(8,128)S(1)}, f32[2,64,128]{2,1,0:T(8,128)S(1)}, u32[]{:S(2)}, u32[]{:S(2)}) collective-permute-start(f32[2,64,128]{2,1,0:T(8,128)S(1)} %get-tuple-element.45), channel_id=1, source_target_pairs={{0,0},{4,8},{8,4},{12,12},{1,1},{5,9},{9,5},{13,13},{2,2},{6,10},{... | collective-permute-start | bytes 196616 | tf_op jit(solution)/shard_map/ppermute | solution.py:445
  11.9 1.3 %collective-permute-start.8 = (f32[4,96,128]{2,1,0:T(8,128)S(1)}, f32[4,96,128]{2,1,0:T(8,128)S(1)}, u32[]{:S(2)}, u32[]{:S(2)}) collective-permute-start(f32[4,96,128]{2,1,0:T(8,128)S(1)} %get-tuple-element.46.rest_a_ref.row_a_ref), channel_id=1, source_target_pairs={{0,4},{4,0},{8,12},{12,8},{1,5},{5,1},{9,13},{13,9},{2,6},{6,2},{1... | collective-permute-start | bytes 589832 | tf_op jit(solution)/shard_map/ppermute | solution.py:445
  13.2 0.2 collective-permute-done.4.from_corner_a_ref
  13.5 0.7 %collective-permute-start.9 = (f32[4,96,128]{2,1,0:T(8,128)S(1)}, f32[4,96,128]{2,1,0:T(8,128)S(1)}, u32[]{:S(2)}, u32[]{:S(2)}) collective-permute-start(f32[4,96,128]{2,1,0:T(8,128)S(1)} %get-tuple-element.47.rest_b_ref.row_b_ref), channel_id=1, source_target_pairs={{0,0},{4,8},{8,4},{12,12},{1,1},{5,9},{9,5},{13,13},{2,2},{6,10},{... | collective-permute-start | bytes 589832 | tf_op jit(solution)/shard_map/ppermute | solution.py:445
  14.1 0.0 collective-permute-done.5.from_corner_b_ref
  14.1 0.0 collective-permute-done.from_row_a_ref
  14.2 2.6 %shard_map.96 = (f32[5,32,128]{2,1,0:T(8,128)S(1)}, f32[4,32,128]{2,1,0:T(8,128)S(1)}, f32[32,128]{1,0:T(8,128)S(1)}, f32[24,32,128]{2,1,0:T(8,128)S(1)}) custom-call(s32[8,5]{1,0:T(8,128)S(1)} %bitcast.19, s32[8,5]{1,0:T(8,128)S(1)} %bitcast.21, f32[8,128]{1,0:T(8,128)S(1)} %iota.7.flags_ref, f32[4,64,128]{2,1,0:T(8,128)S(1)} %get-tuple-element.37.row_a_ref, ...), custom_call_target="tpu_custom_call" | custom-call | flops 1000000000 | tf_op jit(solution)/shard_map/pallas_call | solution.py:486
  16.9 3.3 %collective-permute-start.6 = (f32[5,32,128]{2,1,0:T(8,128)S(1)}, f32[5,32,128]{2,1,0:T(8,128)S(1)}, u32[]{:S(2)}, u32[]{:S(2)}) collective-permute-start(f32[5,32,128]{2,1,0:T(8,128)S(1)} %get-tuple-element.49.row_a_ref), channel_id=1, source_target_pairs={{0,4},{4,0},{8,12},{12,8},{1,5},{5,1},{9,13},{13,9},{2,6},{6,2},{1... | collective-permute-start | bytes 245768 | tf_op jit(solution)/shard_map/ppermute | solution.py:445
  20.2 0.7 %collective-permute-start.12 = (f32[4,32,128]{2,1,0:T(8,128)S(1)}, f32[4,32,128]{2,1,0:T(8,128)S(1)}, u32[]{:S(2)}, u32[]{:S(2)}) collective-permute-start(f32[4,32,128]{2,1,0:T(8,128)S(1)} %get-tuple-element.53.row_b_ref), channel_id=1, source_target_pairs={{0,0},{4,8},{8,4},{12,12},{1,1},{5,9},{9,5},{13,13},{2,2},{6,10},{... | collective-permute-start | bytes 196616 | tf_op jit(solution)/shard_map/ppermute | solution.py:445
  20.8 0.0 collective-permute-done.8.from_row_a_ref.from_rest_a_ref
  20.9 1.3 %collective-permute-start.10 = (f32[4,96,128]{2,1,0:T(8,128)S(1)}, f32[4,96,128]{2,1,0:T(8,128)S(1)}, u32[]{:S(2)}, u32[]{:S(2)}) collective-permute-start(f32[4,96,128]{2,1,0:T(8,128)S(1)} %get-tuple-element.50), channel_id=1, source_target_pairs={{0,1},{1,0},{2,3},{3,2},{4,5},{5,4},{6,7},{7,6},{8,9},{9,8},{10,11... | collective-permute-start | bytes 589832 | tf_op jit(solution)/shard_map/ppermute | solution.py:445
  22.2 0.7 %collective-permute-start.11 = (f32[4,96,128]{2,1,0:T(8,128)S(1)}, f32[4,96,128]{2,1,0:T(8,128)S(1)}, u32[]{:S(2)}, u32[]{:S(2)}) collective-permute-start(f32[4,96,128]{2,1,0:T(8,128)S(1)} %get-tuple-element.51), channel_id=1, source_target_pairs={{0,0},{1,2},{2,1},{3,3},{4,4},{5,6},{6,5},{7,7},{8,8},{9,10},{10,9... | collective-permute-start | bytes 589832 | tf_op jit(solution)/shard_map/ppermute | solution.py:445
  22.9 3.7 %collective-permute-start.7 = (f32[32,128]{1,0:T(8,128)S(1)}, f32[32,128]{1,0:T(8,128)S(1)}, u32[]{:S(2)}, u32[]{:S(2)}) collective-permute-start(f32[32,128]{1,0:T(8,128)S(1)} %fusion.1), channel_id=1, source_target_pairs={{0,8},{1,9},{2,10},{3,11},{4,12},{5,13},{6,14},{7,15},{8,0},{9,1},... | collective-permute-start | bytes 49160 | tf_op jit(solution)/shard_map/ppermute | solution.py:437
  26.7 1.7 %collective-permute-done.7 = f32[32,128]{1,0:T(8,128)S(1)} collective-permute-done((f32[32,128]{1,0:T(8,128)S(1)}, f32[32,128]{1,0:T(8,128)S(1)}, u32[]{:S(2)}, u32[]{:S(2)}) %collective-permute-start.7) | collective-permute-done | bytes 16416 | tf_op jit(solution)/shard_map/ppermute | solution.py:437
  28.4 2.3 %collective-permute-start.13 = (f32[5,32,128]{2,1,0:T(8,128)S(1)}, f32[5,32,128]{2,1,0:T(8,128)S(1)}, u32[]{:S(2)}, u32[]{:S(2)}) collective-permute-start(f32[5,32,128]{2,1,0:T(8,128)S(1)} %get-tuple-element.54), channel_id=1, source_target_pairs={{0,1},{1,0},{2,3},{3,2},{4,5},{5,4},{6,7},{7,6},{8,9},{9,8},{10,11... | collective-permute-start | bytes 245768 | tf_op jit(solution)/shard_map/ppermute | solution.py:445
  30.7 0.7 %collective-permute-start.15 = (f32[4,32,128]{2,1,0:T(8,128)S(1)}, f32[4,32,128]{2,1,0:T(8,128)S(1)}, u32[]{:S(2)}, u32[]{:S(2)}) collective-permute-start(f32[4,32,128]{2,1,0:T(8,128)S(1)} %get-tuple-element.55), channel_id=1, source_target_pairs={{0,0},{1,2},{2,1},{3,3},{4,4},{5,6},{6,5},{7,7},{8,8},{9,10},{10,9... | collective-permute-start | bytes 196616 | tf_op jit(solution)/shard_map/ppermute | solution.py:445
  31.4 0.3 collective-permute-done.13.from_side_a_ref
  31.7 2.7 %collective-permute-start.14 = (f32[32,128]{1,0:T(8,128)S(1)}, f32[32,128]{1,0:T(8,128)S(1)}, u32[]{:S(2)}, u32[]{:S(2)}) collective-permute-start(f32[32,128]{1,0:T(8,128)S(1)} %fusion), channel_id=1, source_target_pairs={{0,2},{1,3},{2,0},{3,1},{4,6},{5,7},{6,4},{7,5},{8,10},{9,11},{10,... | collective-permute-start | bytes 49160 | tf_op jit(solution)/shard_map/ppermute | solution.py:437
  34.4 0.3 shard_map.99
  34.7 2.0 %collective-permute-done.14 = f32[32,128]{1,0:T(8,128)S(1)} collective-permute-done((f32[32,128]{1,0:T(8,128)S(1)}, f32[32,128]{1,0:T(8,128)S(1)}, u32[]{:S(2)}, u32[]{:S(2)}) %collective-permute-start.14) | collective-permute-done | bytes 16416 | tf_op jit(solution)/shard_map/ppermute | solution.py:437
  36.7 2.9 %shard_map.100 = (f32[4,32,128]{2,1,0:T(8,128)S(1)}, f32[4,32,128]{2,1,0:T(8,128)S(1)}, f32[32,128]{1,0:T(8,128)}, f32[48,128]{1,0:T(8,128)S(1)}, f32[48,128]{1,0:T(8,128)S(1)}) custom-call(s32[8,5]{1,0:T(8,128)S(1)} %bitcast.20, s32[8,5]{1,0:T(8,128)S(1)} %bitcast.22, f32[8,128]{1,0:T(8,128)S(1)} %iota.7.flags_ref, f32[32,128]{1,0:T(8,128)S(1)} %add.50.partial_ref, ...), custom_call_target="tpu_custom_call" | custom-call | tf_op jit(solution)/shard_map/pallas_call | solution.py:486
  39.6 0.2 collective-permute-start.16
  39.8 1.1 %collective-permute-done.16 = f32[48,128]{1,0:T(8,128)S(1)} collective-permute-done((f32[48,128]{1,0:T(8,128)S(1)}, f32[48,128]{1,0:T(8,128)S(1)}, u32[]{:S(2)}, u32[]{:S(2)}) %collective-permute-start.16) | collective-permute-done | bytes 24608 | tf_op jit(solution)/shard_map/ppermute | solution.py:437
  40.8 4.1 %collective-permute-start.17 = (f32[48,128]{1,0:T(8,128)S(1)}, f32[48,128]{1,0:T(8,128)S(1)}, u32[]{:S(2)}, u32[]{:S(2)}) collective-permute-start(f32[48,128]{1,0:T(8,128)S(1)} %add.51), channel_id=1, source_target_pairs={{0,6},{1,7},{2,4},{3,5},{4,2},{5,3},{6,0},{7,1},{8,14},{9,15},{10,... | collective-permute-start | bytes 73736 | tf_op jit(solution)/shard_map/ppermute | solution.py:437
  44.9 0.6 %collective-permute-start.18 = (f32[48,128]{1,0:T(8,128)S(1)}, f32[48,128]{1,0:T(8,128)S(1)}, u32[]{:S(2)}, u32[]{:S(2)}) collective-permute-start(f32[48,128]{1,0:T(8,128)S(1)} %add.51), channel_id=1, source_target_pairs={{0,2},{1,3},{2,0},{3,1},{4,6},{5,7},{6,4},{7,5},{8,10},{9,11},{10,... | collective-permute-start | bytes 73736 | tf_op jit(solution)/shard_map/ppermute | solution.py:437
  45.5 0.0 collective-permute-start.19
  45.6 1.2 %collective-permute-done.17 = f32[48,128]{1,0:T(8,128)S(1)} collective-permute-done((f32[48,128]{1,0:T(8,128)S(1)}, f32[48,128]{1,0:T(8,128)S(1)}, u32[]{:S(2)}, u32[]{:S(2)}) %collective-permute-start.17) | collective-permute-done | bytes 24608 | tf_op jit(solution)/shard_map/ppermute | solution.py:437
  46.7 2.0 %collective-permute-done.18 = f32[48,128]{1,0:T(8,128)S(1)} collective-permute-done((f32[48,128]{1,0:T(8,128)S(1)}, f32[48,128]{1,0:T(8,128)S(1)}, u32[]{:S(2)}, u32[]{:S(2)}) %collective-permute-start.18) | collective-permute-done | bytes 24608 | tf_op jit(solution)/shard_map/ppermute | solution.py:437
  48.7 0.6 %collective-permute-done.19 = f32[48,128]{1,0:T(8,128)S(1)} collective-permute-done((f32[48,128]{1,0:T(8,128)S(1)}, f32[48,128]{1,0:T(8,128)S(1)}, u32[]{:S(2)}, u32[]{:S(2)}) %collective-permute-start.19) | collective-permute-done | bytes 24608 | tf_op jit(solution)/shard_map/ppermute | solution.py:437
  49.3 0.3 collective-permute-start.20
  49.7 4.4 %collective-permute-done.20 = f32[48,128]{1,0:T(8,128)S(1)} collective-permute-done((f32[48,128]{1,0:T(8,128)S(1)}, f32[48,128]{1,0:T(8,128)S(1)}, u32[]{:S(2)}, u32[]{:S(2)}) %collective-permute-start.20) | collective-permute-done | bytes 24608 | tf_op jit(solution)/shard_map/ppermute | solution.py:437
  54.1 0.1 collective-permute-start.21
  54.2 2.9 %shard_map.101 = (f32[256,128]{1,0:T(8,128)}, f32[32,32]{1,0:T(8,128)}, f32[32,32]{1,0:T(8,128)S(1)}, f32[32,160]{1,0:T(8,128)S(1)}) custom-call(f32[48,128]{1,0:T(8,128)S(1)} %add.55.sums_ref, f32[4,32,128]{2,1,0:T(8,128)S(1)} %get-tuple-element.63.weighted_low_ref, f32[4,32,128]{2,1,0:T(8,128)S(1)} %get-tuple-element.64.weighted_high_ref), custom_call_target="tpu_custom_call" | custom-call | flops 1000000000 | tf_op jit(solution)/shard_map/pallas_call | solution.py:486
  57.2 1.0 %shard_map.102 = f32[2,32,160]{2,1,0:T(8,128)} custom-call(f32[8,128]{1,0:T(8,128)S(1)} %iota.7.flags_ref, f32[32,32]{1,0:T(8,128)S(1)} %get-tuple-element.68.inverse_ref, f32[40,128]{1,0:T(8,128)S(1)} %collective-permute-done.21.other_ref, f32[32,160]{1,0:T(8,128)S(1)} %get-tuple-element.69.half_ref), custom_call_target="tpu_custom_call" | custom-call | tf_op jit(solution)/shard_map/pallas_call | solution.py:486
  (25 shorter events, 0.2 us)
Async XLA Ops:
  1.9 12.3 %copy-start.3 = (f32[8,128,128]{2,1,0:T(8,128)S(1)}, f32[8,128,128]{2,1,0:T(8,128)}, u32[]{:S(2)}) copy-start(f32[8,128,128]{2,1,0:T(8,128)} %mass_ref.3) | copy-start | bytes 1572868
  2.0 12.2 %copy-start.2 = (f32[8,128,128]{2,1,0:T(8,128)S(1)}, f32[8,128,128]{2,1,0:T(8,128)}, u32[]{:S(2)}) copy-start(f32[8,128,128]{2,1,0:T(8,128)} %stiff_ref.3) | copy-start | bytes 1572868
  2.0 4.7 %collective-permute-start.2 = (f32[2,64,128]{2,1,0:T(8,128)S(1)}, f32[2,64,128]{2,1,0:T(8,128)S(1)}, u32[]{:S(2)}, u32[]{:S(2)}) collective-permute-start(f32[2,64,128]{2,1,0:T(8,128)S(1)} %get-tuple-element.39), channel_id=1, source_target_pairs={{0,1},{1,0},{2,3},{3,2},{4,5},{5,4},{6,7},{7,6},{8,9},{9,8},{10,11... | collective-permute-start | bytes 196616 | tf_op jit(solution)/shard_map/ppermute | solution.py:445
  2.5 4.2 %collective-permute-start.3 = (f32[2,64,128]{2,1,0:T(8,128)S(1)}, f32[2,64,128]{2,1,0:T(8,128)S(1)}, u32[]{:S(2)}, u32[]{:S(2)}) collective-permute-start(f32[2,64,128]{2,1,0:T(8,128)S(1)} %get-tuple-element.43), channel_id=1, source_target_pairs={{0,0},{1,2},{2,1},{3,3},{4,4},{5,6},{6,5},{7,7},{8,8},{9,10},{10,9... | collective-permute-start | bytes 196616 | tf_op jit(solution)/shard_map/ppermute | solution.py:445
  3.1 11.0 %collective-permute-start = (f32[4,64,128]{2,1,0:T(8,128)S(1)}, f32[4,64,128]{2,1,0:T(8,128)S(1)}, u32[]{:S(2)}, u32[]{:S(2)}) collective-permute-start(f32[4,64,128]{2,1,0:T(8,128)S(1)} %get-tuple-element.37.row_a_ref), channel_id=1, source_target_pairs={{0,4},{4,0},{8,12},{12,8},{1,5},{5,1},{9,13},{13,9},{2,6},{6,2},{1... | collective-permute-start | bytes 393224 | tf_op jit(solution)/shard_map/ppermute | solution.py:445
  5.9 8.2 %collective-permute-start.1 = (f32[4,64,128]{2,1,0:T(8,128)S(1)}, f32[4,64,128]{2,1,0:T(8,128)S(1)}, u32[]{:S(2)}, u32[]{:S(2)}) collective-permute-start(f32[4,64,128]{2,1,0:T(8,128)S(1)} %get-tuple-element.38.row_b_ref), channel_id=1, source_target_pairs={{0,0},{4,8},{8,4},{12,12},{1,1},{5,9},{9,5},{13,13},{2,2},{6,10},{... | collective-permute-start | bytes 393224 | tf_op jit(solution)/shard_map/ppermute | solution.py:445
  6.7 7.5 %copy-start.1 = (s32[5,2,4]{0,2,1:T(4,128)S(1)}, s32[5,2,4]{0,2,1:T(4,128)}, u32[]{:S(2)}) copy-start(s32[5,2,4]{0,2,1:T(4,128)} %param.9) | copy-start | bytes 484
  6.7 7.4 %copy-start = (s32[5,2,4]{0,2,1:T(4,128)S(1)}, s32[5,2,4]{0,2,1:T(4,128)}, u32[]{:S(2)}) copy-start(s32[5,2,4]{0,2,1:T(4,128)} %param.8) | copy-start | bytes 484
  6.8 6.7 %collective-permute-start.4 = (f32[2,64,128]{2,1,0:T(8,128)S(1)}, f32[2,64,128]{2,1,0:T(8,128)S(1)}, u32[]{:S(2)}, u32[]{:S(2)}) collective-permute-start(f32[2,64,128]{2,1,0:T(8,128)S(1)} %get-tuple-element.44), channel_id=1, source_target_pairs={{0,4},{4,0},{8,12},{12,8},{1,5},{5,1},{9,13},{13,9},{2,6},{6,2},{1... | collective-permute-start | bytes 196616 | tf_op jit(solution)/shard_map/ppermute | solution.py:445
  11.2 2.9 %collective-permute-start.5 = (f32[2,64,128]{2,1,0:T(8,128)S(1)}, f32[2,64,128]{2,1,0:T(8,128)S(1)}, u32[]{:S(2)}, u32[]{:S(2)}) collective-permute-start(f32[2,64,128]{2,1,0:T(8,128)S(1)} %get-tuple-element.45), channel_id=1, source_target_pairs={{0,0},{4,8},{8,4},{12,12},{1,1},{5,9},{9,5},{13,13},{2,2},{6,10},{... | collective-permute-start | bytes 196616 | tf_op jit(solution)/shard_map/ppermute | solution.py:445
  11.9 9.0 %collective-permute-start.8 = (f32[4,96,128]{2,1,0:T(8,128)S(1)}, f32[4,96,128]{2,1,0:T(8,128)S(1)}, u32[]{:S(2)}, u32[]{:S(2)}) collective-permute-start(f32[4,96,128]{2,1,0:T(8,128)S(1)} %get-tuple-element.46.rest_a_ref.row_a_ref), channel_id=1, source_target_pairs={{0,4},{4,0},{8,12},{12,8},{1,5},{5,1},{9,13},{13,9},{2,6},{6,2},{1... | collective-permute-start | bytes 589832 | tf_op jit(solution)/shard_map/ppermute | solution.py:445
  13.5 7.4 %collective-permute-start.9 = (f32[4,96,128]{2,1,0:T(8,128)S(1)}, f32[4,96,128]{2,1,0:T(8,128)S(1)}, u32[]{:S(2)}, u32[]{:S(2)}) collective-permute-start(f32[4,96,128]{2,1,0:T(8,128)S(1)} %get-tuple-element.47.rest_b_ref.row_b_ref), channel_id=1, source_target_pairs={{0,0},{4,8},{8,4},{12,12},{1,1},{5,9},{9,5},{13,13},{2,2},{6,10},{... | collective-permute-start | bytes 589832 | tf_op jit(solution)/shard_map/ppermute | solution.py:445
  16.9 6.0 %collective-permute-start.6 = (f32[5,32,128]{2,1,0:T(8,128)S(1)}, f32[5,32,128]{2,1,0:T(8,128)S(1)}, u32[]{:S(2)}, u32[]{:S(2)}) collective-permute-start(f32[5,32,128]{2,1,0:T(8,128)S(1)} %get-tuple-element.49.row_a_ref), channel_id=1, source_target_pairs={{0,4},{4,0},{8,12},{12,8},{1,5},{5,1},{9,13},{13,9},{2,6},{6,2},{1... | collective-permute-start | bytes 245768 | tf_op jit(solution)/shard_map/ppermute | solution.py:445
  20.2 8.2 %collective-permute-start.12 = (f32[4,32,128]{2,1,0:T(8,128)S(1)}, f32[4,32,128]{2,1,0:T(8,128)S(1)}, u32[]{:S(2)}, u32[]{:S(2)}) collective-permute-start(f32[4,32,128]{2,1,0:T(8,128)S(1)} %get-tuple-element.53.row_b_ref), channel_id=1, source_target_pairs={{0,0},{4,8},{8,4},{12,12},{1,1},{5,9},{9,5},{13,13},{2,2},{6,10},{... | collective-permute-start | bytes 196616 | tf_op jit(solution)/shard_map/ppermute | solution.py:445
  20.9 7.5 %collective-permute-start.10 = (f32[4,96,128]{2,1,0:T(8,128)S(1)}, f32[4,96,128]{2,1,0:T(8,128)S(1)}, u32[]{:S(2)}, u32[]{:S(2)}) collective-permute-start(f32[4,96,128]{2,1,0:T(8,128)S(1)} %get-tuple-element.50), channel_id=1, source_target_pairs={{0,1},{1,0},{2,3},{3,2},{4,5},{5,4},{6,7},{7,6},{8,9},{9,8},{10,11... | collective-permute-start | bytes 589832 | tf_op jit(solution)/shard_map/ppermute | solution.py:445
  22.2 6.2 %collective-permute-start.11 = (f32[4,96,128]{2,1,0:T(8,128)S(1)}, f32[4,96,128]{2,1,0:T(8,128)S(1)}, u32[]{:S(2)}, u32[]{:S(2)}) collective-permute-start(f32[4,96,128]{2,1,0:T(8,128)S(1)} %get-tuple-element.51), channel_id=1, source_target_pairs={{0,0},{1,2},{2,1},{3,3},{4,4},{5,6},{6,5},{7,7},{8,8},{9,10},{10,9... | collective-permute-start | bytes 589832 | tf_op jit(solution)/shard_map/ppermute | solution.py:445
  22.9 5.5 %collective-permute-start.7 = (f32[32,128]{1,0:T(8,128)S(1)}, f32[32,128]{1,0:T(8,128)S(1)}, u32[]{:S(2)}, u32[]{:S(2)}) collective-permute-start(f32[32,128]{1,0:T(8,128)S(1)} %fusion.1), channel_id=1, source_target_pairs={{0,8},{1,9},{2,10},{3,11},{4,12},{5,13},{6,14},{7,15},{8,0},{9,1},... | collective-permute-start | bytes 49160 | tf_op jit(solution)/shard_map/ppermute | solution.py:437
  28.4 3.2 %collective-permute-start.13 = (f32[5,32,128]{2,1,0:T(8,128)S(1)}, f32[5,32,128]{2,1,0:T(8,128)S(1)}, u32[]{:S(2)}, u32[]{:S(2)}) collective-permute-start(f32[5,32,128]{2,1,0:T(8,128)S(1)} %get-tuple-element.54), channel_id=1, source_target_pairs={{0,1},{1,0},{2,3},{3,2},{4,5},{5,4},{6,7},{7,6},{8,9},{9,8},{10,11... | collective-permute-start | bytes 245768 | tf_op jit(solution)/shard_map/ppermute | solution.py:445
  30.7 6.0 %collective-permute-start.15 = (f32[4,32,128]{2,1,0:T(8,128)S(1)}, f32[4,32,128]{2,1,0:T(8,128)S(1)}, u32[]{:S(2)}, u32[]{:S(2)}) collective-permute-start(f32[4,32,128]{2,1,0:T(8,128)S(1)} %get-tuple-element.55), channel_id=1, source_target_pairs={{0,0},{1,2},{2,1},{3,3},{4,4},{5,6},{6,5},{7,7},{8,8},{9,10},{10,9... | collective-permute-start | bytes 196616 | tf_op jit(solution)/shard_map/ppermute | solution.py:445
  31.7 5.0 %collective-permute-start.14 = (f32[32,128]{1,0:T(8,128)S(1)}, f32[32,128]{1,0:T(8,128)S(1)}, u32[]{:S(2)}, u32[]{:S(2)}) collective-permute-start(f32[32,128]{1,0:T(8,128)S(1)} %fusion), channel_id=1, source_target_pairs={{0,2},{1,3},{2,0},{3,1},{4,6},{5,7},{6,4},{7,5},{8,10},{9,11},{10,... | collective-permute-start | bytes 49160 | tf_op jit(solution)/shard_map/ppermute | solution.py:437
  39.6 1.3 %collective-permute-start.16 = (f32[48,128]{1,0:T(8,128)S(1)}, f32[48,128]{1,0:T(8,128)S(1)}, u32[]{:S(2)}, u32[]{:S(2)}) collective-permute-start(f32[48,128]{1,0:T(8,128)S(1)} %get-tuple-element.62), channel_id=1, source_target_pairs={{0,1},{1,0},{2,3},{3,2},{4,5},{5,4},{6,7},{7,6},{8,9},{9,8},{10,11... | collective-permute-start | bytes 73736 | tf_op jit(solution)/shard_map/ppermute | solution.py:437
  40.8 5.9 %collective-permute-start.17 = (f32[48,128]{1,0:T(8,128)S(1)}, f32[48,128]{1,0:T(8,128)S(1)}, u32[]{:S(2)}, u32[]{:S(2)}) collective-permute-start(f32[48,128]{1,0:T(8,128)S(1)} %add.51), channel_id=1, source_target_pairs={{0,6},{1,7},{2,4},{3,5},{4,2},{5,3},{6,0},{7,1},{8,14},{9,15},{10,... | collective-permute-start | bytes 73736 | tf_op jit(solution)/shard_map/ppermute | solution.py:437
  44.9 3.8 %collective-permute-start.18 = (f32[48,128]{1,0:T(8,128)S(1)}, f32[48,128]{1,0:T(8,128)S(1)}, u32[]{:S(2)}, u32[]{:S(2)}) collective-permute-start(f32[48,128]{1,0:T(8,128)S(1)} %add.51), channel_id=1, source_target_pairs={{0,2},{1,3},{2,0},{3,1},{4,6},{5,7},{6,4},{7,5},{8,10},{9,11},{10,... | collective-permute-start | bytes 73736 | tf_op jit(solution)/shard_map/ppermute | solution.py:437
  45.5 3.8 %collective-permute-start.19 = (f32[48,128]{1,0:T(8,128)S(1)}, f32[48,128]{1,0:T(8,128)S(1)}, u32[]{:S(2)}, u32[]{:S(2)}) collective-permute-start(f32[48,128]{1,0:T(8,128)S(1)} %add.51), channel_id=1, source_target_pairs={{0,4},{1,5},{2,6},{3,7},{4,0},{5,1},{6,2},{7,3},{8,12},{9,13},{10,... | collective-permute-start | bytes 73736 | tf_op jit(solution)/shard_map/ppermute | solution.py:437
  49.3 4.8 %collective-permute-start.20 = (f32[48,128]{1,0:T(8,128)S(1)}, f32[48,128]{1,0:T(8,128)S(1)}, u32[]{:S(2)}, u32[]{:S(2)}) collective-permute-start(f32[48,128]{1,0:T(8,128)S(1)} %add_add_fusion), channel_id=1, source_target_pairs={{0,8},{1,9},{2,10},{3,11},{4,12},{5,13},{6,14},{7,15},{8,0},{9,1},... | collective-permute-start | bytes 73736 | tf_op jit(solution)/shard_map/ppermute | solution.py:437
  54.1 3.0 %collective-permute-start.21 = (f32[40,128]{1,0:T(8,128)S(1)}, f32[40,128]{1,0:T(8,128)S(1)}, u32[]{:S(2)}, u32[]{:S(2)}) collective-permute-start(f32[40,128]{1,0:T(8,128)S(1)} %slice.14), channel_id=1, source_target_pairs={{0,1},{1,0},{2,3},{3,2},{4,5},{5,4},{6,7},{7,6},{8,9},{9,8},{10,11... | collective-permute-start | bytes 61448 | tf_op jit(solution)/shard_map/ppermute | solution.py:437

commit v11 on v10

--- a/solution.py
+++ b/solution.py
@@ -226,8 +226,11 @@
         partial = partial + pair_sum(stacked(total), *split(basis_tile))
     for j in range(count_y):
         residual_a_ref[j], residual_b_ref[j] = pick(odd_x, totals[0, j], totals[1, j])
-    residual_a_ref[count_y] = partial
     partial_ref[...] = partial
+
+
+def tables_kernel(stiff_ref, mass_ref, table_ref):
+    split_tables(stiff_ref, mass_ref, table_ref, 0)
 
 
 def prepare_kernel(
@@ -237,15 +240,11 @@
     from_rest_a_ref,
     from_rest_b_ref,
     current_ref,
-    stiff_ref,
-    mass_ref,
     basis_ref,
-    table_ref,
 ):
     count_y, rest, _ = rest_a_ref.shape
     prior = rest + current_ref.shape[1]
     odd_x = flag_at(flags_ref, 1)
-    split_tables(stiff_ref, mass_ref, table_ref, 0)
     for j in range(count_y):
         rests = list(pick(odd_x, from_rest_a_ref[j], from_rest_b_ref[j]))
         rests[1:1] = pick(odd_x, rest_a_ref[j], rest_b_ref[j])
@@ -367,21 +366,8 @@
     return jnp.concatenate([rows[:, n * 32 : (n + 1) * 32] for n in range(4)], axis=0)
 
 
-def factor_kernel(
-    inverse_rows,
-    sums_ref,
-    weighted_low_ref,
-    weighted_high_ref,
-    new_hbm_ref,
-    factor_ref,
-    inverse_ref,
-    reduced_ref,
-    new_ref,
-    semaphore,
-):
-    count_y, block, _ = weighted_low_ref.shape
-    prior = sums_ref.shape[1]
-    tiles = 2 * count_y
+def factor_kernel(inverse_rows, sums_ref, work_ref):
+    block = work_ref.shape[0]
     gram = unfolded(sums_ref[block + 8 :, :]) * inverse_rows
     row_ids = lax.broadcasted_iota(jnp.int32, (block, block), 0)
     column_ids = lax.broadcasted_iota(jnp.int32, (block, block), 1)
@@ -402,33 +388,37 @@
                 pivots[b] = pivots[b] - ratio[j + b : j + b + 1, :] * pivots[a]
             work = work - jnp.where(rows > at, ratio, 0.0) * pivots[a]
     work = work * lax.rsqrt(jnp.sum(work[:, :block] * unit, axis=1, keepdims=True))
-    inverse = work[:, block:]
+    work_ref[...] = work
+
+
+def finish_kernel(
+    inverse_rows,
+    flags_ref,
+    work_ref,
+    sums_ref,
+    other_ref,
+    weighted_low_ref,
+    weighted_high_ref,
+    new_ref,
+    factor_ref,
+    reduced_ref,
+):
+    count_y, block, _ = weighted_low_ref.shape
+    prior = sums_ref.shape[1]
+    tiles = 2 * count_y
+    row_ids = lax.broadcasted_iota(jnp.int32, (block, block), 0)
+    column_ids = lax.broadcasted_iota(jnp.int32, (block, block), 1)
+    factor_ref[...] = jnp.where(column_ids >= row_ids, work_ref[:, :block], 0.0)
+    inverse = work_ref[:, block:]
     for tile in range(tiles):
         own = (weighted_low_ref, weighted_high_ref)[tile // count_y][tile % count_y]
         new_ref[pl.ds(tile, block, stride=tiles), :] = mul3(inverse, own)
-    copy = pltpu.make_async_copy(new_ref, new_hbm_ref, semaphore)
-    copy.start()
-    factor_ref[...] = jnp.where(column_ids >= row_ids, work[:, :block], 0.0)
-    inverse_ref[...] = inverse
-    reduce_half(inverse, sums_ref, inverse_rows, reduced_ref)
-    copy.wait()
-
-
-def reduce_half(inverse, sums_ref, inverse_rows, out_ref):
-    block, prior = inverse.shape[0], sums_ref.shape[1]
-    out_ref[:, :prior] = mul3(inverse, sums_ref[:block, :] * inverse_rows)
-    own = unfolded(sums_ref[block : block + 8, :]) * inverse_rows
-    out_ref[:, prior:] = mul3_t(mul3_t(inverse, own), inverse)
-
-
-def reduced_kernel(inverse_rows, flags_ref, inverse_ref, other_ref, half_ref, out_ref, work_ref):
-    reduce_half(inverse_ref[...], other_ref, inverse_rows, work_ref)
     odd_y = flag_at(flags_ref, 0)
-    for span in (slice(0, 128), slice(128, out_ref.shape[2])):
-        flag = odd_y[:, : work_ref[:, span].shape[1]]
-        out_ref[0, :, span], out_ref[1, :, span] = pick(
-            flag, work_ref[:, span], half_ref[:, span]
-        )
+    halves = pick(odd_y, other_ref[...], sums_ref[: block + 8, :])
+    for part, half in enumerate(halves):
+        reduced_ref[part, :, :prior] = mul3(inverse, half[:block] * inverse_rows)
+        own = unfolded(half[block:]) * inverse_rows
+        reduced_ref[part, :, prior:] = mul3_t(mul3_t(inverse, own), inverse)
 
 
 def swap(value, mask):
@@ -481,13 +471,13 @@
     bits += 16 * (at_x > 0) + 32 * (at_x < lax.axis_size("px") - 1)
     flags = ((bits >> lax.broadcasted_iota(jnp.int32, (8, side), 0)) & 1).astype(F32)
 
-    def call(kernel, inputs, outputs, scratch=(), plain=0, plain_out=0, limit=8, cost=None):
+    def call(kernel, inputs, outputs, scratch=(), plain=0, limit=8, cost=None):
         specs = [ANY] * plain + [VMEM] * (len(inputs) - plain)
         return pl.pallas_call(
             kernel,
             out_shape=outputs,
             in_specs=specs,
-            out_specs=[ANY] * plain_out + [VMEM] * (len(outputs) - plain_out),
+            out_specs=[VMEM] * len(outputs),
             scratch_shapes=scratch,
             compiler_params=pltpu.CompilerParams(vmem_limit_bytes=limit * MIB),
             cost_estimate=cost,
@@ -533,7 +523,7 @@
             stiff_tiles,
             mass_tiles,
         ),
-        [shape(count_y + 1, block, side), shape(count_y, block, side)]
+        [shape(count_y, block, side)] * 2
         + [shape(block, prior), shape(4 * wide, block, side)],
         [pltpu.VMEM((4 * wide, 2 * block, 2 * side), BF16)]
         + [pltpu.VMEM((kinds, 2 * side, 2 * side), BF16)]
@@ -542,10 +532,19 @@
         cost=pl.CostEstimate(flops=10**9, bytes_accessed=0, transcendentals=0),
     )
     count_py = lax.axis_size("py")
-    from_row_a, from_row_b = exchange(residual_a, residual_b, "px")
-    partial = total_over(
-        partial + from_row_a[-1], 2 * count_py, count_py * lax.axis_size("px")
-    )
+    stiff_tiles, residual_a = lax.optimization_barrier((stiff_tiles, residual_a))
+    (table,) = call(
+        tables_kernel,
+        (stiff_tiles, mass_tiles),
+        [shape(kinds, 2 * side, 2 * side, dtype=BF16)],
+        cost=pl.CostEstimate(flops=10**9, bytes_accessed=0, transcendentals=0),
+    )
+    partial = total_over(partial, 2 * count_py, count_py * lax.axis_size("px"))
+    partial, table = lax.optimization_barrier((partial, table))
+    from_row_a, from_row_b = exchange(
+        jnp.concatenate([residual_a, partial[None]], axis=0), residual_b, "px"
+    )
+    partial = partial + from_row_a[-1]
     partial, rest_side_a, rest_side_b = lax.optimization_barrier(
         (partial, rest_side_a, rest_side_b)
     )
@@ -556,11 +555,10 @@
     )
     from_side_a, from_side_b = exchange(side_a, side_b, "py")
     partial = total_over(partial + from_side_a[-1], 2, count_py)
-    basis_parts, table = call(
+    (basis_parts,) = call(
         prepare_kernel,
-        (flags, rest_a, rest_b, from_rest_a, from_rest_b, current, stiff_tiles, mass_tiles),
-        [shape(4 * count_y, 2 * prior, side, dtype=BF16)]
-        + [shape(kinds, 2 * side, 2 * side, dtype=BF16)],
+        (flags, rest_a, rest_b, from_rest_a, from_rest_b, current),
+        [shape(4 * count_y, 2 * prior, side, dtype=BF16)],
         cost=pl.CostEstimate(flops=10**9, bytes_accessed=0, transcendentals=0),
     )
     weighted_low, weighted_high, coupling, sent, kept = call(
@@ -589,24 +587,20 @@
     )
     kept = half_total(sent, kept)
     other = swap(kept[: block + 8], 1)
-    new_block, factor, inverse, half = call(
+    (work,) = call(
         functools.partial(factor_kernel, inverse_rows),
-        (kept, weighted_low, weighted_high),
+        (kept,),
+        [shape(block, 2 * block)],
+        cost=pl.CostEstimate(flops=10**9, bytes_accessed=0, transcendentals=0),
+    )
+    new_block, factor, reduced = call(
+        functools.partial(finish_kernel, inverse_rows),
+        (flags, work, kept, other, weighted_low, weighted_high),
         [
             shape(block * tiles, side),
             shape(block, block),
-            shape(block, block),
-            shape(block, prior + block),
+            shape(2, block, prior + block),
         ],
-        [pltpu.VMEM((block * tiles, side), F32), pltpu.SemaphoreType.DMA],
-        plain_out=1,
-        cost=pl.CostEstimate(flops=10**9, bytes_accessed=0, transcendentals=0),
-    )
-    (reduced,) = call(
-        functools.partial(reduced_kernel, inverse_rows),
-        (flags, inverse, other, half),
-        [shape(2, block, prior + block)],
-        [pltpu.VMEM((block, prior + block), F32)],
     )
     return (
         new_block.reshape(previous.shape),

time: 58.5 us -> 62.7 us (1.072)
  waiting for transfers between devices: 13.5 us -> 18.4 us
  Pallas kernels: 9.95 us -> 8.64 us
  starting transfers between devices: 32.4 us -> 33.1 us
    ppermute x7, waiting for transfers between devices: 0.51 us -> 3.37 us  [exchange(): lax.ppermute(message_a, axis, near)]
    ppermute x8, waiting for transfers between devices: 13 us -> 15 us  [swap(): return lax.ppermute(value, axes, pairs)]
    ppermute x8, starting transfers between devices: 11.8 us -> 13.1 us  [swap(): return lax.ppermute(value, axes, pairs)]
    pallas_call x10 -> x11, Pallas kernels: 9.95 us -> 8.64 us  [call(): pl.pallas_call(kernel, out_shape=outputs, in_specs=specs, out_specs=[VMEM...]
    ppermute x7, starting transfers between devices: 16 us -> 15.4 us  [exchange(): lax.ppermute(message_a, axis, near)]
  transfers between devices with their start and end apart: 22 -> 22, of which waited for: 9 -> 10; matrix products, arithmetic and copies ran while one was open for 0% -> 0% of each run, Pallas kernels for 10% -> 7%
where the time goes in v11:
time: 62.7 us; the launch traced here: 62.4 us
  starting transfers between devices  33.1 us (53%)
  waiting for transfers between devices  18.4 us (29%)
  Pallas kernels  8.64 us (14%)
  other arithmetic  1.21 us (2%)
  between operations  0.94 us (1%)
    ppermute x7, starting transfers between devices, exchange(): lax.ppermute(message_a, axis, near)  15.4 us
    ppermute x8, waiting for transfers between devices, swap(): return lax.ppermute(value, axes, pairs)  15 us
    ppermute x8, starting transfers between devices, swap(): return lax.ppermute(value, axes, pairs)  13.1 us
    pallas_call x11, Pallas kernels, call(): pl.pallas_call(kernel, out_shape=outputs, in_specs=specs, out_specs=[VMEM...  8.64 us
    ppermute x7, starting transfers between devices, exchange(): lax.ppermute(message_b, axis, pairs)  4.59 us
    ppermute x7, waiting for transfers between devices, exchange(): lax.ppermute(message_a, axis, near)  3.37 us
  transfers between devices with their start and end apart: 22, of which 10 were waited for; matrix products, arithmetic and copies ran while one was open for 0% of the time, Pallas kernels for 7%

profile of v11, /device:TPU:0, one launch (start us, length us, event | category | flops | bytes accessed | tf_op | source)
XLA Modules:
  0.0 62.4 jit_solution(14463275101510485958)
XLA Ops:
  0.7 1.2 %pad_maximum_fusion.vectors_ref = f32[1280,128]{1,0:T(8,128)S(1)} fusion(f32[256,128]{1,0:T(8,128)} %bitcast.26, f32[1024,128]{1,0:T(8,128)} %bitcast.24), kind=kLoop, calls=%fused_computation | loop fusion | flops 163840 | bytes 1310720 | tf_op jit(solution)/shard_map/concatenate | solution.py:464
  1.8 0.1 iota.7.flags_ref
  1.9 0.1 shard_map.93
  2.0 0.0 copy-start.2
  2.0 0.5 collective-permute-start.2
  2.5 0.7 %collective-permute-start.3 = (f32[2,64,128]{2,1,0:T(8,128)S(1)}, f32[2,64,128]{2,1,0:T(8,128)S(1)}, u32[]{:S(2)}, u32[]{:S(2)}) collective-permute-start(f32[2,64,128]{2,1,0:T(8,128)S(1)} %get-tuple-element.44), channel_id=1, source_target_pairs={{0,0},{1,2},{2,1},{3,3},{4,4},{5,6},{6,5},{7,7},{8,8},{9,10},{10,9... | collective-permute-start | bytes 196616 | tf_op jit(solution)/shard_map/ppermute | solution.py:435
  3.1 2.8 %collective-permute-start = (f32[4,64,128]{2,1,0:T(8,128)S(1)}, f32[4,64,128]{2,1,0:T(8,128)S(1)}, u32[]{:S(2)}, u32[]{:S(2)}) collective-permute-start(f32[4,64,128]{2,1,0:T(8,128)S(1)} %get-tuple-element.38.row_a_ref), channel_id=1, source_target_pairs={{0,4},{4,0},{8,12},{12,8},{1,5},{5,1},{9,13},{13,9},{2,6},{6,2},{1... | collective-permute-start | bytes 393224 | tf_op jit(solution)/shard_map/ppermute | solution.py:435
  5.9 0.7 %collective-permute-start.1 = (f32[4,64,128]{2,1,0:T(8,128)S(1)}, f32[4,64,128]{2,1,0:T(8,128)S(1)}, u32[]{:S(2)}, u32[]{:S(2)}) collective-permute-start(f32[4,64,128]{2,1,0:T(8,128)S(1)} %get-tuple-element.39.row_b_ref), channel_id=1, source_target_pairs={{0,0},{4,8},{8,4},{12,12},{1,1},{5,9},{9,5},{13,13},{2,2},{6,10},{... | collective-permute-start | bytes 393224 | tf_op jit(solution)/shard_map/ppermute | solution.py:435
  6.6 0.1 shard_map.94
  6.7 0.0 copy-start.1
  6.7 0.0 copy-start
  6.8 4.5 %collective-permute-start.4 = (f32[2,64,128]{2,1,0:T(8,128)S(1)}, f32[2,64,128]{2,1,0:T(8,128)S(1)}, u32[]{:S(2)}, u32[]{:S(2)}) collective-permute-start(f32[2,64,128]{2,1,0:T(8,128)S(1)} %get-tuple-element.45), channel_id=1, source_target_pairs={{0,4},{4,0},{8,12},{12,8},{1,5},{5,1},{9,13},{13,9},{2,6},{6,2},{1... | collective-permute-start | bytes 196616 | tf_op jit(solution)/shard_map/ppermute | solution.py:435
  11.2 0.7 %collective-permute-start.5 = (f32[2,64,128]{2,1,0:T(8,128)S(1)}, f32[2,64,128]{2,1,0:T(8,128)S(1)}, u32[]{:S(2)}, u32[]{:S(2)}) collective-permute-start(f32[2,64,128]{2,1,0:T(8,128)S(1)} %get-tuple-element.46), channel_id=1, source_target_pairs={{0,0},{4,8},{8,4},{12,12},{1,1},{5,9},{9,5},{13,13},{2,2},{6,10},{... | collective-permute-start | bytes 196616 | tf_op jit(solution)/shard_map/ppermute | solution.py:435
  11.9 1.3 %collective-permute-start.8 = (f32[4,96,128]{2,1,0:T(8,128)S(1)}, f32[4,96,128]{2,1,0:T(8,128)S(1)}, u32[]{:S(2)}, u32[]{:S(2)}) collective-permute-start(f32[4,96,128]{2,1,0:T(8,128)S(1)} %get-tuple-element.47.rest_a_ref.row_a_ref), channel_id=1, source_target_pairs={{0,4},{4,0},{8,12},{12,8},{1,5},{5,1},{9,13},{13,9},{2,6},{6,2},{1... | collective-permute-start | bytes 589832 | tf_op jit(solution)/shard_map/ppermute | solution.py:435
  13.2 0.2 collective-permute-done.4.from_corner_a_ref
  13.5 0.7 %collective-permute-start.9 = (f32[4,96,128]{2,1,0:T(8,128)S(1)}, f32[4,96,128]{2,1,0:T(8,128)S(1)}, u32[]{:S(2)}, u32[]{:S(2)}) collective-permute-start(f32[4,96,128]{2,1,0:T(8,128)S(1)} %get-tuple-element.48.rest_b_ref.row_b_ref), channel_id=1, source_target_pairs={{0,0},{4,8},{8,4},{12,12},{1,1},{5,9},{9,5},{13,13},{2,2},{6,10},{... | collective-permute-start | bytes 589832 | tf_op jit(solution)/shard_map/ppermute | solution.py:435
  14.1 0.0 collective-permute-done.5.from_corner_b_ref
  14.1 0.0 collective-permute-done.1.from_row_b_ref
  14.2 2.6 %shard_map.96 = (f32[4,32,128]{2,1,0:T(8,128)S(1)}, f32[4,32,128]{2,1,0:T(8,128)S(1)}, f32[32,128]{1,0:T(8,128)S(1)}, f32[24,32,128]{2,1,0:T(8,128)S(1)}) custom-call(s32[8,5]{1,0:T(8,128)S(1)} %bitcast.20, s32[8,5]{1,0:T(8,128)S(1)} %bitcast.22, f32[8,128]{1,0:T(8,128)S(1)} %iota.7.flags_ref, f32[4,64,128]{2,1,0:T(8,128)S(1)} %get-tuple-element.38.row_a_ref, ...), custom_call_target="tpu_custom_call" | custom-call | flops 1000000000 | tf_op jit(solution)/shard_map/pallas_call | solution.py:476
  16.9 4.8 %collective-permute-start.6 = (f32[32,128]{1,0:T(8,128)S(1)}, f32[32,128]{1,0:T(8,128)S(1)}, u32[]{:S(2)}, u32[]{:S(2)}) collective-permute-start(f32[32,128]{1,0:T(8,128)S(1)} %get-tuple-element.49), channel_id=1, source_target_pairs={{0,8},{1,9},{2,10},{3,11},{4,12},{5,13},{6,14},{7,15},{8,0},{9,1},... | collective-permute-start | bytes 49160 | tf_op jit(solution)/shard_map/ppermute | solution.py:427
  21.6 0.2 shard_map.97.table_ref
  21.8 2.8 %collective-permute-done.6 = f32[32,128]{1,0:T(8,128)S(1)} collective-permute-done((f32[32,128]{1,0:T(8,128)S(1)}, f32[32,128]{1,0:T(8,128)S(1)}, u32[]{:S(2)}, u32[]{:S(2)}) %collective-permute-start.6) | collective-permute-done | bytes 16416 | tf_op jit(solution)/shard_map/ppermute | solution.py:427
  24.6 0.4 collective-permute-start.7
  25.0 0.7 %collective-permute-start.12 = (f32[4,32,128]{2,1,0:T(8,128)S(1)}, f32[4,32,128]{2,1,0:T(8,128)S(1)}, u32[]{:S(2)}, u32[]{:S(2)}) collective-permute-start(f32[4,32,128]{2,1,0:T(8,128)S(1)} %get-tuple-element.57.row_b_ref), channel_id=1, source_target_pairs={{0,0},{4,8},{8,4},{12,12},{1,1},{5,9},{9,5},{13,13},{2,2},{6,10},{... | collective-permute-start | bytes 196616 | tf_op jit(solution)/shard_map/ppermute | solution.py:435
  25.7 0.3 collective-permute-start.10
  26.0 0.7 %collective-permute-start.11 = (f32[4,96,128]{2,1,0:T(8,128)S(1)}, f32[4,96,128]{2,1,0:T(8,128)S(1)}, u32[]{:S(2)}, u32[]{:S(2)}) collective-permute-start(f32[4,96,128]{2,1,0:T(8,128)S(1)} %get-tuple-element.55), channel_id=1, source_target_pairs={{0,0},{1,2},{2,1},{3,3},{4,4},{5,6},{6,5},{7,7},{8,8},{9,10},{10,9... | collective-permute-start | bytes 589832 | tf_op jit(solution)/shard_map/ppermute | solution.py:435
  26.7 2.9 %collective-permute-done.7.from_row_a_ref = f32[5,32,128]{2,1,0:T(8,128)S(1)} collective-permute-done((f32[5,32,128]{2,1,0:T(8,128)S(1)}, f32[5,32,128]{2,1,0:T(8,128)S(1)}, u32[]{:S(2)}, u32[]{:S(2)}) %collective-permute-start.7) | collective-permute-done | bytes 81952 | tf_op jit(solution)/shard_map/ppermute | solution.py:435
  29.6 5.6 %collective-permute-start.13 = (f32[5,32,128]{2,1,0:T(8,128)S(1)}, f32[5,32,128]{2,1,0:T(8,128)S(1)}, u32[]{:S(2)}, u32[]{:S(2)}) collective-permute-start(f32[5,32,128]{2,1,0:T(8,128)S(1)} %get-tuple-element.58), channel_id=1, source_target_pairs={{0,1},{1,0},{2,3},{3,2},{4,5},{5,4},{6,7},{7,6},{8,9},{9,8},{10,11... | collective-permute-start | bytes 245768 | tf_op jit(solution)/shard_map/ppermute | solution.py:435
  35.2 0.7 %collective-permute-start.15 = (f32[4,32,128]{2,1,0:T(8,128)S(1)}, f32[4,32,128]{2,1,0:T(8,128)S(1)}, u32[]{:S(2)}, u32[]{:S(2)}) collective-permute-start(f32[4,32,128]{2,1,0:T(8,128)S(1)} %get-tuple-element.59), channel_id=1, source_target_pairs={{0,0},{1,2},{2,1},{3,3},{4,4},{5,6},{6,5},{7,7},{8,8},{9,10},{10,9... | collective-permute-start | bytes 196616 | tf_op jit(solution)/shard_map/ppermute | solution.py:435
  35.9 0.3 collective-permute-done.13.from_side_a_ref
  36.1 2.7 %collective-permute-start.14 = (f32[32,128]{1,0:T(8,128)S(1)}, f32[32,128]{1,0:T(8,128)S(1)}, u32[]{:S(2)}, u32[]{:S(2)}) collective-permute-start(f32[32,128]{1,0:T(8,128)S(1)} %fusion), channel_id=1, source_target_pairs={{0,2},{1,3},{2,0},{3,1},{4,6},{5,7},{6,4},{7,5},{8,10},{9,11},{10,... | collective-permute-start | bytes 49160 | tf_op jit(solution)/shard_map/ppermute | solution.py:427
  38.8 0.2 shard_map.100.basis_ref
  39.0 2.1 %collective-permute-done.14 = f32[32,128]{1,0:T(8,128)S(1)} collective-permute-done((f32[32,128]{1,0:T(8,128)S(1)}, f32[32,128]{1,0:T(8,128)S(1)}, u32[]{:S(2)}, u32[]{:S(2)}) %collective-permute-start.14) | collective-permute-done | bytes 16416 | tf_op jit(solution)/shard_map/ppermute | solution.py:427
  41.2 2.9 %shard_map.101 = (f32[4,32,128]{2,1,0:T(8,128)S(1)}, f32[4,32,128]{2,1,0:T(8,128)S(1)}, f32[32,128]{1,0:T(8,128)}, f32[48,128]{1,0:T(8,128)S(1)}, f32[48,128]{1,0:T(8,128)S(1)}) custom-call(s32[8,5]{1,0:T(8,128)S(1)} %bitcast.21, s32[8,5]{1,0:T(8,128)S(1)} %bitcast.23, f32[8,128]{1,0:T(8,128)S(1)} %iota.7.flags_ref, f32[32,128]{1,0:T(8,128)S(1)} %add.50.partial_ref, ...), custom_call_target="tpu_custom_call" | custom-call | tf_op jit(solution)/shard_map/pallas_call | solution.py:476
  44.0 0.5 collective-permute-start.16
  44.5 0.8 %collective-permute-done.16 = f32[48,128]{1,0:T(8,128)S(1)} collective-permute-done((f32[48,128]{1,0:T(8,128)S(1)}, f32[48,128]{1,0:T(8,128)S(1)}, u32[]{:S(2)}, u32[]{:S(2)}) %collective-permute-start.16) | collective-permute-done | bytes 24608 | tf_op jit(solution)/shard_map/ppermute | solution.py:427
  45.3 3.3 %collective-permute-start.19 = (f32[48,128]{1,0:T(8,128)S(1)}, f32[48,128]{1,0:T(8,128)S(1)}, u32[]{:S(2)}, u32[]{:S(2)}) collective-permute-start(f32[48,128]{1,0:T(8,128)S(1)} %add.51), channel_id=1, source_target_pairs={{0,4},{1,5},{2,6},{3,7},{4,0},{5,1},{6,2},{7,3},{8,12},{9,13},{10,... | collective-permute-start | bytes 73736 | tf_op jit(solution)/shard_map/ppermute | solution.py:427
  48.6 1.5 %collective-permute-start.18 = (f32[48,128]{1,0:T(8,128)S(1)}, f32[48,128]{1,0:T(8,128)S(1)}, u32[]{:S(2)}, u32[]{:S(2)}) collective-permute-start(f32[48,128]{1,0:T(8,128)S(1)} %add.51), channel_id=1, source_target_pairs={{0,2},{1,3},{2,0},{3,1},{4,6},{5,7},{6,4},{7,5},{8,10},{9,11},{10,... | collective-permute-start | bytes 73736 | tf_op jit(solution)/shard_map/ppermute | solution.py:427
  50.1 0.0 collective-permute-start.17
  50.2 0.3 collective-permute-done.19
  50.4 2.0 %collective-permute-done.18 = f32[48,128]{1,0:T(8,128)S(1)} collective-permute-done((f32[48,128]{1,0:T(8,128)S(1)}, f32[48,128]{1,0:T(8,128)S(1)}, u32[]{:S(2)}, u32[]{:S(2)}) %collective-permute-start.18) | collective-permute-done | bytes 24608 | tf_op jit(solution)/shard_map/ppermute | solution.py:427
  52.5 2.4 %collective-permute-done.17 = f32[48,128]{1,0:T(8,128)S(1)} collective-permute-done((f32[48,128]{1,0:T(8,128)S(1)}, f32[48,128]{1,0:T(8,128)S(1)}, u32[]{:S(2)}, u32[]{:S(2)}) %collective-permute-start.17) | collective-permute-done | bytes 24608 | tf_op jit(solution)/shard_map/ppermute | solution.py:427
  54.9 0.3 collective-permute-start.20
  55.1 4.5 %collective-permute-done.20 = f32[48,128]{1,0:T(8,128)S(1)} collective-permute-done((f32[48,128]{1,0:T(8,128)S(1)}, f32[48,128]{1,0:T(8,128)S(1)}, u32[]{:S(2)}, u32[]{:S(2)}) %collective-permute-start.20) | collective-permute-done | bytes 24608 | tf_op jit(solution)/shard_map/ppermute | solution.py:427
  59.7 0.1 collective-permute-start.21
  59.8 1.4 %shard_map.102.work_ref = f32[32,64]{1,0:T(8,128)S(1)} custom-call(f32[48,128]{1,0:T(8,128)S(1)} %add.55.sums_ref), custom_call_target="tpu_custom_call" | custom-call | flops 1000000000 | tf_op jit(solution)/shard_map/pallas_call | solution.py:476
  61.1 0.0 collective-permute-done.21.other_ref
  61.1 1.2 %shard_map.103 = (f32[256,128]{1,0:T(8,128)}, f32[32,32]{1,0:T(8,128)}, f32[2,32,160]{2,1,0:T(8,128)}) custom-call(f32[8,128]{1,0:T(8,128)S(1)} %iota.7.flags_ref, f32[32,64]{1,0:T(8,128)S(1)} %shard_map.102.work_ref, f32[48,128]{1,0:T(8,128)S(1)} %add.55.sums_ref, f32[40,128]{1,0:T(8,128)S(1)} %collective-permute-done.21.other_ref, ...), custom_call_target="tpu_custom_call" | custom-call | tf_op jit(solution)/shard_map/pallas_call | solution.py:476
  (27 shorter events, 0.2 us)
Async XLA Ops:
  1.9 12.3 %copy-start.3 = (f32[8,128,128]{2,1,0:T(8,128)S(1)}, f32[8,128,128]{2,1,0:T(8,128)}, u32[]{:S(2)}) copy-start(f32[8,128,128]{2,1,0:T(8,128)} %mass_ref.3) | copy-start | bytes 1572868
  2.0 12.2 %copy-start.2 = (f32[8,128,128]{2,1,0:T(8,128)S(1)}, f32[8,128,128]{2,1,0:T(8,128)}, u32[]{:S(2)}) copy-start(f32[8,128,128]{2,1,0:T(8,128)} %stiff_ref.2) | copy-start | bytes 1572868
  2.0 4.7 %collective-permute-start.2 = (f32[2,64,128]{2,1,0:T(8,128)S(1)}, f32[2,64,128]{2,1,0:T(8,128)S(1)}, u32[]{:S(2)}, u32[]{:S(2)}) collective-permute-start(f32[2,64,128]{2,1,0:T(8,128)S(1)} %get-tuple-element.40), channel_id=1, source_target_pairs={{0,1},{1,0},{2,3},{3,2},{4,5},{5,4},{6,7},{7,6},{8,9},{9,8},{10,11... | collective-permute-start | bytes 196616 | tf_op jit(solution)/shard_map/ppermute | solution.py:435
  2.5 4.2 %collective-permute-start.3 = (f32[2,64,128]{2,1,0:T(8,128)S(1)}, f32[2,64,128]{2,1,0:T(8,128)S(1)}, u32[]{:S(2)}, u32[]{:S(2)}) collective-permute-start(f32[2,64,128]{2,1,0:T(8,128)S(1)} %get-tuple-element.44), channel_id=1, source_target_pairs={{0,0},{1,2},{2,1},{3,3},{4,4},{5,6},{6,5},{7,7},{8,8},{9,10},{10,9... | collective-permute-start | bytes 196616 | tf_op jit(solution)/shard_map/ppermute | solution.py:435
  3.1 11.0 %collective-permute-start = (f32[4,64,128]{2,1,0:T(8,128)S(1)}, f32[4,64,128]{2,1,0:T(8,128)S(1)}, u32[]{:S(2)}, u32[]{:S(2)}) collective-permute-start(f32[4,64,128]{2,1,0:T(8,128)S(1)} %get-tuple-element.38.row_a_ref), channel_id=1, source_target_pairs={{0,4},{4,0},{8,12},{12,8},{1,5},{5,1},{9,13},{13,9},{2,6},{6,2},{1... | collective-permute-start | bytes 393224 | tf_op jit(solution)/shard_map/ppermute | solution.py:435
  5.9 8.2 %collective-permute-start.1 = (f32[4,64,128]{2,1,0:T(8,128)S(1)}, f32[4,64,128]{2,1,0:T(8,128)S(1)}, u32[]{:S(2)}, u32[]{:S(2)}) collective-permute-start(f32[4,64,128]{2,1,0:T(8,128)S(1)} %get-tuple-element.39.row_b_ref), channel_id=1, source_target_pairs={{0,0},{4,8},{8,4},{12,12},{1,1},{5,9},{9,5},{13,13},{2,2},{6,10},{... | collective-permute-start | bytes 393224 | tf_op jit(solution)/shard_map/ppermute | solution.py:435
  6.7 7.5 %copy-start.1 = (s32[5,2,4]{0,2,1:T(4,128)S(1)}, s32[5,2,4]{0,2,1:T(4,128)}, u32[]{:S(2)}) copy-start(s32[5,2,4]{0,2,1:T(4,128)} %param.9) | copy-start | bytes 484
  6.7 7.4 %copy-start = (s32[5,2,4]{0,2,1:T(4,128)S(1)}, s32[5,2,4]{0,2,1:T(4,128)}, u32[]{:S(2)}) copy-start(s32[5,2,4]{0,2,1:T(4,128)} %param.8) | copy-start | bytes 484
  6.8 6.7 %collective-permute-start.4 = (f32[2,64,128]{2,1,0:T(8,128)S(1)}, f32[2,64,128]{2,1,0:T(8,128)S(1)}, u32[]{:S(2)}, u32[]{:S(2)}) collective-permute-start(f32[2,64,128]{2,1,0:T(8,128)S(1)} %get-tuple-element.45), channel_id=1, source_target_pairs={{0,4},{4,0},{8,12},{12,8},{1,5},{5,1},{9,13},{13,9},{2,6},{6,2},{1... | collective-permute-start | bytes 196616 | tf_op jit(solution)/shard_map/ppermute | solution.py:435
  11.2 2.9 %collective-permute-start.5 = (f32[2,64,128]{2,1,0:T(8,128)S(1)}, f32[2,64,128]{2,1,0:T(8,128)S(1)}, u32[]{:S(2)}, u32[]{:S(2)}) collective-permute-start(f32[2,64,128]{2,1,0:T(8,128)S(1)} %get-tuple-element.46), channel_id=1, source_target_pairs={{0,0},{4,8},{8,4},{12,12},{1,1},{5,9},{9,5},{13,13},{2,2},{6,10},{... | collective-permute-start | bytes 196616 | tf_op jit(solution)/shard_map/ppermute | solution.py:435
  11.9 13.8 %collective-permute-start.8 = (f32[4,96,128]{2,1,0:T(8,128)S(1)}, f32[4,96,128]{2,1,0:T(8,128)S(1)}, u32[]{:S(2)}, u32[]{:S(2)}) collective-permute-start(f32[4,96,128]{2,1,0:T(8,128)S(1)} %get-tuple-element.47.rest_a_ref.row_a_ref), channel_id=1, source_target_pairs={{0,4},{4,0},{8,12},{12,8},{1,5},{5,1},{9,13},{13,9},{2,6},{6,2},{1... | collective-permute-start | bytes 589832 | tf_op jit(solution)/shard_map/ppermute | solution.py:435
  13.5 12.2 %collective-permute-start.9 = (f32[4,96,128]{2,1,0:T(8,128)S(1)}, f32[4,96,128]{2,1,0:T(8,128)S(1)}, u32[]{:S(2)}, u32[]{:S(2)}) collective-permute-start(f32[4,96,128]{2,1,0:T(8,128)S(1)} %get-tuple-element.48.rest_b_ref.row_b_ref), channel_id=1, source_target_pairs={{0,0},{4,8},{8,4},{12,12},{1,1},{5,9},{9,5},{13,13},{2,2},{6,10},{... | collective-permute-start | bytes 589832 | tf_op jit(solution)/shard_map/ppermute | solution.py:435
  16.9 7.8 %collective-permute-start.6 = (f32[32,128]{1,0:T(8,128)S(1)}, f32[32,128]{1,0:T(8,128)S(1)}, u32[]{:S(2)}, u32[]{:S(2)}) collective-permute-start(f32[32,128]{1,0:T(8,128)S(1)} %get-tuple-element.49), channel_id=1, source_target_pairs={{0,8},{1,9},{2,10},{3,11},{4,12},{5,13},{6,14},{7,15},{8,0},{9,1},... | collective-permute-start | bytes 49160 | tf_op jit(solution)/shard_map/ppermute | solution.py:427
  24.6 4.9 %collective-permute-start.7 = (f32[5,32,128]{2,1,0:T(8,128)S(1)}, f32[5,32,128]{2,1,0:T(8,128)S(1)}, u32[]{:S(2)}, u32[]{:S(2)}) collective-permute-start(f32[5,32,128]{2,1,0:T(8,128)S(1)} %pad_maximum_fusion.1), channel_id=1, source_target_pairs={{0,4},{4,0},{8,12},{12,8},{1,5},{5,1},{9,13},{13,9},{2,6},{6,2},{1... | collective-permute-start | bytes 245768 | tf_op jit(solution)/shard_map/ppermute | solution.py:435
  25.0 4.5 %collective-permute-start.12 = (f32[4,32,128]{2,1,0:T(8,128)S(1)}, f32[4,32,128]{2,1,0:T(8,128)S(1)}, u32[]{:S(2)}, u32[]{:S(2)}) collective-permute-start(f32[4,32,128]{2,1,0:T(8,128)S(1)} %get-tuple-element.57.row_b_ref), channel_id=1, source_target_pairs={{0,0},{4,8},{8,4},{12,12},{1,1},{5,9},{9,5},{13,13},{2,2},{6,10},{... | collective-permute-start | bytes 196616 | tf_op jit(solution)/shard_map/ppermute | solution.py:435
  25.7 3.8 %collective-permute-start.10 = (f32[4,96,128]{2,1,0:T(8,128)S(1)}, f32[4,96,128]{2,1,0:T(8,128)S(1)}, u32[]{:S(2)}, u32[]{:S(2)}) collective-permute-start(f32[4,96,128]{2,1,0:T(8,128)S(1)} %get-tuple-element.54), channel_id=1, source_target_pairs={{0,1},{1,0},{2,3},{3,2},{4,5},{5,4},{6,7},{7,6},{8,9},{9,8},{10,11... | collective-permute-start | bytes 589832 | tf_op jit(solution)/shard_map/ppermute | solution.py:435
  26.0 3.5 %collective-permute-start.11 = (f32[4,96,128]{2,1,0:T(8,128)S(1)}, f32[4,96,128]{2,1,0:T(8,128)S(1)}, u32[]{:S(2)}, u32[]{:S(2)}) collective-permute-start(f32[4,96,128]{2,1,0:T(8,128)S(1)} %get-tuple-element.55), channel_id=1, source_target_pairs={{0,0},{1,2},{2,1},{3,3},{4,4},{5,6},{6,5},{7,7},{8,8},{9,10},{10,9... | collective-permute-start | bytes 589832 | tf_op jit(solution)/shard_map/ppermute | solution.py:435
  29.6 6.5 %collective-permute-start.13 = (f32[5,32,128]{2,1,0:T(8,128)S(1)}, f32[5,32,128]{2,1,0:T(8,128)S(1)}, u32[]{:S(2)}, u32[]{:S(2)}) collective-permute-start(f32[5,32,128]{2,1,0:T(8,128)S(1)} %get-tuple-element.58), channel_id=1, source_target_pairs={{0,1},{1,0},{2,3},{3,2},{4,5},{5,4},{6,7},{7,6},{8,9},{9,8},{10,11... | collective-permute-start | bytes 245768 | tf_op jit(solution)/shard_map/ppermute | solution.py:435
  35.2 6.0 %collective-permute-start.15 = (f32[4,32,128]{2,1,0:T(8,128)S(1)}, f32[4,32,128]{2,1,0:T(8,128)S(1)}, u32[]{:S(2)}, u32[]{:S(2)}) collective-permute-start(f32[4,32,128]{2,1,0:T(8,128)S(1)} %get-tuple-element.59), channel_id=1, source_target_pairs={{0,0},{1,2},{2,1},{3,3},{4,4},{5,6},{6,5},{7,7},{8,8},{9,10},{10,9... | collective-permute-start | bytes 196616 | tf_op jit(solution)/shard_map/ppermute | solution.py:435
  36.1 5.0 %collective-permute-start.14 = (f32[32,128]{1,0:T(8,128)S(1)}, f32[32,128]{1,0:T(8,128)S(1)}, u32[]{:S(2)}, u32[]{:S(2)}) collective-permute-start(f32[32,128]{1,0:T(8,128)S(1)} %fusion), channel_id=1, source_target_pairs={{0,2},{1,3},{2,0},{3,1},{4,6},{5,7},{6,4},{7,5},{8,10},{9,11},{10,... | collective-permute-start | bytes 49160 | tf_op jit(solution)/shard_map/ppermute | solution.py:427
  44.0 1.3 %collective-permute-start.16 = (f32[48,128]{1,0:T(8,128)S(1)}, f32[48,128]{1,0:T(8,128)S(1)}, u32[]{:S(2)}, u32[]{:S(2)}) collective-permute-start(f32[48,128]{1,0:T(8,128)S(1)} %get-tuple-element.65), channel_id=1, source_target_pairs={{0,1},{1,0},{2,3},{3,2},{4,5},{5,4},{6,7},{7,6},{8,9},{9,8},{10,11... | collective-permute-start | bytes 73736 | tf_op jit(solution)/shard_map/ppermute | solution.py:427
  45.3 5.1 %collective-permute-start.19 = (f32[48,128]{1,0:T(8,128)S(1)}, f32[48,128]{1,0:T(8,128)S(1)}, u32[]{:S(2)}, u32[]{:S(2)}) collective-permute-start(f32[48,128]{1,0:T(8,128)S(1)} %add.51), channel_id=1, source_target_pairs={{0,4},{1,5},{2,6},{3,7},{4,0},{5,1},{6,2},{7,3},{8,12},{9,13},{10,... | collective-permute-start | bytes 73736 | tf_op jit(solution)/shard_map/ppermute | solution.py:427
  48.6 3.8 %collective-permute-start.18 = (f32[48,128]{1,0:T(8,128)S(1)}, f32[48,128]{1,0:T(8,128)S(1)}, u32[]{:S(2)}, u32[]{:S(2)}) collective-permute-start(f32[48,128]{1,0:T(8,128)S(1)} %add.51), channel_id=1, source_target_pairs={{0,2},{1,3},{2,0},{3,1},{4,6},{5,7},{6,4},{7,5},{8,10},{9,11},{10,... | collective-permute-start | bytes 73736 | tf_op jit(solution)/shard_map/ppermute | solution.py:427
  50.1 4.7 %collective-permute-start.17 = (f32[48,128]{1,0:T(8,128)S(1)}, f32[48,128]{1,0:T(8,128)S(1)}, u32[]{:S(2)}, u32[]{:S(2)}) collective-permute-start(f32[48,128]{1,0:T(8,128)S(1)} %add.51), channel_id=1, source_target_pairs={{0,6},{1,7},{2,4},{3,5},{4,2},{5,3},{6,0},{7,1},{8,14},{9,15},{10,... | collective-permute-start | bytes 73736 | tf_op jit(solution)/shard_map/ppermute | solution.py:427
  54.9 4.8 %collective-permute-start.20 = (f32[48,128]{1,0:T(8,128)S(1)}, f32[48,128]{1,0:T(8,128)S(1)}, u32[]{:S(2)}, u32[]{:S(2)}) collective-permute-start(f32[48,128]{1,0:T(8,128)S(1)} %add_add_fusion), channel_id=1, source_target_pairs={{0,8},{1,9},{2,10},{3,11},{4,12},{5,13},{6,14},{7,15},{8,0},{9,1},... | collective-permute-start | bytes 73736 | tf_op jit(solution)/shard_map/ppermute | solution.py:427
  59.7 1.5 %collective-permute-start.21 = (f32[40,128]{1,0:T(8,128)S(1)}, f32[40,128]{1,0:T(8,128)S(1)}, u32[]{:S(2)}, u32[]{:S(2)}) collective-permute-start(f32[40,128]{1,0:T(8,128)S(1)} %slice.14), channel_id=1, source_target_pairs={{0,1},{1,0},{2,3},{3,2},{4,5},{5,4},{6,7},{7,6},{8,9},{9,8},{10,11... | collective-permute-start | bytes 61448 | tf_op jit(solution)/shard_map/ppermute | solution.py:427

commit v12 on v11

--- a/solution.py
+++ b/solution.py
@@ -226,11 +226,8 @@
         partial = partial + pair_sum(stacked(total), *split(basis_tile))
     for j in range(count_y):
         residual_a_ref[j], residual_b_ref[j] = pick(odd_x, totals[0, j], totals[1, j])
+    residual_a_ref[count_y] = partial
     partial_ref[...] = partial
-
-
-def tables_kernel(stiff_ref, mass_ref, table_ref):
-    split_tables(stiff_ref, mass_ref, table_ref, 0)
 
 
 def prepare_kernel(
@@ -240,11 +237,15 @@
     from_rest_a_ref,
     from_rest_b_ref,
     current_ref,
+    stiff_ref,
+    mass_ref,
     basis_ref,
+    table_ref,
 ):
     count_y, rest, _ = rest_a_ref.shape
     prior = rest + current_ref.shape[1]
     odd_x = flag_at(flags_ref, 1)
+    split_tables(stiff_ref, mass_ref, table_ref, 0)
     for j in range(count_y):
         rests = list(pick(odd_x, from_rest_a_ref[j], from_rest_b_ref[j]))
         rests[1:1] = pick(odd_x, rest_a_ref[j], rest_b_ref[j])
@@ -523,7 +524,7 @@
             stiff_tiles,
             mass_tiles,
         ),
-        [shape(count_y, block, side)] * 2
+        [shape(count_y + 1, block, side), shape(count_y, block, side)]
         + [shape(block, prior), shape(4 * wide, block, side)],
         [pltpu.VMEM((4 * wide, 2 * block, 2 * side), BF16)]
         + [pltpu.VMEM((kinds, 2 * side, 2 * side), BF16)]
@@ -532,19 +533,10 @@
         cost=pl.CostEstimate(flops=10**9, bytes_accessed=0, transcendentals=0),
     )
     count_py = lax.axis_size("py")
-    stiff_tiles, residual_a = lax.optimization_barrier((stiff_tiles, residual_a))
-    (table,) = call(
-        tables_kernel,
-        (stiff_tiles, mass_tiles),
-        [shape(kinds, 2 * side, 2 * side, dtype=BF16)],
-        cost=pl.CostEstimate(flops=10**9, bytes_accessed=0, transcendentals=0),
-    )
-    partial = total_over(partial, 2 * count_py, count_py * lax.axis_size("px"))
-    partial, table = lax.optimization_barrier((partial, table))
-    from_row_a, from_row_b = exchange(
-        jnp.concatenate([residual_a, partial[None]], axis=0), residual_b, "px"
-    )
-    partial = partial + from_row_a[-1]
+    from_row_a, from_row_b = exchange(residual_a, residual_b, "px")
+    partial = total_over(
+        partial + from_row_a[-1], 2 * count_py, count_py * lax.axis_size("px")
+    )
     partial, rest_side_a, rest_side_b = lax.optimization_barrier(
         (partial, rest_side_a, rest_side_b)
     )
@@ -555,10 +547,11 @@
     )
     from_side_a, from_side_b = exchange(side_a, side_b, "py")
     partial = total_over(partial + from_side_a[-1], 2, count_py)
-    (basis_parts,) = call(
+    basis_parts, table = call(
         prepare_kernel,
-        (flags, rest_a, rest_b, from_rest_a, from_rest_b, current),
-        [shape(4 * count_y, 2 * prior, side, dtype=BF16)],
+        (flags, rest_a, rest_b, from_rest_a, from_rest_b, current, stiff_tiles, mass_tiles),
+        [shape(4 * count_y, 2 * prior, side, dtype=BF16)]
+        + [shape(kinds, 2 * side, 2 * side, dtype=BF16)],
         cost=pl.CostEstimate(flops=10**9, bytes_accessed=0, transcendentals=0),
     )
     weighted_low, weighted_high, coupling, sent, kept = call(

time: 62.7 us -> 57.2 us (0.912)
  waiting for transfers between devices: 18.4 us -> 13.5 us
  starting transfers between devices: 33.1 us -> 32.4 us
    ppermute x7, waiting for transfers between devices: 3.37 us -> 0.51 us  [exchange(): lax.ppermute(message_a, axis, near)]
    ppermute x8, waiting for transfers between devices: 15 us -> 13 us  [swap(): return lax.ppermute(value, axes, pairs)]
    ppermute x8, starting transfers between devices: 13.1 us -> 11.8 us  [swap(): return lax.ppermute(value, axes, pairs)]
    ppermute x7, starting transfers between devices: 15.4 us -> 16 us  [exchange(): lax.ppermute(message_a, axis, near)]
    pallas_call x11 -> x10, Pallas kernels: 8.64 us -> 8.64 us  [call(): pl.pallas_call(kernel, out_shape=outputs, in_specs=specs, out_specs=[VMEM...]
  transfers between devices with their start and end apart: 22 -> 22, of which waited for: 10 -> 9; matrix products, arithmetic and copies ran while one was open for 0% -> 0% of each run, Pallas kernels for 7% -> 8%
where the time goes in v12:
time: 57.2 us; the launch traced here: 56.8 us
  starting transfers between devices  32.4 us (57%)
  waiting for transfers between devices  13.5 us (24%)
  Pallas kernels  8.64 us (15%)
  other arithmetic  1.2 us (2%)
  between operations  0.95 us (2%)
    ppermute x7, starting transfers between devices, exchange(): lax.ppermute(message_a, axis, near)  16 us
    ppermute x8, waiting for transfers between devices, swap(): return lax.ppermute(value, axes, pairs)  13 us
    ppermute x8, starting transfers between devices, swap(): return lax.ppermute(value, axes, pairs)  11.8 us
    pallas_call x10, Pallas kernels, call(): pl.pallas_call(kernel, out_shape=outputs, in_specs=specs, out_specs=[VMEM...  8.64 us
    ppermute x7, starting transfers between devices, exchange(): lax.ppermute(message_b, axis, pairs)  4.59 us
    concatenate x1, other arithmetic, shards(): vectors = jnp.concatenate([basis, previous.reshape(-1, side)], axis=0)  1.16 us
  transfers between devices with their start and end apart: 22, of which 9 were waited for; matrix products, arithmetic and copies ran while one was open for 0% of the time, Pallas kernels for 8%

profile of v12, /device:TPU:0, one launch (start us, length us, event | category | flops | bytes accessed | tf_op | source)
XLA Modules:
  0.0 56.8 jit_solution(16052870223437273362)
XLA Ops:
  0.7 1.2 %pad_maximum_fusion.vectors_ref = f32[1280,128]{1,0:T(8,128)S(1)} fusion(f32[256,128]{1,0:T(8,128)} %bitcast.24, f32[1024,128]{1,0:T(8,128)} %bitcast.23), kind=kLoop, calls=%fused_computation | loop fusion | flops 163840 | bytes 1310720 | tf_op jit(solution)/shard_map/concatenate | solution.py:465
  1.8 0.1 iota.7.flags_ref
  1.9 0.1 shard_map.93
  2.0 0.0 copy-start.2
  2.0 0.5 collective-permute-start.2
  2.5 0.7 %collective-permute-start.3 = (f32[2,64,128]{2,1,0:T(8,128)S(1)}, f32[2,64,128]{2,1,0:T(8,128)S(1)}, u32[]{:S(2)}, u32[]{:S(2)}) collective-permute-start(f32[2,64,128]{2,1,0:T(8,128)S(1)} %get-tuple-element.42), channel_id=1, source_target_pairs={{0,0},{1,2},{2,1},{3,3},{4,4},{5,6},{6,5},{7,7},{8,8},{9,10},{10,9... | collective-permute-start | bytes 196616 | tf_op jit(solution)/shard_map/ppermute | solution.py:436
  3.1 2.8 %collective-permute-start = (f32[4,64,128]{2,1,0:T(8,128)S(1)}, f32[4,64,128]{2,1,0:T(8,128)S(1)}, u32[]{:S(2)}, u32[]{:S(2)}) collective-permute-start(f32[4,64,128]{2,1,0:T(8,128)S(1)} %get-tuple-element.36.row_a_ref), channel_id=1, source_target_pairs={{0,4},{4,0},{8,12},{12,8},{1,5},{5,1},{9,13},{13,9},{2,6},{6,2},{1... | collective-permute-start | bytes 393224 | tf_op jit(solution)/shard_map/ppermute | solution.py:436
  5.9 0.7 %collective-permute-start.1 = (f32[4,64,128]{2,1,0:T(8,128)S(1)}, f32[4,64,128]{2,1,0:T(8,128)S(1)}, u32[]{:S(2)}, u32[]{:S(2)}) collective-permute-start(f32[4,64,128]{2,1,0:T(8,128)S(1)} %get-tuple-element.37.row_b_ref), channel_id=1, source_target_pairs={{0,0},{4,8},{8,4},{12,12},{1,1},{5,9},{9,5},{13,13},{2,2},{6,10},{... | collective-permute-start | bytes 393224 | tf_op jit(solution)/shard_map/ppermute | solution.py:436
  6.6 0.1 shard_map.94
  6.7 0.0 collective-permute-done.2.side_a_ref.from_side_a_ref
  6.7 0.0 collective-permute-done.3.side_b_ref.from_side_b_ref
  6.7 0.0 copy-start.1
  6.7 0.0 copy-start
  6.8 4.5 %collective-permute-start.4 = (f32[2,64,128]{2,1,0:T(8,128)S(1)}, f32[2,64,128]{2,1,0:T(8,128)S(1)}, u32[]{:S(2)}, u32[]{:S(2)}) collective-permute-start(f32[2,64,128]{2,1,0:T(8,128)S(1)} %get-tuple-element.43), channel_id=1, source_target_pairs={{0,4},{4,0},{8,12},{12,8},{1,5},{5,1},{9,13},{13,9},{2,6},{6,2},{1... | collective-permute-start | bytes 196616 | tf_op jit(solution)/shard_map/ppermute | solution.py:436
  11.2 0.7 %collective-permute-start.5 = (f32[2,64,128]{2,1,0:T(8,128)S(1)}, f32[2,64,128]{2,1,0:T(8,128)S(1)}, u32[]{:S(2)}, u32[]{:S(2)}) collective-permute-start(f32[2,64,128]{2,1,0:T(8,128)S(1)} %get-tuple-element.44), channel_id=1, source_target_pairs={{0,0},{4,8},{8,4},{12,12},{1,1},{5,9},{9,5},{13,13},{2,2},{6,10},{... | collective-permute-start | bytes 196616 | tf_op jit(solution)/shard_map/ppermute | solution.py:436
  11.9 1.3 %collective-permute-start.8 = (f32[4,96,128]{2,1,0:T(8,128)S(1)}, f32[4,96,128]{2,1,0:T(8,128)S(1)}, u32[]{:S(2)}, u32[]{:S(2)}) collective-permute-start(f32[4,96,128]{2,1,0:T(8,128)S(1)} %get-tuple-element.45.rest_a_ref.row_a_ref), channel_id=1, source_target_pairs={{0,4},{4,0},{8,12},{12,8},{1,5},{5,1},{9,13},{13,9},{2,6},{6,2},{1... | collective-permute-start | bytes 589832 | tf_op jit(solution)/shard_map/ppermute | solution.py:436
  13.2 0.2 collective-permute-done.4.from_corner_a_ref
  13.5 0.7 %collective-permute-start.9 = (f32[4,96,128]{2,1,0:T(8,128)S(1)}, f32[4,96,128]{2,1,0:T(8,128)S(1)}, u32[]{:S(2)}, u32[]{:S(2)}) collective-permute-start(f32[4,96,128]{2,1,0:T(8,128)S(1)} %get-tuple-element.46.rest_b_ref.row_b_ref), channel_id=1, source_target_pairs={{0,0},{4,8},{8,4},{12,12},{1,1},{5,9},{9,5},{13,13},{2,2},{6,10},{... | collective-permute-start | bytes 589832 | tf_op jit(solution)/shard_map/ppermute | solution.py:436
  14.1 0.0 collective-permute-done.5.from_corner_b_ref
  14.1 0.0 collective-permute-done.from_row_a_ref
  14.2 2.6 %shard_map.96 = (f32[5,32,128]{2,1,0:T(8,128)S(1)}, f32[4,32,128]{2,1,0:T(8,128)S(1)}, f32[32,128]{1,0:T(8,128)S(1)}, f32[24,32,128]{2,1,0:T(8,128)S(1)}) custom-call(s32[8,5]{1,0:T(8,128)S(1)} %bitcast.19, s32[8,5]{1,0:T(8,128)S(1)} %bitcast.21, f32[8,128]{1,0:T(8,128)S(1)} %iota.7.flags_ref, f32[4,64,128]{2,1,0:T(8,128)S(1)} %get-tuple-element.36.row_a_ref, ...), custom_call_target="tpu_custom_call" | custom-call | flops 1000000000 | tf_op jit(solution)/shard_map/pallas_call | solution.py:477
  16.9 3.3 %collective-permute-start.6 = (f32[5,32,128]{2,1,0:T(8,128)S(1)}, f32[5,32,128]{2,1,0:T(8,128)S(1)}, u32[]{:S(2)}, u32[]{:S(2)}) collective-permute-start(f32[5,32,128]{2,1,0:T(8,128)S(1)} %get-tuple-element.48.row_a_ref), channel_id=1, source_target_pairs={{0,4},{4,0},{8,12},{12,8},{1,5},{5,1},{9,13},{13,9},{2,6},{6,2},{1... | collective-permute-start | bytes 245768 | tf_op jit(solution)/shard_map/ppermute | solution.py:436
  20.2 0.7 %collective-permute-start.12 = (f32[4,32,128]{2,1,0:T(8,128)S(1)}, f32[4,32,128]{2,1,0:T(8,128)S(1)}, u32[]{:S(2)}, u32[]{:S(2)}) collective-permute-start(f32[4,32,128]{2,1,0:T(8,128)S(1)} %get-tuple-element.52.row_b_ref), channel_id=1, source_target_pairs={{0,0},{4,8},{8,4},{12,12},{1,1},{5,9},{9,5},{13,13},{2,2},{6,10},{... | collective-permute-start | bytes 196616 | tf_op jit(solution)/shard_map/ppermute | solution.py:436
  20.9 1.3 %collective-permute-start.10 = (f32[4,96,128]{2,1,0:T(8,128)S(1)}, f32[4,96,128]{2,1,0:T(8,128)S(1)}, u32[]{:S(2)}, u32[]{:S(2)}) collective-permute-start(f32[4,96,128]{2,1,0:T(8,128)S(1)} %get-tuple-element.49), channel_id=1, source_target_pairs={{0,1},{1,0},{2,3},{3,2},{4,5},{5,4},{6,7},{7,6},{8,9},{9,8},{10,11... | collective-permute-start | bytes 589832 | tf_op jit(solution)/shard_map/ppermute | solution.py:436
  22.2 0.7 %collective-permute-start.11 = (f32[4,96,128]{2,1,0:T(8,128)S(1)}, f32[4,96,128]{2,1,0:T(8,128)S(1)}, u32[]{:S(2)}, u32[]{:S(2)}) collective-permute-start(f32[4,96,128]{2,1,0:T(8,128)S(1)} %get-tuple-element.50), channel_id=1, source_target_pairs={{0,0},{1,2},{2,1},{3,3},{4,4},{5,6},{6,5},{7,7},{8,8},{9,10},{10,9... | collective-permute-start | bytes 589832 | tf_op jit(solution)/shard_map/ppermute | solution.py:436
  22.9 3.7 %collective-permute-start.7 = (f32[32,128]{1,0:T(8,128)S(1)}, f32[32,128]{1,0:T(8,128)S(1)}, u32[]{:S(2)}, u32[]{:S(2)}) collective-permute-start(f32[32,128]{1,0:T(8,128)S(1)} %fusion.1), channel_id=1, source_target_pairs={{0,8},{1,9},{2,10},{3,11},{4,12},{5,13},{6,14},{7,15},{8,0},{9,1},... | collective-permute-start | bytes 49160 | tf_op jit(solution)/shard_map/ppermute | solution.py:428
  26.7 1.7 %collective-permute-done.7 = f32[32,128]{1,0:T(8,128)S(1)} collective-permute-done((f32[32,128]{1,0:T(8,128)S(1)}, f32[32,128]{1,0:T(8,128)S(1)}, u32[]{:S(2)}, u32[]{:S(2)}) %collective-permute-start.7) | collective-permute-done | bytes 16416 | tf_op jit(solution)/shard_map/ppermute | solution.py:428
  28.4 2.3 %collective-permute-start.13 = (f32[5,32,128]{2,1,0:T(8,128)S(1)}, f32[5,32,128]{2,1,0:T(8,128)S(1)}, u32[]{:S(2)}, u32[]{:S(2)}) collective-permute-start(f32[5,32,128]{2,1,0:T(8,128)S(1)} %get-tuple-element.53), channel_id=1, source_target_pairs={{0,1},{1,0},{2,3},{3,2},{4,5},{5,4},{6,7},{7,6},{8,9},{9,8},{10,11... | collective-permute-start | bytes 245768 | tf_op jit(solution)/shard_map/ppermute | solution.py:436
  30.7 0.7 %collective-permute-start.15 = (f32[4,32,128]{2,1,0:T(8,128)S(1)}, f32[4,32,128]{2,1,0:T(8,128)S(1)}, u32[]{:S(2)}, u32[]{:S(2)}) collective-permute-start(f32[4,32,128]{2,1,0:T(8,128)S(1)} %get-tuple-element.54), channel_id=1, source_target_pairs={{0,0},{1,2},{2,1},{3,3},{4,4},{5,6},{6,5},{7,7},{8,8},{9,10},{10,9... | collective-permute-start | bytes 196616 | tf_op jit(solution)/shard_map/ppermute | solution.py:436
  31.4 0.3 collective-permute-done.13.from_side_a_ref
  31.7 2.7 %collective-permute-start.14 = (f32[32,128]{1,0:T(8,128)S(1)}, f32[32,128]{1,0:T(8,128)S(1)}, u32[]{:S(2)}, u32[]{:S(2)}) collective-permute-start(f32[32,128]{1,0:T(8,128)S(1)} %fusion), channel_id=1, source_target_pairs={{0,2},{1,3},{2,0},{3,1},{4,6},{5,7},{6,4},{7,5},{8,10},{9,11},{10,... | collective-permute-start | bytes 49160 | tf_op jit(solution)/shard_map/ppermute | solution.py:428
  34.4 0.3 shard_map.99
  34.7 2.0 %collective-permute-done.14 = f32[32,128]{1,0:T(8,128)S(1)} collective-permute-done((f32[32,128]{1,0:T(8,128)S(1)}, f32[32,128]{1,0:T(8,128)S(1)}, u32[]{:S(2)}, u32[]{:S(2)}) %collective-permute-start.14) | collective-permute-done | bytes 16416 | tf_op jit(solution)/shard_map/ppermute | solution.py:428
  36.7 2.9 %shard_map.100 = (f32[4,32,128]{2,1,0:T(8,128)S(1)}, f32[4,32,128]{2,1,0:T(8,128)S(1)}, f32[32,128]{1,0:T(8,128)}, f32[48,128]{1,0:T(8,128)S(1)}, f32[48,128]{1,0:T(8,128)S(1)}) custom-call(s32[8,5]{1,0:T(8,128)S(1)} %bitcast.20, s32[8,5]{1,0:T(8,128)S(1)} %bitcast.22, f32[8,128]{1,0:T(8,128)S(1)} %iota.7.flags_ref, f32[32,128]{1,0:T(8,128)S(1)} %add.50.partial_ref, ...), custom_call_target="tpu_custom_call" | custom-call | tf_op jit(solution)/shard_map/pallas_call | solution.py:477
  39.6 0.2 collective-permute-start.16
  39.8 1.1 %collective-permute-done.16 = f32[48,128]{1,0:T(8,128)S(1)} collective-permute-done((f32[48,128]{1,0:T(8,128)S(1)}, f32[48,128]{1,0:T(8,128)S(1)}, u32[]{:S(2)}, u32[]{:S(2)}) %collective-permute-start.16) | collective-permute-done | bytes 24608 | tf_op jit(solution)/shard_map/ppermute | solution.py:428
  40.8 4.1 %collective-permute-start.17 = (f32[48,128]{1,0:T(8,128)S(1)}, f32[48,128]{1,0:T(8,128)S(1)}, u32[]{:S(2)}, u32[]{:S(2)}) collective-permute-start(f32[48,128]{1,0:T(8,128)S(1)} %add.51), channel_id=1, source_target_pairs={{0,6},{1,7},{2,4},{3,5},{4,2},{5,3},{6,0},{7,1},{8,14},{9,15},{10,... | collective-permute-start | bytes 73736 | tf_op jit(solution)/shard_map/ppermute | solution.py:428
  44.9 0.6 %collective-permute-start.18 = (f32[48,128]{1,0:T(8,128)S(1)}, f32[48,128]{1,0:T(8,128)S(1)}, u32[]{:S(2)}, u32[]{:S(2)}) collective-permute-start(f32[48,128]{1,0:T(8,128)S(1)} %add.51), channel_id=1, source_target_pairs={{0,2},{1,3},{2,0},{3,1},{4,6},{5,7},{6,4},{7,5},{8,10},{9,11},{10,... | collective-permute-start | bytes 73736 | tf_op jit(solution)/shard_map/ppermute | solution.py:428
  45.5 0.0 collective-permute-start.19
  45.6 1.2 %collective-permute-done.17 = f32[48,128]{1,0:T(8,128)S(1)} collective-permute-done((f32[48,128]{1,0:T(8,128)S(1)}, f32[48,128]{1,0:T(8,128)S(1)}, u32[]{:S(2)}, u32[]{:S(2)}) %collective-permute-start.17) | collective-permute-done | bytes 24608 | tf_op jit(solution)/shard_map/ppermute | solution.py:428
  46.7 2.0 %collective-permute-done.18 = f32[48,128]{1,0:T(8,128)S(1)} collective-permute-done((f32[48,128]{1,0:T(8,128)S(1)}, f32[48,128]{1,0:T(8,128)S(1)}, u32[]{:S(2)}, u32[]{:S(2)}) %collective-permute-start.18) | collective-permute-done | bytes 24608 | tf_op jit(solution)/shard_map/ppermute | solution.py:428
  48.7 0.6 %collective-permute-done.19 = f32[48,128]{1,0:T(8,128)S(1)} collective-permute-done((f32[48,128]{1,0:T(8,128)S(1)}, f32[48,128]{1,0:T(8,128)S(1)}, u32[]{:S(2)}, u32[]{:S(2)}) %collective-permute-start.19) | collective-permute-done | bytes 24608 | tf_op jit(solution)/shard_map/ppermute | solution.py:428
  49.3 0.3 collective-permute-start.20
  49.7 4.5 %collective-permute-done.20 = f32[48,128]{1,0:T(8,128)S(1)} collective-permute-done((f32[48,128]{1,0:T(8,128)S(1)}, f32[48,128]{1,0:T(8,128)S(1)}, u32[]{:S(2)}, u32[]{:S(2)}) %collective-permute-start.20) | collective-permute-done | bytes 24608 | tf_op jit(solution)/shard_map/ppermute | solution.py:428
  54.1 0.1 collective-permute-start.21
  54.2 1.4 %shard_map.101.work_ref = f32[32,64]{1,0:T(8,128)S(1)} custom-call(f32[48,128]{1,0:T(8,128)S(1)} %add.55.sums_ref), custom_call_target="tpu_custom_call" | custom-call | flops 1000000000 | tf_op jit(solution)/shard_map/pallas_call | solution.py:477
  55.6 0.0 collective-permute-done.21.other_ref
  55.6 1.2 %shard_map.102 = (f32[256,128]{1,0:T(8,128)}, f32[32,32]{1,0:T(8,128)}, f32[2,32,160]{2,1,0:T(8,128)}) custom-call(f32[8,128]{1,0:T(8,128)S(1)} %iota.7.flags_ref, f32[32,64]{1,0:T(8,128)S(1)} %shard_map.101.work_ref, f32[48,128]{1,0:T(8,128)S(1)} %add.55.sums_ref, f32[40,128]{1,0:T(8,128)S(1)} %collective-permute-done.21.other_ref, ...), custom_call_target="tpu_custom_call" | custom-call | tf_op jit(solution)/shard_map/pallas_call | solution.py:477
  (25 shorter events, 0.2 us)
Async XLA Ops:
  1.9 12.3 %copy-start.3 = (f32[8,128,128]{2,1,0:T(8,128)S(1)}, f32[8,128,128]{2,1,0:T(8,128)}, u32[]{:S(2)}) copy-start(f32[8,128,128]{2,1,0:T(8,128)} %mass_ref.3) | copy-start | bytes 1572868
  2.0 12.2 %copy-start.2 = (f32[8,128,128]{2,1,0:T(8,128)S(1)}, f32[8,128,128]{2,1,0:T(8,128)}, u32[]{:S(2)}) copy-start(f32[8,128,128]{2,1,0:T(8,128)} %stiff_ref.3) | copy-start | bytes 1572868
  2.0 4.7 %collective-permute-start.2 = (f32[2,64,128]{2,1,0:T(8,128)S(1)}, f32[2,64,128]{2,1,0:T(8,128)S(1)}, u32[]{:S(2)}, u32[]{:S(2)}) collective-permute-start(f32[2,64,128]{2,1,0:T(8,128)S(1)} %get-tuple-element.38), channel_id=1, source_target_pairs={{0,1},{1,0},{2,3},{3,2},{4,5},{5,4},{6,7},{7,6},{8,9},{9,8},{10,11... | collective-permute-start | bytes 196616 | tf_op jit(solution)/shard_map/ppermute | solution.py:436
  2.5 4.2 %collective-permute-start.3 = (f32[2,64,128]{2,1,0:T(8,128)S(1)}, f32[2,64,128]{2,1,0:T(8,128)S(1)}, u32[]{:S(2)}, u32[]{:S(2)}) collective-permute-start(f32[2,64,128]{2,1,0:T(8,128)S(1)} %get-tuple-element.42), channel_id=1, source_target_pairs={{0,0},{1,2},{2,1},{3,3},{4,4},{5,6},{6,5},{7,7},{8,8},{9,10},{10,9... | collective-permute-start | bytes 196616 | tf_op jit(solution)/shard_map/ppermute | solution.py:436
  3.1 11.0 %collective-permute-start = (f32[4,64,128]{2,1,0:T(8,128)S(1)}, f32[4,64,128]{2,1,0:T(8,128)S(1)}, u32[]{:S(2)}, u32[]{:S(2)}) collective-permute-start(f32[4,64,128]{2,1,0:T(8,128)S(1)} %get-tuple-element.36.row_a_ref), channel_id=1, source_target_pairs={{0,4},{4,0},{8,12},{12,8},{1,5},{5,1},{9,13},{13,9},{2,6},{6,2},{1... | collective-permute-start | bytes 393224 | tf_op jit(solution)/shard_map/ppermute | solution.py:436
  5.9 8.2 %collective-permute-start.1 = (f32[4,64,128]{2,1,0:T(8,128)S(1)}, f32[4,64,128]{2,1,0:T(8,128)S(1)}, u32[]{:S(2)}, u32[]{:S(2)}) collective-permute-start(f32[4,64,128]{2,1,0:T(8,128)S(1)} %get-tuple-element.37.row_b_ref), channel_id=1, source_target_pairs={{0,0},{4,8},{8,4},{12,12},{1,1},{5,9},{9,5},{13,13},{2,2},{6,10},{... | collective-permute-start | bytes 393224 | tf_op jit(solution)/shard_map/ppermute | solution.py:436
  6.7 7.5 %copy-start.1 = (s32[5,2,4]{0,2,1:T(4,128)S(1)}, s32[5,2,4]{0,2,1:T(4,128)}, u32[]{:S(2)}) copy-start(s32[5,2,4]{0,2,1:T(4,128)} %param.9) | copy-start | bytes 484
  6.7 7.4 %copy-start = (s32[5,2,4]{0,2,1:T(4,128)S(1)}, s32[5,2,4]{0,2,1:T(4,128)}, u32[]{:S(2)}) copy-start(s32[5,2,4]{0,2,1:T(4,128)} %param.8) | copy-start | bytes 484
  6.8 6.7 %collective-permute-start.4 = (f32[2,64,128]{2,1,0:T(8,128)S(1)}, f32[2,64,128]{2,1,0:T(8,128)S(1)}, u32[]{:S(2)}, u32[]{:S(2)}) collective-permute-start(f32[2,64,128]{2,1,0:T(8,128)S(1)} %get-tuple-element.43), channel_id=1, source_target_pairs={{0,4},{4,0},{8,12},{12,8},{1,5},{5,1},{9,13},{13,9},{2,6},{6,2},{1... | collective-permute-start | bytes 196616 | tf_op jit(solution)/shard_map/ppermute | solution.py:436
  11.2 2.9 %collective-permute-start.5 = (f32[2,64,128]{2,1,0:T(8,128)S(1)}, f32[2,64,128]{2,1,0:T(8,128)S(1)}, u32[]{:S(2)}, u32[]{:S(2)}) collective-permute-start(f32[2,64,128]{2,1,0:T(8,128)S(1)} %get-tuple-element.44), channel_id=1, source_target_pairs={{0,0},{4,8},{8,4},{12,12},{1,1},{5,9},{9,5},{13,13},{2,2},{6,10},{... | collective-permute-start | bytes 196616 | tf_op jit(solution)/shard_map/ppermute | solution.py:436
  11.9 9.0 %collective-permute-start.8 = (f32[4,96,128]{2,1,0:T(8,128)S(1)}, f32[4,96,128]{2,1,0:T(8,128)S(1)}, u32[]{:S(2)}, u32[]{:S(2)}) collective-permute-start(f32[4,96,128]{2,1,0:T(8,128)S(1)} %get-tuple-element.45.rest_a_ref.row_a_ref), channel_id=1, source_target_pairs={{0,4},{4,0},{8,12},{12,8},{1,5},{5,1},{9,13},{13,9},{2,6},{6,2},{1... | collective-permute-start | bytes 589832 | tf_op jit(solution)/shard_map/ppermute | solution.py:436
  13.5 7.4 %collective-permute-start.9 = (f32[4,96,128]{2,1,0:T(8,128)S(1)}, f32[4,96,128]{2,1,0:T(8,128)S(1)}, u32[]{:S(2)}, u32[]{:S(2)}) collective-permute-start(f32[4,96,128]{2,1,0:T(8,128)S(1)} %get-tuple-element.46.rest_b_ref.row_b_ref), channel_id=1, source_target_pairs={{0,0},{4,8},{8,4},{12,12},{1,1},{5,9},{9,5},{13,13},{2,2},{6,10},{... | collective-permute-start | bytes 589832 | tf_op jit(solution)/shard_map/ppermute | solution.py:436
  16.9 6.0 %collective-permute-start.6 = (f32[5,32,128]{2,1,0:T(8,128)S(1)}, f32[5,32,128]{2,1,0:T(8,128)S(1)}, u32[]{:S(2)}, u32[]{:S(2)}) collective-permute-start(f32[5,32,128]{2,1,0:T(8,128)S(1)} %get-tuple-element.48.row_a_ref), channel_id=1, source_target_pairs={{0,4},{4,0},{8,12},{12,8},{1,5},{5,1},{9,13},{13,9},{2,6},{6,2},{1... | collective-permute-start | bytes 245768 | tf_op jit(solution)/shard_map/ppermute | solution.py:436
  20.2 8.2 %collective-permute-start.12 = (f32[4,32,128]{2,1,0:T(8,128)S(1)}, f32[4,32,128]{2,1,0:T(8,128)S(1)}, u32[]{:S(2)}, u32[]{:S(2)}) collective-permute-start(f32[4,32,128]{2,1,0:T(8,128)S(1)} %get-tuple-element.52.row_b_ref), channel_id=1, source_target_pairs={{0,0},{4,8},{8,4},{12,12},{1,1},{5,9},{9,5},{13,13},{2,2},{6,10},{... | collective-permute-start | bytes 196616 | tf_op jit(solution)/shard_map/ppermute | solution.py:436
  20.9 7.5 %collective-permute-start.10 = (f32[4,96,128]{2,1,0:T(8,128)S(1)}, f32[4,96,128]{2,1,0:T(8,128)S(1)}, u32[]{:S(2)}, u32[]{:S(2)}) collective-permute-start(f32[4,96,128]{2,1,0:T(8,128)S(1)} %get-tuple-element.49), channel_id=1, source_target_pairs={{0,1},{1,0},{2,3},{3,2},{4,5},{5,4},{6,7},{7,6},{8,9},{9,8},{10,11... | collective-permute-start | bytes 589832 | tf_op jit(solution)/shard_map/ppermute | solution.py:436
  22.2 6.2 %collective-permute-start.11 = (f32[4,96,128]{2,1,0:T(8,128)S(1)}, f32[4,96,128]{2,1,0:T(8,128)S(1)}, u32[]{:S(2)}, u32[]{:S(2)}) collective-permute-start(f32[4,96,128]{2,1,0:T(8,128)S(1)} %get-tuple-element.50), channel_id=1, source_target_pairs={{0,0},{1,2},{2,1},{3,3},{4,4},{5,6},{6,5},{7,7},{8,8},{9,10},{10,9... | collective-permute-start | bytes 589832 | tf_op jit(solution)/shard_map/ppermute | solution.py:436
  22.9 5.5 %collective-permute-start.7 = (f32[32,128]{1,0:T(8,128)S(1)}, f32[32,128]{1,0:T(8,128)S(1)}, u32[]{:S(2)}, u32[]{:S(2)}) collective-permute-start(f32[32,128]{1,0:T(8,128)S(1)} %fusion.1), channel_id=1, source_target_pairs={{0,8},{1,9},{2,10},{3,11},{4,12},{5,13},{6,14},{7,15},{8,0},{9,1},... | collective-permute-start | bytes 49160 | tf_op jit(solution)/shard_map/ppermute | solution.py:428
  28.4 3.2 %collective-permute-start.13 = (f32[5,32,128]{2,1,0:T(8,128)S(1)}, f32[5,32,128]{2,1,0:T(8,128)S(1)}, u32[]{:S(2)}, u32[]{:S(2)}) collective-permute-start(f32[5,32,128]{2,1,0:T(8,128)S(1)} %get-tuple-element.53), channel_id=1, source_target_pairs={{0,1},{1,0},{2,3},{3,2},{4,5},{5,4},{6,7},{7,6},{8,9},{9,8},{10,11... | collective-permute-start | bytes 245768 | tf_op jit(solution)/shard_map/ppermute | solution.py:436
  30.7 6.0 %collective-permute-start.15 = (f32[4,32,128]{2,1,0:T(8,128)S(1)}, f32[4,32,128]{2,1,0:T(8,128)S(1)}, u32[]{:S(2)}, u32[]{:S(2)}) collective-permute-start(f32[4,32,128]{2,1,0:T(8,128)S(1)} %get-tuple-element.54), channel_id=1, source_target_pairs={{0,0},{1,2},{2,1},{3,3},{4,4},{5,6},{6,5},{7,7},{8,8},{9,10},{10,9... | collective-permute-start | bytes 196616 | tf_op jit(solution)/shard_map/ppermute | solution.py:436
  31.7 5.0 %collective-permute-start.14 = (f32[32,128]{1,0:T(8,128)S(1)}, f32[32,128]{1,0:T(8,128)S(1)}, u32[]{:S(2)}, u32[]{:S(2)}) collective-permute-start(f32[32,128]{1,0:T(8,128)S(1)} %fusion), channel_id=1, source_target_pairs={{0,2},{1,3},{2,0},{3,1},{4,6},{5,7},{6,4},{7,5},{8,10},{9,11},{10,... | collective-permute-start | bytes 49160 | tf_op jit(solution)/shard_map/ppermute | solution.py:428
  39.6 1.3 %collective-permute-start.16 = (f32[48,128]{1,0:T(8,128)S(1)}, f32[48,128]{1,0:T(8,128)S(1)}, u32[]{:S(2)}, u32[]{:S(2)}) collective-permute-start(f32[48,128]{1,0:T(8,128)S(1)} %get-tuple-element.61), channel_id=1, source_target_pairs={{0,1},{1,0},{2,3},{3,2},{4,5},{5,4},{6,7},{7,6},{8,9},{9,8},{10,11... | collective-permute-start | bytes 73736 | tf_op jit(solution)/shard_map/ppermute | solution.py:428
  40.8 5.9 %collective-permute-start.17 = (f32[48,128]{1,0:T(8,128)S(1)}, f32[48,128]{1,0:T(8,128)S(1)}, u32[]{:S(2)}, u32[]{:S(2)}) collective-permute-start(f32[48,128]{1,0:T(8,128)S(1)} %add.51), channel_id=1, source_target_pairs={{0,6},{1,7},{2,4},{3,5},{4,2},{5,3},{6,0},{7,1},{8,14},{9,15},{10,... | collective-permute-start | bytes 73736 | tf_op jit(solution)/shard_map/ppermute | solution.py:428
  44.9 3.8 %collective-permute-start.18 = (f32[48,128]{1,0:T(8,128)S(1)}, f32[48,128]{1,0:T(8,128)S(1)}, u32[]{:S(2)}, u32[]{:S(2)}) collective-permute-start(f32[48,128]{1,0:T(8,128)S(1)} %add.51), channel_id=1, source_target_pairs={{0,2},{1,3},{2,0},{3,1},{4,6},{5,7},{6,4},{7,5},{8,10},{9,11},{10,... | collective-permute-start | bytes 73736 | tf_op jit(solution)/shard_map/ppermute | solution.py:428
  45.5 3.8 %collective-permute-start.19 = (f32[48,128]{1,0:T(8,128)S(1)}, f32[48,128]{1,0:T(8,128)S(1)}, u32[]{:S(2)}, u32[]{:S(2)}) collective-permute-start(f32[48,128]{1,0:T(8,128)S(1)} %add.51), channel_id=1, source_target_pairs={{0,4},{1,5},{2,6},{3,7},{4,0},{5,1},{6,2},{7,3},{8,12},{9,13},{10,... | collective-permute-start | bytes 73736 | tf_op jit(solution)/shard_map/ppermute | solution.py:428
  49.3 4.8 %collective-permute-start.20 = (f32[48,128]{1,0:T(8,128)S(1)}, f32[48,128]{1,0:T(8,128)S(1)}, u32[]{:S(2)}, u32[]{:S(2)}) collective-permute-start(f32[48,128]{1,0:T(8,128)S(1)} %add_add_fusion), channel_id=1, source_target_pairs={{0,8},{1,9},{2,10},{3,11},{4,12},{5,13},{6,14},{7,15},{8,0},{9,1},... | collective-permute-start | bytes 73736 | tf_op jit(solution)/shard_map/ppermute | solution.py:428
  54.1 1.5 %collective-permute-start.21 = (f32[40,128]{1,0:T(8,128)S(1)}, f32[40,128]{1,0:T(8,128)S(1)}, u32[]{:S(2)}, u32[]{:S(2)}) collective-permute-start(f32[40,128]{1,0:T(8,128)S(1)} %slice.14), channel_id=1, source_target_pairs={{0,1},{1,0},{2,3},{3,2},{4,5},{5,4},{6,7},{7,6},{8,9},{9,8},{10,11... | collective-permute-start | bytes 61448 | tf_op jit(solution)/shard_map/ppermute | solution.py:428

commit v13 on v12

--- a/solution.py
+++ b/solution.py
@@ -445,8 +445,10 @@
 
 def half_total(sent, kept):
     kept = kept + swap(sent, 1)
-    kept = (kept + swap(kept, 6)) + (swap(kept, 2) + swap(kept, 4))
-    return total_over(kept, 8, lax.axis_size(("px", "py")))
+    others = [swap(kept, mask) for mask in (2, 4, 6, 8, 10, 12, 14)]
+    pairs = [kept + others[0]] + [others[n] + others[n + 1] for n in (1, 3, 5)]
+    kept = (pairs[0] + pairs[1]) + (pairs[2] + pairs[3])
+    return total_over(kept, 16, lax.axis_size(("px", "py")))
 
 
 def shape(*dims, dtype=F32):
@@ -534,9 +536,13 @@
     )
     count_py = lax.axis_size("py")
     from_row_a, from_row_b = exchange(residual_a, residual_b, "px")
-    partial = total_over(
-        partial + from_row_a[-1], 2 * count_py, count_py * lax.axis_size("px")
-    )
+    if lax.axis_size("px") == 4:
+        far, cross = swap(partial, 2 * count_py), swap(partial, 3 * count_py)
+        partial = (partial + far) + (from_row_a[-1] + cross)
+    else:
+        partial = total_over(
+            partial + from_row_a[-1], 2 * count_py, count_py * lax.axis_size("px")
+        )
     partial, rest_side_a, rest_side_b = lax.optimization_barrier(
         (partial, rest_side_a, rest_side_b)
     )

time: 57.2 us -> 63.3 us (1.11)
  starting transfers between devices: 32.4 us -> 42.8 us
  waiting for transfers between devices: 13.5 us -> 9.28 us
    ppermute x8 -> x12, starting transfers between devices: 11.8 us -> 18.6 us  [swap(): return lax.ppermute(value, axes, pairs)]
    ppermute x8 -> x12, waiting for transfers between devices: 13 us -> 8.08 us  [swap(): return lax.ppermute(value, axes, pairs)]
    ppermute x7, starting transfers between devices: 16 us -> 19.6 us  [exchange(): lax.ppermute(message_a, axis, near)]
    ppermute x7, waiting for transfers between devices: 0.51 us -> 1.18 us  [exchange(): lax.ppermute(message_a, axis, near)]
  transfers between devices with their start and end apart: 22 -> 26, of which waited for: 9 -> 8; matrix products, arithmetic and copies ran while one was open for 0% -> 0% of each run, Pallas kernels for 8% -> 7%
where the time goes in v13:
time: 63.3 us; the launch traced here: 62.9 us
  starting transfers between devices  42.8 us (68%)
  waiting for transfers between devices  9.28 us (15%)
  Pallas kernels  8.65 us (14%)
  other arithmetic  1.2 us (2%)
  between operations  0.92 us (1%)
    ppermute x7, starting transfers between devices, exchange(): lax.ppermute(message_a, axis, near)  19.6 us
    ppermute x12, starting transfers between devices, swap(): return lax.ppermute(value, axes, pairs)  18.6 us
    pallas_call x10, Pallas kernels, call(): pl.pallas_call(kernel, out_shape=outputs, in_specs=specs, out_specs=[VMEM...  8.65 us
    ppermute x12, waiting for transfers between devices, swap(): return lax.ppermute(value, axes, pairs)  8.08 us
    ppermute x7, starting transfers between devices, exchange(): lax.ppermute(message_b, axis, pairs)  4.6 us
  transfers between devices with their start and end apart: 26, of which 8 were waited for; matrix products, arithmetic and copies ran while one was open for 0% of the time, Pallas kernels for 7%

profile of v13, /device:TPU:0, one launch (start us, length us, event | category | flops | bytes accessed | tf_op | source)
XLA Modules:
  0.0 62.9 jit_solution(11824798395769472148)
XLA Ops:
  0.7 1.2 %pad_maximum_fusion.vectors_ref = f32[1280,128]{1,0:T(8,128)S(1)} fusion(f32[256,128]{1,0:T(8,128)} %bitcast.26, f32[1024,128]{1,0:T(8,128)} %bitcast.25), kind=kLoop, calls=%fused_computation | loop fusion | flops 163840 | bytes 1310720 | tf_op jit(solution)/shard_map/concatenate | solution.py:467
  1.8 0.1 iota.7.flags_ref
  1.9 0.1 shard_map.93
  2.0 0.0 copy-start.2
  2.0 0.5 collective-permute-start.2
  2.5 0.7 %collective-permute-start.3 = (f32[2,64,128]{2,1,0:T(8,128)S(1)}, f32[2,64,128]{2,1,0:T(8,128)S(1)}, u32[]{:S(2)}, u32[]{:S(2)}) collective-permute-start(f32[2,64,128]{2,1,0:T(8,128)S(1)} %get-tuple-element.42), channel_id=1, source_target_pairs={{0,0},{1,2},{2,1},{3,3},{4,4},{5,6},{6,5},{7,7},{8,8},{9,10},{10,9... | collective-permute-start | bytes 196616 | tf_op jit(solution)/shard_map/ppermute | solution.py:436
  3.1 2.8 %collective-permute-start = (f32[4,64,128]{2,1,0:T(8,128)S(1)}, f32[4,64,128]{2,1,0:T(8,128)S(1)}, u32[]{:S(2)}, u32[]{:S(2)}) collective-permute-start(f32[4,64,128]{2,1,0:T(8,128)S(1)} %get-tuple-element.36.row_a_ref), channel_id=1, source_target_pairs={{0,4},{4,0},{8,12},{12,8},{1,5},{5,1},{9,13},{13,9},{2,6},{6,2},{1... | collective-permute-start | bytes 393224 | tf_op jit(solution)/shard_map/ppermute | solution.py:436
  5.9 0.7 %collective-permute-start.1 = (f32[4,64,128]{2,1,0:T(8,128)S(1)}, f32[4,64,128]{2,1,0:T(8,128)S(1)}, u32[]{:S(2)}, u32[]{:S(2)}) collective-permute-start(f32[4,64,128]{2,1,0:T(8,128)S(1)} %get-tuple-element.37.row_b_ref), channel_id=1, source_target_pairs={{0,0},{4,8},{8,4},{12,12},{1,1},{5,9},{9,5},{13,13},{2,2},{6,10},{... | collective-permute-start | bytes 393224 | tf_op jit(solution)/shard_map/ppermute | solution.py:436
  6.6 0.1 shard_map.94
  6.7 0.0 collective-permute-done.2.side_a_ref.from_side_a_ref
  6.7 0.0 copy-start.1
  6.7 0.0 copy-start
  6.8 4.5 %collective-permute-start.4 = (f32[2,64,128]{2,1,0:T(8,128)S(1)}, f32[2,64,128]{2,1,0:T(8,128)S(1)}, u32[]{:S(2)}, u32[]{:S(2)}) collective-permute-start(f32[2,64,128]{2,1,0:T(8,128)S(1)} %get-tuple-element.43), channel_id=1, source_target_pairs={{0,4},{4,0},{8,12},{12,8},{1,5},{5,1},{9,13},{13,9},{2,6},{6,2},{1... | collective-permute-start | bytes 196616 | tf_op jit(solution)/shard_map/ppermute | solution.py:436
  11.2 0.7 %collective-permute-start.5 = (f32[2,64,128]{2,1,0:T(8,128)S(1)}, f32[2,64,128]{2,1,0:T(8,128)S(1)}, u32[]{:S(2)}, u32[]{:S(2)}) collective-permute-start(f32[2,64,128]{2,1,0:T(8,128)S(1)} %get-tuple-element.44), channel_id=1, source_target_pairs={{0,0},{4,8},{8,4},{12,12},{1,1},{5,9},{9,5},{13,13},{2,2},{6,10},{... | collective-permute-start | bytes 196616 | tf_op jit(solution)/shard_map/ppermute | solution.py:436
  11.9 0.7 %collective-permute-start.10 = (f32[4,96,128]{2,1,0:T(8,128)S(1)}, f32[4,96,128]{2,1,0:T(8,128)S(1)}, u32[]{:S(2)}, u32[]{:S(2)}) collective-permute-start(f32[4,96,128]{2,1,0:T(8,128)S(1)} %get-tuple-element.46.rest_b_ref.row_b_ref), channel_id=1, source_target_pairs={{0,0},{4,8},{8,4},{12,12},{1,1},{5,9},{9,5},{13,13},{2,2},{6,10},{... | collective-permute-start | bytes 589832 | tf_op jit(solution)/shard_map/ppermute | solution.py:436
  12.6 0.9 %collective-permute-done.4.from_corner_a_ref = f32[2,64,128]{2,1,0:T(8,128)S(1)} collective-permute-done((f32[2,64,128]{2,1,0:T(8,128)S(1)}, f32[2,64,128]{2,1,0:T(8,128)S(1)}, u32[]{:S(2)}, u32[]{:S(2)}) %collective-permute-start.4) | collective-permute-done | bytes 65568 | tf_op jit(solution)/shard_map/ppermute | solution.py:436
  13.5 3.7 %collective-permute-start.9 = (f32[4,96,128]{2,1,0:T(8,128)S(1)}, f32[4,96,128]{2,1,0:T(8,128)S(1)}, u32[]{:S(2)}, u32[]{:S(2)}) collective-permute-start(f32[4,96,128]{2,1,0:T(8,128)S(1)} %get-tuple-element.45.rest_a_ref.row_a_ref), channel_id=1, source_target_pairs={{0,4},{4,0},{8,12},{12,8},{1,5},{5,1},{9,13},{13,9},{2,6},{6,2},{1... | collective-permute-start | bytes 589832 | tf_op jit(solution)/shard_map/ppermute | solution.py:436
  17.2 2.6 %shard_map.96 = (f32[5,32,128]{2,1,0:T(8,128)S(1)}, f32[4,32,128]{2,1,0:T(8,128)S(1)}, f32[32,128]{1,0:T(8,128)S(1)}, f32[24,32,128]{2,1,0:T(8,128)S(1)}) custom-call(s32[8,5]{1,0:T(8,128)S(1)} %bitcast.21, s32[8,5]{1,0:T(8,128)S(1)} %bitcast.23, f32[8,128]{1,0:T(8,128)S(1)} %iota.7.flags_ref, f32[4,64,128]{2,1,0:T(8,128)S(1)} %get-tuple-element.36.row_a_ref, ...), custom_call_target="tpu_custom_call" | custom-call | flops 1000000000 | tf_op jit(solution)/shard_map/pallas_call | solution.py:479
  19.9 0.3 collective-permute-start.7
  20.1 1.3 %collective-permute-start.6 = (f32[32,128]{1,0:T(8,128)S(1)}, f32[32,128]{1,0:T(8,128)S(1)}, u32[]{:S(2)}, u32[]{:S(2)}) collective-permute-start(f32[32,128]{1,0:T(8,128)S(1)} %get-tuple-element.47), channel_id=1, source_target_pairs={{0,8},{1,9},{2,10},{3,11},{4,12},{5,13},{6,14},{7,15},{8,0},{9,1},... | collective-permute-start | bytes 49160 | tf_op jit(solution)/shard_map/ppermute | solution.py:428
  21.4 2.9 %collective-permute-start.8 = (f32[32,128]{1,0:T(8,128)S(1)}, f32[32,128]{1,0:T(8,128)S(1)}, u32[]{:S(2)}, u32[]{:S(2)}) collective-permute-start(f32[32,128]{1,0:T(8,128)S(1)} %get-tuple-element.47), channel_id=1, source_target_pairs={{0,12},{1,13},{2,14},{3,15},{4,8},{5,9},{6,10},{7,11},{8,4},{9,5},... | collective-permute-start | bytes 49160 | tf_op jit(solution)/shard_map/ppermute | solution.py:428
  24.3 0.0 collective-permute-done.10.from_row_b_ref.from_rest_b_ref
  24.3 0.7 %collective-permute-start.13 = (f32[4,32,128]{2,1,0:T(8,128)S(1)}, f32[4,32,128]{2,1,0:T(8,128)S(1)}, u32[]{:S(2)}, u32[]{:S(2)}) collective-permute-start(f32[4,32,128]{2,1,0:T(8,128)S(1)} %get-tuple-element.52.row_b_ref), channel_id=1, source_target_pairs={{0,0},{4,8},{8,4},{12,12},{1,1},{5,9},{9,5},{13,13},{2,2},{6,10},{... | collective-permute-start | bytes 196616 | tf_op jit(solution)/shard_map/ppermute | solution.py:436
  25.0 0.7 %collective-permute-start.11 = (f32[4,96,128]{2,1,0:T(8,128)S(1)}, f32[4,96,128]{2,1,0:T(8,128)S(1)}, u32[]{:S(2)}, u32[]{:S(2)}) collective-permute-start(f32[4,96,128]{2,1,0:T(8,128)S(1)} %get-tuple-element.49), channel_id=1, source_target_pairs={{0,1},{1,0},{2,3},{3,2},{4,5},{5,4},{6,7},{7,6},{8,9},{9,8},{10,11... | collective-permute-start | bytes 589832 | tf_op jit(solution)/shard_map/ppermute | solution.py:436
  25.7 0.7 %collective-permute-start.12 = (f32[4,96,128]{2,1,0:T(8,128)S(1)}, f32[4,96,128]{2,1,0:T(8,128)S(1)}, u32[]{:S(2)}, u32[]{:S(2)}) collective-permute-start(f32[4,96,128]{2,1,0:T(8,128)S(1)} %get-tuple-element.50), channel_id=1, source_target_pairs={{0,0},{1,2},{2,1},{3,3},{4,4},{5,6},{6,5},{7,7},{8,8},{9,10},{10,9... | collective-permute-start | bytes 589832 | tf_op jit(solution)/shard_map/ppermute | solution.py:436
  26.4 0.5 collective-permute-done.8
  27.0 7.1 %collective-permute-start.14 = (f32[5,32,128]{2,1,0:T(8,128)S(1)}, f32[5,32,128]{2,1,0:T(8,128)S(1)}, u32[]{:S(2)}, u32[]{:S(2)}) collective-permute-start(f32[5,32,128]{2,1,0:T(8,128)S(1)} %get-tuple-element.53), channel_id=1, source_target_pairs={{0,1},{1,0},{2,3},{3,2},{4,5},{5,4},{6,7},{7,6},{8,9},{9,8},{10,11... | collective-permute-start | bytes 245768 | tf_op jit(solution)/shard_map/ppermute | solution.py:436
  34.2 0.7 %collective-permute-start.16 = (f32[4,32,128]{2,1,0:T(8,128)S(1)}, f32[4,32,128]{2,1,0:T(8,128)S(1)}, u32[]{:S(2)}, u32[]{:S(2)}) collective-permute-start(f32[4,32,128]{2,1,0:T(8,128)S(1)} %get-tuple-element.54), channel_id=1, source_target_pairs={{0,0},{1,2},{2,1},{3,3},{4,4},{5,6},{6,5},{7,7},{8,8},{9,10},{10,9... | collective-permute-start | bytes 196616 | tf_op jit(solution)/shard_map/ppermute | solution.py:436
  34.8 0.3 collective-permute-done.14.from_side_a_ref
  35.1 2.7 %collective-permute-start.15 = (f32[32,128]{1,0:T(8,128)S(1)}, f32[32,128]{1,0:T(8,128)S(1)}, u32[]{:S(2)}, u32[]{:S(2)}) collective-permute-start(f32[32,128]{1,0:T(8,128)S(1)} %fusion), channel_id=1, source_target_pairs={{0,2},{1,3},{2,0},{3,1},{4,6},{5,7},{6,4},{7,5},{8,10},{9,11},{10,... | collective-permute-start | bytes 49160 | tf_op jit(solution)/shard_map/ppermute | solution.py:428
  37.8 0.3 shard_map.99
  38.1 2.0 %collective-permute-done.15 = f32[32,128]{1,0:T(8,128)S(1)} collective-permute-done((f32[32,128]{1,0:T(8,128)S(1)}, f32[32,128]{1,0:T(8,128)S(1)}, u32[]{:S(2)}, u32[]{:S(2)}) %collective-permute-start.15) | collective-permute-done | bytes 16416 | tf_op jit(solution)/shard_map/ppermute | solution.py:428
  40.1 2.9 %shard_map.100 = (f32[4,32,128]{2,1,0:T(8,128)S(1)}, f32[4,32,128]{2,1,0:T(8,128)S(1)}, f32[32,128]{1,0:T(8,128)}, f32[48,128]{1,0:T(8,128)S(1)}, f32[48,128]{1,0:T(8,128)S(1)}) custom-call(s32[8,5]{1,0:T(8,128)S(1)} %bitcast.22, s32[8,5]{1,0:T(8,128)S(1)} %bitcast.24, f32[8,128]{1,0:T(8,128)S(1)} %iota.7.flags_ref, f32[32,128]{1,0:T(8,128)S(1)} %add.63.partial_ref, ...), custom_call_target="tpu_custom_call" | custom-call | tf_op jit(solution)/shard_map/pallas_call | solution.py:479
  43.0 0.4 collective-permute-start.17
  43.5 0.8 %collective-permute-done.17 = f32[48,128]{1,0:T(8,128)S(1)} collective-permute-done((f32[48,128]{1,0:T(8,128)S(1)}, f32[48,128]{1,0:T(8,128)S(1)}, u32[]{:S(2)}, u32[]{:S(2)}) %collective-permute-start.17) | collective-permute-done | bytes 24608 | tf_op jit(solution)/shard_map/ppermute | solution.py:428
  44.3 1.5 %collective-permute-start.18 = (f32[48,128]{1,0:T(8,128)S(1)}, f32[48,128]{1,0:T(8,128)S(1)}, u32[]{:S(2)}, u32[]{:S(2)}) collective-permute-start(f32[48,128]{1,0:T(8,128)S(1)} %add.64), channel_id=1, source_target_pairs={{0,2},{1,3},{2,0},{3,1},{4,6},{5,7},{6,4},{7,5},{8,10},{9,11},{10,... | collective-permute-start | bytes 73736 | tf_op jit(solution)/shard_map/ppermute | solution.py:428
  45.8 2.0 %collective-permute-start.19 = (f32[48,128]{1,0:T(8,128)S(1)}, f32[48,128]{1,0:T(8,128)S(1)}, u32[]{:S(2)}, u32[]{:S(2)}) collective-permute-start(f32[48,128]{1,0:T(8,128)S(1)} %add.64), channel_id=1, source_target_pairs={{0,4},{1,5},{2,6},{3,7},{4,0},{5,1},{6,2},{7,3},{8,12},{9,13},{10,... | collective-permute-start | bytes 73736 | tf_op jit(solution)/shard_map/ppermute | solution.py:428
  47.8 2.4 %collective-permute-start.21 = (f32[48,128]{1,0:T(8,128)S(1)}, f32[48,128]{1,0:T(8,128)S(1)}, u32[]{:S(2)}, u32[]{:S(2)}) collective-permute-start(f32[48,128]{1,0:T(8,128)S(1)} %add.64), channel_id=1, source_target_pairs={{0,8},{1,9},{2,10},{3,11},{4,12},{5,13},{6,14},{7,15},{8,0},{9,1},... | collective-permute-start | bytes 73736 | tf_op jit(solution)/shard_map/ppermute | solution.py:428
  50.2 1.5 %collective-permute-start.22 = (f32[48,128]{1,0:T(8,128)S(1)}, f32[48,128]{1,0:T(8,128)S(1)}, u32[]{:S(2)}, u32[]{:S(2)}) collective-permute-start(f32[48,128]{1,0:T(8,128)S(1)} %add.64), channel_id=1, source_target_pairs={{0,10},{1,11},{2,8},{3,9},{4,14},{5,15},{6,12},{7,13},{8,2},{9,3},... | collective-permute-start | bytes 73736 | tf_op jit(solution)/shard_map/ppermute | solution.py:428
  51.7 2.0 %collective-permute-start.23 = (f32[48,128]{1,0:T(8,128)S(1)}, f32[48,128]{1,0:T(8,128)S(1)}, u32[]{:S(2)}, u32[]{:S(2)}) collective-permute-start(f32[48,128]{1,0:T(8,128)S(1)} %add.64), channel_id=1, source_target_pairs={{0,12},{1,13},{2,14},{3,15},{4,8},{5,9},{6,10},{7,11},{8,4},{9,5},... | collective-permute-start | bytes 73736 | tf_op jit(solution)/shard_map/ppermute | solution.py:428
  53.7 1.8 %collective-permute-start.24 = (f32[48,128]{1,0:T(8,128)S(1)}, f32[48,128]{1,0:T(8,128)S(1)}, u32[]{:S(2)}, u32[]{:S(2)}) collective-permute-start(f32[48,128]{1,0:T(8,128)S(1)} %add.64), channel_id=1, source_target_pairs={{0,14},{1,15},{2,12},{3,13},{4,10},{5,11},{6,8},{7,9},{8,6},{9,7},... | collective-permute-start | bytes 73736 | tf_op jit(solution)/shard_map/ppermute | solution.py:428
  55.5 0.4 collective-permute-done.22
  55.9 1.5 %collective-permute-done.23 = f32[48,128]{1,0:T(8,128)S(1)} collective-permute-done((f32[48,128]{1,0:T(8,128)S(1)}, f32[48,128]{1,0:T(8,128)S(1)}, u32[]{:S(2)}, u32[]{:S(2)}) %collective-permute-start.23) | collective-permute-done | bytes 24608 | tf_op jit(solution)/shard_map/ppermute | solution.py:428
  57.4 2.7 %collective-permute-done.24 = f32[48,128]{1,0:T(8,128)S(1)} collective-permute-done((f32[48,128]{1,0:T(8,128)S(1)}, f32[48,128]{1,0:T(8,128)S(1)}, u32[]{:S(2)}, u32[]{:S(2)}) %collective-permute-start.24) | collective-permute-done | bytes 24608 | tf_op jit(solution)/shard_map/ppermute | solution.py:428
  60.2 0.1 collective-permute-start.25
  60.3 1.4 %shard_map.101.work_ref = f32[32,64]{1,0:T(8,128)S(1)} custom-call(f32[48,128]{1,0:T(8,128)S(1)} %add_add_fusion.sums_ref), custom_call_target="tpu_custom_call" | custom-call | flops 1000000000 | tf_op jit(solution)/shard_map/pallas_call | solution.py:479
  61.7 0.0 collective-permute-done.25.other_ref
  61.7 1.2 %shard_map.102 = (f32[256,128]{1,0:T(8,128)}, f32[32,32]{1,0:T(8,128)}, f32[2,32,160]{2,1,0:T(8,128)}) custom-call(f32[8,128]{1,0:T(8,128)S(1)} %iota.7.flags_ref, f32[32,64]{1,0:T(8,128)S(1)} %shard_map.101.work_ref, f32[48,128]{1,0:T(8,128)S(1)} %add_add_fusion.sums_ref, f32[40,128]{1,0:T(8,128)S(1)} %collective-permute-done.25.other_ref, ...), custom_call_target="tpu_custom_call" | custom-call | tf_op jit(solution)/shard_map/pallas_call | solution.py:479
  (31 shorter events, 0.2 us)
Async XLA Ops:
  1.9 15.3 %copy-start.3 = (f32[8,128,128]{2,1,0:T(8,128)S(1)}, f32[8,128,128]{2,1,0:T(8,128)}, u32[]{:S(2)}) copy-start(f32[8,128,128]{2,1,0:T(8,128)} %mass_ref.3) | copy-start | bytes 1572868
  2.0 15.2 %copy-start.2 = (f32[8,128,128]{2,1,0:T(8,128)S(1)}, f32[8,128,128]{2,1,0:T(8,128)}, u32[]{:S(2)}) copy-start(f32[8,128,128]{2,1,0:T(8,128)} %stiff_ref.3) | copy-start | bytes 1572868
  2.0 4.7 %collective-permute-start.2 = (f32[2,64,128]{2,1,0:T(8,128)S(1)}, f32[2,64,128]{2,1,0:T(8,128)S(1)}, u32[]{:S(2)}, u32[]{:S(2)}) collective-permute-start(f32[2,64,128]{2,1,0:T(8,128)S(1)} %get-tuple-element.38), channel_id=1, source_target_pairs={{0,1},{1,0},{2,3},{3,2},{4,5},{5,4},{6,7},{7,6},{8,9},{9,8},{10,11... | collective-permute-start | bytes 196616 | tf_op jit(solution)/shard_map/ppermute | solution.py:436
  2.5 4.2 %collective-permute-start.3 = (f32[2,64,128]{2,1,0:T(8,128)S(1)}, f32[2,64,128]{2,1,0:T(8,128)S(1)}, u32[]{:S(2)}, u32[]{:S(2)}) collective-permute-start(f32[2,64,128]{2,1,0:T(8,128)S(1)} %get-tuple-element.42), channel_id=1, source_target_pairs={{0,0},{1,2},{2,1},{3,3},{4,4},{5,6},{6,5},{7,7},{8,8},{9,10},{10,9... | collective-permute-start | bytes 196616 | tf_op jit(solution)/shard_map/ppermute | solution.py:436
  3.1 14.0 %collective-permute-start = (f32[4,64,128]{2,1,0:T(8,128)S(1)}, f32[4,64,128]{2,1,0:T(8,128)S(1)}, u32[]{:S(2)}, u32[]{:S(2)}) collective-permute-start(f32[4,64,128]{2,1,0:T(8,128)S(1)} %get-tuple-element.36.row_a_ref), channel_id=1, source_target_pairs={{0,4},{4,0},{8,12},{12,8},{1,5},{5,1},{9,13},{13,9},{2,6},{6,2},{1... | collective-permute-start | bytes 393224 | tf_op jit(solution)/shard_map/ppermute | solution.py:436
  5.9 11.2 %collective-permute-start.1 = (f32[4,64,128]{2,1,0:T(8,128)S(1)}, f32[4,64,128]{2,1,0:T(8,128)S(1)}, u32[]{:S(2)}, u32[]{:S(2)}) collective-permute-start(f32[4,64,128]{2,1,0:T(8,128)S(1)} %get-tuple-element.37.row_b_ref), channel_id=1, source_target_pairs={{0,0},{4,8},{8,4},{12,12},{1,1},{5,9},{9,5},{13,13},{2,2},{6,10},{... | collective-permute-start | bytes 393224 | tf_op jit(solution)/shard_map/ppermute | solution.py:436
  6.7 10.5 %copy-start.1 = (s32[5,2,4]{0,2,1:T(4,128)S(1)}, s32[5,2,4]{0,2,1:T(4,128)}, u32[]{:S(2)}) copy-start(s32[5,2,4]{0,2,1:T(4,128)} %param.9) | copy-start | bytes 484
  6.7 10.5 %copy-start = (s32[5,2,4]{0,2,1:T(4,128)S(1)}, s32[5,2,4]{0,2,1:T(4,128)}, u32[]{:S(2)}) copy-start(s32[5,2,4]{0,2,1:T(4,128)} %param.8) | copy-start | bytes 484
  6.8 6.7 %collective-permute-start.4 = (f32[2,64,128]{2,1,0:T(8,128)S(1)}, f32[2,64,128]{2,1,0:T(8,128)S(1)}, u32[]{:S(2)}, u32[]{:S(2)}) collective-permute-start(f32[2,64,128]{2,1,0:T(8,128)S(1)} %get-tuple-element.43), channel_id=1, source_target_pairs={{0,4},{4,0},{8,12},{12,8},{1,5},{5,1},{9,13},{13,9},{2,6},{6,2},{1... | collective-permute-start | bytes 196616 | tf_op jit(solution)/shard_map/ppermute | solution.py:436
  11.2 6.0 %collective-permute-start.5 = (f32[2,64,128]{2,1,0:T(8,128)S(1)}, f32[2,64,128]{2,1,0:T(8,128)S(1)}, u32[]{:S(2)}, u32[]{:S(2)}) collective-permute-start(f32[2,64,128]{2,1,0:T(8,128)S(1)} %get-tuple-element.44), channel_id=1, source_target_pairs={{0,0},{4,8},{8,4},{12,12},{1,1},{5,9},{9,5},{13,13},{2,2},{6,10},{... | collective-permute-start | bytes 196616 | tf_op jit(solution)/shard_map/ppermute | solution.py:436
  11.9 12.5 %collective-permute-start.10 = (f32[4,96,128]{2,1,0:T(8,128)S(1)}, f32[4,96,128]{2,1,0:T(8,128)S(1)}, u32[]{:S(2)}, u32[]{:S(2)}) collective-permute-start(f32[4,96,128]{2,1,0:T(8,128)S(1)} %get-tuple-element.46.rest_b_ref.row_b_ref), channel_id=1, source_target_pairs={{0,0},{4,8},{8,4},{12,12},{1,1},{5,9},{9,5},{13,13},{2,2},{6,10},{... | collective-permute-start | bytes 589832 | tf_op jit(solution)/shard_map/ppermute | solution.py:436
  13.5 11.5 %collective-permute-start.9 = (f32[4,96,128]{2,1,0:T(8,128)S(1)}, f32[4,96,128]{2,1,0:T(8,128)S(1)}, u32[]{:S(2)}, u32[]{:S(2)}) collective-permute-start(f32[4,96,128]{2,1,0:T(8,128)S(1)} %get-tuple-element.45.rest_a_ref.row_a_ref), channel_id=1, source_target_pairs={{0,4},{4,0},{8,12},{12,8},{1,5},{5,1},{9,13},{13,9},{2,6},{6,2},{1... | collective-permute-start | bytes 589832 | tf_op jit(solution)/shard_map/ppermute | solution.py:436
  19.9 7.1 %collective-permute-start.7 = (f32[5,32,128]{2,1,0:T(8,128)S(1)}, f32[5,32,128]{2,1,0:T(8,128)S(1)}, u32[]{:S(2)}, u32[]{:S(2)}) collective-permute-start(f32[5,32,128]{2,1,0:T(8,128)S(1)} %get-tuple-element.48.row_a_ref), channel_id=1, source_target_pairs={{0,4},{4,0},{8,12},{12,8},{1,5},{5,1},{9,13},{13,9},{2,6},{6,2},{1... | collective-permute-start | bytes 245768 | tf_op jit(solution)/shard_map/ppermute | solution.py:436
  20.1 5.6 %collective-permute-start.6 = (f32[32,128]{1,0:T(8,128)S(1)}, f32[32,128]{1,0:T(8,128)S(1)}, u32[]{:S(2)}, u32[]{:S(2)}) collective-permute-start(f32[32,128]{1,0:T(8,128)S(1)} %get-tuple-element.47), channel_id=1, source_target_pairs={{0,8},{1,9},{2,10},{3,11},{4,12},{5,13},{6,14},{7,15},{8,0},{9,1},... | collective-permute-start | bytes 49160 | tf_op jit(solution)/shard_map/ppermute | solution.py:428
  21.4 5.5 %collective-permute-start.8 = (f32[32,128]{1,0:T(8,128)S(1)}, f32[32,128]{1,0:T(8,128)S(1)}, u32[]{:S(2)}, u32[]{:S(2)}) collective-permute-start(f32[32,128]{1,0:T(8,128)S(1)} %get-tuple-element.47), channel_id=1, source_target_pairs={{0,12},{1,13},{2,14},{3,15},{4,8},{5,9},{6,10},{7,11},{8,4},{9,5},... | collective-permute-start | bytes 49160 | tf_op jit(solution)/shard_map/ppermute | solution.py:428
  24.3 2.7 %collective-permute-start.13 = (f32[4,32,128]{2,1,0:T(8,128)S(1)}, f32[4,32,128]{2,1,0:T(8,128)S(1)}, u32[]{:S(2)}, u32[]{:S(2)}) collective-permute-start(f32[4,32,128]{2,1,0:T(8,128)S(1)} %get-tuple-element.52.row_b_ref), channel_id=1, source_target_pairs={{0,0},{4,8},{8,4},{12,12},{1,1},{5,9},{9,5},{13,13},{2,2},{6,10},{... | collective-permute-start | bytes 196616 | tf_op jit(solution)/shard_map/ppermute | solution.py:436
  25.0 1.9 %collective-permute-start.11 = (f32[4,96,128]{2,1,0:T(8,128)S(1)}, f32[4,96,128]{2,1,0:T(8,128)S(1)}, u32[]{:S(2)}, u32[]{:S(2)}) collective-permute-start(f32[4,96,128]{2,1,0:T(8,128)S(1)} %get-tuple-element.49), channel_id=1, source_target_pairs={{0,1},{1,0},{2,3},{3,2},{4,5},{5,4},{6,7},{7,6},{8,9},{9,8},{10,11... | collective-permute-start | bytes 589832 | tf_op jit(solution)/shard_map/ppermute | solution.py:436
  25.7 1.2 %collective-permute-start.12 = (f32[4,96,128]{2,1,0:T(8,128)S(1)}, f32[4,96,128]{2,1,0:T(8,128)S(1)}, u32[]{:S(2)}, u32[]{:S(2)}) collective-permute-start(f32[4,96,128]{2,1,0:T(8,128)S(1)} %get-tuple-element.50), channel_id=1, source_target_pairs={{0,0},{1,2},{2,1},{3,3},{4,4},{5,6},{6,5},{7,7},{8,8},{9,10},{10,9... | collective-permute-start | bytes 589832 | tf_op jit(solution)/shard_map/ppermute | solution.py:436
  27.0 8.1 %collective-permute-start.14 = (f32[5,32,128]{2,1,0:T(8,128)S(1)}, f32[5,32,128]{2,1,0:T(8,128)S(1)}, u32[]{:S(2)}, u32[]{:S(2)}) collective-permute-start(f32[5,32,128]{2,1,0:T(8,128)S(1)} %get-tuple-element.53), channel_id=1, source_target_pairs={{0,1},{1,0},{2,3},{3,2},{4,5},{5,4},{6,7},{7,6},{8,9},{9,8},{10,11... | collective-permute-start | bytes 245768 | tf_op jit(solution)/shard_map/ppermute | solution.py:436
  34.2 6.0 %collective-permute-start.16 = (f32[4,32,128]{2,1,0:T(8,128)S(1)}, f32[4,32,128]{2,1,0:T(8,128)S(1)}, u32[]{:S(2)}, u32[]{:S(2)}) collective-permute-start(f32[4,32,128]{2,1,0:T(8,128)S(1)} %get-tuple-element.54), channel_id=1, source_target_pairs={{0,0},{1,2},{2,1},{3,3},{4,4},{5,6},{6,5},{7,7},{8,8},{9,10},{10,9... | collective-permute-start | bytes 196616 | tf_op jit(solution)/shard_map/ppermute | solution.py:436
  35.1 5.0 %collective-permute-start.15 = (f32[32,128]{1,0:T(8,128)S(1)}, f32[32,128]{1,0:T(8,128)S(1)}, u32[]{:S(2)}, u32[]{:S(2)}) collective-permute-start(f32[32,128]{1,0:T(8,128)S(1)} %fusion), channel_id=1, source_target_pairs={{0,2},{1,3},{2,0},{3,1},{4,6},{5,7},{6,4},{7,5},{8,10},{9,11},{10,... | collective-permute-start | bytes 49160 | tf_op jit(solution)/shard_map/ppermute | solution.py:428
  43.0 1.3 %collective-permute-start.17 = (f32[48,128]{1,0:T(8,128)S(1)}, f32[48,128]{1,0:T(8,128)S(1)}, u32[]{:S(2)}, u32[]{:S(2)}) collective-permute-start(f32[48,128]{1,0:T(8,128)S(1)} %get-tuple-element.61), channel_id=1, source_target_pairs={{0,1},{1,0},{2,3},{3,2},{4,5},{5,4},{6,7},{7,6},{8,9},{9,8},{10,11... | collective-permute-start | bytes 73736 | tf_op jit(solution)/shard_map/ppermute | solution.py:428
  44.3 7.4 %collective-permute-start.18 = (f32[48,128]{1,0:T(8,128)S(1)}, f32[48,128]{1,0:T(8,128)S(1)}, u32[]{:S(2)}, u32[]{:S(2)}) collective-permute-start(f32[48,128]{1,0:T(8,128)S(1)} %add.64), channel_id=1, source_target_pairs={{0,2},{1,3},{2,0},{3,1},{4,6},{5,7},{6,4},{7,5},{8,10},{9,11},{10,... | collective-permute-start | bytes 73736 | tf_op jit(solution)/shard_map/ppermute | solution.py:428
  45.8 7.8 %collective-permute-start.19 = (f32[48,128]{1,0:T(8,128)S(1)}, f32[48,128]{1,0:T(8,128)S(1)}, u32[]{:S(2)}, u32[]{:S(2)}) collective-permute-start(f32[48,128]{1,0:T(8,128)S(1)} %add.64), channel_id=1, source_target_pairs={{0,4},{1,5},{2,6},{3,7},{4,0},{5,1},{6,2},{7,3},{8,12},{9,13},{10,... | collective-permute-start | bytes 73736 | tf_op jit(solution)/shard_map/ppermute | solution.py:428
  47.8 7.7 %collective-permute-start.20 = (f32[48,128]{1,0:T(8,128)S(1)}, f32[48,128]{1,0:T(8,128)S(1)}, u32[]{:S(2)}, u32[]{:S(2)}) collective-permute-start(f32[48,128]{1,0:T(8,128)S(1)} %add.64), channel_id=1, source_target_pairs={{0,6},{1,7},{2,4},{3,5},{4,2},{5,3},{6,0},{7,1},{8,14},{9,15},{10,... | collective-permute-start | bytes 73736 | tf_op jit(solution)/shard_map/ppermute | solution.py:428
  47.8 7.7 %collective-permute-start.21 = (f32[48,128]{1,0:T(8,128)S(1)}, f32[48,128]{1,0:T(8,128)S(1)}, u32[]{:S(2)}, u32[]{:S(2)}) collective-permute-start(f32[48,128]{1,0:T(8,128)S(1)} %add.64), channel_id=1, source_target_pairs={{0,8},{1,9},{2,10},{3,11},{4,12},{5,13},{6,14},{7,15},{8,0},{9,1},... | collective-permute-start | bytes 73736 | tf_op jit(solution)/shard_map/ppermute | solution.py:428
  50.2 5.7 %collective-permute-start.22 = (f32[48,128]{1,0:T(8,128)S(1)}, f32[48,128]{1,0:T(8,128)S(1)}, u32[]{:S(2)}, u32[]{:S(2)}) collective-permute-start(f32[48,128]{1,0:T(8,128)S(1)} %add.64), channel_id=1, source_target_pairs={{0,10},{1,11},{2,8},{3,9},{4,14},{5,15},{6,12},{7,13},{8,2},{9,3},... | collective-permute-start | bytes 73736 | tf_op jit(solution)/shard_map/ppermute | solution.py:428
  51.7 5.7 %collective-permute-start.23 = (f32[48,128]{1,0:T(8,128)S(1)}, f32[48,128]{1,0:T(8,128)S(1)}, u32[]{:S(2)}, u32[]{:S(2)}) collective-permute-start(f32[48,128]{1,0:T(8,128)S(1)} %add.64), channel_id=1, source_target_pairs={{0,12},{1,13},{2,14},{3,15},{4,8},{5,9},{6,10},{7,11},{8,4},{9,5},... | collective-permute-start | bytes 73736 | tf_op jit(solution)/shard_map/ppermute | solution.py:428
  53.7 6.5 %collective-permute-start.24 = (f32[48,128]{1,0:T(8,128)S(1)}, f32[48,128]{1,0:T(8,128)S(1)}, u32[]{:S(2)}, u32[]{:S(2)}) collective-permute-start(f32[48,128]{1,0:T(8,128)S(1)} %add.64), channel_id=1, source_target_pairs={{0,14},{1,15},{2,12},{3,13},{4,10},{5,11},{6,8},{7,9},{8,6},{9,7},... | collective-permute-start | bytes 73736 | tf_op jit(solution)/shard_map/ppermute | solution.py:428
  60.2 1.5 %collective-permute-start.25 = (f32[40,128]{1,0:T(8,128)S(1)}, f32[40,128]{1,0:T(8,128)S(1)}, u32[]{:S(2)}, u32[]{:S(2)}) collective-permute-start(f32[40,128]{1,0:T(8,128)S(1)} %slice.14), channel_id=1, source_target_pairs={{0,1},{1,0},{2,3},{3,2},{4,5},{5,4},{6,7},{7,6},{8,9},{9,8},{10,11... | collective-permute-start | bytes 61448 | tf_op jit(solution)/shard_map/ppermute | solution.py:428

commit v14 on v12

--- a/solution.py
+++ b/solution.py
@@ -429,11 +429,15 @@
 
 
 def exchange(message_a, message_b, axis):
-    count = lax.axis_size(axis)
-    pairs = [(i, ((i + 1) ^ 1) - 1) for i in range(count)]
-    pairs = [(i, j if 0 <= j < count else i) for i, j in pairs]
+    cases, count = lax.axis_size("case"), lax.axis_size(axis)
     near = [(i, i ^ 1) for i in range(count)]
-    return lax.ppermute(message_a, axis, near), lax.ppermute(message_b, axis, pairs)
+    pairs = []
+    for case in range(cases):
+        for i in range(count):
+            j = ((i + 1) ^ 1) - 1
+            target = (case, j) if 0 <= j < count else ((case ^ 1) % cases, i)
+            pairs.append((case * count + i, target[0] * count + target[1]))
+    return lax.ppermute(message_a, axis, near), lax.ppermute(message_b, ("case", axis), pairs)
 
 
 def total_over(value, first, last):

time: 57.2 us -> 50.2 us (0.88)
  starting transfers between devices: 32.4 us -> 26.2 us
    ppermute x7, starting transfers between devices: 16 us -> 8 us  [exchange(): lax.ppermute(message_a, axis, near)]
    ppermute x7, starting transfers between devices: 4.59 us -> 8.78 us  [exchange(): lax.ppermute(message_b, ('case', axis), pairs)]
    ppermute x8, starting transfers between devices: 11.8 us -> 9.41 us  [swap(): return lax.ppermute(value, axes, pairs)]
    ppermute x8, waiting for transfers between devices: 13 us -> 11.8 us  [swap(): return lax.ppermute(value, axes, pairs)]
  transfers between devices with their start and end apart: 22 -> 22, of which waited for: 9 -> 11; matrix products, arithmetic and copies ran while one was open for 0% -> 0% of each run, Pallas kernels for 8% -> 9%
where the time goes in v14:
time: 50.2 us; the launch traced here: 50 us
  starting transfers between devices  26.2 us (52%)
  waiting for transfers between devices  13 us (26%)
  Pallas kernels  8.63 us (17%)
  other arithmetic  1.2 us (2%)
  between operations  0.84 us (2%)
    ppermute x8, waiting for transfers between devices, swap(): return lax.ppermute(value, axes, pairs)  11.8 us
    ppermute x8, starting transfers between devices, swap(): return lax.ppermute(value, axes, pairs)  9.41 us
    ppermute x7, starting transfers between devices, exchange(): lax.ppermute(message_b, ('case', axis), pairs)  8.78 us
    pallas_call x10, Pallas kernels, call(): pl.pallas_call(kernel, out_shape=outputs, in_specs=specs, out_specs=[VMEM...  8.63 us
    ppermute x7, starting transfers between devices, exchange(): lax.ppermute(message_a, axis, near)  8 us
    concatenate x1, other arithmetic, shards(): vectors = jnp.concatenate([basis, previous.reshape(-1, side)], axis=0)  1.16 us
    ppermute x7, waiting for transfers between devices, exchange(): lax.ppermute(message_a, axis, near)  1.02 us
  transfers between devices with their start and end apart: 22, of which 11 were waited for; matrix products, arithmetic and copies ran while one was open for 0% of the time, Pallas kernels for 9%

profile of v14, /device:TPU:0, one launch (start us, length us, event | category | flops | bytes accessed | tf_op | source)
XLA Modules:
  0.0 50.0 jit_solution(17730910440537267685)
XLA Ops:
  0.7 1.2 %pad_maximum_fusion.vectors_ref = f32[1280,128]{1,0:T(8,128)S(1)} fusion(f32[256,128]{1,0:T(8,128)} %bitcast.24, f32[1024,128]{1,0:T(8,128)} %bitcast.23), kind=kLoop, calls=%fused_computation | loop fusion | flops 163840 | bytes 1310720 | tf_op jit(solution)/shard_map/concatenate | solution.py:469
  1.8 0.1 iota.7.flags_ref
  1.9 0.1 shard_map.93
  2.0 0.0 copy-start.2
  2.0 0.5 %collective-permute-start.2 = (f32[2,64,128]{2,1,0:T(8,128)S(1)}, f32[2,64,128]{2,1,0:T(8,128)S(1)}, u32[]{:S(2)}, u32[]{:S(2)}) collective-permute-start(f32[2,64,128]{2,1,0:T(8,128)S(1)} %get-tuple-element.38), channel_id=1, source_target_pairs={{0,1},{1,0},{2,3},{3,2},{4,5},{5,4},{6,7},{7,6},{8,9},{9,8},{10,11... | collective-permute-start | bytes 196616 | tf_op jit(solution)/shard_map/ppermute | solution.py:440
  2.5 2.6 %collective-permute-start.3 = (f32[2,64,128]{2,1,0:T(8,128)S(1)}, f32[2,64,128]{2,1,0:T(8,128)S(1)}, u32[]{:S(2)}, u32[]{:S(2)}) collective-permute-start(f32[2,64,128]{2,1,0:T(8,128)S(1)} %get-tuple-element.42), channel_id=1, source_target_pairs={{0,16},{1,2},{2,1},{3,19},{16,0},{17,18},{18,17},{19,3},{4,20},{5,... | collective-permute-start | bytes 196616 | tf_op jit(solution)/shard_map/ppermute | solution.py:440
  5.1 1.6 %collective-permute-start = (f32[4,64,128]{2,1,0:T(8,128)S(1)}, f32[4,64,128]{2,1,0:T(8,128)S(1)}, u32[]{:S(2)}, u32[]{:S(2)}) collective-permute-start(f32[4,64,128]{2,1,0:T(8,128)S(1)} %get-tuple-element.36.row_a_ref), channel_id=1, source_target_pairs={{0,4},{4,0},{8,12},{12,8},{1,5},{5,1},{9,13},{13,9},{2,6},{6,2},{1... | collective-permute-start | bytes 393224 | tf_op jit(solution)/shard_map/ppermute | solution.py:440
  6.7 0.5 %collective-permute-start.1 = (f32[4,64,128]{2,1,0:T(8,128)S(1)}, f32[4,64,128]{2,1,0:T(8,128)S(1)}, u32[]{:S(2)}, u32[]{:S(2)}) collective-permute-start(f32[4,64,128]{2,1,0:T(8,128)S(1)} %get-tuple-element.37.row_b_ref), channel_id=1, source_target_pairs={{0,16},{4,8},{8,4},{12,28},{16,0},{20,24},{24,20},{28,12},{1,17},{... | collective-permute-start | bytes 393224 | tf_op jit(solution)/shard_map/ppermute | solution.py:440
  7.2 0.1 shard_map.94
  7.2 0.0 collective-permute-done.2.side_a_ref.from_side_a_ref
  7.2 0.1 collective-permute-done.3.side_b_ref.from_side_b_ref
  7.4 0.0 copy-start
  7.4 2.7 %collective-permute-start.4 = (f32[2,64,128]{2,1,0:T(8,128)S(1)}, f32[2,64,128]{2,1,0:T(8,128)S(1)}, u32[]{:S(2)}, u32[]{:S(2)}) collective-permute-start(f32[2,64,128]{2,1,0:T(8,128)S(1)} %get-tuple-element.43), channel_id=1, source_target_pairs={{0,4},{4,0},{8,12},{12,8},{1,5},{5,1},{9,13},{13,9},{2,6},{6,2},{1... | collective-permute-start | bytes 196616 | tf_op jit(solution)/shard_map/ppermute | solution.py:440
  10.0 1.0 %collective-permute-start.5 = (f32[2,64,128]{2,1,0:T(8,128)S(1)}, f32[2,64,128]{2,1,0:T(8,128)S(1)}, u32[]{:S(2)}, u32[]{:S(2)}) collective-permute-start(f32[2,64,128]{2,1,0:T(8,128)S(1)} %get-tuple-element.44), channel_id=1, source_target_pairs={{0,16},{4,8},{8,4},{12,28},{16,0},{20,24},{24,20},{28,12},{1,17},{... | collective-permute-start | bytes 196616 | tf_op jit(solution)/shard_map/ppermute | solution.py:440
  11.0 1.6 %collective-permute-start.8 = (f32[4,96,128]{2,1,0:T(8,128)S(1)}, f32[4,96,128]{2,1,0:T(8,128)S(1)}, u32[]{:S(2)}, u32[]{:S(2)}) collective-permute-start(f32[4,96,128]{2,1,0:T(8,128)S(1)} %get-tuple-element.45.rest_a_ref.row_a_ref), channel_id=1, source_target_pairs={{0,4},{4,0},{8,12},{12,8},{1,5},{5,1},{9,13},{13,9},{2,6},{6,2},{1... | collective-permute-start | bytes 589832 | tf_op jit(solution)/shard_map/ppermute | solution.py:440
  12.7 0.0 collective-permute-done.4.from_corner_a_ref
  12.7 1.5 %collective-permute-start.9 = (f32[4,96,128]{2,1,0:T(8,128)S(1)}, f32[4,96,128]{2,1,0:T(8,128)S(1)}, u32[]{:S(2)}, u32[]{:S(2)}) collective-permute-start(f32[4,96,128]{2,1,0:T(8,128)S(1)} %get-tuple-element.46.rest_b_ref.row_b_ref), channel_id=1, source_target_pairs={{0,16},{4,8},{8,4},{12,28},{16,0},{20,24},{24,20},{28,12},{1,17},{... | collective-permute-start | bytes 589832 | tf_op jit(solution)/shard_map/ppermute | solution.py:440
  14.2 0.1 collective-permute-done.5.from_corner_b_ref
  14.3 0.0 collective-permute-done.from_row_a_ref
  14.3 2.6 %shard_map.96 = (f32[5,32,128]{2,1,0:T(8,128)S(1)}, f32[4,32,128]{2,1,0:T(8,128)S(1)}, f32[32,128]{1,0:T(8,128)S(1)}, f32[24,32,128]{2,1,0:T(8,128)S(1)}) custom-call(s32[8,5]{1,0:T(8,128)S(1)} %bitcast.19, s32[8,5]{1,0:T(8,128)S(1)} %bitcast.21, f32[8,128]{1,0:T(8,128)S(1)} %iota.7.flags_ref, f32[4,64,128]{2,1,0:T(8,128)S(1)} %get-tuple-element.36.row_a_ref, ...), custom_call_target="tpu_custom_call" | custom-call | flops 1000000000 | tf_op jit(solution)/shard_map/pallas_call | solution.py:481
  17.0 1.5 %collective-permute-start.6 = (f32[5,32,128]{2,1,0:T(8,128)S(1)}, f32[5,32,128]{2,1,0:T(8,128)S(1)}, u32[]{:S(2)}, u32[]{:S(2)}) collective-permute-start(f32[5,32,128]{2,1,0:T(8,128)S(1)} %get-tuple-element.48.row_a_ref), channel_id=1, source_target_pairs={{0,4},{4,0},{8,12},{12,8},{1,5},{5,1},{9,13},{13,9},{2,6},{6,2},{1... | collective-permute-start | bytes 245768 | tf_op jit(solution)/shard_map/ppermute | solution.py:440
  18.5 1.5 %collective-permute-start.12 = (f32[4,32,128]{2,1,0:T(8,128)S(1)}, f32[4,32,128]{2,1,0:T(8,128)S(1)}, u32[]{:S(2)}, u32[]{:S(2)}) collective-permute-start(f32[4,32,128]{2,1,0:T(8,128)S(1)} %get-tuple-element.52.row_b_ref), channel_id=1, source_target_pairs={{0,16},{4,8},{8,4},{12,28},{16,0},{20,24},{24,20},{28,12},{1,17},{... | collective-permute-start | bytes 196616 | tf_op jit(solution)/shard_map/ppermute | solution.py:440
  20.0 0.1 collective-permute-start.10
  20.1 0.6 %collective-permute-start.11 = (f32[4,96,128]{2,1,0:T(8,128)S(1)}, f32[4,96,128]{2,1,0:T(8,128)S(1)}, u32[]{:S(2)}, u32[]{:S(2)}) collective-permute-start(f32[4,96,128]{2,1,0:T(8,128)S(1)} %get-tuple-element.50), channel_id=1, source_target_pairs={{0,16},{1,2},{2,1},{3,19},{16,0},{17,18},{18,17},{19,3},{4,20},{5,... | collective-permute-start | bytes 589832 | tf_op jit(solution)/shard_map/ppermute | solution.py:440
  20.7 0.8 %collective-permute-done.6.from_row_a_ref = f32[5,32,128]{2,1,0:T(8,128)S(1)} collective-permute-done((f32[5,32,128]{2,1,0:T(8,128)S(1)}, f32[5,32,128]{2,1,0:T(8,128)S(1)}, u32[]{:S(2)}, u32[]{:S(2)}) %collective-permute-start.6) | collective-permute-done | bytes 81952 | tf_op jit(solution)/shard_map/ppermute | solution.py:440
  21.5 2.3 %collective-permute-start.7 = (f32[32,128]{1,0:T(8,128)S(1)}, f32[32,128]{1,0:T(8,128)S(1)}, u32[]{:S(2)}, u32[]{:S(2)}) collective-permute-start(f32[32,128]{1,0:T(8,128)S(1)} %fusion.1), channel_id=1, source_target_pairs={{0,8},{1,9},{2,10},{3,11},{4,12},{5,13},{6,14},{7,15},{8,0},{9,1},... | collective-permute-start | bytes 49160 | tf_op jit(solution)/shard_map/ppermute | solution.py:428
  23.8 2.4 %collective-permute-done.7 = f32[32,128]{1,0:T(8,128)S(1)} collective-permute-done((f32[32,128]{1,0:T(8,128)S(1)}, f32[32,128]{1,0:T(8,128)S(1)}, u32[]{:S(2)}, u32[]{:S(2)}) %collective-permute-start.7) | collective-permute-done | bytes 16416 | tf_op jit(solution)/shard_map/ppermute | solution.py:428
  26.2 0.1 collective-permute-start.13
  26.3 1.1 %collective-permute-start.15 = (f32[4,32,128]{2,1,0:T(8,128)S(1)}, f32[4,32,128]{2,1,0:T(8,128)S(1)}, u32[]{:S(2)}, u32[]{:S(2)}) collective-permute-start(f32[4,32,128]{2,1,0:T(8,128)S(1)} %get-tuple-element.54), channel_id=1, source_target_pairs={{0,16},{1,2},{2,1},{3,19},{16,0},{17,18},{18,17},{19,3},{4,20},{5,... | collective-permute-start | bytes 196616 | tf_op jit(solution)/shard_map/ppermute | solution.py:440
  27.3 0.2 collective-permute-done.13.from_side_a_ref
  27.5 0.9 %collective-permute-start.14 = (f32[32,128]{1,0:T(8,128)S(1)}, f32[32,128]{1,0:T(8,128)S(1)}, u32[]{:S(2)}, u32[]{:S(2)}) collective-permute-start(f32[32,128]{1,0:T(8,128)S(1)} %fusion), channel_id=1, source_target_pairs={{0,2},{1,3},{2,0},{3,1},{4,6},{5,7},{6,4},{7,5},{8,10},{9,11},{10,... | collective-permute-start | bytes 49160 | tf_op jit(solution)/shard_map/ppermute | solution.py:428
  28.5 0.3 shard_map.99
  28.8 2.5 %collective-permute-done.14 = f32[32,128]{1,0:T(8,128)S(1)} collective-permute-done((f32[32,128]{1,0:T(8,128)S(1)}, f32[32,128]{1,0:T(8,128)S(1)}, u32[]{:S(2)}, u32[]{:S(2)}) %collective-permute-start.14) | collective-permute-done | bytes 16416 | tf_op jit(solution)/shard_map/ppermute | solution.py:428
  31.3 2.9 %shard_map.100 = (f32[4,32,128]{2,1,0:T(8,128)S(1)}, f32[4,32,128]{2,1,0:T(8,128)S(1)}, f32[32,128]{1,0:T(8,128)}, f32[48,128]{1,0:T(8,128)S(1)}, f32[48,128]{1,0:T(8,128)S(1)}) custom-call(s32[8,5]{1,0:T(8,128)S(1)} %bitcast.20, s32[8,5]{1,0:T(8,128)S(1)} %bitcast.22, f32[8,128]{1,0:T(8,128)S(1)} %iota.7.flags_ref, f32[32,128]{1,0:T(8,128)S(1)} %add.50.partial_ref, ...), custom_call_target="tpu_custom_call" | custom-call | tf_op jit(solution)/shard_map/pallas_call | solution.py:481
  34.2 0.1 collective-permute-start.16
  34.3 1.2 %collective-permute-done.16 = f32[48,128]{1,0:T(8,128)S(1)} collective-permute-done((f32[48,128]{1,0:T(8,128)S(1)}, f32[48,128]{1,0:T(8,128)S(1)}, u32[]{:S(2)}, u32[]{:S(2)}) %collective-permute-start.16) | collective-permute-done | bytes 24608 | tf_op jit(solution)/shard_map/ppermute | solution.py:428
  35.4 2.2 %collective-permute-start.17 = (f32[48,128]{1,0:T(8,128)S(1)}, f32[48,128]{1,0:T(8,128)S(1)}, u32[]{:S(2)}, u32[]{:S(2)}) collective-permute-start(f32[48,128]{1,0:T(8,128)S(1)} %add.51), channel_id=1, source_target_pairs={{0,6},{1,7},{2,4},{3,5},{4,2},{5,3},{6,0},{7,1},{8,14},{9,15},{10,... | collective-permute-start | bytes 73736 | tf_op jit(solution)/shard_map/ppermute | solution.py:428
  37.6 1.0 %collective-permute-start.18 = (f32[48,128]{1,0:T(8,128)S(1)}, f32[48,128]{1,0:T(8,128)S(1)}, u32[]{:S(2)}, u32[]{:S(2)}) collective-permute-start(f32[48,128]{1,0:T(8,128)S(1)} %add.51), channel_id=1, source_target_pairs={{0,2},{1,3},{2,0},{3,1},{4,6},{5,7},{6,4},{7,5},{8,10},{9,11},{10,... | collective-permute-start | bytes 73736 | tf_op jit(solution)/shard_map/ppermute | solution.py:428
  38.7 0.3 collective-permute-start.19
  38.9 1.2 %collective-permute-done.17 = f32[48,128]{1,0:T(8,128)S(1)} collective-permute-done((f32[48,128]{1,0:T(8,128)S(1)}, f32[48,128]{1,0:T(8,128)S(1)}, u32[]{:S(2)}, u32[]{:S(2)}) %collective-permute-start.17) | collective-permute-done | bytes 24608 | tf_op jit(solution)/shard_map/ppermute | solution.py:428
  40.2 1.3 %collective-permute-done.18 = f32[48,128]{1,0:T(8,128)S(1)} collective-permute-done((f32[48,128]{1,0:T(8,128)S(1)}, f32[48,128]{1,0:T(8,128)S(1)}, u32[]{:S(2)}, u32[]{:S(2)}) %collective-permute-start.18) | collective-permute-done | bytes 24608 | tf_op jit(solution)/shard_map/ppermute | solution.py:428
  41.5 1.0 %collective-permute-done.19 = f32[48,128]{1,0:T(8,128)S(1)} collective-permute-done((f32[48,128]{1,0:T(8,128)S(1)}, f32[48,128]{1,0:T(8,128)S(1)}, u32[]{:S(2)}, u32[]{:S(2)}) %collective-permute-start.19) | collective-permute-done | bytes 24608 | tf_op jit(solution)/shard_map/ppermute | solution.py:428
  42.5 2.6 %collective-permute-start.20 = (f32[48,128]{1,0:T(8,128)S(1)}, f32[48,128]{1,0:T(8,128)S(1)}, u32[]{:S(2)}, u32[]{:S(2)}) collective-permute-start(f32[48,128]{1,0:T(8,128)S(1)} %add_add_fusion), channel_id=1, source_target_pairs={{0,8},{1,9},{2,10},{3,11},{4,12},{5,13},{6,14},{7,15},{8,0},{9,1},... | collective-permute-start | bytes 73736 | tf_op jit(solution)/shard_map/ppermute | solution.py:428
  45.1 2.2 %collective-permute-done.20 = f32[48,128]{1,0:T(8,128)S(1)} collective-permute-done((f32[48,128]{1,0:T(8,128)S(1)}, f32[48,128]{1,0:T(8,128)S(1)}, u32[]{:S(2)}, u32[]{:S(2)}) %collective-permute-start.20) | collective-permute-done | bytes 24608 | tf_op jit(solution)/shard_map/ppermute | solution.py:428
  47.3 0.1 collective-permute-start.21
  47.4 1.4 %shard_map.101.work_ref = f32[32,64]{1,0:T(8,128)S(1)} custom-call(f32[48,128]{1,0:T(8,128)S(1)} %add.55.sums_ref), custom_call_target="tpu_custom_call" | custom-call | flops 1000000000 | tf_op jit(solution)/shard_map/pallas_call | solution.py:481
  48.7 0.0 collective-permute-done.21.other_ref
  48.8 1.2 %shard_map.102 = (f32[256,128]{1,0:T(8,128)}, f32[32,32]{1,0:T(8,128)}, f32[2,32,160]{2,1,0:T(8,128)}) custom-call(f32[8,128]{1,0:T(8,128)S(1)} %iota.7.flags_ref, f32[32,64]{1,0:T(8,128)S(1)} %shard_map.101.work_ref, f32[48,128]{1,0:T(8,128)S(1)} %add.55.sums_ref, f32[40,128]{1,0:T(8,128)S(1)} %collective-permute-done.21.other_ref, ...), custom_call_target="tpu_custom_call" | custom-call | tf_op jit(solution)/shard_map/pallas_call | solution.py:481
  (25 shorter events, 0.2 us)
Async XLA Ops:
  1.9 12.4 %copy-start.3 = (f32[8,128,128]{2,1,0:T(8,128)S(1)}, f32[8,128,128]{2,1,0:T(8,128)}, u32[]{:S(2)}) copy-start(f32[8,128,128]{2,1,0:T(8,128)} %mass_ref.3) | copy-start | bytes 1572868
  2.0 12.3 %copy-start.2 = (f32[8,128,128]{2,1,0:T(8,128)S(1)}, f32[8,128,128]{2,1,0:T(8,128)}, u32[]{:S(2)}) copy-start(f32[8,128,128]{2,1,0:T(8,128)} %stiff_ref.3) | copy-start | bytes 1572868
  2.0 5.3 %collective-permute-start.2 = (f32[2,64,128]{2,1,0:T(8,128)S(1)}, f32[2,64,128]{2,1,0:T(8,128)S(1)}, u32[]{:S(2)}, u32[]{:S(2)}) collective-permute-start(f32[2,64,128]{2,1,0:T(8,128)S(1)} %get-tuple-element.38), channel_id=1, source_target_pairs={{0,1},{1,0},{2,3},{3,2},{4,5},{5,4},{6,7},{7,6},{8,9},{9,8},{10,11... | collective-permute-start | bytes 196616 | tf_op jit(solution)/shard_map/ppermute | solution.py:440
  2.5 4.8 %collective-permute-start.3 = (f32[2,64,128]{2,1,0:T(8,128)S(1)}, f32[2,64,128]{2,1,0:T(8,128)S(1)}, u32[]{:S(2)}, u32[]{:S(2)}) collective-permute-start(f32[2,64,128]{2,1,0:T(8,128)S(1)} %get-tuple-element.42), channel_id=1, source_target_pairs={{0,16},{1,2},{2,1},{3,19},{16,0},{17,18},{18,17},{19,3},{4,20},{5,... | collective-permute-start | bytes 196616 | tf_op jit(solution)/shard_map/ppermute | solution.py:440
  5.1 9.2 %collective-permute-start = (f32[4,64,128]{2,1,0:T(8,128)S(1)}, f32[4,64,128]{2,1,0:T(8,128)S(1)}, u32[]{:S(2)}, u32[]{:S(2)}) collective-permute-start(f32[4,64,128]{2,1,0:T(8,128)S(1)} %get-tuple-element.36.row_a_ref), channel_id=1, source_target_pairs={{0,4},{4,0},{8,12},{12,8},{1,5},{5,1},{9,13},{13,9},{2,6},{6,2},{1... | collective-permute-start | bytes 393224 | tf_op jit(solution)/shard_map/ppermute | solution.py:440
  6.7 7.6 %collective-permute-start.1 = (f32[4,64,128]{2,1,0:T(8,128)S(1)}, f32[4,64,128]{2,1,0:T(8,128)S(1)}, u32[]{:S(2)}, u32[]{:S(2)}) collective-permute-start(f32[4,64,128]{2,1,0:T(8,128)S(1)} %get-tuple-element.37.row_b_ref), channel_id=1, source_target_pairs={{0,16},{4,8},{8,4},{12,28},{16,0},{20,24},{24,20},{28,12},{1,17},{... | collective-permute-start | bytes 393224 | tf_op jit(solution)/shard_map/ppermute | solution.py:440
  7.3 7.0 %copy-start.1 = (s32[5,2,4]{0,2,1:T(4,128)S(1)}, s32[5,2,4]{0,2,1:T(4,128)}, u32[]{:S(2)}) copy-start(s32[5,2,4]{0,2,1:T(4,128)} %param.9) | copy-start | bytes 484
  7.4 7.0 %copy-start = (s32[5,2,4]{0,2,1:T(4,128)S(1)}, s32[5,2,4]{0,2,1:T(4,128)}, u32[]{:S(2)}) copy-start(s32[5,2,4]{0,2,1:T(4,128)} %param.8) | copy-start | bytes 484
  7.4 5.3 %collective-permute-start.4 = (f32[2,64,128]{2,1,0:T(8,128)S(1)}, f32[2,64,128]{2,1,0:T(8,128)S(1)}, u32[]{:S(2)}, u32[]{:S(2)}) collective-permute-start(f32[2,64,128]{2,1,0:T(8,128)S(1)} %get-tuple-element.43), channel_id=1, source_target_pairs={{0,4},{4,0},{8,12},{12,8},{1,5},{5,1},{9,13},{13,9},{2,6},{6,2},{1... | collective-permute-start | bytes 196616 | tf_op jit(solution)/shard_map/ppermute | solution.py:440
  10.0 4.3 %collective-permute-start.5 = (f32[2,64,128]{2,1,0:T(8,128)S(1)}, f32[2,64,128]{2,1,0:T(8,128)S(1)}, u32[]{:S(2)}, u32[]{:S(2)}) collective-permute-start(f32[2,64,128]{2,1,0:T(8,128)S(1)} %get-tuple-element.44), channel_id=1, source_target_pairs={{0,16},{4,8},{8,4},{12,28},{16,0},{20,24},{24,20},{28,12},{1,17},{... | collective-permute-start | bytes 196616 | tf_op jit(solution)/shard_map/ppermute | solution.py:440
  11.0 8.9 %collective-permute-start.8 = (f32[4,96,128]{2,1,0:T(8,128)S(1)}, f32[4,96,128]{2,1,0:T(8,128)S(1)}, u32[]{:S(2)}, u32[]{:S(2)}) collective-permute-start(f32[4,96,128]{2,1,0:T(8,128)S(1)} %get-tuple-element.45.rest_a_ref.row_a_ref), channel_id=1, source_target_pairs={{0,4},{4,0},{8,12},{12,8},{1,5},{5,1},{9,13},{13,9},{2,6},{6,2},{1... | collective-permute-start | bytes 589832 | tf_op jit(solution)/shard_map/ppermute | solution.py:440
  12.7 7.3 %collective-permute-start.9 = (f32[4,96,128]{2,1,0:T(8,128)S(1)}, f32[4,96,128]{2,1,0:T(8,128)S(1)}, u32[]{:S(2)}, u32[]{:S(2)}) collective-permute-start(f32[4,96,128]{2,1,0:T(8,128)S(1)} %get-tuple-element.46.rest_b_ref.row_b_ref), channel_id=1, source_target_pairs={{0,16},{4,8},{8,4},{12,28},{16,0},{20,24},{24,20},{28,12},{1,17},{... | collective-permute-start | bytes 589832 | tf_op jit(solution)/shard_map/ppermute | solution.py:440
  17.0 4.5 %collective-permute-start.6 = (f32[5,32,128]{2,1,0:T(8,128)S(1)}, f32[5,32,128]{2,1,0:T(8,128)S(1)}, u32[]{:S(2)}, u32[]{:S(2)}) collective-permute-start(f32[5,32,128]{2,1,0:T(8,128)S(1)} %get-tuple-element.48.row_a_ref), channel_id=1, source_target_pairs={{0,4},{4,0},{8,12},{12,8},{1,5},{5,1},{9,13},{13,9},{2,6},{6,2},{1... | collective-permute-start | bytes 245768 | tf_op jit(solution)/shard_map/ppermute | solution.py:440
  18.5 7.7 %collective-permute-start.12 = (f32[4,32,128]{2,1,0:T(8,128)S(1)}, f32[4,32,128]{2,1,0:T(8,128)S(1)}, u32[]{:S(2)}, u32[]{:S(2)}) collective-permute-start(f32[4,32,128]{2,1,0:T(8,128)S(1)} %get-tuple-element.52.row_b_ref), channel_id=1, source_target_pairs={{0,16},{4,8},{8,4},{12,28},{16,0},{20,24},{24,20},{28,12},{1,17},{... | collective-permute-start | bytes 196616 | tf_op jit(solution)/shard_map/ppermute | solution.py:440
  20.0 6.2 %collective-permute-start.10 = (f32[4,96,128]{2,1,0:T(8,128)S(1)}, f32[4,96,128]{2,1,0:T(8,128)S(1)}, u32[]{:S(2)}, u32[]{:S(2)}) collective-permute-start(f32[4,96,128]{2,1,0:T(8,128)S(1)} %get-tuple-element.49), channel_id=1, source_target_pairs={{0,1},{1,0},{2,3},{3,2},{4,5},{5,4},{6,7},{7,6},{8,9},{9,8},{10,11... | collective-permute-start | bytes 589832 | tf_op jit(solution)/shard_map/ppermute | solution.py:440
  20.1 6.1 %collective-permute-start.11 = (f32[4,96,128]{2,1,0:T(8,128)S(1)}, f32[4,96,128]{2,1,0:T(8,128)S(1)}, u32[]{:S(2)}, u32[]{:S(2)}) collective-permute-start(f32[4,96,128]{2,1,0:T(8,128)S(1)} %get-tuple-element.50), channel_id=1, source_target_pairs={{0,16},{1,2},{2,1},{3,19},{16,0},{17,18},{18,17},{19,3},{4,20},{5,... | collective-permute-start | bytes 589832 | tf_op jit(solution)/shard_map/ppermute | solution.py:440
  21.5 4.6 %collective-permute-start.7 = (f32[32,128]{1,0:T(8,128)S(1)}, f32[32,128]{1,0:T(8,128)S(1)}, u32[]{:S(2)}, u32[]{:S(2)}) collective-permute-start(f32[32,128]{1,0:T(8,128)S(1)} %fusion.1), channel_id=1, source_target_pairs={{0,8},{1,9},{2,10},{3,11},{4,12},{5,13},{6,14},{7,15},{8,0},{9,1},... | collective-permute-start | bytes 49160 | tf_op jit(solution)/shard_map/ppermute | solution.py:428
  26.2 1.3 %collective-permute-start.13 = (f32[5,32,128]{2,1,0:T(8,128)S(1)}, f32[5,32,128]{2,1,0:T(8,128)S(1)}, u32[]{:S(2)}, u32[]{:S(2)}) collective-permute-start(f32[5,32,128]{2,1,0:T(8,128)S(1)} %get-tuple-element.53), channel_id=1, source_target_pairs={{0,1},{1,0},{2,3},{3,2},{4,5},{5,4},{6,7},{7,6},{8,9},{9,8},{10,11... | collective-permute-start | bytes 245768 | tf_op jit(solution)/shard_map/ppermute | solution.py:440
  26.3 5.0 %collective-permute-start.15 = (f32[4,32,128]{2,1,0:T(8,128)S(1)}, f32[4,32,128]{2,1,0:T(8,128)S(1)}, u32[]{:S(2)}, u32[]{:S(2)}) collective-permute-start(f32[4,32,128]{2,1,0:T(8,128)S(1)} %get-tuple-element.54), channel_id=1, source_target_pairs={{0,16},{1,2},{2,1},{3,19},{16,0},{17,18},{18,17},{19,3},{4,20},{5,... | collective-permute-start | bytes 196616 | tf_op jit(solution)/shard_map/ppermute | solution.py:440
  27.5 3.7 %collective-permute-start.14 = (f32[32,128]{1,0:T(8,128)S(1)}, f32[32,128]{1,0:T(8,128)S(1)}, u32[]{:S(2)}, u32[]{:S(2)}) collective-permute-start(f32[32,128]{1,0:T(8,128)S(1)} %fusion), channel_id=1, source_target_pairs={{0,2},{1,3},{2,0},{3,1},{4,6},{5,7},{6,4},{7,5},{8,10},{9,11},{10,... | collective-permute-start | bytes 49160 | tf_op jit(solution)/shard_map/ppermute | solution.py:428
  34.2 1.3 %collective-permute-start.16 = (f32[48,128]{1,0:T(8,128)S(1)}, f32[48,128]{1,0:T(8,128)S(1)}, u32[]{:S(2)}, u32[]{:S(2)}) collective-permute-start(f32[48,128]{1,0:T(8,128)S(1)} %get-tuple-element.61), channel_id=1, source_target_pairs={{0,1},{1,0},{2,3},{3,2},{4,5},{5,4},{6,7},{7,6},{8,9},{9,8},{10,11... | collective-permute-start | bytes 73736 | tf_op jit(solution)/shard_map/ppermute | solution.py:428
  35.4 4.7 %collective-permute-start.17 = (f32[48,128]{1,0:T(8,128)S(1)}, f32[48,128]{1,0:T(8,128)S(1)}, u32[]{:S(2)}, u32[]{:S(2)}) collective-permute-start(f32[48,128]{1,0:T(8,128)S(1)} %add.51), channel_id=1, source_target_pairs={{0,6},{1,7},{2,4},{3,5},{4,2},{5,3},{6,0},{7,1},{8,14},{9,15},{10,... | collective-permute-start | bytes 73736 | tf_op jit(solution)/shard_map/ppermute | solution.py:428
  37.6 3.8 %collective-permute-start.18 = (f32[48,128]{1,0:T(8,128)S(1)}, f32[48,128]{1,0:T(8,128)S(1)}, u32[]{:S(2)}, u32[]{:S(2)}) collective-permute-start(f32[48,128]{1,0:T(8,128)S(1)} %add.51), channel_id=1, source_target_pairs={{0,2},{1,3},{2,0},{3,1},{4,6},{5,7},{6,4},{7,5},{8,10},{9,11},{10,... | collective-permute-start | bytes 73736 | tf_op jit(solution)/shard_map/ppermute | solution.py:428
  38.7 3.8 %collective-permute-start.19 = (f32[48,128]{1,0:T(8,128)S(1)}, f32[48,128]{1,0:T(8,128)S(1)}, u32[]{:S(2)}, u32[]{:S(2)}) collective-permute-start(f32[48,128]{1,0:T(8,128)S(1)} %add.51), channel_id=1, source_target_pairs={{0,4},{1,5},{2,6},{3,7},{4,0},{5,1},{6,2},{7,3},{8,12},{9,13},{10,... | collective-permute-start | bytes 73736 | tf_op jit(solution)/shard_map/ppermute | solution.py:428
  42.5 4.8 %collective-permute-start.20 = (f32[48,128]{1,0:T(8,128)S(1)}, f32[48,128]{1,0:T(8,128)S(1)}, u32[]{:S(2)}, u32[]{:S(2)}) collective-permute-start(f32[48,128]{1,0:T(8,128)S(1)} %add_add_fusion), channel_id=1, source_target_pairs={{0,8},{1,9},{2,10},{3,11},{4,12},{5,13},{6,14},{7,15},{8,0},{9,1},... | collective-permute-start | bytes 73736 | tf_op jit(solution)/shard_map/ppermute | solution.py:428
  47.3 1.5 %collective-permute-start.21 = (f32[40,128]{1,0:T(8,128)S(1)}, f32[40,128]{1,0:T(8,128)S(1)}, u32[]{:S(2)}, u32[]{:S(2)}) collective-permute-start(f32[40,128]{1,0:T(8,128)S(1)} %slice.14), channel_id=1, source_target_pairs={{0,1},{1,0},{2,3},{3,2},{4,5},{5,4},{6,7},{7,6},{8,9},{9,8},{10,11... | collective-permute-start | bytes 61448 | tf_op jit(solution)/shard_map/ppermute | solution.py:428

commit v15 on v14

--- a/solution.py
+++ b/solution.py
@@ -541,15 +541,15 @@
     partial = total_over(
         partial + from_row_a[-1], 2 * count_py, count_py * lax.axis_size("px")
     )
-    partial, rest_side_a, rest_side_b = lax.optimization_barrier(
-        (partial, rest_side_a, rest_side_b)
-    )
     side_a, side_b = call(
         columns_kernel,
         (flags, residual_a, residual_b, from_row_a, from_row_b, partial),
         [shape(5, block, side), shape(4, block, side)],
     )
     from_side_a, from_side_b = exchange(side_a, side_b, "py")
+    from_side_a, rest_side_a, rest_side_b = lax.optimization_barrier(
+        (from_side_a, rest_side_a, rest_side_b)
+    )
     partial = total_over(partial + from_side_a[-1], 2, count_py)
     basis_parts, table = call(
         prepare_kernel,

time: 50.2 us -> 50.2 us (level)
  no operation moved by 1% of the time
where the time goes in v15:
time: 50.2 us; the launch traced here: 50 us
  starting transfers between devices  26.3 us (52%)
  waiting for transfers between devices  13 us (26%)
  Pallas kernels  8.64 us (17%)
  other arithmetic  1.2 us (2%)
  between operations  0.83 us (2%)
    ppermute x8, waiting for transfers between devices, swap(): return lax.ppermute(value, axes, pairs)  11.7 us
    ppermute x8, starting transfers between devices, swap(): return lax.ppermute(value, axes, pairs)  9.52 us
    ppermute x7, starting transfers between devices, exchange(): lax.ppermute(message_b, ('case', axis), pairs)  8.78 us
    pallas_call x10, Pallas kernels, call(): pl.pallas_call(kernel, out_shape=outputs, in_specs=specs, out_specs=[VMEM...  8.64 us
    ppermute x7, starting transfers between devices, exchange(): lax.ppermute(message_a, axis, near)  8 us
    concatenate x1, other arithmetic, shards(): vectors = jnp.concatenate([basis, previous.reshape(-1, side)], axis=0)  1.16 us
    ppermute x7, waiting for transfers between devices, exchange(): lax.ppermute(message_a, axis, near)  1.02 us
  transfers between devices with their start and end apart: 22, of which 11 were waited for; matrix products, arithmetic and copies ran while one was open for 0% of the time, Pallas kernels for 9%

profile of v15, /device:TPU:0, one launch (start us, length us, event | category | flops | bytes accessed | tf_op | source)
XLA Modules:
  0.0 50.0 jit_solution(3285023188818969789)
XLA Ops:
  0.7 1.2 %pad_maximum_fusion.vectors_ref = f32[1280,128]{1,0:T(8,128)S(1)} fusion(f32[256,128]{1,0:T(8,128)} %bitcast.22, f32[1024,128]{1,0:T(8,128)} %bitcast.21), kind=kLoop, calls=%fused_computation | loop fusion | flops 163840 | bytes 1310720 | tf_op jit(solution)/shard_map/concatenate | solution.py:469
  1.8 0.1 iota.7.flags_ref
  1.9 0.1 shard_map.93
  2.0 0.0 copy-start.2
  2.0 0.5 %collective-permute-start.2 = (f32[2,64,128]{2,1,0:T(8,128)S(1)}, f32[2,64,128]{2,1,0:T(8,128)S(1)}, u32[]{:S(2)}, u32[]{:S(2)}) collective-permute-start(f32[2,64,128]{2,1,0:T(8,128)S(1)} %get-tuple-element.38), channel_id=1, source_target_pairs={{0,1},{1,0},{2,3},{3,2},{4,5},{5,4},{6,7},{7,6},{8,9},{9,8},{10,11... | collective-permute-start | bytes 196616 | tf_op jit(solution)/shard_map/ppermute | solution.py:440
  2.5 2.6 %collective-permute-start.3 = (f32[2,64,128]{2,1,0:T(8,128)S(1)}, f32[2,64,128]{2,1,0:T(8,128)S(1)}, u32[]{:S(2)}, u32[]{:S(2)}) collective-permute-start(f32[2,64,128]{2,1,0:T(8,128)S(1)} %get-tuple-element.42), channel_id=1, source_target_pairs={{0,16},{1,2},{2,1},{3,19},{16,0},{17,18},{18,17},{19,3},{4,20},{5,... | collective-permute-start | bytes 196616 | tf_op jit(solution)/shard_map/ppermute | solution.py:440
  5.1 1.6 %collective-permute-start = (f32[4,64,128]{2,1,0:T(8,128)S(1)}, f32[4,64,128]{2,1,0:T(8,128)S(1)}, u32[]{:S(2)}, u32[]{:S(2)}) collective-permute-start(f32[4,64,128]{2,1,0:T(8,128)S(1)} %get-tuple-element.36.row_a_ref), channel_id=1, source_target_pairs={{0,4},{4,0},{8,12},{12,8},{1,5},{5,1},{9,13},{13,9},{2,6},{6,2},{1... | collective-permute-start | bytes 393224 | tf_op jit(solution)/shard_map/ppermute | solution.py:440
  6.7 0.5 %collective-permute-start.1 = (f32[4,64,128]{2,1,0:T(8,128)S(1)}, f32[4,64,128]{2,1,0:T(8,128)S(1)}, u32[]{:S(2)}, u32[]{:S(2)}) collective-permute-start(f32[4,64,128]{2,1,0:T(8,128)S(1)} %get-tuple-element.37.row_b_ref), channel_id=1, source_target_pairs={{0,16},{4,8},{8,4},{12,28},{16,0},{20,24},{24,20},{28,12},{1,17},{... | collective-permute-start | bytes 393224 | tf_op jit(solution)/shard_map/ppermute | solution.py:440
  7.2 0.1 shard_map.94
  7.2 0.1 collective-permute-done.3.side_b_ref.from_side_b_ref
  7.4 0.0 copy-start
  7.4 2.7 %collective-permute-start.4 = (f32[2,64,128]{2,1,0:T(8,128)S(1)}, f32[2,64,128]{2,1,0:T(8,128)S(1)}, u32[]{:S(2)}, u32[]{:S(2)}) collective-permute-start(f32[2,64,128]{2,1,0:T(8,128)S(1)} %get-tuple-element.43), channel_id=1, source_target_pairs={{0,4},{4,0},{8,12},{12,8},{1,5},{5,1},{9,13},{13,9},{2,6},{6,2},{1... | collective-permute-start | bytes 196616 | tf_op jit(solution)/shard_map/ppermute | solution.py:440
  10.0 1.0 %collective-permute-start.5 = (f32[2,64,128]{2,1,0:T(8,128)S(1)}, f32[2,64,128]{2,1,0:T(8,128)S(1)}, u32[]{:S(2)}, u32[]{:S(2)}) collective-permute-start(f32[2,64,128]{2,1,0:T(8,128)S(1)} %get-tuple-element.44), channel_id=1, source_target_pairs={{0,16},{4,8},{8,4},{12,28},{16,0},{20,24},{24,20},{28,12},{1,17},{... | collective-permute-start | bytes 196616 | tf_op jit(solution)/shard_map/ppermute | solution.py:440
  11.0 1.6 %collective-permute-start.10 = (f32[4,96,128]{2,1,0:T(8,128)S(1)}, f32[4,96,128]{2,1,0:T(8,128)S(1)}, u32[]{:S(2)}, u32[]{:S(2)}) collective-permute-start(f32[4,96,128]{2,1,0:T(8,128)S(1)} %get-tuple-element.45.rest_a_ref.row_a_ref), channel_id=1, source_target_pairs={{0,4},{4,0},{8,12},{12,8},{1,5},{5,1},{9,13},{13,9},{2,6},{6,2},{1... | collective-permute-start | bytes 589832 | tf_op jit(solution)/shard_map/ppermute | solution.py:440
  12.7 0.0 collective-permute-done.4.from_corner_a_ref
  12.7 1.5 %collective-permute-start.11 = (f32[4,96,128]{2,1,0:T(8,128)S(1)}, f32[4,96,128]{2,1,0:T(8,128)S(1)}, u32[]{:S(2)}, u32[]{:S(2)}) collective-permute-start(f32[4,96,128]{2,1,0:T(8,128)S(1)} %get-tuple-element.46.rest_b_ref.row_b_ref), channel_id=1, source_target_pairs={{0,16},{4,8},{8,4},{12,28},{16,0},{20,24},{24,20},{28,12},{1,17},{... | collective-permute-start | bytes 589832 | tf_op jit(solution)/shard_map/ppermute | solution.py:440
  14.2 0.1 collective-permute-done.5.from_corner_b_ref
  14.3 0.0 collective-permute-done.from_row_a_ref
  14.3 2.6 %shard_map.96 = (f32[5,32,128]{2,1,0:T(8,128)S(1)}, f32[4,32,128]{2,1,0:T(8,128)S(1)}, f32[32,128]{1,0:T(8,128)S(1)}, f32[24,32,128]{2,1,0:T(8,128)S(1)}) custom-call(s32[8,5]{1,0:T(8,128)S(1)} %bitcast.17, s32[8,5]{1,0:T(8,128)S(1)} %bitcast.19, f32[8,128]{1,0:T(8,128)S(1)} %iota.7.flags_ref, f32[4,64,128]{2,1,0:T(8,128)S(1)} %get-tuple-element.36.row_a_ref, ...), custom_call_target="tpu_custom_call" | custom-call | flops 1000000000 | tf_op jit(solution)/shard_map/pallas_call | solution.py:481
  17.0 1.5 %collective-permute-start.6 = (f32[5,32,128]{2,1,0:T(8,128)S(1)}, f32[5,32,128]{2,1,0:T(8,128)S(1)}, u32[]{:S(2)}, u32[]{:S(2)}) collective-permute-start(f32[5,32,128]{2,1,0:T(8,128)S(1)} %get-tuple-element.48.row_a_ref), channel_id=1, source_target_pairs={{0,4},{4,0},{8,12},{12,8},{1,5},{5,1},{9,13},{13,9},{2,6},{6,2},{1... | collective-permute-start | bytes 245768 | tf_op jit(solution)/shard_map/ppermute | solution.py:440
  18.5 1.5 %collective-permute-start.8 = (f32[4,32,128]{2,1,0:T(8,128)S(1)}, f32[4,32,128]{2,1,0:T(8,128)S(1)}, u32[]{:S(2)}, u32[]{:S(2)}) collective-permute-start(f32[4,32,128]{2,1,0:T(8,128)S(1)} %get-tuple-element.49.row_b_ref), channel_id=1, source_target_pairs={{0,16},{4,8},{8,4},{12,28},{16,0},{20,24},{24,20},{28,12},{1,17},{... | collective-permute-start | bytes 196616 | tf_op jit(solution)/shard_map/ppermute | solution.py:440
  20.0 0.1 collective-permute-start.12
  20.1 0.6 %collective-permute-start.13 = (f32[4,96,128]{2,1,0:T(8,128)S(1)}, f32[4,96,128]{2,1,0:T(8,128)S(1)}, u32[]{:S(2)}, u32[]{:S(2)}) collective-permute-start(f32[4,96,128]{2,1,0:T(8,128)S(1)} %get-tuple-element.52), channel_id=1, source_target_pairs={{0,16},{1,2},{2,1},{3,19},{16,0},{17,18},{18,17},{19,3},{4,20},{5,... | collective-permute-start | bytes 589832 | tf_op jit(solution)/shard_map/ppermute | solution.py:440
  20.7 0.8 %collective-permute-done.6.from_row_a_ref = f32[5,32,128]{2,1,0:T(8,128)S(1)} collective-permute-done((f32[5,32,128]{2,1,0:T(8,128)S(1)}, f32[5,32,128]{2,1,0:T(8,128)S(1)}, u32[]{:S(2)}, u32[]{:S(2)}) %collective-permute-start.6) | collective-permute-done | bytes 81952 | tf_op jit(solution)/shard_map/ppermute | solution.py:440
  21.5 2.3 %collective-permute-start.7 = (f32[32,128]{1,0:T(8,128)S(1)}, f32[32,128]{1,0:T(8,128)S(1)}, u32[]{:S(2)}, u32[]{:S(2)}) collective-permute-start(f32[32,128]{1,0:T(8,128)S(1)} %fusion), channel_id=1, source_target_pairs={{0,8},{1,9},{2,10},{3,11},{4,12},{5,13},{6,14},{7,15},{8,0},{9,1},... | collective-permute-start | bytes 49160 | tf_op jit(solution)/shard_map/ppermute | solution.py:428
  23.8 2.4 %collective-permute-done.7 = f32[32,128]{1,0:T(8,128)S(1)} collective-permute-done((f32[32,128]{1,0:T(8,128)S(1)}, f32[32,128]{1,0:T(8,128)S(1)}, u32[]{:S(2)}, u32[]{:S(2)}) %collective-permute-start.7) | collective-permute-done | bytes 16416 | tf_op jit(solution)/shard_map/ppermute | solution.py:428
  26.2 0.1 collective-permute-start.9
  26.3 1.1 %collective-permute-start.15 = (f32[4,32,128]{2,1,0:T(8,128)S(1)}, f32[4,32,128]{2,1,0:T(8,128)S(1)}, u32[]{:S(2)}, u32[]{:S(2)}) collective-permute-start(f32[4,32,128]{2,1,0:T(8,128)S(1)} %get-tuple-element.54), channel_id=1, source_target_pairs={{0,16},{1,2},{2,1},{3,19},{16,0},{17,18},{18,17},{19,3},{4,20},{5,... | collective-permute-start | bytes 196616 | tf_op jit(solution)/shard_map/ppermute | solution.py:440
  27.3 0.2 collective-permute-done.9.from_side_a_ref
  27.5 0.0 collective-permute-done.12.rest_side_a_ref
  27.5 1.0 %collective-permute-start.14 = (f32[32,128]{1,0:T(8,128)S(1)}, f32[32,128]{1,0:T(8,128)S(1)}, u32[]{:S(2)}, u32[]{:S(2)}) collective-permute-start(f32[32,128]{1,0:T(8,128)S(1)} %bitcast_add_fusion), channel_id=1, source_target_pairs={{0,2},{1,3},{2,0},{3,1},{4,6},{5,7},{6,4},{7,5},{8,10},{9,11},{10,... | collective-permute-start | bytes 49160 | tf_op jit(solution)/shard_map/ppermute | solution.py:428
  28.5 0.3 shard_map.99
  28.8 2.5 %collective-permute-done.14 = f32[32,128]{1,0:T(8,128)S(1)} collective-permute-done((f32[32,128]{1,0:T(8,128)S(1)}, f32[32,128]{1,0:T(8,128)S(1)}, u32[]{:S(2)}, u32[]{:S(2)}) %collective-permute-start.14) | collective-permute-done | bytes 16416 | tf_op jit(solution)/shard_map/ppermute | solution.py:428
  31.4 2.9 %shard_map.100 = (f32[4,32,128]{2,1,0:T(8,128)S(1)}, f32[4,32,128]{2,1,0:T(8,128)S(1)}, f32[32,128]{1,0:T(8,128)}, f32[48,128]{1,0:T(8,128)S(1)}, f32[48,128]{1,0:T(8,128)S(1)}) custom-call(s32[8,5]{1,0:T(8,128)S(1)} %bitcast.18, s32[8,5]{1,0:T(8,128)S(1)} %bitcast.20, f32[8,128]{1,0:T(8,128)S(1)} %iota.7.flags_ref, f32[32,128]{1,0:T(8,128)S(1)} %add.50.partial_ref, ...), custom_call_target="tpu_custom_call" | custom-call | tf_op jit(solution)/shard_map/pallas_call | solution.py:481
  34.2 0.1 collective-permute-start.16
  34.3 1.2 %collective-permute-done.16 = f32[48,128]{1,0:T(8,128)S(1)} collective-permute-done((f32[48,128]{1,0:T(8,128)S(1)}, f32[48,128]{1,0:T(8,128)S(1)}, u32[]{:S(2)}, u32[]{:S(2)}) %collective-permute-start.16) | collective-permute-done | bytes 24608 | tf_op jit(solution)/shard_map/ppermute | solution.py:428
  35.5 2.2 %collective-permute-start.17 = (f32[48,128]{1,0:T(8,128)S(1)}, f32[48,128]{1,0:T(8,128)S(1)}, u32[]{:S(2)}, u32[]{:S(2)}) collective-permute-start(f32[48,128]{1,0:T(8,128)S(1)} %add.51), channel_id=1, source_target_pairs={{0,6},{1,7},{2,4},{3,5},{4,2},{5,3},{6,0},{7,1},{8,14},{9,15},{10,... | collective-permute-start | bytes 73736 | tf_op jit(solution)/shard_map/ppermute | solution.py:428
  37.7 1.0 %collective-permute-start.18 = (f32[48,128]{1,0:T(8,128)S(1)}, f32[48,128]{1,0:T(8,128)S(1)}, u32[]{:S(2)}, u32[]{:S(2)}) collective-permute-start(f32[48,128]{1,0:T(8,128)S(1)} %add.51), channel_id=1, source_target_pairs={{0,2},{1,3},{2,0},{3,1},{4,6},{5,7},{6,4},{7,5},{8,10},{9,11},{10,... | collective-permute-start | bytes 73736 | tf_op jit(solution)/shard_map/ppermute | solution.py:428
  38.7 0.3 collective-permute-start.19
  39.0 1.2 %collective-permute-done.17 = f32[48,128]{1,0:T(8,128)S(1)} collective-permute-done((f32[48,128]{1,0:T(8,128)S(1)}, f32[48,128]{1,0:T(8,128)S(1)}, u32[]{:S(2)}, u32[]{:S(2)}) %collective-permute-start.17) | collective-permute-done | bytes 24608 | tf_op jit(solution)/shard_map/ppermute | solution.py:428
  40.2 1.3 %collective-permute-done.18 = f32[48,128]{1,0:T(8,128)S(1)} collective-permute-done((f32[48,128]{1,0:T(8,128)S(1)}, f32[48,128]{1,0:T(8,128)S(1)}, u32[]{:S(2)}, u32[]{:S(2)}) %collective-permute-start.18) | collective-permute-done | bytes 24608 | tf_op jit(solution)/shard_map/ppermute | solution.py:428
  41.5 1.0 %collective-permute-done.19 = f32[48,128]{1,0:T(8,128)S(1)} collective-permute-done((f32[48,128]{1,0:T(8,128)S(1)}, f32[48,128]{1,0:T(8,128)S(1)}, u32[]{:S(2)}, u32[]{:S(2)}) %collective-permute-start.19) | collective-permute-done | bytes 24608 | tf_op jit(solution)/shard_map/ppermute | solution.py:428
  42.5 2.6 %collective-permute-start.20 = (f32[48,128]{1,0:T(8,128)S(1)}, f32[48,128]{1,0:T(8,128)S(1)}, u32[]{:S(2)}, u32[]{:S(2)}) collective-permute-start(f32[48,128]{1,0:T(8,128)S(1)} %add_add_fusion), channel_id=1, source_target_pairs={{0,8},{1,9},{2,10},{3,11},{4,12},{5,13},{6,14},{7,15},{8,0},{9,1},... | collective-permute-start | bytes 73736 | tf_op jit(solution)/shard_map/ppermute | solution.py:428
  45.1 2.2 %collective-permute-done.20 = f32[48,128]{1,0:T(8,128)S(1)} collective-permute-done((f32[48,128]{1,0:T(8,128)S(1)}, f32[48,128]{1,0:T(8,128)S(1)}, u32[]{:S(2)}, u32[]{:S(2)}) %collective-permute-start.20) | collective-permute-done | bytes 24608 | tf_op jit(solution)/shard_map/ppermute | solution.py:428
  47.3 0.1 collective-permute-start.21
  47.4 1.4 %shard_map.101.work_ref = f32[32,64]{1,0:T(8,128)S(1)} custom-call(f32[48,128]{1,0:T(8,128)S(1)} %add.55.sums_ref), custom_call_target="tpu_custom_call" | custom-call | flops 1000000000 | tf_op jit(solution)/shard_map/pallas_call | solution.py:481
  48.8 0.0 collective-permute-done.21.other_ref
  48.8 1.2 %shard_map.102 = (f32[256,128]{1,0:T(8,128)}, f32[32,32]{1,0:T(8,128)}, f32[2,32,160]{2,1,0:T(8,128)}) custom-call(f32[8,128]{1,0:T(8,128)S(1)} %iota.7.flags_ref, f32[32,64]{1,0:T(8,128)S(1)} %shard_map.101.work_ref, f32[48,128]{1,0:T(8,128)S(1)} %add.55.sums_ref, f32[40,128]{1,0:T(8,128)S(1)} %collective-permute-done.21.other_ref, ...), custom_call_target="tpu_custom_call" | custom-call | tf_op jit(solution)/shard_map/pallas_call | solution.py:481
  (25 shorter events, 0.2 us)
Async XLA Ops:
  1.9 12.4 %copy-start.3 = (f32[8,128,128]{2,1,0:T(8,128)S(1)}, f32[8,128,128]{2,1,0:T(8,128)}, u32[]{:S(2)}) copy-start(f32[8,128,128]{2,1,0:T(8,128)} %mass_ref.3) | copy-start | bytes 1572868
  2.0 12.3 %copy-start.2 = (f32[8,128,128]{2,1,0:T(8,128)S(1)}, f32[8,128,128]{2,1,0:T(8,128)}, u32[]{:S(2)}) copy-start(f32[8,128,128]{2,1,0:T(8,128)} %stiff_ref.3) | copy-start | bytes 1572868
  2.0 5.3 %collective-permute-start.2 = (f32[2,64,128]{2,1,0:T(8,128)S(1)}, f32[2,64,128]{2,1,0:T(8,128)S(1)}, u32[]{:S(2)}, u32[]{:S(2)}) collective-permute-start(f32[2,64,128]{2,1,0:T(8,128)S(1)} %get-tuple-element.38), channel_id=1, source_target_pairs={{0,1},{1,0},{2,3},{3,2},{4,5},{5,4},{6,7},{7,6},{8,9},{9,8},{10,11... | collective-permute-start | bytes 196616 | tf_op jit(solution)/shard_map/ppermute | solution.py:440
  2.5 4.8 %collective-permute-start.3 = (f32[2,64,128]{2,1,0:T(8,128)S(1)}, f32[2,64,128]{2,1,0:T(8,128)S(1)}, u32[]{:S(2)}, u32[]{:S(2)}) collective-permute-start(f32[2,64,128]{2,1,0:T(8,128)S(1)} %get-tuple-element.42), channel_id=1, source_target_pairs={{0,16},{1,2},{2,1},{3,19},{16,0},{17,18},{18,17},{19,3},{4,20},{5,... | collective-permute-start | bytes 196616 | tf_op jit(solution)/shard_map/ppermute | solution.py:440
  5.1 9.2 %collective-permute-start = (f32[4,64,128]{2,1,0:T(8,128)S(1)}, f32[4,64,128]{2,1,0:T(8,128)S(1)}, u32[]{:S(2)}, u32[]{:S(2)}) collective-permute-start(f32[4,64,128]{2,1,0:T(8,128)S(1)} %get-tuple-element.36.row_a_ref), channel_id=1, source_target_pairs={{0,4},{4,0},{8,12},{12,8},{1,5},{5,1},{9,13},{13,9},{2,6},{6,2},{1... | collective-permute-start | bytes 393224 | tf_op jit(solution)/shard_map/ppermute | solution.py:440
  6.7 7.6 %collective-permute-start.1 = (f32[4,64,128]{2,1,0:T(8,128)S(1)}, f32[4,64,128]{2,1,0:T(8,128)S(1)}, u32[]{:S(2)}, u32[]{:S(2)}) collective-permute-start(f32[4,64,128]{2,1,0:T(8,128)S(1)} %get-tuple-element.37.row_b_ref), channel_id=1, source_target_pairs={{0,16},{4,8},{8,4},{12,28},{16,0},{20,24},{24,20},{28,12},{1,17},{... | collective-permute-start | bytes 393224 | tf_op jit(solution)/shard_map/ppermute | solution.py:440
  7.3 7.0 %copy-start.1 = (s32[5,2,4]{0,2,1:T(4,128)S(1)}, s32[5,2,4]{0,2,1:T(4,128)}, u32[]{:S(2)}) copy-start(s32[5,2,4]{0,2,1:T(4,128)} %param.9) | copy-start | bytes 484
  7.4 7.0 %copy-start = (s32[5,2,4]{0,2,1:T(4,128)S(1)}, s32[5,2,4]{0,2,1:T(4,128)}, u32[]{:S(2)}) copy-start(s32[5,2,4]{0,2,1:T(4,128)} %param.8) | copy-start | bytes 484
  7.4 5.3 %collective-permute-start.4 = (f32[2,64,128]{2,1,0:T(8,128)S(1)}, f32[2,64,128]{2,1,0:T(8,128)S(1)}, u32[]{:S(2)}, u32[]{:S(2)}) collective-permute-start(f32[2,64,128]{2,1,0:T(8,128)S(1)} %get-tuple-element.43), channel_id=1, source_target_pairs={{0,4},{4,0},{8,12},{12,8},{1,5},{5,1},{9,13},{13,9},{2,6},{6,2},{1... | collective-permute-start | bytes 196616 | tf_op jit(solution)/shard_map/ppermute | solution.py:440
  10.0 4.3 %collective-permute-start.5 = (f32[2,64,128]{2,1,0:T(8,128)S(1)}, f32[2,64,128]{2,1,0:T(8,128)S(1)}, u32[]{:S(2)}, u32[]{:S(2)}) collective-permute-start(f32[2,64,128]{2,1,0:T(8,128)S(1)} %get-tuple-element.44), channel_id=1, source_target_pairs={{0,16},{4,8},{8,4},{12,28},{16,0},{20,24},{24,20},{28,12},{1,17},{... | collective-permute-start | bytes 196616 | tf_op jit(solution)/shard_map/ppermute | solution.py:440
  11.0 8.9 %collective-permute-start.10 = (f32[4,96,128]{2,1,0:T(8,128)S(1)}, f32[4,96,128]{2,1,0:T(8,128)S(1)}, u32[]{:S(2)}, u32[]{:S(2)}) collective-permute-start(f32[4,96,128]{2,1,0:T(8,128)S(1)} %get-tuple-element.45.rest_a_ref.row_a_ref), channel_id=1, source_target_pairs={{0,4},{4,0},{8,12},{12,8},{1,5},{5,1},{9,13},{13,9},{2,6},{6,2},{1... | collective-permute-start | bytes 589832 | tf_op jit(solution)/shard_map/ppermute | solution.py:440
  12.7 7.3 %collective-permute-start.11 = (f32[4,96,128]{2,1,0:T(8,128)S(1)}, f32[4,96,128]{2,1,0:T(8,128)S(1)}, u32[]{:S(2)}, u32[]{:S(2)}) collective-permute-start(f32[4,96,128]{2,1,0:T(8,128)S(1)} %get-tuple-element.46.rest_b_ref.row_b_ref), channel_id=1, source_target_pairs={{0,16},{4,8},{8,4},{12,28},{16,0},{20,24},{24,20},{28,12},{1,17},{... | collective-permute-start | bytes 589832 | tf_op jit(solution)/shard_map/ppermute | solution.py:440
  17.0 4.5 %collective-permute-start.6 = (f32[5,32,128]{2,1,0:T(8,128)S(1)}, f32[5,32,128]{2,1,0:T(8,128)S(1)}, u32[]{:S(2)}, u32[]{:S(2)}) collective-permute-start(f32[5,32,128]{2,1,0:T(8,128)S(1)} %get-tuple-element.48.row_a_ref), channel_id=1, source_target_pairs={{0,4},{4,0},{8,12},{12,8},{1,5},{5,1},{9,13},{13,9},{2,6},{6,2},{1... | collective-permute-start | bytes 245768 | tf_op jit(solution)/shard_map/ppermute | solution.py:440
  18.5 7.7 %collective-permute-start.8 = (f32[4,32,128]{2,1,0:T(8,128)S(1)}, f32[4,32,128]{2,1,0:T(8,128)S(1)}, u32[]{:S(2)}, u32[]{:S(2)}) collective-permute-start(f32[4,32,128]{2,1,0:T(8,128)S(1)} %get-tuple-element.49.row_b_ref), channel_id=1, source_target_pairs={{0,16},{4,8},{8,4},{12,28},{16,0},{20,24},{24,20},{28,12},{1,17},{... | collective-permute-start | bytes 196616 | tf_op jit(solution)/shard_map/ppermute | solution.py:440
  20.0 7.5 %collective-permute-start.12 = (f32[4,96,128]{2,1,0:T(8,128)S(1)}, f32[4,96,128]{2,1,0:T(8,128)S(1)}, u32[]{:S(2)}, u32[]{:S(2)}) collective-permute-start(f32[4,96,128]{2,1,0:T(8,128)S(1)} %get-tuple-element.51), channel_id=1, source_target_pairs={{0,1},{1,0},{2,3},{3,2},{4,5},{5,4},{6,7},{7,6},{8,9},{9,8},{10,11... | collective-permute-start | bytes 589832 | tf_op jit(solution)/shard_map/ppermute | solution.py:440
  20.1 7.5 %collective-permute-start.13 = (f32[4,96,128]{2,1,0:T(8,128)S(1)}, f32[4,96,128]{2,1,0:T(8,128)S(1)}, u32[]{:S(2)}, u32[]{:S(2)}) collective-permute-start(f32[4,96,128]{2,1,0:T(8,128)S(1)} %get-tuple-element.52), channel_id=1, source_target_pairs={{0,16},{1,2},{2,1},{3,19},{16,0},{17,18},{18,17},{19,3},{4,20},{5,... | collective-permute-start | bytes 589832 | tf_op jit(solution)/shard_map/ppermute | solution.py:440
  21.5 4.6 %collective-permute-start.7 = (f32[32,128]{1,0:T(8,128)S(1)}, f32[32,128]{1,0:T(8,128)S(1)}, u32[]{:S(2)}, u32[]{:S(2)}) collective-permute-start(f32[32,128]{1,0:T(8,128)S(1)} %fusion), channel_id=1, source_target_pairs={{0,8},{1,9},{2,10},{3,11},{4,12},{5,13},{6,14},{7,15},{8,0},{9,1},... | collective-permute-start | bytes 49160 | tf_op jit(solution)/shard_map/ppermute | solution.py:428
  26.2 1.3 %collective-permute-start.9 = (f32[5,32,128]{2,1,0:T(8,128)S(1)}, f32[5,32,128]{2,1,0:T(8,128)S(1)}, u32[]{:S(2)}, u32[]{:S(2)}) collective-permute-start(f32[5,32,128]{2,1,0:T(8,128)S(1)} %get-tuple-element.50), channel_id=1, source_target_pairs={{0,1},{1,0},{2,3},{3,2},{4,5},{5,4},{6,7},{7,6},{8,9},{9,8},{10,11... | collective-permute-start | bytes 245768 | tf_op jit(solution)/shard_map/ppermute | solution.py:440
  26.3 5.1 %collective-permute-start.15 = (f32[4,32,128]{2,1,0:T(8,128)S(1)}, f32[4,32,128]{2,1,0:T(8,128)S(1)}, u32[]{:S(2)}, u32[]{:S(2)}) collective-permute-start(f32[4,32,128]{2,1,0:T(8,128)S(1)} %get-tuple-element.54), channel_id=1, source_target_pairs={{0,16},{1,2},{2,1},{3,19},{16,0},{17,18},{18,17},{19,3},{4,20},{5,... | collective-permute-start | bytes 196616 | tf_op jit(solution)/shard_map/ppermute | solution.py:440
  27.5 3.8 %collective-permute-start.14 = (f32[32,128]{1,0:T(8,128)S(1)}, f32[32,128]{1,0:T(8,128)S(1)}, u32[]{:S(2)}, u32[]{:S(2)}) collective-permute-start(f32[32,128]{1,0:T(8,128)S(1)} %bitcast_add_fusion), channel_id=1, source_target_pairs={{0,2},{1,3},{2,0},{3,1},{4,6},{5,7},{6,4},{7,5},{8,10},{9,11},{10,... | collective-permute-start | bytes 49160 | tf_op jit(solution)/shard_map/ppermute | solution.py:428
  34.2 1.3 %collective-permute-start.16 = (f32[48,128]{1,0:T(8,128)S(1)}, f32[48,128]{1,0:T(8,128)S(1)}, u32[]{:S(2)}, u32[]{:S(2)}) collective-permute-start(f32[48,128]{1,0:T(8,128)S(1)} %get-tuple-element.61), channel_id=1, source_target_pairs={{0,1},{1,0},{2,3},{3,2},{4,5},{5,4},{6,7},{7,6},{8,9},{9,8},{10,11... | collective-permute-start | bytes 73736 | tf_op jit(solution)/shard_map/ppermute | solution.py:428
  35.5 4.7 %collective-permute-start.17 = (f32[48,128]{1,0:T(8,128)S(1)}, f32[48,128]{1,0:T(8,128)S(1)}, u32[]{:S(2)}, u32[]{:S(2)}) collective-permute-start(f32[48,128]{1,0:T(8,128)S(1)} %add.51), channel_id=1, source_target_pairs={{0,6},{1,7},{2,4},{3,5},{4,2},{5,3},{6,0},{7,1},{8,14},{9,15},{10,... | collective-permute-start | bytes 73736 | tf_op jit(solution)/shard_map/ppermute | solution.py:428
  37.7 3.8 %collective-permute-start.18 = (f32[48,128]{1,0:T(8,128)S(1)}, f32[48,128]{1,0:T(8,128)S(1)}, u32[]{:S(2)}, u32[]{:S(2)}) collective-permute-start(f32[48,128]{1,0:T(8,128)S(1)} %add.51), channel_id=1, source_target_pairs={{0,2},{1,3},{2,0},{3,1},{4,6},{5,7},{6,4},{7,5},{8,10},{9,11},{10,... | collective-permute-start | bytes 73736 | tf_op jit(solution)/shard_map/ppermute | solution.py:428
  38.7 3.8 %collective-permute-start.19 = (f32[48,128]{1,0:T(8,128)S(1)}, f32[48,128]{1,0:T(8,128)S(1)}, u32[]{:S(2)}, u32[]{:S(2)}) collective-permute-start(f32[48,128]{1,0:T(8,128)S(1)} %add.51), channel_id=1, source_target_pairs={{0,4},{1,5},{2,6},{3,7},{4,0},{5,1},{6,2},{7,3},{8,12},{9,13},{10,... | collective-permute-start | bytes 73736 | tf_op jit(solution)/shard_map/ppermute | solution.py:428
  42.5 4.8 %collective-permute-start.20 = (f32[48,128]{1,0:T(8,128)S(1)}, f32[48,128]{1,0:T(8,128)S(1)}, u32[]{:S(2)}, u32[]{:S(2)}) collective-permute-start(f32[48,128]{1,0:T(8,128)S(1)} %add_add_fusion), channel_id=1, source_target_pairs={{0,8},{1,9},{2,10},{3,11},{4,12},{5,13},{6,14},{7,15},{8,0},{9,1},... | collective-permute-start | bytes 73736 | tf_op jit(solution)/shard_map/ppermute | solution.py:428
  47.3 1.5 %collective-permute-start.21 = (f32[40,128]{1,0:T(8,128)S(1)}, f32[40,128]{1,0:T(8,128)S(1)}, u32[]{:S(2)}, u32[]{:S(2)}) collective-permute-start(f32[40,128]{1,0:T(8,128)S(1)} %slice.13), channel_id=1, source_target_pairs={{0,1},{1,0},{2,3},{3,2},{4,5},{5,4},{6,7},{7,6},{8,9},{9,8},{10,11... | collective-permute-start | bytes 61448 | tf_op jit(solution)/shard_map/ppermute | solution.py:428

commit v16 on v14

--- a/solution.py
+++ b/solution.py
@@ -375,7 +375,7 @@
     unit = jnp.where(row_ids == column_ids, 1.0, 0.0).astype(F32)
     work = jnp.concatenate([gram, unit], axis=1)
     rows = lax.broadcasted_iota(jnp.int32, work.shape, 0)
-    group = 4
+    group = 8
     for j in range(0, block, group):
         columns = [
             jnp.broadcast_to(work[:, j + a : j + a + 1], work.shape) for a in range(group)
@@ -449,8 +449,12 @@
 
 def half_total(sent, kept):
     kept = kept + swap(sent, 1)
-    kept = (kept + swap(kept, 6)) + (swap(kept, 2) + swap(kept, 4))
-    return total_over(kept, 8, lax.axis_size(("px", "py")))
+    count_py = lax.axis_size("py")
+    kept = total_over(kept, 2, count_py)
+    if lax.axis_size("px") != 4:
+        return total_over(kept, count_py, count_py * lax.axis_size("px"))
+    near, far, cross = (swap(kept, step * count_py) for step in (1, 2, 3))
+    return (kept + far) + (near + cross)
 
 
 def shape(*dims, dtype=F32):

time: 50.2 us -> 51.8 us (1.032)
  waiting for transfers between devices: 13 us -> 16 us
  starting transfers between devices: 26.2 us -> 25.4 us
    ppermute x8, waiting for transfers between devices: 11.8 us -> 14.7 us  [swap(): return lax.ppermute(value, axes, pairs)]
    ppermute x8, starting transfers between devices: 9.41 us -> 8.64 us  [swap(): return lax.ppermute(value, axes, pairs)]
  transfers between devices with their start and end apart: 22 -> 22, of which waited for: 11 -> 12; matrix products, arithmetic and copies ran while one was open for 0% -> 0% of each run, Pallas kernels for 9% -> 8%
where the time goes in v16:
time: 51.8 us; the launch traced here: 51.7 us
  starting transfers between devices  25.4 us (49%)
  waiting for transfers between devices  16 us (31%)
  Pallas kernels  8.17 us (16%)
  other arithmetic  1.2 us (2%)
  between operations  0.84 us (2%)
    ppermute x8, waiting for transfers between devices, swap(): return lax.ppermute(value, axes, pairs)  14.7 us
    ppermute x7, starting transfers between devices, exchange(): lax.ppermute(message_b, ('case', axis), pairs)  8.78 us
    ppermute x8, starting transfers between devices, swap(): return lax.ppermute(value, axes, pairs)  8.64 us
    pallas_call x10, Pallas kernels, call(): pl.pallas_call(kernel, out_shape=outputs, in_specs=specs, out_specs=[VMEM...  8.17 us
    ppermute x7, starting transfers between devices, exchange(): lax.ppermute(message_a, axis, near)  8 us
    concatenate x1, other arithmetic, shards(): vectors = jnp.concatenate([basis, previous.reshape(-1, side)], axis=0)  1.16 us
  transfers between devices with their start and end apart: 22, of which 12 were waited for; matrix products, arithmetic and copies ran while one was open for 0% of the time, Pallas kernels for 8%

profile of v16, /device:TPU:0, one launch (start us, length us, event | category | flops | bytes accessed | tf_op | source)
XLA Modules:
  0.0 51.7 jit_solution(4455586600103182613)
XLA Ops:
  0.7 1.2 %pad_maximum_fusion.vectors_ref = f32[1280,128]{1,0:T(8,128)S(1)} fusion(f32[256,128]{1,0:T(8,128)} %bitcast.24, f32[1024,128]{1,0:T(8,128)} %bitcast.23), kind=kLoop, calls=%fused_computation | loop fusion | flops 163840 | bytes 1310720 | tf_op jit(solution)/shard_map/concatenate | solution.py:473
  1.8 0.1 iota.7.flags_ref
  1.9 0.1 shard_map.93
  2.0 0.0 copy-start.2
  2.0 0.5 %collective-permute-start.2 = (f32[2,64,128]{2,1,0:T(8,128)S(1)}, f32[2,64,128]{2,1,0:T(8,128)S(1)}, u32[]{:S(2)}, u32[]{:S(2)}) collective-permute-start(f32[2,64,128]{2,1,0:T(8,128)S(1)} %get-tuple-element.38), channel_id=1, source_target_pairs={{0,1},{1,0},{2,3},{3,2},{4,5},{5,4},{6,7},{7,6},{8,9},{9,8},{10,11... | collective-permute-start | bytes 196616 | tf_op jit(solution)/shard_map/ppermute | solution.py:440
  2.5 2.6 %collective-permute-start.3 = (f32[2,64,128]{2,1,0:T(8,128)S(1)}, f32[2,64,128]{2,1,0:T(8,128)S(1)}, u32[]{:S(2)}, u32[]{:S(2)}) collective-permute-start(f32[2,64,128]{2,1,0:T(8,128)S(1)} %get-tuple-element.42), channel_id=1, source_target_pairs={{0,16},{1,2},{2,1},{3,19},{16,0},{17,18},{18,17},{19,3},{4,20},{5,... | collective-permute-start | bytes 196616 | tf_op jit(solution)/shard_map/ppermute | solution.py:440
  5.1 1.6 %collective-permute-start = (f32[4,64,128]{2,1,0:T(8,128)S(1)}, f32[4,64,128]{2,1,0:T(8,128)S(1)}, u32[]{:S(2)}, u32[]{:S(2)}) collective-permute-start(f32[4,64,128]{2,1,0:T(8,128)S(1)} %get-tuple-element.36.row_a_ref), channel_id=1, source_target_pairs={{0,4},{4,0},{8,12},{12,8},{1,5},{5,1},{9,13},{13,9},{2,6},{6,2},{1... | collective-permute-start | bytes 393224 | tf_op jit(solution)/shard_map/ppermute | solution.py:440
  6.7 0.5 collective-permute-start.1
  7.2 0.1 shard_map.94
  7.2 0.0 collective-permute-done.2.side_a_ref.from_side_a_ref
  7.2 0.1 collective-permute-done.3.side_b_ref.from_side_b_ref
  7.4 0.0 copy-start
  7.4 2.7 %collective-permute-start.4 = (f32[2,64,128]{2,1,0:T(8,128)S(1)}, f32[2,64,128]{2,1,0:T(8,128)S(1)}, u32[]{:S(2)}, u32[]{:S(2)}) collective-permute-start(f32[2,64,128]{2,1,0:T(8,128)S(1)} %get-tuple-element.43), channel_id=1, source_target_pairs={{0,4},{4,0},{8,12},{12,8},{1,5},{5,1},{9,13},{13,9},{2,6},{6,2},{1... | collective-permute-start | bytes 196616 | tf_op jit(solution)/shard_map/ppermute | solution.py:440
  10.0 1.0 %collective-permute-start.5 = (f32[2,64,128]{2,1,0:T(8,128)S(1)}, f32[2,64,128]{2,1,0:T(8,128)S(1)}, u32[]{:S(2)}, u32[]{:S(2)}) collective-permute-start(f32[2,64,128]{2,1,0:T(8,128)S(1)} %get-tuple-element.44), channel_id=1, source_target_pairs={{0,16},{4,8},{8,4},{12,28},{16,0},{20,24},{24,20},{28,12},{1,17},{... | collective-permute-start | bytes 196616 | tf_op jit(solution)/shard_map/ppermute | solution.py:440
  11.0 1.6 %collective-permute-start.8 = (f32[4,96,128]{2,1,0:T(8,128)S(1)}, f32[4,96,128]{2,1,0:T(8,128)S(1)}, u32[]{:S(2)}, u32[]{:S(2)}) collective-permute-start(f32[4,96,128]{2,1,0:T(8,128)S(1)} %get-tuple-element.45.rest_a_ref.row_a_ref), channel_id=1, source_target_pairs={{0,4},{4,0},{8,12},{12,8},{1,5},{5,1},{9,13},{13,9},{2,6},{6,2},{1... | collective-permute-start | bytes 589832 | tf_op jit(solution)/shard_map/ppermute | solution.py:440
  12.7 0.0 collective-permute-done.4.from_corner_a_ref
  12.7 1.5 %collective-permute-start.9 = (f32[4,96,128]{2,1,0:T(8,128)S(1)}, f32[4,96,128]{2,1,0:T(8,128)S(1)}, u32[]{:S(2)}, u32[]{:S(2)}) collective-permute-start(f32[4,96,128]{2,1,0:T(8,128)S(1)} %get-tuple-element.46.rest_b_ref.row_b_ref), channel_id=1, source_target_pairs={{0,16},{4,8},{8,4},{12,28},{16,0},{20,24},{24,20},{28,12},{1,17},{... | collective-permute-start | bytes 589832 | tf_op jit(solution)/shard_map/ppermute | solution.py:440
  14.2 0.1 collective-permute-done.5.from_corner_b_ref
  14.3 0.0 collective-permute-done.from_row_a_ref
  14.3 2.6 %shard_map.96 = (f32[5,32,128]{2,1,0:T(8,128)S(1)}, f32[4,32,128]{2,1,0:T(8,128)S(1)}, f32[32,128]{1,0:T(8,128)S(1)}, f32[24,32,128]{2,1,0:T(8,128)S(1)}) custom-call(s32[8,5]{1,0:T(8,128)S(1)} %bitcast.19, s32[8,5]{1,0:T(8,128)S(1)} %bitcast.21, f32[8,128]{1,0:T(8,128)S(1)} %iota.7.flags_ref, f32[4,64,128]{2,1,0:T(8,128)S(1)} %get-tuple-element.36.row_a_ref, ...), custom_call_target="tpu_custom_call" | custom-call | flops 1000000000 | tf_op jit(solution)/shard_map/pallas_call | solution.py:485
  17.0 1.5 %collective-permute-start.6 = (f32[5,32,128]{2,1,0:T(8,128)S(1)}, f32[5,32,128]{2,1,0:T(8,128)S(1)}, u32[]{:S(2)}, u32[]{:S(2)}) collective-permute-start(f32[5,32,128]{2,1,0:T(8,128)S(1)} %get-tuple-element.48.row_a_ref), channel_id=1, source_target_pairs={{0,4},{4,0},{8,12},{12,8},{1,5},{5,1},{9,13},{13,9},{2,6},{6,2},{1... | collective-permute-start | bytes 245768 | tf_op jit(solution)/shard_map/ppermute | solution.py:440
  18.5 1.5 %collective-permute-start.12 = (f32[4,32,128]{2,1,0:T(8,128)S(1)}, f32[4,32,128]{2,1,0:T(8,128)S(1)}, u32[]{:S(2)}, u32[]{:S(2)}) collective-permute-start(f32[4,32,128]{2,1,0:T(8,128)S(1)} %get-tuple-element.52.row_b_ref), channel_id=1, source_target_pairs={{0,16},{4,8},{8,4},{12,28},{16,0},{20,24},{24,20},{28,12},{1,17},{... | collective-permute-start | bytes 196616 | tf_op jit(solution)/shard_map/ppermute | solution.py:440
  20.0 0.1 collective-permute-start.10
  20.1 0.6 %collective-permute-start.11 = (f32[4,96,128]{2,1,0:T(8,128)S(1)}, f32[4,96,128]{2,1,0:T(8,128)S(1)}, u32[]{:S(2)}, u32[]{:S(2)}) collective-permute-start(f32[4,96,128]{2,1,0:T(8,128)S(1)} %get-tuple-element.50), channel_id=1, source_target_pairs={{0,16},{1,2},{2,1},{3,19},{16,0},{17,18},{18,17},{19,3},{4,20},{5,... | collective-permute-start | bytes 589832 | tf_op jit(solution)/shard_map/ppermute | solution.py:440
  20.7 0.8 %collective-permute-done.6.from_row_a_ref = f32[5,32,128]{2,1,0:T(8,128)S(1)} collective-permute-done((f32[5,32,128]{2,1,0:T(8,128)S(1)}, f32[5,32,128]{2,1,0:T(8,128)S(1)}, u32[]{:S(2)}, u32[]{:S(2)}) %collective-permute-start.6) | collective-permute-done | bytes 81952 | tf_op jit(solution)/shard_map/ppermute | solution.py:440
  21.5 2.3 %collective-permute-start.7 = (f32[32,128]{1,0:T(8,128)S(1)}, f32[32,128]{1,0:T(8,128)S(1)}, u32[]{:S(2)}, u32[]{:S(2)}) collective-permute-start(f32[32,128]{1,0:T(8,128)S(1)} %fusion.1), channel_id=1, source_target_pairs={{0,8},{1,9},{2,10},{3,11},{4,12},{5,13},{6,14},{7,15},{8,0},{9,1},... | collective-permute-start | bytes 49160 | tf_op jit(solution)/shard_map/ppermute | solution.py:428
  23.8 2.4 %collective-permute-done.7 = f32[32,128]{1,0:T(8,128)S(1)} collective-permute-done((f32[32,128]{1,0:T(8,128)S(1)}, f32[32,128]{1,0:T(8,128)S(1)}, u32[]{:S(2)}, u32[]{:S(2)}) %collective-permute-start.7) | collective-permute-done | bytes 16416 | tf_op jit(solution)/shard_map/ppermute | solution.py:428
  26.2 0.1 collective-permute-start.13
  26.3 1.1 %collective-permute-start.15 = (f32[4,32,128]{2,1,0:T(8,128)S(1)}, f32[4,32,128]{2,1,0:T(8,128)S(1)}, u32[]{:S(2)}, u32[]{:S(2)}) collective-permute-start(f32[4,32,128]{2,1,0:T(8,128)S(1)} %get-tuple-element.54), channel_id=1, source_target_pairs={{0,16},{1,2},{2,1},{3,19},{16,0},{17,18},{18,17},{19,3},{4,20},{5,... | collective-permute-start | bytes 196616 | tf_op jit(solution)/shard_map/ppermute | solution.py:440
  27.3 0.2 collective-permute-done.13.from_side_a_ref
  27.5 0.9 %collective-permute-start.14 = (f32[32,128]{1,0:T(8,128)S(1)}, f32[32,128]{1,0:T(8,128)S(1)}, u32[]{:S(2)}, u32[]{:S(2)}) collective-permute-start(f32[32,128]{1,0:T(8,128)S(1)} %fusion), channel_id=1, source_target_pairs={{0,2},{1,3},{2,0},{3,1},{4,6},{5,7},{6,4},{7,5},{8,10},{9,11},{10,... | collective-permute-start | bytes 49160 | tf_op jit(solution)/shard_map/ppermute | solution.py:428
  28.5 0.3 shard_map.99
  28.8 2.5 %collective-permute-done.14 = f32[32,128]{1,0:T(8,128)S(1)} collective-permute-done((f32[32,128]{1,0:T(8,128)S(1)}, f32[32,128]{1,0:T(8,128)S(1)}, u32[]{:S(2)}, u32[]{:S(2)}) %collective-permute-start.14) | collective-permute-done | bytes 16416 | tf_op jit(solution)/shard_map/ppermute | solution.py:428
  31.3 2.9 %shard_map.100 = (f32[4,32,128]{2,1,0:T(8,128)S(1)}, f32[4,32,128]{2,1,0:T(8,128)S(1)}, f32[32,128]{1,0:T(8,128)}, f32[48,128]{1,0:T(8,128)S(1)}, f32[48,128]{1,0:T(8,128)S(1)}) custom-call(s32[8,5]{1,0:T(8,128)S(1)} %bitcast.20, s32[8,5]{1,0:T(8,128)S(1)} %bitcast.22, f32[8,128]{1,0:T(8,128)S(1)} %iota.7.flags_ref, f32[32,128]{1,0:T(8,128)S(1)} %add.50.partial_ref, ...), custom_call_target="tpu_custom_call" | custom-call | tf_op jit(solution)/shard_map/pallas_call | solution.py:485
  34.2 0.1 collective-permute-start.16
  34.3 1.2 %collective-permute-done.16 = f32[48,128]{1,0:T(8,128)S(1)} collective-permute-done((f32[48,128]{1,0:T(8,128)S(1)}, f32[48,128]{1,0:T(8,128)S(1)}, u32[]{:S(2)}, u32[]{:S(2)}) %collective-permute-start.16) | collective-permute-done | bytes 24608 | tf_op jit(solution)/shard_map/ppermute | solution.py:428
  35.4 0.9 %collective-permute-start.17 = (f32[48,128]{1,0:T(8,128)S(1)}, f32[48,128]{1,0:T(8,128)S(1)}, u32[]{:S(2)}, u32[]{:S(2)}) collective-permute-start(f32[48,128]{1,0:T(8,128)S(1)} %add.51), channel_id=1, source_target_pairs={{0,2},{1,3},{2,0},{3,1},{4,6},{5,7},{6,4},{7,5},{8,10},{9,11},{10,... | collective-permute-start | bytes 73736 | tf_op jit(solution)/shard_map/ppermute | solution.py:428
  36.4 2.9 %collective-permute-done.17 = f32[48,128]{1,0:T(8,128)S(1)} collective-permute-done((f32[48,128]{1,0:T(8,128)S(1)}, f32[48,128]{1,0:T(8,128)S(1)}, u32[]{:S(2)}, u32[]{:S(2)}) %collective-permute-start.17) | collective-permute-done | bytes 24608 | tf_op jit(solution)/shard_map/ppermute | solution.py:428
  39.3 2.4 %collective-permute-start.18 = (f32[48,128]{1,0:T(8,128)S(1)}, f32[48,128]{1,0:T(8,128)S(1)}, u32[]{:S(2)}, u32[]{:S(2)}) collective-permute-start(f32[48,128]{1,0:T(8,128)S(1)} %add.52), channel_id=1, source_target_pairs={{0,8},{1,9},{2,10},{3,11},{4,12},{5,13},{6,14},{7,15},{8,0},{9,1},... | collective-permute-start | bytes 73736 | tf_op jit(solution)/shard_map/ppermute | solution.py:428
  41.7 1.8 %collective-permute-start.19 = (f32[48,128]{1,0:T(8,128)S(1)}, f32[48,128]{1,0:T(8,128)S(1)}, u32[]{:S(2)}, u32[]{:S(2)}) collective-permute-start(f32[48,128]{1,0:T(8,128)S(1)} %add.52), channel_id=1, source_target_pairs={{0,4},{1,5},{2,6},{3,7},{4,0},{5,1},{6,2},{7,3},{8,12},{9,13},{10,... | collective-permute-start | bytes 73736 | tf_op jit(solution)/shard_map/ppermute | solution.py:428
  43.6 0.1 collective-permute-start.20
  43.7 0.3 collective-permute-done.18
  44.0 1.5 %collective-permute-done.19 = f32[48,128]{1,0:T(8,128)S(1)} collective-permute-done((f32[48,128]{1,0:T(8,128)S(1)}, f32[48,128]{1,0:T(8,128)S(1)}, u32[]{:S(2)}, u32[]{:S(2)}) %collective-permute-start.19) | collective-permute-done | bytes 24608 | tf_op jit(solution)/shard_map/ppermute | solution.py:428
  45.6 3.6 %collective-permute-done.20 = f32[48,128]{1,0:T(8,128)S(1)} collective-permute-done((f32[48,128]{1,0:T(8,128)S(1)}, f32[48,128]{1,0:T(8,128)S(1)}, u32[]{:S(2)}, u32[]{:S(2)}) %collective-permute-start.20) | collective-permute-done | bytes 24608 | tf_op jit(solution)/shard_map/ppermute | solution.py:428
  49.2 0.1 collective-permute-start.21
  49.3 0.9 %shard_map.101.work_ref = f32[32,64]{1,0:T(8,128)S(1)} custom-call(f32[48,128]{1,0:T(8,128)S(1)} %add_add_fusion.sums_ref), custom_call_target="tpu_custom_call" | custom-call | flops 1000000000 | tf_op jit(solution)/shard_map/pallas_call | solution.py:485
  50.2 0.3 collective-permute-done.21.other_ref
  50.5 1.2 %shard_map.102 = (f32[256,128]{1,0:T(8,128)}, f32[32,32]{1,0:T(8,128)}, f32[2,32,160]{2,1,0:T(8,128)}) custom-call(f32[8,128]{1,0:T(8,128)S(1)} %iota.7.flags_ref, f32[32,64]{1,0:T(8,128)S(1)} %shard_map.101.work_ref, f32[48,128]{1,0:T(8,128)S(1)} %add_add_fusion.sums_ref, f32[40,128]{1,0:T(8,128)S(1)} %collective-permute-done.21.other_ref, ...), custom_call_target="tpu_custom_call" | custom-call | tf_op jit(solution)/shard_map/pallas_call | solution.py:485
  (25 shorter events, 0.2 us)
Async XLA Ops:
  1.9 12.4 %copy-start.3 = (f32[8,128,128]{2,1,0:T(8,128)S(1)}, f32[8,128,128]{2,1,0:T(8,128)}, u32[]{:S(2)}) copy-start(f32[8,128,128]{2,1,0:T(8,128)} %mass_ref.3) | copy-start | bytes 1572868
  2.0 12.3 %copy-start.2 = (f32[8,128,128]{2,1,0:T(8,128)S(1)}, f32[8,128,128]{2,1,0:T(8,128)}, u32[]{:S(2)}) copy-start(f32[8,128,128]{2,1,0:T(8,128)} %stiff_ref.3) | copy-start | bytes 1572868
  2.0 5.3 %collective-permute-start.2 = (f32[2,64,128]{2,1,0:T(8,128)S(1)}, f32[2,64,128]{2,1,0:T(8,128)S(1)}, u32[]{:S(2)}, u32[]{:S(2)}) collective-permute-start(f32[2,64,128]{2,1,0:T(8,128)S(1)} %get-tuple-element.38), channel_id=1, source_target_pairs={{0,1},{1,0},{2,3},{3,2},{4,5},{5,4},{6,7},{7,6},{8,9},{9,8},{10,11... | collective-permute-start | bytes 196616 | tf_op jit(solution)/shard_map/ppermute | solution.py:440
  2.5 4.8 %collective-permute-start.3 = (f32[2,64,128]{2,1,0:T(8,128)S(1)}, f32[2,64,128]{2,1,0:T(8,128)S(1)}, u32[]{:S(2)}, u32[]{:S(2)}) collective-permute-start(f32[2,64,128]{2,1,0:T(8,128)S(1)} %get-tuple-element.42), channel_id=1, source_target_pairs={{0,16},{1,2},{2,1},{3,19},{16,0},{17,18},{18,17},{19,3},{4,20},{5,... | collective-permute-start | bytes 196616 | tf_op jit(solution)/shard_map/ppermute | solution.py:440
  5.1 9.2 %collective-permute-start = (f32[4,64,128]{2,1,0:T(8,128)S(1)}, f32[4,64,128]{2,1,0:T(8,128)S(1)}, u32[]{:S(2)}, u32[]{:S(2)}) collective-permute-start(f32[4,64,128]{2,1,0:T(8,128)S(1)} %get-tuple-element.36.row_a_ref), channel_id=1, source_target_pairs={{0,4},{4,0},{8,12},{12,8},{1,5},{5,1},{9,13},{13,9},{2,6},{6,2},{1... | collective-permute-start | bytes 393224 | tf_op jit(solution)/shard_map/ppermute | solution.py:440
  6.7 7.6 %collective-permute-start.1 = (f32[4,64,128]{2,1,0:T(8,128)S(1)}, f32[4,64,128]{2,1,0:T(8,128)S(1)}, u32[]{:S(2)}, u32[]{:S(2)}) collective-permute-start(f32[4,64,128]{2,1,0:T(8,128)S(1)} %get-tuple-element.37.row_b_ref), channel_id=1, source_target_pairs={{0,16},{4,8},{8,4},{12,28},{16,0},{20,24},{24,20},{28,12},{1,17},{... | collective-permute-start | bytes 393224 | tf_op jit(solution)/shard_map/ppermute | solution.py:440
  7.3 7.0 %copy-start.1 = (s32[5,2,4]{0,2,1:T(4,128)S(1)}, s32[5,2,4]{0,2,1:T(4,128)}, u32[]{:S(2)}) copy-start(s32[5,2,4]{0,2,1:T(4,128)} %param.9) | copy-start | bytes 484
  7.4 7.0 %copy-start = (s32[5,2,4]{0,2,1:T(4,128)S(1)}, s32[5,2,4]{0,2,1:T(4,128)}, u32[]{:S(2)}) copy-start(s32[5,2,4]{0,2,1:T(4,128)} %param.8) | copy-start | bytes 484
  7.4 5.3 %collective-permute-start.4 = (f32[2,64,128]{2,1,0:T(8,128)S(1)}, f32[2,64,128]{2,1,0:T(8,128)S(1)}, u32[]{:S(2)}, u32[]{:S(2)}) collective-permute-start(f32[2,64,128]{2,1,0:T(8,128)S(1)} %get-tuple-element.43), channel_id=1, source_target_pairs={{0,4},{4,0},{8,12},{12,8},{1,5},{5,1},{9,13},{13,9},{2,6},{6,2},{1... | collective-permute-start | bytes 196616 | tf_op jit(solution)/shard_map/ppermute | solution.py:440
  10.0 4.3 %collective-permute-start.5 = (f32[2,64,128]{2,1,0:T(8,128)S(1)}, f32[2,64,128]{2,1,0:T(8,128)S(1)}, u32[]{:S(2)}, u32[]{:S(2)}) collective-permute-start(f32[2,64,128]{2,1,0:T(8,128)S(1)} %get-tuple-element.44), channel_id=1, source_target_pairs={{0,16},{4,8},{8,4},{12,28},{16,0},{20,24},{24,20},{28,12},{1,17},{... | collective-permute-start | bytes 196616 | tf_op jit(solution)/shard_map/ppermute | solution.py:440
  11.0 8.9 %collective-permute-start.8 = (f32[4,96,128]{2,1,0:T(8,128)S(1)}, f32[4,96,128]{2,1,0:T(8,128)S(1)}, u32[]{:S(2)}, u32[]{:S(2)}) collective-permute-start(f32[4,96,128]{2,1,0:T(8,128)S(1)} %get-tuple-element.45.rest_a_ref.row_a_ref), channel_id=1, source_target_pairs={{0,4},{4,0},{8,12},{12,8},{1,5},{5,1},{9,13},{13,9},{2,6},{6,2},{1... | collective-permute-start | bytes 589832 | tf_op jit(solution)/shard_map/ppermute | solution.py:440
  12.7 7.3 %collective-permute-start.9 = (f32[4,96,128]{2,1,0:T(8,128)S(1)}, f32[4,96,128]{2,1,0:T(8,128)S(1)}, u32[]{:S(2)}, u32[]{:S(2)}) collective-permute-start(f32[4,96,128]{2,1,0:T(8,128)S(1)} %get-tuple-element.46.rest_b_ref.row_b_ref), channel_id=1, source_target_pairs={{0,16},{4,8},{8,4},{12,28},{16,0},{20,24},{24,20},{28,12},{1,17},{... | collective-permute-start | bytes 589832 | tf_op jit(solution)/shard_map/ppermute | solution.py:440
  17.0 4.5 %collective-permute-start.6 = (f32[5,32,128]{2,1,0:T(8,128)S(1)}, f32[5,32,128]{2,1,0:T(8,128)S(1)}, u32[]{:S(2)}, u32[]{:S(2)}) collective-permute-start(f32[5,32,128]{2,1,0:T(8,128)S(1)} %get-tuple-element.48.row_a_ref), channel_id=1, source_target_pairs={{0,4},{4,0},{8,12},{12,8},{1,5},{5,1},{9,13},{13,9},{2,6},{6,2},{1... | collective-permute-start | bytes 245768 | tf_op jit(solution)/shard_map/ppermute | solution.py:440
  18.5 7.7 %collective-permute-start.12 = (f32[4,32,128]{2,1,0:T(8,128)S(1)}, f32[4,32,128]{2,1,0:T(8,128)S(1)}, u32[]{:S(2)}, u32[]{:S(2)}) collective-permute-start(f32[4,32,128]{2,1,0:T(8,128)S(1)} %get-tuple-element.52.row_b_ref), channel_id=1, source_target_pairs={{0,16},{4,8},{8,4},{12,28},{16,0},{20,24},{24,20},{28,12},{1,17},{... | collective-permute-start | bytes 196616 | tf_op jit(solution)/shard_map/ppermute | solution.py:440
  20.0 6.2 %collective-permute-start.10 = (f32[4,96,128]{2,1,0:T(8,128)S(1)}, f32[4,96,128]{2,1,0:T(8,128)S(1)}, u32[]{:S(2)}, u32[]{:S(2)}) collective-permute-start(f32[4,96,128]{2,1,0:T(8,128)S(1)} %get-tuple-element.49), channel_id=1, source_target_pairs={{0,1},{1,0},{2,3},{3,2},{4,5},{5,4},{6,7},{7,6},{8,9},{9,8},{10,11... | collective-permute-start | bytes 589832 | tf_op jit(solution)/shard_map/ppermute | solution.py:440
  20.1 6.1 %collective-permute-start.11 = (f32[4,96,128]{2,1,0:T(8,128)S(1)}, f32[4,96,128]{2,1,0:T(8,128)S(1)}, u32[]{:S(2)}, u32[]{:S(2)}) collective-permute-start(f32[4,96,128]{2,1,0:T(8,128)S(1)} %get-tuple-element.50), channel_id=1, source_target_pairs={{0,16},{1,2},{2,1},{3,19},{16,0},{17,18},{18,17},{19,3},{4,20},{5,... | collective-permute-start | bytes 589832 | tf_op jit(solution)/shard_map/ppermute | solution.py:440
  21.5 4.6 %collective-permute-start.7 = (f32[32,128]{1,0:T(8,128)S(1)}, f32[32,128]{1,0:T(8,128)S(1)}, u32[]{:S(2)}, u32[]{:S(2)}) collective-permute-start(f32[32,128]{1,0:T(8,128)S(1)} %fusion.1), channel_id=1, source_target_pairs={{0,8},{1,9},{2,10},{3,11},{4,12},{5,13},{6,14},{7,15},{8,0},{9,1},... | collective-permute-start | bytes 49160 | tf_op jit(solution)/shard_map/ppermute | solution.py:428
  26.2 1.3 %collective-permute-start.13 = (f32[5,32,128]{2,1,0:T(8,128)S(1)}, f32[5,32,128]{2,1,0:T(8,128)S(1)}, u32[]{:S(2)}, u32[]{:S(2)}) collective-permute-start(f32[5,32,128]{2,1,0:T(8,128)S(1)} %get-tuple-element.53), channel_id=1, source_target_pairs={{0,1},{1,0},{2,3},{3,2},{4,5},{5,4},{6,7},{7,6},{8,9},{9,8},{10,11... | collective-permute-start | bytes 245768 | tf_op jit(solution)/shard_map/ppermute | solution.py:440
  26.3 5.0 %collective-permute-start.15 = (f32[4,32,128]{2,1,0:T(8,128)S(1)}, f32[4,32,128]{2,1,0:T(8,128)S(1)}, u32[]{:S(2)}, u32[]{:S(2)}) collective-permute-start(f32[4,32,128]{2,1,0:T(8,128)S(1)} %get-tuple-element.54), channel_id=1, source_target_pairs={{0,16},{1,2},{2,1},{3,19},{16,0},{17,18},{18,17},{19,3},{4,20},{5,... | collective-permute-start | bytes 196616 | tf_op jit(solution)/shard_map/ppermute | solution.py:440
  27.5 3.7 %collective-permute-start.14 = (f32[32,128]{1,0:T(8,128)S(1)}, f32[32,128]{1,0:T(8,128)S(1)}, u32[]{:S(2)}, u32[]{:S(2)}) collective-permute-start(f32[32,128]{1,0:T(8,128)S(1)} %fusion), channel_id=1, source_target_pairs={{0,2},{1,3},{2,0},{3,1},{4,6},{5,7},{6,4},{7,5},{8,10},{9,11},{10,... | collective-permute-start | bytes 49160 | tf_op jit(solution)/shard_map/ppermute | solution.py:428
  34.2 1.3 %collective-permute-start.16 = (f32[48,128]{1,0:T(8,128)S(1)}, f32[48,128]{1,0:T(8,128)S(1)}, u32[]{:S(2)}, u32[]{:S(2)}) collective-permute-start(f32[48,128]{1,0:T(8,128)S(1)} %get-tuple-element.61), channel_id=1, source_target_pairs={{0,1},{1,0},{2,3},{3,2},{4,5},{5,4},{6,7},{7,6},{8,9},{9,8},{10,11... | collective-permute-start | bytes 73736 | tf_op jit(solution)/shard_map/ppermute | solution.py:428
  35.4 3.8 %collective-permute-start.17 = (f32[48,128]{1,0:T(8,128)S(1)}, f32[48,128]{1,0:T(8,128)S(1)}, u32[]{:S(2)}, u32[]{:S(2)}) collective-permute-start(f32[48,128]{1,0:T(8,128)S(1)} %add.51), channel_id=1, source_target_pairs={{0,2},{1,3},{2,0},{3,1},{4,6},{5,7},{6,4},{7,5},{8,10},{9,11},{10,... | collective-permute-start | bytes 73736 | tf_op jit(solution)/shard_map/ppermute | solution.py:428
  39.3 4.7 %collective-permute-start.18 = (f32[48,128]{1,0:T(8,128)S(1)}, f32[48,128]{1,0:T(8,128)S(1)}, u32[]{:S(2)}, u32[]{:S(2)}) collective-permute-start(f32[48,128]{1,0:T(8,128)S(1)} %add.52), channel_id=1, source_target_pairs={{0,8},{1,9},{2,10},{3,11},{4,12},{5,13},{6,14},{7,15},{8,0},{9,1},... | collective-permute-start | bytes 73736 | tf_op jit(solution)/shard_map/ppermute | solution.py:428
  41.7 3.8 %collective-permute-start.19 = (f32[48,128]{1,0:T(8,128)S(1)}, f32[48,128]{1,0:T(8,128)S(1)}, u32[]{:S(2)}, u32[]{:S(2)}) collective-permute-start(f32[48,128]{1,0:T(8,128)S(1)} %add.52), channel_id=1, source_target_pairs={{0,4},{1,5},{2,6},{3,7},{4,0},{5,1},{6,2},{7,3},{8,12},{9,13},{10,... | collective-permute-start | bytes 73736 | tf_op jit(solution)/shard_map/ppermute | solution.py:428
  43.6 5.6 %collective-permute-start.20 = (f32[48,128]{1,0:T(8,128)S(1)}, f32[48,128]{1,0:T(8,128)S(1)}, u32[]{:S(2)}, u32[]{:S(2)}) collective-permute-start(f32[48,128]{1,0:T(8,128)S(1)} %add.52), channel_id=1, source_target_pairs={{0,12},{1,13},{2,14},{3,15},{4,8},{5,9},{6,10},{7,11},{8,4},{9,5},... | collective-permute-start | bytes 73736 | tf_op jit(solution)/shard_map/ppermute | solution.py:428
  49.2 1.3 %collective-permute-start.21 = (f32[40,128]{1,0:T(8,128)S(1)}, f32[40,128]{1,0:T(8,128)S(1)}, u32[]{:S(2)}, u32[]{:S(2)}) collective-permute-start(f32[40,128]{1,0:T(8,128)S(1)} %slice.14), channel_id=1, source_target_pairs={{0,1},{1,0},{2,3},{3,2},{4,5},{5,4},{6,7},{7,6},{8,9},{9,8},{10,11... | collective-permute-start | bytes 61448 | tf_op jit(solution)/shard_map/ppermute | solution.py:428

commit v17 on v14

--- a/solution.py
+++ b/solution.py
@@ -240,6 +240,7 @@
     stiff_ref,
     mass_ref,
     basis_ref,
+    turned_ref,
     table_ref,
 ):
     count_y, rest, _ = rest_a_ref.shape
@@ -254,6 +255,9 @@
             basis_ref[i * count_y + j, :prior, :], basis_ref[i * count_y + j, prior:, :] = split(
                 tile
             )
+            if 0 < i < 3:
+                place = (i - 1) * count_y + j
+                turned_ref[place, :, :prior], turned_ref[place, :, prior:] = split(tile.T)
 
 
 def operators_kernel(
@@ -272,6 +276,7 @@
     rest_side_b_ref,
     current_ref,
     basis_ref,
+    turned_ref,
     table_ref,
     weighted_low_ref,
     weighted_high_ref,
@@ -339,9 +344,9 @@
             source, kind = source_and_kind(neighbours_ref, kinds_ref, tile, k, count_y)
             totals = totals + halves_sum(mul(ext_ref[source], table_ref[kind]))
         applied = jnp.concatenate([totals[:, :side], totals[:, side:]], axis=0)
-        basis_tile = basis_parts(i + 1, j + 1)
-        with_basis = with_basis + pair_sum(
-            stacked(applied), basis_tile[:prior], basis_tile[prior:]
+        pairs = mul(stacked(applied), turned_ref[tile])
+        with_basis = with_basis + (
+            halves_sum(pairs[:, :prior]) + pairs[: 2 * block, prior:]
         )
         right = jnp.concatenate([applied, own, jnp.zeros_like(own)], axis=0)
         with_own = with_own + pair_sum(stacked(own), *split(right))
@@ -373,21 +378,24 @@
     row_ids = lax.broadcasted_iota(jnp.int32, (block, block), 0)
     column_ids = lax.broadcasted_iota(jnp.int32, (block, block), 1)
     unit = jnp.where(row_ids == column_ids, 1.0, 0.0).astype(F32)
-    work = jnp.concatenate([gram, unit], axis=1)
-    rows = lax.broadcasted_iota(jnp.int32, work.shape, 0)
-    group = 4
+    rest = jnp.concatenate([gram, unit], axis=1)
+    group = 8
+    done = []
     for j in range(0, block, group):
+        rows = lax.broadcasted_iota(jnp.int32, rest.shape, 0)
         columns = [
-            jnp.broadcast_to(work[:, j + a : j + a + 1], work.shape) for a in range(group)
+            jnp.broadcast_to(rest[:, j + a : j + a + 1], rest.shape) for a in range(group)
         ]
-        pivots = [work[j + a : j + a + 1, :] for a in range(group)]
+        pivots = [rest[a : a + 1, :] for a in range(group)]
         for a in range(group):
-            at = j + a
-            ratio = columns[a] * (1.0 / columns[a][at : at + 1, :])
+            ratio = columns[a] * (1.0 / columns[a][a : a + 1, :])
             for b in range(a + 1, group):
-                columns[b] = columns[b] - ratio * columns[b][at : at + 1, :]
-                pivots[b] = pivots[b] - ratio[j + b : j + b + 1, :] * pivots[a]
-            work = work - jnp.where(rows > at, ratio, 0.0) * pivots[a]
+                columns[b] = columns[b] - ratio * columns[b][a : a + 1, :]
+                pivots[b] = pivots[b] - ratio[b : b + 1, :] * pivots[a]
+            rest = rest - jnp.where(rows > a, ratio, 0.0) * pivots[a]
+        done.append(rest[:group])
+        rest = rest[group:]
+    work = jnp.concatenate(done, axis=0)
     work = work * lax.rsqrt(jnp.sum(work[:, :block] * unit, axis=1, keepdims=True))
     work_ref[...] = work
 
@@ -551,10 +559,11 @@
     )
     from_side_a, from_side_b = exchange(side_a, side_b, "py")
     partial = total_over(partial + from_side_a[-1], 2, count_py)
-    basis_parts, table = call(
+    basis_parts, turned, table = call(
         prepare_kernel,
         (flags, rest_a, rest_b, from_rest_a, from_rest_b, current, stiff_tiles, mass_tiles),
         [shape(4 * count_y, 2 * prior, side, dtype=BF16)]
+        + [shape(tiles, side, 2 * prior, dtype=BF16)]
         + [shape(kinds, 2 * side, 2 * side, dtype=BF16)],
         cost=pl.CostEstimate(flops=10**9, bytes_accessed=0, transcendentals=0),
     )
@@ -574,6 +583,7 @@
             rest_side_b,
             current,
             basis_parts,
+            turned,
             table,
         ),
         [shape(count_y, block, side)] * 2

time: 50.2 us -> 50.9 us (1.014)
  Pallas kernels: 8.63 us -> 9.29 us
    pallas_call x10, Pallas kernels: 8.63 us -> 9.29 us  [call(): pl.pallas_call(kernel, out_shape=outputs, in_specs=specs, out_specs=[VMEM...]
  transfers between devices with their start and end apart: 22 -> 22, of which waited for: 11 -> 12; matrix products, arithmetic and copies ran while one was open for 0% -> 0% of each run, Pallas kernels for 9% -> 8%
where the time goes in v17:
time: 50.9 us; the launch traced here: 50.8 us
  starting transfers between devices  26.2 us (51%)
  waiting for transfers between devices  13.2 us (26%)
  Pallas kernels  9.29 us (18%)
  other arithmetic  1.2 us (2%)
  between operations  0.84 us (2%)
    ppermute x8, waiting for transfers between devices, swap(): return lax.ppermute(value, axes, pairs)  12 us
    ppermute x8, starting transfers between devices, swap(): return lax.ppermute(value, axes, pairs)  9.41 us
    pallas_call x10, Pallas kernels, call(): pl.pallas_call(kernel, out_shape=outputs, in_specs=specs, out_specs=[VMEM...  9.29 us
    ppermute x7, starting transfers between devices, exchange(): lax.ppermute(message_b, ('case', axis), pairs)  8.77 us
    ppermute x7, starting transfers between devices, exchange(): lax.ppermute(message_a, axis, near)  8 us
    concatenate x1, other arithmetic, shards(): vectors = jnp.concatenate([basis, previous.reshape(-1, side)], axis=0)  1.16 us
    ppermute x7, waiting for transfers between devices, exchange(): lax.ppermute(message_a, axis, near)  1.02 us
  transfers between devices with their start and end apart: 22, of which 12 were waited for; matrix products, arithmetic and copies ran while one was open for 0% of the time, Pallas kernels for 8%

profile of v17, /device:TPU:0, one launch (start us, length us, event | category | flops | bytes accessed | tf_op | source)
XLA Modules:
  0.0 50.8 jit_solution(12229679925480158384)
XLA Ops:
  0.7 1.2 %pad_maximum_fusion.vectors_ref = f32[1280,128]{1,0:T(8,128)S(1)} fusion(f32[256,128]{1,0:T(8,128)} %bitcast.24, f32[1024,128]{1,0:T(8,128)} %bitcast.23), kind=kLoop, calls=%fused_computation | loop fusion | flops 163840 | bytes 1310720 | tf_op jit(solution)/shard_map/concatenate | solution.py:477
  1.8 0.1 iota.7.flags_ref
  1.9 0.1 shard_map.93
  2.0 0.0 copy-start.2
  2.0 0.5 %collective-permute-start.2 = (f32[2,64,128]{2,1,0:T(8,128)S(1)}, f32[2,64,128]{2,1,0:T(8,128)S(1)}, u32[]{:S(2)}, u32[]{:S(2)}) collective-permute-start(f32[2,64,128]{2,1,0:T(8,128)S(1)} %get-tuple-element.39), channel_id=1, source_target_pairs={{0,1},{1,0},{2,3},{3,2},{4,5},{5,4},{6,7},{7,6},{8,9},{9,8},{10,11... | collective-permute-start | bytes 196616 | tf_op jit(solution)/shard_map/ppermute | solution.py:448
  2.5 2.6 %collective-permute-start.3 = (f32[2,64,128]{2,1,0:T(8,128)S(1)}, f32[2,64,128]{2,1,0:T(8,128)S(1)}, u32[]{:S(2)}, u32[]{:S(2)}) collective-permute-start(f32[2,64,128]{2,1,0:T(8,128)S(1)} %get-tuple-element.43), channel_id=1, source_target_pairs={{0,16},{1,2},{2,1},{3,19},{16,0},{17,18},{18,17},{19,3},{4,20},{5,... | collective-permute-start | bytes 196616 | tf_op jit(solution)/shard_map/ppermute | solution.py:448
  5.1 1.6 %collective-permute-start = (f32[4,64,128]{2,1,0:T(8,128)S(1)}, f32[4,64,128]{2,1,0:T(8,128)S(1)}, u32[]{:S(2)}, u32[]{:S(2)}) collective-permute-start(f32[4,64,128]{2,1,0:T(8,128)S(1)} %get-tuple-element.37.row_a_ref), channel_id=1, source_target_pairs={{0,4},{4,0},{8,12},{12,8},{1,5},{5,1},{9,13},{13,9},{2,6},{6,2},{1... | collective-permute-start | bytes 393224 | tf_op jit(solution)/shard_map/ppermute | solution.py:448
  6.7 0.5 collective-permute-start.1
  7.2 0.1 shard_map.94
  7.2 0.1 collective-permute-done.3.side_b_ref.from_side_b_ref
  7.3 0.0 copy-start
  7.4 2.7 %collective-permute-start.4 = (f32[2,64,128]{2,1,0:T(8,128)S(1)}, f32[2,64,128]{2,1,0:T(8,128)S(1)}, u32[]{:S(2)}, u32[]{:S(2)}) collective-permute-start(f32[2,64,128]{2,1,0:T(8,128)S(1)} %get-tuple-element.44), channel_id=1, source_target_pairs={{0,4},{4,0},{8,12},{12,8},{1,5},{5,1},{9,13},{13,9},{2,6},{6,2},{1... | collective-permute-start | bytes 196616 | tf_op jit(solution)/shard_map/ppermute | solution.py:448
  10.0 1.0 %collective-permute-start.5 = (f32[2,64,128]{2,1,0:T(8,128)S(1)}, f32[2,64,128]{2,1,0:T(8,128)S(1)}, u32[]{:S(2)}, u32[]{:S(2)}) collective-permute-start(f32[2,64,128]{2,1,0:T(8,128)S(1)} %get-tuple-element.45), channel_id=1, source_target_pairs={{0,16},{4,8},{8,4},{12,28},{16,0},{20,24},{24,20},{28,12},{1,17},{... | collective-permute-start | bytes 196616 | tf_op jit(solution)/shard_map/ppermute | solution.py:448
  11.0 1.6 %collective-permute-start.8 = (f32[4,96,128]{2,1,0:T(8,128)S(1)}, f32[4,96,128]{2,1,0:T(8,128)S(1)}, u32[]{:S(2)}, u32[]{:S(2)}) collective-permute-start(f32[4,96,128]{2,1,0:T(8,128)S(1)} %get-tuple-element.46.rest_a_ref.row_a_ref), channel_id=1, source_target_pairs={{0,4},{4,0},{8,12},{12,8},{1,5},{5,1},{9,13},{13,9},{2,6},{6,2},{1... | collective-permute-start | bytes 589832 | tf_op jit(solution)/shard_map/ppermute | solution.py:448
  12.7 0.0 collective-permute-done.4.from_corner_a_ref
  12.7 1.5 %collective-permute-start.9 = (f32[4,96,128]{2,1,0:T(8,128)S(1)}, f32[4,96,128]{2,1,0:T(8,128)S(1)}, u32[]{:S(2)}, u32[]{:S(2)}) collective-permute-start(f32[4,96,128]{2,1,0:T(8,128)S(1)} %get-tuple-element.47.rest_b_ref.row_b_ref), channel_id=1, source_target_pairs={{0,16},{4,8},{8,4},{12,28},{16,0},{20,24},{24,20},{28,12},{1,17},{... | collective-permute-start | bytes 589832 | tf_op jit(solution)/shard_map/ppermute | solution.py:448
  14.2 0.1 collective-permute-done.5.from_corner_b_ref
  14.3 2.6 %shard_map.96 = (f32[5,32,128]{2,1,0:T(8,128)S(1)}, f32[4,32,128]{2,1,0:T(8,128)S(1)}, f32[32,128]{1,0:T(8,128)S(1)}, f32[24,32,128]{2,1,0:T(8,128)S(1)}) custom-call(s32[8,5]{1,0:T(8,128)S(1)} %bitcast.19, s32[8,5]{1,0:T(8,128)S(1)} %bitcast.21, f32[8,128]{1,0:T(8,128)S(1)} %iota.7.flags_ref, f32[4,64,128]{2,1,0:T(8,128)S(1)} %get-tuple-element.37.row_a_ref, ...), custom_call_target="tpu_custom_call" | custom-call | flops 1000000000 | tf_op jit(solution)/shard_map/pallas_call | solution.py:489
  17.0 1.5 %collective-permute-start.6 = (f32[5,32,128]{2,1,0:T(8,128)S(1)}, f32[5,32,128]{2,1,0:T(8,128)S(1)}, u32[]{:S(2)}, u32[]{:S(2)}) collective-permute-start(f32[5,32,128]{2,1,0:T(8,128)S(1)} %get-tuple-element.49.row_a_ref), channel_id=1, source_target_pairs={{0,4},{4,0},{8,12},{12,8},{1,5},{5,1},{9,13},{13,9},{2,6},{6,2},{1... | collective-permute-start | bytes 245768 | tf_op jit(solution)/shard_map/ppermute | solution.py:448
  18.5 1.5 %collective-permute-start.12 = (f32[4,32,128]{2,1,0:T(8,128)S(1)}, f32[4,32,128]{2,1,0:T(8,128)S(1)}, u32[]{:S(2)}, u32[]{:S(2)}) collective-permute-start(f32[4,32,128]{2,1,0:T(8,128)S(1)} %get-tuple-element.53.row_b_ref), channel_id=1, source_target_pairs={{0,16},{4,8},{8,4},{12,28},{16,0},{20,24},{24,20},{28,12},{1,17},{... | collective-permute-start | bytes 196616 | tf_op jit(solution)/shard_map/ppermute | solution.py:448
  19.9 0.0 collective-permute-done.8.from_row_a_ref.from_rest_a_ref
  19.9 0.0 collective-permute-done.9.from_row_b_ref.from_rest_b_ref
  20.0 0.1 collective-permute-start.10
  20.1 0.6 %collective-permute-start.11 = (f32[4,96,128]{2,1,0:T(8,128)S(1)}, f32[4,96,128]{2,1,0:T(8,128)S(1)}, u32[]{:S(2)}, u32[]{:S(2)}) collective-permute-start(f32[4,96,128]{2,1,0:T(8,128)S(1)} %get-tuple-element.51), channel_id=1, source_target_pairs={{0,16},{1,2},{2,1},{3,19},{16,0},{17,18},{18,17},{19,3},{4,20},{5,... | collective-permute-start | bytes 589832 | tf_op jit(solution)/shard_map/ppermute | solution.py:448
  20.7 0.8 %collective-permute-done.6.from_row_a_ref = f32[5,32,128]{2,1,0:T(8,128)S(1)} collective-permute-done((f32[5,32,128]{2,1,0:T(8,128)S(1)}, f32[5,32,128]{2,1,0:T(8,128)S(1)}, u32[]{:S(2)}, u32[]{:S(2)}) %collective-permute-start.6) | collective-permute-done | bytes 81952 | tf_op jit(solution)/shard_map/ppermute | solution.py:448
  21.5 2.3 %collective-permute-start.7 = (f32[32,128]{1,0:T(8,128)S(1)}, f32[32,128]{1,0:T(8,128)S(1)}, u32[]{:S(2)}, u32[]{:S(2)}) collective-permute-start(f32[32,128]{1,0:T(8,128)S(1)} %fusion.1), channel_id=1, source_target_pairs={{0,8},{1,9},{2,10},{3,11},{4,12},{5,13},{6,14},{7,15},{8,0},{9,1},... | collective-permute-start | bytes 49160 | tf_op jit(solution)/shard_map/ppermute | solution.py:436
  23.7 2.4 %collective-permute-done.7 = f32[32,128]{1,0:T(8,128)S(1)} collective-permute-done((f32[32,128]{1,0:T(8,128)S(1)}, f32[32,128]{1,0:T(8,128)S(1)}, u32[]{:S(2)}, u32[]{:S(2)}) %collective-permute-start.7) | collective-permute-done | bytes 16416 | tf_op jit(solution)/shard_map/ppermute | solution.py:436
  26.2 0.1 collective-permute-start.13
  26.3 1.1 %collective-permute-start.15 = (f32[4,32,128]{2,1,0:T(8,128)S(1)}, f32[4,32,128]{2,1,0:T(8,128)S(1)}, u32[]{:S(2)}, u32[]{:S(2)}) collective-permute-start(f32[4,32,128]{2,1,0:T(8,128)S(1)} %get-tuple-element.55), channel_id=1, source_target_pairs={{0,16},{1,2},{2,1},{3,19},{16,0},{17,18},{18,17},{19,3},{4,20},{5,... | collective-permute-start | bytes 196616 | tf_op jit(solution)/shard_map/ppermute | solution.py:448
  27.3 0.2 collective-permute-done.13.from_side_a_ref
  27.5 0.9 %collective-permute-start.14 = (f32[32,128]{1,0:T(8,128)S(1)}, f32[32,128]{1,0:T(8,128)S(1)}, u32[]{:S(2)}, u32[]{:S(2)}) collective-permute-start(f32[32,128]{1,0:T(8,128)S(1)} %fusion), channel_id=1, source_target_pairs={{0,2},{1,3},{2,0},{3,1},{4,6},{5,7},{6,4},{7,5},{8,10},{9,11},{10,... | collective-permute-start | bytes 49160 | tf_op jit(solution)/shard_map/ppermute | solution.py:436
  28.5 0.4 shard_map.99
  28.9 2.4 %collective-permute-done.14 = f32[32,128]{1,0:T(8,128)S(1)} collective-permute-done((f32[32,128]{1,0:T(8,128)S(1)}, f32[32,128]{1,0:T(8,128)S(1)}, u32[]{:S(2)}, u32[]{:S(2)}) %collective-permute-start.14) | collective-permute-done | bytes 16416 | tf_op jit(solution)/shard_map/ppermute | solution.py:436
  31.3 3.9 %shard_map.100 = (f32[4,32,128]{2,1,0:T(8,128)S(1)}, f32[4,32,128]{2,1,0:T(8,128)S(1)}, f32[32,128]{1,0:T(8,128)}, f32[48,128]{1,0:T(8,128)S(1)}, f32[48,128]{1,0:T(8,128)S(1)}) custom-call(s32[8,5]{1,0:T(8,128)S(1)} %bitcast.20, s32[8,5]{1,0:T(8,128)S(1)} %bitcast.22, f32[8,128]{1,0:T(8,128)S(1)} %iota.7.flags_ref, f32[32,128]{1,0:T(8,128)S(1)} %add.50.partial_ref, ...), custom_call_target="tpu_custom_call" | custom-call | tf_op jit(solution)/shard_map/pallas_call | solution.py:489
  35.2 0.1 collective-permute-start.16
  35.3 1.2 %collective-permute-done.16 = f32[48,128]{1,0:T(8,128)S(1)} collective-permute-done((f32[48,128]{1,0:T(8,128)S(1)}, f32[48,128]{1,0:T(8,128)S(1)}, u32[]{:S(2)}, u32[]{:S(2)}) %collective-permute-start.16) | collective-permute-done | bytes 24608 | tf_op jit(solution)/shard_map/ppermute | solution.py:436
  36.5 2.2 %collective-permute-start.17 = (f32[48,128]{1,0:T(8,128)S(1)}, f32[48,128]{1,0:T(8,128)S(1)}, u32[]{:S(2)}, u32[]{:S(2)}) collective-permute-start(f32[48,128]{1,0:T(8,128)S(1)} %add.51), channel_id=1, source_target_pairs={{0,6},{1,7},{2,4},{3,5},{4,2},{5,3},{6,0},{7,1},{8,14},{9,15},{10,... | collective-permute-start | bytes 73736 | tf_op jit(solution)/shard_map/ppermute | solution.py:436
  38.6 1.0 %collective-permute-start.18 = (f32[48,128]{1,0:T(8,128)S(1)}, f32[48,128]{1,0:T(8,128)S(1)}, u32[]{:S(2)}, u32[]{:S(2)}) collective-permute-start(f32[48,128]{1,0:T(8,128)S(1)} %add.51), channel_id=1, source_target_pairs={{0,2},{1,3},{2,0},{3,1},{4,6},{5,7},{6,4},{7,5},{8,10},{9,11},{10,... | collective-permute-start | bytes 73736 | tf_op jit(solution)/shard_map/ppermute | solution.py:436
  39.7 0.3 collective-permute-start.19
  40.0 1.2 %collective-permute-done.17 = f32[48,128]{1,0:T(8,128)S(1)} collective-permute-done((f32[48,128]{1,0:T(8,128)S(1)}, f32[48,128]{1,0:T(8,128)S(1)}, u32[]{:S(2)}, u32[]{:S(2)}) %collective-permute-start.17) | collective-permute-done | bytes 24608 | tf_op jit(solution)/shard_map/ppermute | solution.py:436
  41.2 1.3 %collective-permute-done.18 = f32[48,128]{1,0:T(8,128)S(1)} collective-permute-done((f32[48,128]{1,0:T(8,128)S(1)}, f32[48,128]{1,0:T(8,128)S(1)}, u32[]{:S(2)}, u32[]{:S(2)}) %collective-permute-start.18) | collective-permute-done | bytes 24608 | tf_op jit(solution)/shard_map/ppermute | solution.py:436
  42.5 1.0 %collective-permute-done.19 = f32[48,128]{1,0:T(8,128)S(1)} collective-permute-done((f32[48,128]{1,0:T(8,128)S(1)}, f32[48,128]{1,0:T(8,128)S(1)}, u32[]{:S(2)}, u32[]{:S(2)}) %collective-permute-start.19) | collective-permute-done | bytes 24608 | tf_op jit(solution)/shard_map/ppermute | solution.py:436
  43.5 2.6 %collective-permute-start.20 = (f32[48,128]{1,0:T(8,128)S(1)}, f32[48,128]{1,0:T(8,128)S(1)}, u32[]{:S(2)}, u32[]{:S(2)}) collective-permute-start(f32[48,128]{1,0:T(8,128)S(1)} %add_add_fusion), channel_id=1, source_target_pairs={{0,8},{1,9},{2,10},{3,11},{4,12},{5,13},{6,14},{7,15},{8,0},{9,1},... | collective-permute-start | bytes 73736 | tf_op jit(solution)/shard_map/ppermute | solution.py:436
  46.1 2.2 %collective-permute-done.20 = f32[48,128]{1,0:T(8,128)S(1)} collective-permute-done((f32[48,128]{1,0:T(8,128)S(1)}, f32[48,128]{1,0:T(8,128)S(1)}, u32[]{:S(2)}, u32[]{:S(2)}) %collective-permute-start.20) | collective-permute-done | bytes 24608 | tf_op jit(solution)/shard_map/ppermute | solution.py:436
  48.3 0.1 collective-permute-start.21
  48.4 0.9 %shard_map.101.work_ref = f32[32,64]{1,0:T(8,128)S(1)} custom-call(f32[48,128]{1,0:T(8,128)S(1)} %add.55.sums_ref), custom_call_target="tpu_custom_call" | custom-call | flops 1000000000 | tf_op jit(solution)/shard_map/pallas_call | solution.py:489
  49.3 0.3 collective-permute-done.21.other_ref
  49.6 1.2 %shard_map.102 = (f32[256,128]{1,0:T(8,128)}, f32[32,32]{1,0:T(8,128)}, f32[2,32,160]{2,1,0:T(8,128)}) custom-call(f32[8,128]{1,0:T(8,128)S(1)} %iota.7.flags_ref, f32[32,64]{1,0:T(8,128)S(1)} %shard_map.101.work_ref, f32[48,128]{1,0:T(8,128)S(1)} %add.55.sums_ref, f32[40,128]{1,0:T(8,128)S(1)} %collective-permute-done.21.other_ref, ...), custom_call_target="tpu_custom_call" | custom-call | tf_op jit(solution)/shard_map/pallas_call | solution.py:489
  (25 shorter events, 0.2 us)
Async XLA Ops:
  1.9 12.4 %copy-start.3 = (f32[8,128,128]{2,1,0:T(8,128)S(1)}, f32[8,128,128]{2,1,0:T(8,128)}, u32[]{:S(2)}) copy-start(f32[8,128,128]{2,1,0:T(8,128)} %mass_ref.3) | copy-start | bytes 1572868
  2.0 12.3 %copy-start.2 = (f32[8,128,128]{2,1,0:T(8,128)S(1)}, f32[8,128,128]{2,1,0:T(8,128)}, u32[]{:S(2)}) copy-start(f32[8,128,128]{2,1,0:T(8,128)} %stiff_ref.3) | copy-start | bytes 1572868
  2.0 5.3 %collective-permute-start.2 = (f32[2,64,128]{2,1,0:T(8,128)S(1)}, f32[2,64,128]{2,1,0:T(8,128)S(1)}, u32[]{:S(2)}, u32[]{:S(2)}) collective-permute-start(f32[2,64,128]{2,1,0:T(8,128)S(1)} %get-tuple-element.39), channel_id=1, source_target_pairs={{0,1},{1,0},{2,3},{3,2},{4,5},{5,4},{6,7},{7,6},{8,9},{9,8},{10,11... | collective-permute-start | bytes 196616 | tf_op jit(solution)/shard_map/ppermute | solution.py:448
  2.5 4.8 %collective-permute-start.3 = (f32[2,64,128]{2,1,0:T(8,128)S(1)}, f32[2,64,128]{2,1,0:T(8,128)S(1)}, u32[]{:S(2)}, u32[]{:S(2)}) collective-permute-start(f32[2,64,128]{2,1,0:T(8,128)S(1)} %get-tuple-element.43), channel_id=1, source_target_pairs={{0,16},{1,2},{2,1},{3,19},{16,0},{17,18},{18,17},{19,3},{4,20},{5,... | collective-permute-start | bytes 196616 | tf_op jit(solution)/shard_map/ppermute | solution.py:448
  5.1 9.2 %collective-permute-start = (f32[4,64,128]{2,1,0:T(8,128)S(1)}, f32[4,64,128]{2,1,0:T(8,128)S(1)}, u32[]{:S(2)}, u32[]{:S(2)}) collective-permute-start(f32[4,64,128]{2,1,0:T(8,128)S(1)} %get-tuple-element.37.row_a_ref), channel_id=1, source_target_pairs={{0,4},{4,0},{8,12},{12,8},{1,5},{5,1},{9,13},{13,9},{2,6},{6,2},{1... | collective-permute-start | bytes 393224 | tf_op jit(solution)/shard_map/ppermute | solution.py:448
  6.7 7.6 %collective-permute-start.1 = (f32[4,64,128]{2,1,0:T(8,128)S(1)}, f32[4,64,128]{2,1,0:T(8,128)S(1)}, u32[]{:S(2)}, u32[]{:S(2)}) collective-permute-start(f32[4,64,128]{2,1,0:T(8,128)S(1)} %get-tuple-element.38.row_b_ref), channel_id=1, source_target_pairs={{0,16},{4,8},{8,4},{12,28},{16,0},{20,24},{24,20},{28,12},{1,17},{... | collective-permute-start | bytes 393224 | tf_op jit(solution)/shard_map/ppermute | solution.py:448
  7.3 7.0 %copy-start.1 = (s32[5,2,4]{0,2,1:T(4,128)S(1)}, s32[5,2,4]{0,2,1:T(4,128)}, u32[]{:S(2)}) copy-start(s32[5,2,4]{0,2,1:T(4,128)} %param.9) | copy-start | bytes 484
  7.3 7.0 %copy-start = (s32[5,2,4]{0,2,1:T(4,128)S(1)}, s32[5,2,4]{0,2,1:T(4,128)}, u32[]{:S(2)}) copy-start(s32[5,2,4]{0,2,1:T(4,128)} %param.8) | copy-start | bytes 484
  7.4 5.3 %collective-permute-start.4 = (f32[2,64,128]{2,1,0:T(8,128)S(1)}, f32[2,64,128]{2,1,0:T(8,128)S(1)}, u32[]{:S(2)}, u32[]{:S(2)}) collective-permute-start(f32[2,64,128]{2,1,0:T(8,128)S(1)} %get-tuple-element.44), channel_id=1, source_target_pairs={{0,4},{4,0},{8,12},{12,8},{1,5},{5,1},{9,13},{13,9},{2,6},{6,2},{1... | collective-permute-start | bytes 196616 | tf_op jit(solution)/shard_map/ppermute | solution.py:448
  10.0 4.3 %collective-permute-start.5 = (f32[2,64,128]{2,1,0:T(8,128)S(1)}, f32[2,64,128]{2,1,0:T(8,128)S(1)}, u32[]{:S(2)}, u32[]{:S(2)}) collective-permute-start(f32[2,64,128]{2,1,0:T(8,128)S(1)} %get-tuple-element.45), channel_id=1, source_target_pairs={{0,16},{4,8},{8,4},{12,28},{16,0},{20,24},{24,20},{28,12},{1,17},{... | collective-permute-start | bytes 196616 | tf_op jit(solution)/shard_map/ppermute | solution.py:448
  11.0 8.9 %collective-permute-start.8 = (f32[4,96,128]{2,1,0:T(8,128)S(1)}, f32[4,96,128]{2,1,0:T(8,128)S(1)}, u32[]{:S(2)}, u32[]{:S(2)}) collective-permute-start(f32[4,96,128]{2,1,0:T(8,128)S(1)} %get-tuple-element.46.rest_a_ref.row_a_ref), channel_id=1, source_target_pairs={{0,4},{4,0},{8,12},{12,8},{1,5},{5,1},{9,13},{13,9},{2,6},{6,2},{1... | collective-permute-start | bytes 589832 | tf_op jit(solution)/shard_map/ppermute | solution.py:448
  12.7 7.3 %collective-permute-start.9 = (f32[4,96,128]{2,1,0:T(8,128)S(1)}, f32[4,96,128]{2,1,0:T(8,128)S(1)}, u32[]{:S(2)}, u32[]{:S(2)}) collective-permute-start(f32[4,96,128]{2,1,0:T(8,128)S(1)} %get-tuple-element.47.rest_b_ref.row_b_ref), channel_id=1, source_target_pairs={{0,16},{4,8},{8,4},{12,28},{16,0},{20,24},{24,20},{28,12},{1,17},{... | collective-permute-start | bytes 589832 | tf_op jit(solution)/shard_map/ppermute | solution.py:448
  17.0 4.5 %collective-permute-start.6 = (f32[5,32,128]{2,1,0:T(8,128)S(1)}, f32[5,32,128]{2,1,0:T(8,128)S(1)}, u32[]{:S(2)}, u32[]{:S(2)}) collective-permute-start(f32[5,32,128]{2,1,0:T(8,128)S(1)} %get-tuple-element.49.row_a_ref), channel_id=1, source_target_pairs={{0,4},{4,0},{8,12},{12,8},{1,5},{5,1},{9,13},{13,9},{2,6},{6,2},{1... | collective-permute-start | bytes 245768 | tf_op jit(solution)/shard_map/ppermute | solution.py:448
  18.5 7.7 %collective-permute-start.12 = (f32[4,32,128]{2,1,0:T(8,128)S(1)}, f32[4,32,128]{2,1,0:T(8,128)S(1)}, u32[]{:S(2)}, u32[]{:S(2)}) collective-permute-start(f32[4,32,128]{2,1,0:T(8,128)S(1)} %get-tuple-element.53.row_b_ref), channel_id=1, source_target_pairs={{0,16},{4,8},{8,4},{12,28},{16,0},{20,24},{24,20},{28,12},{1,17},{... | collective-permute-start | bytes 196616 | tf_op jit(solution)/shard_map/ppermute | solution.py:448
  20.0 6.2 %collective-permute-start.10 = (f32[4,96,128]{2,1,0:T(8,128)S(1)}, f32[4,96,128]{2,1,0:T(8,128)S(1)}, u32[]{:S(2)}, u32[]{:S(2)}) collective-permute-start(f32[4,96,128]{2,1,0:T(8,128)S(1)} %get-tuple-element.50), channel_id=1, source_target_pairs={{0,1},{1,0},{2,3},{3,2},{4,5},{5,4},{6,7},{7,6},{8,9},{9,8},{10,11... | collective-permute-start | bytes 589832 | tf_op jit(solution)/shard_map/ppermute | solution.py:448
  20.1 6.1 %collective-permute-start.11 = (f32[4,96,128]{2,1,0:T(8,128)S(1)}, f32[4,96,128]{2,1,0:T(8,128)S(1)}, u32[]{:S(2)}, u32[]{:S(2)}) collective-permute-start(f32[4,96,128]{2,1,0:T(8,128)S(1)} %get-tuple-element.51), channel_id=1, source_target_pairs={{0,16},{1,2},{2,1},{3,19},{16,0},{17,18},{18,17},{19,3},{4,20},{5,... | collective-permute-start | bytes 589832 | tf_op jit(solution)/shard_map/ppermute | solution.py:448
  21.5 4.6 %collective-permute-start.7 = (f32[32,128]{1,0:T(8,128)S(1)}, f32[32,128]{1,0:T(8,128)S(1)}, u32[]{:S(2)}, u32[]{:S(2)}) collective-permute-start(f32[32,128]{1,0:T(8,128)S(1)} %fusion.1), channel_id=1, source_target_pairs={{0,8},{1,9},{2,10},{3,11},{4,12},{5,13},{6,14},{7,15},{8,0},{9,1},... | collective-permute-start | bytes 49160 | tf_op jit(solution)/shard_map/ppermute | solution.py:436
  26.2 1.3 %collective-permute-start.13 = (f32[5,32,128]{2,1,0:T(8,128)S(1)}, f32[5,32,128]{2,1,0:T(8,128)S(1)}, u32[]{:S(2)}, u32[]{:S(2)}) collective-permute-start(f32[5,32,128]{2,1,0:T(8,128)S(1)} %get-tuple-element.54), channel_id=1, source_target_pairs={{0,1},{1,0},{2,3},{3,2},{4,5},{5,4},{6,7},{7,6},{8,9},{9,8},{10,11... | collective-permute-start | bytes 245768 | tf_op jit(solution)/shard_map/ppermute | solution.py:448
  26.3 5.0 %collective-permute-start.15 = (f32[4,32,128]{2,1,0:T(8,128)S(1)}, f32[4,32,128]{2,1,0:T(8,128)S(1)}, u32[]{:S(2)}, u32[]{:S(2)}) collective-permute-start(f32[4,32,128]{2,1,0:T(8,128)S(1)} %get-tuple-element.55), channel_id=1, source_target_pairs={{0,16},{1,2},{2,1},{3,19},{16,0},{17,18},{18,17},{19,3},{4,20},{5,... | collective-permute-start | bytes 196616 | tf_op jit(solution)/shard_map/ppermute | solution.py:448
  27.5 3.7 %collective-permute-start.14 = (f32[32,128]{1,0:T(8,128)S(1)}, f32[32,128]{1,0:T(8,128)S(1)}, u32[]{:S(2)}, u32[]{:S(2)}) collective-permute-start(f32[32,128]{1,0:T(8,128)S(1)} %fusion), channel_id=1, source_target_pairs={{0,2},{1,3},{2,0},{3,1},{4,6},{5,7},{6,4},{7,5},{8,10},{9,11},{10,... | collective-permute-start | bytes 49160 | tf_op jit(solution)/shard_map/ppermute | solution.py:436
  35.2 1.3 %collective-permute-start.16 = (f32[48,128]{1,0:T(8,128)S(1)}, f32[48,128]{1,0:T(8,128)S(1)}, u32[]{:S(2)}, u32[]{:S(2)}) collective-permute-start(f32[48,128]{1,0:T(8,128)S(1)} %get-tuple-element.63), channel_id=1, source_target_pairs={{0,1},{1,0},{2,3},{3,2},{4,5},{5,4},{6,7},{7,6},{8,9},{9,8},{10,11... | collective-permute-start | bytes 73736 | tf_op jit(solution)/shard_map/ppermute | solution.py:436
  36.5 4.7 %collective-permute-start.17 = (f32[48,128]{1,0:T(8,128)S(1)}, f32[48,128]{1,0:T(8,128)S(1)}, u32[]{:S(2)}, u32[]{:S(2)}) collective-permute-start(f32[48,128]{1,0:T(8,128)S(1)} %add.51), channel_id=1, source_target_pairs={{0,6},{1,7},{2,4},{3,5},{4,2},{5,3},{6,0},{7,1},{8,14},{9,15},{10,... | collective-permute-start | bytes 73736 | tf_op jit(solution)/shard_map/ppermute | solution.py:436
  38.6 3.8 %collective-permute-start.18 = (f32[48,128]{1,0:T(8,128)S(1)}, f32[48,128]{1,0:T(8,128)S(1)}, u32[]{:S(2)}, u32[]{:S(2)}) collective-permute-start(f32[48,128]{1,0:T(8,128)S(1)} %add.51), channel_id=1, source_target_pairs={{0,2},{1,3},{2,0},{3,1},{4,6},{5,7},{6,4},{7,5},{8,10},{9,11},{10,... | collective-permute-start | bytes 73736 | tf_op jit(solution)/shard_map/ppermute | solution.py:436
  39.7 3.8 %collective-permute-start.19 = (f32[48,128]{1,0:T(8,128)S(1)}, f32[48,128]{1,0:T(8,128)S(1)}, u32[]{:S(2)}, u32[]{:S(2)}) collective-permute-start(f32[48,128]{1,0:T(8,128)S(1)} %add.51), channel_id=1, source_target_pairs={{0,4},{1,5},{2,6},{3,7},{4,0},{5,1},{6,2},{7,3},{8,12},{9,13},{10,... | collective-permute-start | bytes 73736 | tf_op jit(solution)/shard_map/ppermute | solution.py:436
  43.5 4.8 %collective-permute-start.20 = (f32[48,128]{1,0:T(8,128)S(1)}, f32[48,128]{1,0:T(8,128)S(1)}, u32[]{:S(2)}, u32[]{:S(2)}) collective-permute-start(f32[48,128]{1,0:T(8,128)S(1)} %add_add_fusion), channel_id=1, source_target_pairs={{0,8},{1,9},{2,10},{3,11},{4,12},{5,13},{6,14},{7,15},{8,0},{9,1},... | collective-permute-start | bytes 73736 | tf_op jit(solution)/shard_map/ppermute | solution.py:436
  48.3 1.3 %collective-permute-start.21 = (f32[40,128]{1,0:T(8,128)S(1)}, f32[40,128]{1,0:T(8,128)S(1)}, u32[]{:S(2)}, u32[]{:S(2)}) collective-permute-start(f32[40,128]{1,0:T(8,128)S(1)} %slice.14), channel_id=1, source_target_pairs={{0,1},{1,0},{2,3},{3,2},{4,5},{5,4},{6,7},{7,6},{8,9},{9,8},{10,11... | collective-permute-start | bytes 61448 | tf_op jit(solution)/shard_map/ppermute | solution.py:436

commit v18 on v17

--- a/solution.py
+++ b/solution.py
@@ -66,6 +66,10 @@
 def halves_sum(value):
     half = value.shape[0] // 2
     return value[:half] + value[half:]
+
+
+def mul_deep(left_deep, right):
+    return halves_sum(mul(left_deep, stacked(right)))
 
 
 def pair_sum(left, right_high, right_low):
@@ -240,7 +244,6 @@
     stiff_ref,
     mass_ref,
     basis_ref,
-    turned_ref,
     table_ref,
 ):
     count_y, rest, _ = rest_a_ref.shape
@@ -255,9 +258,6 @@
             basis_ref[i * count_y + j, :prior, :], basis_ref[i * count_y + j, prior:, :] = split(
                 tile
             )
-            if 0 < i < 3:
-                place = (i - 1) * count_y + j
-                turned_ref[place, :, :prior], turned_ref[place, :, prior:] = split(tile.T)
 
 
 def operators_kernel(
@@ -276,7 +276,6 @@
     rest_side_b_ref,
     current_ref,
     basis_ref,
-    turned_ref,
     table_ref,
     weighted_low_ref,
     weighted_high_ref,
@@ -344,9 +343,9 @@
             source, kind = source_and_kind(neighbours_ref, kinds_ref, tile, k, count_y)
             totals = totals + halves_sum(mul(ext_ref[source], table_ref[kind]))
         applied = jnp.concatenate([totals[:, :side], totals[:, side:]], axis=0)
-        pairs = mul(stacked(applied), turned_ref[tile])
-        with_basis = with_basis + (
-            halves_sum(pairs[:, :prior]) + pairs[: 2 * block, prior:]
+        basis_tile = basis_parts(i + 1, j + 1)
+        with_basis = with_basis + pair_sum(
+            stacked(applied), basis_tile[:prior], basis_tile[prior:]
         )
         right = jnp.concatenate([applied, own, jnp.zeros_like(own)], axis=0)
         with_own = with_own + pair_sum(stacked(own), *split(right))
@@ -419,13 +418,14 @@
     column_ids = lax.broadcasted_iota(jnp.int32, (block, block), 1)
     factor_ref[...] = jnp.where(column_ids >= row_ids, work_ref[:, :block], 0.0)
     inverse = work_ref[:, block:]
+    inverse_deep = deep(inverse)
     for tile in range(tiles):
         own = (weighted_low_ref, weighted_high_ref)[tile // count_y][tile % count_y]
-        new_ref[pl.ds(tile, block, stride=tiles), :] = mul3(inverse, own)
+        new_ref[pl.ds(tile, block, stride=tiles), :] = mul_deep(inverse_deep, own)
     odd_y = flag_at(flags_ref, 0)
     halves = pick(odd_y, other_ref[...], sums_ref[: block + 8, :])
     for part, half in enumerate(halves):
-        reduced_ref[part, :, :prior] = mul3(inverse, half[:block] * inverse_rows)
+        reduced_ref[part, :, :prior] = mul_deep(inverse_deep, half[:block] * inverse_rows)
         own = unfolded(half[block:]) * inverse_rows
         reduced_ref[part, :, prior:] = mul3_t(mul3_t(inverse, own), inverse)
 
@@ -559,11 +559,10 @@
     )
     from_side_a, from_side_b = exchange(side_a, side_b, "py")
     partial = total_over(partial + from_side_a[-1], 2, count_py)
-    basis_parts, turned, table = call(
+    basis_parts, table = call(
         prepare_kernel,
         (flags, rest_a, rest_b, from_rest_a, from_rest_b, current, stiff_tiles, mass_tiles),
         [shape(4 * count_y, 2 * prior, side, dtype=BF16)]
-        + [shape(tiles, side, 2 * prior, dtype=BF16)]
         + [shape(kinds, 2 * side, 2 * side, dtype=BF16)],
         cost=pl.CostEstimate(flops=10**9, bytes_accessed=0, transcendentals=0),
     )
@@ -583,7 +582,6 @@
             rest_side_b,
             current,
             basis_parts,
-            turned,
             table,
         ),
         [shape(count_y, block, side)] * 2

time: 50.9 us -> 49.9 us (0.980)
  Pallas kernels: 9.29 us -> 8.13 us
    pallas_call x10, Pallas kernels: 9.29 us -> 8.13 us  [call(): pl.pallas_call(kernel, out_shape=outputs, in_specs=specs, out_specs=[VMEM...]
where the time goes in v18:
time: 49.9 us; the launch traced here: 49.7 us
  starting transfers between devices  26.2 us (53%)
  waiting for transfers between devices  13.3 us (27%)
  Pallas kernels  8.13 us (16%)
  other arithmetic  1.2 us (2%)
  between operations  0.84 us (2%)
    ppermute x8, waiting for transfers between devices, swap(): return lax.ppermute(value, axes, pairs)  12.1 us
    ppermute x8, starting transfers between devices, swap(): return lax.ppermute(value, axes, pairs)  9.41 us
    ppermute x7, starting transfers between devices, exchange(): lax.ppermute(message_b, ('case', axis), pairs)  8.78 us
    pallas_call x10, Pallas kernels, call(): pl.pallas_call(kernel, out_shape=outputs, in_specs=specs, out_specs=[VMEM...  8.13 us
    ppermute x7, starting transfers between devices, exchange(): lax.ppermute(message_a, axis, near)  8 us
    concatenate x1, other arithmetic, shards(): vectors = jnp.concatenate([basis, previous.reshape(-1, side)], axis=0)  1.16 us
    ppermute x7, waiting for transfers between devices, exchange(): lax.ppermute(message_a, axis, near)  1.02 us
  transfers between devices with their start and end apart: 22, of which 12 were waited for; matrix products, arithmetic and copies ran while one was open for 0% of the time, Pallas kernels for 8%

profile of v18, /device:TPU:0, one launch (start us, length us, event | category | flops | bytes accessed | tf_op | source)
XLA Modules:
  0.0 49.7 jit_solution(2574179230018149287)
XLA Ops:
  0.7 1.2 %pad_maximum_fusion.vectors_ref = f32[1280,128]{1,0:T(8,128)S(1)} fusion(f32[256,128]{1,0:T(8,128)} %bitcast.24, f32[1024,128]{1,0:T(8,128)} %bitcast.23), kind=kLoop, calls=%fused_computation | loop fusion | flops 163840 | bytes 1310720 | tf_op jit(solution)/shard_map/concatenate | solution.py:477
  1.8 0.1 iota.7.flags_ref
  1.9 0.1 shard_map.93
  2.0 0.0 copy-start.2
  2.0 0.5 %collective-permute-start.2 = (f32[2,64,128]{2,1,0:T(8,128)S(1)}, f32[2,64,128]{2,1,0:T(8,128)S(1)}, u32[]{:S(2)}, u32[]{:S(2)}) collective-permute-start(f32[2,64,128]{2,1,0:T(8,128)S(1)} %get-tuple-element.38), channel_id=1, source_target_pairs={{0,1},{1,0},{2,3},{3,2},{4,5},{5,4},{6,7},{7,6},{8,9},{9,8},{10,11... | collective-permute-start | bytes 196616 | tf_op jit(solution)/shard_map/ppermute | solution.py:448
  2.5 2.6 %collective-permute-start.3 = (f32[2,64,128]{2,1,0:T(8,128)S(1)}, f32[2,64,128]{2,1,0:T(8,128)S(1)}, u32[]{:S(2)}, u32[]{:S(2)}) collective-permute-start(f32[2,64,128]{2,1,0:T(8,128)S(1)} %get-tuple-element.42), channel_id=1, source_target_pairs={{0,16},{1,2},{2,1},{3,19},{16,0},{17,18},{18,17},{19,3},{4,20},{5,... | collective-permute-start | bytes 196616 | tf_op jit(solution)/shard_map/ppermute | solution.py:448
  5.1 1.6 %collective-permute-start = (f32[4,64,128]{2,1,0:T(8,128)S(1)}, f32[4,64,128]{2,1,0:T(8,128)S(1)}, u32[]{:S(2)}, u32[]{:S(2)}) collective-permute-start(f32[4,64,128]{2,1,0:T(8,128)S(1)} %get-tuple-element.36.row_a_ref), channel_id=1, source_target_pairs={{0,4},{4,0},{8,12},{12,8},{1,5},{5,1},{9,13},{13,9},{2,6},{6,2},{1... | collective-permute-start | bytes 393224 | tf_op jit(solution)/shard_map/ppermute | solution.py:448
  6.7 0.5 %collective-permute-start.1 = (f32[4,64,128]{2,1,0:T(8,128)S(1)}, f32[4,64,128]{2,1,0:T(8,128)S(1)}, u32[]{:S(2)}, u32[]{:S(2)}) collective-permute-start(f32[4,64,128]{2,1,0:T(8,128)S(1)} %get-tuple-element.37.row_b_ref), channel_id=1, source_target_pairs={{0,16},{4,8},{8,4},{12,28},{16,0},{20,24},{24,20},{28,12},{1,17},{... | collective-permute-start | bytes 393224 | tf_op jit(solution)/shard_map/ppermute | solution.py:448
  7.2 0.1 shard_map.94
  7.2 0.1 collective-permute-done.3.side_b_ref.from_side_b_ref
  7.4 0.0 copy-start
  7.4 2.7 %collective-permute-start.4 = (f32[2,64,128]{2,1,0:T(8,128)S(1)}, f32[2,64,128]{2,1,0:T(8,128)S(1)}, u32[]{:S(2)}, u32[]{:S(2)}) collective-permute-start(f32[2,64,128]{2,1,0:T(8,128)S(1)} %get-tuple-element.43), channel_id=1, source_target_pairs={{0,4},{4,0},{8,12},{12,8},{1,5},{5,1},{9,13},{13,9},{2,6},{6,2},{1... | collective-permute-start | bytes 196616 | tf_op jit(solution)/shard_map/ppermute | solution.py:448
  10.0 1.0 %collective-permute-start.5 = (f32[2,64,128]{2,1,0:T(8,128)S(1)}, f32[2,64,128]{2,1,0:T(8,128)S(1)}, u32[]{:S(2)}, u32[]{:S(2)}) collective-permute-start(f32[2,64,128]{2,1,0:T(8,128)S(1)} %get-tuple-element.44), channel_id=1, source_target_pairs={{0,16},{4,8},{8,4},{12,28},{16,0},{20,24},{24,20},{28,12},{1,17},{... | collective-permute-start | bytes 196616 | tf_op jit(solution)/shard_map/ppermute | solution.py:448
  11.0 1.6 %collective-permute-start.8 = (f32[4,96,128]{2,1,0:T(8,128)S(1)}, f32[4,96,128]{2,1,0:T(8,128)S(1)}, u32[]{:S(2)}, u32[]{:S(2)}) collective-permute-start(f32[4,96,128]{2,1,0:T(8,128)S(1)} %get-tuple-element.45.rest_a_ref.row_a_ref), channel_id=1, source_target_pairs={{0,4},{4,0},{8,12},{12,8},{1,5},{5,1},{9,13},{13,9},{2,6},{6,2},{1... | collective-permute-start | bytes 589832 | tf_op jit(solution)/shard_map/ppermute | solution.py:448
  12.7 1.5 %collective-permute-start.9 = (f32[4,96,128]{2,1,0:T(8,128)S(1)}, f32[4,96,128]{2,1,0:T(8,128)S(1)}, u32[]{:S(2)}, u32[]{:S(2)}) collective-permute-start(f32[4,96,128]{2,1,0:T(8,128)S(1)} %get-tuple-element.46.rest_b_ref.row_b_ref), channel_id=1, source_target_pairs={{0,16},{4,8},{8,4},{12,28},{16,0},{20,24},{24,20},{28,12},{1,17},{... | collective-permute-start | bytes 589832 | tf_op jit(solution)/shard_map/ppermute | solution.py:448
  14.2 0.1 collective-permute-done.5.from_corner_b_ref
  14.3 2.6 %shard_map.96 = (f32[5,32,128]{2,1,0:T(8,128)S(1)}, f32[4,32,128]{2,1,0:T(8,128)S(1)}, f32[32,128]{1,0:T(8,128)S(1)}, f32[24,32,128]{2,1,0:T(8,128)S(1)}) custom-call(s32[8,5]{1,0:T(8,128)S(1)} %bitcast.19, s32[8,5]{1,0:T(8,128)S(1)} %bitcast.21, f32[8,128]{1,0:T(8,128)S(1)} %iota.7.flags_ref, f32[4,64,128]{2,1,0:T(8,128)S(1)} %get-tuple-element.36.row_a_ref, ...), custom_call_target="tpu_custom_call" | custom-call | flops 1000000000 | tf_op jit(solution)/shard_map/pallas_call | solution.py:489
  17.0 1.5 %collective-permute-start.6 = (f32[5,32,128]{2,1,0:T(8,128)S(1)}, f32[5,32,128]{2,1,0:T(8,128)S(1)}, u32[]{:S(2)}, u32[]{:S(2)}) collective-permute-start(f32[5,32,128]{2,1,0:T(8,128)S(1)} %get-tuple-element.48.row_a_ref), channel_id=1, source_target_pairs={{0,4},{4,0},{8,12},{12,8},{1,5},{5,1},{9,13},{13,9},{2,6},{6,2},{1... | collective-permute-start | bytes 245768 | tf_op jit(solution)/shard_map/ppermute | solution.py:448
  18.5 1.5 %collective-permute-start.12 = (f32[4,32,128]{2,1,0:T(8,128)S(1)}, f32[4,32,128]{2,1,0:T(8,128)S(1)}, u32[]{:S(2)}, u32[]{:S(2)}) collective-permute-start(f32[4,32,128]{2,1,0:T(8,128)S(1)} %get-tuple-element.52.row_b_ref), channel_id=1, source_target_pairs={{0,16},{4,8},{8,4},{12,28},{16,0},{20,24},{24,20},{28,12},{1,17},{... | collective-permute-start | bytes 196616 | tf_op jit(solution)/shard_map/ppermute | solution.py:448
  19.9 0.0 collective-permute-done.9.from_row_b_ref.from_rest_b_ref
  20.0 0.1 collective-permute-start.10
  20.1 0.6 %collective-permute-start.11 = (f32[4,96,128]{2,1,0:T(8,128)S(1)}, f32[4,96,128]{2,1,0:T(8,128)S(1)}, u32[]{:S(2)}, u32[]{:S(2)}) collective-permute-start(f32[4,96,128]{2,1,0:T(8,128)S(1)} %get-tuple-element.50), channel_id=1, source_target_pairs={{0,16},{1,2},{2,1},{3,19},{16,0},{17,18},{18,17},{19,3},{4,20},{5,... | collective-permute-start | bytes 589832 | tf_op jit(solution)/shard_map/ppermute | solution.py:448
  20.7 0.8 %collective-permute-done.6.from_row_a_ref = f32[5,32,128]{2,1,0:T(8,128)S(1)} collective-permute-done((f32[5,32,128]{2,1,0:T(8,128)S(1)}, f32[5,32,128]{2,1,0:T(8,128)S(1)}, u32[]{:S(2)}, u32[]{:S(2)}) %collective-permute-start.6) | collective-permute-done | bytes 81952 | tf_op jit(solution)/shard_map/ppermute | solution.py:448
  21.5 2.3 %collective-permute-start.7 = (f32[32,128]{1,0:T(8,128)S(1)}, f32[32,128]{1,0:T(8,128)S(1)}, u32[]{:S(2)}, u32[]{:S(2)}) collective-permute-start(f32[32,128]{1,0:T(8,128)S(1)} %fusion.1), channel_id=1, source_target_pairs={{0,8},{1,9},{2,10},{3,11},{4,12},{5,13},{6,14},{7,15},{8,0},{9,1},... | collective-permute-start | bytes 49160 | tf_op jit(solution)/shard_map/ppermute | solution.py:436
  23.8 2.4 %collective-permute-done.7 = f32[32,128]{1,0:T(8,128)S(1)} collective-permute-done((f32[32,128]{1,0:T(8,128)S(1)}, f32[32,128]{1,0:T(8,128)S(1)}, u32[]{:S(2)}, u32[]{:S(2)}) %collective-permute-start.7) | collective-permute-done | bytes 16416 | tf_op jit(solution)/shard_map/ppermute | solution.py:436
  26.2 0.0 collective-permute-done.11.rest_side_b_ref
  26.2 0.0 collective-permute-done.12.from_row_b_ref
  26.2 0.1 collective-permute-start.13
  26.3 1.1 %collective-permute-start.15 = (f32[4,32,128]{2,1,0:T(8,128)S(1)}, f32[4,32,128]{2,1,0:T(8,128)S(1)}, u32[]{:S(2)}, u32[]{:S(2)}) collective-permute-start(f32[4,32,128]{2,1,0:T(8,128)S(1)} %get-tuple-element.54), channel_id=1, source_target_pairs={{0,16},{1,2},{2,1},{3,19},{16,0},{17,18},{18,17},{19,3},{4,20},{5,... | collective-permute-start | bytes 196616 | tf_op jit(solution)/shard_map/ppermute | solution.py:448
  27.3 0.2 collective-permute-done.13.from_side_a_ref
  27.5 0.9 %collective-permute-start.14 = (f32[32,128]{1,0:T(8,128)S(1)}, f32[32,128]{1,0:T(8,128)S(1)}, u32[]{:S(2)}, u32[]{:S(2)}) collective-permute-start(f32[32,128]{1,0:T(8,128)S(1)} %fusion), channel_id=1, source_target_pairs={{0,2},{1,3},{2,0},{3,1},{4,6},{5,7},{6,4},{7,5},{8,10},{9,11},{10,... | collective-permute-start | bytes 49160 | tf_op jit(solution)/shard_map/ppermute | solution.py:436
  28.5 0.3 shard_map.99
  28.8 2.5 %collective-permute-done.14 = f32[32,128]{1,0:T(8,128)S(1)} collective-permute-done((f32[32,128]{1,0:T(8,128)S(1)}, f32[32,128]{1,0:T(8,128)S(1)}, u32[]{:S(2)}, u32[]{:S(2)}) %collective-permute-start.14) | collective-permute-done | bytes 16416 | tf_op jit(solution)/shard_map/ppermute | solution.py:436
  31.3 2.9 %shard_map.100 = (f32[4,32,128]{2,1,0:T(8,128)S(1)}, f32[4,32,128]{2,1,0:T(8,128)S(1)}, f32[32,128]{1,0:T(8,128)}, f32[48,128]{1,0:T(8,128)S(1)}, f32[48,128]{1,0:T(8,128)S(1)}) custom-call(s32[8,5]{1,0:T(8,128)S(1)} %bitcast.20, s32[8,5]{1,0:T(8,128)S(1)} %bitcast.22, f32[8,128]{1,0:T(8,128)S(1)} %iota.7.flags_ref, f32[32,128]{1,0:T(8,128)S(1)} %add.50.partial_ref, ...), custom_call_target="tpu_custom_call" | custom-call | tf_op jit(solution)/shard_map/pallas_call | solution.py:489
  34.2 0.1 collective-permute-start.16
  34.3 1.2 %collective-permute-done.16 = f32[48,128]{1,0:T(8,128)S(1)} collective-permute-done((f32[48,128]{1,0:T(8,128)S(1)}, f32[48,128]{1,0:T(8,128)S(1)}, u32[]{:S(2)}, u32[]{:S(2)}) %collective-permute-start.16) | collective-permute-done | bytes 24608 | tf_op jit(solution)/shard_map/ppermute | solution.py:436
  35.4 2.2 %collective-permute-start.17 = (f32[48,128]{1,0:T(8,128)S(1)}, f32[48,128]{1,0:T(8,128)S(1)}, u32[]{:S(2)}, u32[]{:S(2)}) collective-permute-start(f32[48,128]{1,0:T(8,128)S(1)} %add.51), channel_id=1, source_target_pairs={{0,6},{1,7},{2,4},{3,5},{4,2},{5,3},{6,0},{7,1},{8,14},{9,15},{10,... | collective-permute-start | bytes 73736 | tf_op jit(solution)/shard_map/ppermute | solution.py:436
  37.6 1.0 %collective-permute-start.18 = (f32[48,128]{1,0:T(8,128)S(1)}, f32[48,128]{1,0:T(8,128)S(1)}, u32[]{:S(2)}, u32[]{:S(2)}) collective-permute-start(f32[48,128]{1,0:T(8,128)S(1)} %add.51), channel_id=1, source_target_pairs={{0,2},{1,3},{2,0},{3,1},{4,6},{5,7},{6,4},{7,5},{8,10},{9,11},{10,... | collective-permute-start | bytes 73736 | tf_op jit(solution)/shard_map/ppermute | solution.py:436
  38.7 0.3 collective-permute-start.19
  38.9 1.2 %collective-permute-done.17 = f32[48,128]{1,0:T(8,128)S(1)} collective-permute-done((f32[48,128]{1,0:T(8,128)S(1)}, f32[48,128]{1,0:T(8,128)S(1)}, u32[]{:S(2)}, u32[]{:S(2)}) %collective-permute-start.17) | collective-permute-done | bytes 24608 | tf_op jit(solution)/shard_map/ppermute | solution.py:436
  40.2 1.3 %collective-permute-done.18 = f32[48,128]{1,0:T(8,128)S(1)} collective-permute-done((f32[48,128]{1,0:T(8,128)S(1)}, f32[48,128]{1,0:T(8,128)S(1)}, u32[]{:S(2)}, u32[]{:S(2)}) %collective-permute-start.18) | collective-permute-done | bytes 24608 | tf_op jit(solution)/shard_map/ppermute | solution.py:436
  41.5 1.0 %collective-permute-done.19 = f32[48,128]{1,0:T(8,128)S(1)} collective-permute-done((f32[48,128]{1,0:T(8,128)S(1)}, f32[48,128]{1,0:T(8,128)S(1)}, u32[]{:S(2)}, u32[]{:S(2)}) %collective-permute-start.19) | collective-permute-done | bytes 24608 | tf_op jit(solution)/shard_map/ppermute | solution.py:436
  42.5 2.6 %collective-permute-start.20 = (f32[48,128]{1,0:T(8,128)S(1)}, f32[48,128]{1,0:T(8,128)S(1)}, u32[]{:S(2)}, u32[]{:S(2)}) collective-permute-start(f32[48,128]{1,0:T(8,128)S(1)} %add_add_fusion), channel_id=1, source_target_pairs={{0,8},{1,9},{2,10},{3,11},{4,12},{5,13},{6,14},{7,15},{8,0},{9,1},... | collective-permute-start | bytes 73736 | tf_op jit(solution)/shard_map/ppermute | solution.py:436
  45.1 2.2 %collective-permute-done.20 = f32[48,128]{1,0:T(8,128)S(1)} collective-permute-done((f32[48,128]{1,0:T(8,128)S(1)}, f32[48,128]{1,0:T(8,128)S(1)}, u32[]{:S(2)}, u32[]{:S(2)}) %collective-permute-start.20) | collective-permute-done | bytes 24608 | tf_op jit(solution)/shard_map/ppermute | solution.py:436
  47.3 0.1 collective-permute-start.21
  47.4 0.9 %shard_map.101.work_ref = f32[32,64]{1,0:T(8,128)S(1)} custom-call(f32[48,128]{1,0:T(8,128)S(1)} %add.55.sums_ref), custom_call_target="tpu_custom_call" | custom-call | flops 1000000000 | tf_op jit(solution)/shard_map/pallas_call | solution.py:489
  48.3 0.3 collective-permute-done.21.other_ref
  48.5 1.2 %shard_map.102 = (f32[256,128]{1,0:T(8,128)}, f32[32,32]{1,0:T(8,128)}, f32[2,32,160]{2,1,0:T(8,128)}) custom-call(f32[8,128]{1,0:T(8,128)S(1)} %iota.7.flags_ref, f32[32,64]{1,0:T(8,128)S(1)} %shard_map.101.work_ref, f32[48,128]{1,0:T(8,128)S(1)} %add.55.sums_ref, f32[40,128]{1,0:T(8,128)S(1)} %collective-permute-done.21.other_ref, ...), custom_call_target="tpu_custom_call" | custom-call | tf_op jit(solution)/shard_map/pallas_call | solution.py:489
  (25 shorter events, 0.2 us)
Async XLA Ops:
  1.9 12.4 %copy-start.3 = (f32[8,128,128]{2,1,0:T(8,128)S(1)}, f32[8,128,128]{2,1,0:T(8,128)}, u32[]{:S(2)}) copy-start(f32[8,128,128]{2,1,0:T(8,128)} %mass_ref.3) | copy-start | bytes 1572868
  2.0 12.3 %copy-start.2 = (f32[8,128,128]{2,1,0:T(8,128)S(1)}, f32[8,128,128]{2,1,0:T(8,128)}, u32[]{:S(2)}) copy-start(f32[8,128,128]{2,1,0:T(8,128)} %stiff_ref.3) | copy-start | bytes 1572868
  2.0 5.3 %collective-permute-start.2 = (f32[2,64,128]{2,1,0:T(8,128)S(1)}, f32[2,64,128]{2,1,0:T(8,128)S(1)}, u32[]{:S(2)}, u32[]{:S(2)}) collective-permute-start(f32[2,64,128]{2,1,0:T(8,128)S(1)} %get-tuple-element.38), channel_id=1, source_target_pairs={{0,1},{1,0},{2,3},{3,2},{4,5},{5,4},{6,7},{7,6},{8,9},{9,8},{10,11... | collective-permute-start | bytes 196616 | tf_op jit(solution)/shard_map/ppermute | solution.py:448
  2.5 4.8 %collective-permute-start.3 = (f32[2,64,128]{2,1,0:T(8,128)S(1)}, f32[2,64,128]{2,1,0:T(8,128)S(1)}, u32[]{:S(2)}, u32[]{:S(2)}) collective-permute-start(f32[2,64,128]{2,1,0:T(8,128)S(1)} %get-tuple-element.42), channel_id=1, source_target_pairs={{0,16},{1,2},{2,1},{3,19},{16,0},{17,18},{18,17},{19,3},{4,20},{5,... | collective-permute-start | bytes 196616 | tf_op jit(solution)/shard_map/ppermute | solution.py:448
  5.1 9.2 %collective-permute-start = (f32[4,64,128]{2,1,0:T(8,128)S(1)}, f32[4,64,128]{2,1,0:T(8,128)S(1)}, u32[]{:S(2)}, u32[]{:S(2)}) collective-permute-start(f32[4,64,128]{2,1,0:T(8,128)S(1)} %get-tuple-element.36.row_a_ref), channel_id=1, source_target_pairs={{0,4},{4,0},{8,12},{12,8},{1,5},{5,1},{9,13},{13,9},{2,6},{6,2},{1... | collective-permute-start | bytes 393224 | tf_op jit(solution)/shard_map/ppermute | solution.py:448
  6.7 7.6 %collective-permute-start.1 = (f32[4,64,128]{2,1,0:T(8,128)S(1)}, f32[4,64,128]{2,1,0:T(8,128)S(1)}, u32[]{:S(2)}, u32[]{:S(2)}) collective-permute-start(f32[4,64,128]{2,1,0:T(8,128)S(1)} %get-tuple-element.37.row_b_ref), channel_id=1, source_target_pairs={{0,16},{4,8},{8,4},{12,28},{16,0},{20,24},{24,20},{28,12},{1,17},{... | collective-permute-start | bytes 393224 | tf_op jit(solution)/shard_map/ppermute | solution.py:448
  7.3 7.0 %copy-start.1 = (s32[5,2,4]{0,2,1:T(4,128)S(1)}, s32[5,2,4]{0,2,1:T(4,128)}, u32[]{:S(2)}) copy-start(s32[5,2,4]{0,2,1:T(4,128)} %param.9) | copy-start | bytes 484
  7.4 7.0 %copy-start = (s32[5,2,4]{0,2,1:T(4,128)S(1)}, s32[5,2,4]{0,2,1:T(4,128)}, u32[]{:S(2)}) copy-start(s32[5,2,4]{0,2,1:T(4,128)} %param.8) | copy-start | bytes 484
  7.4 5.3 %collective-permute-start.4 = (f32[2,64,128]{2,1,0:T(8,128)S(1)}, f32[2,64,128]{2,1,0:T(8,128)S(1)}, u32[]{:S(2)}, u32[]{:S(2)}) collective-permute-start(f32[2,64,128]{2,1,0:T(8,128)S(1)} %get-tuple-element.43), channel_id=1, source_target_pairs={{0,4},{4,0},{8,12},{12,8},{1,5},{5,1},{9,13},{13,9},{2,6},{6,2},{1... | collective-permute-start | bytes 196616 | tf_op jit(solution)/shard_map/ppermute | solution.py:448
  10.0 4.3 %collective-permute-start.5 = (f32[2,64,128]{2,1,0:T(8,128)S(1)}, f32[2,64,128]{2,1,0:T(8,128)S(1)}, u32[]{:S(2)}, u32[]{:S(2)}) collective-permute-start(f32[2,64,128]{2,1,0:T(8,128)S(1)} %get-tuple-element.44), channel_id=1, source_target_pairs={{0,16},{4,8},{8,4},{12,28},{16,0},{20,24},{24,20},{28,12},{1,17},{... | collective-permute-start | bytes 196616 | tf_op jit(solution)/shard_map/ppermute | solution.py:448
  11.0 8.9 %collective-permute-start.8 = (f32[4,96,128]{2,1,0:T(8,128)S(1)}, f32[4,96,128]{2,1,0:T(8,128)S(1)}, u32[]{:S(2)}, u32[]{:S(2)}) collective-permute-start(f32[4,96,128]{2,1,0:T(8,128)S(1)} %get-tuple-element.45.rest_a_ref.row_a_ref), channel_id=1, source_target_pairs={{0,4},{4,0},{8,12},{12,8},{1,5},{5,1},{9,13},{13,9},{2,6},{6,2},{1... | collective-permute-start | bytes 589832 | tf_op jit(solution)/shard_map/ppermute | solution.py:448
  12.7 7.3 %collective-permute-start.9 = (f32[4,96,128]{2,1,0:T(8,128)S(1)}, f32[4,96,128]{2,1,0:T(8,128)S(1)}, u32[]{:S(2)}, u32[]{:S(2)}) collective-permute-start(f32[4,96,128]{2,1,0:T(8,128)S(1)} %get-tuple-element.46.rest_b_ref.row_b_ref), channel_id=1, source_target_pairs={{0,16},{4,8},{8,4},{12,28},{16,0},{20,24},{24,20},{28,12},{1,17},{... | collective-permute-start | bytes 589832 | tf_op jit(solution)/shard_map/ppermute | solution.py:448
  17.0 4.5 %collective-permute-start.6 = (f32[5,32,128]{2,1,0:T(8,128)S(1)}, f32[5,32,128]{2,1,0:T(8,128)S(1)}, u32[]{:S(2)}, u32[]{:S(2)}) collective-permute-start(f32[5,32,128]{2,1,0:T(8,128)S(1)} %get-tuple-element.48.row_a_ref), channel_id=1, source_target_pairs={{0,4},{4,0},{8,12},{12,8},{1,5},{5,1},{9,13},{13,9},{2,6},{6,2},{1... | collective-permute-start | bytes 245768 | tf_op jit(solution)/shard_map/ppermute | solution.py:448
  18.5 7.7 %collective-permute-start.12 = (f32[4,32,128]{2,1,0:T(8,128)S(1)}, f32[4,32,128]{2,1,0:T(8,128)S(1)}, u32[]{:S(2)}, u32[]{:S(2)}) collective-permute-start(f32[4,32,128]{2,1,0:T(8,128)S(1)} %get-tuple-element.52.row_b_ref), channel_id=1, source_target_pairs={{0,16},{4,8},{8,4},{12,28},{16,0},{20,24},{24,20},{28,12},{1,17},{... | collective-permute-start | bytes 196616 | tf_op jit(solution)/shard_map/ppermute | solution.py:448
  20.0 6.2 %collective-permute-start.10 = (f32[4,96,128]{2,1,0:T(8,128)S(1)}, f32[4,96,128]{2,1,0:T(8,128)S(1)}, u32[]{:S(2)}, u32[]{:S(2)}) collective-permute-start(f32[4,96,128]{2,1,0:T(8,128)S(1)} %get-tuple-element.49), channel_id=1, source_target_pairs={{0,1},{1,0},{2,3},{3,2},{4,5},{5,4},{6,7},{7,6},{8,9},{9,8},{10,11... | collective-permute-start | bytes 589832 | tf_op jit(solution)/shard_map/ppermute | solution.py:448
  20.1 6.1 %collective-permute-start.11 = (f32[4,96,128]{2,1,0:T(8,128)S(1)}, f32[4,96,128]{2,1,0:T(8,128)S(1)}, u32[]{:S(2)}, u32[]{:S(2)}) collective-permute-start(f32[4,96,128]{2,1,0:T(8,128)S(1)} %get-tuple-element.50), channel_id=1, source_target_pairs={{0,16},{1,2},{2,1},{3,19},{16,0},{17,18},{18,17},{19,3},{4,20},{5,... | collective-permute-start | bytes 589832 | tf_op jit(solution)/shard_map/ppermute | solution.py:448
  21.5 4.6 %collective-permute-start.7 = (f32[32,128]{1,0:T(8,128)S(1)}, f32[32,128]{1,0:T(8,128)S(1)}, u32[]{:S(2)}, u32[]{:S(2)}) collective-permute-start(f32[32,128]{1,0:T(8,128)S(1)} %fusion.1), channel_id=1, source_target_pairs={{0,8},{1,9},{2,10},{3,11},{4,12},{5,13},{6,14},{7,15},{8,0},{9,1},... | collective-permute-start | bytes 49160 | tf_op jit(solution)/shard_map/ppermute | solution.py:436
  26.2 1.3 %collective-permute-start.13 = (f32[5,32,128]{2,1,0:T(8,128)S(1)}, f32[5,32,128]{2,1,0:T(8,128)S(1)}, u32[]{:S(2)}, u32[]{:S(2)}) collective-permute-start(f32[5,32,128]{2,1,0:T(8,128)S(1)} %get-tuple-element.53), channel_id=1, source_target_pairs={{0,1},{1,0},{2,3},{3,2},{4,5},{5,4},{6,7},{7,6},{8,9},{9,8},{10,11... | collective-permute-start | bytes 245768 | tf_op jit(solution)/shard_map/ppermute | solution.py:448
  26.3 5.0 %collective-permute-start.15 = (f32[4,32,128]{2,1,0:T(8,128)S(1)}, f32[4,32,128]{2,1,0:T(8,128)S(1)}, u32[]{:S(2)}, u32[]{:S(2)}) collective-permute-start(f32[4,32,128]{2,1,0:T(8,128)S(1)} %get-tuple-element.54), channel_id=1, source_target_pairs={{0,16},{1,2},{2,1},{3,19},{16,0},{17,18},{18,17},{19,3},{4,20},{5,... | collective-permute-start | bytes 196616 | tf_op jit(solution)/shard_map/ppermute | solution.py:448
  27.5 3.7 %collective-permute-start.14 = (f32[32,128]{1,0:T(8,128)S(1)}, f32[32,128]{1,0:T(8,128)S(1)}, u32[]{:S(2)}, u32[]{:S(2)}) collective-permute-start(f32[32,128]{1,0:T(8,128)S(1)} %fusion), channel_id=1, source_target_pairs={{0,2},{1,3},{2,0},{3,1},{4,6},{5,7},{6,4},{7,5},{8,10},{9,11},{10,... | collective-permute-start | bytes 49160 | tf_op jit(solution)/shard_map/ppermute | solution.py:436
  34.2 1.3 %collective-permute-start.16 = (f32[48,128]{1,0:T(8,128)S(1)}, f32[48,128]{1,0:T(8,128)S(1)}, u32[]{:S(2)}, u32[]{:S(2)}) collective-permute-start(f32[48,128]{1,0:T(8,128)S(1)} %get-tuple-element.61), channel_id=1, source_target_pairs={{0,1},{1,0},{2,3},{3,2},{4,5},{5,4},{6,7},{7,6},{8,9},{9,8},{10,11... | collective-permute-start | bytes 73736 | tf_op jit(solution)/shard_map/ppermute | solution.py:436
  35.4 4.7 %collective-permute-start.17 = (f32[48,128]{1,0:T(8,128)S(1)}, f32[48,128]{1,0:T(8,128)S(1)}, u32[]{:S(2)}, u32[]{:S(2)}) collective-permute-start(f32[48,128]{1,0:T(8,128)S(1)} %add.51), channel_id=1, source_target_pairs={{0,6},{1,7},{2,4},{3,5},{4,2},{5,3},{6,0},{7,1},{8,14},{9,15},{10,... | collective-permute-start | bytes 73736 | tf_op jit(solution)/shard_map/ppermute | solution.py:436
  37.6 3.8 %collective-permute-start.18 = (f32[48,128]{1,0:T(8,128)S(1)}, f32[48,128]{1,0:T(8,128)S(1)}, u32[]{:S(2)}, u32[]{:S(2)}) collective-permute-start(f32[48,128]{1,0:T(8,128)S(1)} %add.51), channel_id=1, source_target_pairs={{0,2},{1,3},{2,0},{3,1},{4,6},{5,7},{6,4},{7,5},{8,10},{9,11},{10,... | collective-permute-start | bytes 73736 | tf_op jit(solution)/shard_map/ppermute | solution.py:436
  38.7 3.8 %collective-permute-start.19 = (f32[48,128]{1,0:T(8,128)S(1)}, f32[48,128]{1,0:T(8,128)S(1)}, u32[]{:S(2)}, u32[]{:S(2)}) collective-permute-start(f32[48,128]{1,0:T(8,128)S(1)} %add.51), channel_id=1, source_target_pairs={{0,4},{1,5},{2,6},{3,7},{4,0},{5,1},{6,2},{7,3},{8,12},{9,13},{10,... | collective-permute-start | bytes 73736 | tf_op jit(solution)/shard_map/ppermute | solution.py:436
  42.5 4.8 %collective-permute-start.20 = (f32[48,128]{1,0:T(8,128)S(1)}, f32[48,128]{1,0:T(8,128)S(1)}, u32[]{:S(2)}, u32[]{:S(2)}) collective-permute-start(f32[48,128]{1,0:T(8,128)S(1)} %add_add_fusion), channel_id=1, source_target_pairs={{0,8},{1,9},{2,10},{3,11},{4,12},{5,13},{6,14},{7,15},{8,0},{9,1},... | collective-permute-start | bytes 73736 | tf_op jit(solution)/shard_map/ppermute | solution.py:436
  47.3 1.3 %collective-permute-start.21 = (f32[40,128]{1,0:T(8,128)S(1)}, f32[40,128]{1,0:T(8,128)S(1)}, u32[]{:S(2)}, u32[]{:S(2)}) collective-permute-start(f32[40,128]{1,0:T(8,128)S(1)} %slice.14), channel_id=1, source_target_pairs={{0,1},{1,0},{2,3},{3,2},{4,5},{5,4},{6,7},{7,6},{8,9},{9,8},{10,11... | collective-permute-start | bytes 61448 | tf_op jit(solution)/shard_map/ppermute | solution.py:436

commit v19 on v18

--- a/solution.py
+++ b/solution.py
@@ -175,6 +175,9 @@
     neighbours_ref,
     kinds_ref,
     semaphores,
+    total_ref,
+    parts_ref,
+    prior_ref,
 ):
     copies = code_copies(
         (neighbours_hbm_ref, kinds_hbm_ref), (neighbours_ref, kinds_ref), semaphores
@@ -197,11 +200,12 @@
             ext_ref[i * wide + j, :block, part * side : (part + 1) * side] = high
             ext_ref[i * wide + j, block:, part * side : (part + 1) * side] = low
 
-    own = {}
+    def own_tile(i, j):
+        return pick(odd_x, row_a_ref[j], row_b_ref[j])[i]
+
     for j in range(count_y):
-        own[0, j], own[1, j] = pick(odd_x, row_a_ref[j], row_b_ref[j])
-        store(1, j + 1, own[0, j])
-        store(2, j + 1, own[1, j])
+        store(1, j + 1, own_tile(0, j))
+        store(2, j + 1, own_tile(1, j))
         low, high = pick(odd_x, from_row_a_ref[j], from_row_b_ref[j])
         store(0, j + 1, low * in_low_x)
         store(3, j + 1, high * in_high_x)
@@ -215,21 +219,25 @@
         store(3, j, high * (in_high_x * inside))
     for copy in copies:
         copy.wait()
-    partial = jnp.zeros((block, rest + block), F32)
-    totals = {}
     for tile in range(2 * count_y):
         i, j = tile // count_y, tile % count_y
-        total = 4.0 * own[i, j][:block] + own[i, j][block:]
+        own = own_tile(i, j)
+        total = 4.0 * own[:block] + own[block:]
         for k in range(neighbours_ref.shape[1]):
             source, kind = source_and_kind(neighbours_ref, kinds_ref, tile, k, count_y)
             pair = mul(ext_ref[source], table_ref[kind])
             total = total + (pair[:block, :side] + (pair[block:, :side] + pair[:block, side:]))
-        totals[i, j] = total
+        total_ref[tile] = total
+        span = slice(tile * side, (tile + 1) * side)
+        parts_ref[:, span] = stacked(total)
         rest_tile = pick(odd_x, rest_a_ref[j], rest_b_ref[j])[i]
-        basis_tile = jnp.concatenate([rest_tile, own[i, j][:block]], axis=0)
-        partial = partial + pair_sum(stacked(total), *split(basis_tile))
+        basis_tile = jnp.concatenate([rest_tile, own[:block]], axis=0)
+        prior_ref[0, :, span], prior_ref[1, :, span] = split(basis_tile)
+    partial = pair_sum(parts_ref[...], prior_ref[0], prior_ref[1])
     for j in range(count_y):
-        residual_a_ref[j], residual_b_ref[j] = pick(odd_x, totals[0, j], totals[1, j])
+        residual_a_ref[j], residual_b_ref[j] = pick(
+            odd_x, total_ref[j], total_ref[count_y + j]
+        )
     residual_a_ref[count_y] = partial
     partial_ref[...] = partial
 
@@ -244,9 +252,10 @@
     stiff_ref,
     mass_ref,
     basis_ref,
+    prior_ref,
     table_ref,
 ):
-    count_y, rest, _ = rest_a_ref.shape
+    count_y, rest, side = rest_a_ref.shape
     prior = rest + current_ref.shape[1]
     odd_x = flag_at(flags_ref, 1)
     split_tables(stiff_ref, mass_ref, table_ref, 0)
@@ -255,9 +264,14 @@
         rests[1:1] = pick(odd_x, rest_a_ref[j], rest_b_ref[j])
         for i in range(4):
             tile = jnp.concatenate([rests[i], current_ref[i * (count_y + 2) + j + 1]], axis=0)
-            basis_ref[i * count_y + j, :prior, :], basis_ref[i * count_y + j, prior:, :] = split(
-                tile
-            )
+            high, low = split(tile)
+            basis_ref[i * count_y + j, :prior, :] = high
+            basis_ref[i * count_y + j, prior:, :] = low
+            if 0 < i < 3:
+                place = (i - 1) * count_y + j
+                span = slice(place * side, (place + 1) * side)
+                prior_ref[0, :, span] = high
+                prior_ref[1, :, span] = low
 
 
 def operators_kernel(
@@ -276,6 +290,7 @@
     rest_side_b_ref,
     current_ref,
     basis_ref,
+    prior_ref,
     table_ref,
     weighted_low_ref,
     weighted_high_ref,
@@ -286,6 +301,7 @@
     neighbours_ref,
     kinds_ref,
     semaphores,
+    parts_ref,
 ):
     copies = code_copies(
         (neighbours_hbm_ref, kinds_hbm_ref), (neighbours_ref, kinds_ref), semaphores
@@ -333,8 +349,6 @@
             ext_ref[i * wide + j] = deep(value)
     for copy in copies:
         copy.wait()
-    with_basis = jnp.zeros((2 * block, prior), F32)
-    with_own = jnp.zeros((block, 4 * block), F32)
     for tile in range(2 * count_y):
         i, j = tile // count_y, tile % count_y
         own = (weighted_low_ref, weighted_high_ref)[i][j]
@@ -342,13 +356,17 @@
         for k in range(neighbours_ref.shape[1]):
             source, kind = source_and_kind(neighbours_ref, kinds_ref, tile, k, count_y)
             totals = totals + halves_sum(mul(ext_ref[source], table_ref[kind]))
-        applied = jnp.concatenate([totals[:, :side], totals[:, side:]], axis=0)
-        basis_tile = basis_parts(i + 1, j + 1)
-        with_basis = with_basis + pair_sum(
-            stacked(applied), basis_tile[:prior], basis_tile[prior:]
-        )
-        right = jnp.concatenate([applied, own, jnp.zeros_like(own)], axis=0)
-        with_own = with_own + pair_sum(stacked(own), *split(right))
+        rows = jnp.concatenate([totals[:, :side], totals[:, side:], own, own], axis=0)
+        span = slice(tile * side, (tile + 1) * side)
+        parts_ref[0, :, span], parts_ref[1, :, span] = split(rows)
+    applied = [parts_ref[part, : 2 * block, :] for part in range(2)]
+    own_parts = [parts_ref[part, 2 * block : 3 * block, :] for part in range(2)]
+    with_basis = mul_t(applied[0], prior_ref[0]) + (
+        mul_t(applied[0], prior_ref[1]) + mul_t(applied[1], prior_ref[0])
+    )
+    with_own = mul_t(own_parts[0], parts_ref[0]) + (
+        mul_t(own_parts[0], parts_ref[1]) + mul_t(own_parts[1], parts_ref[0])
+    )
     halves = [
         jnp.concatenate(
             [
@@ -540,7 +558,12 @@
         + [shape(block, prior), shape(4 * wide, block, side)],
         [pltpu.VMEM((4 * wide, 2 * block, 2 * side), BF16)]
         + [pltpu.VMEM((kinds, 2 * side, 2 * side), BF16)]
-        + code_scratch,
+        + code_scratch
+        + [
+            pltpu.VMEM((tiles, block, side), F32),
+            pltpu.VMEM((2 * block, tiles * side), BF16),
+            pltpu.VMEM((2, prior, tiles * side), BF16),
+        ],
         plain=2,
         cost=pl.CostEstimate(flops=10**9, bytes_accessed=0, transcendentals=0),
     )
@@ -559,10 +582,11 @@
     )
     from_side_a, from_side_b = exchange(side_a, side_b, "py")
     partial = total_over(partial + from_side_a[-1], 2, count_py)
-    basis_parts, table = call(
+    basis_parts, prior_parts, table = call(
         prepare_kernel,
         (flags, rest_a, rest_b, from_rest_a, from_rest_b, current, stiff_tiles, mass_tiles),
         [shape(4 * count_y, 2 * prior, side, dtype=BF16)]
+        + [shape(2, prior, tiles * side, dtype=BF16)]
         + [shape(kinds, 2 * side, 2 * side, dtype=BF16)],
         cost=pl.CostEstimate(flops=10**9, bytes_accessed=0, transcendentals=0),
     )
@@ -582,12 +606,15 @@
             rest_side_b,
             current,
             basis_parts,
+            prior_parts,
             table,
         ),
         [shape(count_y, block, side)] * 2
         + [shape(block, prior)]
         + [shape(block + 16, prior)] * 2,
-        [pltpu.VMEM((4 * wide, 2 * block, 2 * side), BF16)] + code_scratch,
+        [pltpu.VMEM((4 * wide, 2 * block, 2 * side), BF16)]
+        + code_scratch
+        + [pltpu.VMEM((2, 4 * block, tiles * side), BF16)],
         plain=2,
     )
     kept = half_total(sent, kept)

time: 49.9 us -> 49.1 us (0.984)
  Pallas kernels: 8.13 us -> 7.43 us
  waiting for transfers between devices: 13.3 us -> 12.8 us
    pallas_call x10, Pallas kernels: 8.13 us -> 7.43 us  [call(): pl.pallas_call(kernel, out_shape=outputs, in_specs=specs, out_specs=[VMEM...]
  transfers between devices with their start and end apart: 22 -> 22, of which waited for: 12 -> 12; matrix products, arithmetic and copies ran while one was open for 0% -> 0% of each run, Pallas kernels for 8% -> 7%
where the time goes in v19:
time: 49.1 us; the launch traced here: 48.9 us
  starting transfers between devices  26.6 us (54%)
  waiting for transfers between devices  12.8 us (26%)
  Pallas kernels  7.43 us (15%)
  other arithmetic  1.2 us (2%)
  between operations  0.84 us (2%)
    ppermute x8, waiting for transfers between devices, swap(): return lax.ppermute(value, axes, pairs)  12 us
    ppermute x8, starting transfers between devices, swap(): return lax.ppermute(value, axes, pairs)  9.4 us
    ppermute x7, starting transfers between devices, exchange(): lax.ppermute(message_b, ('case', axis), pairs)  9.16 us
    ppermute x7, starting transfers between devices, exchange(): lax.ppermute(message_a, axis, near)  8 us
    pallas_call x10, Pallas kernels, call(): pl.pallas_call(kernel, out_shape=outputs, in_specs=specs, out_specs=[VMEM...  7.43 us
    concatenate x1, other arithmetic, shards(): vectors = jnp.concatenate([basis, previous.reshape(-1, side)], axis=0)  1.16 us
  transfers between devices with their start and end apart: 22, of which 12 were waited for; matrix products, arithmetic and copies ran while one was open for 0% of the time, Pallas kernels for 7%

profile of v19, /device:TPU:0, one launch (start us, length us, event | category | flops | bytes accessed | tf_op | source)
XLA Modules:
  0.0 48.9 jit_solution(9273727594768802410)
XLA Ops:
  0.7 1.2 %pad_maximum_fusion.vectors_ref = f32[1280,128]{1,0:T(8,128)S(1)} fusion(f32[256,128]{1,0:T(8,128)} %bitcast.24, f32[1024,128]{1,0:T(8,128)} %bitcast.23), kind=kLoop, calls=%fused_computation | loop fusion | flops 163840 | bytes 1310720 | tf_op jit(solution)/shard_map/concatenate | solution.py:495
  1.8 0.1 iota.7.flags_ref
  1.9 0.1 shard_map.93
  2.0 0.0 copy-start.2
  2.0 0.5 %collective-permute-start.2 = (f32[2,64,128]{2,1,0:T(8,128)S(1)}, f32[2,64,128]{2,1,0:T(8,128)S(1)}, u32[]{:S(2)}, u32[]{:S(2)}) collective-permute-start(f32[2,64,128]{2,1,0:T(8,128)S(1)} %get-tuple-element.39), channel_id=1, source_target_pairs={{0,1},{1,0},{2,3},{3,2},{4,5},{5,4},{6,7},{7,6},{8,9},{9,8},{10,11... | collective-permute-start | bytes 196616 | tf_op jit(solution)/shard_map/ppermute | solution.py:466
  2.5 2.6 %collective-permute-start.3 = (f32[2,64,128]{2,1,0:T(8,128)S(1)}, f32[2,64,128]{2,1,0:T(8,128)S(1)}, u32[]{:S(2)}, u32[]{:S(2)}) collective-permute-start(f32[2,64,128]{2,1,0:T(8,128)S(1)} %get-tuple-element.43), channel_id=1, source_target_pairs={{0,16},{1,2},{2,1},{3,19},{16,0},{17,18},{18,17},{19,3},{4,20},{5,... | collective-permute-start | bytes 196616 | tf_op jit(solution)/shard_map/ppermute | solution.py:466
  5.1 1.6 %collective-permute-start = (f32[4,64,128]{2,1,0:T(8,128)S(1)}, f32[4,64,128]{2,1,0:T(8,128)S(1)}, u32[]{:S(2)}, u32[]{:S(2)}) collective-permute-start(f32[4,64,128]{2,1,0:T(8,128)S(1)} %get-tuple-element.37.row_a_ref), channel_id=1, source_target_pairs={{0,4},{4,0},{8,12},{12,8},{1,5},{5,1},{9,13},{13,9},{2,6},{6,2},{1... | collective-permute-start | bytes 393224 | tf_op jit(solution)/shard_map/ppermute | solution.py:466
  6.7 0.5 %collective-permute-start.1 = (f32[4,64,128]{2,1,0:T(8,128)S(1)}, f32[4,64,128]{2,1,0:T(8,128)S(1)}, u32[]{:S(2)}, u32[]{:S(2)}) collective-permute-start(f32[4,64,128]{2,1,0:T(8,128)S(1)} %get-tuple-element.38.row_b_ref), channel_id=1, source_target_pairs={{0,16},{4,8},{8,4},{12,28},{16,0},{20,24},{24,20},{28,12},{1,17},{... | collective-permute-start | bytes 393224 | tf_op jit(solution)/shard_map/ppermute | solution.py:466
  7.2 0.1 shard_map.94
  7.2 0.0 collective-permute-done.2.side_a_ref.from_side_a_ref
  7.2 0.1 collective-permute-done.3.side_b_ref.from_side_b_ref
  7.3 0.0 copy-start
  7.4 2.7 %collective-permute-start.4 = (f32[2,64,128]{2,1,0:T(8,128)S(1)}, f32[2,64,128]{2,1,0:T(8,128)S(1)}, u32[]{:S(2)}, u32[]{:S(2)}) collective-permute-start(f32[2,64,128]{2,1,0:T(8,128)S(1)} %get-tuple-element.44), channel_id=1, source_target_pairs={{0,4},{4,0},{8,12},{12,8},{1,5},{5,1},{9,13},{13,9},{2,6},{6,2},{1... | collective-permute-start | bytes 196616 | tf_op jit(solution)/shard_map/ppermute | solution.py:466
  10.0 1.0 %collective-permute-start.5 = (f32[2,64,128]{2,1,0:T(8,128)S(1)}, f32[2,64,128]{2,1,0:T(8,128)S(1)}, u32[]{:S(2)}, u32[]{:S(2)}) collective-permute-start(f32[2,64,128]{2,1,0:T(8,128)S(1)} %get-tuple-element.45), channel_id=1, source_target_pairs={{0,16},{4,8},{8,4},{12,28},{16,0},{20,24},{24,20},{28,12},{1,17},{... | collective-permute-start | bytes 196616 | tf_op jit(solution)/shard_map/ppermute | solution.py:466
  11.0 1.6 %collective-permute-start.8 = (f32[4,96,128]{2,1,0:T(8,128)S(1)}, f32[4,96,128]{2,1,0:T(8,128)S(1)}, u32[]{:S(2)}, u32[]{:S(2)}) collective-permute-start(f32[4,96,128]{2,1,0:T(8,128)S(1)} %get-tuple-element.46.rest_a_ref.row_a_ref), channel_id=1, source_target_pairs={{0,4},{4,0},{8,12},{12,8},{1,5},{5,1},{9,13},{13,9},{2,6},{6,2},{1... | collective-permute-start | bytes 589832 | tf_op jit(solution)/shard_map/ppermute | solution.py:466
  12.7 1.5 %collective-permute-start.9 = (f32[4,96,128]{2,1,0:T(8,128)S(1)}, f32[4,96,128]{2,1,0:T(8,128)S(1)}, u32[]{:S(2)}, u32[]{:S(2)}) collective-permute-start(f32[4,96,128]{2,1,0:T(8,128)S(1)} %get-tuple-element.47.rest_b_ref.row_b_ref), channel_id=1, source_target_pairs={{0,16},{4,8},{8,4},{12,28},{16,0},{20,24},{24,20},{28,12},{1,17},{... | collective-permute-start | bytes 589832 | tf_op jit(solution)/shard_map/ppermute | solution.py:466
  14.2 0.1 collective-permute-done.5.from_corner_b_ref
  14.3 0.0 collective-permute-done.from_row_a_ref
  14.3 0.0 collective-permute-done.1.from_row_b_ref
  14.3 2.1 %shard_map.96 = (f32[5,32,128]{2,1,0:T(8,128)S(1)}, f32[4,32,128]{2,1,0:T(8,128)S(1)}, f32[32,128]{1,0:T(8,128)S(1)}, f32[24,32,128]{2,1,0:T(8,128)S(1)}) custom-call(s32[8,5]{1,0:T(8,128)S(1)} %bitcast.19, s32[8,5]{1,0:T(8,128)S(1)} %bitcast.21, f32[8,128]{1,0:T(8,128)S(1)} %iota.7.flags_ref, f32[4,64,128]{2,1,0:T(8,128)S(1)} %get-tuple-element.37.row_a_ref, ...), custom_call_target="tpu_custom_call" | custom-call | flops 1000000000 | tf_op jit(solution)/shard_map/pallas_call | solution.py:507
  16.4 1.5 %collective-permute-start.6 = (f32[5,32,128]{2,1,0:T(8,128)S(1)}, f32[5,32,128]{2,1,0:T(8,128)S(1)}, u32[]{:S(2)}, u32[]{:S(2)}) collective-permute-start(f32[5,32,128]{2,1,0:T(8,128)S(1)} %get-tuple-element.49.row_a_ref), channel_id=1, source_target_pairs={{0,4},{4,0},{8,12},{12,8},{1,5},{5,1},{9,13},{13,9},{2,6},{6,2},{1... | collective-permute-start | bytes 245768 | tf_op jit(solution)/shard_map/ppermute | solution.py:466
  17.9 1.5 %collective-permute-start.12 = (f32[4,32,128]{2,1,0:T(8,128)S(1)}, f32[4,32,128]{2,1,0:T(8,128)S(1)}, u32[]{:S(2)}, u32[]{:S(2)}) collective-permute-start(f32[4,32,128]{2,1,0:T(8,128)S(1)} %get-tuple-element.53.row_b_ref), channel_id=1, source_target_pairs={{0,16},{4,8},{8,4},{12,28},{16,0},{20,24},{24,20},{28,12},{1,17},{... | collective-permute-start | bytes 196616 | tf_op jit(solution)/shard_map/ppermute | solution.py:466
  19.4 0.1 collective-permute-start.10
  19.5 1.0 %collective-permute-start.11 = (f32[4,96,128]{2,1,0:T(8,128)S(1)}, f32[4,96,128]{2,1,0:T(8,128)S(1)}, u32[]{:S(2)}, u32[]{:S(2)}) collective-permute-start(f32[4,96,128]{2,1,0:T(8,128)S(1)} %get-tuple-element.51), channel_id=1, source_target_pairs={{0,16},{1,2},{2,1},{3,19},{16,0},{17,18},{18,17},{19,3},{4,20},{5,... | collective-permute-start | bytes 589832 | tf_op jit(solution)/shard_map/ppermute | solution.py:466
  20.5 0.4 collective-permute-done.6.from_row_a_ref
  20.9 2.3 %collective-permute-start.7 = (f32[32,128]{1,0:T(8,128)S(1)}, f32[32,128]{1,0:T(8,128)S(1)}, u32[]{:S(2)}, u32[]{:S(2)}) collective-permute-start(f32[32,128]{1,0:T(8,128)S(1)} %fusion.1), channel_id=1, source_target_pairs={{0,8},{1,9},{2,10},{3,11},{4,12},{5,13},{6,14},{7,15},{8,0},{9,1},... | collective-permute-start | bytes 49160 | tf_op jit(solution)/shard_map/ppermute | solution.py:454
  23.2 2.4 %collective-permute-done.7 = f32[32,128]{1,0:T(8,128)S(1)} collective-permute-done((f32[32,128]{1,0:T(8,128)S(1)}, f32[32,128]{1,0:T(8,128)S(1)}, u32[]{:S(2)}, u32[]{:S(2)}) %collective-permute-start.7) | collective-permute-done | bytes 16416 | tf_op jit(solution)/shard_map/ppermute | solution.py:454
  25.6 0.1 collective-permute-start.13
  25.7 1.1 %collective-permute-start.15 = (f32[4,32,128]{2,1,0:T(8,128)S(1)}, f32[4,32,128]{2,1,0:T(8,128)S(1)}, u32[]{:S(2)}, u32[]{:S(2)}) collective-permute-start(f32[4,32,128]{2,1,0:T(8,128)S(1)} %get-tuple-element.55), channel_id=1, source_target_pairs={{0,16},{1,2},{2,1},{3,19},{16,0},{17,18},{18,17},{19,3},{4,20},{5,... | collective-permute-start | bytes 196616 | tf_op jit(solution)/shard_map/ppermute | solution.py:466
  26.8 0.2 collective-permute-done.13.from_side_a_ref
  27.0 0.9 %collective-permute-start.14 = (f32[32,128]{1,0:T(8,128)S(1)}, f32[32,128]{1,0:T(8,128)S(1)}, u32[]{:S(2)}, u32[]{:S(2)}) collective-permute-start(f32[32,128]{1,0:T(8,128)S(1)} %fusion), channel_id=1, source_target_pairs={{0,2},{1,3},{2,0},{3,1},{4,6},{5,7},{6,4},{7,5},{8,10},{9,11},{10,... | collective-permute-start | bytes 49160 | tf_op jit(solution)/shard_map/ppermute | solution.py:454
  27.9 0.4 shard_map.99
  28.3 2.4 %collective-permute-done.14 = f32[32,128]{1,0:T(8,128)S(1)} collective-permute-done((f32[32,128]{1,0:T(8,128)S(1)}, f32[32,128]{1,0:T(8,128)S(1)}, u32[]{:S(2)}, u32[]{:S(2)}) %collective-permute-start.14) | collective-permute-done | bytes 16416 | tf_op jit(solution)/shard_map/ppermute | solution.py:454
  30.7 2.6 %shard_map.100 = (f32[4,32,128]{2,1,0:T(8,128)S(1)}, f32[4,32,128]{2,1,0:T(8,128)S(1)}, f32[32,128]{1,0:T(8,128)}, f32[48,128]{1,0:T(8,128)S(1)}, f32[48,128]{1,0:T(8,128)S(1)}) custom-call(s32[8,5]{1,0:T(8,128)S(1)} %bitcast.20, s32[8,5]{1,0:T(8,128)S(1)} %bitcast.22, f32[8,128]{1,0:T(8,128)S(1)} %iota.7.flags_ref, f32[32,128]{1,0:T(8,128)S(1)} %add.50.partial_ref, ...), custom_call_target="tpu_custom_call" | custom-call | tf_op jit(solution)/shard_map/pallas_call | solution.py:507
  33.4 0.1 collective-permute-start.16
  33.4 1.2 %collective-permute-done.16 = f32[48,128]{1,0:T(8,128)S(1)} collective-permute-done((f32[48,128]{1,0:T(8,128)S(1)}, f32[48,128]{1,0:T(8,128)S(1)}, u32[]{:S(2)}, u32[]{:S(2)}) %collective-permute-start.16) | collective-permute-done | bytes 24608 | tf_op jit(solution)/shard_map/ppermute | solution.py:454
  34.6 2.2 %collective-permute-start.17 = (f32[48,128]{1,0:T(8,128)S(1)}, f32[48,128]{1,0:T(8,128)S(1)}, u32[]{:S(2)}, u32[]{:S(2)}) collective-permute-start(f32[48,128]{1,0:T(8,128)S(1)} %add.51), channel_id=1, source_target_pairs={{0,6},{1,7},{2,4},{3,5},{4,2},{5,3},{6,0},{7,1},{8,14},{9,15},{10,... | collective-permute-start | bytes 73736 | tf_op jit(solution)/shard_map/ppermute | solution.py:454
  36.8 1.0 %collective-permute-start.18 = (f32[48,128]{1,0:T(8,128)S(1)}, f32[48,128]{1,0:T(8,128)S(1)}, u32[]{:S(2)}, u32[]{:S(2)}) collective-permute-start(f32[48,128]{1,0:T(8,128)S(1)} %add.51), channel_id=1, source_target_pairs={{0,2},{1,3},{2,0},{3,1},{4,6},{5,7},{6,4},{7,5},{8,10},{9,11},{10,... | collective-permute-start | bytes 73736 | tf_op jit(solution)/shard_map/ppermute | solution.py:454
  37.9 0.3 collective-permute-start.19
  38.1 1.2 %collective-permute-done.17 = f32[48,128]{1,0:T(8,128)S(1)} collective-permute-done((f32[48,128]{1,0:T(8,128)S(1)}, f32[48,128]{1,0:T(8,128)S(1)}, u32[]{:S(2)}, u32[]{:S(2)}) %collective-permute-start.17) | collective-permute-done | bytes 24608 | tf_op jit(solution)/shard_map/ppermute | solution.py:454
  39.4 1.3 %collective-permute-done.18 = f32[48,128]{1,0:T(8,128)S(1)} collective-permute-done((f32[48,128]{1,0:T(8,128)S(1)}, f32[48,128]{1,0:T(8,128)S(1)}, u32[]{:S(2)}, u32[]{:S(2)}) %collective-permute-start.18) | collective-permute-done | bytes 24608 | tf_op jit(solution)/shard_map/ppermute | solution.py:454
  40.7 1.0 %collective-permute-done.19 = f32[48,128]{1,0:T(8,128)S(1)} collective-permute-done((f32[48,128]{1,0:T(8,128)S(1)}, f32[48,128]{1,0:T(8,128)S(1)}, u32[]{:S(2)}, u32[]{:S(2)}) %collective-permute-start.19) | collective-permute-done | bytes 24608 | tf_op jit(solution)/shard_map/ppermute | solution.py:454
  41.7 2.6 %collective-permute-start.20 = (f32[48,128]{1,0:T(8,128)S(1)}, f32[48,128]{1,0:T(8,128)S(1)}, u32[]{:S(2)}, u32[]{:S(2)}) collective-permute-start(f32[48,128]{1,0:T(8,128)S(1)} %add_add_fusion), channel_id=1, source_target_pairs={{0,8},{1,9},{2,10},{3,11},{4,12},{5,13},{6,14},{7,15},{8,0},{9,1},... | collective-permute-start | bytes 73736 | tf_op jit(solution)/shard_map/ppermute | solution.py:454
  44.3 2.2 %collective-permute-done.20 = f32[48,128]{1,0:T(8,128)S(1)} collective-permute-done((f32[48,128]{1,0:T(8,128)S(1)}, f32[48,128]{1,0:T(8,128)S(1)}, u32[]{:S(2)}, u32[]{:S(2)}) %collective-permute-start.20) | collective-permute-done | bytes 24608 | tf_op jit(solution)/shard_map/ppermute | solution.py:454
  46.5 0.1 collective-permute-start.21
  46.6 0.9 %shard_map.101.work_ref = f32[32,64]{1,0:T(8,128)S(1)} custom-call(f32[48,128]{1,0:T(8,128)S(1)} %add.55.sums_ref), custom_call_target="tpu_custom_call" | custom-call | flops 1000000000 | tf_op jit(solution)/shard_map/pallas_call | solution.py:507
  47.5 0.3 collective-permute-done.21.other_ref
  47.8 1.2 %shard_map.102 = (f32[256,128]{1,0:T(8,128)}, f32[32,32]{1,0:T(8,128)}, f32[2,32,160]{2,1,0:T(8,128)}) custom-call(f32[8,128]{1,0:T(8,128)S(1)} %iota.7.flags_ref, f32[32,64]{1,0:T(8,128)S(1)} %shard_map.101.work_ref, f32[48,128]{1,0:T(8,128)S(1)} %add.55.sums_ref, f32[40,128]{1,0:T(8,128)S(1)} %collective-permute-done.21.other_ref, ...), custom_call_target="tpu_custom_call" | custom-call | tf_op jit(solution)/shard_map/pallas_call | solution.py:507
  (25 shorter events, 0.2 us)
Async XLA Ops:
  1.9 12.4 %copy-start.3 = (f32[8,128,128]{2,1,0:T(8,128)S(1)}, f32[8,128,128]{2,1,0:T(8,128)}, u32[]{:S(2)}) copy-start(f32[8,128,128]{2,1,0:T(8,128)} %mass_ref.3) | copy-start | bytes 1572868
  2.0 12.3 %copy-start.2 = (f32[8,128,128]{2,1,0:T(8,128)S(1)}, f32[8,128,128]{2,1,0:T(8,128)}, u32[]{:S(2)}) copy-start(f32[8,128,128]{2,1,0:T(8,128)} %stiff_ref.3) | copy-start | bytes 1572868
  2.0 5.3 %collective-permute-start.2 = (f32[2,64,128]{2,1,0:T(8,128)S(1)}, f32[2,64,128]{2,1,0:T(8,128)S(1)}, u32[]{:S(2)}, u32[]{:S(2)}) collective-permute-start(f32[2,64,128]{2,1,0:T(8,128)S(1)} %get-tuple-element.39), channel_id=1, source_target_pairs={{0,1},{1,0},{2,3},{3,2},{4,5},{5,4},{6,7},{7,6},{8,9},{9,8},{10,11... | collective-permute-start | bytes 196616 | tf_op jit(solution)/shard_map/ppermute | solution.py:466
  2.5 4.8 %collective-permute-start.3 = (f32[2,64,128]{2,1,0:T(8,128)S(1)}, f32[2,64,128]{2,1,0:T(8,128)S(1)}, u32[]{:S(2)}, u32[]{:S(2)}) collective-permute-start(f32[2,64,128]{2,1,0:T(8,128)S(1)} %get-tuple-element.43), channel_id=1, source_target_pairs={{0,16},{1,2},{2,1},{3,19},{16,0},{17,18},{18,17},{19,3},{4,20},{5,... | collective-permute-start | bytes 196616 | tf_op jit(solution)/shard_map/ppermute | solution.py:466
  5.1 9.2 %collective-permute-start = (f32[4,64,128]{2,1,0:T(8,128)S(1)}, f32[4,64,128]{2,1,0:T(8,128)S(1)}, u32[]{:S(2)}, u32[]{:S(2)}) collective-permute-start(f32[4,64,128]{2,1,0:T(8,128)S(1)} %get-tuple-element.37.row_a_ref), channel_id=1, source_target_pairs={{0,4},{4,0},{8,12},{12,8},{1,5},{5,1},{9,13},{13,9},{2,6},{6,2},{1... | collective-permute-start | bytes 393224 | tf_op jit(solution)/shard_map/ppermute | solution.py:466
  6.7 7.6 %collective-permute-start.1 = (f32[4,64,128]{2,1,0:T(8,128)S(1)}, f32[4,64,128]{2,1,0:T(8,128)S(1)}, u32[]{:S(2)}, u32[]{:S(2)}) collective-permute-start(f32[4,64,128]{2,1,0:T(8,128)S(1)} %get-tuple-element.38.row_b_ref), channel_id=1, source_target_pairs={{0,16},{4,8},{8,4},{12,28},{16,0},{20,24},{24,20},{28,12},{1,17},{... | collective-permute-start | bytes 393224 | tf_op jit(solution)/shard_map/ppermute | solution.py:466
  7.3 7.0 %copy-start.1 = (s32[5,2,4]{0,2,1:T(4,128)S(1)}, s32[5,2,4]{0,2,1:T(4,128)}, u32[]{:S(2)}) copy-start(s32[5,2,4]{0,2,1:T(4,128)} %param.9) | copy-start | bytes 484
  7.3 7.0 %copy-start = (s32[5,2,4]{0,2,1:T(4,128)S(1)}, s32[5,2,4]{0,2,1:T(4,128)}, u32[]{:S(2)}) copy-start(s32[5,2,4]{0,2,1:T(4,128)} %param.8) | copy-start | bytes 484
  7.4 5.3 %collective-permute-start.4 = (f32[2,64,128]{2,1,0:T(8,128)S(1)}, f32[2,64,128]{2,1,0:T(8,128)S(1)}, u32[]{:S(2)}, u32[]{:S(2)}) collective-permute-start(f32[2,64,128]{2,1,0:T(8,128)S(1)} %get-tuple-element.44), channel_id=1, source_target_pairs={{0,4},{4,0},{8,12},{12,8},{1,5},{5,1},{9,13},{13,9},{2,6},{6,2},{1... | collective-permute-start | bytes 196616 | tf_op jit(solution)/shard_map/ppermute | solution.py:466
  10.0 4.3 %collective-permute-start.5 = (f32[2,64,128]{2,1,0:T(8,128)S(1)}, f32[2,64,128]{2,1,0:T(8,128)S(1)}, u32[]{:S(2)}, u32[]{:S(2)}) collective-permute-start(f32[2,64,128]{2,1,0:T(8,128)S(1)} %get-tuple-element.45), channel_id=1, source_target_pairs={{0,16},{4,8},{8,4},{12,28},{16,0},{20,24},{24,20},{28,12},{1,17},{... | collective-permute-start | bytes 196616 | tf_op jit(solution)/shard_map/ppermute | solution.py:466
  11.0 8.4 %collective-permute-start.8 = (f32[4,96,128]{2,1,0:T(8,128)S(1)}, f32[4,96,128]{2,1,0:T(8,128)S(1)}, u32[]{:S(2)}, u32[]{:S(2)}) collective-permute-start(f32[4,96,128]{2,1,0:T(8,128)S(1)} %get-tuple-element.46.rest_a_ref.row_a_ref), channel_id=1, source_target_pairs={{0,4},{4,0},{8,12},{12,8},{1,5},{5,1},{9,13},{13,9},{2,6},{6,2},{1... | collective-permute-start | bytes 589832 | tf_op jit(solution)/shard_map/ppermute | solution.py:466
  12.7 6.7 %collective-permute-start.9 = (f32[4,96,128]{2,1,0:T(8,128)S(1)}, f32[4,96,128]{2,1,0:T(8,128)S(1)}, u32[]{:S(2)}, u32[]{:S(2)}) collective-permute-start(f32[4,96,128]{2,1,0:T(8,128)S(1)} %get-tuple-element.47.rest_b_ref.row_b_ref), channel_id=1, source_target_pairs={{0,16},{4,8},{8,4},{12,28},{16,0},{20,24},{24,20},{28,12},{1,17},{... | collective-permute-start | bytes 589832 | tf_op jit(solution)/shard_map/ppermute | solution.py:466
  16.4 4.5 %collective-permute-start.6 = (f32[5,32,128]{2,1,0:T(8,128)S(1)}, f32[5,32,128]{2,1,0:T(8,128)S(1)}, u32[]{:S(2)}, u32[]{:S(2)}) collective-permute-start(f32[5,32,128]{2,1,0:T(8,128)S(1)} %get-tuple-element.49.row_a_ref), channel_id=1, source_target_pairs={{0,4},{4,0},{8,12},{12,8},{1,5},{5,1},{9,13},{13,9},{2,6},{6,2},{1... | collective-permute-start | bytes 245768 | tf_op jit(solution)/shard_map/ppermute | solution.py:466
  17.9 7.7 %collective-permute-start.12 = (f32[4,32,128]{2,1,0:T(8,128)S(1)}, f32[4,32,128]{2,1,0:T(8,128)S(1)}, u32[]{:S(2)}, u32[]{:S(2)}) collective-permute-start(f32[4,32,128]{2,1,0:T(8,128)S(1)} %get-tuple-element.53.row_b_ref), channel_id=1, source_target_pairs={{0,16},{4,8},{8,4},{12,28},{16,0},{20,24},{24,20},{28,12},{1,17},{... | collective-permute-start | bytes 196616 | tf_op jit(solution)/shard_map/ppermute | solution.py:466
  19.4 6.1 %collective-permute-start.10 = (f32[4,96,128]{2,1,0:T(8,128)S(1)}, f32[4,96,128]{2,1,0:T(8,128)S(1)}, u32[]{:S(2)}, u32[]{:S(2)}) collective-permute-start(f32[4,96,128]{2,1,0:T(8,128)S(1)} %get-tuple-element.50), channel_id=1, source_target_pairs={{0,1},{1,0},{2,3},{3,2},{4,5},{5,4},{6,7},{7,6},{8,9},{9,8},{10,11... | collective-permute-start | bytes 589832 | tf_op jit(solution)/shard_map/ppermute | solution.py:466
  19.5 6.1 %collective-permute-start.11 = (f32[4,96,128]{2,1,0:T(8,128)S(1)}, f32[4,96,128]{2,1,0:T(8,128)S(1)}, u32[]{:S(2)}, u32[]{:S(2)}) collective-permute-start(f32[4,96,128]{2,1,0:T(8,128)S(1)} %get-tuple-element.51), channel_id=1, source_target_pairs={{0,16},{1,2},{2,1},{3,19},{16,0},{17,18},{18,17},{19,3},{4,20},{5,... | collective-permute-start | bytes 589832 | tf_op jit(solution)/shard_map/ppermute | solution.py:466
  20.9 4.6 %collective-permute-start.7 = (f32[32,128]{1,0:T(8,128)S(1)}, f32[32,128]{1,0:T(8,128)S(1)}, u32[]{:S(2)}, u32[]{:S(2)}) collective-permute-start(f32[32,128]{1,0:T(8,128)S(1)} %fusion.1), channel_id=1, source_target_pairs={{0,8},{1,9},{2,10},{3,11},{4,12},{5,13},{6,14},{7,15},{8,0},{9,1},... | collective-permute-start | bytes 49160 | tf_op jit(solution)/shard_map/ppermute | solution.py:454
  25.6 1.3 %collective-permute-start.13 = (f32[5,32,128]{2,1,0:T(8,128)S(1)}, f32[5,32,128]{2,1,0:T(8,128)S(1)}, u32[]{:S(2)}, u32[]{:S(2)}) collective-permute-start(f32[5,32,128]{2,1,0:T(8,128)S(1)} %get-tuple-element.54), channel_id=1, source_target_pairs={{0,1},{1,0},{2,3},{3,2},{4,5},{5,4},{6,7},{7,6},{8,9},{9,8},{10,11... | collective-permute-start | bytes 245768 | tf_op jit(solution)/shard_map/ppermute | solution.py:466
  25.7 5.0 %collective-permute-start.15 = (f32[4,32,128]{2,1,0:T(8,128)S(1)}, f32[4,32,128]{2,1,0:T(8,128)S(1)}, u32[]{:S(2)}, u32[]{:S(2)}) collective-permute-start(f32[4,32,128]{2,1,0:T(8,128)S(1)} %get-tuple-element.55), channel_id=1, source_target_pairs={{0,16},{1,2},{2,1},{3,19},{16,0},{17,18},{18,17},{19,3},{4,20},{5,... | collective-permute-start | bytes 196616 | tf_op jit(solution)/shard_map/ppermute | solution.py:466
  27.0 3.7 %collective-permute-start.14 = (f32[32,128]{1,0:T(8,128)S(1)}, f32[32,128]{1,0:T(8,128)S(1)}, u32[]{:S(2)}, u32[]{:S(2)}) collective-permute-start(f32[32,128]{1,0:T(8,128)S(1)} %fusion), channel_id=1, source_target_pairs={{0,2},{1,3},{2,0},{3,1},{4,6},{5,7},{6,4},{7,5},{8,10},{9,11},{10,... | collective-permute-start | bytes 49160 | tf_op jit(solution)/shard_map/ppermute | solution.py:454
  33.4 1.3 %collective-permute-start.16 = (f32[48,128]{1,0:T(8,128)S(1)}, f32[48,128]{1,0:T(8,128)S(1)}, u32[]{:S(2)}, u32[]{:S(2)}) collective-permute-start(f32[48,128]{1,0:T(8,128)S(1)} %get-tuple-element.63), channel_id=1, source_target_pairs={{0,1},{1,0},{2,3},{3,2},{4,5},{5,4},{6,7},{7,6},{8,9},{9,8},{10,11... | collective-permute-start | bytes 73736 | tf_op jit(solution)/shard_map/ppermute | solution.py:454
  34.6 4.7 %collective-permute-start.17 = (f32[48,128]{1,0:T(8,128)S(1)}, f32[48,128]{1,0:T(8,128)S(1)}, u32[]{:S(2)}, u32[]{:S(2)}) collective-permute-start(f32[48,128]{1,0:T(8,128)S(1)} %add.51), channel_id=1, source_target_pairs={{0,6},{1,7},{2,4},{3,5},{4,2},{5,3},{6,0},{7,1},{8,14},{9,15},{10,... | collective-permute-start | bytes 73736 | tf_op jit(solution)/shard_map/ppermute | solution.py:454
  36.8 3.8 %collective-permute-start.18 = (f32[48,128]{1,0:T(8,128)S(1)}, f32[48,128]{1,0:T(8,128)S(1)}, u32[]{:S(2)}, u32[]{:S(2)}) collective-permute-start(f32[48,128]{1,0:T(8,128)S(1)} %add.51), channel_id=1, source_target_pairs={{0,2},{1,3},{2,0},{3,1},{4,6},{5,7},{6,4},{7,5},{8,10},{9,11},{10,... | collective-permute-start | bytes 73736 | tf_op jit(solution)/shard_map/ppermute | solution.py:454
  37.9 3.8 %collective-permute-start.19 = (f32[48,128]{1,0:T(8,128)S(1)}, f32[48,128]{1,0:T(8,128)S(1)}, u32[]{:S(2)}, u32[]{:S(2)}) collective-permute-start(f32[48,128]{1,0:T(8,128)S(1)} %add.51), channel_id=1, source_target_pairs={{0,4},{1,5},{2,6},{3,7},{4,0},{5,1},{6,2},{7,3},{8,12},{9,13},{10,... | collective-permute-start | bytes 73736 | tf_op jit(solution)/shard_map/ppermute | solution.py:454
  41.7 4.8 %collective-permute-start.20 = (f32[48,128]{1,0:T(8,128)S(1)}, f32[48,128]{1,0:T(8,128)S(1)}, u32[]{:S(2)}, u32[]{:S(2)}) collective-permute-start(f32[48,128]{1,0:T(8,128)S(1)} %add_add_fusion), channel_id=1, source_target_pairs={{0,8},{1,9},{2,10},{3,11},{4,12},{5,13},{6,14},{7,15},{8,0},{9,1},... | collective-permute-start | bytes 73736 | tf_op jit(solution)/shard_map/ppermute | solution.py:454
  46.5 1.3 %collective-permute-start.21 = (f32[40,128]{1,0:T(8,128)S(1)}, f32[40,128]{1,0:T(8,128)S(1)}, u32[]{:S(2)}, u32[]{:S(2)}) collective-permute-start(f32[40,128]{1,0:T(8,128)S(1)} %slice.14), channel_id=1, source_target_pairs={{0,1},{1,0},{2,3},{3,2},{4,5},{5,4},{6,7},{7,6},{8,9},{9,8},{10,11... | collective-permute-start | bytes 61448 | tf_op jit(solution)/shard_map/ppermute | solution.py:454

commit v20 on v19

--- a/solution.py
+++ b/solution.py
@@ -248,6 +248,8 @@
     rest_b_ref,
     from_rest_a_ref,
     from_rest_b_ref,
+    rest_side_a_ref,
+    rest_side_b_ref,
     current_ref,
     stiff_ref,
     mass_ref,
@@ -256,20 +258,27 @@
     table_ref,
 ):
     count_y, rest, side = rest_a_ref.shape
+    wide = count_y + 2
     prior = rest + current_ref.shape[1]
-    odd_x = flag_at(flags_ref, 1)
+    odd_y, odd_x = flag_at(flags_ref, 0), flag_at(flags_ref, 1)
     split_tables(stiff_ref, mass_ref, table_ref, 0)
-    for j in range(count_y):
-        rests = list(pick(odd_x, from_rest_a_ref[j], from_rest_b_ref[j]))
-        rests[1:1] = pick(odd_x, rest_a_ref[j], rest_b_ref[j])
+    for j in range(wide):
+        if 0 < j < wide - 1:
+            rests = list(pick(odd_x, from_rest_a_ref[j - 1], from_rest_b_ref[j - 1]))
+            rests[1:1] = pick(odd_x, rest_a_ref[j - 1], rest_b_ref[j - 1])
+        else:
+            rests = [
+                pick(odd_y, rest_side_a_ref[i], rest_side_b_ref[i])[j // (wide - 1)]
+                for i in range(4)
+            ]
         for i in range(4):
-            tile = jnp.concatenate([rests[i], current_ref[i * (count_y + 2) + j + 1]], axis=0)
-            high, low = split(tile)
-            basis_ref[i * count_y + j, :prior, :] = high
-            basis_ref[i * count_y + j, prior:, :] = low
-            if 0 < i < 3:
-                place = (i - 1) * count_y + j
-                span = slice(place * side, (place + 1) * side)
+            place = i * wide + j
+            high, low = split(jnp.concatenate([rests[i], current_ref[place]], axis=0))
+            basis_ref[place, :prior, :] = high
+            basis_ref[place, prior:, :] = low
+            if 0 < i < 3 and 0 < j < wide - 1:
+                tile = (i - 1) * count_y + j - 1
+                span = slice(tile * side, (tile + 1) * side)
                 prior_ref[0, :, span] = high
                 prior_ref[1, :, span] = low
 
@@ -286,15 +295,11 @@
     from_row_b_ref,
     from_side_a_ref,
     from_side_b_ref,
-    rest_side_a_ref,
-    rest_side_b_ref,
-    current_ref,
     basis_ref,
     prior_ref,
     table_ref,
     weighted_low_ref,
     weighted_high_ref,
-    coupling_ref,
     sent_ref,
     kept_ref,
     ext_ref,
@@ -310,20 +315,10 @@
         copy.start()
     count_y, block, side = weighted_low_ref.shape
     wide = count_y + 2
-    rest = rest_side_a_ref.shape[1]
-    prior = rest + block
     odd_y, odd_x, in_low_y, in_high_y, in_low_x, in_high_x = (
         flag_at(flags_ref, place) for place in range(6)
     )
-    coupling = partial_ref[...] * inverse_rows
-    coupling_ref[...] = coupling
-    coupling_deep = deep(coupling)
-
-    def basis_parts(i, j):
-        if 0 < j < wide - 1:
-            return basis_ref[i * count_y + j - 1]
-        rest_tile = pick(odd_y, rest_side_a_ref[i], rest_side_b_ref[i])[j // (wide - 1)]
-        return stacked(jnp.concatenate([rest_tile, current_ref[i * wide + j]], axis=0))
+    coupling_deep = deep(partial_ref[...] * inverse_rows)
 
     for j in range(wide):
         if 0 < j < wide - 1:
@@ -335,7 +330,7 @@
                 for i in range(4)
             ]
         for i in range(4):
-            value = rows[i] - halves_sum(mul(coupling_deep, basis_parts(i, j)))
+            value = rows[i] - halves_sum(mul(coupling_deep, basis_ref[i * wide + j]))
             if i == 0:
                 value = value * in_low_x
             if i == 3:
@@ -423,12 +418,15 @@
     work_ref,
     sums_ref,
     other_ref,
+    partial_ref,
     weighted_low_ref,
     weighted_high_ref,
     new_ref,
+    coupling_ref,
     factor_ref,
     reduced_ref,
 ):
+    coupling_ref[...] = partial_ref[...] * inverse_rows
     count_y, block, _ = weighted_low_ref.shape
     prior = sums_ref.shape[1]
     tiles = 2 * count_y
@@ -584,13 +582,24 @@
     partial = total_over(partial + from_side_a[-1], 2, count_py)
     basis_parts, prior_parts, table = call(
         prepare_kernel,
-        (flags, rest_a, rest_b, from_rest_a, from_rest_b, current, stiff_tiles, mass_tiles),
-        [shape(4 * count_y, 2 * prior, side, dtype=BF16)]
+        (
+            flags,
+            rest_a,
+            rest_b,
+            from_rest_a,
+            from_rest_b,
+            rest_side_a,
+            rest_side_b,
+            current,
+            stiff_tiles,
+            mass_tiles,
+        ),
+        [shape(4 * wide, 2 * prior, side, dtype=BF16)]
         + [shape(2, prior, tiles * side, dtype=BF16)]
         + [shape(kinds, 2 * side, 2 * side, dtype=BF16)],
         cost=pl.CostEstimate(flops=10**9, bytes_accessed=0, transcendentals=0),
     )
-    weighted_low, weighted_high, coupling, sent, kept = call(
+    weighted_low, weighted_high, sent, kept = call(
         functools.partial(operators_kernel, inverse_rows),
         (
             *codes,
@@ -602,16 +611,11 @@
             from_row_b,
             from_side_a,
             from_side_b,
-            rest_side_a,
-            rest_side_b,
-            current,
             basis_parts,
             prior_parts,
             table,
         ),
-        [shape(count_y, block, side)] * 2
-        + [shape(block, prior)]
-        + [shape(block + 16, prior)] * 2,
+        [shape(count_y, block, side)] * 2 + [shape(block + 16, prior)] * 2,
         [pltpu.VMEM((4 * wide, 2 * block, 2 * side), BF16)]
         + code_scratch
         + [pltpu.VMEM((2, 4 * block, tiles * side), BF16)],
@@ -625,11 +629,12 @@
         [shape(block, 2 * block)],
         cost=pl.CostEstimate(flops=10**9, bytes_accessed=0, transcendentals=0),
     )
-    new_block, factor, reduced = call(
+    new_block, coupling, factor, reduced = call(
         functools.partial(finish_kernel, inverse_rows),
-        (flags, work, kept, other, weighted_low, weighted_high),
+        (flags, work, kept, other, partial, weighted_low, weighted_high),
         [
             shape(block * tiles, side),
+            shape(block, prior),
             shape(block, block),
             shape(2, block, prior + block),
         ],

time: 49.1 us -> 49.2 us (level)
  no operation moved by 1% of the time
where the time goes in v20:
time: 49.2 us; the launch traced here: 49.1 us
  starting transfers between devices  26.6 us (54%)
  waiting for transfers between devices  12.7 us (26%)
  Pallas kernels  7.54 us (15%)
  other arithmetic  1.27 us (3%)
  between operations  0.86 us (2%)
    ppermute x8, waiting for transfers between devices, swap(): return lax.ppermute(value, axes, pairs)  11.9 us
    ppermute x8, starting transfers between devices, swap(): return lax.ppermute(value, axes, pairs)  9.41 us
    ppermute x7, starting transfers between devices, exchange(): lax.ppermute(message_b, ('case', axis), pairs)  9.16 us
    ppermute x7, starting transfers between devices, exchange(): lax.ppermute(message_a, axis, near)  8 us
    pallas_call x10, Pallas kernels, call(): pl.pallas_call(kernel, out_shape=outputs, in_specs=specs, out_specs=[VMEM...  7.54 us
    concatenate x1, other arithmetic, shards(): vectors = jnp.concatenate([basis, previous.reshape(-1, side)], axis=0)  1.23 us
  transfers between devices with their start and end apart: 22, of which 12 were waited for; matrix products, arithmetic and copies ran while one was open for 0% of the time, Pallas kernels for 7%

profile of v20, /device:TPU:0, one launch (start us, length us, event | category | flops | bytes accessed | tf_op | source)
XLA Modules:
  0.0 49.1 jit_solution(14805222877206455016)
XLA Ops:
  0.7 1.2 %pad_maximum_fusion.vectors_ref = f32[1280,128]{1,0:T(8,128)S(1)} fusion(f32[256,128]{1,0:T(8,128)} %bitcast.24, f32[1024,128]{1,0:T(8,128)} %bitcast.23), kind=kLoop, calls=%fused_computation | loop fusion | flops 163840 | bytes 1310720 | tf_op jit(solution)/shard_map/concatenate | solution.py:493
  1.9 0.1 iota.7.flags_ref
  2.0 0.1 shard_map.93
  2.1 0.5 %collective-permute-start.2 = (f32[2,64,128]{2,1,0:T(8,128)S(1)}, f32[2,64,128]{2,1,0:T(8,128)S(1)}, u32[]{:S(2)}, u32[]{:S(2)}) collective-permute-start(f32[2,64,128]{2,1,0:T(8,128)S(1)} %get-tuple-element.39), channel_id=1, source_target_pairs={{0,1},{1,0},{2,3},{3,2},{4,5},{5,4},{6,7},{7,6},{8,9},{9,8},{10,11... | collective-permute-start | bytes 196616 | tf_op jit(solution)/shard_map/ppermute | solution.py:464
  2.6 2.6 %collective-permute-start.3 = (f32[2,64,128]{2,1,0:T(8,128)S(1)}, f32[2,64,128]{2,1,0:T(8,128)S(1)}, u32[]{:S(2)}, u32[]{:S(2)}) collective-permute-start(f32[2,64,128]{2,1,0:T(8,128)S(1)} %get-tuple-element.43), channel_id=1, source_target_pairs={{0,16},{1,2},{2,1},{3,19},{16,0},{17,18},{18,17},{19,3},{4,20},{5,... | collective-permute-start | bytes 196616 | tf_op jit(solution)/shard_map/ppermute | solution.py:464
  5.2 1.6 %collective-permute-start = (f32[4,64,128]{2,1,0:T(8,128)S(1)}, f32[4,64,128]{2,1,0:T(8,128)S(1)}, u32[]{:S(2)}, u32[]{:S(2)}) collective-permute-start(f32[4,64,128]{2,1,0:T(8,128)S(1)} %get-tuple-element.37.row_a_ref), channel_id=1, source_target_pairs={{0,4},{4,0},{8,12},{12,8},{1,5},{5,1},{9,13},{13,9},{2,6},{6,2},{1... | collective-permute-start | bytes 393224 | tf_op jit(solution)/shard_map/ppermute | solution.py:464
  6.8 0.5 %collective-permute-start.1 = (f32[4,64,128]{2,1,0:T(8,128)S(1)}, f32[4,64,128]{2,1,0:T(8,128)S(1)}, u32[]{:S(2)}, u32[]{:S(2)}) collective-permute-start(f32[4,64,128]{2,1,0:T(8,128)S(1)} %get-tuple-element.38.row_b_ref), channel_id=1, source_target_pairs={{0,16},{4,8},{8,4},{12,28},{16,0},{20,24},{24,20},{28,12},{1,17},{... | collective-permute-start | bytes 393224 | tf_op jit(solution)/shard_map/ppermute | solution.py:464
  7.3 0.1 shard_map.94
  7.3 0.0 collective-permute-done.2.side_a_ref.from_side_a_ref
  7.3 0.1 collective-permute-done.3.side_b_ref.from_side_b_ref
  7.4 2.6 %collective-permute-start.4 = (f32[2,64,128]{2,1,0:T(8,128)S(1)}, f32[2,64,128]{2,1,0:T(8,128)S(1)}, u32[]{:S(2)}, u32[]{:S(2)}) collective-permute-start(f32[2,64,128]{2,1,0:T(8,128)S(1)} %get-tuple-element.44), channel_id=1, source_target_pairs={{0,4},{4,0},{8,12},{12,8},{1,5},{5,1},{9,13},{13,9},{2,6},{6,2},{1... | collective-permute-start | bytes 196616 | tf_op jit(solution)/shard_map/ppermute | solution.py:464
  10.1 1.0 %collective-permute-start.5 = (f32[2,64,128]{2,1,0:T(8,128)S(1)}, f32[2,64,128]{2,1,0:T(8,128)S(1)}, u32[]{:S(2)}, u32[]{:S(2)}) collective-permute-start(f32[2,64,128]{2,1,0:T(8,128)S(1)} %get-tuple-element.45), channel_id=1, source_target_pairs={{0,16},{4,8},{8,4},{12,28},{16,0},{20,24},{24,20},{28,12},{1,17},{... | collective-permute-start | bytes 196616 | tf_op jit(solution)/shard_map/ppermute | solution.py:464
  11.1 1.6 %collective-permute-start.8 = (f32[4,96,128]{2,1,0:T(8,128)S(1)}, f32[4,96,128]{2,1,0:T(8,128)S(1)}, u32[]{:S(2)}, u32[]{:S(2)}) collective-permute-start(f32[4,96,128]{2,1,0:T(8,128)S(1)} %get-tuple-element.46.rest_a_ref.row_a_ref), channel_id=1, source_target_pairs={{0,4},{4,0},{8,12},{12,8},{1,5},{5,1},{9,13},{13,9},{2,6},{6,2},{1... | collective-permute-start | bytes 589832 | tf_op jit(solution)/shard_map/ppermute | solution.py:464
  12.7 0.0 collective-permute-done.4.from_corner_a_ref
  12.7 1.5 %collective-permute-start.9 = (f32[4,96,128]{2,1,0:T(8,128)S(1)}, f32[4,96,128]{2,1,0:T(8,128)S(1)}, u32[]{:S(2)}, u32[]{:S(2)}) collective-permute-start(f32[4,96,128]{2,1,0:T(8,128)S(1)} %get-tuple-element.47.rest_b_ref.row_b_ref), channel_id=1, source_target_pairs={{0,16},{4,8},{8,4},{12,28},{16,0},{20,24},{24,20},{28,12},{1,17},{... | collective-permute-start | bytes 589832 | tf_op jit(solution)/shard_map/ppermute | solution.py:464
  14.3 0.1 collective-permute-done.5.from_corner_b_ref
  14.4 2.1 %shard_map.96 = (f32[5,32,128]{2,1,0:T(8,128)S(1)}, f32[4,32,128]{2,1,0:T(8,128)S(1)}, f32[32,128]{1,0:T(8,128)S(1)}, f32[24,32,128]{2,1,0:T(8,128)S(1)}) custom-call(s32[8,5]{1,0:T(8,128)S(1)} %bitcast.19, s32[8,5]{1,0:T(8,128)S(1)} %bitcast.21, f32[8,128]{1,0:T(8,128)S(1)} %iota.7.flags_ref, f32[4,64,128]{2,1,0:T(8,128)S(1)} %get-tuple-element.37.row_a_ref, ...), custom_call_target="tpu_custom_call" | custom-call | flops 1000000000 | tf_op jit(solution)/shard_map/pallas_call | solution.py:505
  16.5 1.5 %collective-permute-start.6 = (f32[5,32,128]{2,1,0:T(8,128)S(1)}, f32[5,32,128]{2,1,0:T(8,128)S(1)}, u32[]{:S(2)}, u32[]{:S(2)}) collective-permute-start(f32[5,32,128]{2,1,0:T(8,128)S(1)} %get-tuple-element.49.row_a_ref), channel_id=1, source_target_pairs={{0,4},{4,0},{8,12},{12,8},{1,5},{5,1},{9,13},{13,9},{2,6},{6,2},{1... | collective-permute-start | bytes 245768 | tf_op jit(solution)/shard_map/ppermute | solution.py:464
  18.0 1.5 %collective-permute-start.12 = (f32[4,32,128]{2,1,0:T(8,128)S(1)}, f32[4,32,128]{2,1,0:T(8,128)S(1)}, u32[]{:S(2)}, u32[]{:S(2)}) collective-permute-start(f32[4,32,128]{2,1,0:T(8,128)S(1)} %get-tuple-element.53.row_b_ref), channel_id=1, source_target_pairs={{0,16},{4,8},{8,4},{12,28},{16,0},{20,24},{24,20},{28,12},{1,17},{... | collective-permute-start | bytes 196616 | tf_op jit(solution)/shard_map/ppermute | solution.py:464
  19.5 0.0 collective-permute-done.9.from_row_b_ref.from_rest_b_ref
  19.5 0.1 collective-permute-start.10
  19.6 1.0 %collective-permute-start.11 = (f32[4,96,128]{2,1,0:T(8,128)S(1)}, f32[4,96,128]{2,1,0:T(8,128)S(1)}, u32[]{:S(2)}, u32[]{:S(2)}) collective-permute-start(f32[4,96,128]{2,1,0:T(8,128)S(1)} %get-tuple-element.51), channel_id=1, source_target_pairs={{0,16},{1,2},{2,1},{3,19},{16,0},{17,18},{18,17},{19,3},{4,20},{5,... | collective-permute-start | bytes 589832 | tf_op jit(solution)/shard_map/ppermute | solution.py:464
  20.6 0.5 collective-permute-done.6.from_row_a_ref
  21.0 2.3 %collective-permute-start.7 = (f32[32,128]{1,0:T(8,128)S(1)}, f32[32,128]{1,0:T(8,128)S(1)}, u32[]{:S(2)}, u32[]{:S(2)}) collective-permute-start(f32[32,128]{1,0:T(8,128)S(1)} %fusion.1), channel_id=1, source_target_pairs={{0,8},{1,9},{2,10},{3,11},{4,12},{5,13},{6,14},{7,15},{8,0},{9,1},... | collective-permute-start | bytes 49160 | tf_op jit(solution)/shard_map/ppermute | solution.py:452
  23.3 2.4 %collective-permute-done.7 = f32[32,128]{1,0:T(8,128)S(1)} collective-permute-done((f32[32,128]{1,0:T(8,128)S(1)}, f32[32,128]{1,0:T(8,128)S(1)}, u32[]{:S(2)}, u32[]{:S(2)}) %collective-permute-start.7) | collective-permute-done | bytes 16416 | tf_op jit(solution)/shard_map/ppermute | solution.py:452
  25.7 0.0 collective-permute-done.11.rest_side_b_ref
  25.7 0.0 collective-permute-done.12.from_row_b_ref
  25.7 0.1 collective-permute-start.13
  25.8 1.1 %collective-permute-start.15 = (f32[4,32,128]{2,1,0:T(8,128)S(1)}, f32[4,32,128]{2,1,0:T(8,128)S(1)}, u32[]{:S(2)}, u32[]{:S(2)}) collective-permute-start(f32[4,32,128]{2,1,0:T(8,128)S(1)} %get-tuple-element.55), channel_id=1, source_target_pairs={{0,16},{1,2},{2,1},{3,19},{16,0},{17,18},{18,17},{19,3},{4,20},{5,... | collective-permute-start | bytes 196616 | tf_op jit(solution)/shard_map/ppermute | solution.py:464
  26.9 0.2 collective-permute-done.13.from_side_a_ref
  27.1 0.9 %collective-permute-start.14 = (f32[32,128]{1,0:T(8,128)S(1)}, f32[32,128]{1,0:T(8,128)S(1)}, u32[]{:S(2)}, u32[]{:S(2)}) collective-permute-start(f32[32,128]{1,0:T(8,128)S(1)} %fusion), channel_id=1, source_target_pairs={{0,2},{1,3},{2,0},{3,1},{4,6},{5,7},{6,4},{7,5},{8,10},{9,11},{10,... | collective-permute-start | bytes 49160 | tf_op jit(solution)/shard_map/ppermute | solution.py:452
  28.0 0.5 shard_map.99
  28.5 2.3 %collective-permute-done.14 = f32[32,128]{1,0:T(8,128)S(1)} collective-permute-done((f32[32,128]{1,0:T(8,128)S(1)}, f32[32,128]{1,0:T(8,128)S(1)}, u32[]{:S(2)}, u32[]{:S(2)}) %collective-permute-start.14) | collective-permute-done | bytes 16416 | tf_op jit(solution)/shard_map/ppermute | solution.py:452
  30.8 2.6 %shard_map.100 = (f32[4,32,128]{2,1,0:T(8,128)S(1)}, f32[4,32,128]{2,1,0:T(8,128)S(1)}, f32[48,128]{1,0:T(8,128)S(1)}, f32[48,128]{1,0:T(8,128)S(1)}) custom-call(s32[8,5]{1,0:T(8,128)S(1)} %bitcast.20, s32[8,5]{1,0:T(8,128)S(1)} %bitcast.22, f32[8,128]{1,0:T(8,128)S(1)} %iota.7.flags_ref, f32[32,128]{1,0:T(8,128)S(1)} %add.50.partial_ref, ...), custom_call_target="tpu_custom_call" | custom-call | tf_op jit(solution)/shard_map/pallas_call | solution.py:505
  33.5 0.1 collective-permute-start.16
  33.6 1.2 %collective-permute-done.16 = f32[48,128]{1,0:T(8,128)S(1)} collective-permute-done((f32[48,128]{1,0:T(8,128)S(1)}, f32[48,128]{1,0:T(8,128)S(1)}, u32[]{:S(2)}, u32[]{:S(2)}) %collective-permute-start.16) | collective-permute-done | bytes 24608 | tf_op jit(solution)/shard_map/ppermute | solution.py:452
  34.7 2.2 %collective-permute-start.17 = (f32[48,128]{1,0:T(8,128)S(1)}, f32[48,128]{1,0:T(8,128)S(1)}, u32[]{:S(2)}, u32[]{:S(2)}) collective-permute-start(f32[48,128]{1,0:T(8,128)S(1)} %add.51), channel_id=1, source_target_pairs={{0,6},{1,7},{2,4},{3,5},{4,2},{5,3},{6,0},{7,1},{8,14},{9,15},{10,... | collective-permute-start | bytes 73736 | tf_op jit(solution)/shard_map/ppermute | solution.py:452
  36.9 1.0 %collective-permute-start.18 = (f32[48,128]{1,0:T(8,128)S(1)}, f32[48,128]{1,0:T(8,128)S(1)}, u32[]{:S(2)}, u32[]{:S(2)}) collective-permute-start(f32[48,128]{1,0:T(8,128)S(1)} %add.51), channel_id=1, source_target_pairs={{0,2},{1,3},{2,0},{3,1},{4,6},{5,7},{6,4},{7,5},{8,10},{9,11},{10,... | collective-permute-start | bytes 73736 | tf_op jit(solution)/shard_map/ppermute | solution.py:452
  38.0 0.3 collective-permute-start.19
  38.2 1.2 %collective-permute-done.17 = f32[48,128]{1,0:T(8,128)S(1)} collective-permute-done((f32[48,128]{1,0:T(8,128)S(1)}, f32[48,128]{1,0:T(8,128)S(1)}, u32[]{:S(2)}, u32[]{:S(2)}) %collective-permute-start.17) | collective-permute-done | bytes 24608 | tf_op jit(solution)/shard_map/ppermute | solution.py:452
  39.5 1.3 %collective-permute-done.18 = f32[48,128]{1,0:T(8,128)S(1)} collective-permute-done((f32[48,128]{1,0:T(8,128)S(1)}, f32[48,128]{1,0:T(8,128)S(1)}, u32[]{:S(2)}, u32[]{:S(2)}) %collective-permute-start.18) | collective-permute-done | bytes 24608 | tf_op jit(solution)/shard_map/ppermute | solution.py:452
  40.8 1.0 %collective-permute-done.19 = f32[48,128]{1,0:T(8,128)S(1)} collective-permute-done((f32[48,128]{1,0:T(8,128)S(1)}, f32[48,128]{1,0:T(8,128)S(1)}, u32[]{:S(2)}, u32[]{:S(2)}) %collective-permute-start.19) | collective-permute-done | bytes 24608 | tf_op jit(solution)/shard_map/ppermute | solution.py:452
  41.8 2.6 %collective-permute-start.20 = (f32[48,128]{1,0:T(8,128)S(1)}, f32[48,128]{1,0:T(8,128)S(1)}, u32[]{:S(2)}, u32[]{:S(2)}) collective-permute-start(f32[48,128]{1,0:T(8,128)S(1)} %add_add_fusion), channel_id=1, source_target_pairs={{0,8},{1,9},{2,10},{3,11},{4,12},{5,13},{6,14},{7,15},{8,0},{9,1},... | collective-permute-start | bytes 73736 | tf_op jit(solution)/shard_map/ppermute | solution.py:452
  44.4 2.2 %collective-permute-done.20 = f32[48,128]{1,0:T(8,128)S(1)} collective-permute-done((f32[48,128]{1,0:T(8,128)S(1)}, f32[48,128]{1,0:T(8,128)S(1)}, u32[]{:S(2)}, u32[]{:S(2)}) %collective-permute-start.20) | collective-permute-done | bytes 24608 | tf_op jit(solution)/shard_map/ppermute | solution.py:452
  46.6 0.1 collective-permute-start.21
  46.7 0.9 %shard_map.101.work_ref = f32[32,64]{1,0:T(8,128)S(1)} custom-call(f32[48,128]{1,0:T(8,128)S(1)} %add.55.sums_ref), custom_call_target="tpu_custom_call" | custom-call | flops 1000000000 | tf_op jit(solution)/shard_map/pallas_call | solution.py:505
  47.6 0.3 collective-permute-done.21.other_ref
  47.9 1.2 %shard_map.102 = (f32[256,128]{1,0:T(8,128)}, f32[32,128]{1,0:T(8,128)}, f32[32,32]{1,0:T(8,128)}, f32[2,32,160]{2,1,0:T(8,128)}) custom-call(f32[8,128]{1,0:T(8,128)S(1)} %iota.7.flags_ref, f32[32,64]{1,0:T(8,128)S(1)} %shard_map.101.work_ref, f32[48,128]{1,0:T(8,128)S(1)} %add.55.sums_ref, f32[40,128]{1,0:T(8,128)S(1)} %collective-permute-done.21.other_ref, ...), custom_call_target="tpu_custom_call" | custom-call | tf_op jit(solution)/shard_map/pallas_call | solution.py:505
  (25 shorter events, 0.2 us)
Async XLA Ops:
  0.6 13.7 %copy-start = (s32[5,2,4]{0,2,1:T(4,128)S(1)}, s32[5,2,4]{0,2,1:T(4,128)}, u32[]{:S(2)}) copy-start(s32[5,2,4]{0,2,1:T(4,128)} %param.8) | copy-start | bytes 484
  0.6 13.7 %copy-start.1 = (s32[5,2,4]{0,2,1:T(4,128)S(1)}, s32[5,2,4]{0,2,1:T(4,128)}, u32[]{:S(2)}) copy-start(s32[5,2,4]{0,2,1:T(4,128)} %param.9) | copy-start | bytes 484
  0.7 13.7 %copy-start.2 = (f32[8,128,128]{2,1,0:T(8,128)S(1)}, f32[8,128,128]{2,1,0:T(8,128)}, u32[]{:S(2)}) copy-start(f32[8,128,128]{2,1,0:T(8,128)} %stiff_ref.3) | copy-start | bytes 1572868
  0.7 13.7 %copy-start.3 = (f32[8,128,128]{2,1,0:T(8,128)S(1)}, f32[8,128,128]{2,1,0:T(8,128)}, u32[]{:S(2)}) copy-start(f32[8,128,128]{2,1,0:T(8,128)} %mass_ref.3) | copy-start | bytes 1572868
  2.1 5.3 %collective-permute-start.2 = (f32[2,64,128]{2,1,0:T(8,128)S(1)}, f32[2,64,128]{2,1,0:T(8,128)S(1)}, u32[]{:S(2)}, u32[]{:S(2)}) collective-permute-start(f32[2,64,128]{2,1,0:T(8,128)S(1)} %get-tuple-element.39), channel_id=1, source_target_pairs={{0,1},{1,0},{2,3},{3,2},{4,5},{5,4},{6,7},{7,6},{8,9},{9,8},{10,11... | collective-permute-start | bytes 196616 | tf_op jit(solution)/shard_map/ppermute | solution.py:464
  2.6 4.8 %collective-permute-start.3 = (f32[2,64,128]{2,1,0:T(8,128)S(1)}, f32[2,64,128]{2,1,0:T(8,128)S(1)}, u32[]{:S(2)}, u32[]{:S(2)}) collective-permute-start(f32[2,64,128]{2,1,0:T(8,128)S(1)} %get-tuple-element.43), channel_id=1, source_target_pairs={{0,16},{1,2},{2,1},{3,19},{16,0},{17,18},{18,17},{19,3},{4,20},{5,... | collective-permute-start | bytes 196616 | tf_op jit(solution)/shard_map/ppermute | solution.py:464
  5.2 9.2 %collective-permute-start = (f32[4,64,128]{2,1,0:T(8,128)S(1)}, f32[4,64,128]{2,1,0:T(8,128)S(1)}, u32[]{:S(2)}, u32[]{:S(2)}) collective-permute-start(f32[4,64,128]{2,1,0:T(8,128)S(1)} %get-tuple-element.37.row_a_ref), channel_id=1, source_target_pairs={{0,4},{4,0},{8,12},{12,8},{1,5},{5,1},{9,13},{13,9},{2,6},{6,2},{1... | collective-permute-start | bytes 393224 | tf_op jit(solution)/shard_map/ppermute | solution.py:464
  6.8 7.6 %collective-permute-start.1 = (f32[4,64,128]{2,1,0:T(8,128)S(1)}, f32[4,64,128]{2,1,0:T(8,128)S(1)}, u32[]{:S(2)}, u32[]{:S(2)}) collective-permute-start(f32[4,64,128]{2,1,0:T(8,128)S(1)} %get-tuple-element.38.row_b_ref), channel_id=1, source_target_pairs={{0,16},{4,8},{8,4},{12,28},{16,0},{20,24},{24,20},{28,12},{1,17},{... | collective-permute-start | bytes 393224 | tf_op jit(solution)/shard_map/ppermute | solution.py:464
  7.4 5.3 %collective-permute-start.4 = (f32[2,64,128]{2,1,0:T(8,128)S(1)}, f32[2,64,128]{2,1,0:T(8,128)S(1)}, u32[]{:S(2)}, u32[]{:S(2)}) collective-permute-start(f32[2,64,128]{2,1,0:T(8,128)S(1)} %get-tuple-element.44), channel_id=1, source_target_pairs={{0,4},{4,0},{8,12},{12,8},{1,5},{5,1},{9,13},{13,9},{2,6},{6,2},{1... | collective-permute-start | bytes 196616 | tf_op jit(solution)/shard_map/ppermute | solution.py:464
  10.1 4.3 %collective-permute-start.5 = (f32[2,64,128]{2,1,0:T(8,128)S(1)}, f32[2,64,128]{2,1,0:T(8,128)S(1)}, u32[]{:S(2)}, u32[]{:S(2)}) collective-permute-start(f32[2,64,128]{2,1,0:T(8,128)S(1)} %get-tuple-element.45), channel_id=1, source_target_pairs={{0,16},{4,8},{8,4},{12,28},{16,0},{20,24},{24,20},{28,12},{1,17},{... | collective-permute-start | bytes 196616 | tf_op jit(solution)/shard_map/ppermute | solution.py:464
  11.1 8.4 %collective-permute-start.8 = (f32[4,96,128]{2,1,0:T(8,128)S(1)}, f32[4,96,128]{2,1,0:T(8,128)S(1)}, u32[]{:S(2)}, u32[]{:S(2)}) collective-permute-start(f32[4,96,128]{2,1,0:T(8,128)S(1)} %get-tuple-element.46.rest_a_ref.row_a_ref), channel_id=1, source_target_pairs={{0,4},{4,0},{8,12},{12,8},{1,5},{5,1},{9,13},{13,9},{2,6},{6,2},{1... | collective-permute-start | bytes 589832 | tf_op jit(solution)/shard_map/ppermute | solution.py:464
  12.7 6.7 %collective-permute-start.9 = (f32[4,96,128]{2,1,0:T(8,128)S(1)}, f32[4,96,128]{2,1,0:T(8,128)S(1)}, u32[]{:S(2)}, u32[]{:S(2)}) collective-permute-start(f32[4,96,128]{2,1,0:T(8,128)S(1)} %get-tuple-element.47.rest_b_ref.row_b_ref), channel_id=1, source_target_pairs={{0,16},{4,8},{8,4},{12,28},{16,0},{20,24},{24,20},{28,12},{1,17},{... | collective-permute-start | bytes 589832 | tf_op jit(solution)/shard_map/ppermute | solution.py:464
  16.5 4.5 %collective-permute-start.6 = (f32[5,32,128]{2,1,0:T(8,128)S(1)}, f32[5,32,128]{2,1,0:T(8,128)S(1)}, u32[]{:S(2)}, u32[]{:S(2)}) collective-permute-start(f32[5,32,128]{2,1,0:T(8,128)S(1)} %get-tuple-element.49.row_a_ref), channel_id=1, source_target_pairs={{0,4},{4,0},{8,12},{12,8},{1,5},{5,1},{9,13},{13,9},{2,6},{6,2},{1... | collective-permute-start | bytes 245768 | tf_op jit(solution)/shard_map/ppermute | solution.py:464
  18.0 7.7 %collective-permute-start.12 = (f32[4,32,128]{2,1,0:T(8,128)S(1)}, f32[4,32,128]{2,1,0:T(8,128)S(1)}, u32[]{:S(2)}, u32[]{:S(2)}) collective-permute-start(f32[4,32,128]{2,1,0:T(8,128)S(1)} %get-tuple-element.53.row_b_ref), channel_id=1, source_target_pairs={{0,16},{4,8},{8,4},{12,28},{16,0},{20,24},{24,20},{28,12},{1,17},{... | collective-permute-start | bytes 196616 | tf_op jit(solution)/shard_map/ppermute | solution.py:464
  19.5 6.1 %collective-permute-start.10 = (f32[4,96,128]{2,1,0:T(8,128)S(1)}, f32[4,96,128]{2,1,0:T(8,128)S(1)}, u32[]{:S(2)}, u32[]{:S(2)}) collective-permute-start(f32[4,96,128]{2,1,0:T(8,128)S(1)} %get-tuple-element.50), channel_id=1, source_target_pairs={{0,1},{1,0},{2,3},{3,2},{4,5},{5,4},{6,7},{7,6},{8,9},{9,8},{10,11... | collective-permute-start | bytes 589832 | tf_op jit(solution)/shard_map/ppermute | solution.py:464
  19.6 6.1 %collective-permute-start.11 = (f32[4,96,128]{2,1,0:T(8,128)S(1)}, f32[4,96,128]{2,1,0:T(8,128)S(1)}, u32[]{:S(2)}, u32[]{:S(2)}) collective-permute-start(f32[4,96,128]{2,1,0:T(8,128)S(1)} %get-tuple-element.51), channel_id=1, source_target_pairs={{0,16},{1,2},{2,1},{3,19},{16,0},{17,18},{18,17},{19,3},{4,20},{5,... | collective-permute-start | bytes 589832 | tf_op jit(solution)/shard_map/ppermute | solution.py:464
  21.0 4.6 %collective-permute-start.7 = (f32[32,128]{1,0:T(8,128)S(1)}, f32[32,128]{1,0:T(8,128)S(1)}, u32[]{:S(2)}, u32[]{:S(2)}) collective-permute-start(f32[32,128]{1,0:T(8,128)S(1)} %fusion.1), channel_id=1, source_target_pairs={{0,8},{1,9},{2,10},{3,11},{4,12},{5,13},{6,14},{7,15},{8,0},{9,1},... | collective-permute-start | bytes 49160 | tf_op jit(solution)/shard_map/ppermute | solution.py:452
  25.7 1.3 %collective-permute-start.13 = (f32[5,32,128]{2,1,0:T(8,128)S(1)}, f32[5,32,128]{2,1,0:T(8,128)S(1)}, u32[]{:S(2)}, u32[]{:S(2)}) collective-permute-start(f32[5,32,128]{2,1,0:T(8,128)S(1)} %get-tuple-element.54), channel_id=1, source_target_pairs={{0,1},{1,0},{2,3},{3,2},{4,5},{5,4},{6,7},{7,6},{8,9},{9,8},{10,11... | collective-permute-start | bytes 245768 | tf_op jit(solution)/shard_map/ppermute | solution.py:464
  25.8 5.0 %collective-permute-start.15 = (f32[4,32,128]{2,1,0:T(8,128)S(1)}, f32[4,32,128]{2,1,0:T(8,128)S(1)}, u32[]{:S(2)}, u32[]{:S(2)}) collective-permute-start(f32[4,32,128]{2,1,0:T(8,128)S(1)} %get-tuple-element.55), channel_id=1, source_target_pairs={{0,16},{1,2},{2,1},{3,19},{16,0},{17,18},{18,17},{19,3},{4,20},{5,... | collective-permute-start | bytes 196616 | tf_op jit(solution)/shard_map/ppermute | solution.py:464
  27.1 3.7 %collective-permute-start.14 = (f32[32,128]{1,0:T(8,128)S(1)}, f32[32,128]{1,0:T(8,128)S(1)}, u32[]{:S(2)}, u32[]{:S(2)}) collective-permute-start(f32[32,128]{1,0:T(8,128)S(1)} %fusion), channel_id=1, source_target_pairs={{0,2},{1,3},{2,0},{3,1},{4,6},{5,7},{6,4},{7,5},{8,10},{9,11},{10,... | collective-permute-start | bytes 49160 | tf_op jit(solution)/shard_map/ppermute | solution.py:452
  33.5 1.3 %collective-permute-start.16 = (f32[48,128]{1,0:T(8,128)S(1)}, f32[48,128]{1,0:T(8,128)S(1)}, u32[]{:S(2)}, u32[]{:S(2)}) collective-permute-start(f32[48,128]{1,0:T(8,128)S(1)} %get-tuple-element.63), channel_id=1, source_target_pairs={{0,1},{1,0},{2,3},{3,2},{4,5},{5,4},{6,7},{7,6},{8,9},{9,8},{10,11... | collective-permute-start | bytes 73736 | tf_op jit(solution)/shard_map/ppermute | solution.py:452
  34.7 4.7 %collective-permute-start.17 = (f32[48,128]{1,0:T(8,128)S(1)}, f32[48,128]{1,0:T(8,128)S(1)}, u32[]{:S(2)}, u32[]{:S(2)}) collective-permute-start(f32[48,128]{1,0:T(8,128)S(1)} %add.51), channel_id=1, source_target_pairs={{0,6},{1,7},{2,4},{3,5},{4,2},{5,3},{6,0},{7,1},{8,14},{9,15},{10,... | collective-permute-start | bytes 73736 | tf_op jit(solution)/shard_map/ppermute | solution.py:452
  36.9 3.8 %collective-permute-start.18 = (f32[48,128]{1,0:T(8,128)S(1)}, f32[48,128]{1,0:T(8,128)S(1)}, u32[]{:S(2)}, u32[]{:S(2)}) collective-permute-start(f32[48,128]{1,0:T(8,128)S(1)} %add.51), channel_id=1, source_target_pairs={{0,2},{1,3},{2,0},{3,1},{4,6},{5,7},{6,4},{7,5},{8,10},{9,11},{10,... | collective-permute-start | bytes 73736 | tf_op jit(solution)/shard_map/ppermute | solution.py:452
  38.0 3.8 %collective-permute-start.19 = (f32[48,128]{1,0:T(8,128)S(1)}, f32[48,128]{1,0:T(8,128)S(1)}, u32[]{:S(2)}, u32[]{:S(2)}) collective-permute-start(f32[48,128]{1,0:T(8,128)S(1)} %add.51), channel_id=1, source_target_pairs={{0,4},{1,5},{2,6},{3,7},{4,0},{5,1},{6,2},{7,3},{8,12},{9,13},{10,... | collective-permute-start | bytes 73736 | tf_op jit(solution)/shard_map/ppermute | solution.py:452
  41.8 4.8 %collective-permute-start.20 = (f32[48,128]{1,0:T(8,128)S(1)}, f32[48,128]{1,0:T(8,128)S(1)}, u32[]{:S(2)}, u32[]{:S(2)}) collective-permute-start(f32[48,128]{1,0:T(8,128)S(1)} %add_add_fusion), channel_id=1, source_target_pairs={{0,8},{1,9},{2,10},{3,11},{4,12},{5,13},{6,14},{7,15},{8,0},{9,1},... | collective-permute-start | bytes 73736 | tf_op jit(solution)/shard_map/ppermute | solution.py:452
  46.6 1.3 %collective-permute-start.21 = (f32[40,128]{1,0:T(8,128)S(1)}, f32[40,128]{1,0:T(8,128)S(1)}, u32[]{:S(2)}, u32[]{:S(2)}) collective-permute-start(f32[40,128]{1,0:T(8,128)S(1)} %slice.14), channel_id=1, source_target_pairs={{0,1},{1,0},{2,3},{3,2},{4,5},{5,4},{6,7},{7,6},{8,9},{9,8},{10,11... | collective-permute-start | bytes 61448 | tf_op jit(solution)/shard_map/ppermute | solution.py:452

commit v21 on v20

--- a/solution.py
+++ b/solution.py
@@ -274,8 +274,9 @@
         for i in range(4):
             place = i * wide + j
             high, low = split(jnp.concatenate([rests[i], current_ref[place]], axis=0))
-            basis_ref[place, :prior, :] = high
-            basis_ref[place, prior:, :] = low
+            columns = slice(j * side, (j + 1) * side)
+            basis_ref[i, :prior, columns] = high
+            basis_ref[i, prior:, columns] = low
             if 0 < i < 3 and 0 < j < wide - 1:
                 tile = (i - 1) * count_y + j - 1
                 span = slice(tile * side, (tile + 1) * side)
@@ -320,17 +321,16 @@
     )
     coupling_deep = deep(partial_ref[...] * inverse_rows)
 
-    for j in range(wide):
-        if 0 < j < wide - 1:
-            rows = list(pick(odd_x, from_row_a_ref[j - 1], from_row_b_ref[j - 1]))
-            rows[1:1] = pick(odd_x, row_a_ref[j - 1], row_b_ref[j - 1])
-        else:
-            rows = [
-                pick(odd_y, from_side_a_ref[i], from_side_b_ref[i])[j // (wide - 1)]
-                for i in range(4)
-            ]
-        for i in range(4):
-            value = rows[i] - halves_sum(mul(coupling_deep, basis_ref[i * wide + j]))
+    for i in range(4):
+        moved = halves_sum(mul(coupling_deep, basis_ref[i]))
+        for j in range(wide):
+            if 0 < j < wide - 1:
+                rows = list(pick(odd_x, from_row_a_ref[j - 1], from_row_b_ref[j - 1]))
+                rows[1:1] = pick(odd_x, row_a_ref[j - 1], row_b_ref[j - 1])
+                value = rows[i]
+            else:
+                value = pick(odd_y, from_side_a_ref[i], from_side_b_ref[i])[j // (wide - 1)]
+            value = value - moved[:, j * side : (j + 1) * side]
             if i == 0:
                 value = value * in_low_x
             if i == 3:
@@ -490,7 +490,9 @@
     kinds = stiff_tiles.shape[0]
     inverse_rows = 1.0 / (tiles * side * lax.axis_size("px") * lax.axis_size("py"))
     basis = prior_basis.reshape(-1, side)
-    vectors = jnp.concatenate([basis, previous.reshape(-1, side)], axis=0)
+    first = lax.optimization_barrier(jnp.int32(rest * tiles))
+    current_rows = lax.dynamic_slice_in_dim(basis, first, block * tiles, axis=0)
+    vectors = jnp.concatenate([current_rows, previous.reshape(-1, side)], axis=0)
     codes = [array.transpose(1, 2, 0).reshape(tiles, -1) for array in (neighbours, tile_kinds)]
     code_scratch = [pltpu.SMEM(array.shape, jnp.int32) for array in codes]
     code_scratch += [pltpu.SemaphoreType.DMA((2,))]
@@ -517,7 +519,7 @@
         (flags, vectors),
         [shape(count_x, 2 * block, side)] * 2 + [shape(count_y, 2 * block, side)] * 2,
     )
-    rest_a, rest_b = call(rest_kernel, (flags, vectors), [shape(count_y, rest, side)] * 2)
+    rest_a, rest_b = call(rest_kernel, (flags, basis), [shape(count_y, rest, side)] * 2)
     from_side_a, from_side_b = exchange(side_a, side_b, "py")
     from_row_a, from_row_b = exchange(row_a, row_b, "px")
     from_side_a, rest_a, rest_b = lax.optimization_barrier((from_side_a, rest_a, rest_b))
@@ -594,7 +596,7 @@
             stiff_tiles,
             mass_tiles,
         ),
-        [shape(4 * wide, 2 * prior, side, dtype=BF16)]
+        [shape(4, 2 * prior, wide * side, dtype=BF16)]
         + [shape(2, prior, tiles * side, dtype=BF16)]
         + [shape(kinds, 2 * side, 2 * side, dtype=BF16)],
         cost=pl.CostEstimate(flops=10**9, bytes_accessed=0, transcendentals=0),

time: 49.2 us -> 50.9 us (1.035)
  starting transfers between devices: 26.6 us -> 21 us
  waiting for transfers between devices: 12.7 us -> 18.1 us
  local copies, waits for them, and re-layouts: 0.09 us -> 2.14 us
    ppermute x7, waiting for transfers between devices: 0.64 us -> 3 us  [exchange(): lax.ppermute(message_a, axis, near)]
    ppermute x7, starting transfers between devices: 9.16 us -> 7.13 us  [exchange(): lax.ppermute(message_b, ('case', axis), pairs)]
    ppermute x7, waiting for transfers between devices: 0.19 us -> 2.14 us  [exchange(): lax.ppermute(message_b, ('case', axis), pairs)]
    ppermute x7, starting transfers between devices: 8 us -> 6.17 us  [exchange(): lax.ppermute(message_a, axis, near)]
    ppermute x8, starting transfers between devices: 9.41 us -> 7.72 us  [swap(): return lax.ppermute(value, axes, pairs)]
    ppermute x8, waiting for transfers between devices: 11.9 us -> 13 us  [swap(): return lax.ppermute(value, axes, pairs)]
    unnamed x8 -> x10, local copies, waits for them, and re-layouts: 0.02 us -> 1.06 us
    dynamic_slice x0 -> x1, local copies, waits for them, and re-layouts: none -> 1.01 us  [shards(): current_rows = lax.dynamic_slice_in_dim(basis, first, block * tiles, axis=0)]
  transfers between devices with their start and end apart: 22 -> 22, of which waited for: 12 -> 13; matrix products, arithmetic and copies ran while one was open for 0% -> 0% of each run, Pallas kernels for 7% -> 7%
where the time goes in v21:
time: 50.9 us; the launch traced here: 50.7 us
  starting transfers between devices  21 us (41%)
  waiting for transfers between devices  18.1 us (36%)
  Pallas kernels  7.52 us (15%)
  local copies, waits for them, and re-layouts  2.14 us (4%)
  other arithmetic  0.96 us (2%)
  between operations  0.87 us (2%)
    ppermute x8, waiting for transfers between devices, swap(): return lax.ppermute(value, axes, pairs)  13 us
    ppermute x8, starting transfers between devices, swap(): return lax.ppermute(value, axes, pairs)  7.72 us
    pallas_call x10, Pallas kernels, call(): pl.pallas_call(kernel, out_shape=outputs, in_specs=specs, out_specs=[VMEM...  7.52 us
    ppermute x7, starting transfers between devices, exchange(): lax.ppermute(message_b, ('case', axis), pairs)  7.13 us
    ppermute x7, starting transfers between devices, exchange(): lax.ppermute(message_a, axis, near)  6.17 us
    ppermute x7, waiting for transfers between devices, exchange(): lax.ppermute(message_a, axis, near)  3 us
    ppermute x7, waiting for transfers between devices, exchange(): lax.ppermute(message_b, ('case', axis), pairs)  2.14 us
    unnamed x10, local copies, waits for them, and re-layouts  1.06 us
  transfers between devices with their start and end apart: 22, of which 13 were waited for; matrix products, arithmetic and copies ran while one was open for 0% of the time, Pallas kernels for 7%

profile of v21, /device:TPU:0, one launch (start us, length us, event | category | flops | bytes accessed | tf_op | source)
XLA Modules:
  0.0 50.7 jit_solution(15336629047684341890)
XLA Ops:
  0.7 1.0 %constant_dynamic-slice_fusion = f32[256,128]{1,0:T(8,128)S(1)} fusion(f32[1024,128]{1,0:T(8,128)} %bitcast.19, s32[]{:T(128)S(6)} %select_n.3), kind=kLoop, calls=%fused_computation.7 | loop fusion | bytes 262148 | tf_op jit(solution)/shard_map/dynamic_slice | solution.py:494
  1.7 0.9 %pad_maximum_fusion.vectors_ref = f32[512,128]{1,0:T(8,128)S(1)} fusion(f32[256,128]{1,0:T(8,128)} %bitcast.25, f32[256,128]{1,0:T(8,128)S(1)} %constant_dynamic-slice_fusion), kind=kLoop, calls=%fused_computation | loop fusion | flops 65536 | bytes 524288 | tf_op jit(solution)/shard_map/concatenate | solution.py:495
  2.6 0.1 iota.7.flags_ref
  2.7 0.1 shard_map.93
  2.8 0.5 %collective-permute-start.2 = (f32[2,64,128]{2,1,0:T(8,128)S(1)}, f32[2,64,128]{2,1,0:T(8,128)S(1)}, u32[]{:S(2)}, u32[]{:S(2)}) collective-permute-start(f32[2,64,128]{2,1,0:T(8,128)S(1)} %get-tuple-element.39), channel_id=1, source_target_pairs={{0,1},{1,0},{2,3},{3,2},{4,5},{5,4},{6,7},{7,6},{8,9},{9,8},{10,11... | collective-permute-start | bytes 196616 | tf_op jit(solution)/shard_map/ppermute | solution.py:464
  3.3 2.6 %collective-permute-start.3 = (f32[2,64,128]{2,1,0:T(8,128)S(1)}, f32[2,64,128]{2,1,0:T(8,128)S(1)}, u32[]{:S(2)}, u32[]{:S(2)}) collective-permute-start(f32[2,64,128]{2,1,0:T(8,128)S(1)} %get-tuple-element.43), channel_id=1, source_target_pairs={{0,16},{1,2},{2,1},{3,19},{16,0},{17,18},{18,17},{19,3},{4,20},{5,... | collective-permute-start | bytes 196616 | tf_op jit(solution)/shard_map/ppermute | solution.py:464
  5.9 1.6 %collective-permute-start = (f32[4,64,128]{2,1,0:T(8,128)S(1)}, f32[4,64,128]{2,1,0:T(8,128)S(1)}, u32[]{:S(2)}, u32[]{:S(2)}) collective-permute-start(f32[4,64,128]{2,1,0:T(8,128)S(1)} %get-tuple-element.37.row_a_ref), channel_id=1, source_target_pairs={{0,4},{4,0},{8,12},{12,8},{1,5},{5,1},{9,13},{13,9},{2,6},{6,2},{1... | collective-permute-start | bytes 393224 | tf_op jit(solution)/shard_map/ppermute | solution.py:464
  7.5 0.5 collective-permute-start.1
  8.0 1.0 %copy-done = f32[128,2,4,128]{3,2,1,0:T(4,128)S(1)} copy-done((f32[128,2,4,128]{3,2,1,0:T(4,128)S(1)}, f32[128,2,4,128]{3,2,1,0:T(4,128)}, u32[]{:S(2)}) %copy-start) | copy-done | bytes 524312
  9.0 0.1 shard_map.94
  9.1 0.0 collective-permute-done.2.side_a_ref.from_side_a_ref
  9.1 0.0 collective-permute-done.3.side_b_ref.from_side_b_ref
  9.1 2.7 %collective-permute-start.4 = (f32[2,64,128]{2,1,0:T(8,128)S(1)}, f32[2,64,128]{2,1,0:T(8,128)S(1)}, u32[]{:S(2)}, u32[]{:S(2)}) collective-permute-start(f32[2,64,128]{2,1,0:T(8,128)S(1)} %get-tuple-element.44), channel_id=1, source_target_pairs={{0,4},{4,0},{8,12},{12,8},{1,5},{5,1},{9,13},{13,9},{2,6},{6,2},{1... | collective-permute-start | bytes 196616 | tf_op jit(solution)/shard_map/ppermute | solution.py:464
  11.8 0.5 collective-permute-start.5
  12.3 1.1 %collective-permute-start.8 = (f32[4,96,128]{2,1,0:T(8,128)S(1)}, f32[4,96,128]{2,1,0:T(8,128)S(1)}, u32[]{:S(2)}, u32[]{:S(2)}) collective-permute-start(f32[4,96,128]{2,1,0:T(8,128)S(1)} %get-tuple-element.46.rest_a_ref.row_a_ref), channel_id=1, source_target_pairs={{0,4},{4,0},{8,12},{12,8},{1,5},{5,1},{9,13},{13,9},{2,6},{6,2},{1... | collective-permute-start | bytes 589832 | tf_op jit(solution)/shard_map/ppermute | solution.py:464
  13.4 0.7 %collective-permute-done.4.from_corner_a_ref = f32[2,64,128]{2,1,0:T(8,128)S(1)} collective-permute-done((f32[2,64,128]{2,1,0:T(8,128)S(1)}, f32[2,64,128]{2,1,0:T(8,128)S(1)}, u32[]{:S(2)}, u32[]{:S(2)}) %collective-permute-start.4) | collective-permute-done | bytes 65568 | tf_op jit(solution)/shard_map/ppermute | solution.py:464
  14.1 1.0 %collective-permute-start.9 = (f32[4,96,128]{2,1,0:T(8,128)S(1)}, f32[4,96,128]{2,1,0:T(8,128)S(1)}, u32[]{:S(2)}, u32[]{:S(2)}) collective-permute-start(f32[4,96,128]{2,1,0:T(8,128)S(1)} %get-tuple-element.47.rest_b_ref.row_b_ref), channel_id=1, source_target_pairs={{0,16},{4,8},{8,4},{12,28},{16,0},{20,24},{24,20},{28,12},{1,17},{... | collective-permute-start | bytes 589832 | tf_op jit(solution)/shard_map/ppermute | solution.py:464
  15.1 1.4 %collective-permute-done.5.from_corner_b_ref = f32[2,64,128]{2,1,0:T(8,128)S(1)} collective-permute-done((f32[2,64,128]{2,1,0:T(8,128)S(1)}, f32[2,64,128]{2,1,0:T(8,128)S(1)}, u32[]{:S(2)}, u32[]{:S(2)}) %collective-permute-start.5) | collective-permute-done | bytes 65568 | tf_op jit(solution)/shard_map/ppermute | solution.py:464
  16.6 2.1 %shard_map.96 = (f32[5,32,128]{2,1,0:T(8,128)S(1)}, f32[4,32,128]{2,1,0:T(8,128)S(1)}, f32[32,128]{1,0:T(8,128)S(1)}, f32[24,32,128]{2,1,0:T(8,128)S(1)}) custom-call(s32[8,5]{1,0:T(8,128)S(1)} %bitcast.21, s32[8,5]{1,0:T(8,128)S(1)} %bitcast.23, f32[8,128]{1,0:T(8,128)S(1)} %iota.7.flags_ref, f32[4,64,128]{2,1,0:T(8,128)S(1)} %get-tuple-element.37.row_a_ref, ...), custom_call_target="tpu_custom_call" | custom-call | flops 1000000000 | tf_op jit(solution)/shard_map/pallas_call | solution.py:507
  18.7 0.1 collective-permute-start.6
  18.9 1.3 %collective-permute-start.12 = (f32[4,32,128]{2,1,0:T(8,128)S(1)}, f32[4,32,128]{2,1,0:T(8,128)S(1)}, u32[]{:S(2)}, u32[]{:S(2)}) collective-permute-start(f32[4,32,128]{2,1,0:T(8,128)S(1)} %get-tuple-element.53.row_b_ref), channel_id=1, source_target_pairs={{0,16},{4,8},{8,4},{12,28},{16,0},{20,24},{24,20},{28,12},{1,17},{... | collective-permute-start | bytes 196616 | tf_op jit(solution)/shard_map/ppermute | solution.py:464
  20.2 0.7 %collective-permute-done.9.from_row_b_ref.from_rest_b_ref = f32[4,96,128]{2,1,0:T(8,128)S(1)} collective-permute-done((f32[4,96,128]{2,1,0:T(8,128)S(1)}, f32[4,96,128]{2,1,0:T(8,128)S(1)}, u32[]{:S(2)}, u32[]{:S(2)}) %collective-permute-start.9) | collective-permute-done | bytes 196640 | tf_op jit(solution)/shard_map/ppermute | solution.py:464
  20.9 0.1 collective-permute-start.10
  21.0 1.1 %collective-permute-start.11 = (f32[4,96,128]{2,1,0:T(8,128)S(1)}, f32[4,96,128]{2,1,0:T(8,128)S(1)}, u32[]{:S(2)}, u32[]{:S(2)}) collective-permute-start(f32[4,96,128]{2,1,0:T(8,128)S(1)} %get-tuple-element.51), channel_id=1, source_target_pairs={{0,16},{1,2},{2,1},{3,19},{16,0},{17,18},{18,17},{19,3},{4,20},{5,... | collective-permute-start | bytes 589832 | tf_op jit(solution)/shard_map/ppermute | solution.py:464
  22.1 1.2 %collective-permute-done.6.from_row_a_ref = f32[5,32,128]{2,1,0:T(8,128)S(1)} collective-permute-done((f32[5,32,128]{2,1,0:T(8,128)S(1)}, f32[5,32,128]{2,1,0:T(8,128)S(1)}, u32[]{:S(2)}, u32[]{:S(2)}) %collective-permute-start.6) | collective-permute-done | bytes 81952 | tf_op jit(solution)/shard_map/ppermute | solution.py:464
  23.2 1.5 %collective-permute-start.7 = (f32[32,128]{1,0:T(8,128)S(1)}, f32[32,128]{1,0:T(8,128)S(1)}, u32[]{:S(2)}, u32[]{:S(2)}) collective-permute-start(f32[32,128]{1,0:T(8,128)S(1)} %fusion.1), channel_id=1, source_target_pairs={{0,8},{1,9},{2,10},{3,11},{4,12},{5,13},{6,14},{7,15},{8,0},{9,1},... | collective-permute-start | bytes 49160 | tf_op jit(solution)/shard_map/ppermute | solution.py:452
  24.8 3.1 %collective-permute-done.7 = f32[32,128]{1,0:T(8,128)S(1)} collective-permute-done((f32[32,128]{1,0:T(8,128)S(1)}, f32[32,128]{1,0:T(8,128)S(1)}, u32[]{:S(2)}, u32[]{:S(2)}) %collective-permute-start.7) | collective-permute-done | bytes 16416 | tf_op jit(solution)/shard_map/ppermute | solution.py:452
  27.9 0.1 collective-permute-start.13
  28.0 0.1 collective-permute-start.15
  28.1 1.2 %collective-permute-done.13.from_side_a_ref = f32[5,32,128]{2,1,0:T(8,128)S(1)} collective-permute-done((f32[5,32,128]{2,1,0:T(8,128)S(1)}, f32[5,32,128]{2,1,0:T(8,128)S(1)}, u32[]{:S(2)}, u32[]{:S(2)}) %collective-permute-start.13) | collective-permute-done | bytes 81952 | tf_op jit(solution)/shard_map/ppermute | solution.py:464
  29.3 0.9 %collective-permute-start.14 = (f32[32,128]{1,0:T(8,128)S(1)}, f32[32,128]{1,0:T(8,128)S(1)}, u32[]{:S(2)}, u32[]{:S(2)}) collective-permute-start(f32[32,128]{1,0:T(8,128)S(1)} %fusion), channel_id=1, source_target_pairs={{0,2},{1,3},{2,0},{3,1},{4,6},{5,7},{6,4},{7,5},{8,10},{9,11},{10,... | collective-permute-start | bytes 49160 | tf_op jit(solution)/shard_map/ppermute | solution.py:452
  30.2 0.5 %shard_map.99 = (bf16[4,256,768]{2,1,0:T(8,128)(2,1)S(1)}, bf16[2,128,1024]{2,1,0:T(8,128)(2,1)S(1)}, bf16[8,256,256]{2,1,0:T(8,128)(2,1)S(1)}) custom-call(f32[8,128]{1,0:T(8,128)S(1)} %iota.7.flags_ref, f32[4,96,128]{2,1,0:T(8,128)S(1)} %get-tuple-element.46.rest_a_ref.row_a_ref, f32[4,96,128]{2,1,0:T(8,128)S(1)} %get-tuple-element.47.rest_b_ref.row_b_ref, ...), custom_call_target="tpu_custom_call" | custom-call | flops 1000000000 | tf_op jit(solution)/shard_map/pallas_call | solution.py:507
  30.7 2.3 %collective-permute-done.14 = f32[32,128]{1,0:T(8,128)S(1)} collective-permute-done((f32[32,128]{1,0:T(8,128)S(1)}, f32[32,128]{1,0:T(8,128)S(1)}, u32[]{:S(2)}, u32[]{:S(2)}) %collective-permute-start.14) | collective-permute-done | bytes 16416 | tf_op jit(solution)/shard_map/ppermute | solution.py:452
  33.0 2.6 %shard_map.100 = (f32[4,32,128]{2,1,0:T(8,128)S(1)}, f32[4,32,128]{2,1,0:T(8,128)S(1)}, f32[48,128]{1,0:T(8,128)S(1)}, f32[48,128]{1,0:T(8,128)S(1)}) custom-call(s32[8,5]{1,0:T(8,128)S(1)} %bitcast.22, s32[8,5]{1,0:T(8,128)S(1)} %bitcast.24, f32[8,128]{1,0:T(8,128)S(1)} %iota.7.flags_ref, f32[32,128]{1,0:T(8,128)S(1)} %add.54.partial_ref, ...), custom_call_target="tpu_custom_call" | custom-call | tf_op jit(solution)/shard_map/pallas_call | solution.py:507
  35.6 0.1 collective-permute-start.16
  35.7 1.2 %collective-permute-done.16 = f32[48,128]{1,0:T(8,128)S(1)} collective-permute-done((f32[48,128]{1,0:T(8,128)S(1)}, f32[48,128]{1,0:T(8,128)S(1)}, u32[]{:S(2)}, u32[]{:S(2)}) %collective-permute-start.16) | collective-permute-done | bytes 24608 | tf_op jit(solution)/shard_map/ppermute | solution.py:452
  36.9 1.6 %collective-permute-start.17 = (f32[48,128]{1,0:T(8,128)S(1)}, f32[48,128]{1,0:T(8,128)S(1)}, u32[]{:S(2)}, u32[]{:S(2)}) collective-permute-start(f32[48,128]{1,0:T(8,128)S(1)} %add.55), channel_id=1, source_target_pairs={{0,6},{1,7},{2,4},{3,5},{4,2},{5,3},{6,0},{7,1},{8,14},{9,15},{10,... | collective-permute-start | bytes 73736 | tf_op jit(solution)/shard_map/ppermute | solution.py:452
  38.5 1.1 %collective-permute-start.18 = (f32[48,128]{1,0:T(8,128)S(1)}, f32[48,128]{1,0:T(8,128)S(1)}, u32[]{:S(2)}, u32[]{:S(2)}) collective-permute-start(f32[48,128]{1,0:T(8,128)S(1)} %add.55), channel_id=1, source_target_pairs={{0,2},{1,3},{2,0},{3,1},{4,6},{5,7},{6,4},{7,5},{8,10},{9,11},{10,... | collective-permute-start | bytes 73736 | tf_op jit(solution)/shard_map/ppermute | solution.py:452
  39.6 0.8 %collective-permute-start.19 = (f32[48,128]{1,0:T(8,128)S(1)}, f32[48,128]{1,0:T(8,128)S(1)}, u32[]{:S(2)}, u32[]{:S(2)}) collective-permute-start(f32[48,128]{1,0:T(8,128)S(1)} %add.55), channel_id=1, source_target_pairs={{0,4},{1,5},{2,6},{3,7},{4,0},{5,1},{6,2},{7,3},{8,12},{9,13},{10,... | collective-permute-start | bytes 73736 | tf_op jit(solution)/shard_map/ppermute | solution.py:452
  40.4 1.2 %collective-permute-done.17 = f32[48,128]{1,0:T(8,128)S(1)} collective-permute-done((f32[48,128]{1,0:T(8,128)S(1)}, f32[48,128]{1,0:T(8,128)S(1)}, u32[]{:S(2)}, u32[]{:S(2)}) %collective-permute-start.17) | collective-permute-done | bytes 24608 | tf_op jit(solution)/shard_map/ppermute | solution.py:452
  41.6 0.7 %collective-permute-done.18 = f32[48,128]{1,0:T(8,128)S(1)} collective-permute-done((f32[48,128]{1,0:T(8,128)S(1)}, f32[48,128]{1,0:T(8,128)S(1)}, u32[]{:S(2)}, u32[]{:S(2)}) %collective-permute-start.18) | collective-permute-done | bytes 24608 | tf_op jit(solution)/shard_map/ppermute | solution.py:452
  42.3 1.1 %collective-permute-done.19 = f32[48,128]{1,0:T(8,128)S(1)} collective-permute-done((f32[48,128]{1,0:T(8,128)S(1)}, f32[48,128]{1,0:T(8,128)S(1)}, u32[]{:S(2)}, u32[]{:S(2)}) %collective-permute-start.19) | collective-permute-done | bytes 24608 | tf_op jit(solution)/shard_map/ppermute | solution.py:452
  43.4 1.7 %collective-permute-start.20 = (f32[48,128]{1,0:T(8,128)S(1)}, f32[48,128]{1,0:T(8,128)S(1)}, u32[]{:S(2)}, u32[]{:S(2)}) collective-permute-start(f32[48,128]{1,0:T(8,128)S(1)} %add_add_fusion), channel_id=1, source_target_pairs={{0,8},{1,9},{2,10},{3,11},{4,12},{5,13},{6,14},{7,15},{8,0},{9,1},... | collective-permute-start | bytes 73736 | tf_op jit(solution)/shard_map/ppermute | solution.py:452
  45.1 3.1 %collective-permute-done.20 = f32[48,128]{1,0:T(8,128)S(1)} collective-permute-done((f32[48,128]{1,0:T(8,128)S(1)}, f32[48,128]{1,0:T(8,128)S(1)}, u32[]{:S(2)}, u32[]{:S(2)}) %collective-permute-start.20) | collective-permute-done | bytes 24608 | tf_op jit(solution)/shard_map/ppermute | solution.py:452
  48.2 0.1 collective-permute-start.21
  48.3 0.9 %shard_map.101.work_ref = f32[32,64]{1,0:T(8,128)S(1)} custom-call(f32[48,128]{1,0:T(8,128)S(1)} %add.59.sums_ref), custom_call_target="tpu_custom_call" | custom-call | flops 1000000000 | tf_op jit(solution)/shard_map/pallas_call | solution.py:507
  49.2 0.3 collective-permute-done.21.other_ref
  49.5 1.2 %shard_map.102 = (f32[256,128]{1,0:T(8,128)}, f32[32,128]{1,0:T(8,128)}, f32[32,32]{1,0:T(8,128)}, f32[2,32,160]{2,1,0:T(8,128)}) custom-call(f32[8,128]{1,0:T(8,128)S(1)} %iota.7.flags_ref, f32[32,64]{1,0:T(8,128)S(1)} %shard_map.101.work_ref, f32[48,128]{1,0:T(8,128)S(1)} %add.59.sums_ref, f32[40,128]{1,0:T(8,128)S(1)} %collective-permute-done.21.other_ref, ...), custom_call_target="tpu_custom_call" | custom-call | tf_op jit(solution)/shard_map/pallas_call | solution.py:507
  (28 shorter events, 0.2 us)
Async XLA Ops:
  0.6 15.9 %copy-start.1 = (s32[5,2,4]{0,2,1:T(4,128)S(1)}, s32[5,2,4]{0,2,1:T(4,128)}, u32[]{:S(2)}) copy-start(s32[5,2,4]{0,2,1:T(4,128)} %param.8) | copy-start | bytes 484
  0.6 15.9 %copy-start.2 = (s32[5,2,4]{0,2,1:T(4,128)S(1)}, s32[5,2,4]{0,2,1:T(4,128)}, u32[]{:S(2)}) copy-start(s32[5,2,4]{0,2,1:T(4,128)} %param.9) | copy-start | bytes 484
  0.7 15.9 %copy-start.3 = (f32[8,128,128]{2,1,0:T(8,128)S(1)}, f32[8,128,128]{2,1,0:T(8,128)}, u32[]{:S(2)}) copy-start(f32[8,128,128]{2,1,0:T(8,128)} %stiff_ref.3) | copy-start | bytes 1572868
  0.7 15.9 %copy-start.4 = (f32[8,128,128]{2,1,0:T(8,128)S(1)}, f32[8,128,128]{2,1,0:T(8,128)}, u32[]{:S(2)}) copy-start(f32[8,128,128]{2,1,0:T(8,128)} %mass_ref.3) | copy-start | bytes 1572868
  2.8 6.3 %collective-permute-start.2 = (f32[2,64,128]{2,1,0:T(8,128)S(1)}, f32[2,64,128]{2,1,0:T(8,128)S(1)}, u32[]{:S(2)}, u32[]{:S(2)}) collective-permute-start(f32[2,64,128]{2,1,0:T(8,128)S(1)} %get-tuple-element.39), channel_id=1, source_target_pairs={{0,1},{1,0},{2,3},{3,2},{4,5},{5,4},{6,7},{7,6},{8,9},{9,8},{10,11... | collective-permute-start | bytes 196616 | tf_op jit(solution)/shard_map/ppermute | solution.py:464
  3.3 5.8 %collective-permute-start.3 = (f32[2,64,128]{2,1,0:T(8,128)S(1)}, f32[2,64,128]{2,1,0:T(8,128)S(1)}, u32[]{:S(2)}, u32[]{:S(2)}) collective-permute-start(f32[2,64,128]{2,1,0:T(8,128)S(1)} %get-tuple-element.43), channel_id=1, source_target_pairs={{0,16},{1,2},{2,1},{3,19},{16,0},{17,18},{18,17},{19,3},{4,20},{5,... | collective-permute-start | bytes 196616 | tf_op jit(solution)/shard_map/ppermute | solution.py:464
  5.9 10.7 %collective-permute-start = (f32[4,64,128]{2,1,0:T(8,128)S(1)}, f32[4,64,128]{2,1,0:T(8,128)S(1)}, u32[]{:S(2)}, u32[]{:S(2)}) collective-permute-start(f32[4,64,128]{2,1,0:T(8,128)S(1)} %get-tuple-element.37.row_a_ref), channel_id=1, source_target_pairs={{0,4},{4,0},{8,12},{12,8},{1,5},{5,1},{9,13},{13,9},{2,6},{6,2},{1... | collective-permute-start | bytes 393224 | tf_op jit(solution)/shard_map/ppermute | solution.py:464
  7.5 9.1 %collective-permute-start.1 = (f32[4,64,128]{2,1,0:T(8,128)S(1)}, f32[4,64,128]{2,1,0:T(8,128)S(1)}, u32[]{:S(2)}, u32[]{:S(2)}) collective-permute-start(f32[4,64,128]{2,1,0:T(8,128)S(1)} %get-tuple-element.38.row_b_ref), channel_id=1, source_target_pairs={{0,16},{4,8},{8,4},{12,28},{16,0},{20,24},{24,20},{28,12},{1,17},{... | collective-permute-start | bytes 393224 | tf_op jit(solution)/shard_map/ppermute | solution.py:464
  8.0 1.0 %copy-start = (f32[128,2,4,128]{3,2,1,0:T(4,128)S(1)}, f32[128,2,4,128]{3,2,1,0:T(4,128)}, u32[]{:S(2)}) copy-start(f32[128,2,4,128]{3,2,1,0:T(4,128)} %param.6) | copy-start | bytes 1572868
  9.1 5.0 %collective-permute-start.4 = (f32[2,64,128]{2,1,0:T(8,128)S(1)}, f32[2,64,128]{2,1,0:T(8,128)S(1)}, u32[]{:S(2)}, u32[]{:S(2)}) collective-permute-start(f32[2,64,128]{2,1,0:T(8,128)S(1)} %get-tuple-element.44), channel_id=1, source_target_pairs={{0,4},{4,0},{8,12},{12,8},{1,5},{5,1},{9,13},{13,9},{2,6},{6,2},{1... | collective-permute-start | bytes 196616 | tf_op jit(solution)/shard_map/ppermute | solution.py:464
  11.8 4.7 %collective-permute-start.5 = (f32[2,64,128]{2,1,0:T(8,128)S(1)}, f32[2,64,128]{2,1,0:T(8,128)S(1)}, u32[]{:S(2)}, u32[]{:S(2)}) collective-permute-start(f32[2,64,128]{2,1,0:T(8,128)S(1)} %get-tuple-element.45), channel_id=1, source_target_pairs={{0,16},{4,8},{8,4},{12,28},{16,0},{20,24},{24,20},{28,12},{1,17},{... | collective-permute-start | bytes 196616 | tf_op jit(solution)/shard_map/ppermute | solution.py:464
  12.3 7.9 %collective-permute-start.8 = (f32[4,96,128]{2,1,0:T(8,128)S(1)}, f32[4,96,128]{2,1,0:T(8,128)S(1)}, u32[]{:S(2)}, u32[]{:S(2)}) collective-permute-start(f32[4,96,128]{2,1,0:T(8,128)S(1)} %get-tuple-element.46.rest_a_ref.row_a_ref), channel_id=1, source_target_pairs={{0,4},{4,0},{8,12},{12,8},{1,5},{5,1},{9,13},{13,9},{2,6},{6,2},{1... | collective-permute-start | bytes 589832 | tf_op jit(solution)/shard_map/ppermute | solution.py:464
  14.1 6.8 %collective-permute-start.9 = (f32[4,96,128]{2,1,0:T(8,128)S(1)}, f32[4,96,128]{2,1,0:T(8,128)S(1)}, u32[]{:S(2)}, u32[]{:S(2)}) collective-permute-start(f32[4,96,128]{2,1,0:T(8,128)S(1)} %get-tuple-element.47.rest_b_ref.row_b_ref), channel_id=1, source_target_pairs={{0,16},{4,8},{8,4},{12,28},{16,0},{20,24},{24,20},{28,12},{1,17},{... | collective-permute-start | bytes 589832 | tf_op jit(solution)/shard_map/ppermute | solution.py:464
  18.7 4.5 %collective-permute-start.6 = (f32[5,32,128]{2,1,0:T(8,128)S(1)}, f32[5,32,128]{2,1,0:T(8,128)S(1)}, u32[]{:S(2)}, u32[]{:S(2)}) collective-permute-start(f32[5,32,128]{2,1,0:T(8,128)S(1)} %get-tuple-element.49.row_a_ref), channel_id=1, source_target_pairs={{0,4},{4,0},{8,12},{12,8},{1,5},{5,1},{9,13},{13,9},{2,6},{6,2},{1... | collective-permute-start | bytes 245768 | tf_op jit(solution)/shard_map/ppermute | solution.py:464
  18.9 9.0 %collective-permute-start.12 = (f32[4,32,128]{2,1,0:T(8,128)S(1)}, f32[4,32,128]{2,1,0:T(8,128)S(1)}, u32[]{:S(2)}, u32[]{:S(2)}) collective-permute-start(f32[4,32,128]{2,1,0:T(8,128)S(1)} %get-tuple-element.53.row_b_ref), channel_id=1, source_target_pairs={{0,16},{4,8},{8,4},{12,28},{16,0},{20,24},{24,20},{28,12},{1,17},{... | collective-permute-start | bytes 196616 | tf_op jit(solution)/shard_map/ppermute | solution.py:464
  20.9 6.9 %collective-permute-start.10 = (f32[4,96,128]{2,1,0:T(8,128)S(1)}, f32[4,96,128]{2,1,0:T(8,128)S(1)}, u32[]{:S(2)}, u32[]{:S(2)}) collective-permute-start(f32[4,96,128]{2,1,0:T(8,128)S(1)} %get-tuple-element.50), channel_id=1, source_target_pairs={{0,1},{1,0},{2,3},{3,2},{4,5},{5,4},{6,7},{7,6},{8,9},{9,8},{10,11... | collective-permute-start | bytes 589832 | tf_op jit(solution)/shard_map/ppermute | solution.py:464
  21.0 6.9 %collective-permute-start.11 = (f32[4,96,128]{2,1,0:T(8,128)S(1)}, f32[4,96,128]{2,1,0:T(8,128)S(1)}, u32[]{:S(2)}, u32[]{:S(2)}) collective-permute-start(f32[4,96,128]{2,1,0:T(8,128)S(1)} %get-tuple-element.51), channel_id=1, source_target_pairs={{0,16},{1,2},{2,1},{3,19},{16,0},{17,18},{18,17},{19,3},{4,20},{5,... | collective-permute-start | bytes 589832 | tf_op jit(solution)/shard_map/ppermute | solution.py:464
  23.2 4.6 %collective-permute-start.7 = (f32[32,128]{1,0:T(8,128)S(1)}, f32[32,128]{1,0:T(8,128)S(1)}, u32[]{:S(2)}, u32[]{:S(2)}) collective-permute-start(f32[32,128]{1,0:T(8,128)S(1)} %fusion.1), channel_id=1, source_target_pairs={{0,8},{1,9},{2,10},{3,11},{4,12},{5,13},{6,14},{7,15},{8,0},{9,1},... | collective-permute-start | bytes 49160 | tf_op jit(solution)/shard_map/ppermute | solution.py:452
  27.9 1.3 %collective-permute-start.13 = (f32[5,32,128]{2,1,0:T(8,128)S(1)}, f32[5,32,128]{2,1,0:T(8,128)S(1)}, u32[]{:S(2)}, u32[]{:S(2)}) collective-permute-start(f32[5,32,128]{2,1,0:T(8,128)S(1)} %get-tuple-element.54), channel_id=1, source_target_pairs={{0,1},{1,0},{2,3},{3,2},{4,5},{5,4},{6,7},{7,6},{8,9},{9,8},{10,11... | collective-permute-start | bytes 245768 | tf_op jit(solution)/shard_map/ppermute | solution.py:464
  28.0 5.0 %collective-permute-start.15 = (f32[4,32,128]{2,1,0:T(8,128)S(1)}, f32[4,32,128]{2,1,0:T(8,128)S(1)}, u32[]{:S(2)}, u32[]{:S(2)}) collective-permute-start(f32[4,32,128]{2,1,0:T(8,128)S(1)} %get-tuple-element.55), channel_id=1, source_target_pairs={{0,16},{1,2},{2,1},{3,19},{16,0},{17,18},{18,17},{19,3},{4,20},{5,... | collective-permute-start | bytes 196616 | tf_op jit(solution)/shard_map/ppermute | solution.py:464
  29.3 3.7 %collective-permute-start.14 = (f32[32,128]{1,0:T(8,128)S(1)}, f32[32,128]{1,0:T(8,128)S(1)}, u32[]{:S(2)}, u32[]{:S(2)}) collective-permute-start(f32[32,128]{1,0:T(8,128)S(1)} %fusion), channel_id=1, source_target_pairs={{0,2},{1,3},{2,0},{3,1},{4,6},{5,7},{6,4},{7,5},{8,10},{9,11},{10,... | collective-permute-start | bytes 49160 | tf_op jit(solution)/shard_map/ppermute | solution.py:452
  35.6 1.3 %collective-permute-start.16 = (f32[48,128]{1,0:T(8,128)S(1)}, f32[48,128]{1,0:T(8,128)S(1)}, u32[]{:S(2)}, u32[]{:S(2)}) collective-permute-start(f32[48,128]{1,0:T(8,128)S(1)} %get-tuple-element.63), channel_id=1, source_target_pairs={{0,1},{1,0},{2,3},{3,2},{4,5},{5,4},{6,7},{7,6},{8,9},{9,8},{10,11... | collective-permute-start | bytes 73736 | tf_op jit(solution)/shard_map/ppermute | solution.py:452
  36.9 4.7 %collective-permute-start.17 = (f32[48,128]{1,0:T(8,128)S(1)}, f32[48,128]{1,0:T(8,128)S(1)}, u32[]{:S(2)}, u32[]{:S(2)}) collective-permute-start(f32[48,128]{1,0:T(8,128)S(1)} %add.55), channel_id=1, source_target_pairs={{0,6},{1,7},{2,4},{3,5},{4,2},{5,3},{6,0},{7,1},{8,14},{9,15},{10,... | collective-permute-start | bytes 73736 | tf_op jit(solution)/shard_map/ppermute | solution.py:452
  38.5 3.8 %collective-permute-start.18 = (f32[48,128]{1,0:T(8,128)S(1)}, f32[48,128]{1,0:T(8,128)S(1)}, u32[]{:S(2)}, u32[]{:S(2)}) collective-permute-start(f32[48,128]{1,0:T(8,128)S(1)} %add.55), channel_id=1, source_target_pairs={{0,2},{1,3},{2,0},{3,1},{4,6},{5,7},{6,4},{7,5},{8,10},{9,11},{10,... | collective-permute-start | bytes 73736 | tf_op jit(solution)/shard_map/ppermute | solution.py:452
  39.6 3.8 %collective-permute-start.19 = (f32[48,128]{1,0:T(8,128)S(1)}, f32[48,128]{1,0:T(8,128)S(1)}, u32[]{:S(2)}, u32[]{:S(2)}) collective-permute-start(f32[48,128]{1,0:T(8,128)S(1)} %add.55), channel_id=1, source_target_pairs={{0,4},{1,5},{2,6},{3,7},{4,0},{5,1},{6,2},{7,3},{8,12},{9,13},{10,... | collective-permute-start | bytes 73736 | tf_op jit(solution)/shard_map/ppermute | solution.py:452
  43.4 4.8 %collective-permute-start.20 = (f32[48,128]{1,0:T(8,128)S(1)}, f32[48,128]{1,0:T(8,128)S(1)}, u32[]{:S(2)}, u32[]{:S(2)}) collective-permute-start(f32[48,128]{1,0:T(8,128)S(1)} %add_add_fusion), channel_id=1, source_target_pairs={{0,8},{1,9},{2,10},{3,11},{4,12},{5,13},{6,14},{7,15},{8,0},{9,1},... | collective-permute-start | bytes 73736 | tf_op jit(solution)/shard_map/ppermute | solution.py:452
  48.2 1.3 %collective-permute-start.21 = (f32[40,128]{1,0:T(8,128)S(1)}, f32[40,128]{1,0:T(8,128)S(1)}, u32[]{:S(2)}, u32[]{:S(2)}) collective-permute-start(f32[40,128]{1,0:T(8,128)S(1)} %slice.14), channel_id=1, source_target_pairs={{0,1},{1,0},{2,3},{3,2},{4,5},{5,4},{6,7},{7,6},{8,9},{9,8},{10,11... | collective-permute-start | bytes 61448 | tf_op jit(solution)/shard_map/ppermute | solution.py:452

commit v22 on v21

--- a/solution.py
+++ b/solution.py
@@ -490,9 +490,7 @@
     kinds = stiff_tiles.shape[0]
     inverse_rows = 1.0 / (tiles * side * lax.axis_size("px") * lax.axis_size("py"))
     basis = prior_basis.reshape(-1, side)
-    first = lax.optimization_barrier(jnp.int32(rest * tiles))
-    current_rows = lax.dynamic_slice_in_dim(basis, first, block * tiles, axis=0)
-    vectors = jnp.concatenate([current_rows, previous.reshape(-1, side)], axis=0)
+    vectors = jnp.concatenate([basis, previous.reshape(-1, side)], axis=0)
     codes = [array.transpose(1, 2, 0).reshape(tiles, -1) for array in (neighbours, tile_kinds)]
     code_scratch = [pltpu.SMEM(array.shape, jnp.int32) for array in codes]
     code_scratch += [pltpu.SemaphoreType.DMA((2,))]
@@ -519,7 +517,7 @@
         (flags, vectors),
         [shape(count_x, 2 * block, side)] * 2 + [shape(count_y, 2 * block, side)] * 2,
     )
-    rest_a, rest_b = call(rest_kernel, (flags, basis), [shape(count_y, rest, side)] * 2)
+    rest_a, rest_b = call(rest_kernel, (flags, vectors), [shape(count_y, rest, side)] * 2)
     from_side_a, from_side_b = exchange(side_a, side_b, "py")
     from_row_a, from_row_b = exchange(row_a, row_b, "px")
     from_side_a, rest_a, rest_b = lax.optimization_barrier((from_side_a, rest_a, rest_b))

time: 50.9 us -> 49.2 us (0.967)
  starting transfers between devices: 21 us -> 26.6 us
  waiting for transfers between devices: 18.1 us -> 12.7 us
  local copies, waits for them, and re-layouts: 2.14 us -> 0.09 us
    ppermute x7, waiting for transfers between devices: 3 us -> 0.64 us  [exchange(): lax.ppermute(message_a, axis, near)]
    ppermute x7, starting transfers between devices: 7.13 us -> 9.16 us  [exchange(): lax.ppermute(message_b, ('case', axis), pairs)]
    ppermute x7, waiting for transfers between devices: 2.14 us -> 0.19 us  [exchange(): lax.ppermute(message_b, ('case', axis), pairs)]
    ppermute x7, starting transfers between devices: 6.17 us -> 8 us  [exchange(): lax.ppermute(message_a, axis, near)]
    ppermute x8, starting transfers between devices: 7.72 us -> 9.41 us  [swap(): return lax.ppermute(value, axes, pairs)]
    ppermute x8, waiting for transfers between devices: 13 us -> 11.9 us  [swap(): return lax.ppermute(value, axes, pairs)]
    unnamed x10 -> x8, local copies, waits for them, and re-layouts: 1.06 us -> 0.02 us
    dynamic_slice x1 -> x0, local copies, waits for them, and re-layouts: 1.01 us -> none  [shards(): current_rows = lax.dynamic_slice_in_dim(basis, first, block * tiles, axis=0)]
  transfers between devices with their start and end apart: 22 -> 22, of which waited for: 13 -> 12; matrix products, arithmetic and copies ran while one was open for 0% -> 0% of each run, Pallas kernels for 7% -> 7%
where the time goes in v22:
time: 49.2 us; the launch traced here: 49 us
  starting transfers between devices  26.6 us (54%)
  waiting for transfers between devices  12.7 us (26%)
  Pallas kernels  7.53 us (15%)
  other arithmetic  1.27 us (3%)
  between operations  0.86 us (2%)
    ppermute x8, waiting for transfers between devices, swap(): return lax.ppermute(value, axes, pairs)  11.9 us
    ppermute x8, starting transfers between devices, swap(): return lax.ppermute(value, axes, pairs)  9.41 us
    ppermute x7, starting transfers between devices, exchange(): lax.ppermute(message_b, ('case', axis), pairs)  9.16 us
    ppermute x7, starting transfers between devices, exchange(): lax.ppermute(message_a, axis, near)  8 us
    pallas_call x10, Pallas kernels, call(): pl.pallas_call(kernel, out_shape=outputs, in_specs=specs, out_specs=[VMEM...  7.53 us
    concatenate x1, other arithmetic, shards(): vectors = jnp.concatenate([basis, previous.reshape(-1, side)], axis=0)  1.23 us
  transfers between devices with their start and end apart: 22, of which 12 were waited for; matrix products, arithmetic and copies ran while one was open for 0% of the time, Pallas kernels for 7%

profile of v22, /device:TPU:0, one launch (start us, length us, event | category | flops | bytes accessed | tf_op | source)
XLA Modules:
  0.0 49.0 jit_solution(8088405877642660838)
XLA Ops:
  0.7 1.2 %pad_maximum_fusion.vectors_ref = f32[1280,128]{1,0:T(8,128)S(1)} fusion(f32[256,128]{1,0:T(8,128)} %bitcast.24, f32[1024,128]{1,0:T(8,128)} %bitcast.23), kind=kLoop, calls=%fused_computation | loop fusion | flops 163840 | bytes 1310720 | tf_op jit(solution)/shard_map/concatenate | solution.py:493
  1.9 0.1 iota.7.flags_ref
  2.0 0.1 shard_map.93
  2.1 0.5 %collective-permute-start.2 = (f32[2,64,128]{2,1,0:T(8,128)S(1)}, f32[2,64,128]{2,1,0:T(8,128)S(1)}, u32[]{:S(2)}, u32[]{:S(2)}) collective-permute-start(f32[2,64,128]{2,1,0:T(8,128)S(1)} %get-tuple-element.39), channel_id=1, source_target_pairs={{0,1},{1,0},{2,3},{3,2},{4,5},{5,4},{6,7},{7,6},{8,9},{9,8},{10,11... | collective-permute-start | bytes 196616 | tf_op jit(solution)/shard_map/ppermute | solution.py:464
  2.6 2.6 %collective-permute-start.3 = (f32[2,64,128]{2,1,0:T(8,128)S(1)}, f32[2,64,128]{2,1,0:T(8,128)S(1)}, u32[]{:S(2)}, u32[]{:S(2)}) collective-permute-start(f32[2,64,128]{2,1,0:T(8,128)S(1)} %get-tuple-element.43), channel_id=1, source_target_pairs={{0,16},{1,2},{2,1},{3,19},{16,0},{17,18},{18,17},{19,3},{4,20},{5,... | collective-permute-start | bytes 196616 | tf_op jit(solution)/shard_map/ppermute | solution.py:464
  5.2 1.6 %collective-permute-start = (f32[4,64,128]{2,1,0:T(8,128)S(1)}, f32[4,64,128]{2,1,0:T(8,128)S(1)}, u32[]{:S(2)}, u32[]{:S(2)}) collective-permute-start(f32[4,64,128]{2,1,0:T(8,128)S(1)} %get-tuple-element.37.row_a_ref), channel_id=1, source_target_pairs={{0,4},{4,0},{8,12},{12,8},{1,5},{5,1},{9,13},{13,9},{2,6},{6,2},{1... | collective-permute-start | bytes 393224 | tf_op jit(solution)/shard_map/ppermute | solution.py:464
  6.8 0.5 %collective-permute-start.1 = (f32[4,64,128]{2,1,0:T(8,128)S(1)}, f32[4,64,128]{2,1,0:T(8,128)S(1)}, u32[]{:S(2)}, u32[]{:S(2)}) collective-permute-start(f32[4,64,128]{2,1,0:T(8,128)S(1)} %get-tuple-element.38.row_b_ref), channel_id=1, source_target_pairs={{0,16},{4,8},{8,4},{12,28},{16,0},{20,24},{24,20},{28,12},{1,17},{... | collective-permute-start | bytes 393224 | tf_op jit(solution)/shard_map/ppermute | solution.py:464
  7.3 0.1 shard_map.94
  7.3 0.0 collective-permute-done.2.side_a_ref.from_side_a_ref
  7.3 0.1 collective-permute-done.3.side_b_ref.from_side_b_ref
  7.4 2.6 %collective-permute-start.4 = (f32[2,64,128]{2,1,0:T(8,128)S(1)}, f32[2,64,128]{2,1,0:T(8,128)S(1)}, u32[]{:S(2)}, u32[]{:S(2)}) collective-permute-start(f32[2,64,128]{2,1,0:T(8,128)S(1)} %get-tuple-element.44), channel_id=1, source_target_pairs={{0,4},{4,0},{8,12},{12,8},{1,5},{5,1},{9,13},{13,9},{2,6},{6,2},{1... | collective-permute-start | bytes 196616 | tf_op jit(solution)/shard_map/ppermute | solution.py:464
  10.1 1.0 %collective-permute-start.5 = (f32[2,64,128]{2,1,0:T(8,128)S(1)}, f32[2,64,128]{2,1,0:T(8,128)S(1)}, u32[]{:S(2)}, u32[]{:S(2)}) collective-permute-start(f32[2,64,128]{2,1,0:T(8,128)S(1)} %get-tuple-element.45), channel_id=1, source_target_pairs={{0,16},{4,8},{8,4},{12,28},{16,0},{20,24},{24,20},{28,12},{1,17},{... | collective-permute-start | bytes 196616 | tf_op jit(solution)/shard_map/ppermute | solution.py:464
  11.1 1.6 %collective-permute-start.8 = (f32[4,96,128]{2,1,0:T(8,128)S(1)}, f32[4,96,128]{2,1,0:T(8,128)S(1)}, u32[]{:S(2)}, u32[]{:S(2)}) collective-permute-start(f32[4,96,128]{2,1,0:T(8,128)S(1)} %get-tuple-element.46.rest_a_ref.row_a_ref), channel_id=1, source_target_pairs={{0,4},{4,0},{8,12},{12,8},{1,5},{5,1},{9,13},{13,9},{2,6},{6,2},{1... | collective-permute-start | bytes 589832 | tf_op jit(solution)/shard_map/ppermute | solution.py:464
  12.7 0.0 collective-permute-done.4.from_corner_a_ref
  12.7 1.5 %collective-permute-start.9 = (f32[4,96,128]{2,1,0:T(8,128)S(1)}, f32[4,96,128]{2,1,0:T(8,128)S(1)}, u32[]{:S(2)}, u32[]{:S(2)}) collective-permute-start(f32[4,96,128]{2,1,0:T(8,128)S(1)} %get-tuple-element.47.rest_b_ref.row_b_ref), channel_id=1, source_target_pairs={{0,16},{4,8},{8,4},{12,28},{16,0},{20,24},{24,20},{28,12},{1,17},{... | collective-permute-start | bytes 589832 | tf_op jit(solution)/shard_map/ppermute | solution.py:464
  14.3 0.1 collective-permute-done.5.from_corner_b_ref
  14.4 2.1 %shard_map.96 = (f32[5,32,128]{2,1,0:T(8,128)S(1)}, f32[4,32,128]{2,1,0:T(8,128)S(1)}, f32[32,128]{1,0:T(8,128)S(1)}, f32[24,32,128]{2,1,0:T(8,128)S(1)}) custom-call(s32[8,5]{1,0:T(8,128)S(1)} %bitcast.19, s32[8,5]{1,0:T(8,128)S(1)} %bitcast.21, f32[8,128]{1,0:T(8,128)S(1)} %iota.7.flags_ref, f32[4,64,128]{2,1,0:T(8,128)S(1)} %get-tuple-element.37.row_a_ref, ...), custom_call_target="tpu_custom_call" | custom-call | flops 1000000000 | tf_op jit(solution)/shard_map/pallas_call | solution.py:505
  16.5 1.5 %collective-permute-start.6 = (f32[5,32,128]{2,1,0:T(8,128)S(1)}, f32[5,32,128]{2,1,0:T(8,128)S(1)}, u32[]{:S(2)}, u32[]{:S(2)}) collective-permute-start(f32[5,32,128]{2,1,0:T(8,128)S(1)} %get-tuple-element.49.row_a_ref), channel_id=1, source_target_pairs={{0,4},{4,0},{8,12},{12,8},{1,5},{5,1},{9,13},{13,9},{2,6},{6,2},{1... | collective-permute-start | bytes 245768 | tf_op jit(solution)/shard_map/ppermute | solution.py:464
  18.0 1.5 %collective-permute-start.12 = (f32[4,32,128]{2,1,0:T(8,128)S(1)}, f32[4,32,128]{2,1,0:T(8,128)S(1)}, u32[]{:S(2)}, u32[]{:S(2)}) collective-permute-start(f32[4,32,128]{2,1,0:T(8,128)S(1)} %get-tuple-element.53.row_b_ref), channel_id=1, source_target_pairs={{0,16},{4,8},{8,4},{12,28},{16,0},{20,24},{24,20},{28,12},{1,17},{... | collective-permute-start | bytes 196616 | tf_op jit(solution)/shard_map/ppermute | solution.py:464
  19.5 0.0 collective-permute-done.9.from_row_b_ref.from_rest_b_ref
  19.5 0.1 collective-permute-start.10
  19.6 1.0 %collective-permute-start.11 = (f32[4,96,128]{2,1,0:T(8,128)S(1)}, f32[4,96,128]{2,1,0:T(8,128)S(1)}, u32[]{:S(2)}, u32[]{:S(2)}) collective-permute-start(f32[4,96,128]{2,1,0:T(8,128)S(1)} %get-tuple-element.51), channel_id=1, source_target_pairs={{0,16},{1,2},{2,1},{3,19},{16,0},{17,18},{18,17},{19,3},{4,20},{5,... | collective-permute-start | bytes 589832 | tf_op jit(solution)/shard_map/ppermute | solution.py:464
  20.6 0.5 collective-permute-done.6.from_row_a_ref
  21.0 2.3 %collective-permute-start.7 = (f32[32,128]{1,0:T(8,128)S(1)}, f32[32,128]{1,0:T(8,128)S(1)}, u32[]{:S(2)}, u32[]{:S(2)}) collective-permute-start(f32[32,128]{1,0:T(8,128)S(1)} %fusion.1), channel_id=1, source_target_pairs={{0,8},{1,9},{2,10},{3,11},{4,12},{5,13},{6,14},{7,15},{8,0},{9,1},... | collective-permute-start | bytes 49160 | tf_op jit(solution)/shard_map/ppermute | solution.py:452
  23.3 2.4 %collective-permute-done.7 = f32[32,128]{1,0:T(8,128)S(1)} collective-permute-done((f32[32,128]{1,0:T(8,128)S(1)}, f32[32,128]{1,0:T(8,128)S(1)}, u32[]{:S(2)}, u32[]{:S(2)}) %collective-permute-start.7) | collective-permute-done | bytes 16416 | tf_op jit(solution)/shard_map/ppermute | solution.py:452
  25.7 0.0 collective-permute-done.11.rest_side_b_ref
  25.7 0.0 collective-permute-done.12.from_row_b_ref
  25.7 0.1 collective-permute-start.13
  25.8 1.1 %collective-permute-start.15 = (f32[4,32,128]{2,1,0:T(8,128)S(1)}, f32[4,32,128]{2,1,0:T(8,128)S(1)}, u32[]{:S(2)}, u32[]{:S(2)}) collective-permute-start(f32[4,32,128]{2,1,0:T(8,128)S(1)} %get-tuple-element.55), channel_id=1, source_target_pairs={{0,16},{1,2},{2,1},{3,19},{16,0},{17,18},{18,17},{19,3},{4,20},{5,... | collective-permute-start | bytes 196616 | tf_op jit(solution)/shard_map/ppermute | solution.py:464
  26.9 0.2 collective-permute-done.13.from_side_a_ref
  27.1 0.9 %collective-permute-start.14 = (f32[32,128]{1,0:T(8,128)S(1)}, f32[32,128]{1,0:T(8,128)S(1)}, u32[]{:S(2)}, u32[]{:S(2)}) collective-permute-start(f32[32,128]{1,0:T(8,128)S(1)} %fusion), channel_id=1, source_target_pairs={{0,2},{1,3},{2,0},{3,1},{4,6},{5,7},{6,4},{7,5},{8,10},{9,11},{10,... | collective-permute-start | bytes 49160 | tf_op jit(solution)/shard_map/ppermute | solution.py:452
  28.0 0.5 %shard_map.99 = (bf16[4,256,768]{2,1,0:T(8,128)(2,1)S(1)}, bf16[2,128,1024]{2,1,0:T(8,128)(2,1)S(1)}, bf16[8,256,256]{2,1,0:T(8,128)(2,1)S(1)}) custom-call(f32[8,128]{1,0:T(8,128)S(1)} %iota.7.flags_ref, f32[4,96,128]{2,1,0:T(8,128)S(1)} %get-tuple-element.46.rest_a_ref.row_a_ref, f32[4,96,128]{2,1,0:T(8,128)S(1)} %get-tuple-element.47.rest_b_ref.row_b_ref, ...), custom_call_target="tpu_custom_call" | custom-call | flops 1000000000 | tf_op jit(solution)/shard_map/pallas_call | solution.py:505
  28.5 2.3 %collective-permute-done.14 = f32[32,128]{1,0:T(8,128)S(1)} collective-permute-done((f32[32,128]{1,0:T(8,128)S(1)}, f32[32,128]{1,0:T(8,128)S(1)}, u32[]{:S(2)}, u32[]{:S(2)}) %collective-permute-start.14) | collective-permute-done | bytes 16416 | tf_op jit(solution)/shard_map/ppermute | solution.py:452
  30.8 2.6 %shard_map.100 = (f32[4,32,128]{2,1,0:T(8,128)S(1)}, f32[4,32,128]{2,1,0:T(8,128)S(1)}, f32[48,128]{1,0:T(8,128)S(1)}, f32[48,128]{1,0:T(8,128)S(1)}) custom-call(s32[8,5]{1,0:T(8,128)S(1)} %bitcast.20, s32[8,5]{1,0:T(8,128)S(1)} %bitcast.22, f32[8,128]{1,0:T(8,128)S(1)} %iota.7.flags_ref, f32[32,128]{1,0:T(8,128)S(1)} %add.50.partial_ref, ...), custom_call_target="tpu_custom_call" | custom-call | tf_op jit(solution)/shard_map/pallas_call | solution.py:505
  33.4 0.1 collective-permute-start.16
  33.5 1.2 %collective-permute-done.16 = f32[48,128]{1,0:T(8,128)S(1)} collective-permute-done((f32[48,128]{1,0:T(8,128)S(1)}, f32[48,128]{1,0:T(8,128)S(1)}, u32[]{:S(2)}, u32[]{:S(2)}) %collective-permute-start.16) | collective-permute-done | bytes 24608 | tf_op jit(solution)/shard_map/ppermute | solution.py:452
  34.7 2.2 %collective-permute-start.17 = (f32[48,128]{1,0:T(8,128)S(1)}, f32[48,128]{1,0:T(8,128)S(1)}, u32[]{:S(2)}, u32[]{:S(2)}) collective-permute-start(f32[48,128]{1,0:T(8,128)S(1)} %add.51), channel_id=1, source_target_pairs={{0,6},{1,7},{2,4},{3,5},{4,2},{5,3},{6,0},{7,1},{8,14},{9,15},{10,... | collective-permute-start | bytes 73736 | tf_op jit(solution)/shard_map/ppermute | solution.py:452
  36.9 1.0 %collective-permute-start.18 = (f32[48,128]{1,0:T(8,128)S(1)}, f32[48,128]{1,0:T(8,128)S(1)}, u32[]{:S(2)}, u32[]{:S(2)}) collective-permute-start(f32[48,128]{1,0:T(8,128)S(1)} %add.51), channel_id=1, source_target_pairs={{0,2},{1,3},{2,0},{3,1},{4,6},{5,7},{6,4},{7,5},{8,10},{9,11},{10,... | collective-permute-start | bytes 73736 | tf_op jit(solution)/shard_map/ppermute | solution.py:452
  37.9 0.3 collective-permute-start.19
  38.2 1.2 %collective-permute-done.17 = f32[48,128]{1,0:T(8,128)S(1)} collective-permute-done((f32[48,128]{1,0:T(8,128)S(1)}, f32[48,128]{1,0:T(8,128)S(1)}, u32[]{:S(2)}, u32[]{:S(2)}) %collective-permute-start.17) | collective-permute-done | bytes 24608 | tf_op jit(solution)/shard_map/ppermute | solution.py:452
  39.4 1.3 %collective-permute-done.18 = f32[48,128]{1,0:T(8,128)S(1)} collective-permute-done((f32[48,128]{1,0:T(8,128)S(1)}, f32[48,128]{1,0:T(8,128)S(1)}, u32[]{:S(2)}, u32[]{:S(2)}) %collective-permute-start.18) | collective-permute-done | bytes 24608 | tf_op jit(solution)/shard_map/ppermute | solution.py:452
  40.7 1.0 %collective-permute-done.19 = f32[48,128]{1,0:T(8,128)S(1)} collective-permute-done((f32[48,128]{1,0:T(8,128)S(1)}, f32[48,128]{1,0:T(8,128)S(1)}, u32[]{:S(2)}, u32[]{:S(2)}) %collective-permute-start.19) | collective-permute-done | bytes 24608 | tf_op jit(solution)/shard_map/ppermute | solution.py:452
  41.8 2.6 %collective-permute-start.20 = (f32[48,128]{1,0:T(8,128)S(1)}, f32[48,128]{1,0:T(8,128)S(1)}, u32[]{:S(2)}, u32[]{:S(2)}) collective-permute-start(f32[48,128]{1,0:T(8,128)S(1)} %add_add_fusion), channel_id=1, source_target_pairs={{0,8},{1,9},{2,10},{3,11},{4,12},{5,13},{6,14},{7,15},{8,0},{9,1},... | collective-permute-start | bytes 73736 | tf_op jit(solution)/shard_map/ppermute | solution.py:452
  44.4 2.2 %collective-permute-done.20 = f32[48,128]{1,0:T(8,128)S(1)} collective-permute-done((f32[48,128]{1,0:T(8,128)S(1)}, f32[48,128]{1,0:T(8,128)S(1)}, u32[]{:S(2)}, u32[]{:S(2)}) %collective-permute-start.20) | collective-permute-done | bytes 24608 | tf_op jit(solution)/shard_map/ppermute | solution.py:452
  46.6 0.1 collective-permute-start.21
  46.6 0.9 %shard_map.101.work_ref = f32[32,64]{1,0:T(8,128)S(1)} custom-call(f32[48,128]{1,0:T(8,128)S(1)} %add.55.sums_ref), custom_call_target="tpu_custom_call" | custom-call | flops 1000000000 | tf_op jit(solution)/shard_map/pallas_call | solution.py:505
  47.5 0.3 collective-permute-done.21.other_ref
  47.8 1.2 %shard_map.102 = (f32[256,128]{1,0:T(8,128)}, f32[32,128]{1,0:T(8,128)}, f32[32,32]{1,0:T(8,128)}, f32[2,32,160]{2,1,0:T(8,128)}) custom-call(f32[8,128]{1,0:T(8,128)S(1)} %iota.7.flags_ref, f32[32,64]{1,0:T(8,128)S(1)} %shard_map.101.work_ref, f32[48,128]{1,0:T(8,128)S(1)} %add.55.sums_ref, f32[40,128]{1,0:T(8,128)S(1)} %collective-permute-done.21.other_ref, ...), custom_call_target="tpu_custom_call" | custom-call | tf_op jit(solution)/shard_map/pallas_call | solution.py:505
  (25 shorter events, 0.2 us)
Async XLA Ops:
  0.6 13.7 %copy-start = (s32[5,2,4]{0,2,1:T(4,128)S(1)}, s32[5,2,4]{0,2,1:T(4,128)}, u32[]{:S(2)}) copy-start(s32[5,2,4]{0,2,1:T(4,128)} %param.8) | copy-start | bytes 484
  0.6 13.7 %copy-start.1 = (s32[5,2,4]{0,2,1:T(4,128)S(1)}, s32[5,2,4]{0,2,1:T(4,128)}, u32[]{:S(2)}) copy-start(s32[5,2,4]{0,2,1:T(4,128)} %param.9) | copy-start | bytes 484
  0.7 13.7 %copy-start.2 = (f32[8,128,128]{2,1,0:T(8,128)S(1)}, f32[8,128,128]{2,1,0:T(8,128)}, u32[]{:S(2)}) copy-start(f32[8,128,128]{2,1,0:T(8,128)} %stiff_ref.3) | copy-start | bytes 1572868
  0.7 13.7 %copy-start.3 = (f32[8,128,128]{2,1,0:T(8,128)S(1)}, f32[8,128,128]{2,1,0:T(8,128)}, u32[]{:S(2)}) copy-start(f32[8,128,128]{2,1,0:T(8,128)} %mass_ref.3) | copy-start | bytes 1572868
  2.1 5.3 %collective-permute-start.2 = (f32[2,64,128]{2,1,0:T(8,128)S(1)}, f32[2,64,128]{2,1,0:T(8,128)S(1)}, u32[]{:S(2)}, u32[]{:S(2)}) collective-permute-start(f32[2,64,128]{2,1,0:T(8,128)S(1)} %get-tuple-element.39), channel_id=1, source_target_pairs={{0,1},{1,0},{2,3},{3,2},{4,5},{5,4},{6,7},{7,6},{8,9},{9,8},{10,11... | collective-permute-start | bytes 196616 | tf_op jit(solution)/shard_map/ppermute | solution.py:464
  2.6 4.8 %collective-permute-start.3 = (f32[2,64,128]{2,1,0:T(8,128)S(1)}, f32[2,64,128]{2,1,0:T(8,128)S(1)}, u32[]{:S(2)}, u32[]{:S(2)}) collective-permute-start(f32[2,64,128]{2,1,0:T(8,128)S(1)} %get-tuple-element.43), channel_id=1, source_target_pairs={{0,16},{1,2},{2,1},{3,19},{16,0},{17,18},{18,17},{19,3},{4,20},{5,... | collective-permute-start | bytes 196616 | tf_op jit(solution)/shard_map/ppermute | solution.py:464
  5.2 9.2 %collective-permute-start = (f32[4,64,128]{2,1,0:T(8,128)S(1)}, f32[4,64,128]{2,1,0:T(8,128)S(1)}, u32[]{:S(2)}, u32[]{:S(2)}) collective-permute-start(f32[4,64,128]{2,1,0:T(8,128)S(1)} %get-tuple-element.37.row_a_ref), channel_id=1, source_target_pairs={{0,4},{4,0},{8,12},{12,8},{1,5},{5,1},{9,13},{13,9},{2,6},{6,2},{1... | collective-permute-start | bytes 393224 | tf_op jit(solution)/shard_map/ppermute | solution.py:464
  6.8 7.6 %collective-permute-start.1 = (f32[4,64,128]{2,1,0:T(8,128)S(1)}, f32[4,64,128]{2,1,0:T(8,128)S(1)}, u32[]{:S(2)}, u32[]{:S(2)}) collective-permute-start(f32[4,64,128]{2,1,0:T(8,128)S(1)} %get-tuple-element.38.row_b_ref), channel_id=1, source_target_pairs={{0,16},{4,8},{8,4},{12,28},{16,0},{20,24},{24,20},{28,12},{1,17},{... | collective-permute-start | bytes 393224 | tf_op jit(solution)/shard_map/ppermute | solution.py:464
  7.4 5.3 %collective-permute-start.4 = (f32[2,64,128]{2,1,0:T(8,128)S(1)}, f32[2,64,128]{2,1,0:T(8,128)S(1)}, u32[]{:S(2)}, u32[]{:S(2)}) collective-permute-start(f32[2,64,128]{2,1,0:T(8,128)S(1)} %get-tuple-element.44), channel_id=1, source_target_pairs={{0,4},{4,0},{8,12},{12,8},{1,5},{5,1},{9,13},{13,9},{2,6},{6,2},{1... | collective-permute-start | bytes 196616 | tf_op jit(solution)/shard_map/ppermute | solution.py:464
  10.1 4.3 %collective-permute-start.5 = (f32[2,64,128]{2,1,0:T(8,128)S(1)}, f32[2,64,128]{2,1,0:T(8,128)S(1)}, u32[]{:S(2)}, u32[]{:S(2)}) collective-permute-start(f32[2,64,128]{2,1,0:T(8,128)S(1)} %get-tuple-element.45), channel_id=1, source_target_pairs={{0,16},{4,8},{8,4},{12,28},{16,0},{20,24},{24,20},{28,12},{1,17},{... | collective-permute-start | bytes 196616 | tf_op jit(solution)/shard_map/ppermute | solution.py:464
  11.1 8.4 %collective-permute-start.8 = (f32[4,96,128]{2,1,0:T(8,128)S(1)}, f32[4,96,128]{2,1,0:T(8,128)S(1)}, u32[]{:S(2)}, u32[]{:S(2)}) collective-permute-start(f32[4,96,128]{2,1,0:T(8,128)S(1)} %get-tuple-element.46.rest_a_ref.row_a_ref), channel_id=1, source_target_pairs={{0,4},{4,0},{8,12},{12,8},{1,5},{5,1},{9,13},{13,9},{2,6},{6,2},{1... | collective-permute-start | bytes 589832 | tf_op jit(solution)/shard_map/ppermute | solution.py:464
  12.7 6.7 %collective-permute-start.9 = (f32[4,96,128]{2,1,0:T(8,128)S(1)}, f32[4,96,128]{2,1,0:T(8,128)S(1)}, u32[]{:S(2)}, u32[]{:S(2)}) collective-permute-start(f32[4,96,128]{2,1,0:T(8,128)S(1)} %get-tuple-element.47.rest_b_ref.row_b_ref), channel_id=1, source_target_pairs={{0,16},{4,8},{8,4},{12,28},{16,0},{20,24},{24,20},{28,12},{1,17},{... | collective-permute-start | bytes 589832 | tf_op jit(solution)/shard_map/ppermute | solution.py:464
  16.5 4.5 %collective-permute-start.6 = (f32[5,32,128]{2,1,0:T(8,128)S(1)}, f32[5,32,128]{2,1,0:T(8,128)S(1)}, u32[]{:S(2)}, u32[]{:S(2)}) collective-permute-start(f32[5,32,128]{2,1,0:T(8,128)S(1)} %get-tuple-element.49.row_a_ref), channel_id=1, source_target_pairs={{0,4},{4,0},{8,12},{12,8},{1,5},{5,1},{9,13},{13,9},{2,6},{6,2},{1... | collective-permute-start | bytes 245768 | tf_op jit(solution)/shard_map/ppermute | solution.py:464
  18.0 7.7 %collective-permute-start.12 = (f32[4,32,128]{2,1,0:T(8,128)S(1)}, f32[4,32,128]{2,1,0:T(8,128)S(1)}, u32[]{:S(2)}, u32[]{:S(2)}) collective-permute-start(f32[4,32,128]{2,1,0:T(8,128)S(1)} %get-tuple-element.53.row_b_ref), channel_id=1, source_target_pairs={{0,16},{4,8},{8,4},{12,28},{16,0},{20,24},{24,20},{28,12},{1,17},{... | collective-permute-start | bytes 196616 | tf_op jit(solution)/shard_map/ppermute | solution.py:464
  19.5 6.1 %collective-permute-start.10 = (f32[4,96,128]{2,1,0:T(8,128)S(1)}, f32[4,96,128]{2,1,0:T(8,128)S(1)}, u32[]{:S(2)}, u32[]{:S(2)}) collective-permute-start(f32[4,96,128]{2,1,0:T(8,128)S(1)} %get-tuple-element.50), channel_id=1, source_target_pairs={{0,1},{1,0},{2,3},{3,2},{4,5},{5,4},{6,7},{7,6},{8,9},{9,8},{10,11... | collective-permute-start | bytes 589832 | tf_op jit(solution)/shard_map/ppermute | solution.py:464
  19.6 6.1 %collective-permute-start.11 = (f32[4,96,128]{2,1,0:T(8,128)S(1)}, f32[4,96,128]{2,1,0:T(8,128)S(1)}, u32[]{:S(2)}, u32[]{:S(2)}) collective-permute-start(f32[4,96,128]{2,1,0:T(8,128)S(1)} %get-tuple-element.51), channel_id=1, source_target_pairs={{0,16},{1,2},{2,1},{3,19},{16,0},{17,18},{18,17},{19,3},{4,20},{5,... | collective-permute-start | bytes 589832 | tf_op jit(solution)/shard_map/ppermute | solution.py:464
  21.0 4.6 %collective-permute-start.7 = (f32[32,128]{1,0:T(8,128)S(1)}, f32[32,128]{1,0:T(8,128)S(1)}, u32[]{:S(2)}, u32[]{:S(2)}) collective-permute-start(f32[32,128]{1,0:T(8,128)S(1)} %fusion.1), channel_id=1, source_target_pairs={{0,8},{1,9},{2,10},{3,11},{4,12},{5,13},{6,14},{7,15},{8,0},{9,1},... | collective-permute-start | bytes 49160 | tf_op jit(solution)/shard_map/ppermute | solution.py:452
  25.7 1.3 %collective-permute-start.13 = (f32[5,32,128]{2,1,0:T(8,128)S(1)}, f32[5,32,128]{2,1,0:T(8,128)S(1)}, u32[]{:S(2)}, u32[]{:S(2)}) collective-permute-start(f32[5,32,128]{2,1,0:T(8,128)S(1)} %get-tuple-element.54), channel_id=1, source_target_pairs={{0,1},{1,0},{2,3},{3,2},{4,5},{5,4},{6,7},{7,6},{8,9},{9,8},{10,11... | collective-permute-start | bytes 245768 | tf_op jit(solution)/shard_map/ppermute | solution.py:464
  25.8 5.0 %collective-permute-start.15 = (f32[4,32,128]{2,1,0:T(8,128)S(1)}, f32[4,32,128]{2,1,0:T(8,128)S(1)}, u32[]{:S(2)}, u32[]{:S(2)}) collective-permute-start(f32[4,32,128]{2,1,0:T(8,128)S(1)} %get-tuple-element.55), channel_id=1, source_target_pairs={{0,16},{1,2},{2,1},{3,19},{16,0},{17,18},{18,17},{19,3},{4,20},{5,... | collective-permute-start | bytes 196616 | tf_op jit(solution)/shard_map/ppermute | solution.py:464
  27.1 3.7 %collective-permute-start.14 = (f32[32,128]{1,0:T(8,128)S(1)}, f32[32,128]{1,0:T(8,128)S(1)}, u32[]{:S(2)}, u32[]{:S(2)}) collective-permute-start(f32[32,128]{1,0:T(8,128)S(1)} %fusion), channel_id=1, source_target_pairs={{0,2},{1,3},{2,0},{3,1},{4,6},{5,7},{6,4},{7,5},{8,10},{9,11},{10,... | collective-permute-start | bytes 49160 | tf_op jit(solution)/shard_map/ppermute | solution.py:452
  33.4 1.3 %collective-permute-start.16 = (f32[48,128]{1,0:T(8,128)S(1)}, f32[48,128]{1,0:T(8,128)S(1)}, u32[]{:S(2)}, u32[]{:S(2)}) collective-permute-start(f32[48,128]{1,0:T(8,128)S(1)} %get-tuple-element.63), channel_id=1, source_target_pairs={{0,1},{1,0},{2,3},{3,2},{4,5},{5,4},{6,7},{7,6},{8,9},{9,8},{10,11... | collective-permute-start | bytes 73736 | tf_op jit(solution)/shard_map/ppermute | solution.py:452
  34.7 4.7 %collective-permute-start.17 = (f32[48,128]{1,0:T(8,128)S(1)}, f32[48,128]{1,0:T(8,128)S(1)}, u32[]{:S(2)}, u32[]{:S(2)}) collective-permute-start(f32[48,128]{1,0:T(8,128)S(1)} %add.51), channel_id=1, source_target_pairs={{0,6},{1,7},{2,4},{3,5},{4,2},{5,3},{6,0},{7,1},{8,14},{9,15},{10,... | collective-permute-start | bytes 73736 | tf_op jit(solution)/shard_map/ppermute | solution.py:452
  36.9 3.8 %collective-permute-start.18 = (f32[48,128]{1,0:T(8,128)S(1)}, f32[48,128]{1,0:T(8,128)S(1)}, u32[]{:S(2)}, u32[]{:S(2)}) collective-permute-start(f32[48,128]{1,0:T(8,128)S(1)} %add.51), channel_id=1, source_target_pairs={{0,2},{1,3},{2,0},{3,1},{4,6},{5,7},{6,4},{7,5},{8,10},{9,11},{10,... | collective-permute-start | bytes 73736 | tf_op jit(solution)/shard_map/ppermute | solution.py:452
  37.9 3.8 %collective-permute-start.19 = (f32[48,128]{1,0:T(8,128)S(1)}, f32[48,128]{1,0:T(8,128)S(1)}, u32[]{:S(2)}, u32[]{:S(2)}) collective-permute-start(f32[48,128]{1,0:T(8,128)S(1)} %add.51), channel_id=1, source_target_pairs={{0,4},{1,5},{2,6},{3,7},{4,0},{5,1},{6,2},{7,3},{8,12},{9,13},{10,... | collective-permute-start | bytes 73736 | tf_op jit(solution)/shard_map/ppermute | solution.py:452
  41.8 4.8 %collective-permute-start.20 = (f32[48,128]{1,0:T(8,128)S(1)}, f32[48,128]{1,0:T(8,128)S(1)}, u32[]{:S(2)}, u32[]{:S(2)}) collective-permute-start(f32[48,128]{1,0:T(8,128)S(1)} %add_add_fusion), channel_id=1, source_target_pairs={{0,8},{1,9},{2,10},{3,11},{4,12},{5,13},{6,14},{7,15},{8,0},{9,1},... | collective-permute-start | bytes 73736 | tf_op jit(solution)/shard_map/ppermute | solution.py:452
  46.6 1.3 %collective-permute-start.21 = (f32[40,128]{1,0:T(8,128)S(1)}, f32[40,128]{1,0:T(8,128)S(1)}, u32[]{:S(2)}, u32[]{:S(2)}) collective-permute-start(f32[40,128]{1,0:T(8,128)S(1)} %slice.14), channel_id=1, source_target_pairs={{0,1},{1,0},{2,3},{3,2},{4,5},{5,4},{6,7},{7,6},{8,9},{9,8},{10,11... | collective-permute-start | bytes 61448 | tf_op jit(solution)/shard_map/ppermute | solution.py:452

commit v23 on v22

--- a/solution.py
+++ b/solution.py
@@ -473,7 +473,7 @@
 
 def half_total(sent, kept):
     kept = kept + swap(sent, 1)
-    kept = (kept + swap(kept, 6)) + (swap(kept, 2) + swap(kept, 4))
+    kept = (kept + swap(kept, 2)) + (swap(kept, 4) + swap(kept, 6))
     return total_over(kept, 8, lax.axis_size(("px", "py")))
 
 

time: 49.2 us -> 49.6 us (level)
  waiting for transfers between devices: 12.7 us -> 13.2 us
    ppermute x8, waiting for transfers between devices: 11.9 us -> 12.4 us  [swap(): return lax.ppermute(value, axes, pairs)]
where the time goes in v23:
time: 49.6 us; the launch traced here: 49.5 us
  starting transfers between devices  26.5 us (53%)
  waiting for transfers between devices  13.2 us (27%)
  Pallas kernels  7.53 us (15%)
  other arithmetic  1.27 us (3%)
  between operations  0.86 us (2%)
    ppermute x8, waiting for transfers between devices, swap(): return lax.ppermute(value, axes, pairs)  12.4 us
    ppermute x8, starting transfers between devices, swap(): return lax.ppermute(value, axes, pairs)  9.35 us
    ppermute x7, starting transfers between devices, exchange(): lax.ppermute(message_b, ('case', axis), pairs)  9.16 us
    ppermute x7, starting transfers between devices, exchange(): lax.ppermute(message_a, axis, near)  8 us
    pallas_call x10, Pallas kernels, call(): pl.pallas_call(kernel, out_shape=outputs, in_specs=specs, out_specs=[VMEM...  7.53 us
    concatenate x1, other arithmetic, shards(): vectors = jnp.concatenate([basis, previous.reshape(-1, side)], axis=0)  1.23 us
  transfers between devices with their start and end apart: 22, of which 12 were waited for; matrix products, arithmetic and copies ran while one was open for 0% of the time, Pallas kernels for 7%

profile of v23, /device:TPU:0, one launch (start us, length us, event | category | flops | bytes accessed | tf_op | source)
XLA Modules:
  0.0 49.5 jit_solution(11779653900649054362)
XLA Ops:
  0.7 1.2 %pad_maximum_fusion.vectors_ref = f32[1280,128]{1,0:T(8,128)S(1)} fusion(f32[256,128]{1,0:T(8,128)} %bitcast.24, f32[1024,128]{1,0:T(8,128)} %bitcast.23), kind=kLoop, calls=%fused_computation | loop fusion | flops 163840 | bytes 1310720 | tf_op jit(solution)/shard_map/concatenate | solution.py:493
  1.9 0.1 iota.7.flags_ref
  2.0 0.1 shard_map.93
  2.1 0.5 %collective-permute-start.2 = (f32[2,64,128]{2,1,0:T(8,128)S(1)}, f32[2,64,128]{2,1,0:T(8,128)S(1)}, u32[]{:S(2)}, u32[]{:S(2)}) collective-permute-start(f32[2,64,128]{2,1,0:T(8,128)S(1)} %get-tuple-element.39), channel_id=1, source_target_pairs={{0,1},{1,0},{2,3},{3,2},{4,5},{5,4},{6,7},{7,6},{8,9},{9,8},{10,11... | collective-permute-start | bytes 196616 | tf_op jit(solution)/shard_map/ppermute | solution.py:464
  2.6 2.6 %collective-permute-start.3 = (f32[2,64,128]{2,1,0:T(8,128)S(1)}, f32[2,64,128]{2,1,0:T(8,128)S(1)}, u32[]{:S(2)}, u32[]{:S(2)}) collective-permute-start(f32[2,64,128]{2,1,0:T(8,128)S(1)} %get-tuple-element.43), channel_id=1, source_target_pairs={{0,16},{1,2},{2,1},{3,19},{16,0},{17,18},{18,17},{19,3},{4,20},{5,... | collective-permute-start | bytes 196616 | tf_op jit(solution)/shard_map/ppermute | solution.py:464
  5.2 1.6 %collective-permute-start = (f32[4,64,128]{2,1,0:T(8,128)S(1)}, f32[4,64,128]{2,1,0:T(8,128)S(1)}, u32[]{:S(2)}, u32[]{:S(2)}) collective-permute-start(f32[4,64,128]{2,1,0:T(8,128)S(1)} %get-tuple-element.37.row_a_ref), channel_id=1, source_target_pairs={{0,4},{4,0},{8,12},{12,8},{1,5},{5,1},{9,13},{13,9},{2,6},{6,2},{1... | collective-permute-start | bytes 393224 | tf_op jit(solution)/shard_map/ppermute | solution.py:464
  6.8 0.5 %collective-permute-start.1 = (f32[4,64,128]{2,1,0:T(8,128)S(1)}, f32[4,64,128]{2,1,0:T(8,128)S(1)}, u32[]{:S(2)}, u32[]{:S(2)}) collective-permute-start(f32[4,64,128]{2,1,0:T(8,128)S(1)} %get-tuple-element.38.row_b_ref), channel_id=1, source_target_pairs={{0,16},{4,8},{8,4},{12,28},{16,0},{20,24},{24,20},{28,12},{1,17},{... | collective-permute-start | bytes 393224 | tf_op jit(solution)/shard_map/ppermute | solution.py:464
  7.3 0.1 shard_map.94
  7.3 0.0 collective-permute-done.2.side_a_ref.from_side_a_ref
  7.3 0.1 collective-permute-done.3.side_b_ref.from_side_b_ref
  7.4 2.6 %collective-permute-start.4 = (f32[2,64,128]{2,1,0:T(8,128)S(1)}, f32[2,64,128]{2,1,0:T(8,128)S(1)}, u32[]{:S(2)}, u32[]{:S(2)}) collective-permute-start(f32[2,64,128]{2,1,0:T(8,128)S(1)} %get-tuple-element.44), channel_id=1, source_target_pairs={{0,4},{4,0},{8,12},{12,8},{1,5},{5,1},{9,13},{13,9},{2,6},{6,2},{1... | collective-permute-start | bytes 196616 | tf_op jit(solution)/shard_map/ppermute | solution.py:464
  10.1 1.0 %collective-permute-start.5 = (f32[2,64,128]{2,1,0:T(8,128)S(1)}, f32[2,64,128]{2,1,0:T(8,128)S(1)}, u32[]{:S(2)}, u32[]{:S(2)}) collective-permute-start(f32[2,64,128]{2,1,0:T(8,128)S(1)} %get-tuple-element.45), channel_id=1, source_target_pairs={{0,16},{4,8},{8,4},{12,28},{16,0},{20,24},{24,20},{28,12},{1,17},{... | collective-permute-start | bytes 196616 | tf_op jit(solution)/shard_map/ppermute | solution.py:464
  11.1 1.6 %collective-permute-start.8 = (f32[4,96,128]{2,1,0:T(8,128)S(1)}, f32[4,96,128]{2,1,0:T(8,128)S(1)}, u32[]{:S(2)}, u32[]{:S(2)}) collective-permute-start(f32[4,96,128]{2,1,0:T(8,128)S(1)} %get-tuple-element.46.rest_a_ref.row_a_ref), channel_id=1, source_target_pairs={{0,4},{4,0},{8,12},{12,8},{1,5},{5,1},{9,13},{13,9},{2,6},{6,2},{1... | collective-permute-start | bytes 589832 | tf_op jit(solution)/shard_map/ppermute | solution.py:464
  12.7 1.5 %collective-permute-start.9 = (f32[4,96,128]{2,1,0:T(8,128)S(1)}, f32[4,96,128]{2,1,0:T(8,128)S(1)}, u32[]{:S(2)}, u32[]{:S(2)}) collective-permute-start(f32[4,96,128]{2,1,0:T(8,128)S(1)} %get-tuple-element.47.rest_b_ref.row_b_ref), channel_id=1, source_target_pairs={{0,16},{4,8},{8,4},{12,28},{16,0},{20,24},{24,20},{28,12},{1,17},{... | collective-permute-start | bytes 589832 | tf_op jit(solution)/shard_map/ppermute | solution.py:464
  14.3 0.1 collective-permute-done.5.from_corner_b_ref
  14.4 0.0 collective-permute-done.from_row_a_ref
  14.4 0.0 collective-permute-done.1.from_row_b_ref
  14.4 2.1 %shard_map.96 = (f32[5,32,128]{2,1,0:T(8,128)S(1)}, f32[4,32,128]{2,1,0:T(8,128)S(1)}, f32[32,128]{1,0:T(8,128)S(1)}, f32[24,32,128]{2,1,0:T(8,128)S(1)}) custom-call(s32[8,5]{1,0:T(8,128)S(1)} %bitcast.19, s32[8,5]{1,0:T(8,128)S(1)} %bitcast.21, f32[8,128]{1,0:T(8,128)S(1)} %iota.7.flags_ref, f32[4,64,128]{2,1,0:T(8,128)S(1)} %get-tuple-element.37.row_a_ref, ...), custom_call_target="tpu_custom_call" | custom-call | flops 1000000000 | tf_op jit(solution)/shard_map/pallas_call | solution.py:505
  16.5 1.5 %collective-permute-start.6 = (f32[5,32,128]{2,1,0:T(8,128)S(1)}, f32[5,32,128]{2,1,0:T(8,128)S(1)}, u32[]{:S(2)}, u32[]{:S(2)}) collective-permute-start(f32[5,32,128]{2,1,0:T(8,128)S(1)} %get-tuple-element.49.row_a_ref), channel_id=1, source_target_pairs={{0,4},{4,0},{8,12},{12,8},{1,5},{5,1},{9,13},{13,9},{2,6},{6,2},{1... | collective-permute-start | bytes 245768 | tf_op jit(solution)/shard_map/ppermute | solution.py:464
  18.0 1.5 %collective-permute-start.12 = (f32[4,32,128]{2,1,0:T(8,128)S(1)}, f32[4,32,128]{2,1,0:T(8,128)S(1)}, u32[]{:S(2)}, u32[]{:S(2)}) collective-permute-start(f32[4,32,128]{2,1,0:T(8,128)S(1)} %get-tuple-element.53.row_b_ref), channel_id=1, source_target_pairs={{0,16},{4,8},{8,4},{12,28},{16,0},{20,24},{24,20},{28,12},{1,17},{... | collective-permute-start | bytes 196616 | tf_op jit(solution)/shard_map/ppermute | solution.py:464
  19.5 0.1 collective-permute-start.10
  19.6 1.0 %collective-permute-start.11 = (f32[4,96,128]{2,1,0:T(8,128)S(1)}, f32[4,96,128]{2,1,0:T(8,128)S(1)}, u32[]{:S(2)}, u32[]{:S(2)}) collective-permute-start(f32[4,96,128]{2,1,0:T(8,128)S(1)} %get-tuple-element.51), channel_id=1, source_target_pairs={{0,16},{1,2},{2,1},{3,19},{16,0},{17,18},{18,17},{19,3},{4,20},{5,... | collective-permute-start | bytes 589832 | tf_op jit(solution)/shard_map/ppermute | solution.py:464
  20.6 0.5 collective-permute-done.6.from_row_a_ref
  21.0 2.3 %collective-permute-start.7 = (f32[32,128]{1,0:T(8,128)S(1)}, f32[32,128]{1,0:T(8,128)S(1)}, u32[]{:S(2)}, u32[]{:S(2)}) collective-permute-start(f32[32,128]{1,0:T(8,128)S(1)} %fusion.1), channel_id=1, source_target_pairs={{0,8},{1,9},{2,10},{3,11},{4,12},{5,13},{6,14},{7,15},{8,0},{9,1},... | collective-permute-start | bytes 49160 | tf_op jit(solution)/shard_map/ppermute | solution.py:452
  23.3 2.4 %collective-permute-done.7 = f32[32,128]{1,0:T(8,128)S(1)} collective-permute-done((f32[32,128]{1,0:T(8,128)S(1)}, f32[32,128]{1,0:T(8,128)S(1)}, u32[]{:S(2)}, u32[]{:S(2)}) %collective-permute-start.7) | collective-permute-done | bytes 16416 | tf_op jit(solution)/shard_map/ppermute | solution.py:452
  25.7 0.0 collective-permute-done.11.rest_side_b_ref
  25.7 0.1 collective-permute-start.13
  25.8 1.1 %collective-permute-start.15 = (f32[4,32,128]{2,1,0:T(8,128)S(1)}, f32[4,32,128]{2,1,0:T(8,128)S(1)}, u32[]{:S(2)}, u32[]{:S(2)}) collective-permute-start(f32[4,32,128]{2,1,0:T(8,128)S(1)} %get-tuple-element.55), channel_id=1, source_target_pairs={{0,16},{1,2},{2,1},{3,19},{16,0},{17,18},{18,17},{19,3},{4,20},{5,... | collective-permute-start | bytes 196616 | tf_op jit(solution)/shard_map/ppermute | solution.py:464
  26.9 0.2 collective-permute-done.13.from_side_a_ref
  27.1 0.9 %collective-permute-start.14 = (f32[32,128]{1,0:T(8,128)S(1)}, f32[32,128]{1,0:T(8,128)S(1)}, u32[]{:S(2)}, u32[]{:S(2)}) collective-permute-start(f32[32,128]{1,0:T(8,128)S(1)} %fusion), channel_id=1, source_target_pairs={{0,2},{1,3},{2,0},{3,1},{4,6},{5,7},{6,4},{7,5},{8,10},{9,11},{10,... | collective-permute-start | bytes 49160 | tf_op jit(solution)/shard_map/ppermute | solution.py:452
  28.0 0.5 %shard_map.99 = (bf16[4,256,768]{2,1,0:T(8,128)(2,1)S(1)}, bf16[2,128,1024]{2,1,0:T(8,128)(2,1)S(1)}, bf16[8,256,256]{2,1,0:T(8,128)(2,1)S(1)}) custom-call(f32[8,128]{1,0:T(8,128)S(1)} %iota.7.flags_ref, f32[4,96,128]{2,1,0:T(8,128)S(1)} %get-tuple-element.46.rest_a_ref.row_a_ref, f32[4,96,128]{2,1,0:T(8,128)S(1)} %get-tuple-element.47.rest_b_ref.row_b_ref, ...), custom_call_target="tpu_custom_call" | custom-call | flops 1000000000 | tf_op jit(solution)/shard_map/pallas_call | solution.py:505
  28.5 2.3 %collective-permute-done.14 = f32[32,128]{1,0:T(8,128)S(1)} collective-permute-done((f32[32,128]{1,0:T(8,128)S(1)}, f32[32,128]{1,0:T(8,128)S(1)}, u32[]{:S(2)}, u32[]{:S(2)}) %collective-permute-start.14) | collective-permute-done | bytes 16416 | tf_op jit(solution)/shard_map/ppermute | solution.py:452
  30.8 0.0 collective-permute-done.15.from_side_b_ref
  30.8 2.6 %shard_map.100 = (f32[4,32,128]{2,1,0:T(8,128)S(1)}, f32[4,32,128]{2,1,0:T(8,128)S(1)}, f32[48,128]{1,0:T(8,128)S(1)}, f32[48,128]{1,0:T(8,128)S(1)}) custom-call(s32[8,5]{1,0:T(8,128)S(1)} %bitcast.20, s32[8,5]{1,0:T(8,128)S(1)} %bitcast.22, f32[8,128]{1,0:T(8,128)S(1)} %iota.7.flags_ref, f32[32,128]{1,0:T(8,128)S(1)} %add.50.partial_ref, ...), custom_call_target="tpu_custom_call" | custom-call | tf_op jit(solution)/shard_map/pallas_call | solution.py:505
  33.4 0.1 collective-permute-start.16
  33.5 1.2 %collective-permute-done.16 = f32[48,128]{1,0:T(8,128)S(1)} collective-permute-done((f32[48,128]{1,0:T(8,128)S(1)}, f32[48,128]{1,0:T(8,128)S(1)}, u32[]{:S(2)}, u32[]{:S(2)}) %collective-permute-start.16) | collective-permute-done | bytes 24608 | tf_op jit(solution)/shard_map/ppermute | solution.py:452
  34.7 0.9 %collective-permute-start.17 = (f32[48,128]{1,0:T(8,128)S(1)}, f32[48,128]{1,0:T(8,128)S(1)}, u32[]{:S(2)}, u32[]{:S(2)}) collective-permute-start(f32[48,128]{1,0:T(8,128)S(1)} %add.51), channel_id=1, source_target_pairs={{0,2},{1,3},{2,0},{3,1},{4,6},{5,7},{6,4},{7,5},{8,10},{9,11},{10,... | collective-permute-start | bytes 73736 | tf_op jit(solution)/shard_map/ppermute | solution.py:452
  35.6 1.8 %collective-permute-start.18 = (f32[48,128]{1,0:T(8,128)S(1)}, f32[48,128]{1,0:T(8,128)S(1)}, u32[]{:S(2)}, u32[]{:S(2)}) collective-permute-start(f32[48,128]{1,0:T(8,128)S(1)} %add.51), channel_id=1, source_target_pairs={{0,4},{1,5},{2,6},{3,7},{4,0},{5,1},{6,2},{7,3},{8,12},{9,13},{10,... | collective-permute-start | bytes 73736 | tf_op jit(solution)/shard_map/ppermute | solution.py:452
  37.5 0.7 %collective-permute-start.19 = (f32[48,128]{1,0:T(8,128)S(1)}, f32[48,128]{1,0:T(8,128)S(1)}, u32[]{:S(2)}, u32[]{:S(2)}) collective-permute-start(f32[48,128]{1,0:T(8,128)S(1)} %add.51), channel_id=1, source_target_pairs={{0,6},{1,7},{2,4},{3,5},{4,2},{5,3},{6,0},{7,1},{8,14},{9,15},{10,... | collective-permute-start | bytes 73736 | tf_op jit(solution)/shard_map/ppermute | solution.py:452
  38.2 0.3 collective-permute-done.17
  38.5 0.9 %collective-permute-done.18 = f32[48,128]{1,0:T(8,128)S(1)} collective-permute-done((f32[48,128]{1,0:T(8,128)S(1)}, f32[48,128]{1,0:T(8,128)S(1)}, u32[]{:S(2)}, u32[]{:S(2)}) %collective-permute-start.18) | collective-permute-done | bytes 24608 | tf_op jit(solution)/shard_map/ppermute | solution.py:452
  39.5 2.7 %collective-permute-done.19 = f32[48,128]{1,0:T(8,128)S(1)} collective-permute-done((f32[48,128]{1,0:T(8,128)S(1)}, f32[48,128]{1,0:T(8,128)S(1)}, u32[]{:S(2)}, u32[]{:S(2)}) %collective-permute-start.19) | collective-permute-done | bytes 24608 | tf_op jit(solution)/shard_map/ppermute | solution.py:452
  42.2 2.5 %collective-permute-start.20 = (f32[48,128]{1,0:T(8,128)S(1)}, f32[48,128]{1,0:T(8,128)S(1)}, u32[]{:S(2)}, u32[]{:S(2)}) collective-permute-start(f32[48,128]{1,0:T(8,128)S(1)} %add_add_fusion), channel_id=1, source_target_pairs={{0,8},{1,9},{2,10},{3,11},{4,12},{5,13},{6,14},{7,15},{8,0},{9,1},... | collective-permute-start | bytes 73736 | tf_op jit(solution)/shard_map/ppermute | solution.py:452
  44.7 2.3 %collective-permute-done.20 = f32[48,128]{1,0:T(8,128)S(1)} collective-permute-done((f32[48,128]{1,0:T(8,128)S(1)}, f32[48,128]{1,0:T(8,128)S(1)}, u32[]{:S(2)}, u32[]{:S(2)}) %collective-permute-start.20) | collective-permute-done | bytes 24608 | tf_op jit(solution)/shard_map/ppermute | solution.py:452
  47.0 0.1 collective-permute-start.21
  47.1 0.9 %shard_map.101.work_ref = f32[32,64]{1,0:T(8,128)S(1)} custom-call(f32[48,128]{1,0:T(8,128)S(1)} %add.55.sums_ref), custom_call_target="tpu_custom_call" | custom-call | flops 1000000000 | tf_op jit(solution)/shard_map/pallas_call | solution.py:505
  48.0 0.3 collective-permute-done.21.other_ref
  48.3 1.2 %shard_map.102 = (f32[256,128]{1,0:T(8,128)}, f32[32,128]{1,0:T(8,128)}, f32[32,32]{1,0:T(8,128)}, f32[2,32,160]{2,1,0:T(8,128)}) custom-call(f32[8,128]{1,0:T(8,128)S(1)} %iota.7.flags_ref, f32[32,64]{1,0:T(8,128)S(1)} %shard_map.101.work_ref, f32[48,128]{1,0:T(8,128)S(1)} %add.55.sums_ref, f32[40,128]{1,0:T(8,128)S(1)} %collective-permute-done.21.other_ref, ...), custom_call_target="tpu_custom_call" | custom-call | tf_op jit(solution)/shard_map/pallas_call | solution.py:505
  (25 shorter events, 0.2 us)
Async XLA Ops:
  0.6 13.7 %copy-start = (s32[5,2,4]{0,2,1:T(4,128)S(1)}, s32[5,2,4]{0,2,1:T(4,128)}, u32[]{:S(2)}) copy-start(s32[5,2,4]{0,2,1:T(4,128)} %param.8) | copy-start | bytes 484
  0.6 13.7 %copy-start.1 = (s32[5,2,4]{0,2,1:T(4,128)S(1)}, s32[5,2,4]{0,2,1:T(4,128)}, u32[]{:S(2)}) copy-start(s32[5,2,4]{0,2,1:T(4,128)} %param.9) | copy-start | bytes 484
  0.7 13.7 %copy-start.2 = (f32[8,128,128]{2,1,0:T(8,128)S(1)}, f32[8,128,128]{2,1,0:T(8,128)}, u32[]{:S(2)}) copy-start(f32[8,128,128]{2,1,0:T(8,128)} %stiff_ref.3) | copy-start | bytes 1572868
  0.7 13.7 %copy-start.3 = (f32[8,128,128]{2,1,0:T(8,128)S(1)}, f32[8,128,128]{2,1,0:T(8,128)}, u32[]{:S(2)}) copy-start(f32[8,128,128]{2,1,0:T(8,128)} %mass_ref.3) | copy-start | bytes 1572868
  2.1 5.3 %collective-permute-start.2 = (f32[2,64,128]{2,1,0:T(8,128)S(1)}, f32[2,64,128]{2,1,0:T(8,128)S(1)}, u32[]{:S(2)}, u32[]{:S(2)}) collective-permute-start(f32[2,64,128]{2,1,0:T(8,128)S(1)} %get-tuple-element.39), channel_id=1, source_target_pairs={{0,1},{1,0},{2,3},{3,2},{4,5},{5,4},{6,7},{7,6},{8,9},{9,8},{10,11... | collective-permute-start | bytes 196616 | tf_op jit(solution)/shard_map/ppermute | solution.py:464
  2.6 4.8 %collective-permute-start.3 = (f32[2,64,128]{2,1,0:T(8,128)S(1)}, f32[2,64,128]{2,1,0:T(8,128)S(1)}, u32[]{:S(2)}, u32[]{:S(2)}) collective-permute-start(f32[2,64,128]{2,1,0:T(8,128)S(1)} %get-tuple-element.43), channel_id=1, source_target_pairs={{0,16},{1,2},{2,1},{3,19},{16,0},{17,18},{18,17},{19,3},{4,20},{5,... | collective-permute-start | bytes 196616 | tf_op jit(solution)/shard_map/ppermute | solution.py:464
  5.2 9.2 %collective-permute-start = (f32[4,64,128]{2,1,0:T(8,128)S(1)}, f32[4,64,128]{2,1,0:T(8,128)S(1)}, u32[]{:S(2)}, u32[]{:S(2)}) collective-permute-start(f32[4,64,128]{2,1,0:T(8,128)S(1)} %get-tuple-element.37.row_a_ref), channel_id=1, source_target_pairs={{0,4},{4,0},{8,12},{12,8},{1,5},{5,1},{9,13},{13,9},{2,6},{6,2},{1... | collective-permute-start | bytes 393224 | tf_op jit(solution)/shard_map/ppermute | solution.py:464
  6.8 7.6 %collective-permute-start.1 = (f32[4,64,128]{2,1,0:T(8,128)S(1)}, f32[4,64,128]{2,1,0:T(8,128)S(1)}, u32[]{:S(2)}, u32[]{:S(2)}) collective-permute-start(f32[4,64,128]{2,1,0:T(8,128)S(1)} %get-tuple-element.38.row_b_ref), channel_id=1, source_target_pairs={{0,16},{4,8},{8,4},{12,28},{16,0},{20,24},{24,20},{28,12},{1,17},{... | collective-permute-start | bytes 393224 | tf_op jit(solution)/shard_map/ppermute | solution.py:464
  7.4 5.3 %collective-permute-start.4 = (f32[2,64,128]{2,1,0:T(8,128)S(1)}, f32[2,64,128]{2,1,0:T(8,128)S(1)}, u32[]{:S(2)}, u32[]{:S(2)}) collective-permute-start(f32[2,64,128]{2,1,0:T(8,128)S(1)} %get-tuple-element.44), channel_id=1, source_target_pairs={{0,4},{4,0},{8,12},{12,8},{1,5},{5,1},{9,13},{13,9},{2,6},{6,2},{1... | collective-permute-start | bytes 196616 | tf_op jit(solution)/shard_map/ppermute | solution.py:464
  10.1 4.3 %collective-permute-start.5 = (f32[2,64,128]{2,1,0:T(8,128)S(1)}, f32[2,64,128]{2,1,0:T(8,128)S(1)}, u32[]{:S(2)}, u32[]{:S(2)}) collective-permute-start(f32[2,64,128]{2,1,0:T(8,128)S(1)} %get-tuple-element.45), channel_id=1, source_target_pairs={{0,16},{4,8},{8,4},{12,28},{16,0},{20,24},{24,20},{28,12},{1,17},{... | collective-permute-start | bytes 196616 | tf_op jit(solution)/shard_map/ppermute | solution.py:464
  11.1 8.4 %collective-permute-start.8 = (f32[4,96,128]{2,1,0:T(8,128)S(1)}, f32[4,96,128]{2,1,0:T(8,128)S(1)}, u32[]{:S(2)}, u32[]{:S(2)}) collective-permute-start(f32[4,96,128]{2,1,0:T(8,128)S(1)} %get-tuple-element.46.rest_a_ref.row_a_ref), channel_id=1, source_target_pairs={{0,4},{4,0},{8,12},{12,8},{1,5},{5,1},{9,13},{13,9},{2,6},{6,2},{1... | collective-permute-start | bytes 589832 | tf_op jit(solution)/shard_map/ppermute | solution.py:464
  12.7 6.7 %collective-permute-start.9 = (f32[4,96,128]{2,1,0:T(8,128)S(1)}, f32[4,96,128]{2,1,0:T(8,128)S(1)}, u32[]{:S(2)}, u32[]{:S(2)}) collective-permute-start(f32[4,96,128]{2,1,0:T(8,128)S(1)} %get-tuple-element.47.rest_b_ref.row_b_ref), channel_id=1, source_target_pairs={{0,16},{4,8},{8,4},{12,28},{16,0},{20,24},{24,20},{28,12},{1,17},{... | collective-permute-start | bytes 589832 | tf_op jit(solution)/shard_map/ppermute | solution.py:464
  16.5 4.5 %collective-permute-start.6 = (f32[5,32,128]{2,1,0:T(8,128)S(1)}, f32[5,32,128]{2,1,0:T(8,128)S(1)}, u32[]{:S(2)}, u32[]{:S(2)}) collective-permute-start(f32[5,32,128]{2,1,0:T(8,128)S(1)} %get-tuple-element.49.row_a_ref), channel_id=1, source_target_pairs={{0,4},{4,0},{8,12},{12,8},{1,5},{5,1},{9,13},{13,9},{2,6},{6,2},{1... | collective-permute-start | bytes 245768 | tf_op jit(solution)/shard_map/ppermute | solution.py:464
  18.0 7.7 %collective-permute-start.12 = (f32[4,32,128]{2,1,0:T(8,128)S(1)}, f32[4,32,128]{2,1,0:T(8,128)S(1)}, u32[]{:S(2)}, u32[]{:S(2)}) collective-permute-start(f32[4,32,128]{2,1,0:T(8,128)S(1)} %get-tuple-element.53.row_b_ref), channel_id=1, source_target_pairs={{0,16},{4,8},{8,4},{12,28},{16,0},{20,24},{24,20},{28,12},{1,17},{... | collective-permute-start | bytes 196616 | tf_op jit(solution)/shard_map/ppermute | solution.py:464
  19.5 6.1 %collective-permute-start.10 = (f32[4,96,128]{2,1,0:T(8,128)S(1)}, f32[4,96,128]{2,1,0:T(8,128)S(1)}, u32[]{:S(2)}, u32[]{:S(2)}) collective-permute-start(f32[4,96,128]{2,1,0:T(8,128)S(1)} %get-tuple-element.50), channel_id=1, source_target_pairs={{0,1},{1,0},{2,3},{3,2},{4,5},{5,4},{6,7},{7,6},{8,9},{9,8},{10,11... | collective-permute-start | bytes 589832 | tf_op jit(solution)/shard_map/ppermute | solution.py:464
  19.6 6.1 %collective-permute-start.11 = (f32[4,96,128]{2,1,0:T(8,128)S(1)}, f32[4,96,128]{2,1,0:T(8,128)S(1)}, u32[]{:S(2)}, u32[]{:S(2)}) collective-permute-start(f32[4,96,128]{2,1,0:T(8,128)S(1)} %get-tuple-element.51), channel_id=1, source_target_pairs={{0,16},{1,2},{2,1},{3,19},{16,0},{17,18},{18,17},{19,3},{4,20},{5,... | collective-permute-start | bytes 589832 | tf_op jit(solution)/shard_map/ppermute | solution.py:464
  21.0 4.6 %collective-permute-start.7 = (f32[32,128]{1,0:T(8,128)S(1)}, f32[32,128]{1,0:T(8,128)S(1)}, u32[]{:S(2)}, u32[]{:S(2)}) collective-permute-start(f32[32,128]{1,0:T(8,128)S(1)} %fusion.1), channel_id=1, source_target_pairs={{0,8},{1,9},{2,10},{3,11},{4,12},{5,13},{6,14},{7,15},{8,0},{9,1},... | collective-permute-start | bytes 49160 | tf_op jit(solution)/shard_map/ppermute | solution.py:452
  25.7 1.3 %collective-permute-start.13 = (f32[5,32,128]{2,1,0:T(8,128)S(1)}, f32[5,32,128]{2,1,0:T(8,128)S(1)}, u32[]{:S(2)}, u32[]{:S(2)}) collective-permute-start(f32[5,32,128]{2,1,0:T(8,128)S(1)} %get-tuple-element.54), channel_id=1, source_target_pairs={{0,1},{1,0},{2,3},{3,2},{4,5},{5,4},{6,7},{7,6},{8,9},{9,8},{10,11... | collective-permute-start | bytes 245768 | tf_op jit(solution)/shard_map/ppermute | solution.py:464
  25.8 5.0 %collective-permute-start.15 = (f32[4,32,128]{2,1,0:T(8,128)S(1)}, f32[4,32,128]{2,1,0:T(8,128)S(1)}, u32[]{:S(2)}, u32[]{:S(2)}) collective-permute-start(f32[4,32,128]{2,1,0:T(8,128)S(1)} %get-tuple-element.55), channel_id=1, source_target_pairs={{0,16},{1,2},{2,1},{3,19},{16,0},{17,18},{18,17},{19,3},{4,20},{5,... | collective-permute-start | bytes 196616 | tf_op jit(solution)/shard_map/ppermute | solution.py:464
  27.1 3.7 %collective-permute-start.14 = (f32[32,128]{1,0:T(8,128)S(1)}, f32[32,128]{1,0:T(8,128)S(1)}, u32[]{:S(2)}, u32[]{:S(2)}) collective-permute-start(f32[32,128]{1,0:T(8,128)S(1)} %fusion), channel_id=1, source_target_pairs={{0,2},{1,3},{2,0},{3,1},{4,6},{5,7},{6,4},{7,5},{8,10},{9,11},{10,... | collective-permute-start | bytes 49160 | tf_op jit(solution)/shard_map/ppermute | solution.py:452
  33.4 1.3 %collective-permute-start.16 = (f32[48,128]{1,0:T(8,128)S(1)}, f32[48,128]{1,0:T(8,128)S(1)}, u32[]{:S(2)}, u32[]{:S(2)}) collective-permute-start(f32[48,128]{1,0:T(8,128)S(1)} %get-tuple-element.63), channel_id=1, source_target_pairs={{0,1},{1,0},{2,3},{3,2},{4,5},{5,4},{6,7},{7,6},{8,9},{9,8},{10,11... | collective-permute-start | bytes 73736 | tf_op jit(solution)/shard_map/ppermute | solution.py:452
  34.7 3.8 %collective-permute-start.17 = (f32[48,128]{1,0:T(8,128)S(1)}, f32[48,128]{1,0:T(8,128)S(1)}, u32[]{:S(2)}, u32[]{:S(2)}) collective-permute-start(f32[48,128]{1,0:T(8,128)S(1)} %add.51), channel_id=1, source_target_pairs={{0,2},{1,3},{2,0},{3,1},{4,6},{5,7},{6,4},{7,5},{8,10},{9,11},{10,... | collective-permute-start | bytes 73736 | tf_op jit(solution)/shard_map/ppermute | solution.py:452
  35.6 3.8 %collective-permute-start.18 = (f32[48,128]{1,0:T(8,128)S(1)}, f32[48,128]{1,0:T(8,128)S(1)}, u32[]{:S(2)}, u32[]{:S(2)}) collective-permute-start(f32[48,128]{1,0:T(8,128)S(1)} %add.51), channel_id=1, source_target_pairs={{0,4},{1,5},{2,6},{3,7},{4,0},{5,1},{6,2},{7,3},{8,12},{9,13},{10,... | collective-permute-start | bytes 73736 | tf_op jit(solution)/shard_map/ppermute | solution.py:452
  37.5 4.7 %collective-permute-start.19 = (f32[48,128]{1,0:T(8,128)S(1)}, f32[48,128]{1,0:T(8,128)S(1)}, u32[]{:S(2)}, u32[]{:S(2)}) collective-permute-start(f32[48,128]{1,0:T(8,128)S(1)} %add.51), channel_id=1, source_target_pairs={{0,6},{1,7},{2,4},{3,5},{4,2},{5,3},{6,0},{7,1},{8,14},{9,15},{10,... | collective-permute-start | bytes 73736 | tf_op jit(solution)/shard_map/ppermute | solution.py:452
  42.2 4.8 %collective-permute-start.20 = (f32[48,128]{1,0:T(8,128)S(1)}, f32[48,128]{1,0:T(8,128)S(1)}, u32[]{:S(2)}, u32[]{:S(2)}) collective-permute-start(f32[48,128]{1,0:T(8,128)S(1)} %add_add_fusion), channel_id=1, source_target_pairs={{0,8},{1,9},{2,10},{3,11},{4,12},{5,13},{6,14},{7,15},{8,0},{9,1},... | collective-permute-start | bytes 73736 | tf_op jit(solution)/shard_map/ppermute | solution.py:452
  47.0 1.3 %collective-permute-start.21 = (f32[40,128]{1,0:T(8,128)S(1)}, f32[40,128]{1,0:T(8,128)S(1)}, u32[]{:S(2)}, u32[]{:S(2)}) collective-permute-start(f32[40,128]{1,0:T(8,128)S(1)} %slice.14), channel_id=1, source_target_pairs={{0,1},{1,0},{2,3},{3,2},{4,5},{5,4},{6,7},{7,6},{8,9},{9,8},{10,11... | collective-permute-start | bytes 61448 | tf_op jit(solution)/shard_map/ppermute | solution.py:452

commit v24 on v22

--- a/solution.py
+++ b/solution.py
@@ -570,15 +570,15 @@
     partial = total_over(
         partial + from_row_a[-1], 2 * count_py, count_py * lax.axis_size("px")
     )
-    partial, rest_side_a, rest_side_b = lax.optimization_barrier(
-        (partial, rest_side_a, rest_side_b)
-    )
     side_a, side_b = call(
         columns_kernel,
         (flags, residual_a, residual_b, from_row_a, from_row_b, partial),
         [shape(5, block, side), shape(4, block, side)],
     )
     from_side_a, from_side_b = exchange(side_a, side_b, "py")
+    from_side_a, rest_side_a, rest_side_b = lax.optimization_barrier(
+        (from_side_a, rest_side_a, rest_side_b)
+    )
     partial = total_over(partial + from_side_a[-1], 2, count_py)
     basis_parts, prior_parts, table = call(
         prepare_kernel,

time: 49.2 us -> 49.7 us (1.010)
  waiting for transfers between devices: 12.7 us -> 13.3 us
    ppermute x8, waiting for transfers between devices: 11.9 us -> 12.5 us  [swap(): return lax.ppermute(value, axes, pairs)]
where the time goes in v24:
time: 49.7 us; the launch traced here: 49.5 us
  starting transfers between devices  26.5 us (53%)
  waiting for transfers between devices  13.3 us (27%)
  Pallas kernels  7.54 us (15%)
  other arithmetic  1.26 us (3%)
  between operations  0.84 us (2%)
    ppermute x8, waiting for transfers between devices, swap(): return lax.ppermute(value, axes, pairs)  12.5 us
    ppermute x8, starting transfers between devices, swap(): return lax.ppermute(value, axes, pairs)  9.33 us
    ppermute x7, starting transfers between devices, exchange(): lax.ppermute(message_b, ('case', axis), pairs)  9.16 us
    ppermute x7, starting transfers between devices, exchange(): lax.ppermute(message_a, axis, near)  8 us
    pallas_call x10, Pallas kernels, call(): pl.pallas_call(kernel, out_shape=outputs, in_specs=specs, out_specs=[VMEM...  7.54 us
    concatenate x1, other arithmetic, shards(): vectors = jnp.concatenate([basis, previous.reshape(-1, side)], axis=0)  1.22 us
  transfers between devices with their start and end apart: 22, of which 12 were waited for; matrix products, arithmetic and copies ran while one was open for 0% of the time, Pallas kernels for 7%

profile of v24, /device:TPU:0, one launch (start us, length us, event | category | flops | bytes accessed | tf_op | source)
XLA Modules:
  0.0 49.5 jit_solution(17737274383601368369)
XLA Ops:
  0.7 1.2 %pad_maximum_fusion.vectors_ref = f32[1280,128]{1,0:T(8,128)S(1)} fusion(f32[256,128]{1,0:T(8,128)} %bitcast.22, f32[1024,128]{1,0:T(8,128)} %bitcast.21), kind=kLoop, calls=%fused_computation | loop fusion | flops 163840 | bytes 1310720 | tf_op jit(solution)/shard_map/concatenate | solution.py:493
  1.9 0.1 iota.7.flags_ref
  2.0 0.1 shard_map.93
  2.1 0.5 %collective-permute-start.2 = (f32[2,64,128]{2,1,0:T(8,128)S(1)}, f32[2,64,128]{2,1,0:T(8,128)S(1)}, u32[]{:S(2)}, u32[]{:S(2)}) collective-permute-start(f32[2,64,128]{2,1,0:T(8,128)S(1)} %get-tuple-element.39), channel_id=1, source_target_pairs={{0,1},{1,0},{2,3},{3,2},{4,5},{5,4},{6,7},{7,6},{8,9},{9,8},{10,11... | collective-permute-start | bytes 196616 | tf_op jit(solution)/shard_map/ppermute | solution.py:464
  2.6 2.6 %collective-permute-start.3 = (f32[2,64,128]{2,1,0:T(8,128)S(1)}, f32[2,64,128]{2,1,0:T(8,128)S(1)}, u32[]{:S(2)}, u32[]{:S(2)}) collective-permute-start(f32[2,64,128]{2,1,0:T(8,128)S(1)} %get-tuple-element.43), channel_id=1, source_target_pairs={{0,16},{1,2},{2,1},{3,19},{16,0},{17,18},{18,17},{19,3},{4,20},{5,... | collective-permute-start | bytes 196616 | tf_op jit(solution)/shard_map/ppermute | solution.py:464
  5.2 1.6 %collective-permute-start = (f32[4,64,128]{2,1,0:T(8,128)S(1)}, f32[4,64,128]{2,1,0:T(8,128)S(1)}, u32[]{:S(2)}, u32[]{:S(2)}) collective-permute-start(f32[4,64,128]{2,1,0:T(8,128)S(1)} %get-tuple-element.37.row_a_ref), channel_id=1, source_target_pairs={{0,4},{4,0},{8,12},{12,8},{1,5},{5,1},{9,13},{13,9},{2,6},{6,2},{1... | collective-permute-start | bytes 393224 | tf_op jit(solution)/shard_map/ppermute | solution.py:464
  6.8 0.5 %collective-permute-start.1 = (f32[4,64,128]{2,1,0:T(8,128)S(1)}, f32[4,64,128]{2,1,0:T(8,128)S(1)}, u32[]{:S(2)}, u32[]{:S(2)}) collective-permute-start(f32[4,64,128]{2,1,0:T(8,128)S(1)} %get-tuple-element.38.row_b_ref), channel_id=1, source_target_pairs={{0,16},{4,8},{8,4},{12,28},{16,0},{20,24},{24,20},{28,12},{1,17},{... | collective-permute-start | bytes 393224 | tf_op jit(solution)/shard_map/ppermute | solution.py:464
  7.3 0.1 shard_map.94
  7.3 0.0 collective-permute-done.2.side_a_ref.from_side_a_ref
  7.3 0.1 collective-permute-done.3.side_b_ref.from_side_b_ref
  7.4 2.6 %collective-permute-start.4 = (f32[2,64,128]{2,1,0:T(8,128)S(1)}, f32[2,64,128]{2,1,0:T(8,128)S(1)}, u32[]{:S(2)}, u32[]{:S(2)}) collective-permute-start(f32[2,64,128]{2,1,0:T(8,128)S(1)} %get-tuple-element.44), channel_id=1, source_target_pairs={{0,4},{4,0},{8,12},{12,8},{1,5},{5,1},{9,13},{13,9},{2,6},{6,2},{1... | collective-permute-start | bytes 196616 | tf_op jit(solution)/shard_map/ppermute | solution.py:464
  10.1 1.0 %collective-permute-start.5 = (f32[2,64,128]{2,1,0:T(8,128)S(1)}, f32[2,64,128]{2,1,0:T(8,128)S(1)}, u32[]{:S(2)}, u32[]{:S(2)}) collective-permute-start(f32[2,64,128]{2,1,0:T(8,128)S(1)} %get-tuple-element.45), channel_id=1, source_target_pairs={{0,16},{4,8},{8,4},{12,28},{16,0},{20,24},{24,20},{28,12},{1,17},{... | collective-permute-start | bytes 196616 | tf_op jit(solution)/shard_map/ppermute | solution.py:464
  11.1 1.6 %collective-permute-start.10 = (f32[4,96,128]{2,1,0:T(8,128)S(1)}, f32[4,96,128]{2,1,0:T(8,128)S(1)}, u32[]{:S(2)}, u32[]{:S(2)}) collective-permute-start(f32[4,96,128]{2,1,0:T(8,128)S(1)} %get-tuple-element.46.rest_a_ref.row_a_ref), channel_id=1, source_target_pairs={{0,4},{4,0},{8,12},{12,8},{1,5},{5,1},{9,13},{13,9},{2,6},{6,2},{1... | collective-permute-start | bytes 589832 | tf_op jit(solution)/shard_map/ppermute | solution.py:464
  12.7 0.0 collective-permute-done.4.from_corner_a_ref
  12.7 1.5 %collective-permute-start.11 = (f32[4,96,128]{2,1,0:T(8,128)S(1)}, f32[4,96,128]{2,1,0:T(8,128)S(1)}, u32[]{:S(2)}, u32[]{:S(2)}) collective-permute-start(f32[4,96,128]{2,1,0:T(8,128)S(1)} %get-tuple-element.47.rest_b_ref.row_b_ref), channel_id=1, source_target_pairs={{0,16},{4,8},{8,4},{12,28},{16,0},{20,24},{24,20},{28,12},{1,17},{... | collective-permute-start | bytes 589832 | tf_op jit(solution)/shard_map/ppermute | solution.py:464
  14.3 0.1 collective-permute-done.5.from_corner_b_ref
  14.4 0.0 collective-permute-done.from_row_a_ref
  14.4 0.0 collective-permute-done.1.from_row_b_ref
  14.4 2.1 %shard_map.96 = (f32[5,32,128]{2,1,0:T(8,128)S(1)}, f32[4,32,128]{2,1,0:T(8,128)S(1)}, f32[32,128]{1,0:T(8,128)S(1)}, f32[24,32,128]{2,1,0:T(8,128)S(1)}) custom-call(s32[8,5]{1,0:T(8,128)S(1)} %bitcast.17, s32[8,5]{1,0:T(8,128)S(1)} %bitcast.19, f32[8,128]{1,0:T(8,128)S(1)} %iota.7.flags_ref, f32[4,64,128]{2,1,0:T(8,128)S(1)} %get-tuple-element.37.row_a_ref, ...), custom_call_target="tpu_custom_call" | custom-call | flops 1000000000 | tf_op jit(solution)/shard_map/pallas_call | solution.py:505
  16.5 1.5 %collective-permute-start.6 = (f32[5,32,128]{2,1,0:T(8,128)S(1)}, f32[5,32,128]{2,1,0:T(8,128)S(1)}, u32[]{:S(2)}, u32[]{:S(2)}) collective-permute-start(f32[5,32,128]{2,1,0:T(8,128)S(1)} %get-tuple-element.49.row_a_ref), channel_id=1, source_target_pairs={{0,4},{4,0},{8,12},{12,8},{1,5},{5,1},{9,13},{13,9},{2,6},{6,2},{1... | collective-permute-start | bytes 245768 | tf_op jit(solution)/shard_map/ppermute | solution.py:464
  18.0 1.5 %collective-permute-start.8 = (f32[4,32,128]{2,1,0:T(8,128)S(1)}, f32[4,32,128]{2,1,0:T(8,128)S(1)}, u32[]{:S(2)}, u32[]{:S(2)}) collective-permute-start(f32[4,32,128]{2,1,0:T(8,128)S(1)} %get-tuple-element.50.row_b_ref), channel_id=1, source_target_pairs={{0,16},{4,8},{8,4},{12,28},{16,0},{20,24},{24,20},{28,12},{1,17},{... | collective-permute-start | bytes 196616 | tf_op jit(solution)/shard_map/ppermute | solution.py:464
  19.5 0.1 collective-permute-start.12
  19.6 1.0 %collective-permute-start.13 = (f32[4,96,128]{2,1,0:T(8,128)S(1)}, f32[4,96,128]{2,1,0:T(8,128)S(1)}, u32[]{:S(2)}, u32[]{:S(2)}) collective-permute-start(f32[4,96,128]{2,1,0:T(8,128)S(1)} %get-tuple-element.53), channel_id=1, source_target_pairs={{0,16},{1,2},{2,1},{3,19},{16,0},{17,18},{18,17},{19,3},{4,20},{5,... | collective-permute-start | bytes 589832 | tf_op jit(solution)/shard_map/ppermute | solution.py:464
  20.6 0.5 collective-permute-done.6.from_row_a_ref
  21.0 2.3 %collective-permute-start.7 = (f32[32,128]{1,0:T(8,128)S(1)}, f32[32,128]{1,0:T(8,128)S(1)}, u32[]{:S(2)}, u32[]{:S(2)}) collective-permute-start(f32[32,128]{1,0:T(8,128)S(1)} %fusion), channel_id=1, source_target_pairs={{0,8},{1,9},{2,10},{3,11},{4,12},{5,13},{6,14},{7,15},{8,0},{9,1},... | collective-permute-start | bytes 49160 | tf_op jit(solution)/shard_map/ppermute | solution.py:452
  23.3 2.4 %collective-permute-done.7 = f32[32,128]{1,0:T(8,128)S(1)} collective-permute-done((f32[32,128]{1,0:T(8,128)S(1)}, f32[32,128]{1,0:T(8,128)S(1)}, u32[]{:S(2)}, u32[]{:S(2)}) %collective-permute-start.7) | collective-permute-done | bytes 16416 | tf_op jit(solution)/shard_map/ppermute | solution.py:452
  25.7 0.1 collective-permute-start.9
  25.8 1.1 %collective-permute-start.15 = (f32[4,32,128]{2,1,0:T(8,128)S(1)}, f32[4,32,128]{2,1,0:T(8,128)S(1)}, u32[]{:S(2)}, u32[]{:S(2)}) collective-permute-start(f32[4,32,128]{2,1,0:T(8,128)S(1)} %get-tuple-element.55), channel_id=1, source_target_pairs={{0,16},{1,2},{2,1},{3,19},{16,0},{17,18},{18,17},{19,3},{4,20},{5,... | collective-permute-start | bytes 196616 | tf_op jit(solution)/shard_map/ppermute | solution.py:464
  26.9 0.2 collective-permute-done.9.from_side_a_ref
  27.1 0.9 %collective-permute-start.14 = (f32[32,128]{1,0:T(8,128)S(1)}, f32[32,128]{1,0:T(8,128)S(1)}, u32[]{:S(2)}, u32[]{:S(2)}) collective-permute-start(f32[32,128]{1,0:T(8,128)S(1)} %bitcast_add_fusion), channel_id=1, source_target_pairs={{0,2},{1,3},{2,0},{3,1},{4,6},{5,7},{6,4},{7,5},{8,10},{9,11},{10,... | collective-permute-start | bytes 49160 | tf_op jit(solution)/shard_map/ppermute | solution.py:452
  28.0 0.5 %shard_map.99 = (bf16[4,256,768]{2,1,0:T(8,128)(2,1)S(1)}, bf16[2,128,1024]{2,1,0:T(8,128)(2,1)S(1)}, bf16[8,256,256]{2,1,0:T(8,128)(2,1)S(1)}) custom-call(f32[8,128]{1,0:T(8,128)S(1)} %iota.7.flags_ref, f32[4,96,128]{2,1,0:T(8,128)S(1)} %get-tuple-element.46.rest_a_ref.row_a_ref, f32[4,96,128]{2,1,0:T(8,128)S(1)} %get-tuple-element.47.rest_b_ref.row_b_ref, ...), custom_call_target="tpu_custom_call" | custom-call | flops 1000000000 | tf_op jit(solution)/shard_map/pallas_call | solution.py:505
  28.5 2.3 %collective-permute-done.14 = f32[32,128]{1,0:T(8,128)S(1)} collective-permute-done((f32[32,128]{1,0:T(8,128)S(1)}, f32[32,128]{1,0:T(8,128)S(1)}, u32[]{:S(2)}, u32[]{:S(2)}) %collective-permute-start.14) | collective-permute-done | bytes 16416 | tf_op jit(solution)/shard_map/ppermute | solution.py:452
  30.9 0.0 collective-permute-done.15.from_side_b_ref
  30.9 2.6 %shard_map.100 = (f32[4,32,128]{2,1,0:T(8,128)S(1)}, f32[4,32,128]{2,1,0:T(8,128)S(1)}, f32[48,128]{1,0:T(8,128)S(1)}, f32[48,128]{1,0:T(8,128)S(1)}) custom-call(s32[8,5]{1,0:T(8,128)S(1)} %bitcast.18, s32[8,5]{1,0:T(8,128)S(1)} %bitcast.20, f32[8,128]{1,0:T(8,128)S(1)} %iota.7.flags_ref, f32[32,128]{1,0:T(8,128)S(1)} %add.50.partial_ref, ...), custom_call_target="tpu_custom_call" | custom-call | tf_op jit(solution)/shard_map/pallas_call | solution.py:505
  33.5 0.1 collective-permute-start.16
  33.6 1.2 %collective-permute-done.16 = f32[48,128]{1,0:T(8,128)S(1)} collective-permute-done((f32[48,128]{1,0:T(8,128)S(1)}, f32[48,128]{1,0:T(8,128)S(1)}, u32[]{:S(2)}, u32[]{:S(2)}) %collective-permute-start.16) | collective-permute-done | bytes 24608 | tf_op jit(solution)/shard_map/ppermute | solution.py:452
  34.8 1.7 %collective-permute-start.19 = (f32[48,128]{1,0:T(8,128)S(1)}, f32[48,128]{1,0:T(8,128)S(1)}, u32[]{:S(2)}, u32[]{:S(2)}) collective-permute-start(f32[48,128]{1,0:T(8,128)S(1)} %add.51), channel_id=1, source_target_pairs={{0,4},{1,5},{2,6},{3,7},{4,0},{5,1},{6,2},{7,3},{8,12},{9,13},{10,... | collective-permute-start | bytes 73736 | tf_op jit(solution)/shard_map/ppermute | solution.py:452
  36.5 1.1 %collective-permute-start.18 = (f32[48,128]{1,0:T(8,128)S(1)}, f32[48,128]{1,0:T(8,128)S(1)}, u32[]{:S(2)}, u32[]{:S(2)}) collective-permute-start(f32[48,128]{1,0:T(8,128)S(1)} %add.51), channel_id=1, source_target_pairs={{0,2},{1,3},{2,0},{3,1},{4,6},{5,7},{6,4},{7,5},{8,10},{9,11},{10,... | collective-permute-start | bytes 73736 | tf_op jit(solution)/shard_map/ppermute | solution.py:452
  37.5 0.7 %collective-permute-start.17 = (f32[48,128]{1,0:T(8,128)S(1)}, f32[48,128]{1,0:T(8,128)S(1)}, u32[]{:S(2)}, u32[]{:S(2)}) collective-permute-start(f32[48,128]{1,0:T(8,128)S(1)} %add.51), channel_id=1, source_target_pairs={{0,6},{1,7},{2,4},{3,5},{4,2},{5,3},{6,0},{7,1},{8,14},{9,15},{10,... | collective-permute-start | bytes 73736 | tf_op jit(solution)/shard_map/ppermute | solution.py:452
  38.2 0.3 collective-permute-done.19
  38.6 1.7 %collective-permute-done.18 = f32[48,128]{1,0:T(8,128)S(1)} collective-permute-done((f32[48,128]{1,0:T(8,128)S(1)}, f32[48,128]{1,0:T(8,128)S(1)}, u32[]{:S(2)}, u32[]{:S(2)}) %collective-permute-start.18) | collective-permute-done | bytes 24608 | tf_op jit(solution)/shard_map/ppermute | solution.py:452
  40.3 2.0 %collective-permute-done.17 = f32[48,128]{1,0:T(8,128)S(1)} collective-permute-done((f32[48,128]{1,0:T(8,128)S(1)}, f32[48,128]{1,0:T(8,128)S(1)}, u32[]{:S(2)}, u32[]{:S(2)}) %collective-permute-start.17) | collective-permute-done | bytes 24608 | tf_op jit(solution)/shard_map/ppermute | solution.py:452
  42.3 2.5 %collective-permute-start.20 = (f32[48,128]{1,0:T(8,128)S(1)}, f32[48,128]{1,0:T(8,128)S(1)}, u32[]{:S(2)}, u32[]{:S(2)}) collective-permute-start(f32[48,128]{1,0:T(8,128)S(1)} %add_add_fusion), channel_id=1, source_target_pairs={{0,8},{1,9},{2,10},{3,11},{4,12},{5,13},{6,14},{7,15},{8,0},{9,1},... | collective-permute-start | bytes 73736 | tf_op jit(solution)/shard_map/ppermute | solution.py:452
  44.8 2.3 %collective-permute-done.20 = f32[48,128]{1,0:T(8,128)S(1)} collective-permute-done((f32[48,128]{1,0:T(8,128)S(1)}, f32[48,128]{1,0:T(8,128)S(1)}, u32[]{:S(2)}, u32[]{:S(2)}) %collective-permute-start.20) | collective-permute-done | bytes 24608 | tf_op jit(solution)/shard_map/ppermute | solution.py:452
  47.1 0.1 collective-permute-start.21
  47.1 0.9 %shard_map.101.work_ref = f32[32,64]{1,0:T(8,128)S(1)} custom-call(f32[48,128]{1,0:T(8,128)S(1)} %add.55.sums_ref), custom_call_target="tpu_custom_call" | custom-call | flops 1000000000 | tf_op jit(solution)/shard_map/pallas_call | solution.py:505
  48.0 0.3 collective-permute-done.21.other_ref
  48.3 1.2 %shard_map.102 = (f32[256,128]{1,0:T(8,128)}, f32[32,128]{1,0:T(8,128)}, f32[32,32]{1,0:T(8,128)}, f32[2,32,160]{2,1,0:T(8,128)}) custom-call(f32[8,128]{1,0:T(8,128)S(1)} %iota.7.flags_ref, f32[32,64]{1,0:T(8,128)S(1)} %shard_map.101.work_ref, f32[48,128]{1,0:T(8,128)S(1)} %add.55.sums_ref, f32[40,128]{1,0:T(8,128)S(1)} %collective-permute-done.21.other_ref, ...), custom_call_target="tpu_custom_call" | custom-call | tf_op jit(solution)/shard_map/pallas_call | solution.py:505
  (25 shorter events, 0.2 us)
Async XLA Ops:
  0.6 13.7 %copy-start.3 = (f32[8,128,128]{2,1,0:T(8,128)S(1)}, f32[8,128,128]{2,1,0:T(8,128)}, u32[]{:S(2)}) copy-start(f32[8,128,128]{2,1,0:T(8,128)} %mass_ref.3) | copy-start | bytes 1572868
  0.6 13.7 %copy-start.2 = (f32[8,128,128]{2,1,0:T(8,128)S(1)}, f32[8,128,128]{2,1,0:T(8,128)}, u32[]{:S(2)}) copy-start(f32[8,128,128]{2,1,0:T(8,128)} %stiff_ref.3) | copy-start | bytes 1572868
  0.7 13.7 %copy-start.1 = (s32[5,2,4]{0,2,1:T(4,128)S(1)}, s32[5,2,4]{0,2,1:T(4,128)}, u32[]{:S(2)}) copy-start(s32[5,2,4]{0,2,1:T(4,128)} %param.9) | copy-start | bytes 484
  0.7 13.7 %copy-start = (s32[5,2,4]{0,2,1:T(4,128)S(1)}, s32[5,2,4]{0,2,1:T(4,128)}, u32[]{:S(2)}) copy-start(s32[5,2,4]{0,2,1:T(4,128)} %param.8) | copy-start | bytes 484
  2.1 5.3 %collective-permute-start.2 = (f32[2,64,128]{2,1,0:T(8,128)S(1)}, f32[2,64,128]{2,1,0:T(8,128)S(1)}, u32[]{:S(2)}, u32[]{:S(2)}) collective-permute-start(f32[2,64,128]{2,1,0:T(8,128)S(1)} %get-tuple-element.39), channel_id=1, source_target_pairs={{0,1},{1,0},{2,3},{3,2},{4,5},{5,4},{6,7},{7,6},{8,9},{9,8},{10,11... | collective-permute-start | bytes 196616 | tf_op jit(solution)/shard_map/ppermute | solution.py:464
  2.6 4.8 %collective-permute-start.3 = (f32[2,64,128]{2,1,0:T(8,128)S(1)}, f32[2,64,128]{2,1,0:T(8,128)S(1)}, u32[]{:S(2)}, u32[]{:S(2)}) collective-permute-start(f32[2,64,128]{2,1,0:T(8,128)S(1)} %get-tuple-element.43), channel_id=1, source_target_pairs={{0,16},{1,2},{2,1},{3,19},{16,0},{17,18},{18,17},{19,3},{4,20},{5,... | collective-permute-start | bytes 196616 | tf_op jit(solution)/shard_map/ppermute | solution.py:464
  5.2 9.2 %collective-permute-start = (f32[4,64,128]{2,1,0:T(8,128)S(1)}, f32[4,64,128]{2,1,0:T(8,128)S(1)}, u32[]{:S(2)}, u32[]{:S(2)}) collective-permute-start(f32[4,64,128]{2,1,0:T(8,128)S(1)} %get-tuple-element.37.row_a_ref), channel_id=1, source_target_pairs={{0,4},{4,0},{8,12},{12,8},{1,5},{5,1},{9,13},{13,9},{2,6},{6,2},{1... | collective-permute-start | bytes 393224 | tf_op jit(solution)/shard_map/ppermute | solution.py:464
  6.8 7.6 %collective-permute-start.1 = (f32[4,64,128]{2,1,0:T(8,128)S(1)}, f32[4,64,128]{2,1,0:T(8,128)S(1)}, u32[]{:S(2)}, u32[]{:S(2)}) collective-permute-start(f32[4,64,128]{2,1,0:T(8,128)S(1)} %get-tuple-element.38.row_b_ref), channel_id=1, source_target_pairs={{0,16},{4,8},{8,4},{12,28},{16,0},{20,24},{24,20},{28,12},{1,17},{... | collective-permute-start | bytes 393224 | tf_op jit(solution)/shard_map/ppermute | solution.py:464
  7.4 5.3 %collective-permute-start.4 = (f32[2,64,128]{2,1,0:T(8,128)S(1)}, f32[2,64,128]{2,1,0:T(8,128)S(1)}, u32[]{:S(2)}, u32[]{:S(2)}) collective-permute-start(f32[2,64,128]{2,1,0:T(8,128)S(1)} %get-tuple-element.44), channel_id=1, source_target_pairs={{0,4},{4,0},{8,12},{12,8},{1,5},{5,1},{9,13},{13,9},{2,6},{6,2},{1... | collective-permute-start | bytes 196616 | tf_op jit(solution)/shard_map/ppermute | solution.py:464
  10.1 4.3 %collective-permute-start.5 = (f32[2,64,128]{2,1,0:T(8,128)S(1)}, f32[2,64,128]{2,1,0:T(8,128)S(1)}, u32[]{:S(2)}, u32[]{:S(2)}) collective-permute-start(f32[2,64,128]{2,1,0:T(8,128)S(1)} %get-tuple-element.45), channel_id=1, source_target_pairs={{0,16},{4,8},{8,4},{12,28},{16,0},{20,24},{24,20},{28,12},{1,17},{... | collective-permute-start | bytes 196616 | tf_op jit(solution)/shard_map/ppermute | solution.py:464
  11.1 8.4 %collective-permute-start.10 = (f32[4,96,128]{2,1,0:T(8,128)S(1)}, f32[4,96,128]{2,1,0:T(8,128)S(1)}, u32[]{:S(2)}, u32[]{:S(2)}) collective-permute-start(f32[4,96,128]{2,1,0:T(8,128)S(1)} %get-tuple-element.46.rest_a_ref.row_a_ref), channel_id=1, source_target_pairs={{0,4},{4,0},{8,12},{12,8},{1,5},{5,1},{9,13},{13,9},{2,6},{6,2},{1... | collective-permute-start | bytes 589832 | tf_op jit(solution)/shard_map/ppermute | solution.py:464
  12.7 6.7 %collective-permute-start.11 = (f32[4,96,128]{2,1,0:T(8,128)S(1)}, f32[4,96,128]{2,1,0:T(8,128)S(1)}, u32[]{:S(2)}, u32[]{:S(2)}) collective-permute-start(f32[4,96,128]{2,1,0:T(8,128)S(1)} %get-tuple-element.47.rest_b_ref.row_b_ref), channel_id=1, source_target_pairs={{0,16},{4,8},{8,4},{12,28},{16,0},{20,24},{24,20},{28,12},{1,17},{... | collective-permute-start | bytes 589832 | tf_op jit(solution)/shard_map/ppermute | solution.py:464
  16.5 4.5 %collective-permute-start.6 = (f32[5,32,128]{2,1,0:T(8,128)S(1)}, f32[5,32,128]{2,1,0:T(8,128)S(1)}, u32[]{:S(2)}, u32[]{:S(2)}) collective-permute-start(f32[5,32,128]{2,1,0:T(8,128)S(1)} %get-tuple-element.49.row_a_ref), channel_id=1, source_target_pairs={{0,4},{4,0},{8,12},{12,8},{1,5},{5,1},{9,13},{13,9},{2,6},{6,2},{1... | collective-permute-start | bytes 245768 | tf_op jit(solution)/shard_map/ppermute | solution.py:464
  18.0 7.7 %collective-permute-start.8 = (f32[4,32,128]{2,1,0:T(8,128)S(1)}, f32[4,32,128]{2,1,0:T(8,128)S(1)}, u32[]{:S(2)}, u32[]{:S(2)}) collective-permute-start(f32[4,32,128]{2,1,0:T(8,128)S(1)} %get-tuple-element.50.row_b_ref), channel_id=1, source_target_pairs={{0,16},{4,8},{8,4},{12,28},{16,0},{20,24},{24,20},{28,12},{1,17},{... | collective-permute-start | bytes 196616 | tf_op jit(solution)/shard_map/ppermute | solution.py:464
  19.5 7.5 %collective-permute-start.12 = (f32[4,96,128]{2,1,0:T(8,128)S(1)}, f32[4,96,128]{2,1,0:T(8,128)S(1)}, u32[]{:S(2)}, u32[]{:S(2)}) collective-permute-start(f32[4,96,128]{2,1,0:T(8,128)S(1)} %get-tuple-element.52), channel_id=1, source_target_pairs={{0,1},{1,0},{2,3},{3,2},{4,5},{5,4},{6,7},{7,6},{8,9},{9,8},{10,11... | collective-permute-start | bytes 589832 | tf_op jit(solution)/shard_map/ppermute | solution.py:464
  19.6 7.4 %collective-permute-start.13 = (f32[4,96,128]{2,1,0:T(8,128)S(1)}, f32[4,96,128]{2,1,0:T(8,128)S(1)}, u32[]{:S(2)}, u32[]{:S(2)}) collective-permute-start(f32[4,96,128]{2,1,0:T(8,128)S(1)} %get-tuple-element.53), channel_id=1, source_target_pairs={{0,16},{1,2},{2,1},{3,19},{16,0},{17,18},{18,17},{19,3},{4,20},{5,... | collective-permute-start | bytes 589832 | tf_op jit(solution)/shard_map/ppermute | solution.py:464
  21.0 4.6 %collective-permute-start.7 = (f32[32,128]{1,0:T(8,128)S(1)}, f32[32,128]{1,0:T(8,128)S(1)}, u32[]{:S(2)}, u32[]{:S(2)}) collective-permute-start(f32[32,128]{1,0:T(8,128)S(1)} %fusion), channel_id=1, source_target_pairs={{0,8},{1,9},{2,10},{3,11},{4,12},{5,13},{6,14},{7,15},{8,0},{9,1},... | collective-permute-start | bytes 49160 | tf_op jit(solution)/shard_map/ppermute | solution.py:452
  25.7 1.3 %collective-permute-start.9 = (f32[5,32,128]{2,1,0:T(8,128)S(1)}, f32[5,32,128]{2,1,0:T(8,128)S(1)}, u32[]{:S(2)}, u32[]{:S(2)}) collective-permute-start(f32[5,32,128]{2,1,0:T(8,128)S(1)} %get-tuple-element.51), channel_id=1, source_target_pairs={{0,1},{1,0},{2,3},{3,2},{4,5},{5,4},{6,7},{7,6},{8,9},{9,8},{10,11... | collective-permute-start | bytes 245768 | tf_op jit(solution)/shard_map/ppermute | solution.py:464
  25.8 5.1 %collective-permute-start.15 = (f32[4,32,128]{2,1,0:T(8,128)S(1)}, f32[4,32,128]{2,1,0:T(8,128)S(1)}, u32[]{:S(2)}, u32[]{:S(2)}) collective-permute-start(f32[4,32,128]{2,1,0:T(8,128)S(1)} %get-tuple-element.55), channel_id=1, source_target_pairs={{0,16},{1,2},{2,1},{3,19},{16,0},{17,18},{18,17},{19,3},{4,20},{5,... | collective-permute-start | bytes 196616 | tf_op jit(solution)/shard_map/ppermute | solution.py:464
  27.1 3.8 %collective-permute-start.14 = (f32[32,128]{1,0:T(8,128)S(1)}, f32[32,128]{1,0:T(8,128)S(1)}, u32[]{:S(2)}, u32[]{:S(2)}) collective-permute-start(f32[32,128]{1,0:T(8,128)S(1)} %bitcast_add_fusion), channel_id=1, source_target_pairs={{0,2},{1,3},{2,0},{3,1},{4,6},{5,7},{6,4},{7,5},{8,10},{9,11},{10,... | collective-permute-start | bytes 49160 | tf_op jit(solution)/shard_map/ppermute | solution.py:452
  33.5 1.3 %collective-permute-start.16 = (f32[48,128]{1,0:T(8,128)S(1)}, f32[48,128]{1,0:T(8,128)S(1)}, u32[]{:S(2)}, u32[]{:S(2)}) collective-permute-start(f32[48,128]{1,0:T(8,128)S(1)} %get-tuple-element.63), channel_id=1, source_target_pairs={{0,1},{1,0},{2,3},{3,2},{4,5},{5,4},{6,7},{7,6},{8,9},{9,8},{10,11... | collective-permute-start | bytes 73736 | tf_op jit(solution)/shard_map/ppermute | solution.py:452
  34.8 3.8 %collective-permute-start.19 = (f32[48,128]{1,0:T(8,128)S(1)}, f32[48,128]{1,0:T(8,128)S(1)}, u32[]{:S(2)}, u32[]{:S(2)}) collective-permute-start(f32[48,128]{1,0:T(8,128)S(1)} %add.51), channel_id=1, source_target_pairs={{0,4},{1,5},{2,6},{3,7},{4,0},{5,1},{6,2},{7,3},{8,12},{9,13},{10,... | collective-permute-start | bytes 73736 | tf_op jit(solution)/shard_map/ppermute | solution.py:452
  36.5 3.8 %collective-permute-start.18 = (f32[48,128]{1,0:T(8,128)S(1)}, f32[48,128]{1,0:T(8,128)S(1)}, u32[]{:S(2)}, u32[]{:S(2)}) collective-permute-start(f32[48,128]{1,0:T(8,128)S(1)} %add.51), channel_id=1, source_target_pairs={{0,2},{1,3},{2,0},{3,1},{4,6},{5,7},{6,4},{7,5},{8,10},{9,11},{10,... | collective-permute-start | bytes 73736 | tf_op jit(solution)/shard_map/ppermute | solution.py:452
  37.5 4.7 %collective-permute-start.17 = (f32[48,128]{1,0:T(8,128)S(1)}, f32[48,128]{1,0:T(8,128)S(1)}, u32[]{:S(2)}, u32[]{:S(2)}) collective-permute-start(f32[48,128]{1,0:T(8,128)S(1)} %add.51), channel_id=1, source_target_pairs={{0,6},{1,7},{2,4},{3,5},{4,2},{5,3},{6,0},{7,1},{8,14},{9,15},{10,... | collective-permute-start | bytes 73736 | tf_op jit(solution)/shard_map/ppermute | solution.py:452
  42.3 4.8 %collective-permute-start.20 = (f32[48,128]{1,0:T(8,128)S(1)}, f32[48,128]{1,0:T(8,128)S(1)}, u32[]{:S(2)}, u32[]{:S(2)}) collective-permute-start(f32[48,128]{1,0:T(8,128)S(1)} %add_add_fusion), channel_id=1, source_target_pairs={{0,8},{1,9},{2,10},{3,11},{4,12},{5,13},{6,14},{7,15},{8,0},{9,1},... | collective-permute-start | bytes 73736 | tf_op jit(solution)/shard_map/ppermute | solution.py:452
  47.1 1.3 %collective-permute-start.21 = (f32[40,128]{1,0:T(8,128)S(1)}, f32[40,128]{1,0:T(8,128)S(1)}, u32[]{:S(2)}, u32[]{:S(2)}) collective-permute-start(f32[40,128]{1,0:T(8,128)S(1)} %slice.13), channel_id=1, source_target_pairs={{0,1},{1,0},{2,3},{3,2},{4,5},{5,4},{6,7},{7,6},{8,9},{9,8},{10,11... | collective-permute-start | bytes 61448 | tf_op jit(solution)/shard_map/ppermute | solution.py:452
